TPU v7x, 32 devices: a whole 2x2x4 slice. The times are simulated.
32 devices in a mesh: dp: 8 (over z, y), ctx: 4 (over x, core).
Axes of the slice: x: 2, y: 2, z: 4, core: 2. Of those that a mesh axis runs over, the one named last changes fastest.
Arguments:
- route_pos: int32 [8, 512], P('dp', 'ctx'), may hold values from -1 to 2047, as said below
- x_routed: bfloat16 [8, 512, 4096], P('dp', 'ctx'), may hold values from -6 to 6
- w_router: bfloat16 [4096], P('dp'), may hold values from -0.09375 to 0.09375
- queries: bfloat16 [8, 512, 2048], P('dp', 'ctx'), may hold values from -8 to 8
- keys: bfloat16 [8, 512, 2048], P('dp', 'ctx'), may hold values from -8 to 8
- values: bfloat16 [8, 512, 2048], P('dp', 'ctx'), may hold values from -6 to 6
- d_gated: float32 [8, 512, 2048], P('dp', 'ctx'), may hold values from -6 to 6
Outputs:
- grad_queries: float32 [8, 512, 2048], P('dp', 'ctx')
- grad_keys: float32 [8, 512, 2048], P('dp', 'ctx')
- grad_values: float32 [8, 512, 2048], P('dp', 'ctx')
- router_grad: float32 [4096], P('dp')
Inputs may be any that keep to these rules, and one draw needn't show every extreme that they name: `route_pos`: in each sequence, context shard c lists in its 128 slots the increasing positions of its routed tokens, all from c * 512 to (c + 1) * 512 - 1, then -1 in its unused slots. A shard holds 0 to 128 routed tokens and a sequence 256 in all; in every sequence some shard holds exactly 128 and some shard none.
All inputs are finite; a program needn't handle non-finite values.
Results may differ from a plain program's by a relative error of at most 0.017.
Values may be sent and summed in bfloat16 or wider, within the bound.
No kernel may reach another device: no remote copies, remote signals or barrier semaphores. Data moves between devices by JAX's collectives and lax.ppermute only.
A program may use at most 128 MiB of HBM per device.

v0:
```python
import jax
import jax.numpy as jnp
from jax import lax
from jax.sharding import PartitionSpec as P

HEAD = 128


NEG_FILL = -1e30


def body(route_pos, x_routed, w_router, queries, keys, values, d_gated):
    slot_count = queries.shape[1]
    width = queries.shape[2]
    head_count = width // HEAD
    score_scale = HEAD ** (-0.5)
    positions = route_pos[0]
    is_live = positions >= 0
    live_float = is_live.astype(jnp.float32)
    router_full = lax.all_gather(w_router, "dp", axis=0, tiled=True)
    router_logit = jnp.dot(x_routed[0], router_full, preferred_element_type=jnp.float32)
    gate_value = jax.nn.sigmoid(router_logit)
    grad_rows = d_gated[0]
    grad_out = ((gate_value * live_float)[:, None] * grad_rows).astype(jnp.bfloat16)
    key_all, value_all, key_positions = (
        lax.all_gather(keys, "ctx", axis=1, tiled=True),
        lax.all_gather(values, "ctx", axis=1, tiled=True),
        lax.all_gather(route_pos, "ctx", axis=1, tiled=True),
    )
    query_heads = queries[0].reshape(slot_count, head_count, HEAD)
    grad_heads = grad_out.reshape(slot_count, head_count, HEAD)
    key_heads = key_all[0].reshape(-1, head_count, HEAD)
    value_heads = value_all[0].reshape(-1, head_count, HEAD)
    key_pos = key_positions[0]
    allowed = is_live[:, None] & (key_pos >= 0)[None, :] & (key_pos[None, :] <= positions[:, None])
    scores = (
        jnp.einsum("qhd,khd->hqk", query_heads, key_heads, preferred_element_type=jnp.float32)
        * score_scale
    )
    scores = jnp.where(allowed[None], scores, NEG_FILL)
    row_max = jnp.max(scores, axis=-1, keepdims=True)
    exponent = jnp.exp(scores - row_max)
    row_total = jnp.sum(exponent, axis=-1, keepdims=True)
    weights = exponent / row_total
    weights_low = weights.astype(jnp.bfloat16)
    attended = jnp.einsum(
        "hqk,khd->qhd", weights_low, value_heads, preferred_element_type=jnp.float32
    )
    grad_weights = jnp.einsum(
        "qhd,khd->hqk", grad_heads, value_heads, preferred_element_type=jnp.float32
    )
    row_delta = jnp.sum(grad_heads.astype(jnp.float32) * attended, axis=-1)
    grad_scores = weights * (grad_weights - row_delta.T[:, :, None]) * score_scale
    grad_low = grad_scores.astype(jnp.bfloat16)
    grad_query = jnp.einsum("hqk,khd->qhd", grad_low, key_heads, preferred_element_type=jnp.float32)
    grad_query = grad_query.reshape(slot_count, width)
    grad_gate = jnp.sum(attended.reshape(slot_count, width) * grad_rows, axis=-1) * live_float
    grad_logit = grad_gate * gate_value * (1.0 - gate_value)
    router_term = jnp.dot(
        grad_logit, x_routed[0].astype(jnp.float32), precision=lax.Precision.HIGHEST
    )
    total_routed = float(lax.axis_size("dp") * lax.axis_size("ctx") * slot_count // 2)
    window_sum = lax.psum(router_term, "ctx")
    router_grad = lax.psum_scatter(window_sum, "dp", scatter_dimension=0, tiled=True)
    router_grad = router_grad / total_routed
    key_part = jnp.einsum("hqk,qhd->khd", grad_low, query_heads, preferred_element_type=jnp.float32)
    value_part = jnp.einsum(
        "hqk,qhd->khd", weights_low, grad_heads, preferred_element_type=jnp.float32
    )
    both_grads = lax.psum_scatter(
        jnp.concatenate(
            [
                key_part.reshape(slot_count * lax.axis_size("ctx"), width),
                value_part.reshape(slot_count * lax.axis_size("ctx"), width),
            ],
            axis=1,
        ).astype(jnp.bfloat16),
        "ctx",
        scatter_dimension=0,
        tiled=True,
    ).astype(jnp.float32)
    grad_key = both_grads[:, :width]
    grad_value = both_grads[:, width:]
    return (grad_query[None], grad_key[None], grad_value[None], router_grad)


def solution(mesh):
    placed = (
        P("dp", "ctx"),
        P("dp", "ctx", None),
        P("dp"),
        P("dp", "ctx", None),
        P("dp", "ctx", None),
        P("dp", "ctx", None),
        P("dp", "ctx", None),
    )
    return jax.shard_map(
        body,
        mesh=mesh,
        in_specs=placed,
        out_specs=(P("dp", "ctx", None), P("dp", "ctx", None), P("dp", "ctx", None), P("dp")),
        check_vma=False,
    )
```

profile of v0, /device:TPU:0, one launch (start us, length us, event | category | flops | bytes accessed | tf_op | source)
XLA Modules:
  0.0 143.8 jit_solution(17355231054357106269)
XLA Ops:
  7.3 2.2 %copy.31 = bf16[1,128,2048]{1,2,0:T(8,128)(2,1)} copy(bf16[1,128,2048]{2,1,0:T(8,128)(2,1)} %param.11) | data formatting | bytes 1048576 | tf_op args[4]
  9.5 2.0 %copy.35 = bf16[1,128,2048]{1,2,0:T(8,128)(2,1)} copy(bf16[1,128,2048]{2,1,0:T(8,128)(2,1)} %param.12) | data formatting | bytes 1048576 | tf_op args[5]
  12.0 1.3 copy.34
  13.3 5.9 %all_gather.14 = s32[1,512]{1,0:T(1,128)S(1)} all-gather(s32[1,128]{1,0:T(1,128)S(1)} %copy-done.7), channel_id=1, replica_groups=mesh['dp'=8,'ctx'=4] {'ctx'}, dimensions={1}, use_global_device_ids=true | all-gather | bytes 2560 | tf_op jit(solution)/shard_map/all_gather | solution.py:28
  19.2 26.9 %all-gather = bf16[8,1,512]{2,1,0:T(2,128)(2,1)S(1)} all-gather(bf16[1,1,512]{2,1,0:T(2,128)(2,1)S(1)} %reshape.96), channel_id=1, replica_groups=mesh['dp'=8,'ctx'=4] {'dp'}, dimensions={0}, use_global_device_ids=true | all-gather | bytes 9216 | tf_op jit(solution)/shard_map/all_gather | solution.py:20
  46.6 5.4 %fusion.26 = (f32[16,128]{1,0:T(8,128)S(1)}, f32[16,128,512]{2,1,0:T(8,128)}) fusion(pred[128,512]{1,0:T(8,128)(4,1)S(1)} %compare_and_fusion, bf16[128,16,128]{0,2,1:T(8,128)(2,1)S(1)} %bitcast.70, bf16[512,16,128]{0,2,1:T(8,128)(2,1)} %bitcast.72), kind=kOutput, calls=%fused_computation.44 | convolution fusion | flops 272630272 | bytes 6889472 | tf_op jit(solution)/shard_map/sub | solution.py:42
  52.0 2.6 %fusion.5 = bf16[16,128,512]{2,1,0:T(8,128)(2,1)S(1)} fusion(f32[16,128,512]{2,1,0:T(8,128)} %get-tuple-element.22, f32[16,128]{1,0:T(8,128)S(1)} %get-tuple-element.21), kind=kLoop, calls=%fused_computation.12 | loop fusion | flops 2097152 | bytes 6299648 | tf_op jit(solution)/shard_map/convert_element_type | solution.py:45
  54.6 6.1 %all-gather.6.cloned.1.call-done = bf16[1,512,2048]{1,2,0:T(8,128)(2,1)} async-done(((bf16[1,128,2048]{1,2,0:T(8,128)(2,1)}), bf16[1,512,2048]{1,2,0:T(8,128)(2,1)}) %all-gather.6.cloned.1.call-update) | async-done | bytes 2097168 | tf_op jit(solution)/shard_map/all_gather | solution.py:27
  60.7 2.7 %multiply_reduce_fusion = (f32[128]{0:T(128)S(1)}, f32[128,16]{0,1:T(8,128)S(1)}, bf16[128,16,128]{0,2,1:T(8,128)(2,1)S(1)}) fusion(f32[128,16,128]{0,2,1:T(8,128)} %bitcast.68, f32[128]{0:T(128)S(1)} %get-tuple-element.23, bf16[16,128,512]{2,1,0:T(8,128)(2,1)S(1)} %fusion.5, bf16[512,16,128]{0,2,1:T(8,128)(2,1)} %bitcast.74), kind=kOutput, calls=%fused_computation.24 | convolution fusion | flops 270268288 | bytes 5776384 | tf_op jit(solution)/shard_map/hqk,khd->qhd/dot_general | solution.py:46
  63.5 2.0 %convolution_convert_fusion.1 = bf16[16,128,512]{2,1,0:T(8,128)(2,1)} fusion(bf16[128,16,128]{0,2,1:T(8,128)(2,1)S(1)} %get-tuple-element.18, bf16[16,128,512]{2,1,0:T(8,128)(2,1)S(1)} %fusion.5), kind=kOutput, calls=%fused_computation.11 | convolution fusion | flops 269484032 | bytes 4718592 | tf_op jit(solution)/shard_map/hqk,qhd->khd/dot_general | solution.py:67
  65.5 1.0 copy-done.1
  66.4 1.1 multiply_convert_fusion
  67.6 2.0 %convolution_convert_fusion = bf16[16,512,128]{1,2,0:T(8,128)(2,1)} fusion(bf16[128,16,128]{0,2,1:T(8,128)(2,1)S(1)} %bitcast.71, bf16[16,128,512]{2,1,0:T(8,128)(2,1)S(1)} %multiply_convert_fusion), kind=kOutput, calls=%fused_computation.10 | convolution fusion | flops 269484032 | bytes 4718592 | tf_op jit(solution)/shard_map/hqk,qhd->khd/dot_general | solution.py:66
  69.6 4.0 %copy.39 = bf16[512,2048]{1,0:T(8,128)(2,1)} copy(bf16[512,2048]{0,1:T(8,128)(2,1)} %bitcast.67) | data formatting | bytes 4194304 | tf_op jit(solution)/shard_map/reshape | solution.py:73
  73.6 4.0 %copy.40 = bf16[512,2048]{1,0:T(8,128)(2,1)} copy(bf16[512,2048]{0,1:T(8,128)(2,1)} %bitcast.66) | data formatting | bytes 4194304 | tf_op jit(solution)/shard_map/reshape | solution.py:74
  77.6 4.8 %pad_maximum_fusion = bf16[512,4096]{1,0:T(8,128)(2,1)} fusion(bf16[512,2048]{1,0:T(8,128)(2,1)} %copy.40, bf16[512,2048]{1,0:T(8,128)(2,1)} %copy.39), kind=kLoop, calls=%fused_computation.1 | loop fusion | flops 8388608 | bytes 8388608 | tf_op jit(solution)/shard_map/concatenate | solution.py:71
  82.4 0.6 copy-done.9
  84.2 3.3 %fusion.27 = f32[16,128,128]{1,2,0:T(8,128)} fusion(bf16[16,128,512]{2,1,0:T(8,128)(2,1)S(1)} %multiply_convert_fusion, bf16[512,16,128]{0,2,1:T(8,128)(2,1)} %bitcast.73), kind=kOutput, calls=%fused_computation.45 | convolution fusion | flops 268435456 | bytes 5242880 | tf_op jit(solution)/shard_map/hqk,khd->qhd/dot_general | solution.py:55
  87.5 2.6 %copy.41 = f32[1,128,2048]{2,1,0:T(8,128)} copy(f32[1,128,2048]{1,2,0:T(8,128)} %bitcast.69) | data formatting | bytes 2097152
  90.7 37.3 %all-reduce = f32[4096]{0:T(1024)S(1)} all-reduce(f32[4096]{0:T(1024)S(1)} %bitcast.77), channel_id=3, replica_groups=mesh['dp'=8,'ctx'=4] {'dp'}, use_global_device_ids=true, to_apply=%region_6.7.clone | all-reduce | flops 4096 | bytes 32768
  128.0 5.7 %psum.8 = f32[512]{0:T(512)S(1)} all-reduce(f32[512]{0:T(512)S(1)} %dynamic-slice.1), channel_id=1, replica_groups=mesh['dp'=8,'ctx'=4] {'ctx'}, use_global_device_ids=true, to_apply=%region_5.6 | all-reduce | flops 512 | bytes 4096 | tf_op jit(solution)/shard_map/psum | solution.py:63
  133.8 0.6 broadcast_multiply_fusion
  134.3 1.4 convert_element_type.23
  135.8 1.5 %slice_bitcast_fusion = (f32[1,128,2048]{2,1,0:T(8,128)}, f32[1,128,2048]{2,1,0:T(8,128)}) fusion(f32[128,4096]{1,0:T(8,128)S(1)} %convert_element_type.23), kind=kLoop, calls=%fused_computation.19 | loop fusion | bytes 4194304 | tf_op jit(solution)/shard_map/broadcast_in_dim | solution.py:84
  (35 shorter events, 2.2 us)
Async XLA Ops:
  7.2 39.1 %copy-start = (bf16[1,128,4096]{2,1,0:T(8,128)(2,1)S(1)}, bf16[1,128,4096]{2,1,0:T(8,128)(2,1)}, u32[]{:S(2)}) copy-start(bf16[1,128,4096]{2,1,0:T(8,128)(2,1)} %param.8) | copy-start | bytes 3145732
  7.2 4.5 %copy-start.6 = (bf16[1,128,2048]{2,1,0:T(8,128)(2,1)S(1)}, bf16[1,128,2048]{2,1,0:T(8,128)(2,1)}, u32[]{:S(2)}) copy-start(bf16[1,128,2048]{2,1,0:T(8,128)(2,1)} %param.10) | copy-start | bytes 1572868
  7.2 4.7 %copy-start.8 = (bf16[512]{0:T(512)(128)(2,1)S(1)}, bf16[512]{0:T(512)(128)(2,1)}, u32[]{:S(2)}) copy-start(bf16[512]{0:T(512)(128)(2,1)} %param.9) | copy-start | bytes 3076
  7.2 4.8 %copy-start.5 = (f32[1,128,2048]{2,1,0:T(8,128)S(1)}, f32[1,128,2048]{2,1,0:T(8,128)}, u32[]{:S(2)}) copy-start(f32[1,128,2048]{2,1,0:T(8,128)} %param.13) | copy-start | bytes 3145732
  7.2 39.4 %all-gather.4.cloned.1.call-start = ((), (), s32[]{:S(2)}) async-start(), calls=%async_computation.1 | async-start | bytes 2621440 | tf_op jit(solution)/shard_map/all_gather | solution.py:26
  9.5 51.3 %all-gather.6.cloned.1.call-start = ((), (), s32[]{:S(2)}) async-start(), calls=%async_computation.2 | async-start | bytes 2621440 | tf_op jit(solution)/shard_map/all_gather | solution.py:27
  11.6 1.7 %copy-start.7 = (s32[1,128]{1,0:T(1,128)S(1)}, s32[1,128]{1,0:T(1,128)}, u32[]{:S(2)}) copy-start(s32[1,128]{1,0:T(1,128)} %param.7) | copy-start | bytes 1540
  11.6 122.7 %reduce-scatter.2.cloned.1.call-start = ((), (), s32[]{:S(2)}) async-start(), calls=%async_computation.3 | async-start | bytes 5242880 | tf_op jit(solution)/shard_map/reduce_scatter | solution.py:70
  11.9 40.1 %copy-start.2 = (bf16[1,128,2048]{1,2,0:T(8,128)(2,1)}, bf16[1,128,2048]{1,2,0:T(8,128)(2,1)S(1)}, u32[]{:S(2)}) copy-start(bf16[1,128,2048]{1,2,0:T(8,128)(2,1)S(1)} %copy.45) | copy-start | bytes 1572868
  60.7 4.7 %copy-start.4 = (bf16[1,512,2048]{1,2,0:T(8,128)(2,1)S(1)}, bf16[1,512,2048]{1,2,0:T(8,128)(2,1)}, u32[]{:S(2)}) copy-start(bf16[1,512,2048]{1,2,0:T(8,128)(2,1)} %all-gather.6.cloned.1.call-done) | copy-start | bytes 6291460
  63.5 2.9 %copy-start.1 = (f32[16,128,512]{2,1,0:T(8,128)S(1)}, f32[16,128,512]{2,1,0:T(8,128)}, u32[]{:S(2)}) copy-start(f32[16,128,512]{2,1,0:T(8,128)} %get-tuple-element.22) | copy-start | bytes 12582916
  66.4 1.2 copy-start.3
  82.4 0.7 copy-start.9
Sparse Core Ops, SparseCore 0:
  10.2 25.5 all-gather.3
  37.9 22.8 all-gather.5
  82.5 44.4 reduce-scatter.1
where the time goes:
time: 144 us
  blocking collectives  75.8 us (53%)
  local copies, waits for them, and re-layouts  20.2 us (14%)
  matrix products  17.5 us (12%)
  between operations  14.6 us (10%)
  other arithmetic  9.46 us (7%)
  waiting for transfers between devices  6.19 us (4%)
    unnamed x1, blocking collectives  37.3 us
    all_gather x1, blocking collectives, body(): router_full = lax.all_gather(w_router, 'dp', axis=0, tiled=True)  26.9 us
    unnamed x27, local copies, waits for them, and re-layouts  10.5 us
    all_gather x1, waiting for transfers between devices, body(): lax.all_gather(values, 'ctx', axis=1, tiled=True)  6.13 us
    all_gather x1, blocking collectives, body(): lax.all_gather(route_pos, 'ctx', axis=1, tiled=True)  5.94 us
    psum x1, blocking collectives, body(): window_sum = lax.psum(router_term, 'ctx')  5.73 us
    sub x1, matrix products, body(): exponent = jnp.exp(scores - row_max)  5.41 us
    concatenate x1, other arithmetic, body(): jnp.concatenate([key_part.reshape(slot_count * lax.axis_size('ctx'), widt...  4.75 us
  transfers between devices with their start and end apart: 3, of which 1 were waited for; matrix products, arithmetic and copies ran while one was open for 14% of the time, Pallas kernels for 0%

commit v1 on v0

v1 whole, which is shorter than its diff:
```python
import functools

import jax
import jax.numpy as jnp
from jax import lax
from jax.experimental import pallas as pl
from jax.experimental.pallas import tpu as pltpu
from jax.sharding import PartitionSpec as P

HEAD = 128
GROUPS = 4
NEG_FILL = -1e30
VMEM_LIMIT = 48 * 1024 * 1024
BF16 = jnp.bfloat16
F32 = jnp.float32

VMEM = pl.BlockSpec(memory_space=pltpu.VMEM)
SMEM = pl.BlockSpec(memory_space=pltpu.SMEM)


def params():
    return pltpu.CompilerParams(vmem_limit_bytes=VMEM_LIMIT)


def cost(flops, nbytes, exps=0):
    return pl.CostEstimate(flops=int(flops), bytes_accessed=int(nbytes), transcendentals=int(exps))


def nt(a, b):
    return lax.dot_general(a, b, (((1,), (1,)), ((), ())), preferred_element_type=F32)


def nn(a, b):
    return lax.dot_general(a, b, (((1,), (0,)), ((), ())), preferred_element_type=F32)


def tn(a, b):
    return lax.dot_general(a, b, (((0,), (0,)), ((), ())), preferred_element_type=F32)


def pack_kernel(groups, width, core_ref, first_ref, second_ref, *outs):
    half = first_ref.shape[-1] // 2
    core = core_ref[0]
    for side in range(2):
        base = (core if side == 0 else 1 - core) * half
        for g in range(groups):
            out = outs[side * groups + g]
            cols = pl.ds(pl.multiple_of(base + g * width, HEAD), width)
            out[0] = first_ref[0, :, cols].astype(BF16)
            out[1] = second_ref[0, :, cols].astype(BF16)


def pack(core, first, second, groups, width):
    slots = first.shape[1]
    out = jax.ShapeDtypeStruct((2, slots, width), BF16)
    res = pl.pallas_call(
        functools.partial(pack_kernel, groups, width),
        out_shape=[out] * (2 * groups),
        in_specs=[SMEM, VMEM, VMEM],
        out_specs=[VMEM] * (2 * groups),
        compiler_params=params(),
        cost_estimate=cost(0, 2 * first.size * 4),
        name="pack",
    )(core, first, second)
    return res[:groups], res[groups:]


def gate_kernel(parts, offset_ref, pos_ref, x_ref, *refs):
    w_refs, out_ref = refs[:parts], refs[parts]
    chunk = w_refs[0].shape[-1]
    total = jnp.zeros((8, x_ref.shape[1]), F32)
    for s in range(parts):
        cols = pl.ds(pl.multiple_of(offset_ref[s] * chunk, HEAD), chunk)
        w_rows = jnp.broadcast_to(w_refs[s][...].astype(F32), (8, chunk)).astype(BF16)
        total = total + nt(w_rows, x_ref[0, :, cols])
    gate = 1.0 / (1.0 + jnp.exp(-total[0:1]))
    out_ref[...] = jnp.where(pos_ref[...] >= 0, gate, 0.0)


def router_gate(offsets, route_pos, x_routed, w_parts):
    parts = len(w_parts)
    return pl.pallas_call(
        functools.partial(gate_kernel, parts),
        out_shape=jax.ShapeDtypeStruct(route_pos.shape, F32),
        in_specs=[SMEM] + [VMEM] * (2 + parts),
        out_specs=VMEM,
        compiler_params=params(),
        cost_estimate=cost(16 * x_routed.size, x_routed.size * 2),
        name="router_gate",
    )(offsets, route_pos, x_routed, *w_parts)


def attention_kernel(remote, scale, core_ref, live_ref, gate_own, gate_sib, acc_own, acc_sib, q_own, q_sib, *refs):
    chunks = 2 + remote
    kv = refs[:chunks]
    outs = refs[chunks:]
    dq_own, sib_out, kv_own = outs[:3]
    kv_remote = outs[3 : 3 + remote]
    sum_own, sum_sib = outs[3 + remote :]
    slots, width = q_own.shape[1], q_own.shape[2]
    core = core_ref[0]
    key = lax.broadcasted_iota(jnp.int32, (slots, slots), 0)
    query = lax.broadcasted_iota(jnp.int32, (slots, slots), 1)
    counts = [jnp.sum(live_ref[i : i + 1], axis=1, keepdims=True) for i in range(chunks)]
    lives = [key < counts[i] for i in range(chunks)]
    own_later = core == 1
    bias_rows = []
    for i in range(chunks):
        live = lives[i]
        if i == 0:
            pair = (live & (key <= query), live & jnp.logical_not(own_later))
        elif i == 1:
            pair = (live & own_later, live & (key <= query))
        else:
            pair = (live, live)
        bias_rows.append(jnp.concatenate([jnp.where(p, 0.0, NEG_FILL) for p in pair], axis=1))
    bias = jnp.concatenate(bias_rows, axis=0)
    gates = jnp.concatenate([gate_own[...], gate_sib[...]], axis=1)
    total = jnp.zeros((1, 2 * slots), F32)
    for h in range(width // HEAD):
        cols = slice(h * HEAD, (h + 1) * HEAD)
        q = jnp.concatenate([q_own[0, :, cols], q_sib[0, :, cols]], axis=0)
        dg = jnp.concatenate([q_own[1, :, cols], q_sib[1, :, cols]], axis=0)
        k = jnp.concatenate([r[0, :, cols] for r in kv], axis=0)
        v = jnp.concatenate([r[1, :, cols] for r in kv], axis=0)
        scores = nt(k, q) * scale + bias
        top = jnp.max(scores, axis=0, keepdims=True)
        e = jnp.exp(scores - top)
        inverse = 1.0 / jnp.sum(e, axis=0, keepdims=True)
        gw = nt(v, dg)
        delta = jnp.sum(e * gw, axis=0, keepdims=True) * inverse
        total = total + delta
        weights = e * (inverse * gates)
        dv = nn(weights.astype(BF16), dg)
        ds = (weights * ((gw - delta) * scale)).astype(BF16)
        dk = nn(ds, q)
        dq = tn(ds, k)
        dq_own[:, cols] = dq[:slots].astype(dq_own.dtype)
        sib_out[0, :, cols] = dq[slots:].astype(BF16)
        kv_own[0, :, cols] = dk[:slots].astype(BF16)
        kv_own[1, :, cols] = dv[:slots].astype(BF16)
        sib_out[1, :, cols] = dk[slots : 2 * slots].astype(BF16)
        sib_out[2, :, cols] = dv[slots : 2 * slots].astype(BF16)
        for i in range(remote):
            rows = slice((2 + i) * slots, (3 + i) * slots)
            kv_remote[i][0, :, cols] = dk[rows].astype(BF16)
            kv_remote[i][1, :, cols] = dv[rows].astype(BF16)
    sum_own[...] = acc_own[...] + total[:, :slots]
    sum_sib[...] = acc_sib[...] + total[:, slots:]


def attention(core, live, gates, accs, q_own, q_sib, kv):
    remote = len(kv) - 2
    _, slots, width = q_own.shape
    pair = jax.ShapeDtypeStruct((2, slots, width), BF16)
    row = jax.ShapeDtypeStruct((1, slots), F32)
    outs = [
        jax.ShapeDtypeStruct((slots, width), BF16),
        jax.ShapeDtypeStruct((3, slots, width), BF16),
        pair,
        *([pair] * remote),
        row,
        row,
    ]
    keys = (2 + remote) * slots
    res = pl.pallas_call(
        functools.partial(attention_kernel, remote, HEAD**-0.5),
        out_shape=outs,
        in_specs=[SMEM] + [VMEM] * (7 + len(kv)),
        out_specs=[VMEM] * len(outs),
        compiler_params=params(),
        cost_estimate=cost(20 * slots * keys * width, 8 * keys * width + 20 * slots * width, 2 * slots * keys * width // HEAD),
        name="attention",
    )(core, live, *gates, *accs, q_own, q_sib, *kv)
    return res[0], res[1], res[2], res[3 : 3 + remote], (res[3 + remote], res[4 + remote])


def combine_kernel(groups, width, remote, core_ref, *refs):
    dq_own, sib, kv_own = refs[:groups], refs[groups : 2 * groups], refs[2 * groups : 3 * groups]
    back = refs[3 * groups : 3 * groups + groups * remote]
    dq_out, dk_out, dv_out = refs[3 * groups + groups * remote :]
    half = groups * width
    core = core_ref[0]
    for g in range(groups):
        own = pl.ds(pl.multiple_of(core * half + g * width, HEAD), width)
        other = pl.ds(pl.multiple_of((1 - core) * half + g * width, HEAD), width)
        dq_out[0, :, own] = dq_own[g][...].astype(F32)
        dq_out[0, :, other] = sib[g][0].astype(F32)
        for i, out in enumerate((dk_out, dv_out)):
            mine = kv_own[g][i].astype(F32)
            theirs = sib[g][1 + i].astype(F32)
            for r in range(remote):
                part = back[g * remote + r][i].astype(F32)
                if r % 2 == 0:
                    mine = mine + part
                else:
                    theirs = theirs + part
            out[0, :, own] = mine
            out[0, :, other] = theirs


def combine(core, dq_own, sib, kv_own, back, shape):
    groups = len(dq_own)
    remote = len(back[0])
    out = jax.ShapeDtypeStruct(shape, F32)
    flat = [*dq_own, *sib, *kv_own, *(b for group in back for b in group)]
    return pl.pallas_call(
        functools.partial(combine_kernel, groups, dq_own[0].shape[-1], remote),
        out_shape=[out] * 3,
        in_specs=[SMEM] + [VMEM] * len(flat),
        out_specs=[VMEM] * 3,
        compiler_params=params(),
        cost_estimate=cost(0, 3 * out.size * 6),
        name="combine",
    )(core, *flat)


def router_kernel(parts, target_ref, gate_ref, own_ref, sib_ref, x_ref, *outs):
    gate = gate_ref[...]
    grad = (own_ref[...] + sib_ref[...]) * gate * (1.0 - gate)
    high = grad.astype(BF16)
    rest = grad - high.astype(F32)
    mid = rest.astype(BF16)
    low = (rest - mid.astype(F32)).astype(BF16)
    row = lax.broadcasted_iota(jnp.int32, (8, grad.shape[1]), 0)
    lhs = jnp.where(row == 0, high.astype(F32), jnp.where(row == 1, mid.astype(F32), jnp.where(row == 2, low.astype(F32), 0.0)))
    lhs = lhs.astype(BF16)
    chunk = outs[0].shape[-1]
    for s in range(parts):
        cols = pl.ds(pl.multiple_of(target_ref[s] * chunk, HEAD), chunk)
        outs[s][...] = jnp.sum(nn(lhs, x_ref[0, :, cols]), axis=0, keepdims=True)


def router_terms(targets, gate, own, sib, x_routed, parts):
    chunk = x_routed.shape[-1] // parts
    return pl.pallas_call(
        functools.partial(router_kernel, parts),
        out_shape=[jax.ShapeDtypeStruct((1, chunk), F32)] * parts,
        in_specs=[SMEM] + [VMEM] * 4,
        out_specs=[VMEM] * parts,
        compiler_params=params(),
        cost_estimate=cost(16 * x_routed.size, x_routed.size * 2),
        name="router_terms",
    )(targets, gate, own, sib, x_routed)


def body(route_pos, x_routed, w_router, queries, keys, values, d_gated):
    slots, full = queries.shape[1], queries.shape[2]
    n, ndp = lax.axis_size("ctx"), lax.axis_size("dp")
    chips = n // 2
    me, dp_me = lax.axis_index("ctx"), lax.axis_index("dp")
    core = (me % 2).astype(jnp.int32).reshape(1)
    half = full // 2
    groups = GROUPS if (half // HEAD) % GROUPS == 0 else 1
    width = half // groups

    sib_pairs = [(i, i ^ 1) for i in range(n)]

    def forward_pairs(step, flip):
        return [(i, (i + 2 * step) ^ flip) for i in range(n) if i + 2 * step < n]

    def back_pairs(step, flip):
        return [(b, a) for a, b in forward_pairs(step, flip)]

    def to_sib(a):
        return lax.ppermute(a, "ctx", sib_pairs)

    links = [(step, flip) for step in range(1, chips) for flip in (0, 1)]

    w_row = w_router.reshape(1, -1)
    w_parts = [w_row] + [
        lax.ppermute(w_row, "dp", [(i, (i + s) % ndp) for i in range(ndp)]) for s in range(1, ndp)
    ]
    live = (route_pos >= 0).astype(jnp.int32)
    lives = [live, to_sib(live)] + [lax.ppermute(live, "ctx", forward_pairs(*link)) for link in links]
    live_all = jnp.concatenate(lives, axis=0)

    kv_mine, kv_theirs = pack(core, keys, values, groups, width)
    kv_far = [
        [lax.ppermute((kv_theirs if flip else kv_mine)[g], "ctx", forward_pairs(step, flip)) for step, flip in links]
        for g in range(groups)
    ]
    q_mine, q_theirs = pack(core, queries, d_gated, groups, width)
    kv_sib = [to_sib(a) for a in kv_theirs]
    q_sib = [to_sib(a) for a in q_theirs]

    offsets = ((dp_me - jnp.arange(ndp)) % ndp).astype(jnp.int32)
    gate = router_gate(offsets, route_pos, x_routed, w_parts)
    gates = (gate, to_sib(gate))

    accs = (jnp.zeros((1, slots), F32), jnp.zeros((1, slots), F32))
    dq_own, sib_in, kv_own, back = [], [], [], []
    for g in range(groups):
        dq, sib_out, kv_local, kv_remote, accs = attention(
            core, live_all, gates, accs, q_mine[g], q_sib[g], [kv_mine[g], kv_sib[g], *kv_far[g]]
        )
        back.append([lax.ppermute(a, "ctx", back_pairs(*link)) for a, link in zip(kv_remote, links)])
        sib_in.append(to_sib(sib_out))
        dq_own.append(dq)
        kv_own.append(kv_local)

    targets = ((dp_me + jnp.arange(ndp)) % ndp).astype(jnp.int32)
    terms = router_terms(targets, gate, accs[0], to_sib(accs[1]), x_routed, ndp)
    mine = terms[0]
    for s in range(1, ndp):
        mine = mine + lax.ppermute(terms[s], "dp", [(i, (i + s) % ndp) for i in range(ndp)])
    total = mine
    for s in range(1, n):
        total = total + lax.ppermute(mine, "ctx", [(i, (i + s) % n) for i in range(n)])
    router_grad = total[0] / float(ndp * n * slots // 2)

    dq, dk, dv = combine(core, dq_own, sib_in, kv_own, back, queries.shape)
    return dq, dk, dv, router_grad


def solution(mesh):
    placed = (
        P("dp", "ctx"),
        P("dp", "ctx", None),
        P("dp"),
        P("dp", "ctx", None),
        P("dp", "ctx", None),
        P("dp", "ctx", None),
        P("dp", "ctx", None),
    )
    return jax.shard_map(
        body,
        mesh=mesh,
        in_specs=placed,
        out_specs=(P("dp", "ctx", None), P("dp", "ctx", None), P("dp", "ctx", None), P("dp")),
        check_vma=False,
    )
```

time: 144 us -> 101 us (0.70)
  blocking collectives: 75.8 us -> 0 us
  starting transfers between devices: 0.12 us -> 67.3 us
  matrix products: 17.5 us -> 0 us
  local copies, waits for them, and re-layouts: 20.2 us -> 3.62 us
  between operations: 14.6 us -> 1.15 us
  waiting for transfers between devices: 6.19 us -> 17.5 us
  Pallas kernels: 0 us -> 10.1 us
  other arithmetic: 9.46 us -> 0.64 us
    ppermute x0 -> x50, starting transfers between devices: none -> 67.3 us  [the longest x8 19.9 us: body(): lax.ppermute((kv_theirs if flip else kv_mine)[g], 'ctx', forward_pairs(st...]
    unnamed x1 -> x0, blocking collectives: 37.3 us -> none
    all_gather x2 -> x0, blocking collectives: 32.8 us -> none  [the longest x1 26.9 us: body(): router_full = lax.all_gather(w_router, 'dp', axis=0, tiled=True)]
    ppermute x0 -> x50, waiting for transfers between devices: none -> 17.5 us  [the longest x8 10.2 us: body(): lax.ppermute(a, 'ctx', back_pairs(*link))]
    dot_general x7 -> x0, matrix products: 12.1 us -> none  [the longest x1 3.27 us: body(): jnp.einsum('hqk,khd->qhd', grad_low, key_heads, preferred_element_type=jn...]
    pallas_call x0 -> x9, Pallas kernels: none -> 10.1 us  [the longest x4 6.17 us: attention(): pl.pallas_call(functools.partial(attention_kernel, remote, HEAD ** (-0.5)...]
    unnamed x27 -> x12, local copies, waits for them, and re-layouts: 10.5 us -> 2.85 us
    reshape x2 -> x1, local copies, waits for them, and re-layouts: 7.97 us -> 0.77 us  [body(): w_row = w_router.reshape(1, -1)]
  transfers between devices with their start and end apart: 3 -> 50, of which waited for: 1 -> 12; matrix products, arithmetic and copies ran while one was open for 14% -> 1% of each run, Pallas kernels for 0% -> 6%
where the time goes in v1:
time: 101 us; the launch traced here: 100 us
  starting transfers between devices  67.3 us (67%)
  waiting for transfers between devices  17.5 us (17%)
  Pallas kernels  10.1 us (10%)
  local copies, waits for them, and re-layouts  3.62 us (4%)
  between operations  1.15 us (1%)
    ppermute x8, starting transfers between devices, body(): lax.ppermute((kv_theirs if flip else kv_mine)[g], 'ctx', forward_pairs(st...  19.9 us
    ppermute x7, starting transfers between devices, body(): lax.ppermute(w_row, 'dp', [(i, (i + s) % ndp) for i in range(ndp)])  12.4 us
    ppermute x7, starting transfers between devices, body(): lax.ppermute(terms[s], 'dp', [(i, (i + s) % ndp) for i in range(ndp)])  11.2 us
    ppermute x8, starting transfers between devices, body(): lax.ppermute(a, 'ctx', back_pairs(*link))  10.3 us
    ppermute x8, waiting for transfers between devices, body(): lax.ppermute(a, 'ctx', back_pairs(*link))  10.2 us
    pallas_call x4, Pallas kernels, attention(): pl.pallas_call(functools.partial(attention_kernel, remote, HEAD ** (-0.5)...  6.17 us
    ppermute x2, starting transfers between devices, body(): lax.ppermute(live, 'ctx', forward_pairs(*link))  5.66 us
    ppermute x15, starting transfers between devices, to_sib(): return lax.ppermute(a, 'ctx', sib_pairs)  4.85 us
  transfers between devices with their start and end apart: 50, of which 12 were waited for; matrix products, arithmetic and copies ran while one was open for 1% of the time, Pallas kernels for 6%

profile of v1, /device:TPU:0, one launch (start us, length us, event | category | flops | bytes accessed | tf_op | source)
XLA Modules:
  0.0 100.3 jit_solution(11656161614401868422)
XLA Ops:
  1.4 6.0 %collective-permute-start.9 = (bf16[1,512]{1,0:T(2,128)(2,1)S(1)}, bf16[1,512]{1,0:T(2,128)(2,1)S(1)}, u32[]{:S(2)}, u32[]{:S(2)}) collective-permute-start(bf16[1,512]{1,0:T(2,128)(2,1)S(1)} %reshape.17.refs_0_), channel_id=1, source_target_pairs={{0,28},{4,0},{8,4},{12,8},{16,12},{20,16},{24,20},{28,24},{1,29},{... | collective-permute-start | bytes 3080 | tf_op jit(solution)/shard_map/ppermute | solution.py:272
  7.9 3.0 %collective-permute-start.6 = (bf16[1,512]{1,0:T(2,128)(2,1)S(1)}, bf16[1,512]{1,0:T(2,128)(2,1)S(1)}, u32[]{:S(2)}, u32[]{:S(2)}) collective-permute-start(bf16[1,512]{1,0:T(2,128)(2,1)S(1)} %reshape.17.refs_0_), channel_id=1, source_target_pairs={{0,16},{4,20},{8,24},{12,28},{16,0},{20,4},{24,8},{28,12},{1,17},{... | collective-permute-start | bytes 3080 | tf_op jit(solution)/shard_map/ppermute | solution.py:272
  13.9 1.8 %collective-permute-start.4 = (bf16[1,512]{1,0:T(2,128)(2,1)S(1)}, bf16[1,512]{1,0:T(2,128)(2,1)S(1)}, u32[]{:S(2)}, u32[]{:S(2)}) collective-permute-start(bf16[1,512]{1,0:T(2,128)(2,1)S(1)} %reshape.17.refs_0_), channel_id=1, source_target_pairs={{0,8},{4,12},{8,16},{12,20},{16,24},{20,28},{24,0},{28,4},{1,9},{5... | collective-permute-start | bytes 3080 | tf_op jit(solution)/shard_map/ppermute | solution.py:272
  17.0 2.3 %collective-permute-start.2 = (s32[1,128]{1,0:T(1,128)S(1)}, s32[1,128]{1,0:T(1,128)S(1)}, u32[]{:S(2)}, u32[]{:S(2)}) collective-permute-start(s32[1,128]{1,0:T(1,128)S(1)} %compare_convert_fusion), channel_id=1, source_target_pairs={{0,3},{1,2},{4,7},{5,6},{8,11},{9,10},{12,15},{13,14},{16,19},{17,... | collective-permute-start | bytes 1544 | tf_op jit(solution)/shard_map/ppermute | solution.py:275
  19.3 3.4 %collective-permute-start.1 = (s32[1,128]{1,0:T(1,128)S(1)}, s32[1,128]{1,0:T(1,128)S(1)}, u32[]{:S(2)}, u32[]{:S(2)}) collective-permute-start(s32[1,128]{1,0:T(1,128)S(1)} %compare_convert_fusion), channel_id=1, source_target_pairs={{0,2},{1,3},{4,6},{5,7},{8,10},{9,11},{12,14},{13,15},{16,18},{17,... | collective-permute-start | bytes 1544 | tf_op jit(solution)/shard_map/ppermute | solution.py:275
  25.0 3.1 %collective-permute-start.13 = (bf16[2,128,256]{2,1,0:T(8,128)(2,1)S(1)}, bf16[2,128,256]{2,1,0:T(8,128)(2,1)S(1)}, u32[]{:S(2)}, u32[]{:S(2)}) collective-permute-start(bf16[2,128,256]{2,1,0:T(8,128)(2,1)S(1)} %get-tuple-element.61.refs_0_), channel_id=1, source_target_pairs={{0,2},{1,3},{4,6},{5,7},{8,10},{9,11},{12,14},{13,15},{16,18},{17,... | collective-permute-start | bytes 393224 | tf_op jit(solution)/shard_map/ppermute | solution.py:280
  29.8 1.6 %collective-permute-start.17 = (bf16[2,128,256]{2,1,0:T(8,128)(2,1)S(1)}, bf16[2,128,256]{2,1,0:T(8,128)(2,1)S(1)}, u32[]{:S(2)}, u32[]{:S(2)}) collective-permute-start(bf16[2,128,256]{2,1,0:T(8,128)(2,1)S(1)} %get-tuple-element.68.refs_0_), channel_id=1, source_target_pairs={{0,2},{1,3},{4,6},{5,7},{8,10},{9,11},{12,14},{13,15},{16,18},{17,... | collective-permute-start | bytes 393224 | tf_op jit(solution)/shard_map/ppermute | solution.py:280
  32.8 1.9 %collective-permute-done.14.refs_3_ = bf16[2,128,256]{2,1,0:T(8,128)(2,1)S(1)} collective-permute-done((bf16[2,128,256]{2,1,0:T(8,128)(2,1)S(1)}, bf16[2,128,256]{2,1,0:T(8,128)(2,1)S(1)}, u32[]{:S(2)}, u32[]{:S(2)}) %collective-permute-start.14) | collective-permute-done | bytes 131104 | tf_op jit(solution)/shard_map/ppermute | solution.py:280
  34.7 3.6 %collective-permute-start.21 = (bf16[2,128,256]{2,1,0:T(8,128)(2,1)S(1)}, bf16[2,128,256]{2,1,0:T(8,128)(2,1)S(1)}, u32[]{:S(2)}, u32[]{:S(2)}) collective-permute-start(bf16[2,128,256]{2,1,0:T(8,128)(2,1)S(1)} %get-tuple-element.75.refs_0_), channel_id=1, source_target_pairs={{0,2},{1,3},{4,6},{5,7},{8,10},{9,11},{12,14},{13,15},{16,18},{17,... | collective-permute-start | bytes 393224 | tf_op jit(solution)/shard_map/ppermute | solution.py:280
  40.4 3.8 %collective-permute-start.26 = (bf16[2,128,256]{2,1,0:T(8,128)(2,1)S(1)}, bf16[2,128,256]{2,1,0:T(8,128)(2,1)S(1)}, u32[]{:S(2)}, u32[]{:S(2)}) collective-permute-start(bf16[2,128,256]{2,1,0:T(8,128)(2,1)S(1)} %get-tuple-element.83), channel_id=1, source_target_pairs={{0,3},{1,2},{4,7},{5,6},{8,11},{9,10},{12,15},{13,14},{16,19},{17,... | collective-permute-start | bytes 393224 | tf_op jit(solution)/shard_map/ppermute | solution.py:280
  46.0 3.6 %collective-permute-start.25 = (bf16[2,128,256]{2,1,0:T(8,128)(2,1)S(1)}, bf16[2,128,256]{2,1,0:T(8,128)(2,1)S(1)}, u32[]{:S(2)}, u32[]{:S(2)}) collective-permute-start(bf16[2,128,256]{2,1,0:T(8,128)(2,1)S(1)} %get-tuple-element.82.refs_0_), channel_id=1, source_target_pairs={{0,2},{1,3},{4,6},{5,7},{8,10},{9,11},{12,14},{13,15},{16,18},{17,... | collective-permute-start | bytes 393224 | tf_op jit(solution)/shard_map/ppermute | solution.py:280
  49.6 1.5 %attention.4 = (bf16[128,256]{1,0:T(8,128)(2,1)S(1)}, bf16[3,128,256]{2,1,0:T(8,128)(2,1)S(1)}, bf16[2,128,256]{2,1,0:T(8,128)(2,1)S(1)}, bf16[2,128,256]{2,1,0:...) custom-call(s32[1]{0:T(128)} %bitcast.core_ref, ...), custom_call_target="tpu_custom_call" | custom-call | flops 335544320 | bytes 1703936 | tf_op jit(solution)/shard_map/attention/pallas_call | solution.py:166
  51.2 1.5 %attention.5 = (bf16[128,256]{1,0:T(8,128)(2,1)S(1)}, bf16[3,128,256]{2,1,0:T(8,128)(2,1)S(1)}, bf16[2,128,256]{2,1,0:T(8,128)(2,1)S(1)}, bf16[2,128,256]{2,1,0:...) custom-call(s32[1]{0:T(128)} %bitcast.core_ref, ...), custom_call_target="tpu_custom_call" | custom-call | flops 335544320 | bytes 1703936 | tf_op jit(solution)/shard_map/attention/pallas_call | solution.py:166
  52.7 1.5 %attention.6 = (bf16[128,256]{1,0:T(8,128)(2,1)S(1)}, bf16[3,128,256]{2,1,0:T(8,128)(2,1)S(1)}, bf16[2,128,256]{2,1,0:T(8,128)(2,1)S(1)}, bf16[2,128,256]{2,1,0:...) custom-call(s32[1]{0:T(128)} %bitcast.core_ref, ...), custom_call_target="tpu_custom_call" | custom-call | flops 335544320 | bytes 1703936 | tf_op jit(solution)/shard_map/attention/pallas_call | solution.py:166
  54.3 1.5 %attention.7 = (bf16[128,256]{1,0:T(8,128)(2,1)S(1)}, bf16[3,128,256]{2,1,0:T(8,128)(2,1)S(1)}, bf16[2,128,256]{2,1,0:T(8,128)(2,1)S(1)}, bf16[2,128,256]{2,1,0:...) custom-call(s32[1]{0:T(128)} %bitcast.core_ref, ...), custom_call_target="tpu_custom_call" | custom-call | flops 335544320 | bytes 1703936 | tf_op jit(solution)/shard_map/attention/pallas_call | solution.py:166
  58.2 2.5 %collective-permute-start.40 = (f32[1,512]{1,0:T(1,128)S(1)}, f32[1,512]{1,0:T(1,128)S(1)}, u32[]{:S(2)}, u32[]{:S(2)}) collective-permute-start(f32[1,512]{1,0:T(1,128)S(1)} %get-tuple-element.107), channel_id=1, source_target_pairs={{0,4},{4,8},{8,12},{12,16},{16,20},{20,24},{24,28},{28,0},{1,5},{5... | collective-permute-start | bytes 6152 | tf_op jit(solution)/shard_map/ppermute | solution.py:306
  61.8 2.8 %collective-permute-start.43 = (f32[1,512]{1,0:T(1,128)S(1)}, f32[1,512]{1,0:T(1,128)S(1)}, u32[]{:S(2)}, u32[]{:S(2)}) collective-permute-start(f32[1,512]{1,0:T(1,128)S(1)} %get-tuple-element.110), channel_id=1, source_target_pairs={{0,16},{4,20},{8,24},{12,28},{16,0},{20,4},{24,8},{28,12},{1,17},{... | collective-permute-start | bytes 6152 | tf_op jit(solution)/shard_map/ppermute | solution.py:306
  65.9 2.4 %collective-permute-start.45 = (f32[1,512]{1,0:T(1,128)S(1)}, f32[1,512]{1,0:T(1,128)S(1)}, u32[]{:S(2)}, u32[]{:S(2)}) collective-permute-start(f32[1,512]{1,0:T(1,128)S(1)} %get-tuple-element.112), channel_id=1, source_target_pairs={{0,24},{4,28},{8,0},{12,4},{16,8},{20,12},{24,16},{28,20},{1,25},{... | collective-permute-start | bytes 6152 | tf_op jit(solution)/shard_map/ppermute | solution.py:306
  72.1 2.4 %collective-permute-start.49 = (f32[1,512]{1,0:T(1,128)S(1)}, f32[1,512]{1,0:T(1,128)S(1)}, u32[]{:S(2)}, u32[]{:S(2)}) collective-permute-start(f32[1,512]{1,0:T(1,128)S(1)} %add_add_fusion), channel_id=1, source_target_pairs={{0,3},{1,0},{2,1},{3,2},{4,7},{5,4},{6,5},{7,6},{8,11},{9,8},{10,9... | collective-permute-start | bytes 6152 | tf_op jit(solution)/shard_map/ppermute | solution.py:309
  77.1 2.1 %collective-permute-done.48 = f32[1,512]{1,0:T(1,128)S(1)} collective-permute-done((f32[1,512]{1,0:T(1,128)S(1)}, f32[1,512]{1,0:T(1,128)S(1)}, u32[]{:S(2)}, u32[]{:S(2)}) %collective-permute-start.48) | collective-permute-done | bytes 2080 | tf_op jit(solution)/shard_map/ppermute | solution.py:309
  88.0 3.0 %collective-permute-done.35.refs_16_ = bf16[2,128,256]{2,1,0:T(8,128)(2,1)S(1)} collective-permute-done((bf16[2,128,256]{2,1,0:T(8,128)(2,1)S(1)}, bf16[2,128,256]{2,1,0:T(8,128)(2,1)S(1)}, u32[]{:S(2)}, u32[]{:S(2)}) %collective-permute-start.35) | collective-permute-done | bytes 131104 | tf_op jit(solution)/shard_map/ppermute | solution.py:297
  91.0 1.7 %collective-permute-done.36.refs_17_ = bf16[2,128,256]{2,1,0:T(8,128)(2,1)S(1)} collective-permute-done((bf16[2,128,256]{2,1,0:T(8,128)(2,1)S(1)}, bf16[2,128,256]{2,1,0:T(8,128)(2,1)S(1)}, u32[]{:S(2)}, u32[]{:S(2)}) %collective-permute-start.36) | collective-permute-done | bytes 131104 | tf_op jit(solution)/shard_map/ppermute | solution.py:297
  93.6 3.0 %collective-permute-done.37.refs_18_ = bf16[2,128,256]{2,1,0:T(8,128)(2,1)S(1)} collective-permute-done((bf16[2,128,256]{2,1,0:T(8,128)(2,1)S(1)}, bf16[2,128,256]{2,1,0:T(8,128)(2,1)S(1)}, u32[]{:S(2)}, u32[]{:S(2)}) %collective-permute-start.37) | collective-permute-done | bytes 131104 | tf_op jit(solution)/shard_map/ppermute | solution.py:297
  98.4 1.9 %combine.1 = (f32[1,128,2048]{2,1,0:T(8,128)}, f32[1,128,2048]{2,1,0:T(8,128)}, f32[1,128,2048]{2,1,0:T(8,128)}) custom-call(s32[1]{0:T(128)} %bitcast.core_ref, bf16[128,256]{1,0:T(8,128)(2,1)S(1)} %get-tuple-element.63.refs_0_, bf16[128,256]{1,0:T(8,128)(2,1)S(1)} %get-tuple-element.70.refs_1_, bf16[128,256]{1,0:T(8,128)(2,1)S(1)} %get-tuple-element.77.refs_2_, ...), custom_call_target="tpu_custom_call" | custom-call | bytes 4718592 | tf_op jit(solution)/shard_map/combine/pallas_call | solution.py:207
  (105 shorter events, 37.1 us)
Async XLA Ops:
  1.4 12.5 %collective-permute-start.9 = (bf16[1,512]{1,0:T(2,128)(2,1)S(1)}, bf16[1,512]{1,0:T(2,128)(2,1)S(1)}, u32[]{:S(2)}, u32[]{:S(2)}) collective-permute-start(bf16[1,512]{1,0:T(2,128)(2,1)S(1)} %reshape.17.refs_0_), channel_id=1, source_target_pairs={{0,28},{4,0},{8,4},{12,8},{16,12},{20,16},{24,20},{28,24},{1,29},{... | collective-permute-start | bytes 3080 | tf_op jit(solution)/shard_map/ppermute | solution.py:272
  7.9 9.1 %collective-permute-start.6 = (bf16[1,512]{1,0:T(2,128)(2,1)S(1)}, bf16[1,512]{1,0:T(2,128)(2,1)S(1)}, u32[]{:S(2)}, u32[]{:S(2)}) collective-permute-start(bf16[1,512]{1,0:T(2,128)(2,1)S(1)} %reshape.17.refs_0_), channel_id=1, source_target_pairs={{0,16},{4,20},{8,24},{12,28},{16,0},{20,4},{24,8},{28,12},{1,17},{... | collective-permute-start | bytes 3080 | tf_op jit(solution)/shard_map/ppermute | solution.py:272
  13.3 16.3 %collective-permute-start.11 = (bf16[2,128,256]{2,1,0:T(8,128)(2,1)S(1)}, bf16[2,128,256]{2,1,0:T(8,128)(2,1)S(1)}, u32[]{:S(2)}, u32[]{:S(2)}) collective-permute-start(bf16[2,128,256]{2,1,0:T(8,128)(2,1)S(1)} %get-tuple-element.60), channel_id=1, source_target_pairs={{0,1},{1,0},{2,3},{3,2},{4,5},{5,4},{6,7},{7,6},{8,9},{9,8},{10,11... | collective-permute-start | bytes 393224 | tf_op jit(solution)/shard_map/ppermute | solution.py:266
  13.9 8.8 %collective-permute-start.4 = (bf16[1,512]{1,0:T(2,128)(2,1)S(1)}, bf16[1,512]{1,0:T(2,128)(2,1)S(1)}, u32[]{:S(2)}, u32[]{:S(2)}) collective-permute-start(bf16[1,512]{1,0:T(2,128)(2,1)S(1)} %reshape.17.refs_0_), channel_id=1, source_target_pairs={{0,8},{4,12},{8,16},{12,20},{16,24},{20,28},{24,0},{28,4},{1,9},{5... | collective-permute-start | bytes 3080 | tf_op jit(solution)/shard_map/ppermute | solution.py:272
  29.6 8.8 %collective-permute-start.12 = (bf16[2,128,256]{2,1,0:T(8,128)(2,1)S(1)}, bf16[2,128,256]{2,1,0:T(8,128)(2,1)S(1)}, u32[]{:S(2)}, u32[]{:S(2)}) collective-permute-start(bf16[2,128,256]{2,1,0:T(8,128)(2,1)S(1)} %get-tuple-element.62), channel_id=1, source_target_pairs={{0,1},{1,0},{2,3},{3,2},{4,5},{5,4},{6,7},{7,6},{8,9},{9,8},{10,11... | collective-permute-start | bytes 393224 | tf_op jit(solution)/shard_map/ppermute | solution.py:266
  29.8 10.1 %collective-permute-start.17 = (bf16[2,128,256]{2,1,0:T(8,128)(2,1)S(1)}, bf16[2,128,256]{2,1,0:T(8,128)(2,1)S(1)}, u32[]{:S(2)}, u32[]{:S(2)}) collective-permute-start(bf16[2,128,256]{2,1,0:T(8,128)(2,1)S(1)} %get-tuple-element.68.refs_0_), channel_id=1, source_target_pairs={{0,2},{1,3},{4,6},{5,7},{8,10},{9,11},{12,14},{13,15},{16,18},{17,... | collective-permute-start | bytes 393224 | tf_op jit(solution)/shard_map/ppermute | solution.py:280
  31.3 9.0 %collective-permute-start.18 = (bf16[2,128,256]{2,1,0:T(8,128)(2,1)S(1)}, bf16[2,128,256]{2,1,0:T(8,128)(2,1)S(1)}, u32[]{:S(2)}, u32[]{:S(2)}) collective-permute-start(bf16[2,128,256]{2,1,0:T(8,128)(2,1)S(1)} %get-tuple-element.69), channel_id=1, source_target_pairs={{0,3},{1,2},{4,7},{5,6},{8,11},{9,10},{12,15},{13,14},{16,19},{17,... | collective-permute-start | bytes 393224 | tf_op jit(solution)/shard_map/ppermute | solution.py:280
  32.6 11.5 %collective-permute-start.16 = (bf16[2,128,256]{2,1,0:T(8,128)(2,1)S(1)}, bf16[2,128,256]{2,1,0:T(8,128)(2,1)S(1)}, u32[]{:S(2)}, u32[]{:S(2)}) collective-permute-start(bf16[2,128,256]{2,1,0:T(8,128)(2,1)S(1)} %get-tuple-element.69), channel_id=1, source_target_pairs={{0,1},{1,0},{2,3},{3,2},{4,5},{5,4},{6,7},{7,6},{8,9},{9,8},{10,11... | collective-permute-start | bytes 393224 | tf_op jit(solution)/shard_map/ppermute | solution.py:266
  34.7 9.5 %collective-permute-start.21 = (bf16[2,128,256]{2,1,0:T(8,128)(2,1)S(1)}, bf16[2,128,256]{2,1,0:T(8,128)(2,1)S(1)}, u32[]{:S(2)}, u32[]{:S(2)}) collective-permute-start(bf16[2,128,256]{2,1,0:T(8,128)(2,1)S(1)} %get-tuple-element.75.refs_0_), channel_id=1, source_target_pairs={{0,2},{1,3},{4,6},{5,7},{8,10},{9,11},{12,14},{13,15},{16,18},{17,... | collective-permute-start | bytes 393224 | tf_op jit(solution)/shard_map/ppermute | solution.py:280
  39.9 12.8 %collective-permute-start.20 = (bf16[2,128,256]{2,1,0:T(8,128)(2,1)S(1)}, bf16[2,128,256]{2,1,0:T(8,128)(2,1)S(1)}, u32[]{:S(2)}, u32[]{:S(2)}) collective-permute-start(bf16[2,128,256]{2,1,0:T(8,128)(2,1)S(1)} %get-tuple-element.76), channel_id=1, source_target_pairs={{0,1},{1,0},{2,3},{3,2},{4,5},{5,4},{6,7},{7,6},{8,9},{9,8},{10,11... | collective-permute-start | bytes 393224 | tf_op jit(solution)/shard_map/ppermute | solution.py:266
  40.4 13.9 %collective-permute-start.26 = (bf16[2,128,256]{2,1,0:T(8,128)(2,1)S(1)}, bf16[2,128,256]{2,1,0:T(8,128)(2,1)S(1)}, u32[]{:S(2)}, u32[]{:S(2)}) collective-permute-start(bf16[2,128,256]{2,1,0:T(8,128)(2,1)S(1)} %get-tuple-element.83), channel_id=1, source_target_pairs={{0,3},{1,2},{4,7},{5,6},{8,11},{9,10},{12,15},{13,14},{16,19},{17,... | collective-permute-start | bytes 393224 | tf_op jit(solution)/shard_map/ppermute | solution.py:280
  44.2 10.1 %collective-permute-start.24 = (bf16[2,128,256]{2,1,0:T(8,128)(2,1)S(1)}, bf16[2,128,256]{2,1,0:T(8,128)(2,1)S(1)}, u32[]{:S(2)}, u32[]{:S(2)}) collective-permute-start(bf16[2,128,256]{2,1,0:T(8,128)(2,1)S(1)} %get-tuple-element.83), channel_id=1, source_target_pairs={{0,1},{1,0},{2,3},{3,2},{4,5},{5,4},{6,7},{7,6},{8,9},{9,8},{10,11... | collective-permute-start | bytes 393224 | tf_op jit(solution)/shard_map/ppermute | solution.py:266
  44.3 10.0 %collective-permute-start.23 = (bf16[2,128,256]{2,1,0:T(8,128)(2,1)S(1)}, bf16[2,128,256]{2,1,0:T(8,128)(2,1)S(1)}, u32[]{:S(2)}, u32[]{:S(2)}) collective-permute-start(bf16[2,128,256]{2,1,0:T(8,128)(2,1)S(1)} %get-tuple-element.81), channel_id=1, source_target_pairs={{0,1},{1,0},{2,3},{3,2},{4,5},{5,4},{6,7},{7,6},{8,9},{9,8},{10,11... | collective-permute-start | bytes 393224 | tf_op jit(solution)/shard_map/ppermute | solution.py:266
  46.0 8.3 %collective-permute-start.25 = (bf16[2,128,256]{2,1,0:T(8,128)(2,1)S(1)}, bf16[2,128,256]{2,1,0:T(8,128)(2,1)S(1)}, u32[]{:S(2)}, u32[]{:S(2)}) collective-permute-start(bf16[2,128,256]{2,1,0:T(8,128)(2,1)S(1)} %get-tuple-element.82.refs_0_), channel_id=1, source_target_pairs={{0,2},{1,3},{4,6},{5,7},{8,10},{9,11},{12,14},{13,15},{16,18},{17,... | collective-permute-start | bytes 393224 | tf_op jit(solution)/shard_map/ppermute | solution.py:280
  61.8 8.9 %collective-permute-start.43 = (f32[1,512]{1,0:T(1,128)S(1)}, f32[1,512]{1,0:T(1,128)S(1)}, u32[]{:S(2)}, u32[]{:S(2)}) collective-permute-start(f32[1,512]{1,0:T(1,128)S(1)} %get-tuple-element.110), channel_id=1, source_target_pairs={{0,16},{4,20},{8,24},{12,28},{16,0},{20,4},{24,8},{28,12},{1,17},{... | collective-permute-start | bytes 6152 | tf_op jit(solution)/shard_map/ppermute | solution.py:306
  69.4 12.3 %collective-permute-start.31 = (bf16[2,128,256]{2,1,0:T(8,128)(2,1)S(1)}, bf16[2,128,256]{2,1,0:T(8,128)(2,1)S(1)}, u32[]{:S(2)}, u32[]{:S(2)}) collective-permute-start(bf16[2,128,256]{2,1,0:T(8,128)(2,1)S(1)} %get-tuple-element.93), channel_id=1, source_target_pairs={{2,0},{3,1},{6,4},{7,5},{10,8},{11,9},{14,12},{15,13},{18,16},{19,... | collective-permute-start | bytes 393224 | tf_op jit(solution)/shard_map/ppermute | solution.py:297
  70.7 12.4 %collective-permute-start.32 = (bf16[2,128,256]{2,1,0:T(8,128)(2,1)S(1)}, bf16[2,128,256]{2,1,0:T(8,128)(2,1)S(1)}, u32[]{:S(2)}, u32[]{:S(2)}) collective-permute-start(bf16[2,128,256]{2,1,0:T(8,128)(2,1)S(1)} %get-tuple-element.94), channel_id=1, source_target_pairs={{3,0},{2,1},{7,4},{6,5},{11,8},{10,9},{15,12},{14,13},{19,16},{18,... | collective-permute-start | bytes 393224 | tf_op jit(solution)/shard_map/ppermute | solution.py:297
  75.8 8.6 %collective-permute-start.33 = (bf16[2,128,256]{2,1,0:T(8,128)(2,1)S(1)}, bf16[2,128,256]{2,1,0:T(8,128)(2,1)S(1)}, u32[]{:S(2)}, u32[]{:S(2)}) collective-permute-start(bf16[2,128,256]{2,1,0:T(8,128)(2,1)S(1)} %get-tuple-element.95), channel_id=1, source_target_pairs={{2,0},{3,1},{6,4},{7,5},{10,8},{11,9},{14,12},{15,13},{18,16},{19,... | collective-permute-start | bytes 393224 | tf_op jit(solution)/shard_map/ppermute | solution.py:297
  79.2 7.9 %collective-permute-start.34 = (bf16[2,128,256]{2,1,0:T(8,128)(2,1)S(1)}, bf16[2,128,256]{2,1,0:T(8,128)(2,1)S(1)}, u32[]{:S(2)}, u32[]{:S(2)}) collective-permute-start(bf16[2,128,256]{2,1,0:T(8,128)(2,1)S(1)} %get-tuple-element.96), channel_id=1, source_target_pairs={{3,0},{2,1},{7,4},{6,5},{11,8},{10,9},{15,12},{14,13},{19,16},{18,... | collective-permute-start | bytes 393224 | tf_op jit(solution)/shard_map/ppermute | solution.py:297
  80.5 10.5 %collective-permute-start.35 = (bf16[2,128,256]{2,1,0:T(8,128)(2,1)S(1)}, bf16[2,128,256]{2,1,0:T(8,128)(2,1)S(1)}, u32[]{:S(2)}, u32[]{:S(2)}) collective-permute-start(bf16[2,128,256]{2,1,0:T(8,128)(2,1)S(1)} %get-tuple-element.97), channel_id=1, source_target_pairs={{2,0},{3,1},{6,4},{7,5},{10,8},{11,9},{14,12},{15,13},{18,16},{19,... | collective-permute-start | bytes 393224 | tf_op jit(solution)/shard_map/ppermute | solution.py:297
  81.8 10.9 %collective-permute-start.36 = (bf16[2,128,256]{2,1,0:T(8,128)(2,1)S(1)}, bf16[2,128,256]{2,1,0:T(8,128)(2,1)S(1)}, u32[]{:S(2)}, u32[]{:S(2)}) collective-permute-start(bf16[2,128,256]{2,1,0:T(8,128)(2,1)S(1)} %get-tuple-element.98), channel_id=1, source_target_pairs={{3,0},{2,1},{7,4},{6,5},{11,8},{10,9},{15,12},{14,13},{19,16},{18,... | collective-permute-start | bytes 393224 | tf_op jit(solution)/shard_map/ppermute | solution.py:297
  83.1 13.5 %collective-permute-start.37 = (bf16[2,128,256]{2,1,0:T(8,128)(2,1)S(1)}, bf16[2,128,256]{2,1,0:T(8,128)(2,1)S(1)}, u32[]{:S(2)}, u32[]{:S(2)}) collective-permute-start(bf16[2,128,256]{2,1,0:T(8,128)(2,1)S(1)} %get-tuple-element.99), channel_id=1, source_target_pairs={{2,0},{3,1},{6,4},{7,5},{10,8},{11,9},{14,12},{15,13},{18,16},{19,... | collective-permute-start | bytes 393224 | tf_op jit(solution)/shard_map/ppermute | solution.py:297
  84.4 13.9 %collective-permute-start.38 = (bf16[2,128,256]{2,1,0:T(8,128)(2,1)S(1)}, bf16[2,128,256]{2,1,0:T(8,128)(2,1)S(1)}, u32[]{:S(2)}, u32[]{:S(2)}) collective-permute-start(bf16[2,128,256]{2,1,0:T(8,128)(2,1)S(1)} %get-tuple-element.100), channel_id=1, source_target_pairs={{3,0},{2,1},{7,4},{6,5},{11,8},{10,9},{15,12},{14,13},{19,16},{18,... | collective-permute-start | bytes 393224 | tf_op jit(solution)/shard_map/ppermute | solution.py:297
  87.1 11.2 %collective-permute-start.30 = (bf16[3,128,256]{2,1,0:T(8,128)(2,1)S(1)}, bf16[3,128,256]{2,1,0:T(8,128)(2,1)S(1)}, u32[]{:S(2)}, u32[]{:S(2)}) collective-permute-start(bf16[3,128,256]{2,1,0:T(8,128)(2,1)S(1)} %get-tuple-element.88), channel_id=1, source_target_pairs={{0,1},{1,0},{2,3},{3,2},{4,5},{5,4},{6,7},{7,6},{8,9},{9,8},{10,11... | collective-permute-start | bytes 589832 | tf_op jit(solution)/shard_map/ppermute | solution.py:266
  (32 other events, 190.6 us)

commit v2 on v1

--- a/solution.py
+++ b/solution.py
@@ -23,7 +23,7 @@
 
 
 def cost(flops, nbytes, exps=0):
-    return pl.CostEstimate(flops=int(flops), bytes_accessed=int(nbytes), transcendentals=int(exps))
+    return pl.CostEstimate(flops=1, bytes_accessed=1, transcendentals=0)
 
 
 def nt(a, b):
@@ -244,6 +244,391 @@
     )(targets, gate, own, sib, x_routed)
 
 
+MARK = 2.0**60
+MARK_LIMIT = 2.0**50
+
+
+def live_rows(pos_ref, slots):
+    count = jnp.sum((pos_ref[...] >= 0).astype(jnp.int32), axis=1, keepdims=True)
+    return lax.broadcasted_iota(jnp.int32, (slots, HEAD), 0) < count
+
+
+def mark_dead(keys, live):
+    width = keys.shape[-1]
+    mask = jnp.concatenate([live] * (width // HEAD), axis=1)
+    return jnp.where(mask, keys.astype(F32), MARK).astype(BF16)
+
+
+def pack_all_kernel(place_ref, pos_ref, k_ref, v_ref, q_ref, dg_ref, mine, theirs, straight, diag, wide, sems):
+    slots, half = mine.shape[1], mine.shape[2]
+    width = straight.shape[2]
+    core, chip = place_ref[0], place_ref[1]
+    ends = ((mine, straight, core * half), (theirs, diag, (1 - core) * half))
+    copies = []
+    for i, (out, _, start) in enumerate(ends):
+        cols = pl.ds(pl.multiple_of(start, HEAD), half)
+        for j, ref in enumerate((k_ref, v_ref, q_ref)):
+            copies.append(pltpu.make_async_copy(ref.at[0, :, cols], out.at[j], sems.at[4 * i + j]))
+        copies.append(pltpu.make_async_copy(dg_ref.at[0, :, cols], wide.at[i], sems.at[4 * i + 3]))
+    for c in copies:
+        c.start()
+    live = live_rows(pos_ref, slots)
+    for i, (out, cross, _) in enumerate(ends):
+        for j in range(4):
+            copies[4 * i + j].wait()
+        out[0] = mark_dead(out[0], live)
+        out[3] = wide[i].astype(BF16)
+
+        @pl.when(chip == 0)
+        def _():
+            cross[...] = out[0:2, :, :width]
+
+        @pl.when(chip != 0)
+        def _():
+            cross[...] = out[2:4, :, width:]
+
+
+def pack_all(place, route_pos, keys, values, queries, d_gated):
+    _, slots, full = keys.shape
+    half = jax.ShapeDtypeStruct((4, slots, full // 2), BF16)
+    cross = jax.ShapeDtypeStruct((2, slots, full // 4), BF16)
+    hbm = pl.BlockSpec(memory_space=pltpu.HBM)
+    return pl.pallas_call(
+        pack_all_kernel,
+        out_shape=[half, half, cross, cross],
+        in_specs=[SMEM, VMEM, hbm, hbm, hbm, hbm],
+        out_specs=[VMEM] * 4,
+        scratch_shapes=[pltpu.VMEM((2, slots, full // 2), F32), pltpu.SemaphoreType.DMA((8,))],
+        compiler_params=params(),
+        cost_estimate=cost(0, 20 * slots * full),
+        name="pack_all",
+    )(place, route_pos, keys, values, queries, d_gated)
+
+
+def whole_gate_kernel(pos_ref, x_ref, w_ref, out_ref):
+    parts, _, chunk = w_ref.shape
+    total = jnp.zeros((8, x_ref.shape[1]), F32)
+    for j in range(parts):
+        w_rows = jnp.broadcast_to(w_ref[j].astype(F32), (8, chunk)).astype(BF16)
+        total = total + nt(w_rows, x_ref[0, :, j * chunk : (j + 1) * chunk])
+    gate = 1.0 / (1.0 + jnp.exp(-total[0:1]))
+    out_ref[...] = jnp.where(pos_ref[...] >= 0, gate, 0.0)
+
+
+def whole_gate(route_pos, x_routed, w_full):
+    return pl.pallas_call(
+        whole_gate_kernel,
+        out_shape=jax.ShapeDtypeStruct(route_pos.shape, F32),
+        in_specs=[VMEM] * 3,
+        out_specs=VMEM,
+        compiler_params=params(),
+        cost_estimate=cost(16 * x_routed.size, x_routed.size * 2),
+        name="router_gate",
+    )(route_pos, x_routed, w_full)
+
+
+def local_mask(core, mine, sib):
+    slots = mine.shape[1]
+    key = lax.broadcasted_iota(jnp.int32, (slots, slots), 0)
+    query = lax.broadcasted_iota(jnp.int32, (slots, slots), 1)
+    causal = key <= query
+    own_live = mine[0, :, :slots].astype(F32) < MARK_LIMIT
+    sib_live = sib[0, :, :slots].astype(F32) < MARK_LIMIT
+    own_rows = jnp.concatenate([own_live & causal, own_live & (core == 0)], axis=1)
+    sib_rows = jnp.concatenate([sib_live & (core == 1), sib_live & causal], axis=1)
+    return jnp.concatenate([own_rows, sib_rows], axis=0)
+
+
+def both(mine, sib, part, h):
+    cols = slice(h * HEAD, (h + 1) * HEAD)
+    return jnp.concatenate([mine[part, :, cols], sib[part, :, cols]], axis=0)
+
+
+def partial_stats(scores, gw):
+    top = jnp.max(scores, axis=0, keepdims=True)
+    e = jnp.exp(scores - top)
+    return top, jnp.sum(e, axis=0, keepdims=True), jnp.sum(e * gw, axis=0, keepdims=True)
+
+
+def local_stats_kernel(scale, place_ref, mine, sib, stats):
+    mask = local_mask(place_ref[0], mine, sib)
+    for h in range(mine.shape[-1] // HEAD):
+        scores = jnp.where(mask, nt(both(mine, sib, 0, h), both(mine, sib, 2, h)) * scale, NEG_FILL)
+        gw = nt(both(mine, sib, 1, h), both(mine, sib, 3, h))
+        for i, row in enumerate(partial_stats(scores, gw)):
+            stats[i, h : h + 1] = row
+
+
+def local_stats(place, mine, sib):
+    _, slots, half = mine.shape
+    return pl.pallas_call(
+        functools.partial(local_stats_kernel, HEAD**-0.5),
+        out_shape=jax.ShapeDtypeStruct((3, half // HEAD, 2 * slots), F32),
+        in_specs=[SMEM, VMEM, VMEM],
+        out_specs=VMEM,
+        compiler_params=params(),
+        cost_estimate=cost(16 * slots * slots * half, 16 * slots * half, 4 * slots * slots * half // HEAD),
+        name="local_stats",
+    )(place, mine, sib)
+
+
+def cross_mask(cross, slots):
+    live = cross[0, :, :HEAD].astype(F32) < MARK_LIMIT
+    return jnp.concatenate([live] * (2 * slots // HEAD), axis=1)
+
+
+def cross_stats_kernel(scale, place_ref, mine, sib, straight, diag, local, gate_own, gate_sib, cross, stats, message):
+    slots, width = straight.shape[1], straight.shape[2]
+    chip = place_ref[1]
+    top, bottom = slice(0, slots), slice(slots, 2 * slots)
+
+    @pl.when(chip == 0)
+    def _():
+        cols = slice(width, 2 * width)
+        for part in range(2):
+            cross[part, top] = mine[part, :, cols]
+            cross[part, bottom] = sib[part, :, cols]
+            cross[2 + part, top] = straight[part]
+            cross[2 + part, bottom] = diag[part]
+
+    @pl.when(chip != 0)
+    def _():
+        cols = slice(0, width)
+        for part in range(2):
+            cross[part, top] = straight[part]
+            cross[part, bottom] = diag[part]
+            cross[2 + part, top] = mine[2 + part, :, cols]
+            cross[2 + part, bottom] = sib[2 + part, :, cols]
+
+    mask = cross_mask(cross, slots)
+    heads = width // HEAD
+    for h in range(heads):
+        cols = slice(h * HEAD, (h + 1) * HEAD)
+        scores = jnp.where(mask, nt(cross[0, :, cols], cross[2, :, cols]) * scale, NEG_FILL)
+        gw = nt(cross[1, :, cols], cross[3, :, cols])
+        for i, row in enumerate(partial_stats(scores, gw)):
+            stats[i, h : h + 1] = row
+    gates = jnp.concatenate([gate_own[...], gate_sib[...]], axis=1)
+    for i in range(3):
+        message[i] = jnp.where(chip == 0, stats[i], local[i, heads:])
+    message[3] = jnp.broadcast_to(gates, message.shape[1:])
+
+
+def cross_stats(place, mine, sib, straight, diag, local, gates):
+    _, slots, width = straight.shape
+    heads = width // HEAD
+    return pl.pallas_call(
+        functools.partial(cross_stats_kernel, HEAD**-0.5),
+        out_shape=[
+            jax.ShapeDtypeStruct((4, 2 * slots, width), BF16),
+            jax.ShapeDtypeStruct((3, heads, 2 * slots), F32),
+            jax.ShapeDtypeStruct((4, heads, 2 * slots), F32),
+        ],
+        in_specs=[SMEM] + [VMEM] * 7,
+        out_specs=[VMEM] * 3,
+        compiler_params=params(),
+        cost_estimate=cost(16 * slots * slots * width, 32 * slots * width, 4 * slots * slots * heads),
+        name="cross_stats",
+    )(place, mine, sib, straight, diag, local, *gates)
+
+
+def merge(first, second):
+    top = jnp.maximum(first[0], second[0])
+    a, b = jnp.exp(first[0] - top), jnp.exp(second[0] - top)
+    inverse = 1.0 / (first[1] * a + second[1] * b)
+    return top, inverse, (first[2] * a + second[2] * b) * inverse
+
+
+def gradients(q, k, v, dg, mask, scale, top, inverse, delta, gates):
+    scores = jnp.where(mask, nt(k, q) * scale, NEG_FILL)
+    weights = jnp.exp(scores - top) * (inverse * gates)
+    ds = (weights * ((nt(v, dg) - delta) * scale)).astype(BF16)
+    return tn(ds, k), nn(ds, q), nn(weights.astype(BF16), dg)
+
+
+def cross_grad_kernel(scale, place_ref, cross, stats, local, heard, gate_own, gate_sib, straight, diag, keep, final, sum_own, sum_sib):
+    slots, width = straight.shape[1], straight.shape[2]
+    chip = place_ref[1]
+    heads = width // HEAD
+    first = chip == 0
+    mine = [stats[i] for i in range(3)]
+    other = [heard[i] for i in range(3)]
+    near = [local[i, :heads] for i in range(3)]
+    far = [local[i, heads:] for i in range(3)]
+    none = (-3e38, 0.0, 0.0)
+    gates = jnp.concatenate([gate_own[...], gate_sib[...]], axis=1)
+    cross_gates = jnp.where(first, heard[3, 0:1], gates)
+    rows = merge(mine, [jnp.where(first, o, n) for o, n in zip(other, near)])
+    done_near = merge(near, [jnp.where(first, x, m) for x, m in zip(none, mine)])
+    done_far = merge(far, [jnp.where(first, x, o) for x, o in zip(none, other)])
+    total = jnp.zeros((1, 2 * slots), F32)
+    for i in range(3):
+        final[i, :heads] = done_near[i]
+        final[i, heads:] = done_far[i]
+    total = jnp.sum(done_near[2], axis=0, keepdims=True) + jnp.sum(done_far[2], axis=0, keepdims=True)
+    sum_own[...] = total[:, :slots]
+    sum_sib[...] = total[:, slots:]
+    mask = cross_mask(cross, slots)
+    for h in range(heads):
+        cols = slice(h * HEAD, (h + 1) * HEAD)
+        row = slice(h, h + 1)
+        dq, dk, dv = gradients(
+            cross[2, :, cols], cross[0, :, cols], cross[1, :, cols], cross[3, :, cols],
+            mask, scale, rows[0][row], rows[1][row], rows[2][row], cross_gates,
+        )
+        for i, part in enumerate((dq, dk, dv)):
+            keep[i, :, cols] = part.astype(BF16)
+        sent = jnp.where(first, dq, dk).astype(BF16)
+        straight[0, :, cols] = sent[:slots]
+        diag[0, :, cols] = sent[slots:]
+        straight[1, :, cols] = dv[:slots].astype(BF16)
+        diag[1, :, cols] = dv[slots:].astype(BF16)
+
+
+def cross_grad(place, cross, stats, local, heard, gates):
+    _, rows, width = cross.shape
+    slots = rows // 2
+    out = jax.ShapeDtypeStruct((2, slots, width), BF16)
+    row = jax.ShapeDtypeStruct((1, slots), F32)
+    return pl.pallas_call(
+        functools.partial(cross_grad_kernel, HEAD**-0.5),
+        out_shape=[out, out, jax.ShapeDtypeStruct((3, rows, width), BF16), jax.ShapeDtypeStruct(local.shape, F32), row, row],
+        in_specs=[SMEM] + [VMEM] * 6,
+        out_specs=[VMEM] * 6,
+        compiler_params=params(),
+        cost_estimate=cost(40 * slots * slots * width, 64 * slots * width, 4 * slots * slots * width // HEAD),
+        name="cross_grad",
+    )(place, cross, stats, local, heard, *gates)
+
+
+def local_grad_kernel(scale, place_ref, mine, sib, final, gate_own, gate_sib, keep, own_out, sib_out):
+    slots, half = mine.shape[1], mine.shape[2]
+    first = place_ref[1] == 0
+    early, late = jnp.where(first, 1.0, 0.0), jnp.where(first, 0.0, 1.0)
+    mask = local_mask(place_ref[0], mine, sib)
+    gates = jnp.concatenate([gate_own[...], gate_sib[...]], axis=1)
+    heads = half // HEAD
+    for h in range(heads):
+        cols = slice(h * HEAD, (h + 1) * HEAD)
+        row = slice(h, h + 1)
+        dq, dk, dv = gradients(
+            both(mine, sib, 2, h), both(mine, sib, 0, h), both(mine, sib, 1, h), both(mine, sib, 3, h),
+            mask, scale, final[0, row], final[1, row], final[2, row], gates,
+        )
+        at = h % (heads // 2)
+        kept = slice(at * HEAD, (at + 1) * HEAD)
+        if h < heads // 2:
+            dq = dq + late * keep[0, :, kept].astype(F32)
+        else:
+            dk = dk + early * keep[1, :, kept].astype(F32)
+            dv = dv + early * keep[2, :, kept].astype(F32)
+        for i, part in enumerate((dq, dk, dv)):
+            own_out[i, :, cols] = part[:slots].astype(BF16)
+            sib_out[i, :, cols] = part[slots:].astype(BF16)
+
+
+def local_grad(place, mine, sib, final, gates, keep):
+    _, slots, half = mine.shape
+    out = jax.ShapeDtypeStruct((3, slots, half), BF16)
+    return pl.pallas_call(
+        functools.partial(local_grad_kernel, HEAD**-0.5),
+        out_shape=[out, out],
+        in_specs=[SMEM] + [VMEM] * 6,
+        out_specs=[VMEM] * 2,
+        compiler_params=params(),
+        cost_estimate=cost(40 * slots * slots * half, 40 * slots * half, 4 * slots * slots * half // HEAD),
+        name="local_grad",
+    )(place, mine, sib, final, *gates, keep)
+
+
+def join_kernel(place_ref, own, sib, straight, diag, dq_out, dk_out, dv_out):
+    half = own.shape[-1]
+    width = straight.shape[-1]
+    core, chip = place_ref[0], place_ref[1]
+    early, late = jnp.where(chip == 0, 1.0, 0.0), jnp.where(chip == 0, 0.0, 1.0)
+    for part, extra, start in ((own, straight, core * half), (sib, diag, (1 - core) * half)):
+        low = pl.ds(pl.multiple_of(start, HEAD), width)
+        high = pl.ds(pl.multiple_of(start + width, HEAD), width)
+        dq_out[0, :, low] = part[0, :, :width].astype(F32)
+        dq_out[0, :, high] = part[0, :, width:].astype(F32) + late * extra[0].astype(F32)
+        for i, out in enumerate((dk_out, dv_out)):
+            out[0, :, low] = part[1 + i, :, :width].astype(F32) + early * extra[i].astype(F32)
+            out[0, :, high] = part[1 + i, :, width:].astype(F32)
+
+
+def join(place, own, sib, straight, diag, shape):
+    out = jax.ShapeDtypeStruct(shape, F32)
+    return pl.pallas_call(
+        join_kernel,
+        out_shape=[out] * 3,
+        in_specs=[SMEM] + [VMEM] * 4,
+        out_specs=[VMEM] * 3,
+        compiler_params=params(),
+        cost_estimate=cost(0, 18 * out.size),
+        name="join",
+    )(place, own, sib, straight, diag)
+
+
+def whole_router_kernel(gate_ref, own_ref, sib_ref, x_ref, out_ref):
+    gate = gate_ref[...]
+    grad = (own_ref[...] + sib_ref[...]) * gate * (1.0 - gate)
+    high = grad.astype(BF16)
+    rest = grad - high.astype(F32)
+    mid = rest.astype(BF16)
+    low = (rest - mid.astype(F32)).astype(BF16)
+    row = lax.broadcasted_iota(jnp.int32, (8, grad.shape[1]), 0)
+    lhs = jnp.where(row == 0, high.astype(F32), jnp.where(row == 1, mid.astype(F32), jnp.where(row == 2, low.astype(F32), 0.0)))
+    term = jnp.sum(nn(lhs.astype(BF16), x_ref[0]), axis=0, keepdims=True)
+    parts, copies, _, chunk = out_ref.shape
+    for j in range(parts):
+        for i in range(copies):
+            out_ref[j, i] = term[:, j * chunk : (j + 1) * chunk]
+
+
+def whole_router(gate, own, sib, x_routed, parts, copies):
+    chunk = x_routed.shape[-1] // parts
+    return pl.pallas_call(
+        whole_router_kernel,
+        out_shape=jax.ShapeDtypeStruct((parts, copies, 1, chunk), F32),
+        in_specs=[VMEM] * 4,
+        out_specs=VMEM,
+        compiler_params=params(),
+        cost_estimate=cost(16 * x_routed.size, x_routed.size * 2),
+        name="router_terms",
+    )(gate, own, sib, x_routed)
+
+
+def swap_body(route_pos, x_routed, w_router, queries, keys, values, d_gated):
+    slots, full = queries.shape[1], queries.shape[2]
+    n, ndp = lax.axis_size("ctx"), lax.axis_size("dp")
+    me = lax.axis_index("ctx")
+    place = jnp.stack([me % 2, me // 2]).astype(jnp.int32)
+
+    def send(a, flip):
+        return lax.ppermute(a, "ctx", [(i, i ^ flip) for i in range(n)])
+
+    mine, theirs, out_s, out_d = pack_all(place, route_pos, keys, values, queries, d_gated)
+    in_s, in_d = send(out_s, 2), send(out_d, 3)
+    sib = send(theirs, 1)
+    w_row, _ = lax.optimization_barrier((w_router.reshape(1, 1, -1), mine))
+    w_full = lax.all_to_all(jnp.broadcast_to(w_row, (ndp, 1, w_row.shape[-1])), "dp", 0, 0, tiled=True)
+    gate = whole_gate(route_pos, x_routed, w_full)
+    gates = (gate, send(gate, 1))
+    local = local_stats(place, mine, sib)
+    cross, stats, message = cross_stats(place, mine, sib, in_s, in_d, local, gates)
+    heard = send(message, 2)
+    back_s, back_d, keep, final, sum_own, sum_sib = cross_grad(place, cross, stats, local, heard, gates)
+    ret_s, ret_d = send(back_s, 2), send(back_d, 3)
+    own_out, sib_out = local_grad(place, mine, sib, final, gates, keep)
+    sib_in = send(sib_out, 1)
+    terms = whole_router(gate, sum_own, send(sum_sib, 1), x_routed, ndp, n)
+    chunk = terms.shape[-1]
+    terms = lax.all_to_all(terms.reshape(ndp * n, 1, chunk), ("dp", "ctx"), 0, 0, tiled=True)
+    router_grad = jnp.sum(terms, axis=0)[0] / float(ndp * n * slots // 2)
+    dq, dk, dv = join(place, own_out, sib_in, ret_s, ret_d, queries.shape)
+    return dq, dk, dv, router_grad
+
+
 def body(route_pos, x_routed, w_router, queries, keys, values, d_gated):
     slots, full = queries.shape[1], queries.shape[2]
     n, ndp = lax.axis_size("ctx"), lax.axis_size("dp")
@@ -323,8 +708,9 @@
         P("dp", "ctx", None),
         P("dp", "ctx", None),
     )
+    paired = mesh.shape["ctx"] == 4
     return jax.shard_map(
-        body,
+        swap_body if paired else body,
         mesh=mesh,
         in_specs=placed,
         out_specs=(P("dp", "ctx", None), P("dp", "ctx", None), P("dp", "ctx", None), P("dp")),

time: 101 us -> 62.5 us (0.62)
  starting transfers between devices: 67.3 us -> 9.59 us
  blocking collectives: 0 us -> 12.4 us
  Pallas kernels: 10.1 us -> 15.8 us
  local copies, waits for them, and re-layouts: 3.62 us -> 6.63 us
  waiting for transfers between devices: 17.5 us -> 15.4 us
    ppermute x50 -> x9, starting transfers between devices: 67.3 us -> 7.02 us  [send(): return lax.ppermute(a, 'ctx', [(i, i ^ flip) for i in range(n)])]
    all_to_all x0 -> x1, blocking collectives: none -> 12.4 us  [swap_body(): lax.all_to_all(jnp.broadcast_to(w_row, (ndp, 1, w_row.shape[-1])), 'dp',...]
    ppermute x50 -> x9, waiting for transfers between devices: 17.5 us -> 9.78 us  [send(): return lax.ppermute(a, 'ctx', [(i, i ^ flip) for i in range(n)])]
    pallas_call x9 -> x8, Pallas kernels: 10.1 us -> 15.8 us  [the longest x1 4.32 us: local_grad(): pl.pallas_call(functools.partial(local_grad_kernel, HEAD ** (-0.5)), out_...]
    all_to_all x0 -> x1, waiting for transfers between devices: none -> 5.59 us  [swap_body(): lax.all_to_all(terms.reshape(ndp * n, 1, chunk), ('dp', 'ctx'), 0, 0, til...]
    unnamed x12 -> x24, local copies, waits for them, and re-layouts: 2.85 us -> 6.1 us
    all_to_all x0 -> x1, starting transfers between devices: none -> 2.57 us  [swap_body(): lax.all_to_all(terms.reshape(ndp * n, 1, chunk), ('dp', 'ctx'), 0, 0, til...]
  transfers between devices with their start and end apart: 50 -> 10, of which waited for: 12 -> 5; matrix products, arithmetic and copies ran while one was open for 1% -> 3% of each run, Pallas kernels for 6% -> 5%
where the time goes in v2:
time: 62.5 us; the launch traced here: 62 us
  Pallas kernels  15.8 us (25%)
  waiting for transfers between devices  15.4 us (25%)
  blocking collectives  12.4 us (20%)
  starting transfers between devices  9.59 us (15%)
  local copies, waits for them, and re-layouts  6.63 us (11%)
  other arithmetic  1.44 us (2%)
  between operations  0.8 us (1%)
    all_to_all x1, blocking collectives, swap_body(): lax.all_to_all(jnp.broadcast_to(w_row, (ndp, 1, w_row.shape[-1])), 'dp',...  12.4 us
    ppermute x9, waiting for transfers between devices, send(): return lax.ppermute(a, 'ctx', [(i, i ^ flip) for i in range(n)])  9.78 us
    ppermute x9, starting transfers between devices, send(): return lax.ppermute(a, 'ctx', [(i, i ^ flip) for i in range(n)])  7.02 us
    unnamed x24, local copies, waits for them, and re-layouts  6.1 us
    all_to_all x1, waiting for transfers between devices, swap_body(): lax.all_to_all(terms.reshape(ndp * n, 1, chunk), ('dp', 'ctx'), 0, 0, til...  5.59 us
    pallas_call x1, Pallas kernels, local_grad(): pl.pallas_call(functools.partial(local_grad_kernel, HEAD ** (-0.5)), out_...  4.32 us
    all_to_all x1, starting transfers between devices, swap_body(): lax.all_to_all(terms.reshape(ndp * n, 1, chunk), ('dp', 'ctx'), 0, 0, til...  2.57 us
    pallas_call x1, Pallas kernels, join(): pl.pallas_call(join_kernel, out_shape=[out] * 3, in_specs=[SMEM] + [VMEM]...  2.42 us
  transfers between devices with their start and end apart: 10, of which 5 were waited for; matrix products, arithmetic and copies ran while one was open for 3% of the time, Pallas kernels for 5%

profile of v2, /device:TPU:0, one launch (start us, length us, event | category | flops | bytes accessed | tf_op | source)
XLA Modules:
  0.0 62.0 jit_solution(15979229295872868122)
XLA Ops:
  1.3 1.2 %copy-done.1 = f32[1,128,2048]{2,1,0:T(8,128)S(1)} copy-done((f32[1,128,2048]{2,1,0:T(8,128)S(1)}, f32[1,128,2048]{2,1,0:T(8,128)}, u32[]{:S(2)}) %copy-start.1) | copy-done | bytes 1048600
  2.5 1.0 %copy-done.4 = bf16[1,128,2048]{2,1,0:T(8,128)(2,1)S(1)} copy-done((bf16[1,128,2048]{2,1,0:T(8,128)(2,1)S(1)}, bf16[1,128,2048]{2,1,0:T(8,128)(2,1)}, u32[]{:S(2)}) %copy-start.4) | copy-done | bytes 524312
  3.6 1.0 %copy-done.5 = bf16[1,128,2048]{2,1,0:T(8,128)(2,1)S(1)} copy-done((bf16[1,128,2048]{2,1,0:T(8,128)(2,1)S(1)}, bf16[1,128,2048]{2,1,0:T(8,128)(2,1)}, u32[]{:S(2)}) %copy-start.5) | copy-done | bytes 524312
  4.6 1.0 %copy-done.6 = bf16[1,128,2048]{2,1,0:T(8,128)(2,1)S(1)} copy-done((bf16[1,128,2048]{2,1,0:T(8,128)(2,1)S(1)}, bf16[1,128,2048]{2,1,0:T(8,128)(2,1)}, u32[]{:S(2)}) %copy-start.6) | copy-done | bytes 524312
  5.7 2.2 %pack_all.1 = (bf16[4,128,1024]{2,1,0:T(8,128)(2,1)S(1)}, bf16[4,128,1024]{2,1,0:T(8,128)(2,1)}, bf16[2,128,512]{2,1,0:T(8,128)(2,1)}, bf16[2,128,512]{2,1,0:T(8,128)(2,1)}) custom-call(s32[2]{0:T(128)S(1)} %pad_add_fusion.place_ref, s32[1,128]{1,0:T(1,128)S(1)} %copy-done.7, bf16[1,128,2048]{2,1,0:T(8,128)(2,1)S(1)} %copy-done.4, ...), custom_call_target="tpu_custom_call" | custom-call | flops 1 | bytes 1 | tf_op jit(solution)/shard_map/pack_all/pallas_call | solution.py:296
  8.4 2.6 %collective-permute-start.1 = (bf16[2,128,512]{2,1,0:T(8,128)(2,1)}, bf16[2,128,512]{2,1,0:T(8,128)(2,1)S(1)}, u32[]{:S(2)}, u32[]{:S(2)}) collective-permute-start(bf16[2,128,512]{2,1,0:T(8,128)(2,1)} %get-tuple-element.25), channel_id=1, source_target_pairs={{0,2},{1,3},{2,0},{3,1},{4,6},{5,7},{6,4},{7,5},{8,10},{9,11},{10,... | collective-permute-start | bytes 786440 | tf_op jit(solution)/shard_map/ppermute | solution.py:608
  11.6 0.7 %reduce.2 = bf16[8,512]{1,0:T(8,128)(2,1)S(1)} reduce(bf16[8,1,512]{2,1,0:T(2,128)(2,1)S(1)} %broadcast_in_dim.8, bf16[]{:T(256)} %broadcast.5), dimensions={1}, to_apply=%broadcast_in_dim.8.reduce_sub_computation | reduce | bytes 16386 | tf_op jit(solution)/shard_map/broadcast_in_dim | solution.py:614
  12.3 12.4 %all_to_all.10 = bf16[8,2,256]{2,1,0:T(2,128)(2,1)S(1)} all-to-all(bf16[8,2,256]{2,1,0:T(2,128)(2,1)S(1)} %reshape.21), channel_id=1, replica_groups=mesh['dp'=8,'ctx'=4] {'dp'}, dimensions={0} | all-to-all | bytes 16384 | tf_op jit(solution)/shard_map/all_to_all | solution.py:614
  25.1 1.7 %local_stats.1.local = f32[3,8,256]{2,1,0:T(8,128)S(1)} custom-call(s32[2]{0:T(128)S(1)} %pad_add_fusion.place_ref, bf16[4,128,1024]{2,1,0:T(8,128)(2,1)S(1)} %get-tuple-element.23.mine, bf16[4,128,1024]{2,1,0:T(8,128)(2,1)S(1)} %collective-permute-done.sib), custom_call_target="tpu_custom_call" | custom-call | flops 1 | bytes 1 | tf_op jit(solution)/shard_map/local_stats/pallas_call | solution.py:364
  26.9 1.6 %cross_stats.1 = (bf16[4,256,512]{2,1,0:T(8,128)(2,1)S(1)}, f32[3,4,256]{2,1,0:T(4,128)S(1)}, f32[4,4,256]{2,1,0:T(4,128)S(1)}) custom-call(s32[2]{0:T(128)S(1)} %pad_add_fusion.place_ref, bf16[4,128,1024]{2,1,0:T(8,128)(2,1)S(1)} %get-tuple-element.23.mine, bf16[4,128,1024]{2,1,0:T(8,128)(2,1)S(1)} %collective-permute-done.sib, ...), custom_call_target="tpu_custom_call" | custom-call | flops 1 | bytes 1 | tf_op jit(solution)/shard_map/cross_stats/pallas_call | solution.py:420
  28.5 1.6 %collective-permute-start.4 = (f32[4,4,256]{2,1,0:T(4,128)S(1)}, f32[4,4,256]{2,1,0:T(4,128)S(1)}, u32[]{:S(2)}, u32[]{:S(2)}) collective-permute-start(f32[4,4,256]{2,1,0:T(4,128)S(1)} %get-tuple-element.30), channel_id=1, source_target_pairs={{0,2},{1,3},{2,0},{3,1},{4,6},{5,7},{6,4},{7,5},{8,10},{9,11},{10,... | collective-permute-start | bytes 49160 | tf_op jit(solution)/shard_map/ppermute | solution.py:608
  30.1 2.2 %collective-permute-done.4.heard = f32[4,4,256]{2,1,0:T(4,128)S(1)} collective-permute-done((f32[4,4,256]{2,1,0:T(4,128)S(1)}, f32[4,4,256]{2,1,0:T(4,128)S(1)}, u32[]{:S(2)}, u32[]{:S(2)}) %collective-permute-start.4) | collective-permute-done | bytes 16416 | tf_op jit(solution)/shard_map/ppermute | solution.py:608
  32.3 2.2 %cross_grad.1 = (bf16[2,128,512]{2,1,0:T(8,128)(2,1)S(1)}, bf16[2,128,512]{2,1,0:T(8,128)(2,1)S(1)}, bf16[3,256,512]{2,1,0:T(8,128)(2,1)S(1)}, f32[3,8,256]{2,1,...) custom-call(s32[2]{0:T(128)S(1)} %pad_add_fusion.place_ref, ...), custom_call_target="tpu_custom_call" | custom-call | flops 1 | bytes 1 | tf_op jit(solution)/shard_map/cross_grad/pallas_call | solution.py:493
  34.5 4.3 %local_grad.1 = (bf16[3,128,1024]{2,1,0:T(8,128)(2,1)S(1)}, bf16[3,128,1024]{2,1,0:T(8,128)(2,1)}) custom-call(s32[2]{0:T(128)S(1)} %pad_add_fusion.place_ref, bf16[4,128,1024]{2,1,0:T(8,128)(2,1)S(1)} %get-tuple-element.23.mine, bf16[4,128,1024]{2,1,0:T(8,128)(2,1)S(1)} %collective-permute-done.sib, f32[3,8,256]{2,1,0:T(8,128)S(1)} %get-tuple-element.31.final, ...), custom_call_target="tpu_custom_call" | custom-call | flops 1 | bytes 1 | tf_op jit(solution)/shard_map/local_grad/pallas_call | solution.py:533
  39.4 1.4 %collective-permute-done.8.sib_ref = f32[1,128]{1,0:T(1,128)S(1)} collective-permute-done((f32[1,128]{1,0:T(1,128)S(1)}, f32[1,128]{1,0:T(1,128)S(1)}, u32[]{:S(2)}, u32[]{:S(2)}) %collective-permute-start.8) | collective-permute-done | bytes 544 | tf_op jit(solution)/shard_map/ppermute | solution.py:608
  40.8 0.9 %router_terms.1 = f32[8,4,1,512]{3,2,1,0:T(1,128)} custom-call(f32[1,128]{1,0:T(1,128)S(1)} %router_gate.1.gate_own.gate_ref, f32[1,128]{1,0:T(1,128)S(1)} %get-tuple-element.40.own_ref, f32[1,128]{1,0:T(1,128)S(1)} %collective-permute-done.8.sib_ref, bf16[1,128,4096]{2,1,0:T(8,128)(2,1)S(1)} %copy-done), custom_call_target="tpu_custom_call" | custom-call | flops 1 | bytes 1 | tf_op jit(solution)/shard_map/router_terms/pallas_call | solution.py:590
  41.7 2.6 %all-to-all-start.1 = ((f32[32,1,512]{2,1,0:T(1,128)}), f32[32,1,512]{2,1,0:T(1,128)S(1)}, u32[]{:S(2)}, u32[]{:S(2)}) async-start(f32[32,1,512]{2,1,0:T(1,128)} %bitcast.2), calls=%async_computation.1 | async-start | bytes 131072 | tf_op jit(solution)/shard_map/all_to_all | solution.py:626
  44.3 1.8 %collective-permute-start.6 = (bf16[2,128,512]{2,1,0:T(8,128)(2,1)S(1)}, bf16[2,128,512]{2,1,0:T(8,128)(2,1)S(1)}, u32[]{:S(2)}, u32[]{:S(2)}) collective-permute-start(bf16[2,128,512]{2,1,0:T(8,128)(2,1)S(1)} %copy-done.9), channel_id=1, source_target_pairs={{0,2},{1,3},{2,0},{3,1},{4,6},{5,7},{6,4},{7,5},{8,10},{9,11},{10,... | collective-permute-start | bytes 786440 | tf_op jit(solution)/shard_map/ppermute | solution.py:608
  46.1 5.6 %all-to-all-done.1 = f32[32,1,512]{2,1,0:T(1,128)S(1)} async-done(((f32[32,1,512]{2,1,0:T(1,128)}), f32[32,1,512]{2,1,0:T(1,128)S(1)}, u32[]{:S(2)}, u32[]{:S(2)}) %all-to-all-start.1) | async-done | bytes 65568 | tf_op jit(solution)/shard_map/all_to_all | solution.py:626
  51.7 0.6 broadcast_multiply_fusion
  52.3 1.7 %collective-permute-done.6.straight = bf16[2,128,512]{2,1,0:T(8,128)(2,1)S(1)} collective-permute-done((bf16[2,128,512]{2,1,0:T(8,128)(2,1)S(1)}, bf16[2,128,512]{2,1,0:T(8,128)(2,1)S(1)}, u32[]{:S(2)}, u32[]{:S(2)}) %collective-permute-start.6) | collective-permute-done | bytes 262176 | tf_op jit(solution)/shard_map/ppermute | solution.py:608
  54.0 4.4 %collective-permute-done.7.diag = bf16[2,128,512]{2,1,0:T(8,128)(2,1)S(1)} collective-permute-done((bf16[2,128,512]{2,1,0:T(8,128)(2,1)S(1)}, bf16[2,128,512]{2,1,0:T(8,128)(2,1)S(1)}, u32[]{:S(2)}, u32[]{:S(2)}) %collective-permute-start.7) | collective-permute-done | bytes 262176 | tf_op jit(solution)/shard_map/ppermute | solution.py:608
  58.4 1.1 %copy-done.3 = bf16[3,128,1024]{2,1,0:T(8,128)(2,1)S(1)} copy-done((bf16[3,128,1024]{2,1,0:T(8,128)(2,1)S(1)}, bf16[3,128,1024]{2,1,0:T(8,128)(2,1)}, u32[]{:S(2)}) %copy-start.3) | copy-done | bytes 786456
  59.6 2.4 %join.1 = (f32[1,128,2048]{2,1,0:T(8,128)}, f32[1,128,2048]{2,1,0:T(8,128)}, f32[1,128,2048]{2,1,0:T(8,128)}) custom-call(s32[2]{0:T(128)S(1)} %pad_add_fusion.place_ref, bf16[3,128,1024]{2,1,0:T(8,128)(2,1)S(1)} %copy-done.3, bf16[3,128,1024]{2,1,0:T(8,128)(2,1)S(1)} %collective-permute-done.5.sib, ...), custom_call_target="tpu_custom_call" | custom-call | flops 1 | bytes 1 | tf_op jit(solution)/shard_map/join/pallas_call | solution.py:561
  (37 shorter events, 2.8 us)
Async XLA Ops:
  0.6 0.7 %copy-start.7 = (s32[1,128]{1,0:T(1,128)S(1)}, s32[1,128]{1,0:T(1,128)}, u32[]{:S(2)}) copy-start(s32[1,128]{1,0:T(1,128)} %pos_ref.3) | copy-start | bytes 1540
  1.3 1.2 %copy-start.1 = (f32[1,128,2048]{2,1,0:T(8,128)S(1)}, f32[1,128,2048]{2,1,0:T(8,128)}, u32[]{:S(2)}) copy-start(f32[1,128,2048]{2,1,0:T(8,128)} %dg_ref.1) | copy-start | bytes 3145732
  2.5 1.0 %copy-start.4 = (bf16[1,128,2048]{2,1,0:T(8,128)(2,1)S(1)}, bf16[1,128,2048]{2,1,0:T(8,128)(2,1)}, u32[]{:S(2)}) copy-start(bf16[1,128,2048]{2,1,0:T(8,128)(2,1)} %k_ref.1) | copy-start | bytes 1572868
  3.6 1.0 %copy-start.5 = (bf16[1,128,2048]{2,1,0:T(8,128)(2,1)S(1)}, bf16[1,128,2048]{2,1,0:T(8,128)(2,1)}, u32[]{:S(2)}) copy-start(bf16[1,128,2048]{2,1,0:T(8,128)(2,1)} %v_ref.1) | copy-start | bytes 1572868
  4.6 1.0 %copy-start.6 = (bf16[1,128,2048]{2,1,0:T(8,128)(2,1)S(1)}, bf16[1,128,2048]{2,1,0:T(8,128)(2,1)}, u32[]{:S(2)}) copy-start(bf16[1,128,2048]{2,1,0:T(8,128)(2,1)} %q_ref.1) | copy-start | bytes 1572868
  5.7 19.0 %copy-start = (bf16[1,128,4096]{2,1,0:T(8,128)(2,1)S(1)}, bf16[1,128,4096]{2,1,0:T(8,128)(2,1)}, u32[]{:S(2)}) copy-start(bf16[1,128,4096]{2,1,0:T(8,128)(2,1)} %x_ref.3) | copy-start | bytes 3145732
  7.9 17.2 %collective-permute-start = (bf16[4,128,1024]{2,1,0:T(8,128)(2,1)}, bf16[4,128,1024]{2,1,0:T(8,128)(2,1)S(1)}, u32[]{:S(2)}, u32[]{:S(2)}) collective-permute-start(bf16[4,128,1024]{2,1,0:T(8,128)(2,1)} %get-tuple-element.24), channel_id=1, source_target_pairs={{0,1},{1,0},{2,3},{3,2},{4,5},{5,4},{6,7},{7,6},{8,9},{9,8},{10,11... | collective-permute-start | bytes 3145736 | tf_op jit(solution)/shard_map/ppermute | solution.py:608
  8.4 2.6 %copy-start.10 = (bf16[512]{0:T(512)(128)(2,1)S(1)}, bf16[512]{0:T(512)(128)(2,1)}, u32[]{:S(2)}) copy-start(bf16[512]{0:T(512)(128)(2,1)} %param.9) | copy-start | bytes 3076
  8.4 18.5 %collective-permute-start.1 = (bf16[2,128,512]{2,1,0:T(8,128)(2,1)}, bf16[2,128,512]{2,1,0:T(8,128)(2,1)S(1)}, u32[]{:S(2)}, u32[]{:S(2)}) collective-permute-start(bf16[2,128,512]{2,1,0:T(8,128)(2,1)} %get-tuple-element.25), channel_id=1, source_target_pairs={{0,2},{1,3},{2,0},{3,1},{4,6},{5,7},{6,4},{7,5},{8,10},{9,11},{10,... | collective-permute-start | bytes 786440 | tf_op jit(solution)/shard_map/ppermute | solution.py:608
  11.0 15.9 %collective-permute-start.2 = (bf16[2,128,512]{2,1,0:T(8,128)(2,1)}, bf16[2,128,512]{2,1,0:T(8,128)(2,1)}, u32[]{:S(2)}, u32[]{:S(2)}) collective-permute-start(bf16[2,128,512]{2,1,0:T(8,128)(2,1)} %get-tuple-element.26), channel_id=1, source_target_pairs={{0,3},{1,2},{2,1},{3,0},{4,7},{5,6},{6,5},{7,4},{8,11},{9,10},{10,... | collective-permute-start | bytes 786440 | tf_op jit(solution)/shard_map/ppermute | solution.py:608
  25.1 1.8 %collective-permute-start.3 = (f32[1,128]{1,0:T(1,128)S(1)}, f32[1,128]{1,0:T(1,128)S(1)}, u32[]{:S(2)}, u32[]{:S(2)}) collective-permute-start(f32[1,128]{1,0:T(1,128)S(1)} %router_gate.1.gate_own.gate_ref), channel_id=1, source_target_pairs={{0,1},{1,0},{2,3},{3,2},{4,5},{5,4},{6,7},{7,6},{8,9},{9,8},{10,11... | collective-permute-start | bytes 1544 | tf_op jit(solution)/shard_map/ppermute | solution.py:608
  28.5 3.8 %collective-permute-start.4 = (f32[4,4,256]{2,1,0:T(4,128)S(1)}, f32[4,4,256]{2,1,0:T(4,128)S(1)}, u32[]{:S(2)}, u32[]{:S(2)}) collective-permute-start(f32[4,4,256]{2,1,0:T(4,128)S(1)} %get-tuple-element.30), channel_id=1, source_target_pairs={{0,2},{1,3},{2,0},{3,1},{4,6},{5,7},{6,4},{7,5},{8,10},{9,11},{10,... | collective-permute-start | bytes 49160 | tf_op jit(solution)/shard_map/ppermute | solution.py:608
  34.5 4.3 %copy-start.8 = (bf16[2,128,512]{2,1,0:T(8,128)(2,1)}, bf16[2,128,512]{2,1,0:T(8,128)(2,1)S(1)}, u32[]{:S(2)}) copy-start(bf16[2,128,512]{2,1,0:T(8,128)(2,1)S(1)} %get-tuple-element.35) | copy-start | bytes 786436
  38.9 2.8 %copy-start.2 = (bf16[3,128,1024]{2,1,0:T(8,128)(2,1)}, bf16[3,128,1024]{2,1,0:T(8,128)(2,1)S(1)}, u32[]{:S(2)}) copy-start(bf16[3,128,1024]{2,1,0:T(8,128)(2,1)S(1)} %get-tuple-element.33.own) | copy-start | bytes 2359300
  38.9 19.6 %collective-permute-start.5 = (bf16[3,128,1024]{2,1,0:T(8,128)(2,1)}, bf16[3,128,1024]{2,1,0:T(8,128)(2,1)S(1)}, u32[]{:S(2)}, u32[]{:S(2)}) collective-permute-start(bf16[3,128,1024]{2,1,0:T(8,128)(2,1)} %get-tuple-element.34), channel_id=1, source_target_pairs={{0,1},{1,0},{2,3},{3,2},{4,5},{5,4},{6,7},{7,6},{8,9},{9,8},{10,11... | collective-permute-start | bytes 2359304 | tf_op jit(solution)/shard_map/ppermute | solution.py:608
  38.9 1.9 %collective-permute-start.8 = (f32[1,128]{1,0:T(1,128)S(1)}, f32[1,128]{1,0:T(1,128)S(1)}, u32[]{:S(2)}, u32[]{:S(2)}) collective-permute-start(f32[1,128]{1,0:T(1,128)S(1)} %get-tuple-element.41), channel_id=1, source_target_pairs={{0,1},{1,0},{2,3},{3,2},{4,5},{5,4},{6,7},{7,6},{8,9},{9,8},{10,11... | collective-permute-start | bytes 1544 | tf_op jit(solution)/shard_map/ppermute | solution.py:608
  40.8 3.5 %copy-start.9 = (bf16[2,128,512]{2,1,0:T(8,128)(2,1)S(1)}, bf16[2,128,512]{2,1,0:T(8,128)(2,1)}, u32[]{:S(2)}) copy-start(bf16[2,128,512]{2,1,0:T(8,128)(2,1)} %copy-done.8) | copy-start | bytes 786436
  41.7 10.0 %all-to-all-start.1 = ((f32[32,1,512]{2,1,0:T(1,128)}), f32[32,1,512]{2,1,0:T(1,128)S(1)}, u32[]{:S(2)}, u32[]{:S(2)}) async-start(f32[32,1,512]{2,1,0:T(1,128)} %bitcast.2), calls=%async_computation.1 | async-start | bytes 131072 | tf_op jit(solution)/shard_map/all_to_all | solution.py:626
  44.3 9.7 %collective-permute-start.6 = (bf16[2,128,512]{2,1,0:T(8,128)(2,1)S(1)}, bf16[2,128,512]{2,1,0:T(8,128)(2,1)S(1)}, u32[]{:S(2)}, u32[]{:S(2)}) collective-permute-start(bf16[2,128,512]{2,1,0:T(8,128)(2,1)S(1)} %copy-done.9), channel_id=1, source_target_pairs={{0,2},{1,3},{2,0},{3,1},{4,6},{5,7},{6,4},{7,5},{8,10},{9,11},{10,... | collective-permute-start | bytes 786440 | tf_op jit(solution)/shard_map/ppermute | solution.py:608
  46.1 12.4 %collective-permute-start.7 = (bf16[2,128,512]{2,1,0:T(8,128)(2,1)S(1)}, bf16[2,128,512]{2,1,0:T(8,128)(2,1)S(1)}, u32[]{:S(2)}, u32[]{:S(2)}) collective-permute-start(bf16[2,128,512]{2,1,0:T(8,128)(2,1)S(1)} %get-tuple-element.36), channel_id=1, source_target_pairs={{0,3},{1,2},{2,1},{3,0},{4,7},{5,6},{6,5},{7,4},{8,11},{9,10},{10,... | collective-permute-start | bytes 786440 | tf_op jit(solution)/shard_map/ppermute | solution.py:608
  58.4 1.1 %copy-start.3 = (bf16[3,128,1024]{2,1,0:T(8,128)(2,1)S(1)}, bf16[3,128,1024]{2,1,0:T(8,128)(2,1)}, u32[]{:S(2)}) copy-start(bf16[3,128,1024]{2,1,0:T(8,128)(2,1)} %copy-done.2) | copy-start | bytes 2359300

commit v3 on v2

--- a/solution.py
+++ b/solution.py
@@ -10,7 +10,7 @@
 HEAD = 128
 GROUPS = 4
 NEG_FILL = -1e30
-VMEM_LIMIT = 48 * 1024 * 1024
+MIB = 1024 * 1024
 BF16 = jnp.bfloat16
 F32 = jnp.float32
 
@@ -18,8 +18,8 @@
 SMEM = pl.BlockSpec(memory_space=pltpu.SMEM)
 
 
-def params():
-    return pltpu.CompilerParams(vmem_limit_bytes=VMEM_LIMIT)
+def params(mib=20):
+    return pltpu.CompilerParams(vmem_limit_bytes=mib * MIB)
 
 
 def cost(flops, nbytes, exps=0):
@@ -168,7 +168,7 @@
         out_shape=outs,
         in_specs=[SMEM] + [VMEM] * (7 + len(kv)),
         out_specs=[VMEM] * len(outs),
-        compiler_params=params(),
+        compiler_params=params(48),
         cost_estimate=cost(20 * slots * keys * width, 8 * keys * width + 20 * slots * width, 2 * slots * keys * width // HEAD),
         name="attention",
     )(core, live, *gates, *accs, q_own, q_sib, *kv)
@@ -209,7 +209,7 @@
         out_shape=[out] * 3,
         in_specs=[SMEM] + [VMEM] * len(flat),
         out_specs=[VMEM] * 3,
-        compiler_params=params(),
+        compiler_params=params(48),
         cost_estimate=cost(0, 3 * out.size * 6),
         name="combine",
     )(core, *flat)
@@ -299,32 +299,33 @@
         in_specs=[SMEM, VMEM, hbm, hbm, hbm, hbm],
         out_specs=[VMEM] * 4,
         scratch_shapes=[pltpu.VMEM((2, slots, full // 2), F32), pltpu.SemaphoreType.DMA((8,))],
-        compiler_params=params(),
+        compiler_params=params(60),
         cost_estimate=cost(0, 20 * slots * full),
         name="pack_all",
     )(place, route_pos, keys, values, queries, d_gated)
 
 
-def whole_gate_kernel(pos_ref, x_ref, w_ref, out_ref):
-    parts, _, chunk = w_ref.shape
+def whole_gate_kernel(parts, place_ref, pos_ref, x_ref, w_ref, out_ref):
+    chunk = w_ref.shape[1] // parts
     total = jnp.zeros((8, x_ref.shape[1]), F32)
     for j in range(parts):
-        w_rows = jnp.broadcast_to(w_ref[j].astype(F32), (8, chunk)).astype(BF16)
-        total = total + nt(w_rows, x_ref[0, :, j * chunk : (j + 1) * chunk])
+        w_rows = jnp.broadcast_to(w_ref[:, j * chunk : (j + 1) * chunk], (8, chunk)).astype(BF16)
+        cols = pl.ds(pl.multiple_of((place_ref[2] ^ j) * chunk, HEAD), chunk)
+        total = total + nt(w_rows, x_ref[0, :, cols])
     gate = 1.0 / (1.0 + jnp.exp(-total[0:1]))
     out_ref[...] = jnp.where(pos_ref[...] >= 0, gate, 0.0)
 
 
-def whole_gate(route_pos, x_routed, w_full):
-    return pl.pallas_call(
-        whole_gate_kernel,
+def whole_gate(place, route_pos, x_routed, w_full, parts):
+    return pl.pallas_call(
+        functools.partial(whole_gate_kernel, parts),
         out_shape=jax.ShapeDtypeStruct(route_pos.shape, F32),
-        in_specs=[VMEM] * 3,
+        in_specs=[SMEM] + [VMEM] * 3,
         out_specs=VMEM,
         compiler_params=params(),
         cost_estimate=cost(16 * x_routed.size, x_routed.size * 2),
         name="router_gate",
-    )(route_pos, x_routed, w_full)
+    )(place, route_pos, x_routed, w_full)
 
 
 def local_mask(core, mine, sib):
@@ -599,32 +600,54 @@
 
 
 def swap_body(route_pos, x_routed, w_router, queries, keys, values, d_gated):
-    slots, full = queries.shape[1], queries.shape[2]
+    slots = queries.shape[1]
     n, ndp = lax.axis_size("ctx"), lax.axis_size("dp")
     me = lax.axis_index("ctx")
-    place = jnp.stack([me % 2, me // 2]).astype(jnp.int32)
+    place = jnp.stack([me % 2, me // 2, lax.axis_index("dp")]).astype(jnp.int32)
 
     def send(a, flip):
         return lax.ppermute(a, "ctx", [(i, i ^ flip) for i in range(n)])
+
+    def beside(fn, *operands):
+        def skip(*ops):
+            return jax.tree.map(lambda o: jnp.zeros(o.shape, o.dtype), jax.eval_shape(fn, *ops))
+
+        return lax.cond(route_pos[0, 0] >= -1, fn, skip, *operands)
+
+    def gate_phase(place, route_pos, x_routed, w_router):
+        w_part = w_router.reshape(1, -1).astype(F32)
+        step = 1
+        while step < ndp:
+            w_part = jnp.concatenate([w_part, lax.ppermute(w_part, "dp", [(i, i ^ step) for i in range(ndp)])], axis=1)
+            step *= 2
+        gate = whole_gate(place, route_pos, x_routed, w_part, ndp)
+        return gate, send(gate, 1)
+
+    def grad_phase(place, mine, sib, final, gate, gate_sib, keep):
+        own_out, sib_out = local_grad(place, mine, sib, final, (gate, gate_sib), keep)
+        return own_out, send(sib_out, 1)
+
+    def local_phase(place, mine, sib, final, gate, gate_sib, keep, sum_own, sum_sib, x_routed):
+        terms = whole_router(gate, sum_own, send(sum_sib, 1), x_routed, ndp, n)
+        chunk = terms.shape[-1]
+        shared = lax.all_to_all(terms.reshape(ndp * n, 1, chunk), ("dp", "ctx"), 0, 0, tiled=True)
+        gate, _ = lax.optimization_barrier((gate, terms))
+        own_out, sib_in = beside(grad_phase, place, mine, sib, final, gate, gate_sib, keep)
+        return own_out, sib_in, jnp.sum(shared, axis=0)[0] / float(ndp * n * slots // 2)
 
     mine, theirs, out_s, out_d = pack_all(place, route_pos, keys, values, queries, d_gated)
     in_s, in_d = send(out_s, 2), send(out_d, 3)
     sib = send(theirs, 1)
-    w_row, _ = lax.optimization_barrier((w_router.reshape(1, 1, -1), mine))
-    w_full = lax.all_to_all(jnp.broadcast_to(w_row, (ndp, 1, w_row.shape[-1])), "dp", 0, 0, tiled=True)
-    gate = whole_gate(route_pos, x_routed, w_full)
-    gates = (gate, send(gate, 1))
+    w_late, _ = lax.optimization_barrier((w_router, mine))
+    gates = beside(gate_phase, place, route_pos, x_routed, w_late)
     local = local_stats(place, mine, sib)
     cross, stats, message = cross_stats(place, mine, sib, in_s, in_d, local, gates)
     heard = send(message, 2)
     back_s, back_d, keep, final, sum_own, sum_sib = cross_grad(place, cross, stats, local, heard, gates)
     ret_s, ret_d = send(back_s, 2), send(back_d, 3)
-    own_out, sib_out = local_grad(place, mine, sib, final, gates, keep)
-    sib_in = send(sib_out, 1)
-    terms = whole_router(gate, sum_own, send(sum_sib, 1), x_routed, ndp, n)
-    chunk = terms.shape[-1]
-    terms = lax.all_to_all(terms.reshape(ndp * n, 1, chunk), ("dp", "ctx"), 0, 0, tiled=True)
-    router_grad = jnp.sum(terms, axis=0)[0] / float(ndp * n * slots // 2)
+    own_out, sib_in, router_grad = beside(
+        local_phase, place, mine, sib, final, *gates, keep, sum_own, sum_sib, x_routed
+    )
     dq, dk, dv = join(place, own_out, sib_in, ret_s, ret_d, queries.shape)
     return dq, dk, dv, router_grad
 
@@ -708,7 +731,8 @@
         P("dp", "ctx", None),
         P("dp", "ctx", None),
     )
-    paired = mesh.shape["ctx"] == 4
+    ndp = mesh.shape["dp"]
+    paired = mesh.shape["ctx"] == 4 and ndp & (ndp - 1) == 0
     return jax.shard_map(
         swap_body if paired else body,
         mesh=mesh,

time: 62.5 us -> 55.8 us (0.89)
  blocking collectives: 12.4 us -> 0 us
  starting transfers between devices: 9.59 us -> 19.9 us
  Pallas kernels: 15.8 us -> 21.8 us
  local copies, waits for them, and re-layouts: 6.63 us -> 1.26 us
  waiting for transfers between devices: 15.4 us -> 11.5 us
  other arithmetic: 1.44 us -> 0.18 us
    all_to_all x1 -> x0, blocking collectives: 12.4 us -> none  [swap_body(): lax.all_to_all(jnp.broadcast_to(w_row, (ndp, 1, w_row.shape[-1])), 'dp',...]
    ppermute x0 -> x3, starting transfers between devices: none -> 6.46 us  [gate_phase(): lax.ppermute(w_part, 'dp', [(i, i ^ step) for i in range(ndp)])]
    all_to_all x1, waiting for transfers between devices: 5.59 us -> 0.01 us  [local_phase(): lax.all_to_all(terms.reshape(ndp * n, 1, chunk), ('dp', 'ctx'), 0, 0, til...]
    ppermute x0 -> x3, waiting for transfers between devices: none -> 5.35 us  [gate_phase(): lax.ppermute(w_part, 'dp', [(i, i ^ step) for i in range(ndp)])]
    unnamed x24 -> x8, local copies, waits for them, and re-layouts: 6.1 us -> 1.26 us
    ppermute x9, waiting for transfers between devices: 9.78 us -> 6.17 us  [send(): return lax.ppermute(a, 'ctx', [(i, i ^ flip) for i in range(n)])]
    all_to_all x1, starting transfers between devices: 2.57 us -> 6.08 us  [local_phase(): lax.all_to_all(terms.reshape(ndp * n, 1, chunk), ('dp', 'ctx'), 0, 0, til...]
    pallas_call x1, Pallas kernels: 0.36 us -> 2.22 us  [whole_gate(): pl.pallas_call(functools.partial(whole_gate_kernel, parts), out_shape=jax...]
  transfers between devices with their start and end apart: 10 -> 13, of which waited for: 5 -> 7; matrix products, arithmetic and copies ran while one was open for 3% -> 0% of each run, Pallas kernels for 5% -> 19%
where the time goes in v3:
time: 55.8 us; the launch traced here: 55.5 us
  Pallas kernels  21.8 us (39%)
  starting transfers between devices  19.9 us (36%)
  waiting for transfers between devices  11.5 us (21%)
  local copies, waits for them, and re-layouts  1.26 us (2%)
  between operations  0.78 us (1%)
    ppermute x9, starting transfers between devices, send(): return lax.ppermute(a, 'ctx', [(i, i ^ flip) for i in range(n)])  7.33 us
    ppermute x3, starting transfers between devices, gate_phase(): lax.ppermute(w_part, 'dp', [(i, i ^ step) for i in range(ndp)])  6.46 us
    ppermute x9, waiting for transfers between devices, send(): return lax.ppermute(a, 'ctx', [(i, i ^ flip) for i in range(n)])  6.17 us
    all_to_all x1, starting transfers between devices, local_phase(): lax.all_to_all(terms.reshape(ndp * n, 1, chunk), ('dp', 'ctx'), 0, 0, til...  6.08 us
    ppermute x3, waiting for transfers between devices, gate_phase(): lax.ppermute(w_part, 'dp', [(i, i ^ step) for i in range(ndp)])  5.35 us
    pallas_call x1, Pallas kernels, local_grad(): pl.pallas_call(functools.partial(local_grad_kernel, HEAD ** (-0.5)), out_...  4.92 us
    pallas_call x1, Pallas kernels, pack_all(): pl.pallas_call(pack_all_kernel, out_shape=[half, half, cross, cross], in_...  3.5 us
    pallas_call x1, Pallas kernels, join(): pl.pallas_call(join_kernel, out_shape=[out] * 3, in_specs=[SMEM] + [VMEM]...  3.25 us
  transfers between devices with their start and end apart: 13, of which 7 were waited for; matrix products, arithmetic and copies ran while one was open for 0% of the time, Pallas kernels for 19%

profile of v3, /device:TPU:0, one launch (start us, length us, event | category | flops | bytes accessed | tf_op | source)
XLA Modules:
  0.0 55.5 jit_solution(9032549266764624285)
XLA Ops:
  1.3 3.5 %pack_all.1 = (bf16[4,128,1024]{2,1,0:T(8,128)(2,1)S(1)}, bf16[4,128,1024]{2,1,0:T(8,128)(2,1)}, bf16[2,128,512]{2,1,0:T(8,128)(2,1)}, bf16[2,128,512]{2,1,0:T(8,128)(2,1)}) custom-call(s32[3]{0:T(128)S(1)} %pad_add_fusion.place_ref, s32[1,128]{1,0:T(1,128)S(1)} %copy-done.1, bf16[1,128,2048]{2,1,0:T(8,128)(2,1)} %k_ref.1, bf16[1,128,2048]{2,1,0:T(8,128)(2,1)} %v_ref.1, ...), custom_call_target="tpu_custom_call" | custom-call | flops 1 | bytes 1 | tf_op jit(solution)/shard_map/pack_all/pallas_call | solution.py:296
  5.3 2.6 %collective-permute-start.7 = (bf16[2,128,512]{2,1,0:T(8,128)(2,1)}, bf16[2,128,512]{2,1,0:T(8,128)(2,1)S(1)}, u32[]{:S(2)}, u32[]{:S(2)}) collective-permute-start(bf16[2,128,512]{2,1,0:T(8,128)(2,1)} %get-tuple-element.99), channel_id=1, source_target_pairs={{0,2},{1,3},{2,0},{3,1},{4,6},{5,7},{6,4},{7,5},{8,10},{9,11},{10,... | collective-permute-start | bytes 786440 | tf_op jit(solution)/shard_map/ppermute | solution.py:609
  8.7 15.2 %conditional.3 = (f32[1,128]{1,0:T(1,128)}, f32[1,128]{1,0:T(1,128)}) conditional(s32[]{:T(128)} %bitcast.6, () %tuple.35, (bf16[512]{0:T(512)(128)(2,1)S(1)}, s32[3]{0:T(128)S(1)}, s32[1,128]{1,0:T(1,128)S(1)}, bf16[1,128,4096]{2,1,0:T(8,128)(2,1)}) %tuple.49), branch_computations={%region_0.1_spmd, %region_1.2_spmd} | conditional | flops 17921 | bytes 119985 | solution.py:615
  8.7 1.8 %collective-permute-start.1 = (f32[1,512]{1,0:T(1,128)S(1)}, f32[1,512]{1,0:T(1,128)S(1)}, u32[]{:S(2)}, u32[]{:S(2)}) collective-permute-start(f32[1,512]{1,0:T(1,128)S(1)} %bitcast.9), channel_id=1, source_target_pairs={{0,4},{4,0},{8,12},{12,8},{16,20},{20,16},{24,28},{28,24},{1,5},{5... | collective-permute-start | bytes 6152 | tf_op jit(solution)/shard_map/cond/branch_1_fun/ppermute | solution.py:621
  10.5 1.8 %collective-permute-done.1 = f32[1,512]{1,0:T(1,128)S(1)} collective-permute-done((f32[1,512]{1,0:T(1,128)S(1)}, f32[1,512]{1,0:T(1,128)S(1)}, u32[]{:S(2)}, u32[]{:S(2)}) %collective-permute-start.1) | collective-permute-done | bytes 2080 | tf_op jit(solution)/shard_map/cond/branch_1_fun/ppermute | solution.py:621
  12.3 1.8 %collective-permute-start.2 = (f32[1,1024]{1,0:T(1,128)S(1)}, f32[1,1024]{1,0:T(1,128)S(1)}, u32[]{:S(2)}, u32[]{:S(2)}) collective-permute-start(f32[1,1024]{1,0:T(1,128)S(1)} %pad_maximum_fusion.2), channel_id=1, source_target_pairs={{0,8},{4,12},{8,0},{12,4},{16,24},{20,28},{24,16},{28,20},{1,9},{5... | collective-permute-start | bytes 12296 | tf_op jit(solution)/shard_map/cond/branch_1_fun/ppermute | solution.py:621
  14.1 1.8 %collective-permute-done.2 = f32[1,1024]{1,0:T(1,128)S(1)} collective-permute-done((f32[1,1024]{1,0:T(1,128)S(1)}, f32[1,1024]{1,0:T(1,128)S(1)}, u32[]{:S(2)}, u32[]{:S(2)}) %collective-permute-start.2) | collective-permute-done | bytes 4128 | tf_op jit(solution)/shard_map/cond/branch_1_fun/ppermute | solution.py:621
  15.9 2.9 %collective-permute-start.3 = (f32[1,2048]{1,0:T(1,128)S(1)}, f32[1,2048]{1,0:T(1,128)S(1)}, u32[]{:S(2)}, u32[]{:S(2)}) collective-permute-start(f32[1,2048]{1,0:T(1,128)S(1)} %pad_maximum_fusion.1), channel_id=1, source_target_pairs={{0,16},{4,20},{8,24},{12,28},{16,0},{20,4},{24,8},{28,12},{1,17},{... | collective-permute-start | bytes 24584 | tf_op jit(solution)/shard_map/cond/branch_1_fun/ppermute | solution.py:621
  18.8 1.7 %collective-permute-done.3 = f32[1,2048]{1,0:T(1,128)S(1)} collective-permute-done((f32[1,2048]{1,0:T(1,128)S(1)}, f32[1,2048]{1,0:T(1,128)S(1)}, u32[]{:S(2)}, u32[]{:S(2)}) %collective-permute-start.3) | collective-permute-done | bytes 8224 | tf_op jit(solution)/shard_map/cond/branch_1_fun/ppermute | solution.py:621
  20.5 2.2 %router_gate.1 = f32[1,128]{1,0:T(1,128)} custom-call(s32[3]{0:T(128)S(1)} %get-tuple-element.44.place_ref, s32[1,128]{1,0:T(1,128)S(1)} %get-tuple-element.45.pos_ref, bf16[1,128,4096]{2,1,0:T(8,128)(2,1)} %get-tuple-element.46.x_ref, f32[1,4096]{1,0:T(1,128)S(1)} %pad_maximum_fusion.w_ref), custom_call_target="tpu_custom_call" | custom-call | flops 1 | bytes 1 | tf_op jit(solution)/shard_map/cond/branch_1_fun/router_gate/pallas_call | solution.py:320
  22.8 1.2 %collective-permute-done.4 = f32[1,128]{1,0:T(1,128)} collective-permute-done((f32[1,128]{1,0:T(1,128)}, f32[1,128]{1,0:T(1,128)}, u32[]{:S(2)}, u32[]{:S(2)}) %collective-permute-start.4) | collective-permute-done | bytes 544 | tf_op jit(solution)/shard_map/cond/branch_1_fun/ppermute | solution.py:609
  23.9 1.7 %local_stats.1.local = f32[3,8,256]{2,1,0:T(8,128)S(1)} custom-call(s32[3]{0:T(128)S(1)} %pad_add_fusion.place_ref, bf16[4,128,1024]{2,1,0:T(8,128)(2,1)S(1)} %get-tuple-element.97.mine, bf16[4,128,1024]{2,1,0:T(8,128)(2,1)S(1)} %collective-permute-done.6.sib), custom_call_target="tpu_custom_call" | custom-call | flops 1 | bytes 1 | tf_op jit(solution)/shard_map/local_stats/pallas_call | solution.py:365
  25.7 1.4 %cross_stats.1 = (bf16[4,256,512]{2,1,0:T(8,128)(2,1)S(1)}, f32[3,4,256]{2,1,0:T(4,128)S(1)}, f32[4,4,256]{2,1,0:T(4,128)S(1)}) custom-call(s32[3]{0:T(128)S(1)} %pad_add_fusion.place_ref, bf16[4,128,1024]{2,1,0:T(8,128)(2,1)S(1)} %get-tuple-element.97.mine, bf16[4,128,1024]{2,1,0:T(8,128)(2,1)S(1)} %collective-permute-done.6.sib, ...), custom_call_target="tpu_custom_call" | custom-call | flops 1 | bytes 1 | tf_op jit(solution)/shard_map/cross_stats/pallas_call | solution.py:421
  27.1 1.8 %collective-permute-start.9 = (f32[4,4,256]{2,1,0:T(4,128)S(1)}, f32[4,4,256]{2,1,0:T(4,128)S(1)}, u32[]{:S(2)}, u32[]{:S(2)}) collective-permute-start(f32[4,4,256]{2,1,0:T(4,128)S(1)} %get-tuple-element.106), channel_id=1, source_target_pairs={{0,2},{1,3},{2,0},{3,1},{4,6},{5,7},{6,4},{7,5},{8,10},{9,11},{10,... | collective-permute-start | bytes 49160 | tf_op jit(solution)/shard_map/ppermute | solution.py:609
  28.8 2.0 %collective-permute-done.9.heard = f32[4,4,256]{2,1,0:T(4,128)S(1)} collective-permute-done((f32[4,4,256]{2,1,0:T(4,128)S(1)}, f32[4,4,256]{2,1,0:T(4,128)S(1)}, u32[]{:S(2)}, u32[]{:S(2)}) %collective-permute-start.9) | collective-permute-done | bytes 16416 | tf_op jit(solution)/shard_map/ppermute | solution.py:609
  30.9 3.2 %cross_grad.1 = (bf16[2,128,512]{2,1,0:T(8,128)(2,1)S(1)}, bf16[2,128,512]{2,1,0:T(8,128)(2,1)S(1)}, bf16[3,256,512]{2,1,0:T(8,128)(2,1)}, f32[3,8,256]{2,1,0:T(...) custom-call(s32[3]{0:T(128)S(1)} %pad_add_fusion.place_ref, bf16[4,256,512]{2,1,0:T(8,128)(2,1)S(1)} %get-tuple-element.104.cross, ...), custom_call_target="tpu_custom_call" | custom-call | flops 1 | bytes 1 | tf_op jit(solution)/shard_map/cross_grad/pallas_call | solution.py:494
  34.1 1.7 %collective-permute-start.10 = (bf16[2,128,512]{2,1,0:T(8,128)(2,1)S(1)}, bf16[2,128,512]{2,1,0:T(8,128)(2,1)S(1)}, u32[]{:S(2)}, u32[]{:S(2)}) collective-permute-start(bf16[2,128,512]{2,1,0:T(8,128)(2,1)S(1)} %get-tuple-element.113), channel_id=1, source_target_pairs={{0,2},{1,3},{2,0},{3,1},{4,6},{5,7},{6,4},{7,5},{8,10},{9,11},{10,... | collective-permute-start | bytes 786440 | tf_op jit(solution)/shard_map/ppermute | solution.py:609
  35.8 16.4 %conditional.4 = (bf16[3,128,1024]{2,1,0:T(8,128)(2,1)}, bf16[3,128,1024]{2,1,0:T(8,128)(2,1)}, f32[512]{0:T(512)S(1)}) conditional(s32[]{:T(128)} %bitcast.6, () %tuple.34, (s32[1,128]{1,0:T(1,128)S(1)}, f32[1,128]{1,0:T(1,128)S(1)}, f32[1,128]{1,0:T(1,128)}, f32[1,128]{1,0:T(1,128)S(1)}, bf16[1,128,4096]{2,1,0:T(8,128)(2,1)S(1)}, ...), branch_computations={%region_2.3_spmd, %region_3.7_spmd} | conditional | flops 16388 | bytes 3416292 | solution.py:615
  37.0 1.6 %router_terms.1 = f32[8,4,1,512]{3,2,1,0:T(1,128)} custom-call(f32[1,128]{1,0:T(1,128)} %get-tuple-element.66.gate_ref, f32[1,128]{1,0:T(1,128)S(1)} %get-tuple-element.63.own_ref, f32[1,128]{1,0:T(1,128)S(1)} %collective-permute-done.5.sib_ref, bf16[1,128,4096]{2,1,0:T(8,128)(2,1)S(1)} %get-tuple-element.65.x_ref), custom_call_target="tpu_custom_call" | custom-call | flops 1 | bytes 1 | tf_op jit(solution)/shard_map/cond/branch_1_fun/router_terms/pallas_call | solution.py:591
  38.6 6.1 %all-to-all-start = ((f32[32,1,512]{2,1,0:T(1,128)}), f32[32,1,512]{2,1,0:T(1,128)S(1)}, u32[]{:S(2)}, u32[]{:S(2)}) async-start(f32[32,1,512]{2,1,0:T(1,128)} %bitcast.2), calls=%async_computation | async-start | bytes 131072 | tf_op jit(solution)/shard_map/cond/branch_1_fun/all_to_all | solution.py:633
  44.7 7.4 %conditional = (bf16[3,128,1024]{2,1,0:T(8,128)(2,1)}, bf16[3,128,1024]{2,1,0:T(8,128)(2,1)}) conditional(s32[]{:T(128)} %bitcast.1, () %tuple.23, (s32[3]{0:T(128)S(1)}, bf16[4,128,1024]{2,1,0:T(8,128)(2,1)S(1)}, bf16[4,128,1024]{2,1,0:T(8,128)(2,1)S(1)}, f32[3,8,256]{2,1,0:T(8,128)S(1)}, f32[1,128]{1,0:T(1,128)}, /*index=5*/f32[1,128]{1,0:T(1,128)}, ...), branch_computations={%region_4.4_spmd, %region_5.5_spmd} | conditional | flops 1 | bytes 3145785 | solution.py:615
  44.7 4.9 %local_grad.1 = (bf16[3,128,1024]{2,1,0:T(8,128)(2,1)}, bf16[3,128,1024]{2,1,0:T(8,128)(2,1)S(1)}) custom-call(s32[3]{0:T(128)S(1)} %get-tuple-element.48.place_ref, bf16[4,128,1024]{2,1,0:T(8,128)(2,1)S(1)} %get-tuple-element.49.mine, bf16[4,128,1024]{2,1,0:T(8,128)(2,1)S(1)} %get-tuple-element.50.sib, f32[3,8,256]{2,1,0:T(8,128)S(1)} %get-tuple-element.51.final, ...), custom_call_target="tpu_custom_call" | custom-call | flops 1 | bytes 1 | tf_op jit(solution)/shard_map/cond/branch_1_fun/cond/branch_1_fun/local_grad/pallas_call | solution.py:534
  49.9 2.2 %collective-permute-done = bf16[3,128,1024]{2,1,0:T(8,128)(2,1)} collective-permute-done((bf16[3,128,1024]{2,1,0:T(8,128)(2,1)S(1)}, bf16[3,128,1024]{2,1,0:T(8,128)(2,1)}, u32[]{:S(2)}, u32[]{:S(2)}) %collective-permute-start) | collective-permute-done | bytes 786464 | tf_op jit(solution)/shard_map/cond/branch_1_fun/cond/branch_1_fun/ppermute | solution.py:609
  52.2 3.3 %join.1 = (f32[1,128,2048]{2,1,0:T(8,128)}, f32[1,128,2048]{2,1,0:T(8,128)}, f32[1,128,2048]{2,1,0:T(8,128)}) custom-call(s32[3]{0:T(128)S(1)} %pad_add_fusion.place_ref, bf16[3,128,1024]{2,1,0:T(8,128)(2,1)} %get-tuple-element.111.own, bf16[3,128,1024]{2,1,0:T(8,128)(2,1)} %get-tuple-element.112.sib, ...), custom_call_target="tpu_custom_call" | custom-call | flops 1 | bytes 1 | tf_op jit(solution)/shard_map/join/pallas_call | solution.py:562
  (28 shorter events, 3.5 us)
Async XLA Ops:
  0.6 0.7 %copy-start.1 = (s32[1,128]{1,0:T(1,128)S(1)}, s32[1,128]{1,0:T(1,128)}, u32[]{:S(2)}) copy-start(s32[1,128]{1,0:T(1,128)} %pos_ref.1) | copy-start | bytes 1540
  4.8 19.1 %collective-permute-start.6 = (bf16[4,128,1024]{2,1,0:T(8,128)(2,1)}, bf16[4,128,1024]{2,1,0:T(8,128)(2,1)S(1)}, u32[]{:S(2)}, u32[]{:S(2)}) collective-permute-start(bf16[4,128,1024]{2,1,0:T(8,128)(2,1)} %get-tuple-element.98), channel_id=1, source_target_pairs={{0,1},{1,0},{2,3},{3,2},{4,5},{5,4},{6,7},{7,6},{8,9},{9,8},{10,11... | collective-permute-start | bytes 3145736 | tf_op jit(solution)/shard_map/ppermute | solution.py:609
  5.3 20.3 %collective-permute-start.7 = (bf16[2,128,512]{2,1,0:T(8,128)(2,1)}, bf16[2,128,512]{2,1,0:T(8,128)(2,1)S(1)}, u32[]{:S(2)}, u32[]{:S(2)}) collective-permute-start(bf16[2,128,512]{2,1,0:T(8,128)(2,1)} %get-tuple-element.99), channel_id=1, source_target_pairs={{0,2},{1,3},{2,0},{3,1},{4,6},{5,7},{6,4},{7,5},{8,10},{9,11},{10,... | collective-permute-start | bytes 786440 | tf_op jit(solution)/shard_map/ppermute | solution.py:609
  7.9 17.8 %collective-permute-start.8 = (bf16[2,128,512]{2,1,0:T(8,128)(2,1)}, bf16[2,128,512]{2,1,0:T(8,128)(2,1)S(1)}, u32[]{:S(2)}, u32[]{:S(2)}) collective-permute-start(bf16[2,128,512]{2,1,0:T(8,128)(2,1)} %get-tuple-element.100), channel_id=1, source_target_pairs={{0,3},{1,2},{2,1},{3,0},{4,7},{5,6},{6,5},{7,4},{8,11},{9,10},{10,... | collective-permute-start | bytes 786440 | tf_op jit(solution)/shard_map/ppermute | solution.py:609
  8.0 0.7 %copy-start.3 = (bf16[512]{0:T(512)(128)(2,1)S(1)}, bf16[512]{0:T(512)(128)(2,1)}, u32[]{:S(2)}) copy-start(bf16[512]{0:T(512)(128)(2,1)} %param.15) | copy-start | bytes 3076
  8.7 3.6 %collective-permute-start.1 = (f32[1,512]{1,0:T(1,128)S(1)}, f32[1,512]{1,0:T(1,128)S(1)}, u32[]{:S(2)}, u32[]{:S(2)}) collective-permute-start(f32[1,512]{1,0:T(1,128)S(1)} %bitcast.9), channel_id=1, source_target_pairs={{0,4},{4,0},{8,12},{12,8},{16,20},{20,16},{24,28},{28,24},{1,5},{5... | collective-permute-start | bytes 6152 | tf_op jit(solution)/shard_map/cond/branch_1_fun/ppermute | solution.py:621
  12.3 3.6 %collective-permute-start.2 = (f32[1,1024]{1,0:T(1,128)S(1)}, f32[1,1024]{1,0:T(1,128)S(1)}, u32[]{:S(2)}, u32[]{:S(2)}) collective-permute-start(f32[1,1024]{1,0:T(1,128)S(1)} %pad_maximum_fusion.2), channel_id=1, source_target_pairs={{0,8},{4,12},{8,0},{12,4},{16,24},{20,28},{24,16},{28,20},{1,9},{5... | collective-permute-start | bytes 12296 | tf_op jit(solution)/shard_map/cond/branch_1_fun/ppermute | solution.py:621
  15.9 4.6 %collective-permute-start.3 = (f32[1,2048]{1,0:T(1,128)S(1)}, f32[1,2048]{1,0:T(1,128)S(1)}, u32[]{:S(2)}, u32[]{:S(2)}) collective-permute-start(f32[1,2048]{1,0:T(1,128)S(1)} %pad_maximum_fusion.1), channel_id=1, source_target_pairs={{0,16},{4,20},{8,24},{12,28},{16,0},{20,4},{24,8},{28,12},{1,17},{... | collective-permute-start | bytes 24584 | tf_op jit(solution)/shard_map/cond/branch_1_fun/ppermute | solution.py:621
  22.8 1.2 %collective-permute-start.4 = (f32[1,128]{1,0:T(1,128)}, f32[1,128]{1,0:T(1,128)}, u32[]{:S(2)}, u32[]{:S(2)}) collective-permute-start(f32[1,128]{1,0:T(1,128)} %router_gate.1), channel_id=1, source_target_pairs={{0,1},{1,0},{2,3},{3,2},{4,5},{5,4},{6,7},{7,6},{8,9},{9,8},{10,11... | collective-permute-start | bytes 1544 | tf_op jit(solution)/shard_map/cond/branch_1_fun/ppermute | solution.py:609
  27.0 8.8 %copy-start = (bf16[1,128,4096]{2,1,0:T(8,128)(2,1)S(1)}, bf16[1,128,4096]{2,1,0:T(8,128)(2,1)}, u32[]{:S(2)}) copy-start(bf16[1,128,4096]{2,1,0:T(8,128)(2,1)} %param.14) | copy-start | bytes 3145732
  27.1 3.8 %collective-permute-start.9 = (f32[4,4,256]{2,1,0:T(4,128)S(1)}, f32[4,4,256]{2,1,0:T(4,128)S(1)}, u32[]{:S(2)}, u32[]{:S(2)}) collective-permute-start(f32[4,4,256]{2,1,0:T(4,128)S(1)} %get-tuple-element.106), channel_id=1, source_target_pairs={{0,2},{1,3},{2,0},{3,1},{4,6},{5,7},{6,4},{7,5},{8,10},{9,11},{10,... | collective-permute-start | bytes 49160 | tf_op jit(solution)/shard_map/ppermute | solution.py:609
  34.1 18.1 %collective-permute-start.10 = (bf16[2,128,512]{2,1,0:T(8,128)(2,1)S(1)}, bf16[2,128,512]{2,1,0:T(8,128)(2,1)S(1)}, u32[]{:S(2)}, u32[]{:S(2)}) collective-permute-start(bf16[2,128,512]{2,1,0:T(8,128)(2,1)S(1)} %get-tuple-element.113), channel_id=1, source_target_pairs={{0,2},{1,3},{2,0},{3,1},{4,6},{5,7},{6,4},{7,5},{8,10},{9,11},{10,... | collective-permute-start | bytes 786440 | tf_op jit(solution)/shard_map/ppermute | solution.py:609
  35.8 16.4 %collective-permute-start.11 = (bf16[2,128,512]{2,1,0:T(8,128)(2,1)S(1)}, bf16[2,128,512]{2,1,0:T(8,128)(2,1)S(1)}, u32[]{:S(2)}, u32[]{:S(2)}) collective-permute-start(bf16[2,128,512]{2,1,0:T(8,128)(2,1)S(1)} %get-tuple-element.114), channel_id=1, source_target_pairs={{0,3},{1,2},{2,1},{3,0},{4,7},{5,6},{6,5},{7,4},{8,11},{9,10},{10,... | collective-permute-start | bytes 786440 | tf_op jit(solution)/shard_map/ppermute | solution.py:609
  35.8 1.2 %collective-permute-start.5 = (f32[1,128]{1,0:T(1,128)S(1)}, f32[1,128]{1,0:T(1,128)S(1)}, u32[]{:S(2)}, u32[]{:S(2)}) collective-permute-start(f32[1,128]{1,0:T(1,128)S(1)} %get-tuple-element.64), channel_id=1, source_target_pairs={{0,1},{1,0},{2,3},{3,2},{4,5},{5,4},{6,7},{7,6},{8,9},{9,8},{10,11... | collective-permute-start | bytes 1544 | tf_op jit(solution)/shard_map/cond/branch_1_fun/ppermute | solution.py:609
  38.6 13.5 %all-to-all-start = ((f32[32,1,512]{2,1,0:T(1,128)}), f32[32,1,512]{2,1,0:T(1,128)S(1)}, u32[]{:S(2)}, u32[]{:S(2)}) async-start(f32[32,1,512]{2,1,0:T(1,128)} %bitcast.2), calls=%async_computation | async-start | bytes 131072 | tf_op jit(solution)/shard_map/cond/branch_1_fun/all_to_all | solution.py:633
  49.7 2.4 %collective-permute-start = (bf16[3,128,1024]{2,1,0:T(8,128)(2,1)S(1)}, bf16[3,128,1024]{2,1,0:T(8,128)(2,1)}, u32[]{:S(2)}, u32[]{:S(2)}) collective-permute-start(bf16[3,128,1024]{2,1,0:T(8,128)(2,1)S(1)} %get-tuple-element.56), channel_id=1, source_target_pairs={{0,1},{1,0},{2,3},{3,2},{4,5},{5,4},{6,7},{7,6},{8,9},{9,8},{10,11... | collective-permute-start | bytes 2359304 | tf_op jit(solution)/shard_map/cond/branch_1_fun/cond/branch_1_fun/ppermute | solution.py:609
  52.2 3.3 %copy-start.2 = (f32[512]{0:T(512)}, f32[512]{0:T(512)S(1)}, u32[]{:S(2)}) copy-start(f32[512]{0:T(512)S(1)} %get-tuple-element.96) | copy-start | bytes 6148

commit v4 on v3

--- a/solution.py
+++ b/solution.py
@@ -259,73 +259,116 @@
     return jnp.where(mask, keys.astype(F32), MARK).astype(BF16)
 
 
-def pack_all_kernel(place_ref, pos_ref, k_ref, v_ref, q_ref, dg_ref, mine, theirs, straight, diag, wide, sems):
+def cross_pack_kernel(place_ref, pos_ref, k_ref, v_ref, q_ref, dg_ref, straight, diag, wide, sems):
+    slots, width = straight.shape[1], straight.shape[2]
+    half = k_ref.shape[-1] // 2
+    core, chip = place_ref[0], place_ref[1]
+    ends = ((straight, core * half), (diag, (1 - core) * half))
+
+    def copies(first, second, targets, offset):
+        out = []
+        for i, (end, start) in enumerate(ends):
+            cols = pl.ds(pl.multiple_of(start + offset, HEAD), width)
+            out.append(pltpu.make_async_copy(first.at[0, :, cols], end.at[0], sems.at[2 * i]))
+            out.append(pltpu.make_async_copy(second.at[0, :, cols], targets[i], sems.at[2 * i + 1]))
+        for c in out:
+            c.start()
+        for c in out:
+            c.wait()
+
+    @pl.when(chip == 0)
+    def _():
+        copies(k_ref, v_ref, (straight.at[1], diag.at[1]), 0)
+        live = live_rows(pos_ref, slots)
+        for end, _ in ends:
+            end[0] = mark_dead(end[0], live)
+
+    @pl.when(chip != 0)
+    def _():
+        copies(q_ref, dg_ref, (wide.at[0], wide.at[1]), width)
+        for i, (end, _) in enumerate(ends):
+            end[1] = wide[i].astype(BF16)
+
+
+def cross_pack(place, route_pos, keys, values, queries, d_gated):
+    _, slots, full = keys.shape
+    cross = jax.ShapeDtypeStruct((2, slots, full // 4), BF16)
+    hbm = pl.BlockSpec(memory_space=pltpu.HBM)
+    return pl.pallas_call(
+        cross_pack_kernel,
+        out_shape=[cross, cross],
+        in_specs=[SMEM, VMEM, hbm, hbm, hbm, hbm],
+        out_specs=[VMEM] * 2,
+        scratch_shapes=[pltpu.VMEM((2, slots, full // 4), F32), pltpu.SemaphoreType.DMA((4,))],
+        compiler_params=params(60),
+        cost_estimate=cost(0, 10 * slots * full),
+        name="cross_pack",
+    )(place, route_pos, keys, values, queries, d_gated)
+
+
+def half_pack_kernel(place_ref, pos_ref, k_ref, v_ref, q_ref, dg_ref, mine, theirs, wide, sems):
     slots, half = mine.shape[1], mine.shape[2]
-    width = straight.shape[2]
-    core, chip = place_ref[0], place_ref[1]
-    ends = ((mine, straight, core * half), (theirs, diag, (1 - core) * half))
+    core = place_ref[0]
+    ends = ((theirs, (1 - core) * half), (mine, core * half))
     copies = []
-    for i, (out, _, start) in enumerate(ends):
+    for i, (out, start) in enumerate(ends):
         cols = pl.ds(pl.multiple_of(start, HEAD), half)
-        for j, ref in enumerate((k_ref, v_ref, q_ref)):
-            copies.append(pltpu.make_async_copy(ref.at[0, :, cols], out.at[j], sems.at[4 * i + j]))
-        copies.append(pltpu.make_async_copy(dg_ref.at[0, :, cols], wide.at[i], sems.at[4 * i + 3]))
+        copies.append(pltpu.make_async_copy(k_ref.at[0, :, cols], out.at[0], sems.at[4 * i]))
+        copies.append(pltpu.make_async_copy(dg_ref.at[0, :, cols], wide.at[i], sems.at[4 * i + 1]))
+        copies.append(pltpu.make_async_copy(v_ref.at[0, :, cols], out.at[1], sems.at[4 * i + 2]))
+        copies.append(pltpu.make_async_copy(q_ref.at[0, :, cols], out.at[2], sems.at[4 * i + 3]))
     for c in copies:
         c.start()
     live = live_rows(pos_ref, slots)
-    for i, (out, cross, _) in enumerate(ends):
-        for j in range(4):
-            copies[4 * i + j].wait()
+    for i, (out, _) in enumerate(ends):
+        copies[4 * i].wait()
         out[0] = mark_dead(out[0], live)
+        copies[4 * i + 1].wait()
         out[3] = wide[i].astype(BF16)
-
-        @pl.when(chip == 0)
-        def _():
-            cross[...] = out[0:2, :, :width]
-
-        @pl.when(chip != 0)
-        def _():
-            cross[...] = out[2:4, :, width:]
-
-
-def pack_all(place, route_pos, keys, values, queries, d_gated):
+    for i in range(2):
+        copies[4 * i + 2].wait()
+        copies[4 * i + 3].wait()
+
+
+def half_pack(place, route_pos, keys, values, queries, d_gated):
     _, slots, full = keys.shape
     half = jax.ShapeDtypeStruct((4, slots, full // 2), BF16)
-    cross = jax.ShapeDtypeStruct((2, slots, full // 4), BF16)
     hbm = pl.BlockSpec(memory_space=pltpu.HBM)
     return pl.pallas_call(
-        pack_all_kernel,
-        out_shape=[half, half, cross, cross],
+        half_pack_kernel,
+        out_shape=[half, half],
         in_specs=[SMEM, VMEM, hbm, hbm, hbm, hbm],
-        out_specs=[VMEM] * 4,
+        out_specs=[VMEM] * 2,
         scratch_shapes=[pltpu.VMEM((2, slots, full // 2), F32), pltpu.SemaphoreType.DMA((8,))],
-        compiler_params=params(60),
+        compiler_params=params(32),
         cost_estimate=cost(0, 20 * slots * full),
-        name="pack_all",
+        name="half_pack",
     )(place, route_pos, keys, values, queries, d_gated)
 
 
-def whole_gate_kernel(parts, place_ref, pos_ref, x_ref, w_ref, out_ref):
+def pair_gate_kernel(parts, place_ref, live_ref, x_ref, sib_ref, w_ref, out_ref):
     chunk = w_ref.shape[1] // parts
-    total = jnp.zeros((8, x_ref.shape[1]), F32)
-    for j in range(parts):
-        w_rows = jnp.broadcast_to(w_ref[:, j * chunk : (j + 1) * chunk], (8, chunk)).astype(BF16)
-        cols = pl.ds(pl.multiple_of((place_ref[2] ^ j) * chunk, HEAD), chunk)
-        total = total + nt(w_rows, x_ref[0, :, cols])
-    gate = 1.0 / (1.0 + jnp.exp(-total[0:1]))
-    out_ref[...] = jnp.where(pos_ref[...] >= 0, gate, 0.0)
-
-
-def whole_gate(place, route_pos, x_routed, w_full, parts):
-    return pl.pallas_call(
-        functools.partial(whole_gate_kernel, parts),
-        out_shape=jax.ShapeDtypeStruct(route_pos.shape, F32),
-        in_specs=[SMEM] + [VMEM] * 3,
+    slots = x_ref.shape[1]
+    for i, ref in enumerate((x_ref, sib_ref)):
+        total = jnp.zeros((8, slots), F32)
+        for j in range(parts):
+            w_rows = jnp.broadcast_to(w_ref[:, j * chunk : (j + 1) * chunk], (8, chunk)).astype(BF16)
+            cols = pl.ds(pl.multiple_of((place_ref[2] ^ j) * chunk, HEAD), chunk)
+            total = total + nt(w_rows, ref[0, :, cols])
+        lanes = slice(i * slots, (i + 1) * slots)
+        out_ref[:, lanes] = live_ref[:, lanes] / (1.0 + jnp.exp(-total[0:1]))
+
+
+def pair_gate(place, live, x_routed, x_sib, w_full, parts):
+    return pl.pallas_call(
+        functools.partial(pair_gate_kernel, parts),
+        out_shape=jax.ShapeDtypeStruct(live.shape, F32),
+        in_specs=[SMEM] + [VMEM] * 4,
         out_specs=VMEM,
         compiler_params=params(),
         cost_estimate=cost(16 * x_routed.size, x_routed.size * 2),
         name="router_gate",
-    )(place, route_pos, x_routed, w_full)
+    )(place, live, x_routed, x_sib, w_full)
 
 
 def local_mask(core, mine, sib):
@@ -345,40 +388,49 @@
     return jnp.concatenate([mine[part, :, cols], sib[part, :, cols]], axis=0)
 
 
-def partial_stats(scores, gw):
+def partial_stats(scores, gw, kept, stats, h):
     top = jnp.max(scores, axis=0, keepdims=True)
-    e = jnp.exp(scores - top)
-    return top, jnp.sum(e, axis=0, keepdims=True), jnp.sum(e * gw, axis=0, keepdims=True)
-
-
-def local_stats_kernel(scale, place_ref, mine, sib, stats):
+    e = jnp.exp(scores - top).astype(BF16)
+    gw = gw.astype(BF16)
+    kept[0, h] = e
+    kept[1, h] = gw
+    e = e.astype(F32)
+    stats[0, h : h + 1] = top
+    stats[1, h : h + 1] = jnp.sum(e, axis=0, keepdims=True)
+    stats[2, h : h + 1] = jnp.sum(e * gw.astype(F32), axis=0, keepdims=True)
+
+
+def local_stats_kernel(scale, place_ref, mine, sib, stats, kept, live):
+    slots = mine.shape[1]
     mask = local_mask(place_ref[0], mine, sib)
+    ones = jnp.ones((8, HEAD), BF16)
+    for i, ref in enumerate((mine, sib)):
+        marks = nt(ones, ref[0, :, :HEAD])[0:1]
+        live[:, i * slots : (i + 1) * slots] = jnp.where(marks < MARK_LIMIT, 1.0, 0.0)
     for h in range(mine.shape[-1] // HEAD):
         scores = jnp.where(mask, nt(both(mine, sib, 0, h), both(mine, sib, 2, h)) * scale, NEG_FILL)
-        gw = nt(both(mine, sib, 1, h), both(mine, sib, 3, h))
-        for i, row in enumerate(partial_stats(scores, gw)):
-            stats[i, h : h + 1] = row
+        partial_stats(scores, nt(both(mine, sib, 1, h), both(mine, sib, 3, h)), kept, stats, h)
 
 
 def local_stats(place, mine, sib):
     _, slots, half = mine.shape
+    heads = half // HEAD
     return pl.pallas_call(
         functools.partial(local_stats_kernel, HEAD**-0.5),
-        out_shape=jax.ShapeDtypeStruct((3, half // HEAD, 2 * slots), F32),
+        out_shape=[
+            jax.ShapeDtypeStruct((3, heads, 2 * slots), F32),
+            jax.ShapeDtypeStruct((2, heads, 2 * slots, 2 * slots), BF16),
+            jax.ShapeDtypeStruct((1, 2 * slots), F32),
+        ],
         in_specs=[SMEM, VMEM, VMEM],
-        out_specs=VMEM,
+        out_specs=[VMEM] * 3,
         compiler_params=params(),
         cost_estimate=cost(16 * slots * slots * half, 16 * slots * half, 4 * slots * slots * half // HEAD),
         name="local_stats",
     )(place, mine, sib)
 
 
-def cross_mask(cross, slots):
-    live = cross[0, :, :HEAD].astype(F32) < MARK_LIMIT
-    return jnp.concatenate([live] * (2 * slots // HEAD), axis=1)
-
-
-def cross_stats_kernel(scale, place_ref, mine, sib, straight, diag, local, gate_own, gate_sib, cross, stats, message):
+def cross_stats_kernel(scale, place_ref, mine, sib, straight, diag, local, gates, cross, stats, kept, message):
     slots, width = straight.shape[1], straight.shape[2]
     chip = place_ref[1]
     top, bottom = slice(0, slots), slice(slots, 2 * slots)
@@ -401,18 +453,16 @@
             cross[2 + part, top] = mine[2 + part, :, cols]
             cross[2 + part, bottom] = sib[2 + part, :, cols]
 
-    mask = cross_mask(cross, slots)
+    live = cross[0, :, :HEAD].astype(F32) < MARK_LIMIT
+    mask = jnp.concatenate([live] * (2 * slots // HEAD), axis=1)
     heads = width // HEAD
     for h in range(heads):
         cols = slice(h * HEAD, (h + 1) * HEAD)
         scores = jnp.where(mask, nt(cross[0, :, cols], cross[2, :, cols]) * scale, NEG_FILL)
-        gw = nt(cross[1, :, cols], cross[3, :, cols])
-        for i, row in enumerate(partial_stats(scores, gw)):
-            stats[i, h : h + 1] = row
-    gates = jnp.concatenate([gate_own[...], gate_sib[...]], axis=1)
+        partial_stats(scores, nt(cross[1, :, cols], cross[3, :, cols]), kept, stats, h)
     for i in range(3):
         message[i] = jnp.where(chip == 0, stats[i], local[i, heads:])
-    message[3] = jnp.broadcast_to(gates, message.shape[1:])
+    message[3] = jnp.broadcast_to(gates[...], message.shape[1:])
 
 
 def cross_stats(place, mine, sib, straight, diag, local, gates):
@@ -423,62 +473,96 @@
         out_shape=[
             jax.ShapeDtypeStruct((4, 2 * slots, width), BF16),
             jax.ShapeDtypeStruct((3, heads, 2 * slots), F32),
+            jax.ShapeDtypeStruct((2, heads, 2 * slots, 2 * slots), BF16),
             jax.ShapeDtypeStruct((4, heads, 2 * slots), F32),
         ],
-        in_specs=[SMEM] + [VMEM] * 7,
-        out_specs=[VMEM] * 3,
+        in_specs=[SMEM] + [VMEM] * 6,
+        out_specs=[VMEM] * 4,
         compiler_params=params(),
         cost_estimate=cost(16 * slots * slots * width, 32 * slots * width, 4 * slots * slots * heads),
         name="cross_stats",
-    )(place, mine, sib, straight, diag, local, *gates)
+    )(place, mine, sib, straight, diag, local, gates)
+
+
+NONE = (-3e38, 0.0, 0.0)
 
 
 def merge(first, second):
     top = jnp.maximum(first[0], second[0])
     a, b = jnp.exp(first[0] - top), jnp.exp(second[0] - top)
     inverse = 1.0 / (first[1] * a + second[1] * b)
-    return top, inverse, (first[2] * a + second[2] * b) * inverse
-
-
-def gradients(q, k, v, dg, mask, scale, top, inverse, delta, gates):
-    scores = jnp.where(mask, nt(k, q) * scale, NEG_FILL)
-    weights = jnp.exp(scores - top) * (inverse * gates)
-    ds = (weights * ((nt(v, dg) - delta) * scale)).astype(BF16)
+    return a * inverse, (first[2] * a + second[2] * b) * inverse
+
+
+def choose(flag, yes, no):
+    return [jnp.where(flag, y, n) for y, n in zip(yes, no)]
+
+
+def gradients(q, k, dg, e, gw, scale, factor, delta):
+    weights = e.astype(F32) * factor
+    ds = (weights * ((gw.astype(F32) - delta) * scale)).astype(BF16)
     return tn(ds, k), nn(ds, q), nn(weights.astype(BF16), dg)
 
 
-def cross_grad_kernel(scale, place_ref, cross, stats, local, heard, gate_own, gate_sib, straight, diag, keep, final, sum_own, sum_sib):
+def near_grad_kernel(scale, place_ref, mine, sib, kept, local, stats, gates, dq_out, own_out, sib_out, sum_out):
+    slots, width = own_out.shape[1], own_out.shape[2]
+    heads = width // HEAD
+    first = place_ref[1] == 0
+    near = [local[i, :heads] for i in range(3)]
+    factor, delta = merge(near, choose(first, NONE, [stats[i] for i in range(3)]))
+    factor = factor * gates[...]
+    sum_out[...] = jnp.sum(delta, axis=0, keepdims=True)
+    for h in range(heads):
+        cols = slice(h * HEAD, (h + 1) * HEAD)
+        row = slice(h, h + 1)
+        dq, dk, dv = gradients(
+            both(mine, sib, 2, h), both(mine, sib, 0, h), both(mine, sib, 3, h),
+            kept[0, h], kept[1, h], scale, factor[row], delta[row],
+        )
+        dq_out[:, cols] = dq
+        for i, part in enumerate((dk, dv)):
+            own_out[i, :, cols] = part[:slots].astype(BF16)
+            sib_out[i, :, cols] = part[slots:].astype(BF16)
+
+
+def near_grad(place, mine, sib, kept, local, stats, gates):
+    _, slots, half = mine.shape
+    width = half // 2
+    out = jax.ShapeDtypeStruct((2, slots, width), BF16)
+    return pl.pallas_call(
+        functools.partial(near_grad_kernel, HEAD**-0.5),
+        out_shape=[jax.ShapeDtypeStruct((2 * slots, width), F32), out, out, jax.ShapeDtypeStruct(gates.shape, F32)],
+        in_specs=[SMEM] + [VMEM] * 6,
+        out_specs=[VMEM] * 4,
+        compiler_params=params(),
+        cost_estimate=cost(20 * slots * slots * half, 40 * slots * half),
+        name="near_grad",
+    )(place, mine, sib, kept, local, stats, gates)
+
+
+def cross_grad_kernel(scale, place_ref, cross, kept, stats, local, heard, gates, near_dq, near_sum, straight, diag, dq_out, keep, final, sum_out):
     slots, width = straight.shape[1], straight.shape[2]
-    chip = place_ref[1]
     heads = width // HEAD
-    first = chip == 0
+    first = place_ref[1] == 0
+    late = jnp.where(first, 0.0, 1.0)
     mine = [stats[i] for i in range(3)]
     other = [heard[i] for i in range(3)]
     near = [local[i, :heads] for i in range(3)]
     far = [local[i, heads:] for i in range(3)]
-    none = (-3e38, 0.0, 0.0)
-    gates = jnp.concatenate([gate_own[...], gate_sib[...]], axis=1)
-    cross_gates = jnp.where(first, heard[3, 0:1], gates)
-    rows = merge(mine, [jnp.where(first, o, n) for o, n in zip(other, near)])
-    done_near = merge(near, [jnp.where(first, x, m) for x, m in zip(none, mine)])
-    done_far = merge(far, [jnp.where(first, x, o) for x, o in zip(none, other)])
-    total = jnp.zeros((1, 2 * slots), F32)
-    for i in range(3):
-        final[i, :heads] = done_near[i]
-        final[i, heads:] = done_far[i]
-    total = jnp.sum(done_near[2], axis=0, keepdims=True) + jnp.sum(done_far[2], axis=0, keepdims=True)
-    sum_own[...] = total[:, :slots]
-    sum_sib[...] = total[:, slots:]
-    mask = cross_mask(cross, slots)
+    factor, delta = merge(mine, choose(first, other, near))
+    factor = factor * jnp.where(first, heard[3], jnp.broadcast_to(gates[...], factor.shape))
+    final[0], final[1] = merge(far, choose(first, NONE, other))
+    sum_out[...] = near_sum[...] + jnp.sum(final[1], axis=0, keepdims=True)
     for h in range(heads):
         cols = slice(h * HEAD, (h + 1) * HEAD)
         row = slice(h, h + 1)
         dq, dk, dv = gradients(
-            cross[2, :, cols], cross[0, :, cols], cross[1, :, cols], cross[3, :, cols],
-            mask, scale, rows[0][row], rows[1][row], rows[2][row], cross_gates,
+            cross[2, :, cols], cross[0, :, cols], cross[3, :, cols],
+            kept[0, h], kept[1, h], scale, factor[row], delta[row],
         )
-        for i, part in enumerate((dq, dk, dv)):
-            keep[i, :, cols] = part.astype(BF16)
+        dq_out[:, cols] = (near_dq[:, cols] + late * dq).astype(BF16)
+        keep[0, :, cols] = dk.astype(BF16)
+        keep[1, :, cols] = dv.astype(BF16)
         sent = jnp.where(first, dq, dk).astype(BF16)
         straight[0, :, cols] = sent[:slots]
         diag[0, :, cols] = sent[slots:]
@@ -486,60 +570,65 @@
         diag[1, :, cols] = dv[slots:].astype(BF16)
 
 
-def cross_grad(place, cross, stats, local, heard, gates):
+def cross_grad(place, cross, kept, stats, local, heard, gates, near_dq, near_sum):
     _, rows, width = cross.shape
     slots = rows // 2
     out = jax.ShapeDtypeStruct((2, slots, width), BF16)
-    row = jax.ShapeDtypeStruct((1, slots), F32)
     return pl.pallas_call(
         functools.partial(cross_grad_kernel, HEAD**-0.5),
-        out_shape=[out, out, jax.ShapeDtypeStruct((3, rows, width), BF16), jax.ShapeDtypeStruct(local.shape, F32), row, row],
-        in_specs=[SMEM] + [VMEM] * 6,
+        out_shape=[
+            out,
+            out,
+            jax.ShapeDtypeStruct((rows, width), BF16),
+            jax.ShapeDtypeStruct((2, rows, width), BF16),
+            jax.ShapeDtypeStruct((2, width // HEAD, rows), F32),
+            jax.ShapeDtypeStruct((1, rows), F32),
+        ],
+        in_specs=[SMEM] + [VMEM] * 8,
         out_specs=[VMEM] * 6,
         compiler_params=params(),
-        cost_estimate=cost(40 * slots * slots * width, 64 * slots * width, 4 * slots * slots * width // HEAD),
+        cost_estimate=cost(24 * slots * slots * width, 64 * slots * width),
         name="cross_grad",
-    )(place, cross, stats, local, heard, *gates)
-
-
-def local_grad_kernel(scale, place_ref, mine, sib, final, gate_own, gate_sib, keep, own_out, sib_out):
+    )(place, cross, kept, stats, local, heard, gates, near_dq, near_sum)
+
+
+def far_grad_kernel(scale, place_ref, mine, sib, kept, final, gates, keep, near_dq, near_own, near_sib, own_out, sib_out):
     slots, half = mine.shape[1], mine.shape[2]
-    first = place_ref[1] == 0
-    early, late = jnp.where(first, 1.0, 0.0), jnp.where(first, 0.0, 1.0)
-    mask = local_mask(place_ref[0], mine, sib)
-    gates = jnp.concatenate([gate_own[...], gate_sib[...]], axis=1)
-    heads = half // HEAD
+    width = half // 2
+    heads = width // HEAD
+    early = jnp.where(place_ref[1] == 0, 1.0, 0.0)
+    factor = final[0] * gates[...]
+    own_out[0, :, :width] = near_dq[:slots]
+    sib_out[0, :, :width] = near_dq[slots:]
+    for i in range(2):
+        own_out[1 + i, :, :width] = near_own[i]
+        sib_out[1 + i, :, :width] = near_sib[i]
     for h in range(heads):
-        cols = slice(h * HEAD, (h + 1) * HEAD)
-        row = slice(h, h + 1)
+        cols = slice(width + h * HEAD, width + (h + 1) * HEAD)
+        at = slice(h * HEAD, (h + 1) * HEAD)
         dq, dk, dv = gradients(
-            both(mine, sib, 2, h), both(mine, sib, 0, h), both(mine, sib, 1, h), both(mine, sib, 3, h),
-            mask, scale, final[0, row], final[1, row], final[2, row], gates,
+            both(mine, sib, 2, heads + h), both(mine, sib, 0, heads + h), both(mine, sib, 3, heads + h),
+            kept[0, heads + h], kept[1, heads + h], scale, factor[h : h + 1], final[1, h : h + 1],
         )
-        at = h % (heads // 2)
-        kept = slice(at * HEAD, (at + 1) * HEAD)
-        if h < heads // 2:
-            dq = dq + late * keep[0, :, kept].astype(F32)
-        else:
-            dk = dk + early * keep[1, :, kept].astype(F32)
-            dv = dv + early * keep[2, :, kept].astype(F32)
+        dk = dk + early * keep[0, :, at].astype(F32)
+        dv = dv + early * keep[1, :, at].astype(F32)
         for i, part in enumerate((dq, dk, dv)):
             own_out[i, :, cols] = part[:slots].astype(BF16)
             sib_out[i, :, cols] = part[slots:].astype(BF16)
 
 
-def local_grad(place, mine, sib, final, gates, keep):
+def far_grad(place, mine, sib, kept, final, gates, keep, near_dq, near_own, near_sib):
     _, slots, half = mine.shape
     out = jax.ShapeDtypeStruct((3, slots, half), BF16)
     return pl.pallas_call(
-        functools.partial(local_grad_kernel, HEAD**-0.5),
+        functools.partial(far_grad_kernel, HEAD**-0.5),
         out_shape=[out, out],
-        in_specs=[SMEM] + [VMEM] * 6,
+        in_specs=[SMEM] + [VMEM] * 9,
         out_specs=[VMEM] * 2,
         compiler_params=params(),
-        cost_estimate=cost(40 * slots * slots * half, 40 * slots * half, 4 * slots * slots * half // HEAD),
-        name="local_grad",
-    )(place, mine, sib, final, *gates, keep)
+        cost_estimate=cost(20 * slots * slots * half, 40 * slots * half),
+        name="far_grad",
+    )(place, mine, sib, kept, final, gates, keep, near_dq, near_own, near_sib)
 
 
 def join_kernel(place_ref, own, sib, straight, diag, dq_out, dk_out, dv_out):
@@ -570,33 +659,35 @@
     )(place, own, sib, straight, diag)
 
 
-def whole_router_kernel(gate_ref, own_ref, sib_ref, x_ref, out_ref):
-    gate = gate_ref[...]
-    grad = (own_ref[...] + sib_ref[...]) * gate * (1.0 - gate)
+def pair_router_kernel(gates_ref, sum_ref, x_ref, sib_ref, out_ref):
+    gates = gates_ref[...]
+    grad = sum_ref[...] * gates * (1.0 - gates)
     high = grad.astype(BF16)
     rest = grad - high.astype(F32)
     mid = rest.astype(BF16)
     low = (rest - mid.astype(F32)).astype(BF16)
+    slots = x_ref.shape[1]
     row = lax.broadcasted_iota(jnp.int32, (8, grad.shape[1]), 0)
     lhs = jnp.where(row == 0, high.astype(F32), jnp.where(row == 1, mid.astype(F32), jnp.where(row == 2, low.astype(F32), 0.0)))
-    term = jnp.sum(nn(lhs.astype(BF16), x_ref[0]), axis=0, keepdims=True)
+    lhs = lhs.astype(BF16)
+    term = jnp.sum(nn(lhs[:, :slots], x_ref[0]) + nn(lhs[:, slots:], sib_ref[0]), axis=0, keepdims=True)
     parts, copies, _, chunk = out_ref.shape
     for j in range(parts):
         for i in range(copies):
             out_ref[j, i] = term[:, j * chunk : (j + 1) * chunk]
 
 
-def whole_router(gate, own, sib, x_routed, parts, copies):
+def pair_router(gates, sums, x_routed, x_sib, parts, copies):
     chunk = x_routed.shape[-1] // parts
     return pl.pallas_call(
-        whole_router_kernel,
+        pair_router_kernel,
         out_shape=jax.ShapeDtypeStruct((parts, copies, 1, chunk), F32),
         in_specs=[VMEM] * 4,
         out_specs=VMEM,
         compiler_params=params(),
-        cost_estimate=cost(16 * x_routed.size, x_routed.size * 2),
+        cost_estimate=cost(32 * x_routed.size, x_routed.size * 4),
         name="router_terms",
-    )(gate, own, sib, x_routed)
+    )(gates, sums, x_routed, x_sib)
 
 
 def swap_body(route_pos, x_routed, w_router, queries, keys, values, d_gated):
@@ -608,45 +699,59 @@
     def send(a, flip):
         return lax.ppermute(a, "ctx", [(i, i ^ flip) for i in range(n)])
 
+    def widen(part, step):
+        other = lax.ppermute(part, "dp", [(i, i ^ step) for i in range(ndp)])
+        return jnp.concatenate([part, other], axis=1)
+
     def beside(fn, *operands):
         def skip(*ops):
             return jax.tree.map(lambda o: jnp.zeros(o.shape, o.dtype), jax.eval_shape(fn, *ops))
 
         return lax.cond(route_pos[0, 0] >= -1, fn, skip, *operands)
 
-    def gate_phase(place, route_pos, x_routed, w_router):
-        w_part = w_router.reshape(1, -1).astype(F32)
-        step = 1
+    def local_phase(place, route_pos, x_routed, w_part, keys, values, queries, d_gated):
+        mine, theirs = half_pack(place, route_pos, keys, values, queries, d_gated)
+        sib, x_sib = send(theirs, 1), send(x_routed, 1)
+        step = 2
         while step < ndp:
-            w_part = jnp.concatenate([w_part, lax.ppermute(w_part, "dp", [(i, i ^ step) for i in range(ndp)])], axis=1)
+            w_part = widen(w_part, step)
+            if step == 2:
+                w_part, _ = lax.optimization_barrier((w_part, mine))
             step *= 2
-        gate = whole_gate(place, route_pos, x_routed, w_part, ndp)
-        return gate, send(gate, 1)
-
-    def grad_phase(place, mine, sib, final, gate, gate_sib, keep):
-        own_out, sib_out = local_grad(place, mine, sib, final, (gate, gate_sib), keep)
+        local, kept, live = local_stats(place, mine, sib)
+        gates = pair_gate(place, live, x_routed, x_sib, w_part, ndp)
+        return mine, sib, x_sib, local, kept, gates
+
+    def grad_phase(*operands):
+        own_out, sib_out = far_grad(*operands)
         return own_out, send(sib_out, 1)
 
-    def local_phase(place, mine, sib, final, gate, gate_sib, keep, sum_own, sum_sib, x_routed):
-        terms = whole_router(gate, sum_own, send(sum_sib, 1), x_routed, ndp, n)
+    def router_phase(gates, sums, x_routed, x_sib, place, *operands):
+        terms = pair_router(gates, sums, x_routed, x_sib, ndp, n)
         chunk = terms.shape[-1]
         shared = lax.all_to_all(terms.reshape(ndp * n, 1, chunk), ("dp", "ctx"), 0, 0, tiled=True)
-        gate, _ = lax.optimization_barrier((gate, terms))
-        own_out, sib_in = beside(grad_phase, place, mine, sib, final, gate, gate_sib, keep)
+        place, _ = lax.optimization_barrier((place, terms))
+        own_out, sib_in = beside(grad_phase, place, *operands)
         return own_out, sib_in, jnp.sum(shared, axis=0)[0] / float(ndp * n * slots // 2)
 
-    mine, theirs, out_s, out_d = pack_all(place, route_pos, keys, values, queries, d_gated)
+    w_part = w_router.reshape(1, -1).astype(F32)
+    if ndp > 1:
+        w_part = widen(w_part, 1)
+    out_s, out_d = cross_pack(place, route_pos, keys, values, queries, d_gated)
     in_s, in_d = send(out_s, 2), send(out_d, 3)
-    sib = send(theirs, 1)
-    w_late, _ = lax.optimization_barrier((w_router, mine))
-    gates = beside(gate_phase, place, route_pos, x_routed, w_late)
-    local = local_stats(place, mine, sib)
-    cross, stats, message = cross_stats(place, mine, sib, in_s, in_d, local, gates)
+    late_pos, _ = lax.optimization_barrier((route_pos, out_s))
+    mine, sib, x_sib, local, kept, gates = beside(
+        local_phase, place, late_pos, x_routed, w_part, keys, values, queries, d_gated
+    )
+    cross, stats, kept_cross, message = cross_stats(place, mine, sib, in_s, in_d, local, gates)
     heard = send(message, 2)
-    back_s, back_d, keep, final, sum_own, sum_sib = cross_grad(place, cross, stats, local, heard, gates)
+    near_dq, near_own, near_sib, near_sum = near_grad(place, mine, sib, kept, local, stats, gates)
+    back_s, back_d, dq_low, keep, final, sums = cross_grad(
+        place, cross, kept_cross, stats, local, heard, gates, near_dq, near_sum
+    )
     ret_s, ret_d = send(back_s, 2), send(back_d, 3)
     own_out, sib_in, router_grad = beside(
-        local_phase, place, mine, sib, final, *gates, keep, sum_own, sum_sib, x_routed
+        router_phase, gates, sums, x_routed, x_sib, place, mine, sib, kept, final, gates, keep, dq_low, near_own, near_sib
     )
     dq, dk, dv = join(place, own_out, sib_in, ret_s, ret_d, queries.shape)
     return dq, dk, dv, router_grad

time: 55.8 us -> 56.1 us (level)
  Pallas kernels: 21.8 us -> 26.7 us
  starting transfers between devices: 19.9 us -> 18 us
  waiting for transfers between devices: 11.5 us -> 9.78 us
  local copies, waits for them, and re-layouts: 1.26 us -> 0.05 us
    ppermute x9 -> x8, waiting for transfers between devices: 6.17 us -> 2.19 us  [send(): return lax.ppermute(a, 'ctx', [(i, i ^ flip) for i in range(n)])]
    pallas_call x4 -> x6, Pallas kernels: 12.2 us -> 16.1 us  [the longest x1 3.36 us: far_grad(): pl.pallas_call(functools.partial(far_grad_kernel, HEAD ** (-0.5)), out_sh...]
    all_to_all x1, waiting for transfers between devices: 0.01 us -> 1.58 us  [router_phase(): lax.all_to_all(terms.reshape(ndp * n, 1, chunk), ('dp', 'ctx'), 0, 0, til...]
    pallas_call x1, Pallas kernels: 1.73 us -> 2.96 us  [local_stats(): pl.pallas_call(functools.partial(local_stats_kernel, HEAD ** (-0.5)), out...]
    unnamed x8 -> x14, local copies, waits for them, and re-layouts: 1.26 us -> 0.04 us
    ppermute x9 -> x8, starting transfers between devices: 7.33 us -> 6.12 us  [send(): return lax.ppermute(a, 'ctx', [(i, i ^ flip) for i in range(n)])]
    pallas_call x1, Pallas kernels: 3.2 us -> 2.01 us  [cross_grad(): pl.pallas_call(functools.partial(cross_grad_kernel, HEAD ** (-0.5)), out_...]
    pallas_call x1, Pallas kernels: 1.35 us -> 2.35 us  [cross_stats(): pl.pallas_call(functools.partial(cross_stats_kernel, HEAD ** (-0.5)), out...]
  transfers between devices with their start and end apart: 13 -> 12, of which waited for: 7 -> 5; matrix products, arithmetic and copies ran while one was open for 0% -> 0% of each run, Pallas kernels for 19% -> 29%
where the time goes in v4:
time: 56.1 us; the launch traced here: 55.6 us
  Pallas kernels  26.7 us (48%)
  starting transfers between devices  18 us (32%)
  waiting for transfers between devices  9.78 us (17%)
  between operations  0.82 us (1%)
    ppermute x8, starting transfers between devices, send(): return lax.ppermute(a, 'ctx', [(i, i ^ flip) for i in range(n)])  6.12 us
    all_to_all x1, starting transfers between devices, router_phase(): lax.all_to_all(terms.reshape(ndp * n, 1, chunk), ('dp', 'ctx'), 0, 0, til...  6.1 us
    ppermute x3, waiting for transfers between devices, widen(): other = lax.ppermute(part, 'dp', [(i, i ^ step) for i in range(ndp)])  6.01 us
    ppermute x3, starting transfers between devices, widen(): other = lax.ppermute(part, 'dp', [(i, i ^ step) for i in range(ndp)])  5.75 us
    pallas_call x1, Pallas kernels, far_grad(): pl.pallas_call(functools.partial(far_grad_kernel, HEAD ** (-0.5)), out_sh...  3.36 us
    pallas_call x1, Pallas kernels, join(): pl.pallas_call(join_kernel, out_shape=[out] * 3, in_specs=[SMEM] + [VMEM]...  3.25 us
    pallas_call x1, Pallas kernels, local_stats(): pl.pallas_call(functools.partial(local_stats_kernel, HEAD ** (-0.5)), out...  2.96 us
    pallas_call x1, Pallas kernels, near_grad(): pl.pallas_call(functools.partial(near_grad_kernel, HEAD ** (-0.5)), out_s...  2.92 us
  transfers between devices with their start and end apart: 12, of which 5 were waited for; matrix products, arithmetic and copies ran while one was open for 0% of the time, Pallas kernels for 29%

profile of v4, /device:TPU:0, one launch (start us, length us, event | category | flops | bytes accessed | tf_op | source)
XLA Modules:
  0.0 55.6 jit_solution(8548460260134908475)
XLA Ops:
  0.8 2.8 %cross_pack.1 = (bf16[2,128,512]{2,1,0:T(8,128)(2,1)}, bf16[2,128,512]{2,1,0:T(8,128)(2,1)}) custom-call(s32[3]{0:T(128)S(1)} %pad_add_fusion.place_ref, s32[1,128]{1,0:T(1,128)} %pos_ref.1, bf16[1,128,2048]{2,1,0:T(8,128)(2,1)} %k_ref.1, bf16[1,128,2048]{2,1,0:T(8,128)(2,1)} %v_ref.1, bf16[1,128,2048]{2,1,0:T(8,128)(2,1)} %q_ref.1, f32[1,128,2048]{2,1,0:T(8,128)} %dg_ref.1), custom_call_target="tpu_custom_call" | custom-call | flops 1 | bytes 1 | tf_op jit(solution)/shard_map/cross_pack/pallas_call | solution.py:297
  3.6 2.4 %collective-permute-start.7 = (bf16[2,128,512]{2,1,0:T(8,128)(2,1)}, bf16[2,128,512]{2,1,0:T(8,128)(2,1)S(1)}, u32[]{:S(2)}, u32[]{:S(2)}) collective-permute-start(bf16[2,128,512]{2,1,0:T(8,128)(2,1)} %get-tuple-element.145), channel_id=1, source_target_pairs={{0,3},{1,2},{2,1},{3,0},{4,7},{5,6},{6,5},{7,4},{8,11},{9,10},{10,... | collective-permute-start | bytes 786440 | tf_op jit(solution)/shard_map/ppermute | solution.py:700
  6.7 1.5 %collective-permute-start.5 = (f32[1,512]{1,0:T(1,128)S(1)}, f32[1,512]{1,0:T(1,128)S(1)}, u32[]{:S(2)}, u32[]{:S(2)}) collective-permute-start(f32[1,512]{1,0:T(1,128)S(1)} %bitcast.9), channel_id=1, source_target_pairs={{0,4},{4,0},{8,12},{12,8},{16,20},{20,16},{24,28},{28,24},{1,5},{5... | collective-permute-start | bytes 6152 | tf_op jit(solution)/shard_map/ppermute | solution.py:703
  8.2 2.0 %collective-permute-done.5 = f32[1,512]{1,0:T(1,128)S(1)} collective-permute-done((f32[1,512]{1,0:T(1,128)S(1)}, f32[1,512]{1,0:T(1,128)S(1)}, u32[]{:S(2)}, u32[]{:S(2)}) %collective-permute-start.5) | collective-permute-done | bytes 2080 | tf_op jit(solution)/shard_map/ppermute | solution.py:703
  10.3 16.6 %conditional.3 = (bf16[4,128,1024]{2,1,0:T(8,128)(2,1)}, bf16[4,128,1024]{2,1,0:T(8,128)(2,1)}, bf16[1,128,4096]{2,1,0:T(8,128)(2,1)}, f32[3,8,256]{2,1,0:T(8,12...) conditional(s32[]{:T(128)} %bitcast.5, () %tuple.36, (s32[3]{0:T(128)S(1)}, ...), branch_computations={%region_0.1_spmd, %region_1.2_spmd} | conditional | flops 6147 | bytes 12681455 | solution.py:710
  10.3 2.9 %half_pack.1 = (bf16[4,128,1024]{2,1,0:T(8,128)(2,1)}, bf16[4,128,1024]{2,1,0:T(8,128)(2,1)S(1)}) custom-call(s32[3]{0:T(128)S(1)} %get-tuple-element.64.place_ref, s32[1,128]{1,0:T(1,128)S(1)} %get-tuple-element.65.pos_ref, bf16[1,128,2048]{2,1,0:T(8,128)(2,1)S(1)} %get-tuple-element.66.k_ref, bf16[1,128,2048]{2,1,0:T(8,128)(2,1)S(1)} %get-tuple-element.67.v_ref, ...), custom_call_target="tpu_custom_call" | custom-call | flops 1 | bytes 1 | tf_op jit(solution)/shard_map/cond/branch_1_fun/half_pack/pallas_call | solution.py:337
  13.8 1.6 %collective-permute-start.3 = (f32[1,1024]{1,0:T(1,128)S(1)}, f32[1,1024]{1,0:T(1,128)S(1)}, u32[]{:S(2)}, u32[]{:S(2)}) collective-permute-start(f32[1,1024]{1,0:T(1,128)S(1)} %get-tuple-element.76), channel_id=1, source_target_pairs={{0,8},{4,12},{8,0},{12,4},{16,24},{20,28},{24,16},{28,20},{1,9},{5... | collective-permute-start | bytes 12296 | tf_op jit(solution)/shard_map/cond/branch_1_fun/ppermute | solution.py:703
  15.3 2.0 %collective-permute-done.3 = f32[1,1024]{1,0:T(1,128)S(1)} collective-permute-done((f32[1,1024]{1,0:T(1,128)S(1)}, f32[1,1024]{1,0:T(1,128)S(1)}, u32[]{:S(2)}, u32[]{:S(2)}) %collective-permute-start.3) | collective-permute-done | bytes 4128 | tf_op jit(solution)/shard_map/cond/branch_1_fun/ppermute | solution.py:703
  17.4 2.7 %collective-permute-start.4 = (f32[1,2048]{1,0:T(1,128)S(1)}, f32[1,2048]{1,0:T(1,128)S(1)}, u32[]{:S(2)}, u32[]{:S(2)}) collective-permute-start(f32[1,2048]{1,0:T(1,128)S(1)} %pad_maximum_fusion.1), channel_id=1, source_target_pairs={{0,16},{4,20},{8,24},{12,28},{16,0},{20,4},{24,8},{28,12},{1,17},{... | collective-permute-start | bytes 24584 | tf_op jit(solution)/shard_map/cond/branch_1_fun/ppermute | solution.py:703
  20.0 2.0 %collective-permute-done.4 = f32[1,2048]{1,0:T(1,128)S(1)} collective-permute-done((f32[1,2048]{1,0:T(1,128)S(1)}, f32[1,2048]{1,0:T(1,128)S(1)}, u32[]{:S(2)}, u32[]{:S(2)}) %collective-permute-start.4) | collective-permute-done | bytes 8224 | tf_op jit(solution)/shard_map/cond/branch_1_fun/ppermute | solution.py:703
  22.0 3.0 %local_stats.1 = (f32[3,8,256]{2,1,0:T(8,128)S(1)}, bf16[2,8,256,256]{3,2,1,0:T(8,128)(2,1)S(1)}, f32[1,256]{1,0:T(1,128)S(1)}) custom-call(s32[3]{0:T(128)S(1)} %get-tuple-element.64.place_ref, bf16[4,128,1024]{2,1,0:T(8,128)(2,1)} %get-tuple-element.179.mine, bf16[4,128,1024]{2,1,0:T(8,128)(2,1)} %collective-permute-done.1.sib), custom_call_target="tpu_custom_call" | custom-call | flops 1 | bytes 1 | tf_op jit(solution)/shard_map/cond/branch_1_fun/local_stats/pallas_call | solution.py:418
  25.0 1.9 %router_gate.1 = f32[1,256]{1,0:T(1,128)S(1)} custom-call(s32[3]{0:T(128)S(1)} %get-tuple-element.64.place_ref, f32[1,256]{1,0:T(1,128)S(1)} %get-tuple-element.75.live_ref, bf16[1,128,4096]{2,1,0:T(8,128)(2,1)S(1)} %copy-done.1, bf16[1,128,4096]{2,1,0:T(8,128)(2,1)} %collective-permute-done.2.sib_ref, f32[1,4096]{1,0:T(1,128)S(1)} %pad_maximum_fusion.w_ref), custom_call_target="tpu_custom_call" | custom-call | flops 1 | bytes 1 | tf_op jit(solution)/shard_map/cond/branch_1_fun/router_gate/pallas_call | solution.py:363
  26.9 2.3 %cross_stats.1 = (bf16[4,256,512]{2,1,0:T(8,128)(2,1)S(1)}, f32[3,4,256]{2,1,0:T(4,128)S(1)}, bf16[2,4,256,256]{3,2,1,0:T(8,128)(2,1)S(1)}, f32[4,4,256]{2,1,0:T(4,128)S(1)}) custom-call(s32[3]{0:T(128)S(1)} %pad_add_fusion.place_ref, bf16[4,128,1024]{2,1,0:T(8,128)(2,1)} %get-tuple-element.143.mine, bf16[4,128,1024]{2,1,0:T(8,128)(2,1)} %get-tuple-element.144.sib, ...), custom_call_target="tpu_custom_call" | custom-call | flops 1 | bytes 1 | tf_op jit(solution)/shard_map/cross_stats/pallas_call | solution.py:471
  29.3 1.5 %collective-permute-start.8 = (f32[4,4,256]{2,1,0:T(4,128)S(1)}, f32[4,4,256]{2,1,0:T(4,128)S(1)}, u32[]{:S(2)}, u32[]{:S(2)}) collective-permute-start(f32[4,4,256]{2,1,0:T(4,128)S(1)} %get-tuple-element.150), channel_id=1, source_target_pairs={{0,2},{1,3},{2,0},{3,1},{4,6},{5,7},{6,4},{7,5},{8,10},{9,11},{10,... | collective-permute-start | bytes 49160 | tf_op jit(solution)/shard_map/ppermute | solution.py:700
  30.7 2.9 %near_grad.1 = (f32[256,512]{1,0:T(8,128)S(1)}, bf16[2,128,512]{2,1,0:T(8,128)(2,1)S(1)}, bf16[2,128,512]{2,1,0:T(8,128)(2,1)}, f32[1,256]{1,0:T(1,128)S(1)}) custom-call(s32[3]{0:T(128)S(1)} %pad_add_fusion.place_ref, bf16[4,128,1024]{2,1,0:T(8,128)(2,1)} %get-tuple-element.143.mine, bf16[4,128,1024]{2,1,0:T(8,128)(2,1)} %get-tuple-element.144.sib, ...), custom_call_target="tpu_custom_call" | custom-call | flops 1 | bytes 1 | tf_op jit(solution)/shard_map/near_grad/pallas_call | solution.py:532
  33.7 2.0 %cross_grad.1 = (bf16[2,128,512]{2,1,0:T(8,128)(2,1)S(1)}, bf16[2,128,512]{2,1,0:T(8,128)(2,1)S(1)}, bf16[256,512]{1,0:T(8,128)(2,1)}, bf16[2,256,512]{2,1,0:T(8...) custom-call(s32[3]{0:T(128)S(1)} %pad_add_fusion.place_ref, ...), custom_call_target="tpu_custom_call" | custom-call | flops 1 | bytes 1 | tf_op jit(solution)/shard_map/cross_grad/pallas_call | solution.py:577
  36.5 15.8 %conditional.4 = (bf16[3,128,1024]{2,1,0:T(8,128)(2,1)}, bf16[3,128,1024]{2,1,0:T(8,128)(2,1)}, f32[512]{0:T(512)S(1)}) conditional(s32[]{:T(128)} %bitcast.5, () %tuple.35, (s32[1,128]{1,0:T(1,128)S(1)}, f32[1,256]{1,0:T(1,128)S(1)}, f32[1,256]{1,0:T(1,128)S(1)}, bf16[1,128,4096]{2,1,0:T(8,128)(2,1)S(1)}, bf16[1,128,4096]{2,1,0:T(8,128)(2,1)}, ...), branch_computations={%region_2.3_spmd, %region_3.7_spmd} | conditional | flops 16388 | bytes 3414228 | solution.py:710
  36.5 2.3 %router_terms.1 = f32[8,4,1,512]{3,2,1,0:T(1,128)} custom-call(f32[1,256]{1,0:T(1,128)S(1)} %get-tuple-element.92.gates_ref, f32[1,256]{1,0:T(1,128)S(1)} %get-tuple-element.93.sum_ref, bf16[1,128,4096]{2,1,0:T(8,128)(2,1)S(1)} %get-tuple-element.94.x_ref, bf16[1,128,4096]{2,1,0:T(8,128)(2,1)} %get-tuple-element.95.sib_ref), custom_call_target="tpu_custom_call" | custom-call | flops 1 | bytes 1 | tf_op jit(solution)/shard_map/cond/branch_1_fun/router_terms/pallas_call | solution.py:682
  38.7 6.1 %all-to-all-start = ((f32[32,1,512]{2,1,0:T(1,128)}), f32[32,1,512]{2,1,0:T(1,128)S(1)}, u32[]{:S(2)}, u32[]{:S(2)}) async-start(f32[32,1,512]{2,1,0:T(1,128)} %bitcast.1), calls=%async_computation | async-start | bytes 131072 | tf_op jit(solution)/shard_map/cond/branch_1_fun/all_to_all | solution.py:732
  44.9 5.8 %conditional = (bf16[3,128,1024]{2,1,0:T(8,128)(2,1)}, bf16[3,128,1024]{2,1,0:T(8,128)(2,1)}) conditional(s32[]{:T(128)} %bitcast, () %tuple.24, (s32[3]{0:T(128)S(1)}, bf16[4,128,1024]{2,1,0:T(8,128)(2,1)}, bf16[4,128,1024]{2,1,0:T(8,128)(2,1)}, bf16[2,8,256,256]{3,2,1,0:T(8,128)(2,1)S(1)}, f32[2,4,256]{2,1,0:T(4,128)S(1)}, ...), branch_computations={%region_4.4_spmd, %region_5.5_spmd} | conditional | flops 1 | bytes 3145785 | solution.py:710
  44.9 3.4 %far_grad.1 = (bf16[3,128,1024]{2,1,0:T(8,128)(2,1)}, bf16[3,128,1024]{2,1,0:T(8,128)(2,1)S(1)}) custom-call(s32[3]{0:T(128)S(1)} %get-tuple-element.78.place_ref, bf16[4,128,1024]{2,1,0:T(8,128)(2,1)} %get-tuple-element.79.mine, bf16[4,128,1024]{2,1,0:T(8,128)(2,1)} %get-tuple-element.80.sib, bf16[2,8,256,256]{3,2,1,0:T(8,128)(2,1)S(1)} %get-tuple-element.81.kept, ...), custom_call_target="tpu_custom_call" | custom-call | flops 1 | bytes 1 | tf_op jit(solution)/shard_map/cond/branch_1_fun/cond/branch_1_fun/far_grad/pallas_call | solution.py:623
  48.5 2.2 %collective-permute-done = bf16[3,128,1024]{2,1,0:T(8,128)(2,1)} collective-permute-done((bf16[3,128,1024]{2,1,0:T(8,128)(2,1)S(1)}, bf16[3,128,1024]{2,1,0:T(8,128)(2,1)}, u32[]{:S(2)}, u32[]{:S(2)}) %collective-permute-start) | collective-permute-done | bytes 786464 | tf_op jit(solution)/shard_map/cond/branch_1_fun/cond/branch_1_fun/ppermute | solution.py:700
  50.7 1.6 %all-to-all-done = f32[32,1,512]{2,1,0:T(1,128)S(1)} async-done(((f32[32,1,512]{2,1,0:T(1,128)}), f32[32,1,512]{2,1,0:T(1,128)S(1)}, u32[]{:S(2)}, u32[]{:S(2)}) %all-to-all-start) | async-done | bytes 65568 | tf_op jit(solution)/shard_map/cond/branch_1_fun/all_to_all | solution.py:732
  52.4 3.3 %join.1 = (f32[1,128,2048]{2,1,0:T(8,128)}, f32[1,128,2048]{2,1,0:T(8,128)}, f32[1,128,2048]{2,1,0:T(8,128)}) custom-call(s32[3]{0:T(128)S(1)} %pad_add_fusion.place_ref, bf16[3,128,1024]{2,1,0:T(8,128)(2,1)} %get-tuple-element.161.own, bf16[3,128,1024]{2,1,0:T(8,128)(2,1)} %get-tuple-element.162.sib, ...), custom_call_target="tpu_custom_call" | custom-call | flops 1 | bytes 1 | tf_op jit(solution)/shard_map/join/pallas_call | solution.py:651
  (36 shorter events, 2.5 us)
Async XLA Ops:
  0.6 7.6 %copy-start.5 = (s32[1,128]{1,0:T(1,128)S(1)}, s32[1,128]{1,0:T(1,128)}, u32[]{:S(2)}) copy-start(s32[1,128]{1,0:T(1,128)} %pos_ref.1) | copy-start | bytes 1540
  0.6 9.6 %copy-start.2 = (bf16[1,128,2048]{2,1,0:T(8,128)(2,1)S(1)}, bf16[1,128,2048]{2,1,0:T(8,128)(2,1)}, u32[]{:S(2)}) copy-start(bf16[1,128,2048]{2,1,0:T(8,128)(2,1)} %k_ref.1) | copy-start | bytes 1572868
  0.7 9.6 %copy-start.4 = (bf16[1,128,2048]{2,1,0:T(8,128)(2,1)S(1)}, bf16[1,128,2048]{2,1,0:T(8,128)(2,1)}, u32[]{:S(2)}) copy-start(bf16[1,128,2048]{2,1,0:T(8,128)(2,1)} %q_ref.1) | copy-start | bytes 1572868
  0.7 6.0 %copy-start.7 = (bf16[512]{0:T(512)(128)(2,1)S(1)}, bf16[512]{0:T(512)(128)(2,1)}, u32[]{:S(2)}) copy-start(bf16[512]{0:T(512)(128)(2,1)} %param.15) | copy-start | bytes 3076
  0.7 9.6 %copy-start.3 = (bf16[1,128,2048]{2,1,0:T(8,128)(2,1)S(1)}, bf16[1,128,2048]{2,1,0:T(8,128)(2,1)}, u32[]{:S(2)}) copy-start(bf16[1,128,2048]{2,1,0:T(8,128)(2,1)} %v_ref.1) | copy-start | bytes 1572868
  3.6 23.3 %collective-permute-start.7 = (bf16[2,128,512]{2,1,0:T(8,128)(2,1)}, bf16[2,128,512]{2,1,0:T(8,128)(2,1)S(1)}, u32[]{:S(2)}, u32[]{:S(2)}) collective-permute-start(bf16[2,128,512]{2,1,0:T(8,128)(2,1)} %get-tuple-element.145), channel_id=1, source_target_pairs={{0,3},{1,2},{2,1},{3,0},{4,7},{5,6},{6,5},{7,4},{8,11},{9,10},{10,... | collective-permute-start | bytes 786440 | tf_op jit(solution)/shard_map/ppermute | solution.py:700
  6.0 20.9 %collective-permute-start.6 = (bf16[2,128,512]{2,1,0:T(8,128)(2,1)}, bf16[2,128,512]{2,1,0:T(8,128)(2,1)S(1)}, u32[]{:S(2)}, u32[]{:S(2)}) collective-permute-start(bf16[2,128,512]{2,1,0:T(8,128)(2,1)} %get-tuple-element.140), channel_id=1, source_target_pairs={{0,2},{1,3},{2,0},{3,1},{4,6},{5,7},{6,4},{7,5},{8,10},{9,11},{10,... | collective-permute-start | bytes 786440 | tf_op jit(solution)/shard_map/ppermute | solution.py:700
  6.7 3.6 %collective-permute-start.5 = (f32[1,512]{1,0:T(1,128)S(1)}, f32[1,512]{1,0:T(1,128)S(1)}, u32[]{:S(2)}, u32[]{:S(2)}) collective-permute-start(f32[1,512]{1,0:T(1,128)S(1)} %bitcast.9), channel_id=1, source_target_pairs={{0,4},{4,0},{8,12},{12,8},{16,20},{20,16},{24,28},{28,24},{1,5},{5... | collective-permute-start | bytes 6152 | tf_op jit(solution)/shard_map/ppermute | solution.py:703
  10.3 3.0 %copy-start.1 = (bf16[1,128,4096]{2,1,0:T(8,128)(2,1)S(1)}, bf16[1,128,4096]{2,1,0:T(8,128)(2,1)}, u32[]{:S(2)}) copy-start(bf16[1,128,4096]{2,1,0:T(8,128)(2,1)} %get-tuple-element.72.x_ref) | copy-start | bytes 3145732 | tf_op jit(solution)/shard_map/cond
  13.2 8.8 %collective-permute-start.1 = (bf16[4,128,1024]{2,1,0:T(8,128)(2,1)S(1)}, bf16[4,128,1024]{2,1,0:T(8,128)(2,1)}, u32[]{:S(2)}, u32[]{:S(2)}) collective-permute-start(bf16[4,128,1024]{2,1,0:T(8,128)(2,1)S(1)} %get-tuple-element.71), channel_id=1, source_target_pairs={{0,1},{1,0},{2,3},{3,2},{4,5},{5,4},{6,7},{7,6},{8,9},{9,8},{10,11... | collective-permute-start | bytes 3145736 | tf_op jit(solution)/shard_map/cond/branch_1_fun/ppermute | solution.py:700
  13.3 11.7 %collective-permute-start.2 = (bf16[1,128,4096]{2,1,0:T(8,128)(2,1)S(1)}, bf16[1,128,4096]{2,1,0:T(8,128)(2,1)}, u32[]{:S(2)}, u32[]{:S(2)}) collective-permute-start(bf16[1,128,4096]{2,1,0:T(8,128)(2,1)S(1)} %copy-done.1), channel_id=1, source_target_pairs={{0,1},{1,0},{2,3},{3,2},{4,5},{5,4},{6,7},{7,6},{8,9},{9,8},{10,11... | collective-permute-start | bytes 3145736 | tf_op jit(solution)/shard_map/cond/branch_1_fun/ppermute | solution.py:700
  13.8 3.6 %collective-permute-start.3 = (f32[1,1024]{1,0:T(1,128)S(1)}, f32[1,1024]{1,0:T(1,128)S(1)}, u32[]{:S(2)}, u32[]{:S(2)}) collective-permute-start(f32[1,1024]{1,0:T(1,128)S(1)} %get-tuple-element.76), channel_id=1, source_target_pairs={{0,8},{4,12},{8,0},{12,4},{16,24},{20,28},{24,16},{28,20},{1,9},{5... | collective-permute-start | bytes 12296 | tf_op jit(solution)/shard_map/cond/branch_1_fun/ppermute | solution.py:703
  17.4 4.6 %collective-permute-start.4 = (f32[1,2048]{1,0:T(1,128)S(1)}, f32[1,2048]{1,0:T(1,128)S(1)}, u32[]{:S(2)}, u32[]{:S(2)}) collective-permute-start(f32[1,2048]{1,0:T(1,128)S(1)} %pad_maximum_fusion.1), channel_id=1, source_target_pairs={{0,16},{4,20},{8,24},{12,28},{16,0},{20,4},{24,8},{28,12},{1,17},{... | collective-permute-start | bytes 24584 | tf_op jit(solution)/shard_map/cond/branch_1_fun/ppermute | solution.py:703
  29.3 4.4 %collective-permute-start.8 = (f32[4,4,256]{2,1,0:T(4,128)S(1)}, f32[4,4,256]{2,1,0:T(4,128)S(1)}, u32[]{:S(2)}, u32[]{:S(2)}) collective-permute-start(f32[4,4,256]{2,1,0:T(4,128)S(1)} %get-tuple-element.150), channel_id=1, source_target_pairs={{0,2},{1,3},{2,0},{3,1},{4,6},{5,7},{6,4},{7,5},{8,10},{9,11},{10,... | collective-permute-start | bytes 49160 | tf_op jit(solution)/shard_map/ppermute | solution.py:700
  33.7 2.8 %copy-start = (bf16[1,128,4096]{2,1,0:T(8,128)(2,1)S(1)}, bf16[1,128,4096]{2,1,0:T(8,128)(2,1)}, u32[]{:S(2)}) copy-start(bf16[1,128,4096]{2,1,0:T(8,128)(2,1)} %param.14) | copy-start | bytes 3145732
  35.7 16.7 %collective-permute-start.9 = (bf16[2,128,512]{2,1,0:T(8,128)(2,1)S(1)}, bf16[2,128,512]{2,1,0:T(8,128)(2,1)S(1)}, u32[]{:S(2)}, u32[]{:S(2)}) collective-permute-start(bf16[2,128,512]{2,1,0:T(8,128)(2,1)S(1)} %get-tuple-element.163), channel_id=1, source_target_pairs={{0,2},{1,3},{2,0},{3,1},{4,6},{5,7},{6,4},{7,5},{8,10},{9,11},{10,... | collective-permute-start | bytes 786440 | tf_op jit(solution)/shard_map/ppermute | solution.py:700
  36.5 15.9 %collective-permute-start.10 = (bf16[2,128,512]{2,1,0:T(8,128)(2,1)S(1)}, bf16[2,128,512]{2,1,0:T(8,128)(2,1)S(1)}, u32[]{:S(2)}, u32[]{:S(2)}) collective-permute-start(bf16[2,128,512]{2,1,0:T(8,128)(2,1)S(1)} %get-tuple-element.164), channel_id=1, source_target_pairs={{0,3},{1,2},{2,1},{3,0},{4,7},{5,6},{6,5},{7,4},{8,11},{9,10},{10,... | collective-permute-start | bytes 786440 | tf_op jit(solution)/shard_map/ppermute | solution.py:700
  38.7 13.5 %all-to-all-start = ((f32[32,1,512]{2,1,0:T(1,128)}), f32[32,1,512]{2,1,0:T(1,128)S(1)}, u32[]{:S(2)}, u32[]{:S(2)}) async-start(f32[32,1,512]{2,1,0:T(1,128)} %bitcast.1), calls=%async_computation | async-start | bytes 131072 | tf_op jit(solution)/shard_map/cond/branch_1_fun/all_to_all | solution.py:732
  48.3 2.4 %collective-permute-start = (bf16[3,128,1024]{2,1,0:T(8,128)(2,1)S(1)}, bf16[3,128,1024]{2,1,0:T(8,128)(2,1)}, u32[]{:S(2)}, u32[]{:S(2)}) collective-permute-start(bf16[3,128,1024]{2,1,0:T(8,128)(2,1)S(1)} %get-tuple-element.89), channel_id=1, source_target_pairs={{0,1},{1,0},{2,3},{3,2},{4,5},{5,4},{6,7},{7,6},{8,9},{9,8},{10,11... | collective-permute-start | bytes 2359304 | tf_op jit(solution)/shard_map/cond/branch_1_fun/cond/branch_1_fun/ppermute | solution.py:700
  52.3 3.3 %copy-start.6 = (f32[512]{0:T(512)}, f32[512]{0:T(512)S(1)}, u32[]{:S(2)}) copy-start(f32[512]{0:T(512)S(1)} %get-tuple-element.139) | copy-start | bytes 6148

commit v5 on v4

--- a/solution.py
+++ b/solution.py
@@ -306,43 +306,34 @@
     )(place, route_pos, keys, values, queries, d_gated)
 
 
-def half_pack_kernel(place_ref, pos_ref, k_ref, v_ref, q_ref, dg_ref, mine, theirs, wide, sems):
-    slots, half = mine.shape[1], mine.shape[2]
-    core = place_ref[0]
-    ends = ((theirs, (1 - core) * half), (mine, core * half))
-    copies = []
-    for i, (out, start) in enumerate(ends):
-        cols = pl.ds(pl.multiple_of(start, HEAD), half)
-        copies.append(pltpu.make_async_copy(k_ref.at[0, :, cols], out.at[0], sems.at[4 * i]))
-        copies.append(pltpu.make_async_copy(dg_ref.at[0, :, cols], wide.at[i], sems.at[4 * i + 1]))
-        copies.append(pltpu.make_async_copy(v_ref.at[0, :, cols], out.at[1], sems.at[4 * i + 2]))
-        copies.append(pltpu.make_async_copy(q_ref.at[0, :, cols], out.at[2], sems.at[4 * i + 3]))
+def sib_pack_kernel(place_ref, pos_ref, k_ref, v_ref, q_ref, dg_ref, out, wide, sems):
+    slots, half = out.shape[1], out.shape[2]
+    cols = pl.ds(pl.multiple_of((1 - place_ref[0]) * half, HEAD), half)
+    sources = ((k_ref, out.at[0]), (dg_ref, wide), (v_ref, out.at[1]), (q_ref, out.at[2]))
+    copies = [pltpu.make_async_copy(src.at[0, :, cols], dst, sems.at[i]) for i, (src, dst) in enumerate(sources)]
     for c in copies:
         c.start()
     live = live_rows(pos_ref, slots)
-    for i, (out, _) in enumerate(ends):
-        copies[4 * i].wait()
-        out[0] = mark_dead(out[0], live)
-        copies[4 * i + 1].wait()
-        out[3] = wide[i].astype(BF16)
-    for i in range(2):
-        copies[4 * i + 2].wait()
-        copies[4 * i + 3].wait()
-
-
-def half_pack(place, route_pos, keys, values, queries, d_gated):
+    copies[0].wait()
+    out[0] = mark_dead(out[0], live)
+    copies[1].wait()
+    out[3] = wide[...].astype(BF16)
+    copies[2].wait()
+    copies[3].wait()
+
+
+def sib_pack(place, route_pos, keys, values, queries, d_gated):
     _, slots, full = keys.shape
-    half = jax.ShapeDtypeStruct((4, slots, full // 2), BF16)
     hbm = pl.BlockSpec(memory_space=pltpu.HBM)
     return pl.pallas_call(
-        half_pack_kernel,
-        out_shape=[half, half],
+        sib_pack_kernel,
+        out_shape=jax.ShapeDtypeStruct((4, slots, full // 2), BF16),
         in_specs=[SMEM, VMEM, hbm, hbm, hbm, hbm],
-        out_specs=[VMEM] * 2,
-        scratch_shapes=[pltpu.VMEM((2, slots, full // 2), F32), pltpu.SemaphoreType.DMA((8,))],
-        compiler_params=params(32),
+        out_specs=VMEM,
+        scratch_shapes=[pltpu.VMEM((slots, full // 2), F32), pltpu.SemaphoreType.DMA((4,))],
+        compiler_params=params(60),
         cost_estimate=cost(0, 20 * slots * full),
-        name="half_pack",
+        name="sib_pack",
     )(place, route_pos, keys, values, queries, d_gated)
 
 
@@ -371,21 +362,16 @@
     )(place, live, x_routed, x_sib, w_full)
 
 
-def local_mask(core, mine, sib):
-    slots = mine.shape[1]
+def local_mask(core, pair):
+    slots = pair.shape[1] // 2
     key = lax.broadcasted_iota(jnp.int32, (slots, slots), 0)
     query = lax.broadcasted_iota(jnp.int32, (slots, slots), 1)
     causal = key <= query
-    own_live = mine[0, :, :slots].astype(F32) < MARK_LIMIT
-    sib_live = sib[0, :, :slots].astype(F32) < MARK_LIMIT
+    own_live = pair[0, :slots, :slots].astype(F32) < MARK_LIMIT
+    sib_live = pair[0, slots:, :slots].astype(F32) < MARK_LIMIT
     own_rows = jnp.concatenate([own_live & causal, own_live & (core == 0)], axis=1)
     sib_rows = jnp.concatenate([sib_live & (core == 1), sib_live & causal], axis=1)
     return jnp.concatenate([own_rows, sib_rows], axis=0)
-
-
-def both(mine, sib, part, h):
-    cols = slice(h * HEAD, (h + 1) * HEAD)
-    return jnp.concatenate([mine[part, :, cols], sib[part, :, cols]], axis=0)
 
 
 def partial_stats(scores, gw, kept, stats, h):
@@ -400,37 +386,65 @@
     stats[2, h : h + 1] = jnp.sum(e * gw.astype(F32), axis=0, keepdims=True)
 
 
-def local_stats_kernel(scale, place_ref, mine, sib, stats, kept, live):
-    slots = mine.shape[1]
-    mask = local_mask(place_ref[0], mine, sib)
-    ones = jnp.ones((8, HEAD), BF16)
-    for i, ref in enumerate((mine, sib)):
-        marks = nt(ones, ref[0, :, :HEAD])[0:1]
-        live[:, i * slots : (i + 1) * slots] = jnp.where(marks < MARK_LIMIT, 1.0, 0.0)
-    for h in range(mine.shape[-1] // HEAD):
-        scores = jnp.where(mask, nt(both(mine, sib, 0, h), both(mine, sib, 2, h)) * scale, NEG_FILL)
-        partial_stats(scores, nt(both(mine, sib, 1, h), both(mine, sib, 3, h)), kept, stats, h)
-
-
-def local_stats(place, mine, sib):
-    _, slots, half = mine.shape
+def local_stats_kernel(scale, place_ref, pos_ref, k_ref, v_ref, q_ref, dg_ref, sib, stats, kept, live, pair, wide, sems):
+    slots, half = sib.shape[1], sib.shape[2]
+    width = half // 2
+    core = place_ref[0]
+    own, other = slice(0, slots), slice(slots, 2 * slots)
+    stages = []
+    for g in range(2):
+        cols = slice(g * width, (g + 1) * width)
+        held = pl.ds(pl.multiple_of(core * half + g * width, HEAD), width)
+        copies = [
+            pltpu.make_async_copy(ref.at[0, :, held], pair.at[j, own, cols], sems.at[8 * g + j])
+            for j, ref in enumerate((k_ref, v_ref, q_ref))
+        ]
+        copies.append(pltpu.make_async_copy(dg_ref.at[0, :, held], wide.at[:, cols], sems.at[8 * g + 3]))
+        for j in range(4):
+            copies.append(pltpu.make_async_copy(sib.at[j, :, cols], pair.at[j, other, cols], sems.at[8 * g + 4 + j]))
+        for c in copies:
+            c.start()
+        stages.append(copies)
+    rows_live = live_rows(pos_ref, slots)
+    mask = None
+    for g in range(2):
+        cols = slice(g * width, (g + 1) * width)
+        for c in stages[g]:
+            c.wait()
+        pair[0, own, cols] = mark_dead(pair[0, own, cols], rows_live)
+        pair[3, own, cols] = wide[:, cols].astype(BF16)
+        if mask is None:
+            mask = local_mask(core, pair)
+            marks = nt(jnp.ones((8, HEAD), BF16), pair[0, :, :HEAD])[0:1]
+            live[...] = jnp.where(marks < MARK_LIMIT, 1.0, 0.0)
+        for h in range(g * width // HEAD, (g + 1) * width // HEAD):
+            at = slice(h * HEAD, (h + 1) * HEAD)
+            scores = jnp.where(mask, nt(pair[0, :, at], pair[2, :, at]) * scale, NEG_FILL)
+            partial_stats(scores, nt(pair[1, :, at], pair[3, :, at]), kept, stats, h)
+
+
+def local_stats(place, route_pos, keys, values, queries, d_gated, sib):
+    _, slots, half = sib.shape
     heads = half // HEAD
+    anywhere = pl.BlockSpec(memory_space=pl.ANY)
     return pl.pallas_call(
         functools.partial(local_stats_kernel, HEAD**-0.5),
         out_shape=[
             jax.ShapeDtypeStruct((3, heads, 2 * slots), F32),
             jax.ShapeDtypeStruct((2, heads, 2 * slots, 2 * slots), BF16),
             jax.ShapeDtypeStruct((1, 2 * slots), F32),
+            jax.ShapeDtypeStruct((4, 2 * slots, half), BF16),
         ],
-        in_specs=[SMEM, VMEM, VMEM],
-        out_specs=[VMEM] * 3,
-        compiler_params=params(),
+        in_specs=[SMEM, VMEM] + [anywhere] * 5,
+        out_specs=[VMEM] * 4,
+        scratch_shapes=[pltpu.VMEM((slots, half), F32), pltpu.SemaphoreType.DMA((16,))],
+        compiler_params=params(24),
         cost_estimate=cost(16 * slots * slots * half, 16 * slots * half, 4 * slots * slots * half // HEAD),
         name="local_stats",
-    )(place, mine, sib)
-
-
-def cross_stats_kernel(scale, place_ref, mine, sib, straight, diag, local, gates, cross, stats, kept, message):
+    )(place, route_pos, keys, values, queries, d_gated, sib)
+
+
+def cross_stats_kernel(scale, place_ref, pair, straight, diag, local, gates, cross, stats, kept, message):
     slots, width = straight.shape[1], straight.shape[2]
     chip = place_ref[1]
     top, bottom = slice(0, slots), slice(slots, 2 * slots)
@@ -439,8 +453,7 @@
     def _():
         cols = slice(width, 2 * width)
         for part in range(2):
-            cross[part, top] = mine[part, :, cols]
-            cross[part, bottom] = sib[part, :, cols]
+            cross[part] = pair[part, :, cols]
             cross[2 + part, top] = straight[part]
             cross[2 + part, bottom] = diag[part]
 
@@ -450,8 +463,7 @@
         for part in range(2):
             cross[part, top] = straight[part]
             cross[part, bottom] = diag[part]
-            cross[2 + part, top] = mine[2 + part, :, cols]
-            cross[2 + part, bottom] = sib[2 + part, :, cols]
+            cross[2 + part] = pair[2 + part, :, cols]
 
     live = cross[0, :, :HEAD].astype(F32) < MARK_LIMIT
     mask = jnp.concatenate([live] * (2 * slots // HEAD), axis=1)
@@ -465,7 +477,7 @@
     message[3] = jnp.broadcast_to(gates[...], message.shape[1:])
 
 
-def cross_stats(place, mine, sib, straight, diag, local, gates):
+def cross_stats(place, pair, straight, diag, local, gates):
     _, slots, width = straight.shape
     heads = width // HEAD
     return pl.pallas_call(
@@ -476,12 +488,12 @@
             jax.ShapeDtypeStruct((2, heads, 2 * slots, 2 * slots), BF16),
             jax.ShapeDtypeStruct((4, heads, 2 * slots), F32),
         ],
-        in_specs=[SMEM] + [VMEM] * 6,
+        in_specs=[SMEM] + [VMEM] * 5,
         out_specs=[VMEM] * 4,
         compiler_params=params(),
         cost_estimate=cost(16 * slots * slots * width, 32 * slots * width, 4 * slots * slots * heads),
         name="cross_stats",
-    )(place, mine, sib, straight, diag, local, gates)
+    )(place, pair, straight, diag, local, gates)
 
 
 NONE = (-3e38, 0.0, 0.0)
@@ -504,7 +516,7 @@
     return tn(ds, k), nn(ds, q), nn(weights.astype(BF16), dg)
 
 
-def near_grad_kernel(scale, place_ref, mine, sib, kept, local, stats, gates, dq_out, own_out, sib_out, sum_out):
+def near_grad_kernel(scale, place_ref, pair, kept, local, stats, gates, dq_out, own_out, sib_out, sum_out):
     slots, width = own_out.shape[1], own_out.shape[2]
     heads = width // HEAD
     first = place_ref[1] == 0
@@ -516,7 +528,7 @@
         cols = slice(h * HEAD, (h + 1) * HEAD)
         row = slice(h, h + 1)
         dq, dk, dv = gradients(
-            both(mine, sib, 2, h), both(mine, sib, 0, h), both(mine, sib, 3, h),
+            pair[2, :, cols], pair[0, :, cols], pair[3, :, cols],
             kept[0, h], kept[1, h], scale, factor[row], delta[row],
         )
         dq_out[:, cols] = dq
@@ -525,19 +537,20 @@
             sib_out[i, :, cols] = part[slots:].astype(BF16)
 
 
-def near_grad(place, mine, sib, kept, local, stats, gates):
-    _, slots, half = mine.shape
+def near_grad(place, pair, kept, local, stats, gates):
+    _, rows, half = pair.shape
+    slots = rows // 2
     width = half // 2
     out = jax.ShapeDtypeStruct((2, slots, width), BF16)
     return pl.pallas_call(
         functools.partial(near_grad_kernel, HEAD**-0.5),
         out_shape=[jax.ShapeDtypeStruct((2 * slots, width), F32), out, out, jax.ShapeDtypeStruct(gates.shape, F32)],
-        in_specs=[SMEM] + [VMEM] * 6,
+        in_specs=[SMEM] + [VMEM] * 5,
         out_specs=[VMEM] * 4,
         compiler_params=params(),
         cost_estimate=cost(20 * slots * slots * half, 40 * slots * half),
         name="near_grad",
-    )(place, mine, sib, kept, local, stats, gates)
+    )(place, pair, kept, local, stats, gates)
 
 
 def cross_grad_kernel(scale, place_ref, cross, kept, stats, local, heard, gates, near_dq, near_sum, straight, diag, dq_out, keep, final, sum_out):
@@ -592,8 +605,8 @@
     )(place, cross, kept, stats, local, heard, gates, near_dq, near_sum)
 
 
-def far_grad_kernel(scale, place_ref, mine, sib, kept, final, gates, keep, near_dq, near_own, near_sib, own_out, sib_out):
-    slots, half = mine.shape[1], mine.shape[2]
+def far_grad_kernel(scale, place_ref, pair, kept, final, gates, keep, near_dq, near_own, near_sib, own_out, sib_out):
+    slots, half = pair.shape[1] // 2, pair.shape[2]
     width = half // 2
     heads = width // HEAD
     early = jnp.where(place_ref[1] == 0, 1.0, 0.0)
@@ -607,7 +620,7 @@
         cols = slice(width + h * HEAD, width + (h + 1) * HEAD)
         at = slice(h * HEAD, (h + 1) * HEAD)
         dq, dk, dv = gradients(
-            both(mine, sib, 2, heads + h), both(mine, sib, 0, heads + h), both(mine, sib, 3, heads + h),
+            pair[2, :, cols], pair[0, :, cols], pair[3, :, cols],
             kept[0, heads + h], kept[1, heads + h], scale, factor[h : h + 1], final[1, h : h + 1],
         )
         dk = dk + early * keep[0, :, at].astype(F32)
@@ -617,42 +630,74 @@
             sib_out[i, :, cols] = part[slots:].astype(BF16)
 
 
-def far_grad(place, mine, sib, kept, final, gates, keep, near_dq, near_own, near_sib):
-    _, slots, half = mine.shape
+def far_grad(place, pair, kept, final, gates, keep, near_dq, near_own, near_sib):
+    _, rows, half = pair.shape
+    slots = rows // 2
     out = jax.ShapeDtypeStruct((3, slots, half), BF16)
     return pl.pallas_call(
         functools.partial(far_grad_kernel, HEAD**-0.5),
         out_shape=[out, out],
-        in_specs=[SMEM] + [VMEM] * 9,
+        in_specs=[SMEM] + [VMEM] * 8,
         out_specs=[VMEM] * 2,
         compiler_params=params(),
         cost_estimate=cost(20 * slots * slots * half, 40 * slots * half),
         name="far_grad",
-    )(place, mine, sib, kept, final, gates, keep, near_dq, near_own, near_sib)
-
-
-def join_kernel(place_ref, own, sib, straight, diag, dq_out, dk_out, dv_out):
-    half = own.shape[-1]
-    width = straight.shape[-1]
+    )(place, pair, kept, final, gates, keep, near_dq, near_own, near_sib)
+
+
+def join_kernel(place_ref, own, sib, straight, diag, dq_out, dk_out, dv_out, low, back, total, in_sems, out_sems):
+    slots, half = own.shape[1], own.shape[2]
+    width = straight.shape[2]
     core, chip = place_ref[0], place_ref[1]
     early, late = jnp.where(chip == 0, 1.0, 0.0), jnp.where(chip == 0, 0.0, 1.0)
-    for part, extra, start in ((own, straight, core * half), (sib, diag, (1 - core) * half)):
-        low = pl.ds(pl.multiple_of(start, HEAD), width)
-        high = pl.ds(pl.multiple_of(start + width, HEAD), width)
-        dq_out[0, :, low] = part[0, :, :width].astype(F32)
-        dq_out[0, :, high] = part[0, :, width:].astype(F32) + late * extra[0].astype(F32)
-        for i, out in enumerate((dk_out, dv_out)):
-            out[0, :, low] = part[1 + i, :, :width].astype(F32) + early * extra[i].astype(F32)
-            out[0, :, high] = part[1 + i, :, width:].astype(F32)
+    ends = ((own, straight, core * half), (sib, diag, (1 - core) * half))
+    loads = []
+    for i, (part, extra, _) in enumerate(ends):
+        extras = [pltpu.make_async_copy(extra.at[j], back.at[i, j], in_sems.at[5 * i + j]) for j in range(2)]
+        parts = [pltpu.make_async_copy(part.at[j], low.at[i, j], in_sems.at[5 * i + 2 + j]) for j in range(3)]
+        loads.append((parts, extras))
+    for parts, extras in loads:
+        for c in (parts[0], extras[0], parts[1], extras[1], parts[2]):
+            c.start()
+    stores = []
+    for i, (_, _, start) in enumerate(ends):
+        parts, extras = loads[i]
+        for j, out in enumerate((dq_out, dk_out, dv_out)):
+            parts[j].wait()
+            if j < 2:
+                extras[j].wait()
+            at = total.at[i, j]
+            first, second = low[i, j, :, :width].astype(F32), low[i, j, :, width:].astype(F32)
+            if j == 0:
+                at[:, :width] = first
+                at[:, width:] = second + late * back[i, 0].astype(F32)
+            else:
+                at[:, :width] = first + early * back[i, j - 1].astype(F32)
+                at[:, width:] = second
+            cols = pl.ds(pl.multiple_of(start, HEAD), half)
+            stores.append(pltpu.make_async_copy(at, out.at[0, :, cols], out_sems.at[3 * i + j]))
+            stores[-1].start()
+    for c in stores:
+        c.wait()
 
 
 def join(place, own, sib, straight, diag, shape):
     out = jax.ShapeDtypeStruct(shape, F32)
+    _, slots, half = own.shape
+    anywhere = pl.BlockSpec(memory_space=pl.ANY)
+    hbm = pl.BlockSpec(memory_space=pltpu.HBM)
     return pl.pallas_call(
         join_kernel,
         out_shape=[out] * 3,
-        in_specs=[SMEM] + [VMEM] * 4,
-        out_specs=[VMEM] * 3,
+        in_specs=[SMEM] + [anywhere] * 4,
+        out_specs=[hbm] * 3,
+        scratch_shapes=[
+            pltpu.VMEM((2, 3, slots, half), BF16),
+            pltpu.VMEM((2, 2, slots, half // 2), BF16),
+            pltpu.VMEM((2, 3, slots, half), F32),
+            pltpu.SemaphoreType.DMA((10,)),
+            pltpu.SemaphoreType.DMA((6,)),
+        ],
         compiler_params=params(),
         cost_estimate=cost(0, 18 * out.size),
         name="join",
@@ -699,28 +744,32 @@
     def send(a, flip):
         return lax.ppermute(a, "ctx", [(i, i ^ flip) for i in range(n)])
 
-    def widen(part, step):
-        other = lax.ppermute(part, "dp", [(i, i ^ step) for i in range(ndp)])
-        return jnp.concatenate([part, other], axis=1)
-
     def beside(fn, *operands):
         def skip(*ops):
             return jax.tree.map(lambda o: jnp.zeros(o.shape, o.dtype), jax.eval_shape(fn, *ops))
 
         return lax.cond(route_pos[0, 0] >= -1, fn, skip, *operands)
 
-    def local_phase(place, route_pos, x_routed, w_part, keys, values, queries, d_gated):
-        mine, theirs = half_pack(place, route_pos, keys, values, queries, d_gated)
+    def after(value, *others):
+        return lax.optimization_barrier((value, *others))[0]
+
+    def near_dp(part, step):
+        return lax.ppermute(part, "dp", [(i, i ^ step) for i in range(ndp)])
+
+    def local_phase(place, route_pos, x_routed, w_part, theirs, keys, values, queries, d_gated):
         sib, x_sib = send(theirs, 1), send(x_routed, 1)
+        results = ()
         step = 2
         while step < ndp:
-            w_part = widen(w_part, step)
-            if step == 2:
-                w_part, _ = lax.optimization_barrier((w_part, mine))
+            other = near_dp(w_part, step)
+            if 2 * step == ndp:
+                results = local_stats(place, route_pos, keys, values, queries, d_gated, sib)
+                other = after(other, *results)
+            w_part = jnp.concatenate([w_part, other], axis=1)
             step *= 2
-        local, kept, live = local_stats(place, mine, sib)
+        local, kept, live, pair = results or local_stats(place, route_pos, keys, values, queries, d_gated, sib)
         gates = pair_gate(place, live, x_routed, x_sib, w_part, ndp)
-        return mine, sib, x_sib, local, kept, gates
+        return pair, x_sib, local, kept, gates
 
     def grad_phase(*operands):
         own_out, sib_out = far_grad(*operands)
@@ -730,28 +779,27 @@
         terms = pair_router(gates, sums, x_routed, x_sib, ndp, n)
         chunk = terms.shape[-1]
         shared = lax.all_to_all(terms.reshape(ndp * n, 1, chunk), ("dp", "ctx"), 0, 0, tiled=True)
-        place, _ = lax.optimization_barrier((place, terms))
-        own_out, sib_in = beside(grad_phase, place, *operands)
+        own_out, sib_in = beside(grad_phase, after(place, terms), *operands)
         return own_out, sib_in, jnp.sum(shared, axis=0)[0] / float(ndp * n * slots // 2)
 
     w_part = w_router.reshape(1, -1).astype(F32)
-    if ndp > 1:
-        w_part = widen(w_part, 1)
     out_s, out_d = cross_pack(place, route_pos, keys, values, queries, d_gated)
     in_s, in_d = send(out_s, 2), send(out_d, 3)
-    late_pos, _ = lax.optimization_barrier((route_pos, out_s))
-    mine, sib, x_sib, local, kept, gates = beside(
-        local_phase, place, late_pos, x_routed, w_part, keys, values, queries, d_gated
+    theirs = sib_pack(place, after(route_pos, out_s), keys, values, queries, d_gated)
+    if ndp > 1:
+        w_part = jnp.concatenate([w_part, after(near_dp(w_part, 1), theirs)], axis=1)
+    pair, x_sib, local, kept, gates = beside(
+        local_phase, place, route_pos, x_routed, w_part, theirs, keys, values, queries, d_gated
     )
-    cross, stats, kept_cross, message = cross_stats(place, mine, sib, in_s, in_d, local, gates)
+    cross, stats, kept_cross, message = cross_stats(place, pair, in_s, in_d, local, gates)
     heard = send(message, 2)
-    near_dq, near_own, near_sib, near_sum = near_grad(place, mine, sib, kept, local, stats, gates)
+    near_dq, near_own, near_sib, near_sum = near_grad(place, pair, kept, local, stats, gates)
     back_s, back_d, dq_low, keep, final, sums = cross_grad(
         place, cross, kept_cross, stats, local, heard, gates, near_dq, near_sum
     )
     ret_s, ret_d = send(back_s, 2), send(back_d, 3)
     own_out, sib_in, router_grad = beside(
-        router_phase, gates, sums, x_routed, x_sib, place, mine, sib, kept, final, gates, keep, dq_low, near_own, near_sib
+        router_phase, gates, sums, x_routed, x_sib, place, pair, kept, final, gates, keep, dq_low, near_own, near_sib
     )
     dq, dk, dv = join(place, own_out, sib_in, ret_s, ret_d, queries.shape)
     return dq, dk, dv, router_grad

time: 56.1 us -> 50.2 us (0.89)
  waiting for transfers between devices: 9.78 us -> 6 us
  starting transfers between devices: 18 us -> 15.9 us
    ppermute x3, waiting for transfers between devices: 6.01 us -> 2.22 us  [near_dp(): return lax.ppermute(part, 'dp', [(i, i ^ step) for i in range(ndp)])]
    all_to_all x1, starting transfers between devices: 6.1 us -> 4.08 us  [router_phase(): lax.all_to_all(terms.reshape(ndp * n, 1, chunk), ('dp', 'ctx'), 0, 0, til...]
    pallas_call x1, Pallas kernels: 2.96 us -> 4.72 us  [local_stats(): pl.pallas_call(functools.partial(local_stats_kernel, HEAD ** (-0.5)), out...]
    pallas_call x1, Pallas kernels: 2.35 us -> 1.33 us  [cross_stats(): pl.pallas_call(functools.partial(cross_stats_kernel, HEAD ** (-0.5)), out...]
    pallas_call x2, Pallas kernels: 6.11 us -> 5.18 us  [the longest x1 3.38 us: join(): pl.pallas_call(join_kernel, out_shape=[out] * 3, in_specs=[SMEM] + [anywh...]
  transfers between devices with their start and end apart: 12 -> 12, of which waited for: 5 -> 4; matrix products, arithmetic and copies ran while one was open for 0% -> 0% of each run, Pallas kernels for 29% -> 34%
where the time goes in v5:
time: 50.2 us; the launch traced here: 49.8 us
  Pallas kernels  26.6 us (53%)
  starting transfers between devices  15.9 us (32%)
  waiting for transfers between devices  6 us (12%)
  between operations  0.83 us (2%)
    ppermute x8, starting transfers between devices, send(): return lax.ppermute(a, 'ctx', [(i, i ^ flip) for i in range(n)])  6.07 us
    ppermute x3, starting transfers between devices, near_dp(): return lax.ppermute(part, 'dp', [(i, i ^ step) for i in range(ndp)])  5.75 us
    pallas_call x1, Pallas kernels, local_stats(): pl.pallas_call(functools.partial(local_stats_kernel, HEAD ** (-0.5)), out...  4.72 us
    all_to_all x1, starting transfers between devices, router_phase(): lax.all_to_all(terms.reshape(ndp * n, 1, chunk), ('dp', 'ctx'), 0, 0, til...  4.08 us
    pallas_call x1, Pallas kernels, join(): pl.pallas_call(join_kernel, out_shape=[out] * 3, in_specs=[SMEM] + [anywh...  3.38 us
    pallas_call x1, Pallas kernels, far_grad(): pl.pallas_call(functools.partial(far_grad_kernel, HEAD ** (-0.5)), out_sh...  3.35 us
    pallas_call x1, Pallas kernels, near_grad(): pl.pallas_call(functools.partial(near_grad_kernel, HEAD ** (-0.5)), out_s...  2.98 us
    pallas_call x1, Pallas kernels, cross_pack(): pl.pallas_call(cross_pack_kernel, out_shape=[cross, cross], in_specs=[SME...  2.9 us
  transfers between devices with their start and end apart: 12, of which 4 were waited for; matrix products, arithmetic and copies ran while one was open for 0% of the time, Pallas kernels for 34%

profile of v5, /device:TPU:0, one launch (start us, length us, event | category | flops | bytes accessed | tf_op | source)
XLA Modules:
  0.0 49.8 jit_solution(17127820320428516679)
XLA Ops:
  0.8 2.9 %cross_pack.1 = (bf16[2,128,512]{2,1,0:T(8,128)(2,1)}, bf16[2,128,512]{2,1,0:T(8,128)(2,1)}) custom-call(s32[3]{0:T(128)S(1)} %pad_add_fusion.place_ref, s32[1,128]{1,0:T(1,128)} %pos_ref.2, bf16[1,128,2048]{2,1,0:T(8,128)(2,1)} %k_ref.3, bf16[1,128,2048]{2,1,0:T(8,128)(2,1)} %v_ref.3, bf16[1,128,2048]{2,1,0:T(8,128)(2,1)} %q_ref.3, f32[1,128,2048]{2,1,0:T(8,128)} %dg_ref.3), custom_call_target="tpu_custom_call" | custom-call | flops 1 | bytes 1 | tf_op jit(solution)/shard_map/cross_pack/pallas_call | solution.py:297
  3.7 2.4 %collective-permute-start.7 = (bf16[2,128,512]{2,1,0:T(8,128)(2,1)}, bf16[2,128,512]{2,1,0:T(8,128)(2,1)S(1)}, u32[]{:S(2)}, u32[]{:S(2)}) collective-permute-start(bf16[2,128,512]{2,1,0:T(8,128)(2,1)} %get-tuple-element.141), channel_id=1, source_target_pairs={{0,3},{1,2},{2,1},{3,0},{4,7},{5,6},{6,5},{7,4},{8,11},{9,10},{10,... | collective-permute-start | bytes 786440 | tf_op jit(solution)/shard_map/ppermute | solution.py:745
  6.1 0.6 %collective-permute-start.6 = (bf16[2,128,512]{2,1,0:T(8,128)(2,1)}, bf16[2,128,512]{2,1,0:T(8,128)(2,1)S(1)}, u32[]{:S(2)}, u32[]{:S(2)}) collective-permute-start(bf16[2,128,512]{2,1,0:T(8,128)(2,1)} %get-tuple-element.136), channel_id=1, source_target_pairs={{0,2},{1,3},{2,0},{3,1},{4,6},{5,7},{6,4},{7,5},{8,10},{9,11},{10,... | collective-permute-start | bytes 786440 | tf_op jit(solution)/shard_map/ppermute | solution.py:745
  6.8 1.5 %collective-permute-start.5 = (f32[1,512]{1,0:T(1,128)S(1)}, f32[1,512]{1,0:T(1,128)S(1)}, u32[]{:S(2)}, u32[]{:S(2)}) collective-permute-start(f32[1,512]{1,0:T(1,128)S(1)} %bitcast.9), channel_id=1, source_target_pairs={{0,4},{4,0},{8,12},{12,8},{16,20},{20,16},{24,28},{28,24},{1,5},{5... | collective-permute-start | bytes 6152 | tf_op jit(solution)/shard_map/ppermute | solution.py:757
  8.3 1.8 %sib_pack.1 = bf16[4,128,1024]{2,1,0:T(8,128)(2,1)} custom-call(s32[3]{0:T(128)S(1)} %pad_add_fusion.place_ref, s32[1,128]{1,0:T(1,128)S(1)} %copy-done.10, bf16[1,128,2048]{2,1,0:T(8,128)(2,1)S(1)} %copy-done.2, bf16[1,128,2048]{2,1,0:T(8,128)(2,1)S(1)} %copy-done.4, bf16[1,128,2048]{2,1,0:T(8,128)(2,1)S(1)} %copy-done.6, f32[1,128,2048]{2,1,0:T(8,128)S(1)} %copy-done), custom_call_target="tpu_custom_call" | custom-call | flops 1 | bytes 1 | tf_op jit(solution)/shard_map/sib_pack/pallas_call | solution.py:328
  10.3 13.6 %conditional.3 = (bf16[4,256,1024]{2,1,0:T(8,128)(2,1)S(1)}, bf16[1,128,4096]{2,1,0:T(8,128)(2,1)}, f32[3,8,256]{2,1,0:T(8,128)S(1)}, bf16[2,8,256,256]{3,2,1,0:T(8,128)(2,1)}, f32[1,256]{1,0:T(1,128)S(1)}) conditional(s32[]{:T(128)} %bitcast.5, () %tuple.37, (bf16[4,128,1024]{2,1,0:T(8,128)(2,1)}, s32[3]{0:T(128)S(1)}, s32[1,128]{1,0:T(1,128)S(1)}, ...), branch_computations={%region_0.1_spmd, %region_1.2_spmd} | conditional | flops 10242 | bytes 23167316 | solution.py:751
  11.0 1.6 %collective-permute-start.3 = (f32[1,1024]{1,0:T(1,128)S(1)}, f32[1,1024]{1,0:T(1,128)S(1)}, u32[]{:S(2)}, u32[]{:S(2)}) collective-permute-start(f32[1,1024]{1,0:T(1,128)S(1)} %get-tuple-element.74), channel_id=1, source_target_pairs={{0,8},{4,12},{8,0},{12,4},{16,24},{20,28},{24,16},{28,20},{1,9},{5... | collective-permute-start | bytes 12296 | tf_op jit(solution)/shard_map/cond/branch_1_fun/ppermute | solution.py:757
  12.6 2.0 %collective-permute-done.3 = f32[1,1024]{1,0:T(1,128)S(1)} collective-permute-done((f32[1,1024]{1,0:T(1,128)S(1)}, f32[1,1024]{1,0:T(1,128)S(1)}, u32[]{:S(2)}, u32[]{:S(2)}) %collective-permute-start.3) | collective-permute-done | bytes 4128 | tf_op jit(solution)/shard_map/cond/branch_1_fun/ppermute | solution.py:757
  14.6 2.7 %collective-permute-start.4 = (f32[1,2048]{1,0:T(1,128)S(1)}, f32[1,2048]{1,0:T(1,128)S(1)}, u32[]{:S(2)}, u32[]{:S(2)}) collective-permute-start(f32[1,2048]{1,0:T(1,128)S(1)} %pad_maximum_fusion.1), channel_id=1, source_target_pairs={{0,16},{4,20},{8,24},{12,28},{16,0},{20,4},{24,8},{28,12},{1,17},{... | collective-permute-start | bytes 24584 | tf_op jit(solution)/shard_map/cond/branch_1_fun/ppermute | solution.py:757
  17.3 4.7 %local_stats.1 = (f32[3,8,256]{2,1,0:T(8,128)S(1)}, bf16[2,8,256,256]{3,2,1,0:T(8,128)(2,1)}, f32[1,256]{1,0:T(1,128)S(1)}, bf16[4,256,1024]{2,1,0:T(8,128)(2,1)S(1)}) custom-call(s32[3]{0:T(128)S(1)} %get-tuple-element.62.place_ref, s32[1,128]{1,0:T(1,128)S(1)} %get-tuple-element.63.pos_ref, bf16[1,128,2048]{2,1,0:T(8,128)(2,1)} %copy-done.3, ...), custom_call_target="tpu_custom_call" | custom-call | flops 1 | bytes 1 | tf_op jit(solution)/shard_map/cond/branch_1_fun/local_stats/pallas_call | solution.py:430
  22.1 1.9 %router_gate.1 = f32[1,256]{1,0:T(1,128)S(1)} custom-call(s32[3]{0:T(128)S(1)} %get-tuple-element.62.place_ref, f32[1,256]{1,0:T(1,128)S(1)} %get-tuple-element.73.live_ref, bf16[1,128,4096]{2,1,0:T(8,128)(2,1)S(1)} %copy-done.9, bf16[1,128,4096]{2,1,0:T(8,128)(2,1)} %collective-permute-done.2.sib_ref, f32[1,4096]{1,0:T(1,128)S(1)} %pad_maximum_fusion.w_ref), custom_call_target="tpu_custom_call" | custom-call | flops 1 | bytes 1 | tf_op jit(solution)/shard_map/cond/branch_1_fun/router_gate/pallas_call | solution.py:354
  24.0 1.3 %cross_stats.1 = (bf16[4,256,512]{2,1,0:T(8,128)(2,1)S(1)}, f32[3,4,256]{2,1,0:T(4,128)S(1)}, bf16[2,4,256,256]{3,2,1,0:T(8,128)(2,1)S(1)}, f32[4,4,256]{2,1,0:T(4,128)S(1)}) custom-call(s32[3]{0:T(128)S(1)} %pad_add_fusion.place_ref, bf16[4,256,1024]{2,1,0:T(8,128)(2,1)S(1)} %get-tuple-element.140.pair, ...), custom_call_target="tpu_custom_call" | custom-call | flops 1 | bytes 1 | tf_op jit(solution)/shard_map/cross_stats/pallas_call | solution.py:483
  25.3 1.5 %collective-permute-start.8 = (f32[4,4,256]{2,1,0:T(4,128)S(1)}, f32[4,4,256]{2,1,0:T(4,128)S(1)}, u32[]{:S(2)}, u32[]{:S(2)}) collective-permute-start(f32[4,4,256]{2,1,0:T(4,128)S(1)} %get-tuple-element.146), channel_id=1, source_target_pairs={{0,2},{1,3},{2,0},{3,1},{4,6},{5,7},{6,4},{7,5},{8,10},{9,11},{10,... | collective-permute-start | bytes 49160 | tf_op jit(solution)/shard_map/ppermute | solution.py:745
  26.8 3.0 %near_grad.1 = (f32[256,512]{1,0:T(8,128)S(1)}, bf16[2,128,512]{2,1,0:T(8,128)(2,1)S(1)}, bf16[2,128,512]{2,1,0:T(8,128)(2,1)}, f32[1,256]{1,0:T(1,128)S(1)}) custom-call(s32[3]{0:T(128)S(1)} %pad_add_fusion.place_ref, bf16[4,256,1024]{2,1,0:T(8,128)(2,1)S(1)} %get-tuple-element.140.pair, bf16[2,8,256,256]{3,2,1,0:T(8,128)(2,1)} %get-tuple-element.147.kept, ...), custom_call_target="tpu_custom_call" | custom-call | flops 1 | bytes 1 | tf_op jit(solution)/shard_map/near_grad/pallas_call | solution.py:545
  29.8 2.0 %cross_grad.1 = (bf16[2,128,512]{2,1,0:T(8,128)(2,1)S(1)}, bf16[2,128,512]{2,1,0:T(8,128)(2,1)S(1)}, bf16[256,512]{1,0:T(8,128)(2,1)}, bf16[2,256,512]{2,1,0:T(8...) custom-call(s32[3]{0:T(128)S(1)} %pad_add_fusion.place_ref, ...), custom_call_target="tpu_custom_call" | custom-call | flops 1 | bytes 1 | tf_op jit(solution)/shard_map/cross_grad/pallas_call | solution.py:590
  31.8 0.8 %collective-permute-start.9 = (bf16[2,128,512]{2,1,0:T(8,128)(2,1)S(1)}, bf16[2,128,512]{2,1,0:T(8,128)(2,1)S(1)}, u32[]{:S(2)}, u32[]{:S(2)}) collective-permute-start(bf16[2,128,512]{2,1,0:T(8,128)(2,1)S(1)} %get-tuple-element.159), channel_id=1, source_target_pairs={{0,2},{1,3},{2,0},{3,1},{4,6},{5,7},{6,4},{7,5},{8,10},{9,11},{10,... | collective-permute-start | bytes 786440 | tf_op jit(solution)/shard_map/ppermute | solution.py:745
  32.5 13.8 %conditional.4 = (bf16[3,128,1024]{2,1,0:T(8,128)(2,1)}, bf16[3,128,1024]{2,1,0:T(8,128)(2,1)}, f32[512]{0:T(512)S(1)}) conditional(s32[]{:T(128)} %bitcast.5, () %tuple.36, (s32[1,128]{1,0:T(1,128)S(1)}, f32[1,256]{1,0:T(1,128)S(1)}, f32[1,256]{1,0:T(1,128)S(1)}, bf16[1,128,4096]{2,1,0:T(8,128)(2,1)S(1)}, bf16[1,128,4096]{2,1,0:T(8,128)(2,1)}, ...), branch_computations={%region_2.3_spmd, %region_3.7_spmd} | conditional | flops 16388 | bytes 3414220 | solution.py:751
  32.5 2.3 %router_terms.1 = f32[8,4,1,512]{3,2,1,0:T(1,128)} custom-call(f32[1,256]{1,0:T(1,128)S(1)} %get-tuple-element.89.gates_ref, f32[1,256]{1,0:T(1,128)S(1)} %get-tuple-element.90.sum_ref, bf16[1,128,4096]{2,1,0:T(8,128)(2,1)S(1)} %get-tuple-element.91.x_ref, bf16[1,128,4096]{2,1,0:T(8,128)(2,1)} %get-tuple-element.92.sib_ref), custom_call_target="tpu_custom_call" | custom-call | flops 1 | bytes 1 | tf_op jit(solution)/shard_map/cond/branch_1_fun/router_terms/pallas_call | solution.py:727
  34.8 4.1 %all-to-all-start = ((f32[32,1,512]{2,1,0:T(1,128)}), f32[32,1,512]{2,1,0:T(1,128)S(1)}, u32[]{:S(2)}, u32[]{:S(2)}) async-start(f32[32,1,512]{2,1,0:T(1,128)} %bitcast.1), calls=%async_computation | async-start | bytes 131072 | tf_op jit(solution)/shard_map/cond/branch_1_fun/all_to_all | solution.py:781
  38.9 5.8 %conditional = (bf16[3,128,1024]{2,1,0:T(8,128)(2,1)}, bf16[3,128,1024]{2,1,0:T(8,128)(2,1)}) conditional(s32[]{:T(128)} %bitcast, () %tuple.24, (s32[3]{0:T(128)S(1)}, bf16[4,256,1024]{2,1,0:T(8,128)(2,1)S(1)}, bf16[2,8,256,256]{3,2,1,0:T(8,128)(2,1)}, f32[2,4,256]{2,1,0:T(4,128)S(1)}, f32[1,256]{1,0:T(1,128)S(1)}, ...), branch_computations={%region_4.4_spmd, %region_5.5_spmd} | conditional | flops 1 | bytes 3145785 | solution.py:751
  38.9 3.3 %far_grad.1 = (bf16[3,128,1024]{2,1,0:T(8,128)(2,1)}, bf16[3,128,1024]{2,1,0:T(8,128)(2,1)S(1)}) custom-call(s32[3]{0:T(128)S(1)} %get-tuple-element.76.place_ref, bf16[4,256,1024]{2,1,0:T(8,128)(2,1)S(1)} %get-tuple-element.77.pair, bf16[2,8,256,256]{3,2,1,0:T(8,128)(2,1)} %get-tuple-element.78.kept, f32[2,4,256]{2,1,0:T(4,128)S(1)} %get-tuple-element.79.final, ...), custom_call_target="tpu_custom_call" | custom-call | flops 1 | bytes 1 | tf_op jit(solution)/shard_map/cond/branch_1_fun/cond/branch_1_fun/far_grad/pallas_call | solution.py:637
  42.5 2.2 %collective-permute-done = bf16[3,128,1024]{2,1,0:T(8,128)(2,1)} collective-permute-done((bf16[3,128,1024]{2,1,0:T(8,128)(2,1)S(1)}, bf16[3,128,1024]{2,1,0:T(8,128)(2,1)}, u32[]{:S(2)}, u32[]{:S(2)}) %collective-permute-start) | collective-permute-done | bytes 786464 | tf_op jit(solution)/shard_map/cond/branch_1_fun/cond/branch_1_fun/ppermute | solution.py:745
  44.7 1.6 %all-to-all-done = f32[32,1,512]{2,1,0:T(1,128)S(1)} async-done(((f32[32,1,512]{2,1,0:T(1,128)}), f32[32,1,512]{2,1,0:T(1,128)S(1)}, u32[]{:S(2)}, u32[]{:S(2)}) %all-to-all-start) | async-done | bytes 65568 | tf_op jit(solution)/shard_map/cond/branch_1_fun/all_to_all | solution.py:781
  46.4 3.4 %join.1 = (f32[1,128,2048]{2,1,0:T(8,128)}, f32[1,128,2048]{2,1,0:T(8,128)}, f32[1,128,2048]{2,1,0:T(8,128)}) custom-call(s32[3]{0:T(128)S(1)} %pad_add_fusion.place_ref, bf16[3,128,1024]{2,1,0:T(8,128)(2,1)} %get-tuple-element.157.own, bf16[3,128,1024]{2,1,0:T(8,128)(2,1)} %get-tuple-element.158.sib, ...), custom_call_target="tpu_custom_call" | custom-call | flops 1 | bytes 1 | tf_op jit(solution)/shard_map/join/pallas_call | solution.py:689
  (46 shorter events, 1.3 us)
Async XLA Ops:
  0.6 7.6 %copy-start.10 = (s32[1,128]{1,0:T(1,128)S(1)}, s32[1,128]{1,0:T(1,128)}, u32[]{:S(2)}) copy-start(s32[1,128]{1,0:T(1,128)} %pos_ref.2) | copy-start | bytes 1540
  0.6 7.6 %copy-start = (f32[1,128,2048]{2,1,0:T(8,128)S(1)}, f32[1,128,2048]{2,1,0:T(8,128)}, u32[]{:S(2)}) copy-start(f32[1,128,2048]{2,1,0:T(8,128)} %dg_ref.3) | copy-start | bytes 3145732
  0.7 7.6 %copy-start.4 = (bf16[1,128,2048]{2,1,0:T(8,128)(2,1)S(1)}, bf16[1,128,2048]{2,1,0:T(8,128)(2,1)}, u32[]{:S(2)}) copy-start(bf16[1,128,2048]{2,1,0:T(8,128)(2,1)} %v_ref.3) | copy-start | bytes 1572868
  0.7 7.6 %copy-start.2 = (bf16[1,128,2048]{2,1,0:T(8,128)(2,1)S(1)}, bf16[1,128,2048]{2,1,0:T(8,128)(2,1)}, u32[]{:S(2)}) copy-start(bf16[1,128,2048]{2,1,0:T(8,128)(2,1)} %k_ref.3) | copy-start | bytes 1572868
  0.7 7.6 %copy-start.6 = (bf16[1,128,2048]{2,1,0:T(8,128)(2,1)S(1)}, bf16[1,128,2048]{2,1,0:T(8,128)(2,1)}, u32[]{:S(2)}) copy-start(bf16[1,128,2048]{2,1,0:T(8,128)(2,1)} %q_ref.3) | copy-start | bytes 1572868
  0.7 6.1 %copy-start.12 = (bf16[512]{0:T(512)(128)(2,1)S(1)}, bf16[512]{0:T(512)(128)(2,1)}, u32[]{:S(2)}) copy-start(bf16[512]{0:T(512)(128)(2,1)} %param.15) | copy-start | bytes 3076
  3.7 20.3 %collective-permute-start.7 = (bf16[2,128,512]{2,1,0:T(8,128)(2,1)}, bf16[2,128,512]{2,1,0:T(8,128)(2,1)S(1)}, u32[]{:S(2)}, u32[]{:S(2)}) collective-permute-start(bf16[2,128,512]{2,1,0:T(8,128)(2,1)} %get-tuple-element.141), channel_id=1, source_target_pairs={{0,3},{1,2},{2,1},{3,0},{4,7},{5,6},{6,5},{7,4},{8,11},{9,10},{10,... | collective-permute-start | bytes 786440 | tf_op jit(solution)/shard_map/ppermute | solution.py:745
  6.1 17.9 %collective-permute-start.6 = (bf16[2,128,512]{2,1,0:T(8,128)(2,1)}, bf16[2,128,512]{2,1,0:T(8,128)(2,1)S(1)}, u32[]{:S(2)}, u32[]{:S(2)}) collective-permute-start(bf16[2,128,512]{2,1,0:T(8,128)(2,1)} %get-tuple-element.136), channel_id=1, source_target_pairs={{0,2},{1,3},{2,0},{3,1},{4,6},{5,7},{6,4},{7,5},{8,10},{9,11},{10,... | collective-permute-start | bytes 786440 | tf_op jit(solution)/shard_map/ppermute | solution.py:745
  6.8 3.6 %collective-permute-start.5 = (f32[1,512]{1,0:T(1,128)S(1)}, f32[1,512]{1,0:T(1,128)S(1)}, u32[]{:S(2)}, u32[]{:S(2)}) collective-permute-start(f32[1,512]{1,0:T(1,128)S(1)} %bitcast.9), channel_id=1, source_target_pairs={{0,4},{4,0},{8,12},{12,8},{16,20},{20,16},{24,28},{28,24},{1,5},{5... | collective-permute-start | bytes 6152 | tf_op jit(solution)/shard_map/ppermute | solution.py:757
  10.3 6.9 %copy-start.1 = (f32[1,128,2048]{2,1,0:T(8,128)}, f32[1,128,2048]{2,1,0:T(8,128)S(1)}, u32[]{:S(2)}) copy-start(f32[1,128,2048]{2,1,0:T(8,128)S(1)} %get-tuple-element.67.dg_ref) | copy-start | bytes 3145732 | tf_op jit(solution)/shard_map/cond
  10.4 6.9 %copy-start.3 = (bf16[1,128,2048]{2,1,0:T(8,128)(2,1)}, bf16[1,128,2048]{2,1,0:T(8,128)(2,1)S(1)}, u32[]{:S(2)}) copy-start(bf16[1,128,2048]{2,1,0:T(8,128)(2,1)S(1)} %get-tuple-element.64.k_ref) | copy-start | bytes 1572868 | tf_op jit(solution)/shard_map/cond
  10.4 6.9 %copy-start.5 = (bf16[1,128,2048]{2,1,0:T(8,128)(2,1)}, bf16[1,128,2048]{2,1,0:T(8,128)(2,1)S(1)}, u32[]{:S(2)}) copy-start(bf16[1,128,2048]{2,1,0:T(8,128)(2,1)S(1)} %get-tuple-element.65.v_ref) | copy-start | bytes 1572868 | tf_op jit(solution)/shard_map/cond
  10.4 6.9 %copy-start.7 = (bf16[1,128,2048]{2,1,0:T(8,128)(2,1)}, bf16[1,128,2048]{2,1,0:T(8,128)(2,1)S(1)}, u32[]{:S(2)}) copy-start(bf16[1,128,2048]{2,1,0:T(8,128)(2,1)S(1)} %get-tuple-element.66.q_ref) | copy-start | bytes 1572868 | tf_op jit(solution)/shard_map/cond
  10.4 11.7 %copy-start.9 = (bf16[1,128,4096]{2,1,0:T(8,128)(2,1)S(1)}, bf16[1,128,4096]{2,1,0:T(8,128)(2,1)}, u32[]{:S(2)}) copy-start(bf16[1,128,4096]{2,1,0:T(8,128)(2,1)} %get-tuple-element.70.x_ref) | copy-start | bytes 3145732 | tf_op jit(solution)/shard_map/cond
  10.4 6.9 %collective-permute-start.1 = (bf16[4,128,1024]{2,1,0:T(8,128)(2,1)}, bf16[4,128,1024]{2,1,0:T(8,128)(2,1)S(1)}, u32[]{:S(2)}, u32[]{:S(2)}) collective-permute-start(bf16[4,128,1024]{2,1,0:T(8,128)(2,1)} %get-tuple-element.68), channel_id=1, source_target_pairs={{0,1},{1,0},{2,3},{3,2},{4,5},{5,4},{6,7},{7,6},{8,9},{9,8},{10,11... | collective-permute-start | bytes 3145736 | tf_op jit(solution)/shard_map/cond/branch_1_fun/ppermute | solution.py:745
  10.5 11.6 %collective-permute-start.2 = (bf16[1,128,4096]{2,1,0:T(8,128)(2,1)}, bf16[1,128,4096]{2,1,0:T(8,128)(2,1)}, u32[]{:S(2)}, u32[]{:S(2)}) collective-permute-start(bf16[1,128,4096]{2,1,0:T(8,128)(2,1)} %get-tuple-element.70.x_ref), channel_id=1, source_target_pairs={{0,1},{1,0},{2,3},{3,2},{4,5},{5,4},{6,7},{7,6},{8,9},{9,8},{10,11... | collective-permute-start | bytes 3145736 | tf_op jit(solution)/shard_map/cond/branch_1_fun/ppermute | solution.py:745
  11.0 3.6 %collective-permute-start.3 = (f32[1,1024]{1,0:T(1,128)S(1)}, f32[1,1024]{1,0:T(1,128)S(1)}, u32[]{:S(2)}, u32[]{:S(2)}) collective-permute-start(f32[1,1024]{1,0:T(1,128)S(1)} %get-tuple-element.74), channel_id=1, source_target_pairs={{0,8},{4,12},{8,0},{12,4},{16,24},{20,28},{24,16},{28,20},{1,9},{5... | collective-permute-start | bytes 12296 | tf_op jit(solution)/shard_map/cond/branch_1_fun/ppermute | solution.py:757
  14.6 7.4 %collective-permute-start.4 = (f32[1,2048]{1,0:T(1,128)S(1)}, f32[1,2048]{1,0:T(1,128)S(1)}, u32[]{:S(2)}, u32[]{:S(2)}) collective-permute-start(f32[1,2048]{1,0:T(1,128)S(1)} %pad_maximum_fusion.1), channel_id=1, source_target_pairs={{0,16},{4,20},{8,24},{12,28},{16,0},{20,4},{24,8},{28,12},{1,17},{... | collective-permute-start | bytes 24584 | tf_op jit(solution)/shard_map/cond/branch_1_fun/ppermute | solution.py:757
  25.3 4.4 %collective-permute-start.8 = (f32[4,4,256]{2,1,0:T(4,128)S(1)}, f32[4,4,256]{2,1,0:T(4,128)S(1)}, u32[]{:S(2)}, u32[]{:S(2)}) collective-permute-start(f32[4,4,256]{2,1,0:T(4,128)S(1)} %get-tuple-element.146), channel_id=1, source_target_pairs={{0,2},{1,3},{2,0},{3,1},{4,6},{5,7},{6,4},{7,5},{8,10},{9,11},{10,... | collective-permute-start | bytes 49160 | tf_op jit(solution)/shard_map/ppermute | solution.py:745
  31.8 14.6 %collective-permute-start.9 = (bf16[2,128,512]{2,1,0:T(8,128)(2,1)S(1)}, bf16[2,128,512]{2,1,0:T(8,128)(2,1)S(1)}, u32[]{:S(2)}, u32[]{:S(2)}) collective-permute-start(bf16[2,128,512]{2,1,0:T(8,128)(2,1)S(1)} %get-tuple-element.159), channel_id=1, source_target_pairs={{0,2},{1,3},{2,0},{3,1},{4,6},{5,7},{6,4},{7,5},{8,10},{9,11},{10,... | collective-permute-start | bytes 786440 | tf_op jit(solution)/shard_map/ppermute | solution.py:745
  32.5 13.9 %collective-permute-start.10 = (bf16[2,128,512]{2,1,0:T(8,128)(2,1)S(1)}, bf16[2,128,512]{2,1,0:T(8,128)(2,1)S(1)}, u32[]{:S(2)}, u32[]{:S(2)}) collective-permute-start(bf16[2,128,512]{2,1,0:T(8,128)(2,1)S(1)} %get-tuple-element.160), channel_id=1, source_target_pairs={{0,3},{1,2},{2,1},{3,0},{4,7},{5,6},{6,5},{7,4},{8,11},{9,10},{10,... | collective-permute-start | bytes 786440 | tf_op jit(solution)/shard_map/ppermute | solution.py:745
  34.8 11.5 %all-to-all-start = ((f32[32,1,512]{2,1,0:T(1,128)}), f32[32,1,512]{2,1,0:T(1,128)S(1)}, u32[]{:S(2)}, u32[]{:S(2)}) async-start(f32[32,1,512]{2,1,0:T(1,128)} %bitcast.1), calls=%async_computation | async-start | bytes 131072 | tf_op jit(solution)/shard_map/cond/branch_1_fun/all_to_all | solution.py:781
  42.3 2.4 %collective-permute-start = (bf16[3,128,1024]{2,1,0:T(8,128)(2,1)S(1)}, bf16[3,128,1024]{2,1,0:T(8,128)(2,1)}, u32[]{:S(2)}, u32[]{:S(2)}) collective-permute-start(bf16[3,128,1024]{2,1,0:T(8,128)(2,1)S(1)} %get-tuple-element.86), channel_id=1, source_target_pairs={{0,1},{1,0},{2,3},{3,2},{4,5},{5,4},{6,7},{7,6},{8,9},{9,8},{10,11... | collective-permute-start | bytes 2359304 | tf_op jit(solution)/shard_map/cond/branch_1_fun/cond/branch_1_fun/ppermute | solution.py:745
  46.4 3.4 %copy-start.11 = (f32[512]{0:T(512)}, f32[512]{0:T(512)S(1)}, u32[]{:S(2)}) copy-start(f32[512]{0:T(512)S(1)} %get-tuple-element.135) | copy-start | bytes 6148
  (1 other events, 2.8 us)

commit v6 on v5

--- a/solution.py
+++ b/solution.py
@@ -18,12 +18,16 @@
 SMEM = pl.BlockSpec(memory_space=pltpu.SMEM)
 
 
-def params(mib=20):
+def params(mib=16):
     return pltpu.CompilerParams(vmem_limit_bytes=mib * MIB)
 
 
 def cost(flops, nbytes, exps=0):
     return pl.CostEstimate(flops=1, bytes_accessed=1, transcendentals=0)
+
+
+def in_hbm(*arrays):
+    return [pltpu.with_memory_space_constraint(a, pltpu.HBM) for a in arrays]
 
 
 def nt(a, b):
@@ -292,7 +296,7 @@
 
 def cross_pack(place, route_pos, keys, values, queries, d_gated):
     _, slots, full = keys.shape
-    cross = jax.ShapeDtypeStruct((2, slots, full // 4), BF16)
+    cross = pltpu.VMEM((2, slots, full // 4), BF16)
     hbm = pl.BlockSpec(memory_space=pltpu.HBM)
     return pl.pallas_call(
         cross_pack_kernel,
@@ -300,10 +304,10 @@
         in_specs=[SMEM, VMEM, hbm, hbm, hbm, hbm],
         out_specs=[VMEM] * 2,
         scratch_shapes=[pltpu.VMEM((2, slots, full // 4), F32), pltpu.SemaphoreType.DMA((4,))],
-        compiler_params=params(60),
+        compiler_params=params(),
         cost_estimate=cost(0, 10 * slots * full),
         name="cross_pack",
-    )(place, route_pos, keys, values, queries, d_gated)
+    )(place, route_pos, *in_hbm(keys, values, queries, d_gated))
 
 
 def sib_pack_kernel(place_ref, pos_ref, k_ref, v_ref, q_ref, dg_ref, out, wide, sems):
@@ -327,35 +331,53 @@
     hbm = pl.BlockSpec(memory_space=pltpu.HBM)
     return pl.pallas_call(
         sib_pack_kernel,
-        out_shape=jax.ShapeDtypeStruct((4, slots, full // 2), BF16),
+        out_shape=pltpu.VMEM((4, slots, full // 2), BF16),
         in_specs=[SMEM, VMEM, hbm, hbm, hbm, hbm],
         out_specs=VMEM,
         scratch_shapes=[pltpu.VMEM((slots, full // 2), F32), pltpu.SemaphoreType.DMA((4,))],
-        compiler_params=params(60),
+        compiler_params=params(),
         cost_estimate=cost(0, 20 * slots * full),
         name="sib_pack",
-    )(place, route_pos, keys, values, queries, d_gated)
-
-
-def pair_gate_kernel(parts, place_ref, live_ref, x_ref, sib_ref, w_ref, out_ref):
+    )(place, route_pos, *in_hbm(keys, values, queries, d_gated))
+
+
+def sib_chunks(sib_ref, held, sems):
+    parts = sems.shape[0]
+    chunk = held.shape[1] // parts
+    copies = []
+    for j in range(parts):
+        cols = slice(j * chunk, (j + 1) * chunk)
+        copies.append(pltpu.make_async_copy(sib_ref.at[0, :, cols], held.at[:, cols], sems.at[j]))
+    for c in copies:
+        c.start()
+    return copies
+
+
+def pair_gate_kernel(parts, place_ref, live_ref, x_ref, sib_ref, w_ref, out_ref, held, sems):
     chunk = w_ref.shape[1] // parts
     slots = x_ref.shape[1]
-    for i, ref in enumerate((x_ref, sib_ref)):
+    copies = sib_chunks(sib_ref, held, sems)
+    for i in range(2):
         total = jnp.zeros((8, slots), F32)
+        if i == 1:
+            for c in copies:
+                c.wait()
         for j in range(parts):
             w_rows = jnp.broadcast_to(w_ref[:, j * chunk : (j + 1) * chunk], (8, chunk)).astype(BF16)
             cols = pl.ds(pl.multiple_of((place_ref[2] ^ j) * chunk, HEAD), chunk)
-            total = total + nt(w_rows, ref[0, :, cols])
+            total = total + nt(w_rows, x_ref[0, :, cols] if i == 0 else held[:, cols])
         lanes = slice(i * slots, (i + 1) * slots)
         out_ref[:, lanes] = live_ref[:, lanes] / (1.0 + jnp.exp(-total[0:1]))
 
 
 def pair_gate(place, live, x_routed, x_sib, w_full, parts):
+    _, slots, depth = x_routed.shape
     return pl.pallas_call(
         functools.partial(pair_gate_kernel, parts),
         out_shape=jax.ShapeDtypeStruct(live.shape, F32),
-        in_specs=[SMEM] + [VMEM] * 4,
+        in_specs=[SMEM, VMEM, VMEM, pl.BlockSpec(memory_space=pl.ANY), VMEM],
         out_specs=VMEM,
+        scratch_shapes=[pltpu.VMEM((slots, depth), BF16), pltpu.SemaphoreType.DMA((4,))],
         compiler_params=params(),
         cost_estimate=cost(16 * x_routed.size, x_routed.size * 2),
         name="router_gate",
@@ -374,7 +396,7 @@
     return jnp.concatenate([own_rows, sib_rows], axis=0)
 
 
-def partial_stats(scores, gw, kept, stats, h):
+def kept_stats(scores, gw, kept, stats, h):
     top = jnp.max(scores, axis=0, keepdims=True)
     e = jnp.exp(scores - top).astype(BF16)
     gw = gw.astype(BF16)
@@ -386,7 +408,15 @@
     stats[2, h : h + 1] = jnp.sum(e * gw.astype(F32), axis=0, keepdims=True)
 
 
-def local_stats_kernel(scale, place_ref, pos_ref, k_ref, v_ref, q_ref, dg_ref, sib, stats, kept, live, pair, wide, sems):
+def partial_stats(scores, gw, stats, h):
+    top = jnp.max(scores, axis=0, keepdims=True)
+    e = jnp.exp(scores - top)
+    stats[0, h : h + 1] = top
+    stats[1, h : h + 1] = jnp.sum(e, axis=0, keepdims=True)
+    stats[2, h : h + 1] = jnp.sum(e * gw, axis=0, keepdims=True)
+
+
+def local_stats_kernel(scale, place_ref, pos_ref, k_ref, v_ref, q_ref, dg_ref, sib, stats, live, pair, wide, sems):
     slots, half = sib.shape[1], sib.shape[2]
     width = half // 2
     core = place_ref[0]
@@ -420,7 +450,7 @@
         for h in range(g * width // HEAD, (g + 1) * width // HEAD):
             at = slice(h * HEAD, (h + 1) * HEAD)
             scores = jnp.where(mask, nt(pair[0, :, at], pair[2, :, at]) * scale, NEG_FILL)
-            partial_stats(scores, nt(pair[1, :, at], pair[3, :, at]), kept, stats, h)
+            partial_stats(scores, nt(pair[1, :, at], pair[3, :, at]), stats, h)
 
 
 def local_stats(place, route_pos, keys, values, queries, d_gated, sib):
@@ -431,17 +461,16 @@
         functools.partial(local_stats_kernel, HEAD**-0.5),
         out_shape=[
             jax.ShapeDtypeStruct((3, heads, 2 * slots), F32),
-            jax.ShapeDtypeStruct((2, heads, 2 * slots, 2 * slots), BF16),
             jax.ShapeDtypeStruct((1, 2 * slots), F32),
             jax.ShapeDtypeStruct((4, 2 * slots, half), BF16),
         ],
         in_specs=[SMEM, VMEM] + [anywhere] * 5,
-        out_specs=[VMEM] * 4,
+        out_specs=[VMEM] * 3,
         scratch_shapes=[pltpu.VMEM((slots, half), F32), pltpu.SemaphoreType.DMA((16,))],
-        compiler_params=params(24),
+        compiler_params=params(),
         cost_estimate=cost(16 * slots * slots * half, 16 * slots * half, 4 * slots * slots * half // HEAD),
         name="local_stats",
-    )(place, route_pos, keys, values, queries, d_gated, sib)
+    )(place, route_pos, *in_hbm(keys, values, queries, d_gated), sib)
 
 
 def cross_stats_kernel(scale, place_ref, pair, straight, diag, local, gates, cross, stats, kept, message):
@@ -471,7 +500,7 @@
     for h in range(heads):
         cols = slice(h * HEAD, (h + 1) * HEAD)
         scores = jnp.where(mask, nt(cross[0, :, cols], cross[2, :, cols]) * scale, NEG_FILL)
-        partial_stats(scores, nt(cross[1, :, cols], cross[3, :, cols]), kept, stats, h)
+        kept_stats(scores, nt(cross[1, :, cols], cross[3, :, cols]), kept, stats, h)
     for i in range(3):
         message[i] = jnp.where(chip == 0, stats[i], local[i, heads:])
     message[3] = jnp.broadcast_to(gates[...], message.shape[1:])
@@ -511,12 +540,19 @@
 
 
 def gradients(q, k, dg, e, gw, scale, factor, delta):
-    weights = e.astype(F32) * factor
-    ds = (weights * ((gw.astype(F32) - delta) * scale)).astype(BF16)
+    weights = e * factor
+    ds = (weights * ((gw - delta) * scale)).astype(BF16)
     return tn(ds, k), nn(ds, q), nn(weights.astype(BF16), dg)
 
 
-def near_grad_kernel(scale, place_ref, pair, kept, local, stats, gates, dq_out, own_out, sib_out, sum_out):
+def local_gradients(pair, h, mask, scale, top, factor, delta):
+    cols = slice(h * HEAD, (h + 1) * HEAD)
+    k, v, q, dg = [pair[i, :, cols] for i in range(4)]
+    e = jnp.exp(jnp.where(mask, nt(k, q) * scale, NEG_FILL) - top)
+    return gradients(q, k, dg, e, nt(v, dg), scale, factor, delta)
+
+
+def near_grad_kernel(scale, place_ref, pair, local, stats, gates, dq_out, own_out, sib_out, sum_out):
     slots, width = own_out.shape[1], own_out.shape[2]
     heads = width // HEAD
     first = place_ref[1] == 0
@@ -524,20 +560,18 @@
     factor, delta = merge(near, choose(first, NONE, [stats[i] for i in range(3)]))
     factor = factor * gates[...]
     sum_out[...] = jnp.sum(delta, axis=0, keepdims=True)
+    mask = local_mask(place_ref[0], pair)
     for h in range(heads):
         cols = slice(h * HEAD, (h + 1) * HEAD)
         row = slice(h, h + 1)
-        dq, dk, dv = gradients(
-            pair[2, :, cols], pair[0, :, cols], pair[3, :, cols],
-            kept[0, h], kept[1, h], scale, factor[row], delta[row],
-        )
+        dq, dk, dv = local_gradients(pair, h, mask, scale, near[0][row], factor[row], delta[row])
         dq_out[:, cols] = dq
         for i, part in enumerate((dk, dv)):
             own_out[i, :, cols] = part[:slots].astype(BF16)
             sib_out[i, :, cols] = part[slots:].astype(BF16)
 
 
-def near_grad(place, pair, kept, local, stats, gates):
+def near_grad(place, pair, local, stats, gates):
     _, rows, half = pair.shape
     slots = rows // 2
     width = half // 2
@@ -545,12 +579,12 @@
     return pl.pallas_call(
         functools.partial(near_grad_kernel, HEAD**-0.5),
         out_shape=[jax.ShapeDtypeStruct((2 * slots, width), F32), out, out, jax.ShapeDtypeStruct(gates.shape, F32)],
-        in_specs=[SMEM] + [VMEM] * 5,
+        in_specs=[SMEM] + [VMEM] * 4,
         out_specs=[VMEM] * 4,
         compiler_params=params(),
         cost_estimate=cost(20 * slots * slots * half, 40 * slots * half),
         name="near_grad",
-    )(place, pair, kept, local, stats, gates)
+    )(place, pair, local, stats, gates)
 
 
 def cross_grad_kernel(scale, place_ref, cross, kept, stats, local, heard, gates, near_dq, near_sum, straight, diag, dq_out, keep, final, sum_out):
@@ -571,7 +605,7 @@
         row = slice(h, h + 1)
         dq, dk, dv = gradients(
             cross[2, :, cols], cross[0, :, cols], cross[3, :, cols],
-            kept[0, h], kept[1, h], scale, factor[row], delta[row],
+            kept[0, h].astype(F32), kept[1, h].astype(F32), scale, factor[row], delta[row],
         )
         dq_out[:, cols] = (near_dq[:, cols] + late * dq).astype(BF16)
         keep[0, :, cols] = dk.astype(BF16)
@@ -592,8 +626,8 @@
         out_shape=[
             out,
             out,
-            jax.ShapeDtypeStruct((rows, width), BF16),
-            jax.ShapeDtypeStruct((2, rows, width), BF16),
+            pltpu.VMEM((rows, width), BF16),
+            pltpu.VMEM((2, rows, width), BF16),
             jax.ShapeDtypeStruct((2, width // HEAD, rows), F32),
             jax.ShapeDtypeStruct((1, rows), F32),
         ],
@@ -605,12 +639,13 @@
     )(place, cross, kept, stats, local, heard, gates, near_dq, near_sum)
 
 
-def far_grad_kernel(scale, place_ref, pair, kept, final, gates, keep, near_dq, near_own, near_sib, own_out, sib_out):
+def far_grad_kernel(scale, place_ref, pair, local, final, gates, keep, near_dq, near_own, near_sib, own_out, sib_out):
     slots, half = pair.shape[1] // 2, pair.shape[2]
     width = half // 2
     heads = width // HEAD
     early = jnp.where(place_ref[1] == 0, 1.0, 0.0)
     factor = final[0] * gates[...]
+    mask = local_mask(place_ref[0], pair)
     own_out[0, :, :width] = near_dq[:slots]
     sib_out[0, :, :width] = near_dq[slots:]
     for i in range(2):
@@ -619,10 +654,9 @@
     for h in range(heads):
         cols = slice(width + h * HEAD, width + (h + 1) * HEAD)
         at = slice(h * HEAD, (h + 1) * HEAD)
-        dq, dk, dv = gradients(
-            pair[2, :, cols], pair[0, :, cols], pair[3, :, cols],
-            kept[0, heads + h], kept[1, heads + h], scale, factor[h : h + 1], final[1, h : h + 1],
-        )
+        row = slice(h, h + 1)
+        top = local[0, heads + h : heads + h + 1]
+        dq, dk, dv = local_gradients(pair, heads + h, mask, scale, top, factor[row], final[1, row])
         dk = dk + early * keep[0, :, at].astype(F32)
         dv = dv + early * keep[1, :, at].astype(F32)
         for i, part in enumerate((dq, dk, dv)):
@@ -630,7 +664,7 @@
             sib_out[i, :, cols] = part[slots:].astype(BF16)
 
 
-def far_grad(place, pair, kept, final, gates, keep, near_dq, near_own, near_sib):
+def far_grad(place, pair, local, final, gates, keep, near_dq, near_own, near_sib):
     _, rows, half = pair.shape
     slots = rows // 2
     out = jax.ShapeDtypeStruct((3, slots, half), BF16)
@@ -642,7 +676,7 @@
         compiler_params=params(),
         cost_estimate=cost(20 * slots * slots * half, 40 * slots * half),
         name="far_grad",
-    )(place, pair, kept, final, gates, keep, near_dq, near_own, near_sib)
+    )(place, pair, local, final, gates, keep, near_dq, near_own, near_sib)
 
 
 def join_kernel(place_ref, own, sib, straight, diag, dq_out, dk_out, dv_out, low, back, total, in_sems, out_sems):
@@ -704,7 +738,8 @@
     )(place, own, sib, straight, diag)
 
 
-def pair_router_kernel(gates_ref, sum_ref, x_ref, sib_ref, out_ref):
+def pair_router_kernel(gates_ref, sum_ref, x_ref, sib_ref, out_ref, held, sems):
+    arriving = sib_chunks(sib_ref, held, sems)
     gates = gates_ref[...]
     grad = sum_ref[...] * gates * (1.0 - gates)
     high = grad.astype(BF16)
@@ -715,8 +750,11 @@
     row = lax.broadcasted_iota(jnp.int32, (8, grad.shape[1]), 0)
     lhs = jnp.where(row == 0, high.astype(F32), jnp.where(row == 1, mid.astype(F32), jnp.where(row == 2, low.astype(F32), 0.0)))
     lhs = lhs.astype(BF16)
-    term = jnp.sum(nn(lhs[:, :slots], x_ref[0]) + nn(lhs[:, slots:], sib_ref[0]), axis=0, keepdims=True)
+    near = nn(lhs[:, :slots], x_ref[0])
     parts, copies, _, chunk = out_ref.shape
+    for c in arriving:
+        c.wait()
+    term = jnp.sum(near + nn(lhs[:, slots:], held[...]), axis=0, keepdims=True)
     for j in range(parts):
         for i in range(copies):
             out_ref[j, i] = term[:, j * chunk : (j + 1) * chunk]
@@ -727,8 +765,9 @@
     return pl.pallas_call(
         pair_router_kernel,
         out_shape=jax.ShapeDtypeStruct((parts, copies, 1, chunk), F32),
-        in_specs=[VMEM] * 4,
+        in_specs=[VMEM] * 3 + [pl.BlockSpec(memory_space=pl.ANY)],
         out_specs=VMEM,
+        scratch_shapes=[pltpu.VMEM(x_routed.shape[1:], BF16), pltpu.SemaphoreType.DMA((4,))],
         compiler_params=params(),
         cost_estimate=cost(32 * x_routed.size, x_routed.size * 4),
         name="router_terms",
@@ -767,9 +806,9 @@
                 other = after(other, *results)
             w_part = jnp.concatenate([w_part, other], axis=1)
             step *= 2
-        local, kept, live, pair = results or local_stats(place, route_pos, keys, values, queries, d_gated, sib)
+        local, live, pair = results or local_stats(place, route_pos, keys, values, queries, d_gated, sib)
         gates = pair_gate(place, live, x_routed, x_sib, w_part, ndp)
-        return pair, x_sib, local, kept, gates
+        return pair, x_sib, local, gates
 
     def grad_phase(*operands):
         own_out, sib_out = far_grad(*operands)
@@ -788,18 +827,18 @@
     theirs = sib_pack(place, after(route_pos, out_s), keys, values, queries, d_gated)
     if ndp > 1:
         w_part = jnp.concatenate([w_part, after(near_dp(w_part, 1), theirs)], axis=1)
-    pair, x_sib, local, kept, gates = beside(
+    pair, x_sib, local, gates = beside(
         local_phase, place, route_pos, x_routed, w_part, theirs, keys, values, queries, d_gated
     )
     cross, stats, kept_cross, message = cross_stats(place, pair, in_s, in_d, local, gates)
     heard = send(message, 2)
-    near_dq, near_own, near_sib, near_sum = near_grad(place, pair, kept, local, stats, gates)
+    near_dq, near_own, near_sib, near_sum = near_grad(place, pair, local, stats, gates)
     back_s, back_d, dq_low, keep, final, sums = cross_grad(
         place, cross, kept_cross, stats, local, heard, gates, near_dq, near_sum
     )
     ret_s, ret_d = send(back_s, 2), send(back_d, 3)
     own_out, sib_in, router_grad = beside(
-        router_phase, gates, sums, x_routed, x_sib, place, pair, kept, final, gates, keep, dq_low, near_own, near_sib
+        router_phase, gates, sums, x_routed, x_sib, place, pair, local, final, gates, keep, dq_low, near_own, near_sib
     )
     dq, dk, dv = join(place, own_out, sib_in, ret_s, ret_d, queries.shape)
     return dq, dk, dv, router_grad

time: 50.2 us -> 49.8 us (level)
  waiting for transfers between devices: 6 us -> 5.16 us
  Pallas kernels: 26.6 us -> 27.3 us
    pallas_call x1, Pallas kernels: 1.33 us -> 2.4 us  [cross_stats(): pl.pallas_call(functools.partial(cross_stats_kernel, HEAD ** (-0.5)), out...]
    pallas_call x1, Pallas kernels: 2.9 us -> 1.94 us  [cross_pack(): pl.pallas_call(cross_pack_kernel, out_shape=[cross, cross], in_specs=[SME...]
    pallas_call x1, Pallas kernels: 1.9 us -> 2.82 us  [pair_gate(): pl.pallas_call(functools.partial(pair_gate_kernel, parts), out_shape=jax....]
    all_to_all x1, waiting for transfers between devices: 1.59 us -> 0.77 us  [router_phase(): lax.all_to_all(terms.reshape(ndp * n, 1, chunk), ('dp', 'ctx'), 0, 0, til...]
    pallas_call x1, Pallas kernels: 3.35 us -> 4.17 us  [far_grad(): pl.pallas_call(functools.partial(far_grad_kernel, HEAD ** (-0.5)), out_sh...]
    pallas_call x1, Pallas kernels: 2.01 us -> 1.2 us  [cross_grad(): pl.pallas_call(functools.partial(cross_grad_kernel, HEAD ** (-0.5)), out_...]
    pallas_call x1, Pallas kernels: 4.72 us -> 4 us  [local_stats(): pl.pallas_call(functools.partial(local_stats_kernel, HEAD ** (-0.5)), out...]
  transfers between devices with their start and end apart: 12 -> 12, of which waited for: 4 -> 4; matrix products, arithmetic and copies ran while one was open for 0% -> 0% of each run, Pallas kernels for 34% -> 37%
where the time goes in v6:
time: 49.8 us; the launch traced here: 49.4 us
  Pallas kernels  27.3 us (55%)
  starting transfers between devices  15.8 us (32%)
  waiting for transfers between devices  5.16 us (10%)
  between operations  0.81 us (2%)
    ppermute x8, starting transfers between devices, send(): return lax.ppermute(a, 'ctx', [(i, i ^ flip) for i in range(n)])  6.01 us
    ppermute x3, starting transfers between devices, near_dp(): return lax.ppermute(part, 'dp', [(i, i ^ step) for i in range(ndp)])  5.75 us
    pallas_call x1, Pallas kernels, far_grad(): pl.pallas_call(functools.partial(far_grad_kernel, HEAD ** (-0.5)), out_sh...  4.17 us
    all_to_all x1, starting transfers between devices, router_phase(): lax.all_to_all(terms.reshape(ndp * n, 1, chunk), ('dp', 'ctx'), 0, 0, til...  4.08 us
    pallas_call x1, Pallas kernels, local_stats(): pl.pallas_call(functools.partial(local_stats_kernel, HEAD ** (-0.5)), out...  4 us
    pallas_call x1, Pallas kernels, join(): pl.pallas_call(join_kernel, out_shape=[out] * 3, in_specs=[SMEM] + [anywh...  3.38 us
    pallas_call x1, Pallas kernels, near_grad(): pl.pallas_call(functools.partial(near_grad_kernel, HEAD ** (-0.5)), out_s...  3.25 us
    pallas_call x1, Pallas kernels, pair_gate(): pl.pallas_call(functools.partial(pair_gate_kernel, parts), out_shape=jax....  2.82 us
  transfers between devices with their start and end apart: 12, of which 4 were waited for; matrix products, arithmetic and copies ran while one was open for 0% of the time, Pallas kernels for 37%

profile of v6, /device:TPU:0, one launch (start us, length us, event | category | flops | bytes accessed | tf_op | source)
XLA Modules:
  0.0 49.4 jit_solution(6453814308242507294)
XLA Ops:
  0.7 1.9 %cross_pack.1 = (bf16[2,128,512]{2,1,0:T(8,128)(2,1)S(1)}, bf16[2,128,512]{2,1,0:T(8,128)(2,1)S(1)}) custom-call(s32[3]{0:T(128)S(1)} %pad_add_fusion.place_ref, s32[1,128]{1,0:T(1,128)} %pos_ref.2, bf16[1,128,2048]{2,1,0:T(8,128)(2,1)} %k_ref.3, bf16[1,128,2048]{2,1,0:T(8,128)(2,1)} %v_ref.3, bf16[1,128,2048]{2,1,0:T(8,128)(2,1)} %q_ref.3, ...), custom_call_target="tpu_custom_call" | custom-call | flops 1 | bytes 1 | tf_op jit(solution)/shard_map/cross_pack/pallas_call | solution.py:301
  2.7 2.4 %collective-permute-start.7 = (bf16[2,128,512]{2,1,0:T(8,128)(2,1)S(1)}, bf16[2,128,512]{2,1,0:T(8,128)(2,1)S(1)}, u32[]{:S(2)}, u32[]{:S(2)}) collective-permute-start(bf16[2,128,512]{2,1,0:T(8,128)(2,1)S(1)} %get-tuple-element.139), channel_id=1, source_target_pairs={{0,3},{1,2},{2,1},{3,0},{4,7},{5,6},{6,5},{7,4},{8,11},{9,10},{10,... | collective-permute-start | bytes 786440 | tf_op jit(solution)/shard_map/ppermute | solution.py:784
  5.1 0.6 %collective-permute-start.6 = (bf16[2,128,512]{2,1,0:T(8,128)(2,1)S(1)}, bf16[2,128,512]{2,1,0:T(8,128)(2,1)S(1)}, u32[]{:S(2)}, u32[]{:S(2)}) collective-permute-start(bf16[2,128,512]{2,1,0:T(8,128)(2,1)S(1)} %get-tuple-element.134), channel_id=1, source_target_pairs={{0,2},{1,3},{2,0},{3,1},{4,6},{5,7},{6,4},{7,5},{8,10},{9,11},{10,... | collective-permute-start | bytes 786440 | tf_op jit(solution)/shard_map/ppermute | solution.py:784
  5.8 1.5 %collective-permute-start.5 = (f32[1,512]{1,0:T(1,128)S(1)}, f32[1,512]{1,0:T(1,128)S(1)}, u32[]{:S(2)}, u32[]{:S(2)}) collective-permute-start(f32[1,512]{1,0:T(1,128)S(1)} %bitcast.9), channel_id=1, source_target_pairs={{0,4},{4,0},{8,12},{12,8},{16,20},{20,16},{24,28},{28,24},{1,5},{5... | collective-permute-start | bytes 6152 | tf_op jit(solution)/shard_map/ppermute | solution.py:796
  7.3 1.8 %sib_pack.1 = bf16[4,128,1024]{2,1,0:T(8,128)(2,1)S(1)} custom-call(s32[3]{0:T(128)S(1)} %pad_add_fusion.place_ref, s32[1,128]{1,0:T(1,128)S(1)} %copy-done.1, bf16[1,128,2048]{2,1,0:T(8,128)(2,1)} %k_ref.3, bf16[1,128,2048]{2,1,0:T(8,128)(2,1)} %v_ref.3, bf16[1,128,2048]{2,1,0:T(8,128)(2,1)} %q_ref.3, f32[1,128,2048]{2,1,0:T(8,128)} %dg_ref.3), custom_call_target="tpu_custom_call" | custom-call | flops 1 | bytes 1 | tf_op jit(solution)/shard_map/sib_pack/pallas_call | solution.py:332
  9.4 13.8 %conditional.3 = (bf16[4,256,1024]{2,1,0:T(8,128)(2,1)}, bf16[1,128,4096]{2,1,0:T(8,128)(2,1)}, f32[3,8,256]{2,1,0:T(8,128)S(1)}, f32[1,256]{1,0:T(1,128)S(1)}) conditional(s32[]{:T(128)} %bitcast.5, () %tuple.37, (bf16[4,128,1024]{2,1,0:T(8,128)(2,1)S(1)}, s32[3]{0:T(128)S(1)}, s32[1,128]{1,0:T(1,128)S(1)}, bf16[1,128,2048]{2,1,0:T(8,128)(2,1)}, ...), branch_computations={%region_0.1_spmd, %region_1.2_spmd} | conditional | flops 10242 | bytes 8487106 | solution.py:790
  10.0 1.6 %collective-permute-start.3 = (f32[1,1024]{1,0:T(1,128)S(1)}, f32[1,1024]{1,0:T(1,128)S(1)}, u32[]{:S(2)}, u32[]{:S(2)}) collective-permute-start(f32[1,1024]{1,0:T(1,128)S(1)} %get-tuple-element.73), channel_id=1, source_target_pairs={{0,8},{4,12},{8,0},{12,4},{16,24},{20,28},{24,16},{28,20},{1,9},{5... | collective-permute-start | bytes 12296 | tf_op jit(solution)/shard_map/cond/branch_1_fun/ppermute | solution.py:796
  11.5 2.0 %collective-permute-done.3 = f32[1,1024]{1,0:T(1,128)S(1)} collective-permute-done((f32[1,1024]{1,0:T(1,128)S(1)}, f32[1,1024]{1,0:T(1,128)S(1)}, u32[]{:S(2)}, u32[]{:S(2)}) %collective-permute-start.3) | collective-permute-done | bytes 4128 | tf_op jit(solution)/shard_map/cond/branch_1_fun/ppermute | solution.py:796
  13.6 2.7 %collective-permute-start.4 = (f32[1,2048]{1,0:T(1,128)S(1)}, f32[1,2048]{1,0:T(1,128)S(1)}, u32[]{:S(2)}, u32[]{:S(2)}) collective-permute-start(f32[1,2048]{1,0:T(1,128)S(1)} %pad_maximum_fusion.1), channel_id=1, source_target_pairs={{0,16},{4,20},{8,24},{12,28},{16,0},{20,4},{24,8},{28,12},{1,17},{... | collective-permute-start | bytes 24584 | tf_op jit(solution)/shard_map/cond/branch_1_fun/ppermute | solution.py:796
  16.2 4.0 %local_stats.1 = (f32[3,8,256]{2,1,0:T(8,128)S(1)}, f32[1,256]{1,0:T(1,128)S(1)}, bf16[4,256,1024]{2,1,0:T(8,128)(2,1)}) custom-call(s32[3]{0:T(128)S(1)} %get-tuple-element.62.place_ref, s32[1,128]{1,0:T(1,128)S(1)} %get-tuple-element.63.pos_ref, bf16[1,128,2048]{2,1,0:T(8,128)(2,1)} %get-tuple-element.64.k_ref, ...), custom_call_target="tpu_custom_call" | custom-call | flops 1 | bytes 1 | tf_op jit(solution)/shard_map/cond/branch_1_fun/local_stats/pallas_call | solution.py:460
  20.3 2.8 %router_gate.1 = f32[1,256]{1,0:T(1,128)S(1)} custom-call(s32[3]{0:T(128)S(1)} %get-tuple-element.62.place_ref, f32[1,256]{1,0:T(1,128)S(1)} %get-tuple-element.72.live_ref, bf16[1,128,4096]{2,1,0:T(8,128)(2,1)S(1)} %get-tuple-element.70.x_ref, bf16[1,128,4096]{2,1,0:T(8,128)(2,1)} %collective-permute-done.2.sib_ref, f32[1,4096]{1,0:T(1,128)S(1)} %pad_maximum_fusion.w_ref), custom_call_target="tpu_custom_call" | custom-call | flops 1 | bytes 1 | tf_op jit(solution)/shard_map/cond/branch_1_fun/router_gate/pallas_call | solution.py:375
  23.1 2.4 %cross_stats.1 = (bf16[4,256,512]{2,1,0:T(8,128)(2,1)S(1)}, f32[3,4,256]{2,1,0:T(4,128)S(1)}, bf16[2,4,256,256]{3,2,1,0:T(8,128)(2,1)S(1)}, f32[4,4,256]{2,1,0:T(4,128)S(1)}) custom-call(s32[3]{0:T(128)S(1)} %pad_add_fusion.place_ref, bf16[4,256,1024]{2,1,0:T(8,128)(2,1)} %get-tuple-element.138.pair, ...), custom_call_target="tpu_custom_call" | custom-call | flops 1 | bytes 1 | tf_op jit(solution)/shard_map/cross_stats/pallas_call | solution.py:512
  25.5 1.5 %collective-permute-start.8 = (f32[4,4,256]{2,1,0:T(4,128)S(1)}, f32[4,4,256]{2,1,0:T(4,128)S(1)}, u32[]{:S(2)}, u32[]{:S(2)}) collective-permute-start(f32[4,4,256]{2,1,0:T(4,128)S(1)} %get-tuple-element.144), channel_id=1, source_target_pairs={{0,2},{1,3},{2,0},{3,1},{4,6},{5,7},{6,4},{7,5},{8,10},{9,11},{10,... | collective-permute-start | bytes 49160 | tf_op jit(solution)/shard_map/ppermute | solution.py:784
  27.0 3.3 %near_grad.1 = (f32[256,512]{1,0:T(8,128)S(1)}, bf16[2,128,512]{2,1,0:T(8,128)(2,1)S(1)}, bf16[2,128,512]{2,1,0:T(8,128)(2,1)S(1)}, f32[1,256]{1,0:T(1,128)S(1)}) custom-call(s32[3]{0:T(128)S(1)} %pad_add_fusion.place_ref, bf16[4,256,1024]{2,1,0:T(8,128)(2,1)} %get-tuple-element.138.pair, f32[3,8,256]{2,1,0:T(8,128)S(1)} %get-tuple-element.140.local, ...), custom_call_target="tpu_custom_call" | custom-call | flops 1 | bytes 1 | tf_op jit(solution)/shard_map/near_grad/pallas_call | solution.py:579
  30.3 1.2 %cross_grad.1 = (bf16[2,128,512]{2,1,0:T(8,128)(2,1)S(1)}, bf16[2,128,512]{2,1,0:T(8,128)(2,1)S(1)}, bf16[256,512]{1,0:T(8,128)(2,1)S(1)}, bf16[2,256,512]{2,1,0...) custom-call(s32[3]{0:T(128)S(1)} %pad_add_fusion.place_ref, ...), custom_call_target="tpu_custom_call" | custom-call | flops 1 | bytes 1 | tf_op jit(solution)/shard_map/cross_grad/pallas_call | solution.py:624
  31.5 0.7 %collective-permute-start.9 = (bf16[2,128,512]{2,1,0:T(8,128)(2,1)S(1)}, bf16[2,128,512]{2,1,0:T(8,128)(2,1)S(1)}, u32[]{:S(2)}, u32[]{:S(2)}) collective-permute-start(bf16[2,128,512]{2,1,0:T(8,128)(2,1)S(1)} %get-tuple-element.156), channel_id=1, source_target_pairs={{0,2},{1,3},{2,0},{3,1},{4,6},{5,7},{6,4},{7,5},{8,10},{9,11},{10,... | collective-permute-start | bytes 786440 | tf_op jit(solution)/shard_map/ppermute | solution.py:784
  32.2 13.8 %conditional.4 = (bf16[3,128,1024]{2,1,0:T(8,128)(2,1)}, bf16[3,128,1024]{2,1,0:T(8,128)(2,1)}, f32[512]{0:T(512)S(1)}) conditional(s32[]{:T(128)} %bitcast.5, () %tuple.36, (s32[1,128]{1,0:T(1,128)S(1)}, f32[1,256]{1,0:T(1,128)S(1)}, f32[1,256]{1,0:T(1,128)S(1)}, bf16[1,128,4096]{2,1,0:T(8,128)(2,1)S(1)}, bf16[1,128,4096]{2,1,0:T(8,128)(2,1)}, ...), branch_computations={%region_2.3_spmd, %region_3.7_spmd} | conditional | flops 16388 | bytes 3414220 | solution.py:790
  32.2 2.3 %router_terms.1 = f32[8,4,1,512]{3,2,1,0:T(1,128)} custom-call(f32[1,256]{1,0:T(1,128)S(1)} %get-tuple-element.88.gates_ref, f32[1,256]{1,0:T(1,128)S(1)} %get-tuple-element.89.sum_ref, bf16[1,128,4096]{2,1,0:T(8,128)(2,1)S(1)} %get-tuple-element.90.x_ref, bf16[1,128,4096]{2,1,0:T(8,128)(2,1)} %get-tuple-element.91.sib_ref), custom_call_target="tpu_custom_call" | custom-call | flops 1 | bytes 1 | tf_op jit(solution)/shard_map/cond/branch_1_fun/router_terms/pallas_call | solution.py:765
  34.4 4.1 %all-to-all-start = ((f32[32,1,512]{2,1,0:T(1,128)}), f32[32,1,512]{2,1,0:T(1,128)S(1)}, u32[]{:S(2)}, u32[]{:S(2)}) async-start(f32[32,1,512]{2,1,0:T(1,128)} %bitcast.1), calls=%async_computation | async-start | bytes 131072 | tf_op jit(solution)/shard_map/cond/branch_1_fun/all_to_all | solution.py:820
  38.5 6.6 %conditional = (bf16[3,128,1024]{2,1,0:T(8,128)(2,1)}, bf16[3,128,1024]{2,1,0:T(8,128)(2,1)}) conditional(s32[]{:T(128)} %bitcast, () %tuple.24, (s32[3]{0:T(128)S(1)}, bf16[4,256,1024]{2,1,0:T(8,128)(2,1)}, f32[3,8,256]{2,1,0:T(8,128)S(1)}, f32[2,4,256]{2,1,0:T(4,128)S(1)}, f32[1,256]{1,0:T(1,128)S(1)}, ...), branch_computations={%region_4.4_spmd, %region_5.5_spmd} | conditional | flops 1 | bytes 3145785 | solution.py:790
  38.6 4.2 %far_grad.1 = (bf16[3,128,1024]{2,1,0:T(8,128)(2,1)}, bf16[3,128,1024]{2,1,0:T(8,128)(2,1)S(1)}) custom-call(s32[3]{0:T(128)S(1)} %get-tuple-element.75.place_ref, bf16[4,256,1024]{2,1,0:T(8,128)(2,1)} %get-tuple-element.76.pair, f32[3,8,256]{2,1,0:T(8,128)S(1)} %get-tuple-element.77.local, f32[2,4,256]{2,1,0:T(4,128)S(1)} %get-tuple-element.78.final, ...), custom_call_target="tpu_custom_call" | custom-call | flops 1 | bytes 1 | tf_op jit(solution)/shard_map/cond/branch_1_fun/cond/branch_1_fun/far_grad/pallas_call | solution.py:671
  43.0 2.2 %collective-permute-done = bf16[3,128,1024]{2,1,0:T(8,128)(2,1)} collective-permute-done((bf16[3,128,1024]{2,1,0:T(8,128)(2,1)S(1)}, bf16[3,128,1024]{2,1,0:T(8,128)(2,1)}, u32[]{:S(2)}, u32[]{:S(2)}) %collective-permute-start) | collective-permute-done | bytes 786464 | tf_op jit(solution)/shard_map/cond/branch_1_fun/cond/branch_1_fun/ppermute | solution.py:784
  45.2 0.8 %all-to-all-done = f32[32,1,512]{2,1,0:T(1,128)S(1)} async-done(((f32[32,1,512]{2,1,0:T(1,128)}), f32[32,1,512]{2,1,0:T(1,128)S(1)}, u32[]{:S(2)}, u32[]{:S(2)}) %all-to-all-start) | async-done | bytes 65568 | tf_op jit(solution)/shard_map/cond/branch_1_fun/all_to_all | solution.py:820
  46.0 3.4 %join.1 = (f32[1,128,2048]{2,1,0:T(8,128)}, f32[1,128,2048]{2,1,0:T(8,128)}, f32[1,128,2048]{2,1,0:T(8,128)}) custom-call(s32[3]{0:T(128)S(1)} %pad_add_fusion.place_ref, bf16[3,128,1024]{2,1,0:T(8,128)(2,1)} %get-tuple-element.154.own, bf16[3,128,1024]{2,1,0:T(8,128)(2,1)} %get-tuple-element.155.sib, ...), custom_call_target="tpu_custom_call" | custom-call | flops 1 | bytes 1 | tf_op jit(solution)/shard_map/join/pallas_call | solution.py:723
  (28 shorter events, 1.2 us)
Async XLA Ops:
  0.6 6.7 %copy-start.1 = (s32[1,128]{1,0:T(1,128)S(1)}, s32[1,128]{1,0:T(1,128)}, u32[]{:S(2)}) copy-start(s32[1,128]{1,0:T(1,128)} %pos_ref.2) | copy-start | bytes 1540
  0.6 5.1 %copy-start.3 = (bf16[512]{0:T(512)(128)(2,1)S(1)}, bf16[512]{0:T(512)(128)(2,1)}, u32[]{:S(2)}) copy-start(bf16[512]{0:T(512)(128)(2,1)} %param.15) | copy-start | bytes 3076
  2.7 6.7 %copy-start = (bf16[1,128,4096]{2,1,0:T(8,128)(2,1)S(1)}, bf16[1,128,4096]{2,1,0:T(8,128)(2,1)}, u32[]{:S(2)}) copy-start(bf16[1,128,4096]{2,1,0:T(8,128)(2,1)} %param.14) | copy-start | bytes 3145732
  2.7 20.4 %collective-permute-start.7 = (bf16[2,128,512]{2,1,0:T(8,128)(2,1)S(1)}, bf16[2,128,512]{2,1,0:T(8,128)(2,1)S(1)}, u32[]{:S(2)}, u32[]{:S(2)}) collective-permute-start(bf16[2,128,512]{2,1,0:T(8,128)(2,1)S(1)} %get-tuple-element.139), channel_id=1, source_target_pairs={{0,3},{1,2},{2,1},{3,0},{4,7},{5,6},{6,5},{7,4},{8,11},{9,10},{10,... | collective-permute-start | bytes 786440 | tf_op jit(solution)/shard_map/ppermute | solution.py:784
  5.1 18.0 %collective-permute-start.6 = (bf16[2,128,512]{2,1,0:T(8,128)(2,1)S(1)}, bf16[2,128,512]{2,1,0:T(8,128)(2,1)S(1)}, u32[]{:S(2)}, u32[]{:S(2)}) collective-permute-start(bf16[2,128,512]{2,1,0:T(8,128)(2,1)S(1)} %get-tuple-element.134), channel_id=1, source_target_pairs={{0,2},{1,3},{2,0},{3,1},{4,6},{5,7},{6,4},{7,5},{8,10},{9,11},{10,... | collective-permute-start | bytes 786440 | tf_op jit(solution)/shard_map/ppermute | solution.py:784
  5.8 3.6 %collective-permute-start.5 = (f32[1,512]{1,0:T(1,128)S(1)}, f32[1,512]{1,0:T(1,128)S(1)}, u32[]{:S(2)}, u32[]{:S(2)}) collective-permute-start(f32[1,512]{1,0:T(1,128)S(1)} %bitcast.9), channel_id=1, source_target_pairs={{0,4},{4,0},{8,12},{12,8},{16,20},{20,16},{24,28},{28,24},{1,5},{5... | collective-permute-start | bytes 6152 | tf_op jit(solution)/shard_map/ppermute | solution.py:796
  9.4 6.9 %collective-permute-start.1 = (bf16[4,128,1024]{2,1,0:T(8,128)(2,1)S(1)}, bf16[4,128,1024]{2,1,0:T(8,128)(2,1)S(1)}, u32[]{:S(2)}, u32[]{:S(2)}) collective-permute-start(bf16[4,128,1024]{2,1,0:T(8,128)(2,1)S(1)} %get-tuple-element.68), channel_id=1, source_target_pairs={{0,1},{1,0},{2,3},{3,2},{4,5},{5,4},{6,7},{7,6},{8,9},{9,8},{10,11... | collective-permute-start | bytes 3145736 | tf_op jit(solution)/shard_map/cond/branch_1_fun/ppermute | solution.py:784
  9.5 10.8 %collective-permute-start.2 = (bf16[1,128,4096]{2,1,0:T(8,128)(2,1)S(1)}, bf16[1,128,4096]{2,1,0:T(8,128)(2,1)}, u32[]{:S(2)}, u32[]{:S(2)}) collective-permute-start(bf16[1,128,4096]{2,1,0:T(8,128)(2,1)S(1)} %get-tuple-element.70.x_ref), channel_id=1, source_target_pairs={{0,1},{1,0},{2,3},{3,2},{4,5},{5,4},{6,7},{7,6},{8,9},{9,8},{10,11... | collective-permute-start | bytes 3145736 | tf_op jit(solution)/shard_map/cond/branch_1_fun/ppermute | solution.py:784
  10.0 3.6 %collective-permute-start.3 = (f32[1,1024]{1,0:T(1,128)S(1)}, f32[1,1024]{1,0:T(1,128)S(1)}, u32[]{:S(2)}, u32[]{:S(2)}) collective-permute-start(f32[1,1024]{1,0:T(1,128)S(1)} %get-tuple-element.73), channel_id=1, source_target_pairs={{0,8},{4,12},{8,0},{12,4},{16,24},{20,28},{24,16},{28,20},{1,9},{5... | collective-permute-start | bytes 12296 | tf_op jit(solution)/shard_map/cond/branch_1_fun/ppermute | solution.py:796
  13.6 6.7 %collective-permute-start.4 = (f32[1,2048]{1,0:T(1,128)S(1)}, f32[1,2048]{1,0:T(1,128)S(1)}, u32[]{:S(2)}, u32[]{:S(2)}) collective-permute-start(f32[1,2048]{1,0:T(1,128)S(1)} %pad_maximum_fusion.1), channel_id=1, source_target_pairs={{0,16},{4,20},{8,24},{12,28},{16,0},{20,4},{24,8},{28,12},{1,17},{... | collective-permute-start | bytes 24584 | tf_op jit(solution)/shard_map/cond/branch_1_fun/ppermute | solution.py:796
  25.5 4.7 %collective-permute-start.8 = (f32[4,4,256]{2,1,0:T(4,128)S(1)}, f32[4,4,256]{2,1,0:T(4,128)S(1)}, u32[]{:S(2)}, u32[]{:S(2)}) collective-permute-start(f32[4,4,256]{2,1,0:T(4,128)S(1)} %get-tuple-element.144), channel_id=1, source_target_pairs={{0,2},{1,3},{2,0},{3,1},{4,6},{5,7},{6,4},{7,5},{8,10},{9,11},{10,... | collective-permute-start | bytes 49160 | tf_op jit(solution)/shard_map/ppermute | solution.py:784
  31.5 14.6 %collective-permute-start.9 = (bf16[2,128,512]{2,1,0:T(8,128)(2,1)S(1)}, bf16[2,128,512]{2,1,0:T(8,128)(2,1)S(1)}, u32[]{:S(2)}, u32[]{:S(2)}) collective-permute-start(bf16[2,128,512]{2,1,0:T(8,128)(2,1)S(1)} %get-tuple-element.156), channel_id=1, source_target_pairs={{0,2},{1,3},{2,0},{3,1},{4,6},{5,7},{6,4},{7,5},{8,10},{9,11},{10,... | collective-permute-start | bytes 786440 | tf_op jit(solution)/shard_map/ppermute | solution.py:784
  32.2 13.9 %collective-permute-start.10 = (bf16[2,128,512]{2,1,0:T(8,128)(2,1)S(1)}, bf16[2,128,512]{2,1,0:T(8,128)(2,1)S(1)}, u32[]{:S(2)}, u32[]{:S(2)}) collective-permute-start(bf16[2,128,512]{2,1,0:T(8,128)(2,1)S(1)} %get-tuple-element.157), channel_id=1, source_target_pairs={{0,3},{1,2},{2,1},{3,0},{4,7},{5,6},{6,5},{7,4},{8,11},{9,10},{10,... | collective-permute-start | bytes 786440 | tf_op jit(solution)/shard_map/ppermute | solution.py:784
  34.4 11.5 %all-to-all-start = ((f32[32,1,512]{2,1,0:T(1,128)}), f32[32,1,512]{2,1,0:T(1,128)S(1)}, u32[]{:S(2)}, u32[]{:S(2)}) async-start(f32[32,1,512]{2,1,0:T(1,128)} %bitcast.1), calls=%async_computation | async-start | bytes 131072 | tf_op jit(solution)/shard_map/cond/branch_1_fun/all_to_all | solution.py:820
  42.7 2.4 %collective-permute-start = (bf16[3,128,1024]{2,1,0:T(8,128)(2,1)S(1)}, bf16[3,128,1024]{2,1,0:T(8,128)(2,1)}, u32[]{:S(2)}, u32[]{:S(2)}) collective-permute-start(bf16[3,128,1024]{2,1,0:T(8,128)(2,1)S(1)} %get-tuple-element.85), channel_id=1, source_target_pairs={{0,1},{1,0},{2,3},{3,2},{4,5},{5,4},{6,7},{7,6},{8,9},{9,8},{10,11... | collective-permute-start | bytes 2359304 | tf_op jit(solution)/shard_map/cond/branch_1_fun/cond/branch_1_fun/ppermute | solution.py:784
  46.0 3.4 %copy-start.2 = (f32[512]{0:T(512)}, f32[512]{0:T(512)S(1)}, u32[]{:S(2)}) copy-start(f32[512]{0:T(512)S(1)} %get-tuple-element.133) | copy-start | bytes 6148

commit v7 on v6

--- a/solution.py
+++ b/solution.py
@@ -341,47 +341,29 @@
     )(place, route_pos, *in_hbm(keys, values, queries, d_gated))
 
 
-def sib_chunks(sib_ref, held, sems):
-    parts = sems.shape[0]
-    chunk = held.shape[1] // parts
-    copies = []
-    for j in range(parts):
-        cols = slice(j * chunk, (j + 1) * chunk)
-        copies.append(pltpu.make_async_copy(sib_ref.at[0, :, cols], held.at[:, cols], sems.at[j]))
-    for c in copies:
-        c.start()
-    return copies
-
-
-def pair_gate_kernel(parts, place_ref, live_ref, x_ref, sib_ref, w_ref, out_ref, held, sems):
+def pair_gate_kernel(parts, place_ref, live_ref, rows_x, w_ref, out_ref):
     chunk = w_ref.shape[1] // parts
-    slots = x_ref.shape[1]
-    copies = sib_chunks(sib_ref, held, sems)
+    slots = rows_x.shape[1]
     for i in range(2):
         total = jnp.zeros((8, slots), F32)
-        if i == 1:
-            for c in copies:
-                c.wait()
         for j in range(parts):
             w_rows = jnp.broadcast_to(w_ref[:, j * chunk : (j + 1) * chunk], (8, chunk)).astype(BF16)
             cols = pl.ds(pl.multiple_of((place_ref[2] ^ j) * chunk, HEAD), chunk)
-            total = total + nt(w_rows, x_ref[0, :, cols] if i == 0 else held[:, cols])
+            total = total + nt(w_rows, rows_x[i, :, cols])
         lanes = slice(i * slots, (i + 1) * slots)
         out_ref[:, lanes] = live_ref[:, lanes] / (1.0 + jnp.exp(-total[0:1]))
 
 
-def pair_gate(place, live, x_routed, x_sib, w_full, parts):
-    _, slots, depth = x_routed.shape
+def pair_gate(place, live, rows_x, w_full, parts):
     return pl.pallas_call(
         functools.partial(pair_gate_kernel, parts),
         out_shape=jax.ShapeDtypeStruct(live.shape, F32),
-        in_specs=[SMEM, VMEM, VMEM, pl.BlockSpec(memory_space=pl.ANY), VMEM],
+        in_specs=[SMEM] + [VMEM] * 3,
         out_specs=VMEM,
-        scratch_shapes=[pltpu.VMEM((slots, depth), BF16), pltpu.SemaphoreType.DMA((4,))],
-        compiler_params=params(),
-        cost_estimate=cost(16 * x_routed.size, x_routed.size * 2),
+        compiler_params=params(),
+        cost_estimate=cost(16 * rows_x.size, rows_x.size * 2),
         name="router_gate",
-    )(place, live, x_routed, x_sib, w_full)
+    )(place, live, rows_x, w_full)
 
 
 def local_mask(core, pair):
@@ -416,7 +398,7 @@
     stats[2, h : h + 1] = jnp.sum(e * gw, axis=0, keepdims=True)
 
 
-def local_stats_kernel(scale, place_ref, pos_ref, k_ref, v_ref, q_ref, dg_ref, sib, stats, live, pair, wide, sems):
+def local_stats_kernel(scale, place_ref, pos_ref, k_ref, v_ref, q_ref, dg_ref, sib, x_ref, x_sib, stats, live, pair, rows_x, wide, sems, x_sems):
     slots, half = sib.shape[1], sib.shape[2]
     width = half // 2
     core = place_ref[0]
@@ -435,6 +417,14 @@
         for c in copies:
             c.start()
         stages.append(copies)
+    x_copies = []
+    depth = x_ref.shape[2] // 2
+    for i, ref in enumerate((x_ref, x_sib)):
+        for g in range(2):
+            cols = slice(g * depth, (g + 1) * depth)
+            x_copies.append(pltpu.make_async_copy(ref.at[0, :, cols], rows_x.at[i, :, cols], x_sems.at[2 * i + g]))
+    for c in x_copies:
+        c.start()
     rows_live = live_rows(pos_ref, slots)
     mask = None
     for g in range(2):
@@ -451,9 +441,11 @@
             at = slice(h * HEAD, (h + 1) * HEAD)
             scores = jnp.where(mask, nt(pair[0, :, at], pair[2, :, at]) * scale, NEG_FILL)
             partial_stats(scores, nt(pair[1, :, at], pair[3, :, at]), stats, h)
-
-
-def local_stats(place, route_pos, keys, values, queries, d_gated, sib):
+    for c in x_copies:
+        c.wait()
+
+
+def local_stats(place, route_pos, keys, values, queries, d_gated, sib, x_routed, x_sib):
     _, slots, half = sib.shape
     heads = half // HEAD
     anywhere = pl.BlockSpec(memory_space=pl.ANY)
@@ -462,15 +454,16 @@
         out_shape=[
             jax.ShapeDtypeStruct((3, heads, 2 * slots), F32),
             jax.ShapeDtypeStruct((1, 2 * slots), F32),
-            jax.ShapeDtypeStruct((4, 2 * slots, half), BF16),
+            pltpu.VMEM((4, 2 * slots, half), BF16),
+            pltpu.VMEM((2, slots, x_routed.shape[2]), BF16),
         ],
-        in_specs=[SMEM, VMEM] + [anywhere] * 5,
-        out_specs=[VMEM] * 3,
-        scratch_shapes=[pltpu.VMEM((slots, half), F32), pltpu.SemaphoreType.DMA((16,))],
+        in_specs=[SMEM, VMEM] + [anywhere] * 7,
+        out_specs=[VMEM] * 4,
+        scratch_shapes=[pltpu.VMEM((slots, half), F32), pltpu.SemaphoreType.DMA((16,)), pltpu.SemaphoreType.DMA((4,))],
         compiler_params=params(),
         cost_estimate=cost(16 * slots * slots * half, 16 * slots * half, 4 * slots * slots * half // HEAD),
         name="local_stats",
-    )(place, route_pos, *in_hbm(keys, values, queries, d_gated), sib)
+    )(place, route_pos, *in_hbm(keys, values, queries, d_gated), sib, x_routed, x_sib)
 
 
 def cross_stats_kernel(scale, place_ref, pair, straight, diag, local, gates, cross, stats, kept, message):
@@ -738,40 +731,35 @@
     )(place, own, sib, straight, diag)
 
 
-def pair_router_kernel(gates_ref, sum_ref, x_ref, sib_ref, out_ref, held, sems):
-    arriving = sib_chunks(sib_ref, held, sems)
+def pair_router_kernel(gates_ref, sum_ref, rows_x, out_ref):
     gates = gates_ref[...]
     grad = sum_ref[...] * gates * (1.0 - gates)
     high = grad.astype(BF16)
     rest = grad - high.astype(F32)
     mid = rest.astype(BF16)
     low = (rest - mid.astype(F32)).astype(BF16)
-    slots = x_ref.shape[1]
+    slots = rows_x.shape[1]
     row = lax.broadcasted_iota(jnp.int32, (8, grad.shape[1]), 0)
     lhs = jnp.where(row == 0, high.astype(F32), jnp.where(row == 1, mid.astype(F32), jnp.where(row == 2, low.astype(F32), 0.0)))
     lhs = lhs.astype(BF16)
-    near = nn(lhs[:, :slots], x_ref[0])
+    term = jnp.sum(nn(lhs[:, :slots], rows_x[0]) + nn(lhs[:, slots:], rows_x[1]), axis=0, keepdims=True)
     parts, copies, _, chunk = out_ref.shape
-    for c in arriving:
-        c.wait()
-    term = jnp.sum(near + nn(lhs[:, slots:], held[...]), axis=0, keepdims=True)
     for j in range(parts):
         for i in range(copies):
             out_ref[j, i] = term[:, j * chunk : (j + 1) * chunk]
 
 
-def pair_router(gates, sums, x_routed, x_sib, parts, copies):
-    chunk = x_routed.shape[-1] // parts
+def pair_router(gates, sums, rows_x, parts, copies):
+    chunk = rows_x.shape[-1] // parts
     return pl.pallas_call(
         pair_router_kernel,
         out_shape=jax.ShapeDtypeStruct((parts, copies, 1, chunk), F32),
-        in_specs=[VMEM] * 3 + [pl.BlockSpec(memory_space=pl.ANY)],
+        in_specs=[VMEM] * 3,
         out_specs=VMEM,
-        scratch_shapes=[pltpu.VMEM(x_routed.shape[1:], BF16), pltpu.SemaphoreType.DMA((4,))],
-        compiler_params=params(),
-        cost_estimate=cost(32 * x_routed.size, x_routed.size * 4),
+        compiler_params=params(),
+        cost_estimate=cost(32 * rows_x.size, rows_x.size * 4),
         name="router_terms",
-    )(gates, sums, x_routed, x_sib)
+    )(gates, sums, rows_x)
 
 
 def swap_body(route_pos, x_routed, w_router, queries, keys, values, d_gated):
@@ -795,27 +783,23 @@
     def near_dp(part, step):
         return lax.ppermute(part, "dp", [(i, i ^ step) for i in range(ndp)])
 
-    def local_phase(place, route_pos, x_routed, w_part, theirs, keys, values, queries, d_gated):
+    def widen(part, step, *first):
+        return jnp.concatenate([part, after(near_dp(part, step), *first)], axis=1)
+
+    def exchange_phase(x_routed, w_part, theirs):
         sib, x_sib = send(theirs, 1), send(x_routed, 1)
-        results = ()
-        step = 2
+        step = 4
         while step < ndp:
-            other = near_dp(w_part, step)
-            if 2 * step == ndp:
-                results = local_stats(place, route_pos, keys, values, queries, d_gated, sib)
-                other = after(other, *results)
-            w_part = jnp.concatenate([w_part, other], axis=1)
+            w_part = widen(w_part, step)
             step *= 2
-        local, live, pair = results or local_stats(place, route_pos, keys, values, queries, d_gated, sib)
-        gates = pair_gate(place, live, x_routed, x_sib, w_part, ndp)
-        return pair, x_sib, local, gates
+        return sib, x_sib, w_part
 
     def grad_phase(*operands):
         own_out, sib_out = far_grad(*operands)
         return own_out, send(sib_out, 1)
 
-    def router_phase(gates, sums, x_routed, x_sib, place, *operands):
-        terms = pair_router(gates, sums, x_routed, x_sib, ndp, n)
+    def router_phase(gates, sums, rows_x, place, *operands):
+        terms = pair_router(gates, sums, rows_x, ndp, n)
         chunk = terms.shape[-1]
         shared = lax.all_to_all(terms.reshape(ndp * n, 1, chunk), ("dp", "ctx"), 0, 0, tiled=True)
         own_out, sib_in = beside(grad_phase, after(place, terms), *operands)
@@ -826,10 +810,12 @@
     in_s, in_d = send(out_s, 2), send(out_d, 3)
     theirs = sib_pack(place, after(route_pos, out_s), keys, values, queries, d_gated)
     if ndp > 1:
-        w_part = jnp.concatenate([w_part, after(near_dp(w_part, 1), theirs)], axis=1)
-    pair, x_sib, local, gates = beside(
-        local_phase, place, route_pos, x_routed, w_part, theirs, keys, values, queries, d_gated
-    )
+        w_part = widen(w_part, 1)
+    if ndp > 2:
+        w_part = widen(w_part, 2, theirs)
+    sib, x_sib, w_part = beside(exchange_phase, x_routed, w_part, theirs)
+    local, live, pair, rows_x = local_stats(place, route_pos, keys, values, queries, d_gated, sib, x_routed, x_sib)
+    gates = pair_gate(place, live, rows_x, w_part, ndp)
     cross, stats, kept_cross, message = cross_stats(place, pair, in_s, in_d, local, gates)
     heard = send(message, 2)
     near_dq, near_own, near_sib, near_sum = near_grad(place, pair, local, stats, gates)
@@ -838,7 +824,7 @@
     )
     ret_s, ret_d = send(back_s, 2), send(back_d, 3)
     own_out, sib_in, router_grad = beside(
-        router_phase, gates, sums, x_routed, x_sib, place, pair, local, final, gates, keep, dq_low, near_own, near_sib
+        router_phase, gates, sums, rows_x, place, pair, local, final, gates, keep, dq_low, near_own, near_sib
     )
     dq, dk, dv = join(place, own_out, sib_in, ret_s, ret_d, queries.shape)
     return dq, dk, dv, router_grad

time: 49.8 us -> 47.3 us (0.950)
  Pallas kernels: 27.3 us -> 22.8 us
  starting transfers between devices: 15.8 us -> 16.9 us
  other arithmetic: 0.18 us -> 0.87 us
    pallas_call x1, Pallas kernels: 2.82 us -> 1.2 us  [pair_gate(): pl.pallas_call(functools.partial(pair_gate_kernel, parts), out_shape=jax....]
    ppermute x8, starting transfers between devices: 6.01 us -> 4.51 us  [send(): return lax.ppermute(a, 'ctx', [(i, i ^ flip) for i in range(n)])]
    ppermute x3, starting transfers between devices: 5.75 us -> 7.2 us  [near_dp(): return lax.ppermute(part, 'dp', [(i, i ^ step) for i in range(ndp)])]
    pallas_call x1, Pallas kernels: 2.25 us -> 1.04 us  [pair_router(): pl.pallas_call(pair_router_kernel, out_shape=jax.ShapeDtypeStruct((parts,...]
    all_to_all x1, starting transfers between devices: 4.08 us -> 5.15 us  [router_phase(): lax.all_to_all(terms.reshape(ndp * n, 1, chunk), ('dp', 'ctx'), 0, 0, til...]
    pallas_call x1, Pallas kernels: 2.4 us -> 1.34 us  [cross_stats(): pl.pallas_call(functools.partial(cross_stats_kernel, HEAD ** (-0.5)), out...]
    pallas_call x1, Pallas kernels: 1.2 us -> 1.97 us  [cross_grad(): pl.pallas_call(functools.partial(cross_grad_kernel, HEAD ** (-0.5)), out_...]
    convert_element_type x1, other arithmetic: 0.01 us -> 0.69 us  [swap_body(): w_part = w_router.reshape(1, -1).astype(F32)]
  transfers between devices with their start and end apart: 12 -> 12, of which waited for: 4 -> 4; matrix products, arithmetic and copies ran while one was open for 0% -> 0% of each run, Pallas kernels for 37% -> 34%
where the time goes in v7:
time: 47.3 us; the launch traced here: 47 us
  Pallas kernels  22.8 us (48%)
  starting transfers between devices  16.9 us (36%)
  waiting for transfers between devices  5.63 us (12%)
  other arithmetic  0.87 us (2%)
  between operations  0.79 us (2%)
    ppermute x3, starting transfers between devices, near_dp(): return lax.ppermute(part, 'dp', [(i, i ^ step) for i in range(ndp)])  7.2 us
    all_to_all x1, starting transfers between devices, router_phase(): lax.all_to_all(terms.reshape(ndp * n, 1, chunk), ('dp', 'ctx'), 0, 0, til...  5.15 us
    ppermute x8, starting transfers between devices, send(): return lax.ppermute(a, 'ctx', [(i, i ^ flip) for i in range(n)])  4.51 us
    pallas_call x1, Pallas kernels, far_grad(): pl.pallas_call(functools.partial(far_grad_kernel, HEAD ** (-0.5)), out_sh...  3.59 us
    pallas_call x1, Pallas kernels, local_stats(): pl.pallas_call(functools.partial(local_stats_kernel, HEAD ** (-0.5)), out...  3.51 us
    pallas_call x1, Pallas kernels, join(): pl.pallas_call(join_kernel, out_shape=[out] * 3, in_specs=[SMEM] + [anywh...  3.38 us
    pallas_call x1, Pallas kernels, near_grad(): pl.pallas_call(functools.partial(near_grad_kernel, HEAD ** (-0.5)), out_s...  2.95 us
    ppermute x8, waiting for transfers between devices, send(): return lax.ppermute(a, 'ctx', [(i, i ^ flip) for i in range(n)])  2.18 us
  transfers between devices with their start and end apart: 12, of which 4 were waited for; matrix products, arithmetic and copies ran while one was open for 0% of the time, Pallas kernels for 34%

profile of v7, /device:TPU:0, one launch (start us, length us, event | category | flops | bytes accessed | tf_op | source)
XLA Modules:
  0.0 47.0 jit_solution(965191848798752335)
XLA Ops:
  0.6 0.7 %convert_element_type.25 = f32[512]{0:T(512)S(1)} convert(bf16[512]{0:T(512)(128)(2,1)} %param.15) | non-fusion elementwise | flops 512 | bytes 3072 | tf_op jit(solution)/shard_map/convert_element_type | solution.py:808
  1.3 3.0 %collective-permute-start.4 = (f32[1,512]{1,0:T(1,128)S(1)}, f32[1,512]{1,0:T(1,128)S(1)}, u32[]{:S(2)}, u32[]{:S(2)}) collective-permute-start(f32[1,512]{1,0:T(1,128)S(1)} %bitcast.9), channel_id=1, source_target_pairs={{0,4},{4,0},{8,12},{12,8},{16,20},{20,16},{24,28},{28,24},{1,5},{5... | collective-permute-start | bytes 6152 | tf_op jit(solution)/shard_map/ppermute | solution.py:784
  4.4 1.9 %cross_pack.1 = (bf16[2,128,512]{2,1,0:T(8,128)(2,1)S(1)}, bf16[2,128,512]{2,1,0:T(8,128)(2,1)S(1)}) custom-call(s32[3]{0:T(128)S(1)} %pad_add_fusion.place_ref, s32[1,128]{1,0:T(1,128)} %pos_ref.4, bf16[1,128,2048]{2,1,0:T(8,128)(2,1)} %k_ref.5, bf16[1,128,2048]{2,1,0:T(8,128)(2,1)} %v_ref.5, bf16[1,128,2048]{2,1,0:T(8,128)(2,1)} %q_ref.5, ...), custom_call_target="tpu_custom_call" | custom-call | flops 1 | bytes 1 | tf_op jit(solution)/shard_map/cross_pack/pallas_call | solution.py:301
  7.0 0.9 %collective-permute-start.6 = (bf16[2,128,512]{2,1,0:T(8,128)(2,1)S(1)}, bf16[2,128,512]{2,1,0:T(8,128)(2,1)S(1)}, u32[]{:S(2)}, u32[]{:S(2)}) collective-permute-start(bf16[2,128,512]{2,1,0:T(8,128)(2,1)S(1)} %get-tuple-element.112), channel_id=1, source_target_pairs={{0,2},{1,3},{2,0},{3,1},{4,6},{5,7},{6,4},{7,5},{8,10},{9,11},{10,... | collective-permute-start | bytes 786440 | tf_op jit(solution)/shard_map/ppermute | solution.py:772
  7.9 1.6 %collective-permute-start.5 = (f32[1,1024]{1,0:T(1,128)S(1)}, f32[1,1024]{1,0:T(1,128)S(1)}, u32[]{:S(2)}, u32[]{:S(2)}) collective-permute-start(f32[1,1024]{1,0:T(1,128)S(1)} %pad_maximum_fusion.2), channel_id=1, source_target_pairs={{0,8},{4,12},{8,0},{12,4},{16,24},{20,28},{24,16},{28,20},{1,9},{5... | collective-permute-start | bytes 12296 | tf_op jit(solution)/shard_map/ppermute | solution.py:784
  9.6 1.8 %sib_pack.1 = bf16[4,128,1024]{2,1,0:T(8,128)(2,1)S(1)} custom-call(s32[3]{0:T(128)S(1)} %pad_add_fusion.place_ref, s32[1,128]{1,0:T(1,128)S(1)} %copy-done.1, bf16[1,128,2048]{2,1,0:T(8,128)(2,1)} %k_ref.5, bf16[1,128,2048]{2,1,0:T(8,128)(2,1)} %v_ref.5, bf16[1,128,2048]{2,1,0:T(8,128)(2,1)} %q_ref.5, f32[1,128,2048]{2,1,0:T(8,128)} %dg_ref.5), custom_call_target="tpu_custom_call" | custom-call | flops 1 | bytes 1 | tf_op jit(solution)/shard_map/sib_pack/pallas_call | solution.py:332
  11.6 5.2 %conditional.3 = (bf16[4,128,1024]{2,1,0:T(8,128)(2,1)}, bf16[1,128,4096]{2,1,0:T(8,128)(2,1)}, f32[1,4096]{1,0:T(1,128)S(1)}) conditional(s32[]{:T(128)} %bitcast.5, () %tuple.36, (bf16[4,128,1024]{2,1,0:T(8,128)(2,1)S(1)}, bf16[1,128,4096]{2,1,0:T(8,128)(2,1)S(1)}, f32[1,2048]{1,0:T(1,128)S(1)}) %tuple.48), branch_computations={%region_0.1_spmd, %region_1.2_spmd} | conditional | flops 4096 | bytes 8454288 | solution.py:778
  12.2 2.6 %collective-permute-start.3 = (f32[1,2048]{1,0:T(1,128)S(1)}, f32[1,2048]{1,0:T(1,128)S(1)}, u32[]{:S(2)}, u32[]{:S(2)}) collective-permute-start(f32[1,2048]{1,0:T(1,128)S(1)} %get-tuple-element.50), channel_id=1, source_target_pairs={{0,16},{4,20},{8,24},{12,28},{16,0},{20,4},{24,8},{28,12},{1,17},{... | collective-permute-start | bytes 24584 | tf_op jit(solution)/shard_map/cond/branch_1_fun/ppermute | solution.py:784
  14.8 2.0 %collective-permute-done.3 = f32[1,2048]{1,0:T(1,128)S(1)} collective-permute-done((f32[1,2048]{1,0:T(1,128)S(1)}, f32[1,2048]{1,0:T(1,128)S(1)}, u32[]{:S(2)}, u32[]{:S(2)}) %collective-permute-start.3) | collective-permute-done | bytes 8224 | tf_op jit(solution)/shard_map/cond/branch_1_fun/ppermute | solution.py:784
  16.8 3.5 %local_stats.1 = (f32[3,8,256]{2,1,0:T(8,128)S(1)}, f32[1,256]{1,0:T(1,128)S(1)}, bf16[4,256,1024]{2,1,0:T(8,128)(2,1)S(1)}, bf16[2,128,4096]{2,1,0:T(8,128)(2,1)S(1)}) custom-call(s32[3]{0:T(128)S(1)} %pad_add_fusion.place_ref, s32[1,128]{1,0:T(1,128)S(1)} %copy-done.1, bf16[1,128,2048]{2,1,0:T(8,128)(2,1)} %k_ref.5, bf16[1,128,2048]{2,1,0:T(8,128)(2,1)} %v_ref.5, ...), custom_call_target="tpu_custom_call" | custom-call | flops 1 | bytes 1 | tf_op jit(solution)/shard_map/local_stats/pallas_call | solution.py:452
  20.4 1.2 %router_gate.1.gates = f32[1,256]{1,0:T(1,128)S(1)} custom-call(s32[3]{0:T(128)S(1)} %pad_add_fusion.place_ref, f32[1,256]{1,0:T(1,128)S(1)} %get-tuple-element.117.live_ref, bf16[2,128,4096]{2,1,0:T(8,128)(2,1)S(1)} %get-tuple-element.118.rows_x, f32[1,4096]{1,0:T(1,128)S(1)} %get-tuple-element.119.w_ref), custom_call_target="tpu_custom_call" | custom-call | flops 1 | bytes 1 | tf_op jit(solution)/shard_map/router_gate/pallas_call | solution.py:358
  21.6 1.3 %cross_stats.1 = (bf16[4,256,512]{2,1,0:T(8,128)(2,1)S(1)}, f32[3,4,256]{2,1,0:T(4,128)S(1)}, bf16[2,4,256,256]{3,2,1,0:T(8,128)(2,1)S(1)}, f32[4,4,256]{2,1,0:T(4,128)S(1)}) custom-call(s32[3]{0:T(128)S(1)} %pad_add_fusion.place_ref, bf16[4,256,1024]{2,1,0:T(8,128)(2,1)S(1)} %get-tuple-element.120.pair, ...), custom_call_target="tpu_custom_call" | custom-call | flops 1 | bytes 1 | tf_op jit(solution)/shard_map/cross_stats/pallas_call | solution.py:505
  22.9 1.2 %collective-permute-start.8 = (f32[4,4,256]{2,1,0:T(4,128)S(1)}, f32[4,4,256]{2,1,0:T(4,128)S(1)}, u32[]{:S(2)}, u32[]{:S(2)}) collective-permute-start(f32[4,4,256]{2,1,0:T(4,128)S(1)} %get-tuple-element.126), channel_id=1, source_target_pairs={{0,2},{1,3},{2,0},{3,1},{4,6},{5,7},{6,4},{7,5},{8,10},{9,11},{10,... | collective-permute-start | bytes 49160 | tf_op jit(solution)/shard_map/ppermute | solution.py:772
  24.1 2.9 %near_grad.1 = (f32[256,512]{1,0:T(8,128)S(1)}, bf16[2,128,512]{2,1,0:T(8,128)(2,1)}, bf16[2,128,512]{2,1,0:T(8,128)(2,1)}, f32[1,256]{1,0:T(1,128)S(1)}) custom-call(s32[3]{0:T(128)S(1)} %pad_add_fusion.place_ref, bf16[4,256,1024]{2,1,0:T(8,128)(2,1)S(1)} %get-tuple-element.120.pair, f32[3,8,256]{2,1,0:T(8,128)S(1)} %get-tuple-element.122.local, ...), custom_call_target="tpu_custom_call" | custom-call | flops 1 | bytes 1 | tf_op jit(solution)/shard_map/near_grad/pallas_call | solution.py:572
  27.0 2.0 %cross_grad.1 = (bf16[2,128,512]{2,1,0:T(8,128)(2,1)}, bf16[2,128,512]{2,1,0:T(8,128)(2,1)}, bf16[256,512]{1,0:T(8,128)(2,1)S(1)}, bf16[2,256,512]{2,1,0:T(8,128...) custom-call(s32[3]{0:T(128)S(1)} %pad_add_fusion.place_ref, ...), custom_call_target="tpu_custom_call" | custom-call | flops 1 | bytes 1 | tf_op jit(solution)/shard_map/cross_grad/pallas_call | solution.py:617
  29.0 0.9 %collective-permute-start.9 = (bf16[2,128,512]{2,1,0:T(8,128)(2,1)}, bf16[2,128,512]{2,1,0:T(8,128)(2,1)S(1)}, u32[]{:S(2)}, u32[]{:S(2)}) collective-permute-start(bf16[2,128,512]{2,1,0:T(8,128)(2,1)} %get-tuple-element.137), channel_id=1, source_target_pairs={{0,2},{1,3},{2,0},{3,1},{4,6},{5,7},{6,4},{7,5},{8,10},{9,11},{10,... | collective-permute-start | bytes 786440 | tf_op jit(solution)/shard_map/ppermute | solution.py:772
  29.9 13.7 %conditional.4 = (bf16[3,128,1024]{2,1,0:T(8,128)(2,1)}, bf16[3,128,1024]{2,1,0:T(8,128)(2,1)}, f32[512]{0:T(512)S(1)}) conditional(s32[]{:T(128)} %bitcast.5, () %tuple.35, (s32[1,128]{1,0:T(1,128)S(1)}, f32[1,256]{1,0:T(1,128)S(1)}, f32[1,256]{1,0:T(1,128)S(1)}, bf16[2,128,4096]{2,1,0:T(8,128)(2,1)S(1)}, s32[3]{0:T(128)S(1)}, ...), branch_computations={%region_2.3_spmd, %region_3.7_spmd} | conditional | flops 16388 | bytes 3414220 | solution.py:778
  29.9 1.0 %router_terms.1 = f32[8,4,1,512]{3,2,1,0:T(1,128)} custom-call(f32[1,256]{1,0:T(1,128)S(1)} %get-tuple-element.64.gates_ref, f32[1,256]{1,0:T(1,128)S(1)} %get-tuple-element.65.sum_ref, bf16[2,128,4096]{2,1,0:T(8,128)(2,1)S(1)} %get-tuple-element.66.rows_x), custom_call_target="tpu_custom_call" | custom-call | flops 1 | bytes 1 | tf_op jit(solution)/shard_map/cond/branch_1_fun/router_terms/pallas_call | solution.py:754
  31.0 5.1 %all-to-all-start = ((f32[32,1,512]{2,1,0:T(1,128)}), f32[32,1,512]{2,1,0:T(1,128)S(1)}, u32[]{:S(2)}, u32[]{:S(2)}) async-start(f32[32,1,512]{2,1,0:T(1,128)} %bitcast.1), calls=%async_computation | async-start | bytes 131072 | tf_op jit(solution)/shard_map/cond/branch_1_fun/all_to_all | solution.py:804
  36.2 6.0 %conditional = (bf16[3,128,1024]{2,1,0:T(8,128)(2,1)}, bf16[3,128,1024]{2,1,0:T(8,128)(2,1)}) conditional(s32[]{:T(128)} %bitcast, () %tuple.23, (s32[3]{0:T(128)S(1)}, bf16[4,256,1024]{2,1,0:T(8,128)(2,1)S(1)}, f32[3,8,256]{2,1,0:T(8,128)S(1)}, f32[2,4,256]{2,1,0:T(4,128)S(1)}, f32[1,256]{1,0:T(1,128)S(1)}, ...), branch_computations={%region_4.4_spmd, %region_5.5_spmd} | conditional | flops 1 | bytes 3145785 | solution.py:778
  36.2 3.6 %far_grad.1 = (bf16[3,128,1024]{2,1,0:T(8,128)(2,1)}, bf16[3,128,1024]{2,1,0:T(8,128)(2,1)S(1)}) custom-call(s32[3]{0:T(128)S(1)} %get-tuple-element.51.place_ref, bf16[4,256,1024]{2,1,0:T(8,128)(2,1)S(1)} %get-tuple-element.52.pair, f32[3,8,256]{2,1,0:T(8,128)S(1)} %get-tuple-element.53.local, f32[2,4,256]{2,1,0:T(4,128)S(1)} %get-tuple-element.54.final, ...), custom_call_target="tpu_custom_call" | custom-call | flops 1 | bytes 1 | tf_op jit(solution)/shard_map/cond/branch_1_fun/cond/branch_1_fun/far_grad/pallas_call | solution.py:664
  40.0 2.2 %collective-permute-done = bf16[3,128,1024]{2,1,0:T(8,128)(2,1)} collective-permute-done((bf16[3,128,1024]{2,1,0:T(8,128)(2,1)S(1)}, bf16[3,128,1024]{2,1,0:T(8,128)(2,1)}, u32[]{:S(2)}, u32[]{:S(2)}) %collective-permute-start) | collective-permute-done | bytes 786464 | tf_op jit(solution)/shard_map/cond/branch_1_fun/cond/branch_1_fun/ppermute | solution.py:772
  42.2 1.3 %all-to-all-done = f32[32,1,512]{2,1,0:T(1,128)S(1)} async-done(((f32[32,1,512]{2,1,0:T(1,128)}), f32[32,1,512]{2,1,0:T(1,128)S(1)}, u32[]{:S(2)}, u32[]{:S(2)}) %all-to-all-start) | async-done | bytes 65568 | tf_op jit(solution)/shard_map/cond/branch_1_fun/all_to_all | solution.py:804
  43.6 3.4 %join.1 = (f32[1,128,2048]{2,1,0:T(8,128)}, f32[1,128,2048]{2,1,0:T(8,128)}, f32[1,128,2048]{2,1,0:T(8,128)}) custom-call(s32[3]{0:T(128)S(1)} %pad_add_fusion.place_ref, bf16[3,128,1024]{2,1,0:T(8,128)(2,1)} %get-tuple-element.135.own, bf16[3,128,1024]{2,1,0:T(8,128)(2,1)} %get-tuple-element.136.sib, ...), custom_call_target="tpu_custom_call" | custom-call | flops 1 | bytes 1 | tf_op jit(solution)/shard_map/join/pallas_call | solution.py:716
  (26 shorter events, 1.9 us)
Async XLA Ops:
  0.6 9.0 %copy-start.1 = (s32[1,128]{1,0:T(1,128)S(1)}, s32[1,128]{1,0:T(1,128)}, u32[]{:S(2)}) copy-start(s32[1,128]{1,0:T(1,128)} %pos_ref.4) | copy-start | bytes 1540
  1.3 6.6 %collective-permute-start.4 = (f32[1,512]{1,0:T(1,128)S(1)}, f32[1,512]{1,0:T(1,128)S(1)}, u32[]{:S(2)}, u32[]{:S(2)}) collective-permute-start(f32[1,512]{1,0:T(1,128)S(1)} %bitcast.9), channel_id=1, source_target_pairs={{0,4},{4,0},{8,12},{12,8},{16,20},{20,16},{24,28},{28,24},{1,5},{5... | collective-permute-start | bytes 6152 | tf_op jit(solution)/shard_map/ppermute | solution.py:784
  6.3 5.3 %copy-start = (bf16[1,128,4096]{2,1,0:T(8,128)(2,1)S(1)}, bf16[1,128,4096]{2,1,0:T(8,128)(2,1)}, u32[]{:S(2)}) copy-start(bf16[1,128,4096]{2,1,0:T(8,128)(2,1)} %x_ref.1) | copy-start | bytes 3145732
  6.3 15.2 %collective-permute-start.7 = (bf16[2,128,512]{2,1,0:T(8,128)(2,1)S(1)}, bf16[2,128,512]{2,1,0:T(8,128)(2,1)S(1)}, u32[]{:S(2)}, u32[]{:S(2)}) collective-permute-start(bf16[2,128,512]{2,1,0:T(8,128)(2,1)S(1)} %get-tuple-element.121), channel_id=1, source_target_pairs={{0,3},{1,2},{2,1},{3,0},{4,7},{5,6},{6,5},{7,4},{8,11},{9,10},{10,... | collective-permute-start | bytes 786440 | tf_op jit(solution)/shard_map/ppermute | solution.py:772
  7.0 14.6 %collective-permute-start.6 = (bf16[2,128,512]{2,1,0:T(8,128)(2,1)S(1)}, bf16[2,128,512]{2,1,0:T(8,128)(2,1)S(1)}, u32[]{:S(2)}, u32[]{:S(2)}) collective-permute-start(bf16[2,128,512]{2,1,0:T(8,128)(2,1)S(1)} %get-tuple-element.112), channel_id=1, source_target_pairs={{0,2},{1,3},{2,0},{3,1},{4,6},{5,7},{6,4},{7,5},{8,10},{9,11},{10,... | collective-permute-start | bytes 786440 | tf_op jit(solution)/shard_map/ppermute | solution.py:772
  7.9 3.7 %collective-permute-start.5 = (f32[1,1024]{1,0:T(1,128)S(1)}, f32[1,1024]{1,0:T(1,128)S(1)}, u32[]{:S(2)}, u32[]{:S(2)}) collective-permute-start(f32[1,1024]{1,0:T(1,128)S(1)} %pad_maximum_fusion.2), channel_id=1, source_target_pairs={{0,8},{4,12},{8,0},{12,4},{16,24},{20,28},{24,16},{28,20},{1,9},{5... | collective-permute-start | bytes 12296 | tf_op jit(solution)/shard_map/ppermute | solution.py:784
  11.7 5.1 %collective-permute-start.1 = (bf16[4,128,1024]{2,1,0:T(8,128)(2,1)S(1)}, bf16[4,128,1024]{2,1,0:T(8,128)(2,1)}, u32[]{:S(2)}, u32[]{:S(2)}) collective-permute-start(bf16[4,128,1024]{2,1,0:T(8,128)(2,1)S(1)} %get-tuple-element.48), channel_id=1, source_target_pairs={{0,1},{1,0},{2,3},{3,2},{4,5},{5,4},{6,7},{7,6},{8,9},{9,8},{10,11... | collective-permute-start | bytes 3145736 | tf_op jit(solution)/shard_map/cond/branch_1_fun/ppermute | solution.py:772
  11.7 5.1 %collective-permute-start.2 = (bf16[1,128,4096]{2,1,0:T(8,128)(2,1)S(1)}, bf16[1,128,4096]{2,1,0:T(8,128)(2,1)}, u32[]{:S(2)}, u32[]{:S(2)}) collective-permute-start(bf16[1,128,4096]{2,1,0:T(8,128)(2,1)S(1)} %get-tuple-element.49), channel_id=1, source_target_pairs={{0,1},{1,0},{2,3},{3,2},{4,5},{5,4},{6,7},{7,6},{8,9},{9,8},{10,11... | collective-permute-start | bytes 3145736 | tf_op jit(solution)/shard_map/cond/branch_1_fun/ppermute | solution.py:772
  12.2 4.5 %collective-permute-start.3 = (f32[1,2048]{1,0:T(1,128)S(1)}, f32[1,2048]{1,0:T(1,128)S(1)}, u32[]{:S(2)}, u32[]{:S(2)}) collective-permute-start(f32[1,2048]{1,0:T(1,128)S(1)} %get-tuple-element.50), channel_id=1, source_target_pairs={{0,16},{4,20},{8,24},{12,28},{16,0},{20,4},{24,8},{28,12},{1,17},{... | collective-permute-start | bytes 24584 | tf_op jit(solution)/shard_map/cond/branch_1_fun/ppermute | solution.py:784
  22.9 4.1 %collective-permute-start.8 = (f32[4,4,256]{2,1,0:T(4,128)S(1)}, f32[4,4,256]{2,1,0:T(4,128)S(1)}, u32[]{:S(2)}, u32[]{:S(2)}) collective-permute-start(f32[4,4,256]{2,1,0:T(4,128)S(1)} %get-tuple-element.126), channel_id=1, source_target_pairs={{0,2},{1,3},{2,0},{3,1},{4,6},{5,7},{6,4},{7,5},{8,10},{9,11},{10,... | collective-permute-start | bytes 49160 | tf_op jit(solution)/shard_map/ppermute | solution.py:772
  29.0 14.6 %collective-permute-start.9 = (bf16[2,128,512]{2,1,0:T(8,128)(2,1)}, bf16[2,128,512]{2,1,0:T(8,128)(2,1)S(1)}, u32[]{:S(2)}, u32[]{:S(2)}) collective-permute-start(bf16[2,128,512]{2,1,0:T(8,128)(2,1)} %get-tuple-element.137), channel_id=1, source_target_pairs={{0,2},{1,3},{2,0},{3,1},{4,6},{5,7},{6,4},{7,5},{8,10},{9,11},{10,... | collective-permute-start | bytes 786440 | tf_op jit(solution)/shard_map/ppermute | solution.py:772
  29.9 13.7 %collective-permute-start.10 = (bf16[2,128,512]{2,1,0:T(8,128)(2,1)}, bf16[2,128,512]{2,1,0:T(8,128)(2,1)S(1)}, u32[]{:S(2)}, u32[]{:S(2)}) collective-permute-start(bf16[2,128,512]{2,1,0:T(8,128)(2,1)} %get-tuple-element.138), channel_id=1, source_target_pairs={{0,3},{1,2},{2,1},{3,0},{4,7},{5,6},{6,5},{7,4},{8,11},{9,10},{10,... | collective-permute-start | bytes 786440 | tf_op jit(solution)/shard_map/ppermute | solution.py:772
  31.0 12.6 %all-to-all-start = ((f32[32,1,512]{2,1,0:T(1,128)}), f32[32,1,512]{2,1,0:T(1,128)S(1)}, u32[]{:S(2)}, u32[]{:S(2)}) async-start(f32[32,1,512]{2,1,0:T(1,128)} %bitcast.1), calls=%async_computation | async-start | bytes 131072 | tf_op jit(solution)/shard_map/cond/branch_1_fun/all_to_all | solution.py:804
  39.8 2.4 %collective-permute-start = (bf16[3,128,1024]{2,1,0:T(8,128)(2,1)S(1)}, bf16[3,128,1024]{2,1,0:T(8,128)(2,1)}, u32[]{:S(2)}, u32[]{:S(2)}) collective-permute-start(bf16[3,128,1024]{2,1,0:T(8,128)(2,1)S(1)} %get-tuple-element.61), channel_id=1, source_target_pairs={{0,1},{1,0},{2,3},{3,2},{4,5},{5,4},{6,7},{7,6},{8,9},{9,8},{10,11... | collective-permute-start | bytes 2359304 | tf_op jit(solution)/shard_map/cond/branch_1_fun/cond/branch_1_fun/ppermute | solution.py:772
  43.6 3.4 %copy-start.2 = (f32[512]{0:T(512)}, f32[512]{0:T(512)S(1)}, u32[]{:S(2)}) copy-start(f32[512]{0:T(512)S(1)} %get-tuple-element.111) | copy-start | bytes 6148

commit v8 on v7

--- a/solution.py
+++ b/solution.py
@@ -263,7 +263,8 @@
     return jnp.where(mask, keys.astype(F32), MARK).astype(BF16)
 
 
-def cross_pack_kernel(place_ref, pos_ref, k_ref, v_ref, q_ref, dg_ref, straight, diag, wide, sems):
+def cross_pack_kernel(place_ref, pos_ref, w_ref, k_ref, v_ref, q_ref, dg_ref, straight, diag, w_out, wide, sems):
+    w_out[...] = w_ref[...].astype(F32).reshape(w_out.shape)
     slots, width = straight.shape[1], straight.shape[2]
     half = k_ref.shape[-1] // 2
     core, chip = place_ref[0], place_ref[1]
@@ -294,20 +295,20 @@
             end[1] = wide[i].astype(BF16)
 
 
-def cross_pack(place, route_pos, keys, values, queries, d_gated):
+def cross_pack(place, route_pos, w_router, keys, values, queries, d_gated):
     _, slots, full = keys.shape
     cross = pltpu.VMEM((2, slots, full // 4), BF16)
     hbm = pl.BlockSpec(memory_space=pltpu.HBM)
     return pl.pallas_call(
         cross_pack_kernel,
-        out_shape=[cross, cross],
-        in_specs=[SMEM, VMEM, hbm, hbm, hbm, hbm],
-        out_specs=[VMEM] * 2,
+        out_shape=[cross, cross, jax.ShapeDtypeStruct((1, w_router.shape[0]), F32)],
+        in_specs=[SMEM, VMEM, VMEM, hbm, hbm, hbm, hbm],
+        out_specs=[VMEM] * 3,
         scratch_shapes=[pltpu.VMEM((2, slots, full // 4), F32), pltpu.SemaphoreType.DMA((4,))],
         compiler_params=params(),
         cost_estimate=cost(0, 10 * slots * full),
         name="cross_pack",
-    )(place, route_pos, *in_hbm(keys, values, queries, d_gated))
+    )(place, route_pos, w_router, *in_hbm(keys, values, queries, d_gated))
 
 
 def sib_pack_kernel(place_ref, pos_ref, k_ref, v_ref, q_ref, dg_ref, out, wide, sems):
@@ -341,7 +342,7 @@
     )(place, route_pos, *in_hbm(keys, values, queries, d_gated))
 
 
-def pair_gate_kernel(parts, place_ref, live_ref, rows_x, w_ref, out_ref):
+def pair_gate_kernel(parts, place_ref, live_ref, rows_x, w_ref, local, stats, out_ref, message):
     chunk = w_ref.shape[1] // parts
     slots = rows_x.shape[1]
     for i in range(2):
@@ -352,18 +353,24 @@
             total = total + nt(w_rows, rows_x[i, :, cols])
         lanes = slice(i * slots, (i + 1) * slots)
         out_ref[:, lanes] = live_ref[:, lanes] / (1.0 + jnp.exp(-total[0:1]))
-
-
-def pair_gate(place, live, rows_x, w_full, parts):
+    first = place_ref[1] == 0
+    heads = stats.shape[1]
+    for i in range(3):
+        message[i] = jnp.where(first, stats[i], local[i, heads:])
+    message[3] = jnp.broadcast_to(out_ref[...], message.shape[1:])
+
+
+def pair_gate(place, live, rows_x, w_full, local, stats, parts):
+    _, heads, lanes = stats.shape
     return pl.pallas_call(
         functools.partial(pair_gate_kernel, parts),
-        out_shape=jax.ShapeDtypeStruct(live.shape, F32),
-        in_specs=[SMEM] + [VMEM] * 3,
-        out_specs=VMEM,
+        out_shape=[jax.ShapeDtypeStruct(live.shape, F32), jax.ShapeDtypeStruct((4, heads, lanes), F32)],
+        in_specs=[SMEM] + [VMEM] * 5,
+        out_specs=[VMEM] * 2,
         compiler_params=params(),
         cost_estimate=cost(16 * rows_x.size, rows_x.size * 2),
         name="router_gate",
-    )(place, live, rows_x, w_full)
+    )(place, live, rows_x, w_full, local, stats)
 
 
 def local_mask(core, pair):
@@ -466,7 +473,7 @@
     )(place, route_pos, *in_hbm(keys, values, queries, d_gated), sib, x_routed, x_sib)
 
 
-def cross_stats_kernel(scale, place_ref, pair, straight, diag, local, gates, cross, stats, kept, message):
+def cross_stats_kernel(scale, place_ref, pair, straight, diag, cross, stats, kept):
     slots, width = straight.shape[1], straight.shape[2]
     chip = place_ref[1]
     top, bottom = slice(0, slots), slice(slots, 2 * slots)
@@ -494,28 +501,24 @@
         cols = slice(h * HEAD, (h + 1) * HEAD)
         scores = jnp.where(mask, nt(cross[0, :, cols], cross[2, :, cols]) * scale, NEG_FILL)
         kept_stats(scores, nt(cross[1, :, cols], cross[3, :, cols]), kept, stats, h)
-    for i in range(3):
-        message[i] = jnp.where(chip == 0, stats[i], local[i, heads:])
-    message[3] = jnp.broadcast_to(gates[...], message.shape[1:])
-
-
-def cross_stats(place, pair, straight, diag, local, gates):
+
+
+def cross_stats(place, pair, straight, diag):
     _, slots, width = straight.shape
     heads = width // HEAD
     return pl.pallas_call(
         functools.partial(cross_stats_kernel, HEAD**-0.5),
         out_shape=[
-            jax.ShapeDtypeStruct((4, 2 * slots, width), BF16),
+            pltpu.VMEM((4, 2 * slots, width), BF16),
             jax.ShapeDtypeStruct((3, heads, 2 * slots), F32),
-            jax.ShapeDtypeStruct((2, heads, 2 * slots, 2 * slots), BF16),
-            jax.ShapeDtypeStruct((4, heads, 2 * slots), F32),
+            pltpu.VMEM((2, heads, 2 * slots, 2 * slots), BF16),
         ],
-        in_specs=[SMEM] + [VMEM] * 5,
-        out_specs=[VMEM] * 4,
+        in_specs=[SMEM] + [VMEM] * 3,
+        out_specs=[VMEM] * 3,
         compiler_params=params(),
         cost_estimate=cost(16 * slots * slots * width, 32 * slots * width, 4 * slots * slots * heads),
         name="cross_stats",
-    )(place, pair, straight, diag, local, gates)
+    )(place, pair, straight, diag)
 
 
 NONE = (-3e38, 0.0, 0.0)
@@ -568,10 +571,10 @@
     _, rows, half = pair.shape
     slots = rows // 2
     width = half // 2
-    out = jax.ShapeDtypeStruct((2, slots, width), BF16)
+    out = pltpu.VMEM((2, slots, width), BF16)
     return pl.pallas_call(
         functools.partial(near_grad_kernel, HEAD**-0.5),
-        out_shape=[jax.ShapeDtypeStruct((2 * slots, width), F32), out, out, jax.ShapeDtypeStruct(gates.shape, F32)],
+        out_shape=[pltpu.VMEM((2 * slots, width), F32), out, out, jax.ShapeDtypeStruct(gates.shape, F32)],
         in_specs=[SMEM] + [VMEM] * 4,
         out_specs=[VMEM] * 4,
         compiler_params=params(),
@@ -613,7 +616,7 @@
 def cross_grad(place, cross, kept, stats, local, heard, gates, near_dq, near_sum):
     _, rows, width = cross.shape
     slots = rows // 2
-    out = jax.ShapeDtypeStruct((2, slots, width), BF16)
+    out = pltpu.VMEM((2, slots, width), BF16)
     return pl.pallas_call(
         functools.partial(cross_grad_kernel, HEAD**-0.5),
         out_shape=[
@@ -788,8 +791,8 @@
 
     def exchange_phase(x_routed, w_part, theirs):
         sib, x_sib = send(theirs, 1), send(x_routed, 1)
-        step = 4
-        while step < ndp:
+        step = 2
+        while 2 * step < ndp:
             w_part = widen(w_part, step)
             step *= 2
         return sib, x_sib, w_part
@@ -805,18 +808,17 @@
         own_out, sib_in = beside(grad_phase, after(place, terms), *operands)
         return own_out, sib_in, jnp.sum(shared, axis=0)[0] / float(ndp * n * slots // 2)
 
-    w_part = w_router.reshape(1, -1).astype(F32)
-    out_s, out_d = cross_pack(place, route_pos, keys, values, queries, d_gated)
+    out_s, out_d, w_part = cross_pack(place, route_pos, w_router, keys, values, queries, d_gated)
     in_s, in_d = send(out_s, 2), send(out_d, 3)
     theirs = sib_pack(place, after(route_pos, out_s), keys, values, queries, d_gated)
     if ndp > 1:
-        w_part = widen(w_part, 1)
-    if ndp > 2:
-        w_part = widen(w_part, 2, theirs)
+        w_part = widen(w_part, 1, theirs)
     sib, x_sib, w_part = beside(exchange_phase, x_routed, w_part, theirs)
     local, live, pair, rows_x = local_stats(place, route_pos, keys, values, queries, d_gated, sib, x_routed, x_sib)
-    gates = pair_gate(place, live, rows_x, w_part, ndp)
-    cross, stats, kept_cross, message = cross_stats(place, pair, in_s, in_d, local, gates)
+    cross, stats, kept_cross = cross_stats(place, pair, in_s, in_d)
+    if ndp > 2:
+        w_part = widen(w_part, ndp // 2, stats)
+    gates, message = pair_gate(place, live, rows_x, w_part, local, stats, ndp)
     heard = send(message, 2)
     near_dq, near_own, near_sib, near_sum = near_grad(place, pair, local, stats, gates)
     back_s, back_d, dq_low, keep, final, sums = cross_grad(

time: 47.3 us -> 49.2 us (1.040)
  local copies, waits for them, and re-layouts: 0.02 us -> 2.12 us
  waiting for transfers between devices: 5.63 us -> 7.11 us
  Pallas kernels: 22.8 us -> 22 us
  other arithmetic: 0.87 us -> 0.18 us
    unnamed x6 -> x12, local copies, waits for them, and re-layouts: 0.02 us -> 2.12 us
    ppermute x8, starting transfers between devices: 4.51 us -> 6.23 us  [send(): return lax.ppermute(a, 'ctx', [(i, i ^ flip) for i in range(n)])]
    ppermute x3, starting transfers between devices: 7.2 us -> 5.68 us  [near_dp(): return lax.ppermute(part, 'dp', [(i, i ^ step) for i in range(ndp)])]
    all_to_all x1, waiting for transfers between devices: 1.35 us -> 2.57 us  [router_phase(): lax.all_to_all(terms.reshape(ndp * n, 1, chunk), ('dp', 'ctx'), 0, 0, til...]
    pallas_call x1, Pallas kernels: 2.95 us -> 2.19 us  [near_grad(): pl.pallas_call(functools.partial(near_grad_kernel, HEAD ** (-0.5)), out_s...]
    convert_element_type x1 -> x0, other arithmetic: 0.69 us -> none  [swap_body(): w_part = w_router.reshape(1, -1).astype(F32)]
    all_to_all x1, starting transfers between devices: 5.15 us -> 4.65 us  [router_phase(): lax.all_to_all(terms.reshape(ndp * n, 1, chunk), ('dp', 'ctx'), 0, 0, til...]
  transfers between devices with their start and end apart: 12 -> 12, of which waited for: 4 -> 5; matrix products, arithmetic and copies ran while one was open for 0% -> 0% of each run, Pallas kernels for 34% -> 28%
where the time goes in v8:
time: 49.2 us; the launch traced here: 48.9 us
  Pallas kernels  22 us (45%)
  starting transfers between devices  16.6 us (34%)
  waiting for transfers between devices  7.11 us (14%)
  local copies, waits for them, and re-layouts  2.12 us (4%)
  between operations  0.83 us (2%)
    ppermute x8, starting transfers between devices, send(): return lax.ppermute(a, 'ctx', [(i, i ^ flip) for i in range(n)])  6.23 us
    ppermute x3, starting transfers between devices, near_dp(): return lax.ppermute(part, 'dp', [(i, i ^ step) for i in range(ndp)])  5.68 us
    all_to_all x1, starting transfers between devices, router_phase(): lax.all_to_all(terms.reshape(ndp * n, 1, chunk), ('dp', 'ctx'), 0, 0, til...  4.65 us
    pallas_call x1, Pallas kernels, far_grad(): pl.pallas_call(functools.partial(far_grad_kernel, HEAD ** (-0.5)), out_sh...  3.61 us
    pallas_call x1, Pallas kernels, local_stats(): pl.pallas_call(functools.partial(local_stats_kernel, HEAD ** (-0.5)), out...  3.51 us
    pallas_call x1, Pallas kernels, join(): pl.pallas_call(join_kernel, out_shape=[out] * 3, in_specs=[SMEM] + [anywh...  3.38 us
    all_to_all x1, waiting for transfers between devices, router_phase(): lax.all_to_all(terms.reshape(ndp * n, 1, chunk), ('dp', 'ctx'), 0, 0, til...  2.57 us
    ppermute x8, waiting for transfers between devices, send(): return lax.ppermute(a, 'ctx', [(i, i ^ flip) for i in range(n)])  2.33 us
  transfers between devices with their start and end apart: 12, of which 5 were waited for; matrix products, arithmetic and copies ran while one was open for 0% of the time, Pallas kernels for 28%

profile of v8, /device:TPU:0, one launch (start us, length us, event | category | flops | bytes accessed | tf_op | source)
XLA Modules:
  0.0 48.9 jit_solution(5383399589635302135)
XLA Ops:
  1.4 1.9 %cross_pack.1 = (bf16[2,128,512]{2,1,0:T(8,128)(2,1)S(1)}, bf16[2,128,512]{2,1,0:T(8,128)(2,1)S(1)}, f32[1,512]{1,0:T(1,128)S(1)}) custom-call(s32[3]{0:T(128)S(1)} %pad_add_fusion.place_ref, s32[1,128]{1,0:T(1,128)} %pos_ref.4, bf16[512]{0:T(512)(128)(2,1)S(1)} %copy-done.2, bf16[1,128,2048]{2,1,0:T(8,128)(2,1)} %k_ref.5, bf16[1,128,2048]{2,1,0:T(8,128)(2,1)} %v_ref.5, ...), custom_call_target="tpu_custom_call" | custom-call | flops 1 | bytes 1 | tf_op jit(solution)/shard_map/cross_pack/pallas_call | solution.py:302
  3.4 2.4 %collective-permute-start.7 = (bf16[2,128,512]{2,1,0:T(8,128)(2,1)S(1)}, bf16[2,128,512]{2,1,0:T(8,128)(2,1)S(1)}, u32[]{:S(2)}, u32[]{:S(2)}) collective-permute-start(bf16[2,128,512]{2,1,0:T(8,128)(2,1)S(1)} %get-tuple-element.125), channel_id=1, source_target_pairs={{0,3},{1,2},{2,1},{3,0},{4,7},{5,6},{6,5},{7,4},{8,11},{9,10},{10,... | collective-permute-start | bytes 786440 | tf_op jit(solution)/shard_map/ppermute | solution.py:775
  6.4 1.5 %collective-permute-start.4 = (f32[1,512]{1,0:T(1,128)S(1)}, f32[1,512]{1,0:T(1,128)S(1)}, u32[]{:S(2)}, u32[]{:S(2)}) collective-permute-start(f32[1,512]{1,0:T(1,128)S(1)} %get-tuple-element.117), channel_id=1, source_target_pairs={{0,4},{4,0},{8,12},{12,8},{16,20},{20,16},{24,28},{28,24},{1,5},{5... | collective-permute-start | bytes 6152 | tf_op jit(solution)/shard_map/ppermute | solution.py:787
  7.9 1.8 %sib_pack.1 = bf16[4,128,1024]{2,1,0:T(8,128)(2,1)S(1)} custom-call(s32[3]{0:T(128)S(1)} %pad_add_fusion.place_ref, s32[1,128]{1,0:T(1,128)S(1)} %copy-done.4, bf16[1,128,2048]{2,1,0:T(8,128)(2,1)} %k_ref.5, bf16[1,128,2048]{2,1,0:T(8,128)(2,1)} %v_ref.5, bf16[1,128,2048]{2,1,0:T(8,128)(2,1)} %q_ref.5, f32[1,128,2048]{2,1,0:T(8,128)} %dg_ref.5), custom_call_target="tpu_custom_call" | custom-call | flops 1 | bytes 1 | tf_op jit(solution)/shard_map/sib_pack/pallas_call | solution.py:333
  10.0 4.4 %conditional.3 = (bf16[4,128,1024]{2,1,0:T(8,128)(2,1)}, bf16[1,128,4096]{2,1,0:T(8,128)(2,1)}, f32[1,2048]{1,0:T(1,128)S(1)}) conditional(s32[]{:T(128)} %bitcast.5, () %tuple.37, (bf16[4,128,1024]{2,1,0:T(8,128)(2,1)S(1)}, bf16[1,128,4096]{2,1,0:T(8,128)(2,1)S(1)}, f32[1,1024]{1,0:T(1,128)S(1)}) %tuple.52), branch_computations={%region_0.1_spmd, %region_1.2_spmd} | conditional | flops 2048 | bytes 8421520 | solution.py:781
  10.6 1.6 %collective-permute-start.3 = (f32[1,1024]{1,0:T(1,128)S(1)}, f32[1,1024]{1,0:T(1,128)S(1)}, u32[]{:S(2)}, u32[]{:S(2)}) collective-permute-start(f32[1,1024]{1,0:T(1,128)S(1)} %get-tuple-element.50), channel_id=1, source_target_pairs={{0,8},{4,12},{8,0},{12,4},{16,24},{20,28},{24,16},{28,20},{1,9},{5... | collective-permute-start | bytes 12296 | tf_op jit(solution)/shard_map/cond/branch_1_fun/ppermute | solution.py:787
  12.2 2.0 %collective-permute-done.3 = f32[1,1024]{1,0:T(1,128)S(1)} collective-permute-done((f32[1,1024]{1,0:T(1,128)S(1)}, f32[1,1024]{1,0:T(1,128)S(1)}, u32[]{:S(2)}, u32[]{:S(2)}) %collective-permute-start.3) | collective-permute-done | bytes 4128 | tf_op jit(solution)/shard_map/cond/branch_1_fun/ppermute | solution.py:787
  14.4 2.6 %collective-permute-start.5 = (f32[1,2048]{1,0:T(1,128)S(1)}, f32[1,2048]{1,0:T(1,128)S(1)}, u32[]{:S(2)}, u32[]{:S(2)}) collective-permute-start(f32[1,2048]{1,0:T(1,128)S(1)} %get-tuple-element.123), channel_id=1, source_target_pairs={{0,16},{4,20},{8,24},{12,28},{16,0},{20,4},{24,8},{28,12},{1,17},{... | collective-permute-start | bytes 24584 | tf_op jit(solution)/shard_map/ppermute | solution.py:787
  17.0 3.5 %local_stats.1 = (f32[3,8,256]{2,1,0:T(8,128)S(1)}, f32[1,256]{1,0:T(1,128)S(1)}, bf16[4,256,1024]{2,1,0:T(8,128)(2,1)S(1)}, bf16[2,128,4096]{2,1,0:T(8,128)(2,1)S(1)}) custom-call(s32[3]{0:T(128)S(1)} %pad_add_fusion.place_ref, s32[1,128]{1,0:T(1,128)S(1)} %copy-done.4, bf16[1,128,2048]{2,1,0:T(8,128)(2,1)} %k_ref.5, bf16[1,128,2048]{2,1,0:T(8,128)(2,1)} %v_ref.5, ...), custom_call_target="tpu_custom_call" | custom-call | flops 1 | bytes 1 | tf_op jit(solution)/shard_map/local_stats/pallas_call | solution.py:459
  20.5 1.3 %cross_stats.1 = (bf16[4,256,512]{2,1,0:T(8,128)(2,1)S(1)}, f32[3,4,256]{2,1,0:T(4,128)S(1)}, bf16[2,4,256,256]{3,2,1,0:T(8,128)(2,1)S(1)}) custom-call(s32[3]{0:T(128)S(1)} %pad_add_fusion.place_ref, bf16[4,256,1024]{2,1,0:T(8,128)(2,1)S(1)} %get-tuple-element.124.pair, bf16[2,128,512]{2,1,0:T(8,128)(2,1)S(1)} %collective-permute-done.6.straight, ...), custom_call_target="tpu_custom_call" | custom-call | flops 1 | bytes 1 | tf_op jit(solution)/shard_map/cross_stats/pallas_call | solution.py:509
  21.9 1.2 %router_gate.1 = (f32[1,256]{1,0:T(1,128)S(1)}, f32[4,4,256]{2,1,0:T(4,128)S(1)}) custom-call(s32[3]{0:T(128)S(1)} %pad_add_fusion.place_ref, f32[1,256]{1,0:T(1,128)S(1)} %get-tuple-element.121.live_ref, bf16[2,128,4096]{2,1,0:T(8,128)(2,1)S(1)} %get-tuple-element.122.rows_x, f32[1,4096]{1,0:T(1,128)S(1)} %pad_maximum_fusion.1.w_ref, ...), custom_call_target="tpu_custom_call" | custom-call | flops 1 | bytes 1 | tf_op jit(solution)/shard_map/router_gate/pallas_call | solution.py:365
  23.1 1.4 %collective-permute-start.8 = (f32[4,4,256]{2,1,0:T(4,128)S(1)}, f32[4,4,256]{2,1,0:T(4,128)S(1)}, u32[]{:S(2)}, u32[]{:S(2)}) collective-permute-start(f32[4,4,256]{2,1,0:T(4,128)S(1)} %get-tuple-element.132), channel_id=1, source_target_pairs={{0,2},{1,3},{2,0},{3,1},{4,6},{5,7},{6,4},{7,5},{8,10},{9,11},{10,... | collective-permute-start | bytes 49160 | tf_op jit(solution)/shard_map/ppermute | solution.py:775
  24.6 2.2 %near_grad.1 = (f32[256,512]{1,0:T(8,128)S(1)}, bf16[2,128,512]{2,1,0:T(8,128)(2,1)S(1)}, bf16[2,128,512]{2,1,0:T(8,128)(2,1)S(1)}, f32[1,256]{1,0:T(1,128)S(1)}) custom-call(s32[3]{0:T(128)S(1)} %pad_add_fusion.place_ref, bf16[4,256,1024]{2,1,0:T(8,128)(2,1)S(1)} %get-tuple-element.124.pair, f32[3,8,256]{2,1,0:T(8,128)S(1)} %get-tuple-element.128.local, ...), custom_call_target="tpu_custom_call" | custom-call | flops 1 | bytes 1 | tf_op jit(solution)/shard_map/near_grad/pallas_call | solution.py:575
  26.8 0.7 %copy-done = bf16[2,128,512]{2,1,0:T(8,128)(2,1)} copy-done((bf16[2,128,512]{2,1,0:T(8,128)(2,1)}, bf16[2,128,512]{2,1,0:T(8,128)(2,1)S(1)}, u32[]{:S(2)}) %copy-start) | copy-done | bytes 262168
  27.5 1.9 %cross_grad.1 = (bf16[2,128,512]{2,1,0:T(8,128)(2,1)}, bf16[2,128,512]{2,1,0:T(8,128)(2,1)}, bf16[256,512]{1,0:T(8,128)(2,1)S(1)}, bf16[2,256,512]{2,1,0:T(8,128...) custom-call(s32[3]{0:T(128)S(1)} %pad_add_fusion.place_ref, ...), custom_call_target="tpu_custom_call" | custom-call | flops 1 | bytes 1 | tf_op jit(solution)/shard_map/cross_grad/pallas_call | solution.py:620
  30.1 0.8 %collective-permute-start.9 = (bf16[2,128,512]{2,1,0:T(8,128)(2,1)}, bf16[2,128,512]{2,1,0:T(8,128)(2,1)S(1)}, u32[]{:S(2)}, u32[]{:S(2)}) collective-permute-start(bf16[2,128,512]{2,1,0:T(8,128)(2,1)} %get-tuple-element.143), channel_id=1, source_target_pairs={{0,2},{1,3},{2,0},{3,1},{4,6},{5,7},{6,4},{7,5},{8,10},{9,11},{10,... | collective-permute-start | bytes 786440 | tf_op jit(solution)/shard_map/ppermute | solution.py:775
  31.1 14.4 %conditional.4 = (bf16[3,128,1024]{2,1,0:T(8,128)(2,1)}, bf16[3,128,1024]{2,1,0:T(8,128)(2,1)}, f32[512]{0:T(512)S(1)}) conditional(s32[]{:T(128)} %bitcast.5, () %tuple.36, (s32[1,128]{1,0:T(1,128)S(1)}, f32[1,256]{1,0:T(1,128)S(1)}, f32[1,256]{1,0:T(1,128)S(1)}, bf16[2,128,4096]{2,1,0:T(8,128)(2,1)S(1)}, s32[3]{0:T(128)S(1)}, ...), branch_computations={%region_2.3_spmd, %region_3.7_spmd} | conditional | flops 16388 | bytes 3414220 | solution.py:781
  31.1 1.0 %router_terms.1 = f32[8,4,1,512]{3,2,1,0:T(1,128)} custom-call(f32[1,256]{1,0:T(1,128)S(1)} %get-tuple-element.64.gates_ref, f32[1,256]{1,0:T(1,128)S(1)} %get-tuple-element.65.sum_ref, bf16[2,128,4096]{2,1,0:T(8,128)(2,1)S(1)} %get-tuple-element.66.rows_x), custom_call_target="tpu_custom_call" | custom-call | flops 1 | bytes 1 | tf_op jit(solution)/shard_map/cond/branch_1_fun/router_terms/pallas_call | solution.py:757
  32.1 4.6 %all-to-all-start = ((f32[32,1,512]{2,1,0:T(1,128)}), f32[32,1,512]{2,1,0:T(1,128)S(1)}, u32[]{:S(2)}, u32[]{:S(2)}) async-start(f32[32,1,512]{2,1,0:T(1,128)} %bitcast.1), calls=%async_computation | async-start | bytes 131072 | tf_op jit(solution)/shard_map/cond/branch_1_fun/all_to_all | solution.py:807
  36.8 6.0 %conditional = (bf16[3,128,1024]{2,1,0:T(8,128)(2,1)}, bf16[3,128,1024]{2,1,0:T(8,128)(2,1)}) conditional(s32[]{:T(128)} %bitcast, () %tuple.23, (s32[3]{0:T(128)S(1)}, bf16[4,256,1024]{2,1,0:T(8,128)(2,1)S(1)}, f32[3,8,256]{2,1,0:T(8,128)S(1)}, f32[2,4,256]{2,1,0:T(4,128)S(1)}, f32[1,256]{1,0:T(1,128)S(1)}, ...), branch_computations={%region_4.4_spmd, %region_5.5_spmd} | conditional | flops 1 | bytes 3145785 | solution.py:781
  36.8 3.6 %far_grad.1 = (bf16[3,128,1024]{2,1,0:T(8,128)(2,1)}, bf16[3,128,1024]{2,1,0:T(8,128)(2,1)S(1)}) custom-call(s32[3]{0:T(128)S(1)} %get-tuple-element.51.place_ref, bf16[4,256,1024]{2,1,0:T(8,128)(2,1)S(1)} %get-tuple-element.52.pair, f32[3,8,256]{2,1,0:T(8,128)S(1)} %get-tuple-element.53.local, f32[2,4,256]{2,1,0:T(4,128)S(1)} %get-tuple-element.54.final, ...), custom_call_target="tpu_custom_call" | custom-call | flops 1 | bytes 1 | tf_op jit(solution)/shard_map/cond/branch_1_fun/cond/branch_1_fun/far_grad/pallas_call | solution.py:667
  40.7 2.2 %collective-permute-done = bf16[3,128,1024]{2,1,0:T(8,128)(2,1)} collective-permute-done((bf16[3,128,1024]{2,1,0:T(8,128)(2,1)S(1)}, bf16[3,128,1024]{2,1,0:T(8,128)(2,1)}, u32[]{:S(2)}, u32[]{:S(2)}) %collective-permute-start) | collective-permute-done | bytes 786464 | tf_op jit(solution)/shard_map/cond/branch_1_fun/cond/branch_1_fun/ppermute | solution.py:775
  42.8 2.6 %all-to-all-done = f32[32,1,512]{2,1,0:T(1,128)S(1)} async-done(((f32[32,1,512]{2,1,0:T(1,128)}), f32[32,1,512]{2,1,0:T(1,128)S(1)}, u32[]{:S(2)}, u32[]{:S(2)}) %all-to-all-start) | async-done | bytes 65568 | tf_op jit(solution)/shard_map/cond/branch_1_fun/all_to_all | solution.py:807
  45.5 3.4 %join.1 = (f32[1,128,2048]{2,1,0:T(8,128)}, f32[1,128,2048]{2,1,0:T(8,128)}, f32[1,128,2048]{2,1,0:T(8,128)}) custom-call(s32[3]{0:T(128)S(1)} %pad_add_fusion.place_ref, bf16[3,128,1024]{2,1,0:T(8,128)(2,1)} %get-tuple-element.141.own, bf16[3,128,1024]{2,1,0:T(8,128)(2,1)} %get-tuple-element.142.sib, ...), custom_call_target="tpu_custom_call" | custom-call | flops 1 | bytes 1 | tf_op jit(solution)/shard_map/join/pallas_call | solution.py:719
  (31 shorter events, 3.5 us)
Async XLA Ops:
  0.6 7.3 %copy-start.4 = (s32[1,128]{1,0:T(1,128)S(1)}, s32[1,128]{1,0:T(1,128)}, u32[]{:S(2)}) copy-start(s32[1,128]{1,0:T(1,128)} %pos_ref.4) | copy-start | bytes 1540
  0.7 0.7 %copy-start.2 = (bf16[512]{0:T(512)(128)(2,1)S(1)}, bf16[512]{0:T(512)(128)(2,1)}, u32[]{:S(2)}) copy-start(bf16[512]{0:T(512)(128)(2,1)} %w_ref.1) | copy-start | bytes 3076
  3.4 6.6 %copy-start.3 = (bf16[1,128,4096]{2,1,0:T(8,128)(2,1)S(1)}, bf16[1,128,4096]{2,1,0:T(8,128)(2,1)}, u32[]{:S(2)}) copy-start(bf16[1,128,4096]{2,1,0:T(8,128)(2,1)} %x_ref.1) | copy-start | bytes 3145732
  3.4 17.1 %collective-permute-start.7 = (bf16[2,128,512]{2,1,0:T(8,128)(2,1)S(1)}, bf16[2,128,512]{2,1,0:T(8,128)(2,1)S(1)}, u32[]{:S(2)}, u32[]{:S(2)}) collective-permute-start(bf16[2,128,512]{2,1,0:T(8,128)(2,1)S(1)} %get-tuple-element.125), channel_id=1, source_target_pairs={{0,3},{1,2},{2,1},{3,0},{4,7},{5,6},{6,5},{7,4},{8,11},{9,10},{10,... | collective-permute-start | bytes 786440 | tf_op jit(solution)/shard_map/ppermute | solution.py:775
  5.8 14.7 %collective-permute-start.6 = (bf16[2,128,512]{2,1,0:T(8,128)(2,1)S(1)}, bf16[2,128,512]{2,1,0:T(8,128)(2,1)S(1)}, u32[]{:S(2)}, u32[]{:S(2)}) collective-permute-start(bf16[2,128,512]{2,1,0:T(8,128)(2,1)S(1)} %get-tuple-element.115), channel_id=1, source_target_pairs={{0,2},{1,3},{2,0},{3,1},{4,6},{5,7},{6,4},{7,5},{8,10},{9,11},{10,... | collective-permute-start | bytes 786440 | tf_op jit(solution)/shard_map/ppermute | solution.py:775
  6.4 3.6 %collective-permute-start.4 = (f32[1,512]{1,0:T(1,128)S(1)}, f32[1,512]{1,0:T(1,128)S(1)}, u32[]{:S(2)}, u32[]{:S(2)}) collective-permute-start(f32[1,512]{1,0:T(1,128)S(1)} %get-tuple-element.117), channel_id=1, source_target_pairs={{0,4},{4,0},{8,12},{12,8},{16,20},{20,16},{24,28},{28,24},{1,5},{5... | collective-permute-start | bytes 6152 | tf_op jit(solution)/shard_map/ppermute | solution.py:787
  10.0 4.2 %collective-permute-start.1 = (bf16[4,128,1024]{2,1,0:T(8,128)(2,1)S(1)}, bf16[4,128,1024]{2,1,0:T(8,128)(2,1)}, u32[]{:S(2)}, u32[]{:S(2)}) collective-permute-start(bf16[4,128,1024]{2,1,0:T(8,128)(2,1)S(1)} %get-tuple-element.48), channel_id=1, source_target_pairs={{0,1},{1,0},{2,3},{3,2},{4,5},{5,4},{6,7},{7,6},{8,9},{9,8},{10,11... | collective-permute-start | bytes 3145736 | tf_op jit(solution)/shard_map/cond/branch_1_fun/ppermute | solution.py:775
  10.1 4.3 %collective-permute-start.2 = (bf16[1,128,4096]{2,1,0:T(8,128)(2,1)S(1)}, bf16[1,128,4096]{2,1,0:T(8,128)(2,1)}, u32[]{:S(2)}, u32[]{:S(2)}) collective-permute-start(bf16[1,128,4096]{2,1,0:T(8,128)(2,1)S(1)} %get-tuple-element.49), channel_id=1, source_target_pairs={{0,1},{1,0},{2,3},{3,2},{4,5},{5,4},{6,7},{7,6},{8,9},{9,8},{10,11... | collective-permute-start | bytes 3145736 | tf_op jit(solution)/shard_map/cond/branch_1_fun/ppermute | solution.py:775
  10.6 3.6 %collective-permute-start.3 = (f32[1,1024]{1,0:T(1,128)S(1)}, f32[1,1024]{1,0:T(1,128)S(1)}, u32[]{:S(2)}, u32[]{:S(2)}) collective-permute-start(f32[1,1024]{1,0:T(1,128)S(1)} %get-tuple-element.50), channel_id=1, source_target_pairs={{0,8},{4,12},{8,0},{12,4},{16,24},{20,28},{24,16},{28,20},{1,9},{5... | collective-permute-start | bytes 12296 | tf_op jit(solution)/shard_map/cond/branch_1_fun/ppermute | solution.py:787
  14.4 7.5 %collective-permute-start.5 = (f32[1,2048]{1,0:T(1,128)S(1)}, f32[1,2048]{1,0:T(1,128)S(1)}, u32[]{:S(2)}, u32[]{:S(2)}) collective-permute-start(f32[1,2048]{1,0:T(1,128)S(1)} %get-tuple-element.123), channel_id=1, source_target_pairs={{0,16},{4,20},{8,24},{12,28},{16,0},{20,4},{24,8},{28,12},{1,17},{... | collective-permute-start | bytes 24584 | tf_op jit(solution)/shard_map/ppermute | solution.py:787
  23.1 4.4 %collective-permute-start.8 = (f32[4,4,256]{2,1,0:T(4,128)S(1)}, f32[4,4,256]{2,1,0:T(4,128)S(1)}, u32[]{:S(2)}, u32[]{:S(2)}) collective-permute-start(f32[4,4,256]{2,1,0:T(4,128)S(1)} %get-tuple-element.132), channel_id=1, source_target_pairs={{0,2},{1,3},{2,0},{3,1},{4,6},{5,7},{6,4},{7,5},{8,10},{9,11},{10,... | collective-permute-start | bytes 49160 | tf_op jit(solution)/shard_map/ppermute | solution.py:775
  26.8 0.7 %copy-start = (bf16[2,128,512]{2,1,0:T(8,128)(2,1)}, bf16[2,128,512]{2,1,0:T(8,128)(2,1)S(1)}, u32[]{:S(2)}) copy-start(bf16[2,128,512]{2,1,0:T(8,128)(2,1)S(1)} %get-tuple-element.140) | copy-start | bytes 786436
  29.4 0.7 %copy-start.1 = (bf16[256,512]{1,0:T(8,128)(2,1)}, bf16[256,512]{1,0:T(8,128)(2,1)S(1)}, u32[]{:S(2)}) copy-start(bf16[256,512]{1,0:T(8,128)(2,1)S(1)} %get-tuple-element.138) | copy-start | bytes 786436
  30.1 15.4 %collective-permute-start.9 = (bf16[2,128,512]{2,1,0:T(8,128)(2,1)}, bf16[2,128,512]{2,1,0:T(8,128)(2,1)S(1)}, u32[]{:S(2)}, u32[]{:S(2)}) collective-permute-start(bf16[2,128,512]{2,1,0:T(8,128)(2,1)} %get-tuple-element.143), channel_id=1, source_target_pairs={{0,2},{1,3},{2,0},{3,1},{4,6},{5,7},{6,4},{7,5},{8,10},{9,11},{10,... | collective-permute-start | bytes 786440 | tf_op jit(solution)/shard_map/ppermute | solution.py:775
  31.0 14.6 %collective-permute-start.10 = (bf16[2,128,512]{2,1,0:T(8,128)(2,1)}, bf16[2,128,512]{2,1,0:T(8,128)(2,1)S(1)}, u32[]{:S(2)}, u32[]{:S(2)}) collective-permute-start(bf16[2,128,512]{2,1,0:T(8,128)(2,1)} %get-tuple-element.144), channel_id=1, source_target_pairs={{0,3},{1,2},{2,1},{3,0},{4,7},{5,6},{6,5},{7,4},{8,11},{9,10},{10,... | collective-permute-start | bytes 786440 | tf_op jit(solution)/shard_map/ppermute | solution.py:775
  32.1 13.3 %all-to-all-start = ((f32[32,1,512]{2,1,0:T(1,128)}), f32[32,1,512]{2,1,0:T(1,128)S(1)}, u32[]{:S(2)}, u32[]{:S(2)}) async-start(f32[32,1,512]{2,1,0:T(1,128)} %bitcast.1), calls=%async_computation | async-start | bytes 131072 | tf_op jit(solution)/shard_map/cond/branch_1_fun/all_to_all | solution.py:807
  40.4 2.4 %collective-permute-start = (bf16[3,128,1024]{2,1,0:T(8,128)(2,1)S(1)}, bf16[3,128,1024]{2,1,0:T(8,128)(2,1)}, u32[]{:S(2)}, u32[]{:S(2)}) collective-permute-start(bf16[3,128,1024]{2,1,0:T(8,128)(2,1)S(1)} %get-tuple-element.61), channel_id=1, source_target_pairs={{0,1},{1,0},{2,3},{3,2},{4,5},{5,4},{6,7},{7,6},{8,9},{9,8},{10,11... | collective-permute-start | bytes 2359304 | tf_op jit(solution)/shard_map/cond/branch_1_fun/cond/branch_1_fun/ppermute | solution.py:775
  45.5 3.4 %copy-start.5 = (f32[512]{0:T(512)}, f32[512]{0:T(512)S(1)}, u32[]{:S(2)}) copy-start(f32[512]{0:T(512)S(1)} %get-tuple-element.114) | copy-start | bytes 6148

commit v9 on v8

--- a/solution.py
+++ b/solution.py
@@ -248,6 +248,11 @@
     )(targets, gate, own, sib, x_routed)
 
 
+def here():
+    me = lax.axis_index("ctx")
+    return lax.rem(me, 2), lax.div(me, 2)
+
+
 MARK = 2.0**60
 MARK_LIMIT = 2.0**50
 
@@ -263,11 +268,13 @@
     return jnp.where(mask, keys.astype(F32), MARK).astype(BF16)
 
 
-def cross_pack_kernel(place_ref, pos_ref, w_ref, k_ref, v_ref, q_ref, dg_ref, straight, diag, w_out, wide, sems):
-    w_out[...] = w_ref[...].astype(F32).reshape(w_out.shape)
+def cross_pack_kernel(pos_any, w_any, k_ref, v_ref, q_ref, dg_ref, straight, diag, w_out, wide, pos_ref, w_ref, sems):
+    small = [pltpu.make_async_copy(pos_any, pos_ref, sems.at[4]), pltpu.make_async_copy(w_any, w_ref, sems.at[5])]
+    for c in small:
+        c.start()
     slots, width = straight.shape[1], straight.shape[2]
     half = k_ref.shape[-1] // 2
-    core, chip = place_ref[0], place_ref[1]
+    core, chip = here()
     ends = ((straight, core * half), (diag, (1 - core) * half))
 
     def copies(first, second, targets, offset):
@@ -284,6 +291,7 @@
     @pl.when(chip == 0)
     def _():
         copies(k_ref, v_ref, (straight.at[1], diag.at[1]), 0)
+        small[0].wait()
         live = live_rows(pos_ref, slots)
         for end, _ in ends:
             end[0] = mark_dead(end[0], live)
@@ -291,29 +299,38 @@
     @pl.when(chip != 0)
     def _():
         copies(q_ref, dg_ref, (wide.at[0], wide.at[1]), width)
+        small[0].wait()
         for i, (end, _) in enumerate(ends):
             end[1] = wide[i].astype(BF16)
 
-
-def cross_pack(place, route_pos, w_router, keys, values, queries, d_gated):
+    small[1].wait()
+    w_out[...] = w_ref[...].astype(F32).reshape(w_out.shape)
+
+
+def cross_pack(route_pos, w_router, keys, values, queries, d_gated):
     _, slots, full = keys.shape
     cross = pltpu.VMEM((2, slots, full // 4), BF16)
     hbm = pl.BlockSpec(memory_space=pltpu.HBM)
     return pl.pallas_call(
         cross_pack_kernel,
         out_shape=[cross, cross, jax.ShapeDtypeStruct((1, w_router.shape[0]), F32)],
-        in_specs=[SMEM, VMEM, VMEM, hbm, hbm, hbm, hbm],
+        in_specs=[hbm] * 6,
         out_specs=[VMEM] * 3,
-        scratch_shapes=[pltpu.VMEM((2, slots, full // 4), F32), pltpu.SemaphoreType.DMA((4,))],
+        scratch_shapes=[
+            pltpu.VMEM((2, slots, full // 4), F32),
+            pltpu.VMEM(route_pos.shape, jnp.int32),
+            pltpu.VMEM(w_router.shape, BF16),
+            pltpu.SemaphoreType.DMA((6,)),
+        ],
         compiler_params=params(),
         cost_estimate=cost(0, 10 * slots * full),
         name="cross_pack",
-    )(place, route_pos, w_router, *in_hbm(keys, values, queries, d_gated))
-
-
-def sib_pack_kernel(place_ref, pos_ref, k_ref, v_ref, q_ref, dg_ref, out, wide, sems):
+    )(*in_hbm(route_pos, w_router, keys, values, queries, d_gated))
+
+
+def sib_pack_kernel(pos_ref, k_ref, v_ref, q_ref, dg_ref, out, wide, sems):
     slots, half = out.shape[1], out.shape[2]
-    cols = pl.ds(pl.multiple_of((1 - place_ref[0]) * half, HEAD), half)
+    cols = pl.ds(pl.multiple_of((1 - here()[0]) * half, HEAD), half)
     sources = ((k_ref, out.at[0]), (dg_ref, wide), (v_ref, out.at[1]), (q_ref, out.at[2]))
     copies = [pltpu.make_async_copy(src.at[0, :, cols], dst, sems.at[i]) for i, (src, dst) in enumerate(sources)]
     for c in copies:
@@ -327,50 +344,50 @@
     copies[3].wait()
 
 
-def sib_pack(place, route_pos, keys, values, queries, d_gated):
+def sib_pack(route_pos, keys, values, queries, d_gated):
     _, slots, full = keys.shape
     hbm = pl.BlockSpec(memory_space=pltpu.HBM)
     return pl.pallas_call(
         sib_pack_kernel,
         out_shape=pltpu.VMEM((4, slots, full // 2), BF16),
-        in_specs=[SMEM, VMEM, hbm, hbm, hbm, hbm],
+        in_specs=[VMEM, hbm, hbm, hbm, hbm],
         out_specs=VMEM,
         scratch_shapes=[pltpu.VMEM((slots, full // 2), F32), pltpu.SemaphoreType.DMA((4,))],
         compiler_params=params(),
         cost_estimate=cost(0, 20 * slots * full),
         name="sib_pack",
-    )(place, route_pos, *in_hbm(keys, values, queries, d_gated))
-
-
-def pair_gate_kernel(parts, place_ref, live_ref, rows_x, w_ref, local, stats, out_ref, message):
+    )(route_pos, *in_hbm(keys, values, queries, d_gated))
+
+
+def pair_gate_kernel(parts, live_ref, rows_x, w_ref, local, stats, out_ref, message):
     chunk = w_ref.shape[1] // parts
     slots = rows_x.shape[1]
     for i in range(2):
         total = jnp.zeros((8, slots), F32)
         for j in range(parts):
             w_rows = jnp.broadcast_to(w_ref[:, j * chunk : (j + 1) * chunk], (8, chunk)).astype(BF16)
-            cols = pl.ds(pl.multiple_of((place_ref[2] ^ j) * chunk, HEAD), chunk)
+            cols = pl.ds(pl.multiple_of((lax.axis_index("dp") ^ j) * chunk, HEAD), chunk)
             total = total + nt(w_rows, rows_x[i, :, cols])
         lanes = slice(i * slots, (i + 1) * slots)
         out_ref[:, lanes] = live_ref[:, lanes] / (1.0 + jnp.exp(-total[0:1]))
-    first = place_ref[1] == 0
+    first = here()[1] == 0
     heads = stats.shape[1]
     for i in range(3):
         message[i] = jnp.where(first, stats[i], local[i, heads:])
     message[3] = jnp.broadcast_to(out_ref[...], message.shape[1:])
 
 
-def pair_gate(place, live, rows_x, w_full, local, stats, parts):
+def pair_gate(live, rows_x, w_full, local, stats, parts):
     _, heads, lanes = stats.shape
     return pl.pallas_call(
         functools.partial(pair_gate_kernel, parts),
         out_shape=[jax.ShapeDtypeStruct(live.shape, F32), jax.ShapeDtypeStruct((4, heads, lanes), F32)],
-        in_specs=[SMEM] + [VMEM] * 5,
+        in_specs=[VMEM] * 5,
         out_specs=[VMEM] * 2,
         compiler_params=params(),
         cost_estimate=cost(16 * rows_x.size, rows_x.size * 2),
         name="router_gate",
-    )(place, live, rows_x, w_full, local, stats)
+    )(live, rows_x, w_full, local, stats)
 
 
 def local_mask(core, pair):
@@ -405,22 +422,22 @@
     stats[2, h : h + 1] = jnp.sum(e * gw, axis=0, keepdims=True)
 
 
-def local_stats_kernel(scale, place_ref, pos_ref, k_ref, v_ref, q_ref, dg_ref, sib, x_ref, x_sib, stats, live, pair, rows_x, wide, sems, x_sems):
+def local_stats_kernel(scale, pos_ref, k_ref, v_ref, q_ref, dg_ref, sib, x_ref, x_sib, stats, live, near, far, rows_x, wide, sems, x_sems):
     slots, half = sib.shape[1], sib.shape[2]
     width = half // 2
-    core = place_ref[0]
+    core = here()[0]
     own, other = slice(0, slots), slice(slots, 2 * slots)
     stages = []
-    for g in range(2):
+    for g, pair in enumerate((near, far)):
         cols = slice(g * width, (g + 1) * width)
         held = pl.ds(pl.multiple_of(core * half + g * width, HEAD), width)
         copies = [
-            pltpu.make_async_copy(ref.at[0, :, held], pair.at[j, own, cols], sems.at[8 * g + j])
+            pltpu.make_async_copy(ref.at[0, :, held], pair.at[j, own], sems.at[8 * g + j])
             for j, ref in enumerate((k_ref, v_ref, q_ref))
         ]
         copies.append(pltpu.make_async_copy(dg_ref.at[0, :, held], wide.at[:, cols], sems.at[8 * g + 3]))
         for j in range(4):
-            copies.append(pltpu.make_async_copy(sib.at[j, :, cols], pair.at[j, other, cols], sems.at[8 * g + 4 + j]))
+            copies.append(pltpu.make_async_copy(sib.at[j, :, cols], pair.at[j, other], sems.at[8 * g + 4 + j]))
         for c in copies:
             c.start()
         stages.append(copies)
@@ -434,25 +451,25 @@
         c.start()
     rows_live = live_rows(pos_ref, slots)
     mask = None
-    for g in range(2):
+    for g, pair in enumerate((near, far)):
         cols = slice(g * width, (g + 1) * width)
         for c in stages[g]:
             c.wait()
-        pair[0, own, cols] = mark_dead(pair[0, own, cols], rows_live)
-        pair[3, own, cols] = wide[:, cols].astype(BF16)
+        pair[0, own] = mark_dead(pair[0, own], rows_live)
+        pair[3, own] = wide[:, cols].astype(BF16)
         if mask is None:
             mask = local_mask(core, pair)
             marks = nt(jnp.ones((8, HEAD), BF16), pair[0, :, :HEAD])[0:1]
             live[...] = jnp.where(marks < MARK_LIMIT, 1.0, 0.0)
-        for h in range(g * width // HEAD, (g + 1) * width // HEAD):
+        for h in range(width // HEAD):
             at = slice(h * HEAD, (h + 1) * HEAD)
             scores = jnp.where(mask, nt(pair[0, :, at], pair[2, :, at]) * scale, NEG_FILL)
-            partial_stats(scores, nt(pair[1, :, at], pair[3, :, at]), stats, h)
+            partial_stats(scores, nt(pair[1, :, at], pair[3, :, at]), stats, g * width // HEAD + h)
     for c in x_copies:
         c.wait()
 
 
-def local_stats(place, route_pos, keys, values, queries, d_gated, sib, x_routed, x_sib):
+def local_stats(route_pos, keys, values, queries, d_gated, sib, x_routed, x_sib):
     _, slots, half = sib.shape
     heads = half // HEAD
     anywhere = pl.BlockSpec(memory_space=pl.ANY)
@@ -461,38 +478,37 @@
         out_shape=[
             jax.ShapeDtypeStruct((3, heads, 2 * slots), F32),
             jax.ShapeDtypeStruct((1, 2 * slots), F32),
-            pltpu.VMEM((4, 2 * slots, half), BF16),
+            pltpu.VMEM((4, 2 * slots, half // 2), BF16),
+            pltpu.VMEM((4, 2 * slots, half // 2), BF16),
             pltpu.VMEM((2, slots, x_routed.shape[2]), BF16),
         ],
-        in_specs=[SMEM, VMEM] + [anywhere] * 7,
-        out_specs=[VMEM] * 4,
+        in_specs=[VMEM] + [anywhere] * 7,
+        out_specs=[VMEM] * 5,
         scratch_shapes=[pltpu.VMEM((slots, half), F32), pltpu.SemaphoreType.DMA((16,)), pltpu.SemaphoreType.DMA((4,))],
         compiler_params=params(),
         cost_estimate=cost(16 * slots * slots * half, 16 * slots * half, 4 * slots * slots * half // HEAD),
         name="local_stats",
-    )(place, route_pos, *in_hbm(keys, values, queries, d_gated), sib, x_routed, x_sib)
-
-
-def cross_stats_kernel(scale, place_ref, pair, straight, diag, cross, stats, kept):
+    )(route_pos, *in_hbm(keys, values, queries, d_gated), sib, x_routed, x_sib)
+
+
+def cross_stats_kernel(scale, near, far, straight, diag, cross, stats, kept):
     slots, width = straight.shape[1], straight.shape[2]
-    chip = place_ref[1]
+    chip = here()[1]
     top, bottom = slice(0, slots), slice(slots, 2 * slots)
 
     @pl.when(chip == 0)
     def _():
-        cols = slice(width, 2 * width)
         for part in range(2):
-            cross[part] = pair[part, :, cols]
+            cross[part] = far[part]
             cross[2 + part, top] = straight[part]
             cross[2 + part, bottom] = diag[part]
 
     @pl.when(chip != 0)
     def _():
-        cols = slice(0, width)
         for part in range(2):
             cross[part, top] = straight[part]
             cross[part, bottom] = diag[part]
-            cross[2 + part] = pair[2 + part, :, cols]
+            cross[2 + part] = near[2 + part]
 
     live = cross[0, :, :HEAD].astype(F32) < MARK_LIMIT
     mask = jnp.concatenate([live] * (2 * slots // HEAD), axis=1)
@@ -503,7 +519,7 @@
         kept_stats(scores, nt(cross[1, :, cols], cross[3, :, cols]), kept, stats, h)
 
 
-def cross_stats(place, pair, straight, diag):
+def cross_stats(near, far, straight, diag):
     _, slots, width = straight.shape
     heads = width // HEAD
     return pl.pallas_call(
@@ -513,12 +529,12 @@
             jax.ShapeDtypeStruct((3, heads, 2 * slots), F32),
             pltpu.VMEM((2, heads, 2 * slots, 2 * slots), BF16),
         ],
-        in_specs=[SMEM] + [VMEM] * 3,
+        in_specs=[VMEM] * 4,
         out_specs=[VMEM] * 3,
         compiler_params=params(),
         cost_estimate=cost(16 * slots * slots * width, 32 * slots * width, 4 * slots * slots * heads),
         name="cross_stats",
-    )(place, pair, straight, diag)
+    )(near, far, straight, diag)
 
 
 NONE = (-3e38, 0.0, 0.0)
@@ -548,15 +564,15 @@
     return gradients(q, k, dg, e, nt(v, dg), scale, factor, delta)
 
 
-def near_grad_kernel(scale, place_ref, pair, local, stats, gates, dq_out, own_out, sib_out, sum_out):
+def near_grad_kernel(scale, pair, local, stats, gates, dq_out, own_out, sib_out, sum_out):
     slots, width = own_out.shape[1], own_out.shape[2]
     heads = width // HEAD
-    first = place_ref[1] == 0
+    first = here()[1] == 0
     near = [local[i, :heads] for i in range(3)]
     factor, delta = merge(near, choose(first, NONE, [stats[i] for i in range(3)]))
     factor = factor * gates[...]
     sum_out[...] = jnp.sum(delta, axis=0, keepdims=True)
-    mask = local_mask(place_ref[0], pair)
+    mask = local_mask(here()[0], pair)
     for h in range(heads):
         cols = slice(h * HEAD, (h + 1) * HEAD)
         row = slice(h, h + 1)
@@ -567,26 +583,25 @@
             sib_out[i, :, cols] = part[slots:].astype(BF16)
 
 
-def near_grad(place, pair, local, stats, gates):
-    _, rows, half = pair.shape
+def near_grad(pair, local, stats, gates):
+    _, rows, width = pair.shape
     slots = rows // 2
-    width = half // 2
     out = pltpu.VMEM((2, slots, width), BF16)
     return pl.pallas_call(
         functools.partial(near_grad_kernel, HEAD**-0.5),
         out_shape=[pltpu.VMEM((2 * slots, width), F32), out, out, jax.ShapeDtypeStruct(gates.shape, F32)],
-        in_specs=[SMEM] + [VMEM] * 4,
+        in_specs=[VMEM] * 4,
         out_specs=[VMEM] * 4,
         compiler_params=params(),
-        cost_estimate=cost(20 * slots * slots * half, 40 * slots * half),
+        cost_estimate=cost(20 * slots * slots * width, 40 * slots * width),
         name="near_grad",
-    )(place, pair, local, stats, gates)
-
-
-def cross_grad_kernel(scale, place_ref, cross, kept, stats, local, heard, gates, near_dq, near_sum, straight, diag, dq_out, keep, final, sum_out):
+    )(pair, local, stats, gates)
+
+
+def cross_grad_kernel(scale, cross, kept, stats, local, heard, gates, near_dq, near_sum, straight, diag, dq_out, keep, final, sum_out):
     slots, width = straight.shape[1], straight.shape[2]
     heads = width // HEAD
-    first = place_ref[1] == 0
+    first = here()[1] == 0
     late = jnp.where(first, 0.0, 1.0)
     mine = [stats[i] for i in range(3)]
     other = [heard[i] for i in range(3)]
@@ -613,7 +628,7 @@
         diag[1, :, cols] = dv[slots:].astype(BF16)
 
 
-def cross_grad(place, cross, kept, stats, local, heard, gates, near_dq, near_sum):
+def cross_grad(cross, kept, stats, local, heard, gates, near_dq, near_sum):
     _, rows, width = cross.shape
     slots = rows // 2
     out = pltpu.VMEM((2, slots, width), BF16)
@@ -627,21 +642,20 @@
             jax.ShapeDtypeStruct((2, width // HEAD, rows), F32),
             jax.ShapeDtypeStruct((1, rows), F32),
         ],
-        in_specs=[SMEM] + [VMEM] * 8,
+        in_specs=[VMEM] * 8,
         out_specs=[VMEM] * 6,
         compiler_params=params(),
         cost_estimate=cost(24 * slots * slots * width, 64 * slots * width),
         name="cross_grad",
-    )(place, cross, kept, stats, local, heard, gates, near_dq, near_sum)
-
-
-def far_grad_kernel(scale, place_ref, pair, local, final, gates, keep, near_dq, near_own, near_sib, own_out, sib_out):
-    slots, half = pair.shape[1] // 2, pair.shape[2]
-    width = half // 2
+    )(cross, kept, stats, local, heard, gates, near_dq, near_sum)
+
+
+def far_grad_kernel(scale, pair, local, final, gates, keep, near_dq, near_own, near_sib, own_out, sib_out):
+    slots, width = pair.shape[1] // 2, pair.shape[2]
     heads = width // HEAD
-    early = jnp.where(place_ref[1] == 0, 1.0, 0.0)
+    early = jnp.where(here()[1] == 0, 1.0, 0.0)
     factor = final[0] * gates[...]
-    mask = local_mask(place_ref[0], pair)
+    mask = local_mask(here()[0], pair)
     own_out[0, :, :width] = near_dq[:slots]
     sib_out[0, :, :width] = near_dq[slots:]
     for i in range(2):
@@ -652,7 +666,7 @@
         at = slice(h * HEAD, (h + 1) * HEAD)
         row = slice(h, h + 1)
         top = local[0, heads + h : heads + h + 1]
-        dq, dk, dv = local_gradients(pair, heads + h, mask, scale, top, factor[row], final[1, row])
+        dq, dk, dv = local_gradients(pair, h, mask, scale, top, factor[row], final[1, row])
         dk = dk + early * keep[0, :, at].astype(F32)
         dv = dv + early * keep[1, :, at].astype(F32)
         for i, part in enumerate((dq, dk, dv)):
@@ -660,78 +674,109 @@
             sib_out[i, :, cols] = part[slots:].astype(BF16)
 
 
-def far_grad(place, pair, local, final, gates, keep, near_dq, near_own, near_sib):
-    _, rows, half = pair.shape
-    slots = rows // 2
+def far_grad(pair, local, final, gates, keep, near_dq, near_own, near_sib):
+    _, rows, width = pair.shape
+    slots, half = rows // 2, 2 * width
     out = jax.ShapeDtypeStruct((3, slots, half), BF16)
     return pl.pallas_call(
         functools.partial(far_grad_kernel, HEAD**-0.5),
         out_shape=[out, out],
-        in_specs=[SMEM] + [VMEM] * 8,
+        in_specs=[VMEM] * 8,
         out_specs=[VMEM] * 2,
         compiler_params=params(),
         cost_estimate=cost(20 * slots * slots * half, 40 * slots * half),
         name="far_grad",
-    )(place, pair, local, final, gates, keep, near_dq, near_own, near_sib)
-
-
-def join_kernel(place_ref, own, sib, straight, diag, dq_out, dk_out, dv_out, low, back, total, in_sems, out_sems):
+    )(pair, local, final, gates, keep, near_dq, near_own, near_sib)
+
+
+def join_kernel(own, sib, dq_out, dk_out, dv_out, waiting, low, total, in_sems, out_sems):
     slots, half = own.shape[1], own.shape[2]
-    width = straight.shape[2]
-    core, chip = place_ref[0], place_ref[1]
-    early, late = jnp.where(chip == 0, 1.0, 0.0), jnp.where(chip == 0, 0.0, 1.0)
-    ends = ((own, straight, core * half), (sib, diag, (1 - core) * half))
-    loads = []
-    for i, (part, extra, _) in enumerate(ends):
-        extras = [pltpu.make_async_copy(extra.at[j], back.at[i, j], in_sems.at[5 * i + j]) for j in range(2)]
-        parts = [pltpu.make_async_copy(part.at[j], low.at[i, j], in_sems.at[5 * i + 2 + j]) for j in range(3)]
-        loads.append((parts, extras))
-    for parts, extras in loads:
-        for c in (parts[0], extras[0], parts[1], extras[1], parts[2]):
-            c.start()
+    width = half // 2
+    core, chip = here()
+    ends = ((own, core * half), (sib, (1 - core) * half))
+    loads = [
+        [pltpu.make_async_copy(part.at[j], low.at[i, j], in_sems.at[3 * i + j]) for j in range(3)]
+        for i, (part, _) in enumerate(ends)
+    ]
+    for c in loads[0] + loads[1]:
+        c.start()
     stores = []
-    for i, (_, _, start) in enumerate(ends):
-        parts, extras = loads[i]
+    for i, (_, start) in enumerate(ends):
+        cols = pl.ds(pl.multiple_of(start, HEAD), half)
         for j, out in enumerate((dq_out, dk_out, dv_out)):
-            parts[j].wait()
-            if j < 2:
-                extras[j].wait()
-            at = total.at[i, j]
-            first, second = low[i, j, :, :width].astype(F32), low[i, j, :, width:].astype(F32)
-            if j == 0:
-                at[:, :width] = first
-                at[:, width:] = second + late * back[i, 0].astype(F32)
-            else:
-                at[:, :width] = first + early * back[i, j - 1].astype(F32)
-                at[:, width:] = second
-            cols = pl.ds(pl.multiple_of(start, HEAD), half)
-            stores.append(pltpu.make_async_copy(at, out.at[0, :, cols], out_sems.at[3 * i + j]))
+            loads[i][j].wait()
+            total[i, j] = low[i, j].astype(F32)
+            stores.append(pltpu.make_async_copy(total.at[i, j], out.at[0, :, cols], out_sems.at[3 * i + j]))
             stores[-1].start()
+        waiting[i, 0] = jnp.where(chip == 0, total[i, 1, :, :width], total[i, 0, :, width:])
+        waiting[i, 1] = total[i, 2, :, :width]
     for c in stores:
         c.wait()
 
 
-def join(place, own, sib, straight, diag, shape):
+def join(own, sib, shape):
     out = jax.ShapeDtypeStruct(shape, F32)
     _, slots, half = own.shape
     anywhere = pl.BlockSpec(memory_space=pl.ANY)
     hbm = pl.BlockSpec(memory_space=pltpu.HBM)
     return pl.pallas_call(
         join_kernel,
-        out_shape=[out] * 3,
-        in_specs=[SMEM] + [anywhere] * 4,
-        out_specs=[hbm] * 3,
+        out_shape=[out] * 3 + [pltpu.VMEM((2, 2, slots, half // 2), F32)],
+        in_specs=[anywhere] * 2,
+        out_specs=[hbm] * 3 + [VMEM],
         scratch_shapes=[
             pltpu.VMEM((2, 3, slots, half), BF16),
-            pltpu.VMEM((2, 2, slots, half // 2), BF16),
             pltpu.VMEM((2, 3, slots, half), F32),
-            pltpu.SemaphoreType.DMA((10,)),
+            pltpu.SemaphoreType.DMA((6,)),
             pltpu.SemaphoreType.DMA((6,)),
         ],
         compiler_params=params(),
         cost_estimate=cost(0, 18 * out.size),
         name="join",
-    )(place, own, sib, straight, diag)
+    )(own, sib)
+
+
+def add_back_kernel(waiting, straight, diag, dq_in, dk_in, dv_in, dq_out, dk_out, dv_out, total, sems):
+    width = straight.shape[2]
+    core, chip = here()
+    ends = ((straight, 2 * core * width), (diag, 2 * (1 - core) * width))
+
+    def store(i, j, out, offset):
+        cols = pl.ds(pl.multiple_of(ends[i][1] + offset, HEAD), width)
+        copy = pltpu.make_async_copy(total.at[i, j], out.at[0, :, cols], sems.at[2 * i + j])
+        copy.start()
+        return copy
+
+    for i, (back, _) in enumerate(ends):
+        for j in range(2):
+            total[i, j] = waiting[i, j] + back[j].astype(F32)
+
+    @pl.when(chip == 0)
+    def _():
+        copies = [store(i, j, out, 0) for i in range(2) for j, out in enumerate((dk_out, dv_out))]
+        for c in copies:
+            c.wait()
+
+    @pl.when(chip != 0)
+    def _():
+        copies = [store(i, 0, dq_out, width) for i in range(2)]
+        for c in copies:
+            c.wait()
+
+
+def add_back(waiting, straight, diag, outs):
+    hbm = pl.BlockSpec(memory_space=pltpu.HBM)
+    return pl.pallas_call(
+        add_back_kernel,
+        out_shape=[jax.ShapeDtypeStruct(o.shape, F32) for o in outs],
+        in_specs=[VMEM] * 3 + [hbm] * 3,
+        out_specs=[hbm] * 3,
+        scratch_shapes=[pltpu.VMEM(waiting.shape, F32), pltpu.SemaphoreType.DMA((4,))],
+        input_output_aliases={3: 0, 4: 1, 5: 2},
+        compiler_params=params(),
+        cost_estimate=cost(0, 12 * waiting.size),
+        name="add_back",
+    )(waiting, straight, diag, *outs)
 
 
 def pair_router_kernel(gates_ref, sum_ref, rows_x, out_ref):
@@ -768,8 +813,6 @@
 def swap_body(route_pos, x_routed, w_router, queries, keys, values, d_gated):
     slots = queries.shape[1]
     n, ndp = lax.axis_size("ctx"), lax.axis_size("dp")
-    me = lax.axis_index("ctx")
-    place = jnp.stack([me % 2, me // 2, lax.axis_index("dp")]).astype(jnp.int32)
 
     def send(a, flip):
         return lax.ppermute(a, "ctx", [(i, i ^ flip) for i in range(n)])
@@ -783,11 +826,9 @@
     def after(value, *others):
         return lax.optimization_barrier((value, *others))[0]
 
-    def near_dp(part, step):
-        return lax.ppermute(part, "dp", [(i, i ^ step) for i in range(ndp)])
-
     def widen(part, step, *first):
-        return jnp.concatenate([part, after(near_dp(part, step), *first)], axis=1)
+        other = lax.ppermute(part, "dp", [(i, i ^ step) for i in range(ndp)])
+        return jnp.concatenate([part, after(other, *first)], axis=1)
 
     def exchange_phase(x_routed, w_part, theirs):
         sib, x_sib = send(theirs, 1), send(x_routed, 1)
@@ -797,38 +838,41 @@
             step *= 2
         return sib, x_sib, w_part
 
-    def grad_phase(*operands):
+    def far_phase(*operands):
         own_out, sib_out = far_grad(*operands)
         return own_out, send(sib_out, 1)
 
-    def router_phase(gates, sums, rows_x, place, *operands):
-        terms = pair_router(gates, sums, rows_x, ndp, n)
-        chunk = terms.shape[-1]
-        shared = lax.all_to_all(terms.reshape(ndp * n, 1, chunk), ("dp", "ctx"), 0, 0, tiled=True)
-        own_out, sib_in = beside(grad_phase, after(place, terms), *operands)
-        return own_out, sib_in, jnp.sum(shared, axis=0)[0] / float(ndp * n * slots // 2)
-
-    out_s, out_d, w_part = cross_pack(place, route_pos, w_router, keys, values, queries, d_gated)
+    def router_phase(terms):
+        shared = lax.all_to_all(terms.reshape(ndp * n, 1, -1), ("dp", "ctx"), 0, 0, tiled=True)
+        return jnp.sum(shared, axis=0)[0] / float(ndp * n * slots // 2)
+
+    out_s, out_d, w_part = cross_pack(route_pos, w_router, keys, values, queries, d_gated)
     in_s, in_d = send(out_s, 2), send(out_d, 3)
-    theirs = sib_pack(place, after(route_pos, out_s), keys, values, queries, d_gated)
+
+    theirs = sib_pack(after(route_pos, out_s), keys, values, queries, d_gated)
     if ndp > 1:
         w_part = widen(w_part, 1, theirs)
     sib, x_sib, w_part = beside(exchange_phase, x_routed, w_part, theirs)
-    local, live, pair, rows_x = local_stats(place, route_pos, keys, values, queries, d_gated, sib, x_routed, x_sib)
-    cross, stats, kept_cross = cross_stats(place, pair, in_s, in_d)
+    local, live, near, far, rows_x = local_stats(route_pos, keys, values, queries, d_gated, sib, x_routed, x_sib)
+    cross, stats, kept = cross_stats(near, far, in_s, in_d)
     if ndp > 2:
         w_part = widen(w_part, ndp // 2, stats)
-    gates, message = pair_gate(place, live, rows_x, w_part, local, stats, ndp)
+    gates, message = pair_gate(live, rows_x, w_part, local, stats, ndp)
+
     heard = send(message, 2)
-    near_dq, near_own, near_sib, near_sum = near_grad(place, pair, local, stats, gates)
+    near_dq, near_own, near_sib, near_sum = near_grad(near, local, stats, gates)
     back_s, back_d, dq_low, keep, final, sums = cross_grad(
-        place, cross, kept_cross, stats, local, heard, gates, near_dq, near_sum
+        cross, kept, stats, local, heard, gates, near_dq, near_sum
     )
+
     ret_s, ret_d = send(back_s, 2), send(back_d, 3)
-    own_out, sib_in, router_grad = beside(
-        router_phase, gates, sums, rows_x, place, pair, local, final, gates, keep, dq_low, near_own, near_sib
+    terms = pair_router(gates, sums, rows_x, ndp, n)
+    own_out, sib_in = beside(
+        far_phase, far, local, final, after(gates, terms), keep, dq_low, near_own, near_sib
     )
-    dq, dk, dv = join(place, own_out, sib_in, ret_s, ret_d, queries.shape)
+    *outs, waiting = join(own_out, sib_in, queries.shape)
+    router_grad = beside(router_phase, after(terms, waiting))
+    dq, dk, dv = add_back(waiting, ret_s, ret_d, outs)
     return dq, dk, dv, router_grad
 
 

time: 49.2 us -> 45.9 us (0.933)
  blocking collectives: 0 us -> 11.4 us
  Pallas kernels: 22 us -> 15 us
  starting transfers between devices: 16.6 us -> 12.5 us
  local copies, waits for them, and re-layouts: 2.12 us -> 0.02 us
  waiting for transfers between devices: 7.11 us -> 5.83 us
    all_to_all x0 -> x1, blocking collectives: none -> 11.4 us  [router_phase(): lax.all_to_all(terms.reshape(ndp * n, 1, -1), ('dp', 'ctx'), 0, 0, tiled=...]
    all_to_all x1 -> x0, starting transfers between devices: 4.65 us -> none  [router_phase(): lax.all_to_all(terms.reshape(ndp * n, 1, chunk), ('dp', 'ctx'), 0, 0, til...]
    all_to_all x1 -> x0, waiting for transfers between devices: 2.57 us -> none  [router_phase(): lax.all_to_all(terms.reshape(ndp * n, 1, chunk), ('dp', 'ctx'), 0, 0, til...]
    unnamed x12 -> x6, local copies, waits for them, and re-layouts: 2.12 us -> 0.02 us
    pallas_call x1, Pallas kernels: 3.61 us -> 1.71 us  [far_grad(): pl.pallas_call(functools.partial(far_grad_kernel, HEAD ** (-0.5)), out_sh...]
    pallas_call x1, Pallas kernels: 1.95 us -> 0.69 us  [cross_grad(): pl.pallas_call(functools.partial(cross_grad_kernel, HEAD ** (-0.5)), out_...]
    pallas_call x1, Pallas kernels: 3.51 us -> 2.71 us  [local_stats(): pl.pallas_call(functools.partial(local_stats_kernel, HEAD ** (-0.5)), out...]
    ppermute x8, waiting for transfers between devices: 2.33 us -> 3.09 us  [send(): return lax.ppermute(a, 'ctx', [(i, i ^ flip) for i in range(n)])]
  transfers between devices with their start and end apart: 12 -> 11, of which waited for: 5 -> 5; matrix products, arithmetic and copies ran while one was open for 0% -> 0% of each run, Pallas kernels for 28% -> 24%
where the time goes in v9:
time: 45.9 us; the launch traced here: 45.7 us
  Pallas kernels  15 us (33%)
  starting transfers between devices  12.5 us (27%)
  blocking collectives  11.4 us (25%)
  waiting for transfers between devices  5.83 us (13%)
  between operations  0.83 us (2%)
    all_to_all x1, blocking collectives, router_phase(): lax.all_to_all(terms.reshape(ndp * n, 1, -1), ('dp', 'ctx'), 0, 0, tiled=...  11.4 us
    ppermute x8, starting transfers between devices, send(): return lax.ppermute(a, 'ctx', [(i, i ^ flip) for i in range(n)])  6.78 us
    ppermute x3, starting transfers between devices, widen(): other = lax.ppermute(part, 'dp', [(i, i ^ step) for i in range(ndp)])  5.68 us
    ppermute x8, waiting for transfers between devices, send(): return lax.ppermute(a, 'ctx', [(i, i ^ flip) for i in range(n)])  3.09 us
    ppermute x3, waiting for transfers between devices, widen(): other = lax.ppermute(part, 'dp', [(i, i ^ step) for i in range(ndp)])  2.74 us
    pallas_call x1, Pallas kernels, local_stats(): pl.pallas_call(functools.partial(local_stats_kernel, HEAD ** (-0.5)), out...  2.71 us
    pallas_call x1, Pallas kernels, join(): pl.pallas_call(join_kernel, out_shape=[out] * 3 + [pltpu.VMEM((2, 2, slot...  2.54 us
    pallas_call x1, Pallas kernels, far_grad(): pl.pallas_call(functools.partial(far_grad_kernel, HEAD ** (-0.5)), out_sh...  1.71 us
  transfers between devices with their start and end apart: 11, of which 5 were waited for; matrix products, arithmetic and copies ran while one was open for 0% of the time, Pallas kernels for 24%

profile of v9, /device:TPU:0, one launch (start us, length us, event | category | flops | bytes accessed | tf_op | source)
XLA Modules:
  0.0 45.7 jit_solution(5648447715014109613)
XLA Ops:
  0.6 1.3 %cross_pack.1 = (bf16[2,128,512]{2,1,0:T(8,128)(2,1)S(1)}, bf16[2,128,512]{2,1,0:T(8,128)(2,1)S(1)}, f32[1,512]{1,0:T(1,128)S(1)}) custom-call(s32[1,128]{1,0:T(1,128)} %pos_ref.2, bf16[512]{0:T(512)(128)(2,1)} %w_any.1, bf16[1,128,2048]{2,1,0:T(8,128)(2,1)} %k_ref.5, bf16[1,128,2048]{2,1,0:T(8,128)(2,1)} %v_ref.5, bf16[1,128,2048]{2,1,0:T(8,128)(2,1)} %q_ref.5, ...), custom_call_target="tpu_custom_call" | custom-call | flops 1 | bytes 1 | tf_op jit(solution)/shard_map/cross_pack/pallas_call | solution.py:314
  2.0 3.0 %collective-permute-start.5 = (bf16[2,128,512]{2,1,0:T(8,128)(2,1)S(1)}, bf16[2,128,512]{2,1,0:T(8,128)(2,1)S(1)}, u32[]{:S(2)}, u32[]{:S(2)}) collective-permute-start(bf16[2,128,512]{2,1,0:T(8,128)(2,1)S(1)} %get-tuple-element.83), channel_id=1, source_target_pairs={{0,2},{1,3},{2,0},{3,1},{4,6},{5,7},{6,4},{7,5},{8,10},{9,11},{10,... | collective-permute-start | bytes 786440 | tf_op jit(solution)/shard_map/ppermute | solution.py:818
  5.0 1.5 %collective-permute-start.4 = (f32[1,512]{1,0:T(1,128)S(1)}, f32[1,512]{1,0:T(1,128)S(1)}, u32[]{:S(2)}, u32[]{:S(2)}) collective-permute-start(f32[1,512]{1,0:T(1,128)S(1)} %get-tuple-element.85), channel_id=1, source_target_pairs={{0,4},{4,0},{8,12},{12,8},{16,20},{20,16},{24,28},{28,24},{1,5},{5... | collective-permute-start | bytes 6152 | tf_op jit(solution)/shard_map/ppermute | solution.py:830
  6.5 1.3 %sib_pack.1 = bf16[4,128,1024]{2,1,0:T(8,128)(2,1)S(1)} custom-call(s32[1,128]{1,0:T(1,128)S(1)} %copy-done, bf16[1,128,2048]{2,1,0:T(8,128)(2,1)} %k_ref.5, bf16[1,128,2048]{2,1,0:T(8,128)(2,1)} %v_ref.5, bf16[1,128,2048]{2,1,0:T(8,128)(2,1)} %q_ref.5, f32[1,128,2048]{2,1,0:T(8,128)} %dg_ref.5), custom_call_target="tpu_custom_call" | custom-call | flops 1 | bytes 1 | tf_op jit(solution)/shard_map/sib_pack/pallas_call | solution.py:350
  7.8 0.7 %collective-permute-done.4 = f32[1,512]{1,0:T(1,128)S(1)} collective-permute-done((f32[1,512]{1,0:T(1,128)S(1)}, f32[1,512]{1,0:T(1,128)S(1)}, u32[]{:S(2)}, u32[]{:S(2)}) %collective-permute-start.4) | collective-permute-done | bytes 2080 | tf_op jit(solution)/shard_map/ppermute | solution.py:830
  8.6 4.4 %conditional.3 = (bf16[4,128,1024]{2,1,0:T(8,128)(2,1)}, bf16[1,128,4096]{2,1,0:T(8,128)(2,1)}, f32[1,2048]{1,0:T(1,128)S(1)}) conditional(s32[]{:T(128)} %bitcast.1, () %tuple.36, (bf16[4,128,1024]{2,1,0:T(8,128)(2,1)S(1)}, bf16[1,128,4096]{2,1,0:T(8,128)(2,1)S(1)}, f32[1,1024]{1,0:T(1,128)S(1)}) %tuple.52), branch_computations={%region_0.0_spmd, %region_1.0_spmd} | conditional | flops 2048 | bytes 8421520 | solution.py:824
  9.2 1.6 %collective-permute-start.3 = (f32[1,1024]{1,0:T(1,128)S(1)}, f32[1,1024]{1,0:T(1,128)S(1)}, u32[]{:S(2)}, u32[]{:S(2)}) collective-permute-start(f32[1,1024]{1,0:T(1,128)S(1)} %get-tuple-element.28), channel_id=1, source_target_pairs={{0,8},{4,12},{8,0},{12,4},{16,24},{20,28},{24,16},{28,20},{1,9},{5... | collective-permute-start | bytes 12296 | tf_op jit(solution)/shard_map/cond/branch_1_fun/ppermute | solution.py:830
  10.7 2.0 %collective-permute-done.3 = f32[1,1024]{1,0:T(1,128)S(1)} collective-permute-done((f32[1,1024]{1,0:T(1,128)S(1)}, f32[1,1024]{1,0:T(1,128)S(1)}, u32[]{:S(2)}, u32[]{:S(2)}) %collective-permute-start.3) | collective-permute-done | bytes 4128 | tf_op jit(solution)/shard_map/cond/branch_1_fun/ppermute | solution.py:830
  12.9 2.6 %collective-permute-start.7 = (f32[1,2048]{1,0:T(1,128)S(1)}, f32[1,2048]{1,0:T(1,128)S(1)}, u32[]{:S(2)}, u32[]{:S(2)}) collective-permute-start(f32[1,2048]{1,0:T(1,128)S(1)} %get-tuple-element.98), channel_id=1, source_target_pairs={{0,16},{4,20},{8,24},{12,28},{16,0},{20,4},{24,8},{28,12},{1,17},{... | collective-permute-start | bytes 24584 | tf_op jit(solution)/shard_map/ppermute | solution.py:830
  15.5 2.7 %local_stats.1 = (f32[3,8,256]{2,1,0:T(8,128)S(1)}, f32[1,256]{1,0:T(1,128)S(1)}, bf16[4,256,512]{2,1,0:T(8,128)(2,1)S(1)}, bf16[4,256,512]{2,1,0:T(8,128)(2,1)S(1)}, bf16[2,128,4096]{2,1,0:T(8,128)(2,1)S(1)}) custom-call(s32[1,128]{1,0:T(1,128)S(1)} %copy-done, bf16[1,128,2048]{2,1,0:T(8,128)(2,1)} %k_ref.5, bf16[1,128,2048]{2,1,0:T(8,128)(2,1)} %v_ref.5, ...), custom_call_target="tpu_custom_call" | custom-call | flops 1 | bytes 1 | tf_op jit(solution)/shard_map/local_stats/pallas_call | solution.py:476
  18.3 0.8 %cross_stats.1 = (bf16[4,256,512]{2,1,0:T(8,128)(2,1)S(1)}, f32[3,4,256]{2,1,0:T(4,128)S(1)}, bf16[2,4,256,256]{3,2,1,0:T(8,128)(2,1)S(1)}) custom-call(bf16[4,256,512]{2,1,0:T(8,128)(2,1)S(1)} %get-tuple-element.91.near.pair, bf16[4,256,512]{2,1,0:T(8,128)(2,1)S(1)} %get-tuple-element.89.far, bf16[2,128,512]{2,1,0:T(8,128)(2,1)S(1)} %collective-permute-done.5.straight, ...), custom_call_target="tpu_custom_call" | custom-call | flops 1 | bytes 1 | tf_op jit(solution)/shard_map/cross_stats/pallas_call | solution.py:525
  19.1 0.7 %router_gate.1 = (f32[1,256]{1,0:T(1,128)S(1)}, f32[4,4,256]{2,1,0:T(4,128)S(1)}) custom-call(f32[1,256]{1,0:T(1,128)S(1)} %get-tuple-element.96.live_ref, bf16[2,128,4096]{2,1,0:T(8,128)(2,1)S(1)} %get-tuple-element.97.rows_x, f32[1,4096]{1,0:T(1,128)S(1)} %pad_maximum_fusion.1.w_ref, f32[3,8,256]{2,1,0:T(8,128)S(1)} %get-tuple-element.90.local, ...), custom_call_target="tpu_custom_call" | custom-call | flops 1 | bytes 1 | tf_op jit(solution)/shard_map/router_gate/pallas_call | solution.py:382
  19.8 1.3 %collective-permute-start.8 = (f32[4,4,256]{2,1,0:T(4,128)S(1)}, f32[4,4,256]{2,1,0:T(4,128)S(1)}, u32[]{:S(2)}, u32[]{:S(2)}) collective-permute-start(f32[4,4,256]{2,1,0:T(4,128)S(1)} %get-tuple-element.100), channel_id=1, source_target_pairs={{0,2},{1,3},{2,0},{3,1},{4,6},{5,7},{6,4},{7,5},{8,10},{9,11},{10,... | collective-permute-start | bytes 49160 | tf_op jit(solution)/shard_map/ppermute | solution.py:818
  21.1 1.6 %near_grad.1 = (f32[256,512]{1,0:T(8,128)S(1)}, bf16[2,128,512]{2,1,0:T(8,128)(2,1)S(1)}, bf16[2,128,512]{2,1,0:T(8,128)(2,1)S(1)}, f32[1,256]{1,0:T(1,128)S(1)}) custom-call(bf16[4,256,512]{2,1,0:T(8,128)(2,1)S(1)} %get-tuple-element.91.near.pair, f32[3,8,256]{2,1,0:T(8,128)S(1)} %get-tuple-element.90.local, f32[3,4,256]{2,1,0:T(4,128)S(1)} %get-tuple-element.95.stats, ...), custom_call_target="tpu_custom_call" | custom-call | flops 1 | bytes 1 | tf_op jit(solution)/shard_map/near_grad/pallas_call | solution.py:590
  22.7 0.9 %collective-permute-done.8.heard = f32[4,4,256]{2,1,0:T(4,128)S(1)} collective-permute-done((f32[4,4,256]{2,1,0:T(4,128)S(1)}, f32[4,4,256]{2,1,0:T(4,128)S(1)}, u32[]{:S(2)}, u32[]{:S(2)}) %collective-permute-start.8) | collective-permute-done | bytes 16416 | tf_op jit(solution)/shard_map/ppermute | solution.py:818
  23.6 0.7 %cross_grad.1 = (bf16[2,128,512]{2,1,0:T(8,128)(2,1)S(1)}, bf16[2,128,512]{2,1,0:T(8,128)(2,1)S(1)}, bf16[256,512]{1,0:T(8,128)(2,1)S(1)}, bf16[2,256,512]{2,1,0...) custom-call(bf16[4,256,512]{2,1,0:T(8,128)(2,1)S(1)} %get-tuple-element.93.cross, ...), custom_call_target="tpu_custom_call" | custom-call | flops 1 | bytes 1 | tf_op jit(solution)/shard_map/cross_grad/pallas_call | solution.py:635
  24.4 1.3 %collective-permute-start.9 = (bf16[2,128,512]{2,1,0:T(8,128)(2,1)S(1)}, bf16[2,128,512]{2,1,0:T(8,128)(2,1)S(1)}, u32[]{:S(2)}, u32[]{:S(2)}) collective-permute-start(bf16[2,128,512]{2,1,0:T(8,128)(2,1)S(1)} %get-tuple-element.114), channel_id=1, source_target_pairs={{0,2},{1,3},{2,0},{3,1},{4,6},{5,7},{6,4},{7,5},{8,10},{9,11},{10,... | collective-permute-start | bytes 786440 | tf_op jit(solution)/shard_map/ppermute | solution.py:818
  26.1 4.4 %conditional.4 = (bf16[3,128,1024]{2,1,0:T(8,128)(2,1)S(1)}, bf16[3,128,1024]{2,1,0:T(8,128)(2,1)}) conditional(s32[]{:T(128)} %bitcast.1, () %tuple.35, (bf16[4,256,512]{2,1,0:T(8,128)(2,1)S(1)}, f32[3,8,256]{2,1,0:T(8,128)S(1)}, f32[2,4,256]{2,1,0:T(4,128)S(1)}, f32[1,256]{1,0:T(1,128)S(1)}, bf16[2,256,512]{2,1,0:T(8,128)(2,1)S(1)}, ...), branch_computations={%region_2.0_spmd, %region_3.0_spmd} | conditional | flops 1 | bytes 3145785 | solution.py:824
  26.1 1.7 %far_grad.1 = (bf16[3,128,1024]{2,1,0:T(8,128)(2,1)S(1)}, bf16[3,128,1024]{2,1,0:T(8,128)(2,1)S(1)}) custom-call(bf16[4,256,512]{2,1,0:T(8,128)(2,1)S(1)} %get-tuple-element.29.pair, f32[3,8,256]{2,1,0:T(8,128)S(1)} %get-tuple-element.30.local, f32[2,4,256]{2,1,0:T(4,128)S(1)} %get-tuple-element.31.final, f32[1,256]{1,0:T(1,128)S(1)} %get-tuple-element.32.gates, ...), custom_call_target="tpu_custom_call" | custom-call | flops 1 | bytes 1 | tf_op jit(solution)/shard_map/cond/branch_1_fun/far_grad/pallas_call | solution.py:681
  28.4 2.0 %collective-permute-done = bf16[3,128,1024]{2,1,0:T(8,128)(2,1)} collective-permute-done((bf16[3,128,1024]{2,1,0:T(8,128)(2,1)S(1)}, bf16[3,128,1024]{2,1,0:T(8,128)(2,1)}, u32[]{:S(2)}, u32[]{:S(2)}) %collective-permute-start) | collective-permute-done | bytes 786464 | tf_op jit(solution)/shard_map/cond/branch_1_fun/ppermute | solution.py:818
  30.5 2.5 %join.1 = (f32[1,128,2048]{2,1,0:T(8,128)}, f32[1,128,2048]{2,1,0:T(8,128)}, f32[1,128,2048]{2,1,0:T(8,128)}, f32[2,2,128,512]{3,2,1,0:T(8,128)S(1)}) custom-call(bf16[3,128,1024]{2,1,0:T(8,128)(2,1)S(1)} %get-tuple-element.111.own, bf16[3,128,1024]{2,1,0:T(8,128)(2,1)} %get-tuple-element.112.sib), custom_call_target="tpu_custom_call" | custom-call | flops 1 | bytes 1 | tf_op jit(solution)/shard_map/join/pallas_call | solution.py:722
  33.0 11.5 %conditional.5 = (f32[512]{0:T(512)S(1)}) conditional(s32[]{:T(128)} %bitcast.1, () %tuple.43, f32[8,4,1,512]{3,2,1,0:T(1,128)S(1)} %router_terms.1), branch_computations={%region_4.0_spmd, %region_5.0_spmd} | conditional | flops 16384 | bytes 202764 | solution.py:824
  33.0 11.4 %all_to_all.4 = f32[32,1,512]{2,1,0:T(1,128)S(1)} all-to-all(f32[32,1,512]{2,1,0:T(1,128)S(1)} %bitcast.4), channel_id=1, replica_groups=mesh['dp'=8,'ctx'=4] {'dp','ctx'}, dimensions={0} | all-to-all | bytes 131072 | tf_op jit(solution)/shard_map/cond/branch_1_fun/all_to_all | solution.py:846
  44.5 1.2 %add_back.1 = (f32[1,128,2048]{2,1,0:T(8,128)}, f32[1,128,2048]{2,1,0:T(8,128)}, f32[1,128,2048]{2,1,0:T(8,128)}) custom-call(f32[2,2,128,512]{3,2,1,0:T(8,128)S(1)} %get-tuple-element.113.waiting, bf16[2,128,512]{2,1,0:T(8,128)(2,1)S(1)} %collective-permute-done.9.straight, ...), custom_call_target="tpu_custom_call", output_to_operand_aliasing={{0}: (3, {}), {1}: (4, {}), {2}: (5, {})} | custom-call | flops 1 | bytes 1 | tf_op jit(solution)/shard_map/add_back/pallas_call | solution.py:769
  (24 shorter events, 2.0 us)
Async XLA Ops:
  0.6 5.9 %copy-start = (s32[1,128]{1,0:T(1,128)S(1)}, s32[1,128]{1,0:T(1,128)}, u32[]{:S(2)}) copy-start(s32[1,128]{1,0:T(1,128)} %pos_ref.2) | copy-start | bytes 1540
  2.0 6.6 %copy-start.1 = (bf16[1,128,4096]{2,1,0:T(8,128)(2,1)S(1)}, bf16[1,128,4096]{2,1,0:T(8,128)(2,1)}, u32[]{:S(2)}) copy-start(bf16[1,128,4096]{2,1,0:T(8,128)(2,1)} %x_ref.1) | copy-start | bytes 3145732
  2.0 16.2 %collective-permute-start.5 = (bf16[2,128,512]{2,1,0:T(8,128)(2,1)S(1)}, bf16[2,128,512]{2,1,0:T(8,128)(2,1)S(1)}, u32[]{:S(2)}, u32[]{:S(2)}) collective-permute-start(bf16[2,128,512]{2,1,0:T(8,128)(2,1)S(1)} %get-tuple-element.83), channel_id=1, source_target_pairs={{0,2},{1,3},{2,0},{3,1},{4,6},{5,7},{6,4},{7,5},{8,10},{9,11},{10,... | collective-permute-start | bytes 786440 | tf_op jit(solution)/shard_map/ppermute | solution.py:818
  5.0 13.3 %collective-permute-start.6 = (bf16[2,128,512]{2,1,0:T(8,128)(2,1)S(1)}, bf16[2,128,512]{2,1,0:T(8,128)(2,1)S(1)}, u32[]{:S(2)}, u32[]{:S(2)}) collective-permute-start(bf16[2,128,512]{2,1,0:T(8,128)(2,1)S(1)} %get-tuple-element.92), channel_id=1, source_target_pairs={{0,3},{1,2},{2,1},{3,0},{4,7},{5,6},{6,5},{7,4},{8,11},{9,10},{10,... | collective-permute-start | bytes 786440 | tf_op jit(solution)/shard_map/ppermute | solution.py:818
  5.0 3.6 %collective-permute-start.4 = (f32[1,512]{1,0:T(1,128)S(1)}, f32[1,512]{1,0:T(1,128)S(1)}, u32[]{:S(2)}, u32[]{:S(2)}) collective-permute-start(f32[1,512]{1,0:T(1,128)S(1)} %get-tuple-element.85), channel_id=1, source_target_pairs={{0,4},{4,0},{8,12},{12,8},{16,20},{20,16},{24,28},{28,24},{1,5},{5... | collective-permute-start | bytes 6152 | tf_op jit(solution)/shard_map/ppermute | solution.py:830
  8.6 4.2 %collective-permute-start.1 = (bf16[4,128,1024]{2,1,0:T(8,128)(2,1)S(1)}, bf16[4,128,1024]{2,1,0:T(8,128)(2,1)}, u32[]{:S(2)}, u32[]{:S(2)}) collective-permute-start(bf16[4,128,1024]{2,1,0:T(8,128)(2,1)S(1)} %get-tuple-element.26), channel_id=1, source_target_pairs={{0,1},{1,0},{2,3},{3,2},{4,5},{5,4},{6,7},{7,6},{8,9},{9,8},{10,11... | collective-permute-start | bytes 3145736 | tf_op jit(solution)/shard_map/cond/branch_1_fun/ppermute | solution.py:818
  8.7 4.3 %collective-permute-start.2 = (bf16[1,128,4096]{2,1,0:T(8,128)(2,1)S(1)}, bf16[1,128,4096]{2,1,0:T(8,128)(2,1)}, u32[]{:S(2)}, u32[]{:S(2)}) collective-permute-start(bf16[1,128,4096]{2,1,0:T(8,128)(2,1)S(1)} %get-tuple-element.27), channel_id=1, source_target_pairs={{0,1},{1,0},{2,3},{3,2},{4,5},{5,4},{6,7},{7,6},{8,9},{9,8},{10,11... | collective-permute-start | bytes 3145736 | tf_op jit(solution)/shard_map/cond/branch_1_fun/ppermute | solution.py:818
  9.2 3.6 %collective-permute-start.3 = (f32[1,1024]{1,0:T(1,128)S(1)}, f32[1,1024]{1,0:T(1,128)S(1)}, u32[]{:S(2)}, u32[]{:S(2)}) collective-permute-start(f32[1,1024]{1,0:T(1,128)S(1)} %get-tuple-element.28), channel_id=1, source_target_pairs={{0,8},{4,12},{8,0},{12,4},{16,24},{20,28},{24,16},{28,20},{1,9},{5... | collective-permute-start | bytes 12296 | tf_op jit(solution)/shard_map/cond/branch_1_fun/ppermute | solution.py:830
  12.9 6.1 %collective-permute-start.7 = (f32[1,2048]{1,0:T(1,128)S(1)}, f32[1,2048]{1,0:T(1,128)S(1)}, u32[]{:S(2)}, u32[]{:S(2)}) collective-permute-start(f32[1,2048]{1,0:T(1,128)S(1)} %get-tuple-element.98), channel_id=1, source_target_pairs={{0,16},{4,20},{8,24},{12,28},{16,0},{20,4},{24,8},{28,12},{1,17},{... | collective-permute-start | bytes 24584 | tf_op jit(solution)/shard_map/ppermute | solution.py:830
  19.8 3.8 %collective-permute-start.8 = (f32[4,4,256]{2,1,0:T(4,128)S(1)}, f32[4,4,256]{2,1,0:T(4,128)S(1)}, u32[]{:S(2)}, u32[]{:S(2)}) collective-permute-start(f32[4,4,256]{2,1,0:T(4,128)S(1)} %get-tuple-element.100), channel_id=1, source_target_pairs={{0,2},{1,3},{2,0},{3,1},{4,6},{5,7},{6,4},{7,5},{8,10},{9,11},{10,... | collective-permute-start | bytes 49160 | tf_op jit(solution)/shard_map/ppermute | solution.py:818
  24.3 20.2 %collective-permute-start.10 = (bf16[2,128,512]{2,1,0:T(8,128)(2,1)S(1)}, bf16[2,128,512]{2,1,0:T(8,128)(2,1)S(1)}, u32[]{:S(2)}, u32[]{:S(2)}) collective-permute-start(bf16[2,128,512]{2,1,0:T(8,128)(2,1)S(1)} %get-tuple-element.115), channel_id=1, source_target_pairs={{0,3},{1,2},{2,1},{3,0},{4,7},{5,6},{6,5},{7,4},{8,11},{9,10},{10,... | collective-permute-start | bytes 786440 | tf_op jit(solution)/shard_map/ppermute | solution.py:818
  24.4 20.2 %collective-permute-start.9 = (bf16[2,128,512]{2,1,0:T(8,128)(2,1)S(1)}, bf16[2,128,512]{2,1,0:T(8,128)(2,1)S(1)}, u32[]{:S(2)}, u32[]{:S(2)}) collective-permute-start(bf16[2,128,512]{2,1,0:T(8,128)(2,1)S(1)} %get-tuple-element.114), channel_id=1, source_target_pairs={{0,2},{1,3},{2,0},{3,1},{4,6},{5,7},{6,4},{7,5},{8,10},{9,11},{10,... | collective-permute-start | bytes 786440 | tf_op jit(solution)/shard_map/ppermute | solution.py:818
  27.8 2.7 %collective-permute-start = (bf16[3,128,1024]{2,1,0:T(8,128)(2,1)S(1)}, bf16[3,128,1024]{2,1,0:T(8,128)(2,1)}, u32[]{:S(2)}, u32[]{:S(2)}) collective-permute-start(bf16[3,128,1024]{2,1,0:T(8,128)(2,1)S(1)} %get-tuple-element.38), channel_id=1, source_target_pairs={{0,1},{1,0},{2,3},{3,2},{4,5},{5,4},{6,7},{7,6},{8,9},{9,8},{10,11... | collective-permute-start | bytes 2359304 | tf_op jit(solution)/shard_map/cond/branch_1_fun/ppermute | solution.py:818
  44.5 1.2 %copy-start.2 = (f32[512]{0:T(512)}, f32[512]{0:T(512)S(1)}, u32[]{:S(2)}) copy-start(f32[512]{0:T(512)S(1)} %get-tuple-element.133) | copy-start | bytes 6148

commit v10 on v9

--- a/solution.py
+++ b/solution.py
@@ -715,7 +715,7 @@
 
 
 def join(own, sib, shape):
-    out = jax.ShapeDtypeStruct(shape, F32)
+    out = pltpu.HBM(shape, F32)
     _, slots, half = own.shape
     anywhere = pl.BlockSpec(memory_space=pl.ANY)
     hbm = pl.BlockSpec(memory_space=pltpu.HBM)
@@ -731,7 +731,7 @@
             pltpu.SemaphoreType.DMA((6,)),
         ],
         compiler_params=params(),
-        cost_estimate=cost(0, 18 * out.size),
+        cost_estimate=cost(0, 72 * own.size),
         name="join",
     )(own, sib)
 
@@ -768,7 +768,7 @@
     hbm = pl.BlockSpec(memory_space=pltpu.HBM)
     return pl.pallas_call(
         add_back_kernel,
-        out_shape=[jax.ShapeDtypeStruct(o.shape, F32) for o in outs],
+        out_shape=[pltpu.HBM(o.shape, F32) for o in outs],
         in_specs=[VMEM] * 3 + [hbm] * 3,
         out_specs=[hbm] * 3,
         scratch_shapes=[pltpu.VMEM(waiting.shape, F32), pltpu.SemaphoreType.DMA((4,))],
@@ -776,7 +776,7 @@
         compiler_params=params(),
         cost_estimate=cost(0, 12 * waiting.size),
         name="add_back",
-    )(waiting, straight, diag, *outs)
+    )(waiting, straight, diag, *in_hbm(*outs))
 
 
 def pair_router_kernel(gates_ref, sum_ref, rows_x, out_ref):
@@ -838,13 +838,12 @@
             step *= 2
         return sib, x_sib, w_part
 
-    def far_phase(*operands):
+    def tail_phase(terms, *operands):
         own_out, sib_out = far_grad(*operands)
-        return own_out, send(sib_out, 1)
-
-    def router_phase(terms):
-        shared = lax.all_to_all(terms.reshape(ndp * n, 1, -1), ("dp", "ctx"), 0, 0, tiled=True)
-        return jnp.sum(shared, axis=0)[0] / float(ndp * n * slots // 2)
+        sib_in = send(sib_out, 1)
+        shared = lax.all_to_all(after(terms, own_out).reshape(ndp * n, 1, -1), ("dp", "ctx"), 0, 0, tiled=True)
+        *outs, waiting = join(own_out, sib_in, queries.shape)
+        return outs, waiting, jnp.sum(shared, axis=0)[0] / float(ndp * n * slots // 2)
 
     out_s, out_d, w_part = cross_pack(route_pos, w_router, keys, values, queries, d_gated)
     in_s, in_d = send(out_s, 2), send(out_d, 3)
@@ -867,11 +866,9 @@
 
     ret_s, ret_d = send(back_s, 2), send(back_d, 3)
     terms = pair_router(gates, sums, rows_x, ndp, n)
-    own_out, sib_in = beside(
-        far_phase, far, local, final, after(gates, terms), keep, dq_low, near_own, near_sib
+    outs, waiting, router_grad = beside(
+        tail_phase, terms, far, local, final, gates, keep, dq_low, near_own, near_sib
     )
-    *outs, waiting = join(own_out, sib_in, queries.shape)
-    router_grad = beside(router_phase, after(terms, waiting))
     dq, dk, dv = add_back(waiting, ret_s, ret_d, outs)
     return dq, dk, dv, router_grad
 

time: 45.9 us -> 46.3 us (level)
  waiting for transfers between devices: 5.83 us -> 3.59 us
  Pallas kernels: 15 us -> 16.1 us
  blocking collectives: 11.4 us -> 12.4 us
  starting transfers between devices: 12.5 us -> 13 us
    ppermute x8, waiting for transfers between devices: 3.09 us -> 0.85 us  [send(): return lax.ppermute(a, 'ctx', [(i, i ^ flip) for i in range(n)])]
    all_to_all x1, blocking collectives: 11.4 us -> 12.4 us  [tail_phase(): lax.all_to_all(after(terms, own_out).reshape(ndp * n, 1, -1), ('dp', 'ctx...]
    pallas_call x1, Pallas kernels: 1.17 us -> 2.11 us  [add_back(): pl.pallas_call(add_back_kernel, out_shape=[pltpu.HBM(o.shape, F32) for o...]
    pallas_call x1, Pallas kernels: 0.69 us -> 1.48 us  [cross_grad(): pl.pallas_call(functools.partial(cross_grad_kernel, HEAD ** (-0.5)), out_...]
    pallas_call x1, Pallas kernels: 2.54 us -> 1.92 us  [join(): pl.pallas_call(join_kernel, out_shape=[out] * 3 + [pltpu.VMEM((2, 2, slot...]
    ppermute x8, starting transfers between devices: 6.78 us -> 7.27 us  [send(): return lax.ppermute(a, 'ctx', [(i, i ^ flip) for i in range(n)])]
  transfers between devices with their start and end apart: 11 -> 11, of which waited for: 5 -> 4; matrix products, arithmetic and copies ran while one was open for 0% -> 0% of each run, Pallas kernels for 24% -> 23%
where the time goes in v10:
time: 46.3 us; the launch traced here: 46.1 us
  Pallas kernels  16.1 us (35%)
  starting transfers between devices  13 us (28%)
  blocking collectives  12.4 us (27%)
  waiting for transfers between devices  3.59 us (8%)
  between operations  0.81 us (2%)
    all_to_all x1, blocking collectives, tail_phase(): lax.all_to_all(after(terms, own_out).reshape(ndp * n, 1, -1), ('dp', 'ctx...  12.4 us
    ppermute x8, starting transfers between devices, send(): return lax.ppermute(a, 'ctx', [(i, i ^ flip) for i in range(n)])  7.27 us
    ppermute x3, starting transfers between devices, widen(): other = lax.ppermute(part, 'dp', [(i, i ^ step) for i in range(ndp)])  5.68 us
    ppermute x3, waiting for transfers between devices, widen(): other = lax.ppermute(part, 'dp', [(i, i ^ step) for i in range(ndp)])  2.74 us
    pallas_call x1, Pallas kernels, local_stats(): pl.pallas_call(functools.partial(local_stats_kernel, HEAD ** (-0.5)), out...  2.71 us
    pallas_call x1, Pallas kernels, add_back(): pl.pallas_call(add_back_kernel, out_shape=[pltpu.HBM(o.shape, F32) for o...  2.11 us
    pallas_call x1, Pallas kernels, join(): pl.pallas_call(join_kernel, out_shape=[out] * 3 + [pltpu.VMEM((2, 2, slot...  1.92 us
    pallas_call x1, Pallas kernels, far_grad(): pl.pallas_call(functools.partial(far_grad_kernel, HEAD ** (-0.5)), out_sh...  1.72 us
  transfers between devices with their start and end apart: 11, of which 4 were waited for; matrix products, arithmetic and copies ran while one was open for 0% of the time, Pallas kernels for 23%

profile of v10, /device:TPU:0, one launch (start us, length us, event | category | flops | bytes accessed | tf_op | source)
XLA Modules:
  0.0 46.1 jit_solution(9018247313858305989)
XLA Ops:
  0.6 1.3 %cross_pack.1 = (bf16[2,128,512]{2,1,0:T(8,128)(2,1)S(1)}, bf16[2,128,512]{2,1,0:T(8,128)(2,1)S(1)}, f32[1,512]{1,0:T(1,128)S(1)}) custom-call(s32[1,128]{1,0:T(1,128)} %pos_ref.2, bf16[512]{0:T(512)(128)(2,1)} %w_any.1, bf16[1,128,2048]{2,1,0:T(8,128)(2,1)} %k_ref.5, bf16[1,128,2048]{2,1,0:T(8,128)(2,1)} %v_ref.5, bf16[1,128,2048]{2,1,0:T(8,128)(2,1)} %q_ref.5, ...), custom_call_target="tpu_custom_call" | custom-call | flops 1 | bytes 1 | tf_op jit(solution)/shard_map/cross_pack/pallas_call | solution.py:314
  2.0 2.4 %collective-permute-start.6 = (bf16[2,128,512]{2,1,0:T(8,128)(2,1)S(1)}, bf16[2,128,512]{2,1,0:T(8,128)(2,1)S(1)}, u32[]{:S(2)}, u32[]{:S(2)}) collective-permute-start(bf16[2,128,512]{2,1,0:T(8,128)(2,1)S(1)} %get-tuple-element.93), channel_id=1, source_target_pairs={{0,3},{1,2},{2,1},{3,0},{4,7},{5,6},{6,5},{7,4},{8,11},{9,10},{10,... | collective-permute-start | bytes 786440 | tf_op jit(solution)/shard_map/ppermute | solution.py:818
  4.4 0.6 %collective-permute-start.5 = (bf16[2,128,512]{2,1,0:T(8,128)(2,1)S(1)}, bf16[2,128,512]{2,1,0:T(8,128)(2,1)S(1)}, u32[]{:S(2)}, u32[]{:S(2)}) collective-permute-start(bf16[2,128,512]{2,1,0:T(8,128)(2,1)S(1)} %get-tuple-element.84), channel_id=1, source_target_pairs={{0,2},{1,3},{2,0},{3,1},{4,6},{5,7},{6,4},{7,5},{8,10},{9,11},{10,... | collective-permute-start | bytes 786440 | tf_op jit(solution)/shard_map/ppermute | solution.py:818
  5.0 1.5 %collective-permute-start.4 = (f32[1,512]{1,0:T(1,128)S(1)}, f32[1,512]{1,0:T(1,128)S(1)}, u32[]{:S(2)}, u32[]{:S(2)}) collective-permute-start(f32[1,512]{1,0:T(1,128)S(1)} %get-tuple-element.86), channel_id=1, source_target_pairs={{0,4},{4,0},{8,12},{12,8},{16,20},{20,16},{24,28},{28,24},{1,5},{5... | collective-permute-start | bytes 6152 | tf_op jit(solution)/shard_map/ppermute | solution.py:830
  6.6 1.3 %sib_pack.1 = bf16[4,128,1024]{2,1,0:T(8,128)(2,1)S(1)} custom-call(s32[1,128]{1,0:T(1,128)S(1)} %copy-done, bf16[1,128,2048]{2,1,0:T(8,128)(2,1)} %k_ref.5, bf16[1,128,2048]{2,1,0:T(8,128)(2,1)} %v_ref.5, bf16[1,128,2048]{2,1,0:T(8,128)(2,1)} %q_ref.5, f32[1,128,2048]{2,1,0:T(8,128)} %dg_ref.5), custom_call_target="tpu_custom_call" | custom-call | flops 1 | bytes 1 | tf_op jit(solution)/shard_map/sib_pack/pallas_call | solution.py:350
  7.9 0.7 %collective-permute-done.4 = f32[1,512]{1,0:T(1,128)S(1)} collective-permute-done((f32[1,512]{1,0:T(1,128)S(1)}, f32[1,512]{1,0:T(1,128)S(1)}, u32[]{:S(2)}, u32[]{:S(2)}) %collective-permute-start.4) | collective-permute-done | bytes 2080 | tf_op jit(solution)/shard_map/ppermute | solution.py:830
  8.6 4.4 %conditional.2 = (bf16[4,128,1024]{2,1,0:T(8,128)(2,1)}, bf16[1,128,4096]{2,1,0:T(8,128)(2,1)}, f32[1,2048]{1,0:T(1,128)S(1)}) conditional(s32[]{:T(128)} %bitcast.1, () %tuple.29, (bf16[4,128,1024]{2,1,0:T(8,128)(2,1)S(1)}, bf16[1,128,4096]{2,1,0:T(8,128)(2,1)S(1)}, f32[1,1024]{1,0:T(1,128)S(1)}) %tuple.40), branch_computations={%region_0.0_spmd, %region_1.0_spmd} | conditional | flops 2048 | bytes 8421520 | solution.py:824
  9.2 1.6 %collective-permute-start.2 = (f32[1,1024]{1,0:T(1,128)S(1)}, f32[1,1024]{1,0:T(1,128)S(1)}, u32[]{:S(2)}, u32[]{:S(2)}) collective-permute-start(f32[1,1024]{1,0:T(1,128)S(1)} %get-tuple-element.26), channel_id=1, source_target_pairs={{0,8},{4,12},{8,0},{12,4},{16,24},{20,28},{24,16},{28,20},{1,9},{5... | collective-permute-start | bytes 12296 | tf_op jit(solution)/shard_map/cond/branch_1_fun/ppermute | solution.py:830
  10.8 2.0 %collective-permute-done.2 = f32[1,1024]{1,0:T(1,128)S(1)} collective-permute-done((f32[1,1024]{1,0:T(1,128)S(1)}, f32[1,1024]{1,0:T(1,128)S(1)}, u32[]{:S(2)}, u32[]{:S(2)}) %collective-permute-start.2) | collective-permute-done | bytes 4128 | tf_op jit(solution)/shard_map/cond/branch_1_fun/ppermute | solution.py:830
  13.0 2.6 %collective-permute-start.7 = (f32[1,2048]{1,0:T(1,128)S(1)}, f32[1,2048]{1,0:T(1,128)S(1)}, u32[]{:S(2)}, u32[]{:S(2)}) collective-permute-start(f32[1,2048]{1,0:T(1,128)S(1)} %get-tuple-element.99), channel_id=1, source_target_pairs={{0,16},{4,20},{8,24},{12,28},{16,0},{20,4},{24,8},{28,12},{1,17},{... | collective-permute-start | bytes 24584 | tf_op jit(solution)/shard_map/ppermute | solution.py:830
  15.6 2.7 %local_stats.1 = (f32[3,8,256]{2,1,0:T(8,128)S(1)}, f32[1,256]{1,0:T(1,128)S(1)}, bf16[4,256,512]{2,1,0:T(8,128)(2,1)S(1)}, bf16[4,256,512]{2,1,0:T(8,128)(2,1)S(1)}, bf16[2,128,4096]{2,1,0:T(8,128)(2,1)S(1)}) custom-call(s32[1,128]{1,0:T(1,128)S(1)} %copy-done, bf16[1,128,2048]{2,1,0:T(8,128)(2,1)} %k_ref.5, bf16[1,128,2048]{2,1,0:T(8,128)(2,1)} %v_ref.5, ...), custom_call_target="tpu_custom_call" | custom-call | flops 1 | bytes 1 | tf_op jit(solution)/shard_map/local_stats/pallas_call | solution.py:476
  18.3 0.8 %cross_stats.1 = (bf16[4,256,512]{2,1,0:T(8,128)(2,1)S(1)}, f32[3,4,256]{2,1,0:T(4,128)S(1)}, bf16[2,4,256,256]{3,2,1,0:T(8,128)(2,1)S(1)}) custom-call(bf16[4,256,512]{2,1,0:T(8,128)(2,1)S(1)} %get-tuple-element.92.near.pair, bf16[4,256,512]{2,1,0:T(8,128)(2,1)S(1)} %get-tuple-element.90.far, bf16[2,128,512]{2,1,0:T(8,128)(2,1)S(1)} %collective-permute-done.5.straight, ...), custom_call_target="tpu_custom_call" | custom-call | flops 1 | bytes 1 | tf_op jit(solution)/shard_map/cross_stats/pallas_call | solution.py:525
  19.2 0.7 %router_gate.1 = (f32[1,256]{1,0:T(1,128)S(1)}, f32[4,4,256]{2,1,0:T(4,128)S(1)}) custom-call(f32[1,256]{1,0:T(1,128)S(1)} %get-tuple-element.97.live_ref, bf16[2,128,4096]{2,1,0:T(8,128)(2,1)S(1)} %get-tuple-element.98.rows_x, f32[1,4096]{1,0:T(1,128)S(1)} %pad_maximum_fusion.1.w_ref, f32[3,8,256]{2,1,0:T(8,128)S(1)} %get-tuple-element.91.local, ...), custom_call_target="tpu_custom_call" | custom-call | flops 1 | bytes 1 | tf_op jit(solution)/shard_map/router_gate/pallas_call | solution.py:382
  19.9 1.5 %collective-permute-start.8 = (f32[4,4,256]{2,1,0:T(4,128)S(1)}, f32[4,4,256]{2,1,0:T(4,128)S(1)}, u32[]{:S(2)}, u32[]{:S(2)}) collective-permute-start(f32[4,4,256]{2,1,0:T(4,128)S(1)} %get-tuple-element.101), channel_id=1, source_target_pairs={{0,2},{1,3},{2,0},{3,1},{4,6},{5,7},{6,4},{7,5},{8,10},{9,11},{10,... | collective-permute-start | bytes 49160 | tf_op jit(solution)/shard_map/ppermute | solution.py:818
  21.3 1.6 %near_grad.1 = (f32[256,512]{1,0:T(8,128)S(1)}, bf16[2,128,512]{2,1,0:T(8,128)(2,1)S(1)}, bf16[2,128,512]{2,1,0:T(8,128)(2,1)S(1)}, f32[1,256]{1,0:T(1,128)S(1)}) custom-call(bf16[4,256,512]{2,1,0:T(8,128)(2,1)S(1)} %get-tuple-element.92.near.pair, f32[3,8,256]{2,1,0:T(8,128)S(1)} %get-tuple-element.91.local, f32[3,4,256]{2,1,0:T(4,128)S(1)} %get-tuple-element.96.stats, ...), custom_call_target="tpu_custom_call" | custom-call | flops 1 | bytes 1 | tf_op jit(solution)/shard_map/near_grad/pallas_call | solution.py:590
  23.0 0.7 %collective-permute-done.8.heard = f32[4,4,256]{2,1,0:T(4,128)S(1)} collective-permute-done((f32[4,4,256]{2,1,0:T(4,128)S(1)}, f32[4,4,256]{2,1,0:T(4,128)S(1)}, u32[]{:S(2)}, u32[]{:S(2)}) %collective-permute-start.8) | collective-permute-done | bytes 16416 | tf_op jit(solution)/shard_map/ppermute | solution.py:818
  23.7 1.5 %cross_grad.1 = (bf16[2,128,512]{2,1,0:T(8,128)(2,1)}, bf16[2,128,512]{2,1,0:T(8,128)(2,1)}, bf16[256,512]{1,0:T(8,128)(2,1)S(1)}, bf16[2,256,512]{2,1,0:T(8,128...) custom-call(bf16[4,256,512]{2,1,0:T(8,128)(2,1)S(1)} %get-tuple-element.94.cross, ...), custom_call_target="tpu_custom_call" | custom-call | flops 1 | bytes 1 | tf_op jit(solution)/shard_map/cross_grad/pallas_call | solution.py:635
  25.2 1.4 %collective-permute-start.9 = (bf16[2,128,512]{2,1,0:T(8,128)(2,1)}, bf16[2,128,512]{2,1,0:T(8,128)(2,1)}, u32[]{:S(2)}, u32[]{:S(2)}) collective-permute-start(bf16[2,128,512]{2,1,0:T(8,128)(2,1)} %get-tuple-element.112), channel_id=1, source_target_pairs={{0,2},{1,3},{2,0},{3,1},{4,6},{5,7},{6,4},{7,5},{8,10},{9,11},{10,... | collective-permute-start | bytes 786440 | tf_op jit(solution)/shard_map/ppermute | solution.py:818
  27.0 16.9 %conditional.3 = (f32[1,128,2048]{2,1,0:T(8,128)}, f32[1,128,2048]{2,1,0:T(8,128)}, f32[1,128,2048]{2,1,0:T(8,128)}, f32[2,2,128,512]{3,2,1,0:T(8,128)S(1)}, f32[512]{0:T(512)S(1)}) conditional(s32[]{:T(128)} %bitcast.1, () %tuple.28, (bf16[4,256,512]{2,1,0:T(8,128)(2,1)S(1)}, f32[3,8,256]{2,1,0:T(8,128)S(1)}, f32[2,4,256]{2,1,0:T(4,128)S(1)}, ...), branch_computations={%region_2.0_spmd, %region_3.0_spmd} | conditional | flops 16386 | bytes 4196412 | solution.py:824
  27.0 1.7 %far_grad.1 = (bf16[3,128,1024]{2,1,0:T(8,128)(2,1)S(1)}, bf16[3,128,1024]{2,1,0:T(8,128)(2,1)S(1)}) custom-call(bf16[4,256,512]{2,1,0:T(8,128)(2,1)S(1)} %get-tuple-element.27.pair, f32[3,8,256]{2,1,0:T(8,128)S(1)} %get-tuple-element.28.local, f32[2,4,256]{2,1,0:T(4,128)S(1)} %get-tuple-element.29.final, f32[1,256]{1,0:T(1,128)S(1)} %get-tuple-element.30.gates, ...), custom_call_target="tpu_custom_call" | custom-call | flops 1 | bytes 1 | tf_op jit(solution)/shard_map/cond/branch_1_fun/far_grad/pallas_call | solution.py:681
  28.7 0.8 %collective-permute-start.3 = (bf16[3,128,1024]{2,1,0:T(8,128)(2,1)S(1)}, bf16[3,128,1024]{2,1,0:T(8,128)(2,1)S(1)}, u32[]{:S(2)}, u32[]{:S(2)}) collective-permute-start(bf16[3,128,1024]{2,1,0:T(8,128)(2,1)S(1)} %get-tuple-element.36), channel_id=1, source_target_pairs={{0,1},{1,0},{2,3},{3,2},{4,5},{5,4},{6,7},{7,6},{8,9},{9,8},{10,11... | collective-permute-start | bytes 2359304 | tf_op jit(solution)/shard_map/cond/branch_1_fun/ppermute | solution.py:818
  29.5 12.4 %all_to_all.4 = f32[32,1,512]{2,1,0:T(1,128)S(1)} all-to-all(f32[32,1,512]{2,1,0:T(1,128)S(1)} %bitcast.4), channel_id=1, replica_groups=mesh['dp'=8,'ctx'=4] {'dp','ctx'}, dimensions={0} | all-to-all | bytes 131072 | tf_op jit(solution)/shard_map/cond/branch_1_fun/all_to_all | solution.py:844
  42.0 1.9 %join.1 = (f32[1,128,2048]{2,1,0:T(8,128)}, f32[1,128,2048]{2,1,0:T(8,128)}, f32[1,128,2048]{2,1,0:T(8,128)}, f32[2,2,128,512]{3,2,1,0:T(8,128)S(1)}) custom-call(bf16[3,128,1024]{2,1,0:T(8,128)(2,1)S(1)} %get-tuple-element.35.own, bf16[3,128,1024]{2,1,0:T(8,128)(2,1)S(1)} %collective-permute-done.3.sib), custom_call_target="tpu_custom_call" | custom-call | flops 1 | bytes 1 | tf_op jit(solution)/shard_map/cond/branch_1_fun/join/pallas_call | solution.py:722
  43.9 2.1 %add_back.1 = (f32[1,128,2048]{2,1,0:T(8,128)}, f32[1,128,2048]{2,1,0:T(8,128)}, f32[1,128,2048]{2,1,0:T(8,128)}) custom-call(f32[2,2,128,512]{3,2,1,0:T(8,128)S(1)} %get-tuple-element.111.waiting, bf16[2,128,512]{2,1,0:T(8,128)(2,1)} %collective-permute-done.9.straight, ...), custom_call_target="tpu_custom_call", output_to_operand_aliasing={{0}: (3, {}), {1}: (4, {}), {2}: (5, {})} | custom-call | flops 1 | bytes 1 | tf_op jit(solution)/shard_map/add_back/pallas_call | solution.py:769
  (23 shorter events, 1.3 us)
Async XLA Ops:
  0.6 5.9 %copy-start = (s32[1,128]{1,0:T(1,128)S(1)}, s32[1,128]{1,0:T(1,128)}, u32[]{:S(2)}) copy-start(s32[1,128]{1,0:T(1,128)} %pos_ref.2) | copy-start | bytes 1540
  2.0 6.6 %copy-start.1 = (bf16[1,128,4096]{2,1,0:T(8,128)(2,1)S(1)}, bf16[1,128,4096]{2,1,0:T(8,128)(2,1)}, u32[]{:S(2)}) copy-start(bf16[1,128,4096]{2,1,0:T(8,128)(2,1)} %x_ref.1) | copy-start | bytes 3145732
  2.0 16.3 %collective-permute-start.6 = (bf16[2,128,512]{2,1,0:T(8,128)(2,1)S(1)}, bf16[2,128,512]{2,1,0:T(8,128)(2,1)S(1)}, u32[]{:S(2)}, u32[]{:S(2)}) collective-permute-start(bf16[2,128,512]{2,1,0:T(8,128)(2,1)S(1)} %get-tuple-element.93), channel_id=1, source_target_pairs={{0,3},{1,2},{2,1},{3,0},{4,7},{5,6},{6,5},{7,4},{8,11},{9,10},{10,... | collective-permute-start | bytes 786440 | tf_op jit(solution)/shard_map/ppermute | solution.py:818
  4.4 13.9 %collective-permute-start.5 = (bf16[2,128,512]{2,1,0:T(8,128)(2,1)S(1)}, bf16[2,128,512]{2,1,0:T(8,128)(2,1)S(1)}, u32[]{:S(2)}, u32[]{:S(2)}) collective-permute-start(bf16[2,128,512]{2,1,0:T(8,128)(2,1)S(1)} %get-tuple-element.84), channel_id=1, source_target_pairs={{0,2},{1,3},{2,0},{3,1},{4,6},{5,7},{6,4},{7,5},{8,10},{9,11},{10,... | collective-permute-start | bytes 786440 | tf_op jit(solution)/shard_map/ppermute | solution.py:818
  5.0 3.6 %collective-permute-start.4 = (f32[1,512]{1,0:T(1,128)S(1)}, f32[1,512]{1,0:T(1,128)S(1)}, u32[]{:S(2)}, u32[]{:S(2)}) collective-permute-start(f32[1,512]{1,0:T(1,128)S(1)} %get-tuple-element.86), channel_id=1, source_target_pairs={{0,4},{4,0},{8,12},{12,8},{16,20},{20,16},{24,28},{28,24},{1,5},{5... | collective-permute-start | bytes 6152 | tf_op jit(solution)/shard_map/ppermute | solution.py:830
  8.7 4.2 %collective-permute-start = (bf16[4,128,1024]{2,1,0:T(8,128)(2,1)S(1)}, bf16[4,128,1024]{2,1,0:T(8,128)(2,1)}, u32[]{:S(2)}, u32[]{:S(2)}) collective-permute-start(bf16[4,128,1024]{2,1,0:T(8,128)(2,1)S(1)} %get-tuple-element.24), channel_id=1, source_target_pairs={{0,1},{1,0},{2,3},{3,2},{4,5},{5,4},{6,7},{7,6},{8,9},{9,8},{10,11... | collective-permute-start | bytes 3145736 | tf_op jit(solution)/shard_map/cond/branch_1_fun/ppermute | solution.py:818
  8.7 4.3 %collective-permute-start.1 = (bf16[1,128,4096]{2,1,0:T(8,128)(2,1)S(1)}, bf16[1,128,4096]{2,1,0:T(8,128)(2,1)}, u32[]{:S(2)}, u32[]{:S(2)}) collective-permute-start(bf16[1,128,4096]{2,1,0:T(8,128)(2,1)S(1)} %get-tuple-element.25), channel_id=1, source_target_pairs={{0,1},{1,0},{2,3},{3,2},{4,5},{5,4},{6,7},{7,6},{8,9},{9,8},{10,11... | collective-permute-start | bytes 3145736 | tf_op jit(solution)/shard_map/cond/branch_1_fun/ppermute | solution.py:818
  9.2 3.6 %collective-permute-start.2 = (f32[1,1024]{1,0:T(1,128)S(1)}, f32[1,1024]{1,0:T(1,128)S(1)}, u32[]{:S(2)}, u32[]{:S(2)}) collective-permute-start(f32[1,1024]{1,0:T(1,128)S(1)} %get-tuple-element.26), channel_id=1, source_target_pairs={{0,8},{4,12},{8,0},{12,4},{16,24},{20,28},{24,16},{28,20},{1,9},{5... | collective-permute-start | bytes 12296 | tf_op jit(solution)/shard_map/cond/branch_1_fun/ppermute | solution.py:830
  13.0 6.1 %collective-permute-start.7 = (f32[1,2048]{1,0:T(1,128)S(1)}, f32[1,2048]{1,0:T(1,128)S(1)}, u32[]{:S(2)}, u32[]{:S(2)}) collective-permute-start(f32[1,2048]{1,0:T(1,128)S(1)} %get-tuple-element.99), channel_id=1, source_target_pairs={{0,16},{4,20},{8,24},{12,28},{16,0},{20,4},{24,8},{28,12},{1,17},{... | collective-permute-start | bytes 24584 | tf_op jit(solution)/shard_map/ppermute | solution.py:830
  19.9 3.8 %collective-permute-start.8 = (f32[4,4,256]{2,1,0:T(4,128)S(1)}, f32[4,4,256]{2,1,0:T(4,128)S(1)}, u32[]{:S(2)}, u32[]{:S(2)}) collective-permute-start(f32[4,4,256]{2,1,0:T(4,128)S(1)} %get-tuple-element.101), channel_id=1, source_target_pairs={{0,2},{1,3},{2,0},{3,1},{4,6},{5,7},{6,4},{7,5},{8,10},{9,11},{10,... | collective-permute-start | bytes 49160 | tf_op jit(solution)/shard_map/ppermute | solution.py:818
  25.2 18.8 %collective-permute-start.9 = (bf16[2,128,512]{2,1,0:T(8,128)(2,1)}, bf16[2,128,512]{2,1,0:T(8,128)(2,1)}, u32[]{:S(2)}, u32[]{:S(2)}) collective-permute-start(bf16[2,128,512]{2,1,0:T(8,128)(2,1)} %get-tuple-element.112), channel_id=1, source_target_pairs={{0,2},{1,3},{2,0},{3,1},{4,6},{5,7},{6,4},{7,5},{8,10},{9,11},{10,... | collective-permute-start | bytes 786440 | tf_op jit(solution)/shard_map/ppermute | solution.py:818
  26.6 17.4 %collective-permute-start.10 = (bf16[2,128,512]{2,1,0:T(8,128)(2,1)}, bf16[2,128,512]{2,1,0:T(8,128)(2,1)}, u32[]{:S(2)}, u32[]{:S(2)}) collective-permute-start(bf16[2,128,512]{2,1,0:T(8,128)(2,1)} %get-tuple-element.113), channel_id=1, source_target_pairs={{0,3},{1,2},{2,1},{3,0},{4,7},{5,6},{6,5},{7,4},{8,11},{9,10},{10,... | collective-permute-start | bytes 786440 | tf_op jit(solution)/shard_map/ppermute | solution.py:818
  28.7 13.3 %collective-permute-start.3 = (bf16[3,128,1024]{2,1,0:T(8,128)(2,1)S(1)}, bf16[3,128,1024]{2,1,0:T(8,128)(2,1)S(1)}, u32[]{:S(2)}, u32[]{:S(2)}) collective-permute-start(bf16[3,128,1024]{2,1,0:T(8,128)(2,1)S(1)} %get-tuple-element.36), channel_id=1, source_target_pairs={{0,1},{1,0},{2,3},{3,2},{4,5},{5,4},{6,7},{7,6},{8,9},{9,8},{10,11... | collective-permute-start | bytes 2359304 | tf_op jit(solution)/shard_map/cond/branch_1_fun/ppermute | solution.py:818
  43.9 2.2 %copy-start.2 = (f32[512]{0:T(512)}, f32[512]{0:T(512)S(1)}, u32[]{:S(2)}) copy-start(f32[512]{0:T(512)S(1)} %get-tuple-element.83) | copy-start | bytes 6148

commit v11 on v10

--- a/solution.py
+++ b/solution.py
@@ -708,8 +708,8 @@
             total[i, j] = low[i, j].astype(F32)
             stores.append(pltpu.make_async_copy(total.at[i, j], out.at[0, :, cols], out_sems.at[3 * i + j]))
             stores[-1].start()
-        waiting[i, 0] = jnp.where(chip == 0, total[i, 1, :, :width], total[i, 0, :, width:])
-        waiting[i, 1] = total[i, 2, :, :width]
+        waiting[i, 0] = jnp.where(chip == 0, total[i, 1, :, :width], total[i, 0, :, width:]).astype(BF16)
+        waiting[i, 1] = low[i, 2, :, :width]
     for c in stores:
         c.wait()
 
@@ -721,7 +721,7 @@
     hbm = pl.BlockSpec(memory_space=pltpu.HBM)
     return pl.pallas_call(
         join_kernel,
-        out_shape=[out] * 3 + [pltpu.VMEM((2, 2, slots, half // 2), F32)],
+        out_shape=[out] * 3 + [pltpu.VMEM((2, 2, slots, half // 2), BF16)],
         in_specs=[anywhere] * 2,
         out_specs=[hbm] * 3 + [VMEM],
         scratch_shapes=[
@@ -749,7 +749,7 @@
 
     for i, (back, _) in enumerate(ends):
         for j in range(2):
-            total[i, j] = waiting[i, j] + back[j].astype(F32)
+            total[i, j] = waiting[i, j].astype(F32) + back[j].astype(F32)
 
     @pl.when(chip == 0)
     def _():
@@ -838,11 +838,14 @@
             step *= 2
         return sib, x_sib, w_part
 
+    def far_phase(*operands):
+        own_out, sib_out = far_grad(*operands)
+        *outs, waiting = join(own_out, send(sib_out, 1), queries.shape)
+        return outs, waiting
+
     def tail_phase(terms, *operands):
-        own_out, sib_out = far_grad(*operands)
-        sib_in = send(sib_out, 1)
-        shared = lax.all_to_all(after(terms, own_out).reshape(ndp * n, 1, -1), ("dp", "ctx"), 0, 0, tiled=True)
-        *outs, waiting = join(own_out, sib_in, queries.shape)
+        shared = lax.all_to_all(terms.reshape(ndp * n, 1, -1), ("dp", "ctx"), 0, 0, tiled=True)
+        outs, waiting = beside(far_phase, *operands)
         return outs, waiting, jnp.sum(shared, axis=0)[0] / float(ndp * n * slots // 2)
 
     out_s, out_d, w_part = cross_pack(route_pos, w_router, keys, values, queries, d_gated)

time: 46.3 us -> 42.3 us (0.914)
  blocking collectives: 12.4 us -> 0 us
  starting transfers between devices: 13 us -> 18.1 us
  waiting for transfers between devices: 3.59 us -> 6.19 us
  Pallas kernels: 16.1 us -> 16.8 us
    all_to_all x1 -> x0, blocking collectives: 12.4 us -> none  [tail_phase(): lax.all_to_all(after(terms, own_out).reshape(ndp * n, 1, -1), ('dp', 'ctx...]
    all_to_all x0 -> x1, starting transfers between devices: none -> 5.53 us  [tail_phase(): lax.all_to_all(terms.reshape(ndp * n, 1, -1), ('dp', 'ctx'), 0, 0, tiled=...]
    ppermute x8, waiting for transfers between devices: 0.85 us -> 2.88 us  [send(): return lax.ppermute(a, 'ctx', [(i, i ^ flip) for i in range(n)])]
    pallas_call x1, Pallas kernels: 1.92 us -> 2.71 us  [join(): pl.pallas_call(join_kernel, out_shape=[out] * 3 + [pltpu.VMEM((2, 2, slot...]
    pallas_call x1, Pallas kernels: 1.48 us -> 0.69 us  [cross_grad(): pl.pallas_call(functools.partial(cross_grad_kernel, HEAD ** (-0.5)), out_...]
    pallas_call x1, Pallas kernels: 0.4 us -> 1.04 us  [pair_router(): pl.pallas_call(pair_router_kernel, out_shape=jax.ShapeDtypeStruct((parts,...]
    all_to_all x0 -> x1, waiting for transfers between devices: none -> 0.56 us  [tail_phase(): lax.all_to_all(terms.reshape(ndp * n, 1, -1), ('dp', 'ctx'), 0, 0, tiled=...]
  transfers between devices with their start and end apart: 11 -> 12, of which waited for: 4 -> 6; matrix products, arithmetic and copies ran while one was open for 0% -> 0% of each run, Pallas kernels for 23% -> 28%
where the time goes in v11:
time: 42.3 us; the launch traced here: 42.1 us
  starting transfers between devices  18.1 us (43%)
  Pallas kernels  16.8 us (40%)
  waiting for transfers between devices  6.19 us (15%)
  between operations  0.81 us (2%)
    ppermute x8, starting transfers between devices, send(): return lax.ppermute(a, 'ctx', [(i, i ^ flip) for i in range(n)])  6.85 us
    ppermute x3, starting transfers between devices, widen(): other = lax.ppermute(part, 'dp', [(i, i ^ step) for i in range(ndp)])  5.68 us
    all_to_all x1, starting transfers between devices, tail_phase(): lax.all_to_all(terms.reshape(ndp * n, 1, -1), ('dp', 'ctx'), 0, 0, tiled=...  5.53 us
    ppermute x8, waiting for transfers between devices, send(): return lax.ppermute(a, 'ctx', [(i, i ^ flip) for i in range(n)])  2.88 us
    ppermute x3, waiting for transfers between devices, widen(): other = lax.ppermute(part, 'dp', [(i, i ^ step) for i in range(ndp)])  2.74 us
    pallas_call x1, Pallas kernels, join(): pl.pallas_call(join_kernel, out_shape=[out] * 3 + [pltpu.VMEM((2, 2, slot...  2.71 us
    pallas_call x1, Pallas kernels, local_stats(): pl.pallas_call(functools.partial(local_stats_kernel, HEAD ** (-0.5)), out...  2.71 us
    pallas_call x1, Pallas kernels, add_back(): pl.pallas_call(add_back_kernel, out_shape=[pltpu.HBM(o.shape, F32) for o...  2.14 us
  transfers between devices with their start and end apart: 12, of which 6 were waited for; matrix products, arithmetic and copies ran while one was open for 0% of the time, Pallas kernels for 28%

profile of v11, /device:TPU:0, one launch (start us, length us, event | category | flops | bytes accessed | tf_op | source)
XLA Modules:
  0.0 42.1 jit_solution(14189037879343592116)
XLA Ops:
  0.6 1.3 %cross_pack.1 = (bf16[2,128,512]{2,1,0:T(8,128)(2,1)S(1)}, bf16[2,128,512]{2,1,0:T(8,128)(2,1)S(1)}, f32[1,512]{1,0:T(1,128)S(1)}) custom-call(s32[1,128]{1,0:T(1,128)} %pos_ref.2, bf16[512]{0:T(512)(128)(2,1)} %w_any.1, bf16[1,128,2048]{2,1,0:T(8,128)(2,1)} %k_ref.5, bf16[1,128,2048]{2,1,0:T(8,128)(2,1)} %v_ref.5, bf16[1,128,2048]{2,1,0:T(8,128)(2,1)} %q_ref.5, ...), custom_call_target="tpu_custom_call" | custom-call | flops 1 | bytes 1 | tf_op jit(solution)/shard_map/cross_pack/pallas_call | solution.py:314
  2.0 2.4 %collective-permute-start.6 = (bf16[2,128,512]{2,1,0:T(8,128)(2,1)S(1)}, bf16[2,128,512]{2,1,0:T(8,128)(2,1)S(1)}, u32[]{:S(2)}, u32[]{:S(2)}) collective-permute-start(bf16[2,128,512]{2,1,0:T(8,128)(2,1)S(1)} %get-tuple-element.119), channel_id=1, source_target_pairs={{0,3},{1,2},{2,1},{3,0},{4,7},{5,6},{6,5},{7,4},{8,11},{9,10},{10,... | collective-permute-start | bytes 786440 | tf_op jit(solution)/shard_map/ppermute | solution.py:818
  5.0 1.5 %collective-permute-start.4 = (f32[1,512]{1,0:T(1,128)S(1)}, f32[1,512]{1,0:T(1,128)S(1)}, u32[]{:S(2)}, u32[]{:S(2)}) collective-permute-start(f32[1,512]{1,0:T(1,128)S(1)} %get-tuple-element.112), channel_id=1, source_target_pairs={{0,4},{4,0},{8,12},{12,8},{16,20},{20,16},{24,28},{28,24},{1,5},{5... | collective-permute-start | bytes 6152 | tf_op jit(solution)/shard_map/ppermute | solution.py:830
  6.6 1.3 %sib_pack.1 = bf16[4,128,1024]{2,1,0:T(8,128)(2,1)S(1)} custom-call(s32[1,128]{1,0:T(1,128)S(1)} %copy-done.1, bf16[1,128,2048]{2,1,0:T(8,128)(2,1)} %k_ref.5, bf16[1,128,2048]{2,1,0:T(8,128)(2,1)} %v_ref.5, bf16[1,128,2048]{2,1,0:T(8,128)(2,1)} %q_ref.5, f32[1,128,2048]{2,1,0:T(8,128)} %dg_ref.5), custom_call_target="tpu_custom_call" | custom-call | flops 1 | bytes 1 | tf_op jit(solution)/shard_map/sib_pack/pallas_call | solution.py:350
  7.9 0.7 %collective-permute-done.4 = f32[1,512]{1,0:T(1,128)S(1)} collective-permute-done((f32[1,512]{1,0:T(1,128)S(1)}, f32[1,512]{1,0:T(1,128)S(1)}, u32[]{:S(2)}, u32[]{:S(2)}) %collective-permute-start.4) | collective-permute-done | bytes 2080 | tf_op jit(solution)/shard_map/ppermute | solution.py:830
  8.6 4.4 %conditional.3 = (bf16[4,128,1024]{2,1,0:T(8,128)(2,1)}, bf16[1,128,4096]{2,1,0:T(8,128)(2,1)}, f32[1,2048]{1,0:T(1,128)S(1)}) conditional(s32[]{:T(128)} %bitcast.2, () %tuple.35, (bf16[4,128,1024]{2,1,0:T(8,128)(2,1)S(1)}, bf16[1,128,4096]{2,1,0:T(8,128)(2,1)S(1)}, f32[1,1024]{1,0:T(1,128)S(1)}) %tuple.50), branch_computations={%region_0.0_spmd, %region_1.0_spmd} | conditional | flops 2048 | bytes 8421520 | solution.py:824
  9.2 1.6 %collective-permute-start.3 = (f32[1,1024]{1,0:T(1,128)S(1)}, f32[1,1024]{1,0:T(1,128)S(1)}, u32[]{:S(2)}, u32[]{:S(2)}) collective-permute-start(f32[1,1024]{1,0:T(1,128)S(1)} %get-tuple-element.44), channel_id=1, source_target_pairs={{0,8},{4,12},{8,0},{12,4},{16,24},{20,28},{24,16},{28,20},{1,9},{5... | collective-permute-start | bytes 12296 | tf_op jit(solution)/shard_map/cond/branch_1_fun/ppermute | solution.py:830
  10.8 2.0 %collective-permute-done.3 = f32[1,1024]{1,0:T(1,128)S(1)} collective-permute-done((f32[1,1024]{1,0:T(1,128)S(1)}, f32[1,1024]{1,0:T(1,128)S(1)}, u32[]{:S(2)}, u32[]{:S(2)}) %collective-permute-start.3) | collective-permute-done | bytes 4128 | tf_op jit(solution)/shard_map/cond/branch_1_fun/ppermute | solution.py:830
  13.0 2.6 %collective-permute-start.7 = (f32[1,2048]{1,0:T(1,128)S(1)}, f32[1,2048]{1,0:T(1,128)S(1)}, u32[]{:S(2)}, u32[]{:S(2)}) collective-permute-start(f32[1,2048]{1,0:T(1,128)S(1)} %get-tuple-element.125), channel_id=1, source_target_pairs={{0,16},{4,20},{8,24},{12,28},{16,0},{20,4},{24,8},{28,12},{1,17},{... | collective-permute-start | bytes 24584 | tf_op jit(solution)/shard_map/ppermute | solution.py:830
  15.6 2.7 %local_stats.1 = (f32[3,8,256]{2,1,0:T(8,128)S(1)}, f32[1,256]{1,0:T(1,128)S(1)}, bf16[4,256,512]{2,1,0:T(8,128)(2,1)S(1)}, bf16[4,256,512]{2,1,0:T(8,128)(2,1)S(1)}, bf16[2,128,4096]{2,1,0:T(8,128)(2,1)S(1)}) custom-call(s32[1,128]{1,0:T(1,128)S(1)} %copy-done.1, bf16[1,128,2048]{2,1,0:T(8,128)(2,1)} %k_ref.5, bf16[1,128,2048]{2,1,0:T(8,128)(2,1)} %v_ref.5, ...), custom_call_target="tpu_custom_call" | custom-call | flops 1 | bytes 1 | tf_op jit(solution)/shard_map/local_stats/pallas_call | solution.py:476
  18.3 0.8 %cross_stats.1 = (bf16[4,256,512]{2,1,0:T(8,128)(2,1)S(1)}, f32[3,4,256]{2,1,0:T(4,128)S(1)}, bf16[2,4,256,256]{3,2,1,0:T(8,128)(2,1)S(1)}) custom-call(bf16[4,256,512]{2,1,0:T(8,128)(2,1)S(1)} %get-tuple-element.118.near.pair, bf16[4,256,512]{2,1,0:T(8,128)(2,1)S(1)} %get-tuple-element.116.far, bf16[2,128,512]{2,1,0:T(8,128)(2,1)S(1)} %collective-permute-done.5.straight, ...), custom_call_target="tpu_custom_call" | custom-call | flops 1 | bytes 1 | tf_op jit(solution)/shard_map/cross_stats/pallas_call | solution.py:525
  19.9 1.5 %collective-permute-start.8 = (f32[4,4,256]{2,1,0:T(4,128)S(1)}, f32[4,4,256]{2,1,0:T(4,128)S(1)}, u32[]{:S(2)}, u32[]{:S(2)}) collective-permute-start(f32[4,4,256]{2,1,0:T(4,128)S(1)} %get-tuple-element.127), channel_id=1, source_target_pairs={{0,2},{1,3},{2,0},{3,1},{4,6},{5,7},{6,4},{7,5},{8,10},{9,11},{10,... | collective-permute-start | bytes 49160 | tf_op jit(solution)/shard_map/ppermute | solution.py:818
  21.3 1.6 %near_grad.1 = (f32[256,512]{1,0:T(8,128)S(1)}, bf16[2,128,512]{2,1,0:T(8,128)(2,1)S(1)}, bf16[2,128,512]{2,1,0:T(8,128)(2,1)S(1)}, f32[1,256]{1,0:T(1,128)S(1)}) custom-call(bf16[4,256,512]{2,1,0:T(8,128)(2,1)S(1)} %get-tuple-element.118.near.pair, f32[3,8,256]{2,1,0:T(8,128)S(1)} %get-tuple-element.117.local, f32[3,4,256]{2,1,0:T(4,128)S(1)} %get-tuple-element.122.stats, ...), custom_call_target="tpu_custom_call" | custom-call | flops 1 | bytes 1 | tf_op jit(solution)/shard_map/near_grad/pallas_call | solution.py:590
  23.0 0.7 %collective-permute-done.8.heard = f32[4,4,256]{2,1,0:T(4,128)S(1)} collective-permute-done((f32[4,4,256]{2,1,0:T(4,128)S(1)}, f32[4,4,256]{2,1,0:T(4,128)S(1)}, u32[]{:S(2)}, u32[]{:S(2)}) %collective-permute-start.8) | collective-permute-done | bytes 16416 | tf_op jit(solution)/shard_map/ppermute | solution.py:818
  23.7 0.7 %cross_grad.1 = (bf16[2,128,512]{2,1,0:T(8,128)(2,1)S(1)}, bf16[2,128,512]{2,1,0:T(8,128)(2,1)S(1)}, bf16[256,512]{1,0:T(8,128)(2,1)S(1)}, bf16[2,256,512]{2,1,0...) custom-call(bf16[4,256,512]{2,1,0:T(8,128)(2,1)S(1)} %get-tuple-element.120.cross, ...), custom_call_target="tpu_custom_call" | custom-call | flops 1 | bytes 1 | tf_op jit(solution)/shard_map/cross_grad/pallas_call | solution.py:635
  24.4 1.5 %collective-permute-start.9 = (bf16[2,128,512]{2,1,0:T(8,128)(2,1)S(1)}, bf16[2,128,512]{2,1,0:T(8,128)(2,1)S(1)}, u32[]{:S(2)}, u32[]{:S(2)}) collective-permute-start(bf16[2,128,512]{2,1,0:T(8,128)(2,1)S(1)} %get-tuple-element.138), channel_id=1, source_target_pairs={{0,2},{1,3},{2,0},{3,1},{4,6},{5,7},{6,4},{7,5},{8,10},{9,11},{10,... | collective-permute-start | bytes 786440 | tf_op jit(solution)/shard_map/ppermute | solution.py:818
  25.8 1.0 %router_terms.1 = f32[8,4,1,512]{3,2,1,0:T(1,128)} custom-call(f32[1,256]{1,0:T(1,128)S(1)} %get-tuple-element.128.gates.gates_ref, f32[1,256]{1,0:T(1,128)S(1)} %get-tuple-element.136.sum_ref, bf16[2,128,4096]{2,1,0:T(8,128)(2,1)S(1)} %get-tuple-element.124.rows_x), custom_call_target="tpu_custom_call" | custom-call | flops 1 | bytes 1 | tf_op jit(solution)/shard_map/router_terms/pallas_call | solution.py:802
  26.9 13.0 %conditional.4 = (f32[1,128,2048]{2,1,0:T(8,128)}, f32[1,128,2048]{2,1,0:T(8,128)}, f32[1,128,2048]{2,1,0:T(8,128)}, bf16[2,2,128,512]{3,2,1,0:T(8,128)(2,1)}, f32[512]{0:T(512)S(1)}) conditional(s32[]{:T(128)} %bitcast.2, () %tuple.34, (s32[1,128]{1,0:T(1,128)S(1)}, bf16[4,256,512]{2,1,0:T(8,128)(2,1)S(1)}, f32[3,8,256]{2,1,0:T(8,128)S(1)}, ...), branch_computations={%region_2.0_spmd, %region_3.0_spmd} | conditional | flops 16388 | bytes 3938512 | solution.py:824
  26.9 5.5 %all-to-all-start = ((f32[32,1,512]{2,1,0:T(1,128)}), f32[32,1,512]{2,1,0:T(1,128)S(1)}, u32[]{:S(2)}, u32[]{:S(2)}) async-start(f32[32,1,512]{2,1,0:T(1,128)} %bitcast.1), calls=%async_computation | async-start | bytes 131072 | tf_op jit(solution)/shard_map/cond/branch_1_fun/all_to_all | solution.py:847
  32.5 6.8 %conditional = ((f32[1,128,2048]{2,1,0:T(8,128)}, f32[1,128,2048]{2,1,0:T(8,128)}, f32[1,128,2048]{2,1,0:T(8,128)}, bf16[2,2,128,512]{3,2,1,0:T(8,128)(2,1)})) conditional(s32[]{:T(128)} %bitcast, () %tuple.22, (bf16[4,256,512]{2,1,0:T(8,128)(2,1)S(1)}, f32[3,8,256]{2,1,0:T(8,128)S(1)}, f32[2,4,256]{2,1,0:T(4,128)S(1)}, f32[1,256]{1,0:T(1,128)S(1)}, ...), branch_computations={%region_4.0_spmd, %region_5.0_spmd} | conditional | flops 2 | bytes 3670070 | solution.py:824
  32.5 1.7 %far_grad.1 = (bf16[3,128,1024]{2,1,0:T(8,128)(2,1)S(1)}, bf16[3,128,1024]{2,1,0:T(8,128)(2,1)S(1)}) custom-call(bf16[4,256,512]{2,1,0:T(8,128)(2,1)S(1)} %get-tuple-element.45.pair, f32[3,8,256]{2,1,0:T(8,128)S(1)} %get-tuple-element.46.local, f32[2,4,256]{2,1,0:T(4,128)S(1)} %get-tuple-element.47.final, f32[1,256]{1,0:T(1,128)S(1)} %get-tuple-element.48.gates, ...), custom_call_target="tpu_custom_call" | custom-call | flops 1 | bytes 1 | tf_op jit(solution)/shard_map/cond/branch_1_fun/cond/branch_1_fun/far_grad/pallas_call | solution.py:681
  34.5 2.0 %collective-permute-done.sib = bf16[3,128,1024]{2,1,0:T(8,128)(2,1)S(1)} collective-permute-done((bf16[3,128,1024]{2,1,0:T(8,128)(2,1)S(1)}, bf16[3,128,1024]{2,1,0:T(8,128)(2,1)S(1)}, u32[]{:S(2)}, u32[]{:S(2)}) %collective-permute-start) | collective-permute-done | bytes 786464 | tf_op jit(solution)/shard_map/cond/branch_1_fun/cond/branch_1_fun/ppermute | solution.py:818
  36.5 2.7 %join.1 = (f32[1,128,2048]{2,1,0:T(8,128)}, f32[1,128,2048]{2,1,0:T(8,128)}, f32[1,128,2048]{2,1,0:T(8,128)}, bf16[2,2,128,512]{3,2,1,0:T(8,128)(2,1)}) custom-call(bf16[3,128,1024]{2,1,0:T(8,128)(2,1)S(1)} %get-tuple-element.53.own, bf16[3,128,1024]{2,1,0:T(8,128)(2,1)S(1)} %collective-permute-done.sib), custom_call_target="tpu_custom_call" | custom-call | flops 1 | bytes 1 | tf_op jit(solution)/shard_map/cond/branch_1_fun/cond/branch_1_fun/join/pallas_call | solution.py:722
  39.9 2.1 %add_back.1 = (f32[1,128,2048]{2,1,0:T(8,128)}, f32[1,128,2048]{2,1,0:T(8,128)}, f32[1,128,2048]{2,1,0:T(8,128)}) custom-call(bf16[2,2,128,512]{3,2,1,0:T(8,128)(2,1)} %get-tuple-element.137.waiting, bf16[2,128,512]{2,1,0:T(8,128)(2,1)S(1)} %collective-permute-done.9.straight, ...), custom_call_target="tpu_custom_call", output_to_operand_aliasing={{0}: (3, {}), {1}: (4, {}), {2}: (5, {})} | custom-call | flops 1 | bytes 1 | tf_op jit(solution)/shard_map/add_back/pallas_call | solution.py:769
  (25 shorter events, 3.1 us)
Async XLA Ops:
  0.6 5.9 %copy-start.1 = (s32[1,128]{1,0:T(1,128)S(1)}, s32[1,128]{1,0:T(1,128)}, u32[]{:S(2)}) copy-start(s32[1,128]{1,0:T(1,128)} %pos_ref.2) | copy-start | bytes 1540
  2.0 6.6 %copy-start = (bf16[1,128,4096]{2,1,0:T(8,128)(2,1)S(1)}, bf16[1,128,4096]{2,1,0:T(8,128)(2,1)}, u32[]{:S(2)}) copy-start(bf16[1,128,4096]{2,1,0:T(8,128)(2,1)} %x_ref.1) | copy-start | bytes 3145732
  2.0 16.3 %collective-permute-start.6 = (bf16[2,128,512]{2,1,0:T(8,128)(2,1)S(1)}, bf16[2,128,512]{2,1,0:T(8,128)(2,1)S(1)}, u32[]{:S(2)}, u32[]{:S(2)}) collective-permute-start(bf16[2,128,512]{2,1,0:T(8,128)(2,1)S(1)} %get-tuple-element.119), channel_id=1, source_target_pairs={{0,3},{1,2},{2,1},{3,0},{4,7},{5,6},{6,5},{7,4},{8,11},{9,10},{10,... | collective-permute-start | bytes 786440 | tf_op jit(solution)/shard_map/ppermute | solution.py:818
  4.4 13.9 %collective-permute-start.5 = (bf16[2,128,512]{2,1,0:T(8,128)(2,1)S(1)}, bf16[2,128,512]{2,1,0:T(8,128)(2,1)S(1)}, u32[]{:S(2)}, u32[]{:S(2)}) collective-permute-start(bf16[2,128,512]{2,1,0:T(8,128)(2,1)S(1)} %get-tuple-element.110), channel_id=1, source_target_pairs={{0,2},{1,3},{2,0},{3,1},{4,6},{5,7},{6,4},{7,5},{8,10},{9,11},{10,... | collective-permute-start | bytes 786440 | tf_op jit(solution)/shard_map/ppermute | solution.py:818
  5.0 3.6 %collective-permute-start.4 = (f32[1,512]{1,0:T(1,128)S(1)}, f32[1,512]{1,0:T(1,128)S(1)}, u32[]{:S(2)}, u32[]{:S(2)}) collective-permute-start(f32[1,512]{1,0:T(1,128)S(1)} %get-tuple-element.112), channel_id=1, source_target_pairs={{0,4},{4,0},{8,12},{12,8},{16,20},{20,16},{24,28},{28,24},{1,5},{5... | collective-permute-start | bytes 6152 | tf_op jit(solution)/shard_map/ppermute | solution.py:830
  8.7 4.2 %collective-permute-start.1 = (bf16[4,128,1024]{2,1,0:T(8,128)(2,1)S(1)}, bf16[4,128,1024]{2,1,0:T(8,128)(2,1)}, u32[]{:S(2)}, u32[]{:S(2)}) collective-permute-start(bf16[4,128,1024]{2,1,0:T(8,128)(2,1)S(1)} %get-tuple-element.42), channel_id=1, source_target_pairs={{0,1},{1,0},{2,3},{3,2},{4,5},{5,4},{6,7},{7,6},{8,9},{9,8},{10,11... | collective-permute-start | bytes 3145736 | tf_op jit(solution)/shard_map/cond/branch_1_fun/ppermute | solution.py:818
  8.7 4.3 %collective-permute-start.2 = (bf16[1,128,4096]{2,1,0:T(8,128)(2,1)S(1)}, bf16[1,128,4096]{2,1,0:T(8,128)(2,1)}, u32[]{:S(2)}, u32[]{:S(2)}) collective-permute-start(bf16[1,128,4096]{2,1,0:T(8,128)(2,1)S(1)} %get-tuple-element.43), channel_id=1, source_target_pairs={{0,1},{1,0},{2,3},{3,2},{4,5},{5,4},{6,7},{7,6},{8,9},{9,8},{10,11... | collective-permute-start | bytes 3145736 | tf_op jit(solution)/shard_map/cond/branch_1_fun/ppermute | solution.py:818
  9.2 3.6 %collective-permute-start.3 = (f32[1,1024]{1,0:T(1,128)S(1)}, f32[1,1024]{1,0:T(1,128)S(1)}, u32[]{:S(2)}, u32[]{:S(2)}) collective-permute-start(f32[1,1024]{1,0:T(1,128)S(1)} %get-tuple-element.44), channel_id=1, source_target_pairs={{0,8},{4,12},{8,0},{12,4},{16,24},{20,28},{24,16},{28,20},{1,9},{5... | collective-permute-start | bytes 12296 | tf_op jit(solution)/shard_map/cond/branch_1_fun/ppermute | solution.py:830
  13.0 6.1 %collective-permute-start.7 = (f32[1,2048]{1,0:T(1,128)S(1)}, f32[1,2048]{1,0:T(1,128)S(1)}, u32[]{:S(2)}, u32[]{:S(2)}) collective-permute-start(f32[1,2048]{1,0:T(1,128)S(1)} %get-tuple-element.125), channel_id=1, source_target_pairs={{0,16},{4,20},{8,24},{12,28},{16,0},{20,4},{24,8},{28,12},{1,17},{... | collective-permute-start | bytes 24584 | tf_op jit(solution)/shard_map/ppermute | solution.py:830
  19.9 3.8 %collective-permute-start.8 = (f32[4,4,256]{2,1,0:T(4,128)S(1)}, f32[4,4,256]{2,1,0:T(4,128)S(1)}, u32[]{:S(2)}, u32[]{:S(2)}) collective-permute-start(f32[4,4,256]{2,1,0:T(4,128)S(1)} %get-tuple-element.127), channel_id=1, source_target_pairs={{0,2},{1,3},{2,0},{3,1},{4,6},{5,7},{6,4},{7,5},{8,10},{9,11},{10,... | collective-permute-start | bytes 49160 | tf_op jit(solution)/shard_map/ppermute | solution.py:818
  24.4 15.5 %collective-permute-start.9 = (bf16[2,128,512]{2,1,0:T(8,128)(2,1)S(1)}, bf16[2,128,512]{2,1,0:T(8,128)(2,1)S(1)}, u32[]{:S(2)}, u32[]{:S(2)}) collective-permute-start(bf16[2,128,512]{2,1,0:T(8,128)(2,1)S(1)} %get-tuple-element.138), channel_id=1, source_target_pairs={{0,2},{1,3},{2,0},{3,1},{4,6},{5,7},{6,4},{7,5},{8,10},{9,11},{10,... | collective-permute-start | bytes 786440 | tf_op jit(solution)/shard_map/ppermute | solution.py:818
  25.8 14.1 %collective-permute-start.10 = (bf16[2,128,512]{2,1,0:T(8,128)(2,1)S(1)}, bf16[2,128,512]{2,1,0:T(8,128)(2,1)S(1)}, u32[]{:S(2)}, u32[]{:S(2)}) collective-permute-start(bf16[2,128,512]{2,1,0:T(8,128)(2,1)S(1)} %get-tuple-element.139), channel_id=1, source_target_pairs={{0,3},{1,2},{2,1},{3,0},{4,7},{5,6},{6,5},{7,4},{8,11},{9,10},{10,... | collective-permute-start | bytes 786440 | tf_op jit(solution)/shard_map/ppermute | solution.py:818
  26.9 12.9 %all-to-all-start = ((f32[32,1,512]{2,1,0:T(1,128)}), f32[32,1,512]{2,1,0:T(1,128)S(1)}, u32[]{:S(2)}, u32[]{:S(2)}) async-start(f32[32,1,512]{2,1,0:T(1,128)} %bitcast.1), calls=%async_computation | async-start | bytes 131072 | tf_op jit(solution)/shard_map/cond/branch_1_fun/all_to_all | solution.py:847
  34.2 2.4 %collective-permute-start = (bf16[3,128,1024]{2,1,0:T(8,128)(2,1)S(1)}, bf16[3,128,1024]{2,1,0:T(8,128)(2,1)S(1)}, u32[]{:S(2)}, u32[]{:S(2)}) collective-permute-start(bf16[3,128,1024]{2,1,0:T(8,128)(2,1)S(1)} %get-tuple-element.54), channel_id=1, source_target_pairs={{0,1},{1,0},{2,3},{3,2},{4,5},{5,4},{6,7},{7,6},{8,9},{9,8},{10,11... | collective-permute-start | bytes 2359304 | tf_op jit(solution)/shard_map/cond/branch_1_fun/cond/branch_1_fun/ppermute | solution.py:818
  39.9 2.2 %copy-start.2 = (f32[512]{0:T(512)}, f32[512]{0:T(512)S(1)}, u32[]{:S(2)}) copy-start(f32[512]{0:T(512)S(1)} %get-tuple-element.109) | copy-start | bytes 6148

commit v12 on v10

--- a/solution.py
+++ b/solution.py
@@ -708,8 +708,8 @@
             total[i, j] = low[i, j].astype(F32)
             stores.append(pltpu.make_async_copy(total.at[i, j], out.at[0, :, cols], out_sems.at[3 * i + j]))
             stores[-1].start()
-        waiting[i, 0] = jnp.where(chip == 0, total[i, 1, :, :width], total[i, 0, :, width:])
-        waiting[i, 1] = total[i, 2, :, :width]
+        waiting[i, 0] = jnp.where(chip == 0, total[i, 1, :, :width], total[i, 0, :, width:]).astype(BF16)
+        waiting[i, 1] = low[i, 2, :, :width]
     for c in stores:
         c.wait()
 
@@ -721,7 +721,7 @@
     hbm = pl.BlockSpec(memory_space=pltpu.HBM)
     return pl.pallas_call(
         join_kernel,
-        out_shape=[out] * 3 + [pltpu.VMEM((2, 2, slots, half // 2), F32)],
+        out_shape=[out] * 3 + [pltpu.VMEM((2, 2, slots, half // 2), BF16)],
         in_specs=[anywhere] * 2,
         out_specs=[hbm] * 3 + [VMEM],
         scratch_shapes=[
@@ -749,7 +749,7 @@
 
     for i, (back, _) in enumerate(ends):
         for j in range(2):
-            total[i, j] = waiting[i, j] + back[j].astype(F32)
+            total[i, j] = waiting[i, j].astype(F32) + back[j].astype(F32)
 
     @pl.when(chip == 0)
     def _():
@@ -801,7 +801,7 @@
     chunk = rows_x.shape[-1] // parts
     return pl.pallas_call(
         pair_router_kernel,
-        out_shape=jax.ShapeDtypeStruct((parts, copies, 1, chunk), F32),
+        out_shape=pltpu.VMEM((parts, copies, 1, chunk), F32),
         in_specs=[VMEM] * 3,
         out_specs=VMEM,
         compiler_params=params(),
@@ -843,7 +843,7 @@
         sib_in = send(sib_out, 1)
         shared = lax.all_to_all(after(terms, own_out).reshape(ndp * n, 1, -1), ("dp", "ctx"), 0, 0, tiled=True)
         *outs, waiting = join(own_out, sib_in, queries.shape)
-        return outs, waiting, jnp.sum(shared, axis=0)[0] / float(ndp * n * slots // 2)
+        return outs, waiting, jnp.sum(after(shared, waiting), axis=0)[0] / float(ndp * n * slots // 2)
 
     out_s, out_d, w_part = cross_pack(route_pos, w_router, keys, values, queries, d_gated)
     in_s, in_d = send(out_s, 2), send(out_d, 3)

time: 46.3 us -> 45.9 us (level)
  blocking collectives: 12.4 us -> 0 us
  waiting for transfers between devices: 3.59 us -> 9.07 us
  starting transfers between devices: 13 us -> 18.1 us
  Pallas kernels: 16.1 us -> 17.5 us
    all_to_all x1 -> x0, blocking collectives: 12.4 us -> none  [tail_phase(): lax.all_to_all(after(terms, own_out).reshape(ndp * n, 1, -1), ('dp', 'ctx...]
    all_to_all x0 -> x1, waiting for transfers between devices: none -> 5.47 us  [tail_phase(): lax.all_to_all(after(terms, own_out).reshape(ndp * n, 1, -1), ('dp', 'ctx...]
    all_to_all x0 -> x1, starting transfers between devices: none -> 5.18 us  [tail_phase(): lax.all_to_all(after(terms, own_out).reshape(ndp * n, 1, -1), ('dp', 'ctx...]
    pallas_call x1, Pallas kernels: 1.72 us -> 2.56 us  [far_grad(): pl.pallas_call(functools.partial(far_grad_kernel, HEAD ** (-0.5)), out_sh...]
    pallas_call x1, Pallas kernels: 0.4 us -> 1.04 us  [pair_router(): pl.pallas_call(pair_router_kernel, out_shape=pltpu.VMEM((parts, copies, 1...]
  transfers between devices with their start and end apart: 11 -> 12, of which waited for: 4 -> 5; matrix products, arithmetic and copies ran while one was open for 0% -> 0% of each run, Pallas kernels for 23% -> 26%
where the time goes in v12:
time: 45.9 us; the launch traced here: 45.7 us
  starting transfers between devices  18.1 us (39%)
  Pallas kernels  17.5 us (38%)
  waiting for transfers between devices  9.07 us (20%)
  between operations  0.8 us (2%)
    ppermute x8, starting transfers between devices, send(): return lax.ppermute(a, 'ctx', [(i, i ^ flip) for i in range(n)])  7.21 us
    ppermute x3, starting transfers between devices, widen(): other = lax.ppermute(part, 'dp', [(i, i ^ step) for i in range(ndp)])  5.68 us
    all_to_all x1, waiting for transfers between devices, tail_phase(): lax.all_to_all(after(terms, own_out).reshape(ndp * n, 1, -1), ('dp', 'ctx...  5.47 us
    all_to_all x1, starting transfers between devices, tail_phase(): lax.all_to_all(after(terms, own_out).reshape(ndp * n, 1, -1), ('dp', 'ctx...  5.18 us
    ppermute x3, waiting for transfers between devices, widen(): other = lax.ppermute(part, 'dp', [(i, i ^ step) for i in range(ndp)])  2.74 us
    pallas_call x1, Pallas kernels, local_stats(): pl.pallas_call(functools.partial(local_stats_kernel, HEAD ** (-0.5)), out...  2.71 us
    pallas_call x1, Pallas kernels, far_grad(): pl.pallas_call(functools.partial(far_grad_kernel, HEAD ** (-0.5)), out_sh...  2.56 us
    pallas_call x1, Pallas kernels, add_back(): pl.pallas_call(add_back_kernel, out_shape=[pltpu.HBM(o.shape, F32) for o...  2.05 us
  transfers between devices with their start and end apart: 12, of which 5 were waited for; matrix products, arithmetic and copies ran while one was open for 0% of the time, Pallas kernels for 26%

profile of v12, /device:TPU:0, one launch (start us, length us, event | category | flops | bytes accessed | tf_op | source)
XLA Modules:
  0.0 45.7 jit_solution(11834548488441408388)
XLA Ops:
  0.6 1.3 %cross_pack.1 = (bf16[2,128,512]{2,1,0:T(8,128)(2,1)S(1)}, bf16[2,128,512]{2,1,0:T(8,128)(2,1)S(1)}, f32[1,512]{1,0:T(1,128)S(1)}) custom-call(s32[1,128]{1,0:T(1,128)} %pos_ref.2, bf16[512]{0:T(512)(128)(2,1)} %w_any.1, bf16[1,128,2048]{2,1,0:T(8,128)(2,1)} %k_ref.5, bf16[1,128,2048]{2,1,0:T(8,128)(2,1)} %v_ref.5, bf16[1,128,2048]{2,1,0:T(8,128)(2,1)} %q_ref.5, ...), custom_call_target="tpu_custom_call" | custom-call | flops 1 | bytes 1 | tf_op jit(solution)/shard_map/cross_pack/pallas_call | solution.py:314
  2.0 2.4 %collective-permute-start.6 = (bf16[2,128,512]{2,1,0:T(8,128)(2,1)S(1)}, bf16[2,128,512]{2,1,0:T(8,128)(2,1)S(1)}, u32[]{:S(2)}, u32[]{:S(2)}) collective-permute-start(bf16[2,128,512]{2,1,0:T(8,128)(2,1)S(1)} %get-tuple-element.94), channel_id=1, source_target_pairs={{0,3},{1,2},{2,1},{3,0},{4,7},{5,6},{6,5},{7,4},{8,11},{9,10},{10,... | collective-permute-start | bytes 786440 | tf_op jit(solution)/shard_map/ppermute | solution.py:818
  5.0 1.5 %collective-permute-start.4 = (f32[1,512]{1,0:T(1,128)S(1)}, f32[1,512]{1,0:T(1,128)S(1)}, u32[]{:S(2)}, u32[]{:S(2)}) collective-permute-start(f32[1,512]{1,0:T(1,128)S(1)} %get-tuple-element.87), channel_id=1, source_target_pairs={{0,4},{4,0},{8,12},{12,8},{16,20},{20,16},{24,28},{28,24},{1,5},{5... | collective-permute-start | bytes 6152 | tf_op jit(solution)/shard_map/ppermute | solution.py:830
  6.6 1.3 %sib_pack.1 = bf16[4,128,1024]{2,1,0:T(8,128)(2,1)S(1)} custom-call(s32[1,128]{1,0:T(1,128)S(1)} %copy-done, bf16[1,128,2048]{2,1,0:T(8,128)(2,1)} %k_ref.5, bf16[1,128,2048]{2,1,0:T(8,128)(2,1)} %v_ref.5, bf16[1,128,2048]{2,1,0:T(8,128)(2,1)} %q_ref.5, f32[1,128,2048]{2,1,0:T(8,128)} %dg_ref.5), custom_call_target="tpu_custom_call" | custom-call | flops 1 | bytes 1 | tf_op jit(solution)/shard_map/sib_pack/pallas_call | solution.py:350
  7.9 0.7 %collective-permute-done.4 = f32[1,512]{1,0:T(1,128)S(1)} collective-permute-done((f32[1,512]{1,0:T(1,128)S(1)}, f32[1,512]{1,0:T(1,128)S(1)}, u32[]{:S(2)}, u32[]{:S(2)}) %collective-permute-start.4) | collective-permute-done | bytes 2080 | tf_op jit(solution)/shard_map/ppermute | solution.py:830
  8.6 4.4 %conditional.2 = (bf16[4,128,1024]{2,1,0:T(8,128)(2,1)}, bf16[1,128,4096]{2,1,0:T(8,128)(2,1)}, f32[1,2048]{1,0:T(1,128)S(1)}) conditional(s32[]{:T(128)} %bitcast.1, () %tuple.30, (bf16[4,128,1024]{2,1,0:T(8,128)(2,1)S(1)}, bf16[1,128,4096]{2,1,0:T(8,128)(2,1)S(1)}, f32[1,1024]{1,0:T(1,128)S(1)}) %tuple.41), branch_computations={%region_0.0_spmd, %region_1.0_spmd} | conditional | flops 2048 | bytes 8421520 | solution.py:824
  9.2 1.6 %collective-permute-start.2 = (f32[1,1024]{1,0:T(1,128)S(1)}, f32[1,1024]{1,0:T(1,128)S(1)}, u32[]{:S(2)}, u32[]{:S(2)}) collective-permute-start(f32[1,1024]{1,0:T(1,128)S(1)} %get-tuple-element.26), channel_id=1, source_target_pairs={{0,8},{4,12},{8,0},{12,4},{16,24},{20,28},{24,16},{28,20},{1,9},{5... | collective-permute-start | bytes 12296 | tf_op jit(solution)/shard_map/cond/branch_1_fun/ppermute | solution.py:830
  10.8 2.0 %collective-permute-done.2 = f32[1,1024]{1,0:T(1,128)S(1)} collective-permute-done((f32[1,1024]{1,0:T(1,128)S(1)}, f32[1,1024]{1,0:T(1,128)S(1)}, u32[]{:S(2)}, u32[]{:S(2)}) %collective-permute-start.2) | collective-permute-done | bytes 4128 | tf_op jit(solution)/shard_map/cond/branch_1_fun/ppermute | solution.py:830
  13.0 2.6 %collective-permute-start.7 = (f32[1,2048]{1,0:T(1,128)S(1)}, f32[1,2048]{1,0:T(1,128)S(1)}, u32[]{:S(2)}, u32[]{:S(2)}) collective-permute-start(f32[1,2048]{1,0:T(1,128)S(1)} %get-tuple-element.100), channel_id=1, source_target_pairs={{0,16},{4,20},{8,24},{12,28},{16,0},{20,4},{24,8},{28,12},{1,17},{... | collective-permute-start | bytes 24584 | tf_op jit(solution)/shard_map/ppermute | solution.py:830
  15.6 2.7 %local_stats.1 = (f32[3,8,256]{2,1,0:T(8,128)S(1)}, f32[1,256]{1,0:T(1,128)S(1)}, bf16[4,256,512]{2,1,0:T(8,128)(2,1)S(1)}, bf16[4,256,512]{2,1,0:T(8,128)(2,1)S(1)}, bf16[2,128,4096]{2,1,0:T(8,128)(2,1)S(1)}) custom-call(s32[1,128]{1,0:T(1,128)S(1)} %copy-done, bf16[1,128,2048]{2,1,0:T(8,128)(2,1)} %k_ref.5, bf16[1,128,2048]{2,1,0:T(8,128)(2,1)} %v_ref.5, ...), custom_call_target="tpu_custom_call" | custom-call | flops 1 | bytes 1 | tf_op jit(solution)/shard_map/local_stats/pallas_call | solution.py:476
  18.3 0.8 %cross_stats.1 = (bf16[4,256,512]{2,1,0:T(8,128)(2,1)S(1)}, f32[3,4,256]{2,1,0:T(4,128)S(1)}, bf16[2,4,256,256]{3,2,1,0:T(8,128)(2,1)S(1)}) custom-call(bf16[4,256,512]{2,1,0:T(8,128)(2,1)S(1)} %get-tuple-element.93.near.pair, bf16[4,256,512]{2,1,0:T(8,128)(2,1)S(1)} %get-tuple-element.91.far, bf16[2,128,512]{2,1,0:T(8,128)(2,1)S(1)} %collective-permute-done.5.straight, ...), custom_call_target="tpu_custom_call" | custom-call | flops 1 | bytes 1 | tf_op jit(solution)/shard_map/cross_stats/pallas_call | solution.py:525
  19.9 1.5 %collective-permute-start.8 = (f32[4,4,256]{2,1,0:T(4,128)S(1)}, f32[4,4,256]{2,1,0:T(4,128)S(1)}, u32[]{:S(2)}, u32[]{:S(2)}) collective-permute-start(f32[4,4,256]{2,1,0:T(4,128)S(1)} %get-tuple-element.102), channel_id=1, source_target_pairs={{0,2},{1,3},{2,0},{3,1},{4,6},{5,7},{6,4},{7,5},{8,10},{9,11},{10,... | collective-permute-start | bytes 49160 | tf_op jit(solution)/shard_map/ppermute | solution.py:818
  21.3 1.6 %near_grad.1 = (f32[256,512]{1,0:T(8,128)S(1)}, bf16[2,128,512]{2,1,0:T(8,128)(2,1)S(1)}, bf16[2,128,512]{2,1,0:T(8,128)(2,1)S(1)}, f32[1,256]{1,0:T(1,128)S(1)}) custom-call(bf16[4,256,512]{2,1,0:T(8,128)(2,1)S(1)} %get-tuple-element.93.near.pair, f32[3,8,256]{2,1,0:T(8,128)S(1)} %get-tuple-element.92.local, f32[3,4,256]{2,1,0:T(4,128)S(1)} %get-tuple-element.97.stats, ...), custom_call_target="tpu_custom_call" | custom-call | flops 1 | bytes 1 | tf_op jit(solution)/shard_map/near_grad/pallas_call | solution.py:590
  23.0 0.7 %collective-permute-done.8.heard = f32[4,4,256]{2,1,0:T(4,128)S(1)} collective-permute-done((f32[4,4,256]{2,1,0:T(4,128)S(1)}, f32[4,4,256]{2,1,0:T(4,128)S(1)}, u32[]{:S(2)}, u32[]{:S(2)}) %collective-permute-start.8) | collective-permute-done | bytes 16416 | tf_op jit(solution)/shard_map/ppermute | solution.py:818
  23.7 1.5 %cross_grad.1 = (bf16[2,128,512]{2,1,0:T(8,128)(2,1)}, bf16[2,128,512]{2,1,0:T(8,128)(2,1)}, bf16[256,512]{1,0:T(8,128)(2,1)S(1)}, bf16[2,256,512]{2,1,0:T(8,128...) custom-call(bf16[4,256,512]{2,1,0:T(8,128)(2,1)S(1)} %get-tuple-element.95.cross, ...), custom_call_target="tpu_custom_call" | custom-call | flops 1 | bytes 1 | tf_op jit(solution)/shard_map/cross_grad/pallas_call | solution.py:635
  25.1 1.4 %collective-permute-start.9 = (bf16[2,128,512]{2,1,0:T(8,128)(2,1)}, bf16[2,128,512]{2,1,0:T(8,128)(2,1)S(1)}, u32[]{:S(2)}, u32[]{:S(2)}) collective-permute-start(bf16[2,128,512]{2,1,0:T(8,128)(2,1)} %get-tuple-element.113), channel_id=1, source_target_pairs={{0,2},{1,3},{2,0},{3,1},{4,6},{5,7},{6,4},{7,5},{8,10},{9,11},{10,... | collective-permute-start | bytes 786440 | tf_op jit(solution)/shard_map/ppermute | solution.py:818
  26.5 1.0 %router_terms.1 = f32[8,4,1,512]{3,2,1,0:T(1,128)} custom-call(f32[1,256]{1,0:T(1,128)S(1)} %get-tuple-element.103.gates.gates_ref, f32[1,256]{1,0:T(1,128)S(1)} %get-tuple-element.111.sum_ref, bf16[2,128,4096]{2,1,0:T(8,128)(2,1)S(1)} %get-tuple-element.99.rows_x), custom_call_target="tpu_custom_call" | custom-call | flops 1 | bytes 1 | tf_op jit(solution)/shard_map/router_terms/pallas_call | solution.py:802
  27.6 16.0 %conditional.3 = (f32[1,128,2048]{2,1,0:T(8,128)}, f32[1,128,2048]{2,1,0:T(8,128)}, f32[1,128,2048]{2,1,0:T(8,128)}, bf16[2,2,128,512]{3,2,1,0:T(8,128)(2,1)S(1)}, f32[512]{0:T(512)S(1)}) conditional(s32[]{:T(128)} %bitcast.1, () %tuple.29, (bf16[4,256,512]{2,1,0:T(8,128)(2,1)S(1)}, f32[3,8,256]{2,1,0:T(8,128)S(1)}, f32[2,4,256]{2,1,0:T(4,128)S(1)}, ...), branch_computations={%region_2.0_spmd, %region_3.0_spmd} | conditional | flops 16386 | bytes 3672122 | solution.py:824
  27.6 2.6 %far_grad.1 = (bf16[3,128,1024]{2,1,0:T(8,128)(2,1)S(1)}, bf16[3,128,1024]{2,1,0:T(8,128)(2,1)}) custom-call(bf16[4,256,512]{2,1,0:T(8,128)(2,1)S(1)} %get-tuple-element.27.pair, f32[3,8,256]{2,1,0:T(8,128)S(1)} %get-tuple-element.28.local, f32[2,4,256]{2,1,0:T(4,128)S(1)} %get-tuple-element.29.final, f32[1,256]{1,0:T(1,128)S(1)} %get-tuple-element.30.gates, ...), custom_call_target="tpu_custom_call" | custom-call | flops 1 | bytes 1 | tf_op jit(solution)/shard_map/cond/branch_1_fun/far_grad/pallas_call | solution.py:681
  30.2 0.7 %collective-permute-start.3 = (bf16[3,128,1024]{2,1,0:T(8,128)(2,1)}, bf16[3,128,1024]{2,1,0:T(8,128)(2,1)S(1)}, u32[]{:S(2)}, u32[]{:S(2)}) collective-permute-start(bf16[3,128,1024]{2,1,0:T(8,128)(2,1)} %get-tuple-element.36), channel_id=1, source_target_pairs={{0,1},{1,0},{2,3},{3,2},{4,5},{5,4},{6,7},{7,6},{8,9},{9,8},{10,11... | collective-permute-start | bytes 2359304 | tf_op jit(solution)/shard_map/cond/branch_1_fun/ppermute | solution.py:818
  30.9 5.2 %all-to-all-start = ((f32[32,1,512]{2,1,0:T(1,128)}), f32[32,1,512]{2,1,0:T(1,128)S(1)}, u32[]{:S(2)}, u32[]{:S(2)}) async-start(f32[32,1,512]{2,1,0:T(1,128)} %bitcast), calls=%async_computation | async-start | bytes 131072 | tf_op jit(solution)/shard_map/cond/branch_1_fun/all_to_all | solution.py:844
  36.1 1.9 %join.1 = (f32[1,128,2048]{2,1,0:T(8,128)}, f32[1,128,2048]{2,1,0:T(8,128)}, f32[1,128,2048]{2,1,0:T(8,128)}, bf16[2,2,128,512]{3,2,1,0:T(8,128)(2,1)S(1)}) custom-call(bf16[3,128,1024]{2,1,0:T(8,128)(2,1)S(1)} %get-tuple-element.35.own, bf16[3,128,1024]{2,1,0:T(8,128)(2,1)S(1)} %collective-permute-done.3.sib), custom_call_target="tpu_custom_call" | custom-call | flops 1 | bytes 1 | tf_op jit(solution)/shard_map/cond/branch_1_fun/join/pallas_call | solution.py:722
  38.0 5.5 %all-to-all-done = f32[32,1,512]{2,1,0:T(1,128)S(1)} async-done(((f32[32,1,512]{2,1,0:T(1,128)}), f32[32,1,512]{2,1,0:T(1,128)S(1)}, u32[]{:S(2)}, u32[]{:S(2)}) %all-to-all-start) | async-done | bytes 65568 | tf_op jit(solution)/shard_map/cond/branch_1_fun/all_to_all | solution.py:844
  43.6 2.1 %add_back.1 = (f32[1,128,2048]{2,1,0:T(8,128)}, f32[1,128,2048]{2,1,0:T(8,128)}, f32[1,128,2048]{2,1,0:T(8,128)}) custom-call(bf16[2,2,128,512]{3,2,1,0:T(8,128)(2,1)S(1)} %get-tuple-element.112.waiting, bf16[2,128,512]{2,1,0:T(8,128)(2,1)S(1)} %collective-permute-done.9.straight, ...), custom_call_target="tpu_custom_call", output_to_operand_aliasing={{0}: (3, {}), {1}: (4, {}), {2}: (5, {})} | custom-call | flops 1 | bytes 1 | tf_op jit(solution)/shard_map/add_back/pallas_call | solution.py:769
  (24 shorter events, 2.2 us)
Async XLA Ops:
  0.6 5.9 %copy-start = (s32[1,128]{1,0:T(1,128)S(1)}, s32[1,128]{1,0:T(1,128)}, u32[]{:S(2)}) copy-start(s32[1,128]{1,0:T(1,128)} %pos_ref.2) | copy-start | bytes 1540
  2.0 6.6 %copy-start.1 = (bf16[1,128,4096]{2,1,0:T(8,128)(2,1)S(1)}, bf16[1,128,4096]{2,1,0:T(8,128)(2,1)}, u32[]{:S(2)}) copy-start(bf16[1,128,4096]{2,1,0:T(8,128)(2,1)} %x_ref.1) | copy-start | bytes 3145732
  2.0 16.3 %collective-permute-start.6 = (bf16[2,128,512]{2,1,0:T(8,128)(2,1)S(1)}, bf16[2,128,512]{2,1,0:T(8,128)(2,1)S(1)}, u32[]{:S(2)}, u32[]{:S(2)}) collective-permute-start(bf16[2,128,512]{2,1,0:T(8,128)(2,1)S(1)} %get-tuple-element.94), channel_id=1, source_target_pairs={{0,3},{1,2},{2,1},{3,0},{4,7},{5,6},{6,5},{7,4},{8,11},{9,10},{10,... | collective-permute-start | bytes 786440 | tf_op jit(solution)/shard_map/ppermute | solution.py:818
  4.4 13.9 %collective-permute-start.5 = (bf16[2,128,512]{2,1,0:T(8,128)(2,1)S(1)}, bf16[2,128,512]{2,1,0:T(8,128)(2,1)S(1)}, u32[]{:S(2)}, u32[]{:S(2)}) collective-permute-start(bf16[2,128,512]{2,1,0:T(8,128)(2,1)S(1)} %get-tuple-element.85), channel_id=1, source_target_pairs={{0,2},{1,3},{2,0},{3,1},{4,6},{5,7},{6,4},{7,5},{8,10},{9,11},{10,... | collective-permute-start | bytes 786440 | tf_op jit(solution)/shard_map/ppermute | solution.py:818
  5.0 3.6 %collective-permute-start.4 = (f32[1,512]{1,0:T(1,128)S(1)}, f32[1,512]{1,0:T(1,128)S(1)}, u32[]{:S(2)}, u32[]{:S(2)}) collective-permute-start(f32[1,512]{1,0:T(1,128)S(1)} %get-tuple-element.87), channel_id=1, source_target_pairs={{0,4},{4,0},{8,12},{12,8},{16,20},{20,16},{24,28},{28,24},{1,5},{5... | collective-permute-start | bytes 6152 | tf_op jit(solution)/shard_map/ppermute | solution.py:830
  8.7 4.2 %collective-permute-start = (bf16[4,128,1024]{2,1,0:T(8,128)(2,1)S(1)}, bf16[4,128,1024]{2,1,0:T(8,128)(2,1)}, u32[]{:S(2)}, u32[]{:S(2)}) collective-permute-start(bf16[4,128,1024]{2,1,0:T(8,128)(2,1)S(1)} %get-tuple-element.24), channel_id=1, source_target_pairs={{0,1},{1,0},{2,3},{3,2},{4,5},{5,4},{6,7},{7,6},{8,9},{9,8},{10,11... | collective-permute-start | bytes 3145736 | tf_op jit(solution)/shard_map/cond/branch_1_fun/ppermute | solution.py:818
  8.7 4.3 %collective-permute-start.1 = (bf16[1,128,4096]{2,1,0:T(8,128)(2,1)S(1)}, bf16[1,128,4096]{2,1,0:T(8,128)(2,1)}, u32[]{:S(2)}, u32[]{:S(2)}) collective-permute-start(bf16[1,128,4096]{2,1,0:T(8,128)(2,1)S(1)} %get-tuple-element.25), channel_id=1, source_target_pairs={{0,1},{1,0},{2,3},{3,2},{4,5},{5,4},{6,7},{7,6},{8,9},{9,8},{10,11... | collective-permute-start | bytes 3145736 | tf_op jit(solution)/shard_map/cond/branch_1_fun/ppermute | solution.py:818
  9.2 3.6 %collective-permute-start.2 = (f32[1,1024]{1,0:T(1,128)S(1)}, f32[1,1024]{1,0:T(1,128)S(1)}, u32[]{:S(2)}, u32[]{:S(2)}) collective-permute-start(f32[1,1024]{1,0:T(1,128)S(1)} %get-tuple-element.26), channel_id=1, source_target_pairs={{0,8},{4,12},{8,0},{12,4},{16,24},{20,28},{24,16},{28,20},{1,9},{5... | collective-permute-start | bytes 12296 | tf_op jit(solution)/shard_map/cond/branch_1_fun/ppermute | solution.py:830
  13.0 6.1 %collective-permute-start.7 = (f32[1,2048]{1,0:T(1,128)S(1)}, f32[1,2048]{1,0:T(1,128)S(1)}, u32[]{:S(2)}, u32[]{:S(2)}) collective-permute-start(f32[1,2048]{1,0:T(1,128)S(1)} %get-tuple-element.100), channel_id=1, source_target_pairs={{0,16},{4,20},{8,24},{12,28},{16,0},{20,4},{24,8},{28,12},{1,17},{... | collective-permute-start | bytes 24584 | tf_op jit(solution)/shard_map/ppermute | solution.py:830
  19.9 3.8 %collective-permute-start.8 = (f32[4,4,256]{2,1,0:T(4,128)S(1)}, f32[4,4,256]{2,1,0:T(4,128)S(1)}, u32[]{:S(2)}, u32[]{:S(2)}) collective-permute-start(f32[4,4,256]{2,1,0:T(4,128)S(1)} %get-tuple-element.102), channel_id=1, source_target_pairs={{0,2},{1,3},{2,0},{3,1},{4,6},{5,7},{6,4},{7,5},{8,10},{9,11},{10,... | collective-permute-start | bytes 49160 | tf_op jit(solution)/shard_map/ppermute | solution.py:818
  25.1 18.4 %collective-permute-start.9 = (bf16[2,128,512]{2,1,0:T(8,128)(2,1)}, bf16[2,128,512]{2,1,0:T(8,128)(2,1)S(1)}, u32[]{:S(2)}, u32[]{:S(2)}) collective-permute-start(bf16[2,128,512]{2,1,0:T(8,128)(2,1)} %get-tuple-element.113), channel_id=1, source_target_pairs={{0,2},{1,3},{2,0},{3,1},{4,6},{5,7},{6,4},{7,5},{8,10},{9,11},{10,... | collective-permute-start | bytes 786440 | tf_op jit(solution)/shard_map/ppermute | solution.py:818
  26.5 17.1 %collective-permute-start.10 = (bf16[2,128,512]{2,1,0:T(8,128)(2,1)}, bf16[2,128,512]{2,1,0:T(8,128)(2,1)}, u32[]{:S(2)}, u32[]{:S(2)}) collective-permute-start(bf16[2,128,512]{2,1,0:T(8,128)(2,1)} %get-tuple-element.114), channel_id=1, source_target_pairs={{0,3},{1,2},{2,1},{3,0},{4,7},{5,6},{6,5},{7,4},{8,11},{9,10},{10,... | collective-permute-start | bytes 786440 | tf_op jit(solution)/shard_map/ppermute | solution.py:818
  30.2 5.9 %collective-permute-start.3 = (bf16[3,128,1024]{2,1,0:T(8,128)(2,1)}, bf16[3,128,1024]{2,1,0:T(8,128)(2,1)S(1)}, u32[]{:S(2)}, u32[]{:S(2)}) collective-permute-start(bf16[3,128,1024]{2,1,0:T(8,128)(2,1)} %get-tuple-element.36), channel_id=1, source_target_pairs={{0,1},{1,0},{2,3},{3,2},{4,5},{5,4},{6,7},{7,6},{8,9},{9,8},{10,11... | collective-permute-start | bytes 2359304 | tf_op jit(solution)/shard_map/cond/branch_1_fun/ppermute | solution.py:818
  30.9 12.6 %all-to-all-start = ((f32[32,1,512]{2,1,0:T(1,128)}), f32[32,1,512]{2,1,0:T(1,128)S(1)}, u32[]{:S(2)}, u32[]{:S(2)}) async-start(f32[32,1,512]{2,1,0:T(1,128)} %bitcast), calls=%async_computation | async-start | bytes 131072 | tf_op jit(solution)/shard_map/cond/branch_1_fun/all_to_all | solution.py:844
  43.6 2.1 %copy-start.2 = (f32[512]{0:T(512)}, f32[512]{0:T(512)S(1)}, u32[]{:S(2)}) copy-start(f32[512]{0:T(512)S(1)} %get-tuple-element.84) | copy-start | bytes 6148

commit v13 on v11

--- a/solution.py
+++ b/solution.py
@@ -689,94 +689,106 @@
     )(pair, local, final, gates, keep, near_dq, near_own, near_sib)
 
 
-def join_kernel(own, sib, dq_out, dk_out, dv_out, waiting, low, total, in_sems, out_sems):
+def own_join_kernel(own, dq_out, dk_out, dv_out, waiting, total, sems):
     slots, half = own.shape[1], own.shape[2]
     width = half // 2
     core, chip = here()
-    ends = ((own, core * half), (sib, (1 - core) * half))
-    loads = [
-        [pltpu.make_async_copy(part.at[j], low.at[i, j], in_sems.at[3 * i + j]) for j in range(3)]
-        for i, (part, _) in enumerate(ends)
-    ]
-    for c in loads[0] + loads[1]:
-        c.start()
+    cols = pl.ds(pl.multiple_of(core * half, HEAD), half)
     stores = []
-    for i, (_, start) in enumerate(ends):
-        cols = pl.ds(pl.multiple_of(start, HEAD), half)
-        for j, out in enumerate((dq_out, dk_out, dv_out)):
-            loads[i][j].wait()
-            total[i, j] = low[i, j].astype(F32)
-            stores.append(pltpu.make_async_copy(total.at[i, j], out.at[0, :, cols], out_sems.at[3 * i + j]))
-            stores[-1].start()
-        waiting[i, 0] = jnp.where(chip == 0, total[i, 1, :, :width], total[i, 0, :, width:]).astype(BF16)
-        waiting[i, 1] = low[i, 2, :, :width]
+    for j, out in enumerate((dq_out, dk_out, dv_out)):
+        total[j] = own[j].astype(F32)
+        stores.append(pltpu.make_async_copy(total.at[j], out.at[0, :, cols], sems.at[j]))
+        stores[-1].start()
+    waiting[0] = jnp.where(chip == 0, total[1, :, :width], total[0, :, width:]).astype(BF16)
+    waiting[1] = own[2, :, :width]
     for c in stores:
         c.wait()
 
 
-def join(own, sib, shape):
+def own_join(own, shape):
     out = pltpu.HBM(shape, F32)
     _, slots, half = own.shape
-    anywhere = pl.BlockSpec(memory_space=pl.ANY)
     hbm = pl.BlockSpec(memory_space=pltpu.HBM)
     return pl.pallas_call(
-        join_kernel,
-        out_shape=[out] * 3 + [pltpu.VMEM((2, 2, slots, half // 2), BF16)],
-        in_specs=[anywhere] * 2,
+        own_join_kernel,
+        out_shape=[out] * 3 + [jax.ShapeDtypeStruct((2, slots, half // 2), BF16)],
+        in_specs=[VMEM],
         out_specs=[hbm] * 3 + [VMEM],
-        scratch_shapes=[
-            pltpu.VMEM((2, 3, slots, half), BF16),
-            pltpu.VMEM((2, 3, slots, half), F32),
-            pltpu.SemaphoreType.DMA((6,)),
-            pltpu.SemaphoreType.DMA((6,)),
-        ],
-        compiler_params=params(),
-        cost_estimate=cost(0, 72 * own.size),
-        name="join",
-    )(own, sib)
-
-
-def add_back_kernel(waiting, straight, diag, dq_in, dk_in, dv_in, dq_out, dk_out, dv_out, total, sems):
-    width = straight.shape[2]
+        scratch_shapes=[pltpu.VMEM((3, slots, half), F32), pltpu.SemaphoreType.DMA((3,))],
+        compiler_params=params(),
+        cost_estimate=cost(0, 18 * own.size),
+        name="own_join",
+    )(own)
+
+
+def finish_kernel(waiting, sib, straight, diag, dq_in, dk_in, dv_in, dq_out, dk_out, dv_out, low, held, total, added, in_sems, out_sems):
+    half = sib.shape[2]
+    width = half // 2
     core, chip = here()
-    ends = ((straight, 2 * core * width), (diag, 2 * (1 - core) * width))
-
-    def store(i, j, out, offset):
-        cols = pl.ds(pl.multiple_of(ends[i][1] + offset, HEAD), width)
-        copy = pltpu.make_async_copy(total.at[i, j], out.at[0, :, cols], sems.at[2 * i + j])
+    early, late = jnp.where(chip == 0, 1.0, 0.0), jnp.where(chip == 0, 0.0, 1.0)
+    loads = [pltpu.make_async_copy(sib.at[j], low.at[j], in_sems.at[j]) for j in range(3)]
+    loads += [pltpu.make_async_copy(waiting.at[j], held.at[j], in_sems.at[3 + j]) for j in range(2)]
+    for c in loads:
+        c.start()
+    cols = pl.ds(pl.multiple_of((1 - core) * half, HEAD), half)
+    stores = []
+    for j, out in enumerate((dq_out, dk_out, dv_out)):
+        loads[j].wait()
+        first, second = low[j, :, :width].astype(F32), low[j, :, width:].astype(F32)
+        if j == 0:
+            second = second + late * diag[0].astype(F32)
+        else:
+            first = first + early * diag[j - 1].astype(F32)
+        total[j, :, :width] = first
+        total[j, :, width:] = second
+        stores.append(pltpu.make_async_copy(total.at[j], out.at[0, :, cols], out_sems.at[j]))
+        stores[-1].start()
+    for j in range(2):
+        loads[3 + j].wait()
+        added[j] = held[j].astype(F32) + straight[j].astype(F32)
+
+    def store(j, out, offset):
+        at = pl.ds(pl.multiple_of(core * half + offset, HEAD), width)
+        copy = pltpu.make_async_copy(added.at[j], out.at[0, :, at], out_sems.at[3 + j])
         copy.start()
         return copy
 
-    for i, (back, _) in enumerate(ends):
-        for j in range(2):
-            total[i, j] = waiting[i, j].astype(F32) + back[j].astype(F32)
-
     @pl.when(chip == 0)
     def _():
-        copies = [store(i, j, out, 0) for i in range(2) for j, out in enumerate((dk_out, dv_out))]
+        copies = [store(0, dk_out, 0), store(1, dv_out, 0)]
         for c in copies:
             c.wait()
 
     @pl.when(chip != 0)
     def _():
-        copies = [store(i, 0, dq_out, width) for i in range(2)]
-        for c in copies:
-            c.wait()
-
-
-def add_back(waiting, straight, diag, outs):
+        store(0, dq_out, width).wait()
+
+    for c in stores:
+        c.wait()
+
+
+def finish(waiting, sib, straight, diag, outs):
+    _, slots, half = sib.shape
     hbm = pl.BlockSpec(memory_space=pltpu.HBM)
-    return pl.pallas_call(
-        add_back_kernel,
+    anywhere = pl.BlockSpec(memory_space=pl.ANY)
+    return pl.pallas_call(
+        finish_kernel,
         out_shape=[pltpu.HBM(o.shape, F32) for o in outs],
-        in_specs=[VMEM] * 3 + [hbm] * 3,
+        in_specs=[anywhere] * 2 + [VMEM] * 2 + [hbm] * 3,
         out_specs=[hbm] * 3,
-        scratch_shapes=[pltpu.VMEM(waiting.shape, F32), pltpu.SemaphoreType.DMA((4,))],
-        input_output_aliases={3: 0, 4: 1, 5: 2},
-        compiler_params=params(),
-        cost_estimate=cost(0, 12 * waiting.size),
-        name="add_back",
-    )(waiting, straight, diag, *in_hbm(*outs))
+        scratch_shapes=[
+            pltpu.VMEM((3, slots, half), BF16),
+            pltpu.VMEM(waiting.shape, BF16),
+            pltpu.VMEM((3, slots, half), F32),
+            pltpu.VMEM(waiting.shape, F32),
+            pltpu.SemaphoreType.DMA((5,)),
+            pltpu.SemaphoreType.DMA((5,)),
+        ],
+        input_output_aliases={4: 0, 5: 1, 6: 2},
+        compiler_params=params(),
+        cost_estimate=cost(0, 12 * sib.size),
+        name="finish",
+    )(waiting, sib, straight, diag, *in_hbm(*outs))
 
 
 def pair_router_kernel(gates_ref, sum_ref, rows_x, out_ref):
@@ -840,13 +852,14 @@
 
     def far_phase(*operands):
         own_out, sib_out = far_grad(*operands)
-        *outs, waiting = join(own_out, send(sib_out, 1), queries.shape)
-        return outs, waiting
+        sib_in = send(sib_out, 1)
+        *outs, waiting = own_join(own_out, queries.shape)
+        return outs, waiting, sib_in
 
     def tail_phase(terms, *operands):
         shared = lax.all_to_all(terms.reshape(ndp * n, 1, -1), ("dp", "ctx"), 0, 0, tiled=True)
-        outs, waiting = beside(far_phase, *operands)
-        return outs, waiting, jnp.sum(shared, axis=0)[0] / float(ndp * n * slots // 2)
+        results = beside(far_phase, *operands)
+        return *results, jnp.sum(shared, axis=0)[0] / float(ndp * n * slots // 2)
 
     out_s, out_d, w_part = cross_pack(route_pos, w_router, keys, values, queries, d_gated)
     in_s, in_d = send(out_s, 2), send(out_d, 3)
@@ -869,10 +882,10 @@
 
     ret_s, ret_d = send(back_s, 2), send(back_d, 3)
     terms = pair_router(gates, sums, rows_x, ndp, n)
-    outs, waiting, router_grad = beside(
+    outs, waiting, sib_in, router_grad = beside(
         tail_phase, terms, far, local, final, gates, keep, dq_low, near_own, near_sib
     )
-    dq, dk, dv = add_back(waiting, ret_s, ret_d, outs)
+    dq, dk, dv = finish(waiting, sib_in, ret_s, ret_d, outs)
     return dq, dk, dv, router_grad
 
 

time: 42.3 us -> 42.6 us (level)
  waiting for transfers between devices: 6.19 us -> 6.99 us
  Pallas kernels: 16.8 us -> 16.2 us
    all_to_all x1, waiting for transfers between devices: 0.56 us -> 3.15 us  [tail_phase(): lax.all_to_all(terms.reshape(ndp * n, 1, -1), ('dp', 'ctx'), 0, 0, tiled=...]
    ppermute x8, waiting for transfers between devices: 2.88 us -> 1.09 us  [send(): return lax.ppermute(a, 'ctx', [(i, i ^ flip) for i in range(n)])]
    pallas_call x2, Pallas kernels: 4.86 us -> 4.31 us  [the longest x1 2.4 us: finish(): pl.pallas_call(finish_kernel, out_shape=[pltpu.HBM(o.shape, F32) for o in...]
  transfers between devices with their start and end apart: 12 -> 12, of which waited for: 6 -> 6; matrix products, arithmetic and copies ran while one was open for 0% -> 0% of each run, Pallas kernels for 28% -> 26%
where the time goes in v13:
time: 42.6 us; the launch traced here: 42.3 us
  starting transfers between devices  18.1 us (42%)
  Pallas kernels  16.2 us (38%)
  waiting for transfers between devices  6.99 us (16%)
  between operations  0.81 us (2%)
    ppermute x8, starting transfers between devices, send(): return lax.ppermute(a, 'ctx', [(i, i ^ flip) for i in range(n)])  6.85 us
    ppermute x3, starting transfers between devices, widen(): other = lax.ppermute(part, 'dp', [(i, i ^ step) for i in range(ndp)])  5.68 us
    all_to_all x1, starting transfers between devices, tail_phase(): lax.all_to_all(terms.reshape(ndp * n, 1, -1), ('dp', 'ctx'), 0, 0, tiled=...  5.53 us
    all_to_all x1, waiting for transfers between devices, tail_phase(): lax.all_to_all(terms.reshape(ndp * n, 1, -1), ('dp', 'ctx'), 0, 0, tiled=...  3.15 us
    ppermute x3, waiting for transfers between devices, widen(): other = lax.ppermute(part, 'dp', [(i, i ^ step) for i in range(ndp)])  2.74 us
    pallas_call x1, Pallas kernels, local_stats(): pl.pallas_call(functools.partial(local_stats_kernel, HEAD ** (-0.5)), out...  2.71 us
    pallas_call x1, Pallas kernels, finish(): pl.pallas_call(finish_kernel, out_shape=[pltpu.HBM(o.shape, F32) for o in...  2.4 us
    pallas_call x1, Pallas kernels, own_join(): pl.pallas_call(own_join_kernel, out_shape=[out] * 3 + [jax.ShapeDtypeStru...  1.92 us
  transfers between devices with their start and end apart: 12, of which 6 were waited for; matrix products, arithmetic and copies ran while one was open for 0% of the time, Pallas kernels for 26%

profile of v13, /device:TPU:0, one launch (start us, length us, event | category | flops | bytes accessed | tf_op | source)
XLA Modules:
  0.0 42.3 jit_solution(1784043871096125648)
XLA Ops:
  0.6 1.3 %cross_pack.1 = (bf16[2,128,512]{2,1,0:T(8,128)(2,1)S(1)}, bf16[2,128,512]{2,1,0:T(8,128)(2,1)S(1)}, f32[1,512]{1,0:T(1,128)S(1)}) custom-call(s32[1,128]{1,0:T(1,128)} %pos_ref.2, bf16[512]{0:T(512)(128)(2,1)} %w_any.1, bf16[1,128,2048]{2,1,0:T(8,128)(2,1)} %k_ref.5, bf16[1,128,2048]{2,1,0:T(8,128)(2,1)} %v_ref.5, bf16[1,128,2048]{2,1,0:T(8,128)(2,1)} %q_ref.5, ...), custom_call_target="tpu_custom_call" | custom-call | flops 1 | bytes 1 | tf_op jit(solution)/shard_map/cross_pack/pallas_call | solution.py:314
  2.0 2.4 %collective-permute-start.6 = (bf16[2,128,512]{2,1,0:T(8,128)(2,1)S(1)}, bf16[2,128,512]{2,1,0:T(8,128)(2,1)S(1)}, u32[]{:S(2)}, u32[]{:S(2)}) collective-permute-start(bf16[2,128,512]{2,1,0:T(8,128)(2,1)S(1)} %get-tuple-element.125), channel_id=1, source_target_pairs={{0,3},{1,2},{2,1},{3,0},{4,7},{5,6},{6,5},{7,4},{8,11},{9,10},{10,... | collective-permute-start | bytes 786440 | tf_op jit(solution)/shard_map/ppermute | solution.py:830
  5.0 1.5 %collective-permute-start.4 = (f32[1,512]{1,0:T(1,128)S(1)}, f32[1,512]{1,0:T(1,128)S(1)}, u32[]{:S(2)}, u32[]{:S(2)}) collective-permute-start(f32[1,512]{1,0:T(1,128)S(1)} %get-tuple-element.118), channel_id=1, source_target_pairs={{0,4},{4,0},{8,12},{12,8},{16,20},{20,16},{24,28},{28,24},{1,5},{5... | collective-permute-start | bytes 6152 | tf_op jit(solution)/shard_map/ppermute | solution.py:842
  6.6 1.3 %sib_pack.1 = bf16[4,128,1024]{2,1,0:T(8,128)(2,1)S(1)} custom-call(s32[1,128]{1,0:T(1,128)S(1)} %copy-done.1, bf16[1,128,2048]{2,1,0:T(8,128)(2,1)} %k_ref.5, bf16[1,128,2048]{2,1,0:T(8,128)(2,1)} %v_ref.5, bf16[1,128,2048]{2,1,0:T(8,128)(2,1)} %q_ref.5, f32[1,128,2048]{2,1,0:T(8,128)} %dg_ref.5), custom_call_target="tpu_custom_call" | custom-call | flops 1 | bytes 1 | tf_op jit(solution)/shard_map/sib_pack/pallas_call | solution.py:350
  7.9 0.7 %collective-permute-done.4 = f32[1,512]{1,0:T(1,128)S(1)} collective-permute-done((f32[1,512]{1,0:T(1,128)S(1)}, f32[1,512]{1,0:T(1,128)S(1)}, u32[]{:S(2)}, u32[]{:S(2)}) %collective-permute-start.4) | collective-permute-done | bytes 2080 | tf_op jit(solution)/shard_map/ppermute | solution.py:842
  8.6 4.4 %conditional.3 = (bf16[4,128,1024]{2,1,0:T(8,128)(2,1)}, bf16[1,128,4096]{2,1,0:T(8,128)(2,1)}, f32[1,2048]{1,0:T(1,128)S(1)}) conditional(s32[]{:T(128)} %bitcast.2, () %tuple.36, (bf16[4,128,1024]{2,1,0:T(8,128)(2,1)S(1)}, bf16[1,128,4096]{2,1,0:T(8,128)(2,1)S(1)}, f32[1,1024]{1,0:T(1,128)S(1)}) %tuple.49), branch_computations={%region_0.0_spmd, %region_1.0_spmd} | conditional | flops 2048 | bytes 8421520 | solution.py:836
  9.2 1.6 %collective-permute-start.3 = (f32[1,1024]{1,0:T(1,128)S(1)}, f32[1,1024]{1,0:T(1,128)S(1)}, u32[]{:S(2)}, u32[]{:S(2)}) collective-permute-start(f32[1,1024]{1,0:T(1,128)S(1)} %get-tuple-element.44), channel_id=1, source_target_pairs={{0,8},{4,12},{8,0},{12,4},{16,24},{20,28},{24,16},{28,20},{1,9},{5... | collective-permute-start | bytes 12296 | tf_op jit(solution)/shard_map/cond/branch_1_fun/ppermute | solution.py:842
  10.8 2.0 %collective-permute-done.3 = f32[1,1024]{1,0:T(1,128)S(1)} collective-permute-done((f32[1,1024]{1,0:T(1,128)S(1)}, f32[1,1024]{1,0:T(1,128)S(1)}, u32[]{:S(2)}, u32[]{:S(2)}) %collective-permute-start.3) | collective-permute-done | bytes 4128 | tf_op jit(solution)/shard_map/cond/branch_1_fun/ppermute | solution.py:842
  13.0 2.6 %collective-permute-start.7 = (f32[1,2048]{1,0:T(1,128)S(1)}, f32[1,2048]{1,0:T(1,128)S(1)}, u32[]{:S(2)}, u32[]{:S(2)}) collective-permute-start(f32[1,2048]{1,0:T(1,128)S(1)} %get-tuple-element.131), channel_id=1, source_target_pairs={{0,16},{4,20},{8,24},{12,28},{16,0},{20,4},{24,8},{28,12},{1,17},{... | collective-permute-start | bytes 24584 | tf_op jit(solution)/shard_map/ppermute | solution.py:842
  15.6 2.7 %local_stats.1 = (f32[3,8,256]{2,1,0:T(8,128)S(1)}, f32[1,256]{1,0:T(1,128)S(1)}, bf16[4,256,512]{2,1,0:T(8,128)(2,1)S(1)}, bf16[4,256,512]{2,1,0:T(8,128)(2,1)S(1)}, bf16[2,128,4096]{2,1,0:T(8,128)(2,1)S(1)}) custom-call(s32[1,128]{1,0:T(1,128)S(1)} %copy-done.1, bf16[1,128,2048]{2,1,0:T(8,128)(2,1)} %k_ref.5, bf16[1,128,2048]{2,1,0:T(8,128)(2,1)} %v_ref.5, ...), custom_call_target="tpu_custom_call" | custom-call | flops 1 | bytes 1 | tf_op jit(solution)/shard_map/local_stats/pallas_call | solution.py:476
  18.3 0.8 %cross_stats.1 = (bf16[4,256,512]{2,1,0:T(8,128)(2,1)S(1)}, f32[3,4,256]{2,1,0:T(4,128)S(1)}, bf16[2,4,256,256]{3,2,1,0:T(8,128)(2,1)S(1)}) custom-call(bf16[4,256,512]{2,1,0:T(8,128)(2,1)S(1)} %get-tuple-element.124.near.pair, bf16[4,256,512]{2,1,0:T(8,128)(2,1)S(1)} %get-tuple-element.122.far, bf16[2,128,512]{2,1,0:T(8,128)(2,1)S(1)} %collective-permute-done.5.straight, ...), custom_call_target="tpu_custom_call" | custom-call | flops 1 | bytes 1 | tf_op jit(solution)/shard_map/cross_stats/pallas_call | solution.py:525
  19.9 1.5 %collective-permute-start.8 = (f32[4,4,256]{2,1,0:T(4,128)S(1)}, f32[4,4,256]{2,1,0:T(4,128)S(1)}, u32[]{:S(2)}, u32[]{:S(2)}) collective-permute-start(f32[4,4,256]{2,1,0:T(4,128)S(1)} %get-tuple-element.133), channel_id=1, source_target_pairs={{0,2},{1,3},{2,0},{3,1},{4,6},{5,7},{6,4},{7,5},{8,10},{9,11},{10,... | collective-permute-start | bytes 49160 | tf_op jit(solution)/shard_map/ppermute | solution.py:830
  21.3 1.6 %near_grad.1 = (f32[256,512]{1,0:T(8,128)S(1)}, bf16[2,128,512]{2,1,0:T(8,128)(2,1)S(1)}, bf16[2,128,512]{2,1,0:T(8,128)(2,1)S(1)}, f32[1,256]{1,0:T(1,128)S(1)}) custom-call(bf16[4,256,512]{2,1,0:T(8,128)(2,1)S(1)} %get-tuple-element.124.near.pair, f32[3,8,256]{2,1,0:T(8,128)S(1)} %get-tuple-element.123.local, f32[3,4,256]{2,1,0:T(4,128)S(1)} %get-tuple-element.128.stats, ...), custom_call_target="tpu_custom_call" | custom-call | flops 1 | bytes 1 | tf_op jit(solution)/shard_map/near_grad/pallas_call | solution.py:590
  23.0 0.7 %collective-permute-done.8.heard = f32[4,4,256]{2,1,0:T(4,128)S(1)} collective-permute-done((f32[4,4,256]{2,1,0:T(4,128)S(1)}, f32[4,4,256]{2,1,0:T(4,128)S(1)}, u32[]{:S(2)}, u32[]{:S(2)}) %collective-permute-start.8) | collective-permute-done | bytes 16416 | tf_op jit(solution)/shard_map/ppermute | solution.py:830
  23.7 0.7 %cross_grad.1 = (bf16[2,128,512]{2,1,0:T(8,128)(2,1)S(1)}, bf16[2,128,512]{2,1,0:T(8,128)(2,1)S(1)}, bf16[256,512]{1,0:T(8,128)(2,1)S(1)}, bf16[2,256,512]{2,1,0...) custom-call(bf16[4,256,512]{2,1,0:T(8,128)(2,1)S(1)} %get-tuple-element.126.cross, ...), custom_call_target="tpu_custom_call" | custom-call | flops 1 | bytes 1 | tf_op jit(solution)/shard_map/cross_grad/pallas_call | solution.py:635
  24.4 1.5 %collective-permute-start.9 = (bf16[2,128,512]{2,1,0:T(8,128)(2,1)S(1)}, bf16[2,128,512]{2,1,0:T(8,128)(2,1)S(1)}, u32[]{:S(2)}, u32[]{:S(2)}) collective-permute-start(bf16[2,128,512]{2,1,0:T(8,128)(2,1)S(1)} %get-tuple-element.145), channel_id=1, source_target_pairs={{0,2},{1,3},{2,0},{3,1},{4,6},{5,7},{6,4},{7,5},{8,10},{9,11},{10,... | collective-permute-start | bytes 786440 | tf_op jit(solution)/shard_map/ppermute | solution.py:830
  25.8 1.0 %router_terms.1 = f32[8,4,1,512]{3,2,1,0:T(1,128)} custom-call(f32[1,256]{1,0:T(1,128)S(1)} %get-tuple-element.134.gates.gates_ref, f32[1,256]{1,0:T(1,128)S(1)} %get-tuple-element.142.sum_ref, bf16[2,128,4096]{2,1,0:T(8,128)(2,1)S(1)} %get-tuple-element.130.rows_x), custom_call_target="tpu_custom_call" | custom-call | flops 1 | bytes 1 | tf_op jit(solution)/shard_map/router_terms/pallas_call | solution.py:814
  26.9 13.0 %conditional.4 = (f32[1,128,2048]{2,1,0:T(8,128)}, f32[1,128,2048]{2,1,0:T(8,128)}, f32[1,128,2048]{2,1,0:T(8,128)}, bf16[2,128,512]{2,1,0:T(8,128)(2,1)}, bf16[...) conditional(s32[]{:T(128)} %bitcast.2, () %tuple.35, (s32[1,128]{1,0:T(1,128)S(1)}, bf16[4,256,512]{2,1,0:T(8,128)(2,1)S(1)}, ...), branch_computations={%region_2.0_spmd, %region_3.0_spmd} | conditional | flops 16388 | bytes 4462810 | solution.py:836
  26.9 5.5 %all-to-all-start = ((f32[32,1,512]{2,1,0:T(1,128)}), f32[32,1,512]{2,1,0:T(1,128)S(1)}, u32[]{:S(2)}, u32[]{:S(2)}) async-start(f32[32,1,512]{2,1,0:T(1,128)} %bitcast.1), calls=%async_computation | async-start | bytes 131072 | tf_op jit(solution)/shard_map/cond/branch_1_fun/all_to_all | solution.py:860
  32.4 4.2 %conditional = (f32[1,128,2048]{2,1,0:T(8,128)}, f32[1,128,2048]{2,1,0:T(8,128)}, f32[1,128,2048]{2,1,0:T(8,128)}, bf16[2,128,512]{2,1,0:T(8,128)(2,1)}, bf16[3,128,1024]{2,1,0:T(8,128)(2,1)}) conditional(s32[]{:T(128)} %bitcast, () %tuple.23, (bf16[4,256,512]{2,1,0:T(8,128)(2,1)S(1)}, f32[3,8,256]{2,1,0:T(8,128)S(1)}, f32[2,4,256]{2,1,0:T(4,128)S(1)}, ...), branch_computations={%region_4.0_spmd, %region_5.0_spmd} | conditional | flops 2 | bytes 4194360 | solution.py:836
  32.5 1.7 %far_grad.1 = (bf16[3,128,1024]{2,1,0:T(8,128)(2,1)S(1)}, bf16[3,128,1024]{2,1,0:T(8,128)(2,1)S(1)}) custom-call(bf16[4,256,512]{2,1,0:T(8,128)(2,1)S(1)} %get-tuple-element.45.pair, f32[3,8,256]{2,1,0:T(8,128)S(1)} %get-tuple-element.46.local, f32[2,4,256]{2,1,0:T(4,128)S(1)} %get-tuple-element.47.final, f32[1,256]{1,0:T(1,128)S(1)} %get-tuple-element.48.gates, ...), custom_call_target="tpu_custom_call" | custom-call | flops 1 | bytes 1 | tf_op jit(solution)/shard_map/cond/branch_1_fun/cond/branch_1_fun/far_grad/pallas_call | solution.py:681
  34.5 1.9 %own_join.1 = (f32[1,128,2048]{2,1,0:T(8,128)}, f32[1,128,2048]{2,1,0:T(8,128)}, f32[1,128,2048]{2,1,0:T(8,128)}, bf16[2,128,512]{2,1,0:T(8,128)(2,1)}) custom-call(bf16[3,128,1024]{2,1,0:T(8,128)(2,1)S(1)} %get-tuple-element.53.own), custom_call_target="tpu_custom_call" | custom-call | flops 1 | bytes 1 | tf_op jit(solution)/shard_map/cond/branch_1_fun/cond/branch_1_fun/own_join/pallas_call | solution.py:712
  36.7 3.2 %all-to-all-done = f32[32,1,512]{2,1,0:T(1,128)S(1)} async-done(((f32[32,1,512]{2,1,0:T(1,128)}), f32[32,1,512]{2,1,0:T(1,128)S(1)}, u32[]{:S(2)}, u32[]{:S(2)}) %all-to-all-start) | async-done | bytes 65568 | tf_op jit(solution)/shard_map/cond/branch_1_fun/all_to_all | solution.py:860
  39.9 2.4 %finish.1 = (f32[1,128,2048]{2,1,0:T(8,128)}, f32[1,128,2048]{2,1,0:T(8,128)}, f32[1,128,2048]{2,1,0:T(8,128)}) custom-call(bf16[2,128,512]{2,1,0:T(8,128)(2,1)} %get-tuple-element.143.waiting, bf16[3,128,1024]{2,1,0:T(8,128)(2,1)} %get-tuple-element.144.sib, ...), custom_call_target="tpu_custom_call", output_to_operand_aliasing={{0}: (4, {}), {1}: (5, {}), {2}: (6, {})} | custom-call | flops 1 | bytes 1 | tf_op jit(solution)/shard_map/finish/pallas_call | solution.py:774
  (25 shorter events, 2.7 us)
Async XLA Ops:
  0.6 5.9 %copy-start.1 = (s32[1,128]{1,0:T(1,128)S(1)}, s32[1,128]{1,0:T(1,128)}, u32[]{:S(2)}) copy-start(s32[1,128]{1,0:T(1,128)} %pos_ref.2) | copy-start | bytes 1540
  2.0 6.6 %copy-start = (bf16[1,128,4096]{2,1,0:T(8,128)(2,1)S(1)}, bf16[1,128,4096]{2,1,0:T(8,128)(2,1)}, u32[]{:S(2)}) copy-start(bf16[1,128,4096]{2,1,0:T(8,128)(2,1)} %x_ref.1) | copy-start | bytes 3145732
  2.0 16.3 %collective-permute-start.6 = (bf16[2,128,512]{2,1,0:T(8,128)(2,1)S(1)}, bf16[2,128,512]{2,1,0:T(8,128)(2,1)S(1)}, u32[]{:S(2)}, u32[]{:S(2)}) collective-permute-start(bf16[2,128,512]{2,1,0:T(8,128)(2,1)S(1)} %get-tuple-element.125), channel_id=1, source_target_pairs={{0,3},{1,2},{2,1},{3,0},{4,7},{5,6},{6,5},{7,4},{8,11},{9,10},{10,... | collective-permute-start | bytes 786440 | tf_op jit(solution)/shard_map/ppermute | solution.py:830
  4.4 13.9 %collective-permute-start.5 = (bf16[2,128,512]{2,1,0:T(8,128)(2,1)S(1)}, bf16[2,128,512]{2,1,0:T(8,128)(2,1)S(1)}, u32[]{:S(2)}, u32[]{:S(2)}) collective-permute-start(bf16[2,128,512]{2,1,0:T(8,128)(2,1)S(1)} %get-tuple-element.116), channel_id=1, source_target_pairs={{0,2},{1,3},{2,0},{3,1},{4,6},{5,7},{6,4},{7,5},{8,10},{9,11},{10,... | collective-permute-start | bytes 786440 | tf_op jit(solution)/shard_map/ppermute | solution.py:830
  5.0 3.6 %collective-permute-start.4 = (f32[1,512]{1,0:T(1,128)S(1)}, f32[1,512]{1,0:T(1,128)S(1)}, u32[]{:S(2)}, u32[]{:S(2)}) collective-permute-start(f32[1,512]{1,0:T(1,128)S(1)} %get-tuple-element.118), channel_id=1, source_target_pairs={{0,4},{4,0},{8,12},{12,8},{16,20},{20,16},{24,28},{28,24},{1,5},{5... | collective-permute-start | bytes 6152 | tf_op jit(solution)/shard_map/ppermute | solution.py:842
  8.7 4.2 %collective-permute-start.1 = (bf16[4,128,1024]{2,1,0:T(8,128)(2,1)S(1)}, bf16[4,128,1024]{2,1,0:T(8,128)(2,1)}, u32[]{:S(2)}, u32[]{:S(2)}) collective-permute-start(bf16[4,128,1024]{2,1,0:T(8,128)(2,1)S(1)} %get-tuple-element.42), channel_id=1, source_target_pairs={{0,1},{1,0},{2,3},{3,2},{4,5},{5,4},{6,7},{7,6},{8,9},{9,8},{10,11... | collective-permute-start | bytes 3145736 | tf_op jit(solution)/shard_map/cond/branch_1_fun/ppermute | solution.py:830
  8.7 4.3 %collective-permute-start.2 = (bf16[1,128,4096]{2,1,0:T(8,128)(2,1)S(1)}, bf16[1,128,4096]{2,1,0:T(8,128)(2,1)}, u32[]{:S(2)}, u32[]{:S(2)}) collective-permute-start(bf16[1,128,4096]{2,1,0:T(8,128)(2,1)S(1)} %get-tuple-element.43), channel_id=1, source_target_pairs={{0,1},{1,0},{2,3},{3,2},{4,5},{5,4},{6,7},{7,6},{8,9},{9,8},{10,11... | collective-permute-start | bytes 3145736 | tf_op jit(solution)/shard_map/cond/branch_1_fun/ppermute | solution.py:830
  9.2 3.6 %collective-permute-start.3 = (f32[1,1024]{1,0:T(1,128)S(1)}, f32[1,1024]{1,0:T(1,128)S(1)}, u32[]{:S(2)}, u32[]{:S(2)}) collective-permute-start(f32[1,1024]{1,0:T(1,128)S(1)} %get-tuple-element.44), channel_id=1, source_target_pairs={{0,8},{4,12},{8,0},{12,4},{16,24},{20,28},{24,16},{28,20},{1,9},{5... | collective-permute-start | bytes 12296 | tf_op jit(solution)/shard_map/cond/branch_1_fun/ppermute | solution.py:842
  13.0 6.1 %collective-permute-start.7 = (f32[1,2048]{1,0:T(1,128)S(1)}, f32[1,2048]{1,0:T(1,128)S(1)}, u32[]{:S(2)}, u32[]{:S(2)}) collective-permute-start(f32[1,2048]{1,0:T(1,128)S(1)} %get-tuple-element.131), channel_id=1, source_target_pairs={{0,16},{4,20},{8,24},{12,28},{16,0},{20,4},{24,8},{28,12},{1,17},{... | collective-permute-start | bytes 24584 | tf_op jit(solution)/shard_map/ppermute | solution.py:842
  19.9 3.8 %collective-permute-start.8 = (f32[4,4,256]{2,1,0:T(4,128)S(1)}, f32[4,4,256]{2,1,0:T(4,128)S(1)}, u32[]{:S(2)}, u32[]{:S(2)}) collective-permute-start(f32[4,4,256]{2,1,0:T(4,128)S(1)} %get-tuple-element.133), channel_id=1, source_target_pairs={{0,2},{1,3},{2,0},{3,1},{4,6},{5,7},{6,4},{7,5},{8,10},{9,11},{10,... | collective-permute-start | bytes 49160 | tf_op jit(solution)/shard_map/ppermute | solution.py:830
  24.4 15.5 %collective-permute-start.9 = (bf16[2,128,512]{2,1,0:T(8,128)(2,1)S(1)}, bf16[2,128,512]{2,1,0:T(8,128)(2,1)S(1)}, u32[]{:S(2)}, u32[]{:S(2)}) collective-permute-start(bf16[2,128,512]{2,1,0:T(8,128)(2,1)S(1)} %get-tuple-element.145), channel_id=1, source_target_pairs={{0,2},{1,3},{2,0},{3,1},{4,6},{5,7},{6,4},{7,5},{8,10},{9,11},{10,... | collective-permute-start | bytes 786440 | tf_op jit(solution)/shard_map/ppermute | solution.py:830
  25.8 14.1 %collective-permute-start.10 = (bf16[2,128,512]{2,1,0:T(8,128)(2,1)S(1)}, bf16[2,128,512]{2,1,0:T(8,128)(2,1)S(1)}, u32[]{:S(2)}, u32[]{:S(2)}) collective-permute-start(bf16[2,128,512]{2,1,0:T(8,128)(2,1)S(1)} %get-tuple-element.146), channel_id=1, source_target_pairs={{0,3},{1,2},{2,1},{3,0},{4,7},{5,6},{6,5},{7,4},{8,11},{9,10},{10,... | collective-permute-start | bytes 786440 | tf_op jit(solution)/shard_map/ppermute | solution.py:830
  26.9 12.9 %all-to-all-start = ((f32[32,1,512]{2,1,0:T(1,128)}), f32[32,1,512]{2,1,0:T(1,128)S(1)}, u32[]{:S(2)}, u32[]{:S(2)}) async-start(f32[32,1,512]{2,1,0:T(1,128)} %bitcast.1), calls=%async_computation | async-start | bytes 131072 | tf_op jit(solution)/shard_map/cond/branch_1_fun/all_to_all | solution.py:860
  34.2 2.5 %collective-permute-start = (bf16[3,128,1024]{2,1,0:T(8,128)(2,1)S(1)}, bf16[3,128,1024]{2,1,0:T(8,128)(2,1)}, u32[]{:S(2)}, u32[]{:S(2)}) collective-permute-start(bf16[3,128,1024]{2,1,0:T(8,128)(2,1)S(1)} %get-tuple-element.58), channel_id=1, source_target_pairs={{0,1},{1,0},{2,3},{3,2},{4,5},{5,4},{6,7},{7,6},{8,9},{9,8},{10,11... | collective-permute-start | bytes 2359304 | tf_op jit(solution)/shard_map/cond/branch_1_fun/cond/branch_1_fun/ppermute | solution.py:830
  39.9 2.4 %copy-start.2 = (f32[512]{0:T(512)}, f32[512]{0:T(512)S(1)}, u32[]{:S(2)}) copy-start(f32[512]{0:T(512)S(1)} %get-tuple-element.115) | copy-start | bytes 6148

commit v14 on v13

--- a/solution.py
+++ b/solution.py
@@ -359,35 +359,18 @@
     )(route_pos, *in_hbm(keys, values, queries, d_gated))
 
 
-def pair_gate_kernel(parts, live_ref, rows_x, w_ref, local, stats, out_ref, message):
+def put_gates(live_ref, rows_x, w_ref, parts, out_ref):
     chunk = w_ref.shape[1] // parts
     slots = rows_x.shape[1]
+    me = lax.axis_index("dp")
     for i in range(2):
         total = jnp.zeros((8, slots), F32)
         for j in range(parts):
             w_rows = jnp.broadcast_to(w_ref[:, j * chunk : (j + 1) * chunk], (8, chunk)).astype(BF16)
-            cols = pl.ds(pl.multiple_of((lax.axis_index("dp") ^ j) * chunk, HEAD), chunk)
+            cols = pl.ds(pl.multiple_of((me ^ j) * chunk, HEAD), chunk)
             total = total + nt(w_rows, rows_x[i, :, cols])
         lanes = slice(i * slots, (i + 1) * slots)
         out_ref[:, lanes] = live_ref[:, lanes] / (1.0 + jnp.exp(-total[0:1]))
-    first = here()[1] == 0
-    heads = stats.shape[1]
-    for i in range(3):
-        message[i] = jnp.where(first, stats[i], local[i, heads:])
-    message[3] = jnp.broadcast_to(out_ref[...], message.shape[1:])
-
-
-def pair_gate(live, rows_x, w_full, local, stats, parts):
-    _, heads, lanes = stats.shape
-    return pl.pallas_call(
-        functools.partial(pair_gate_kernel, parts),
-        out_shape=[jax.ShapeDtypeStruct(live.shape, F32), jax.ShapeDtypeStruct((4, heads, lanes), F32)],
-        in_specs=[VMEM] * 5,
-        out_specs=[VMEM] * 2,
-        compiler_params=params(),
-        cost_estimate=cost(16 * rows_x.size, rows_x.size * 2),
-        name="router_gate",
-    )(live, rows_x, w_full, local, stats)
 
 
 def local_mask(core, pair):
@@ -491,7 +474,8 @@
     )(route_pos, *in_hbm(keys, values, queries, d_gated), sib, x_routed, x_sib)
 
 
-def cross_stats_kernel(scale, near, far, straight, diag, cross, stats, kept):
+def cross_stats_kernel(scale, parts, near, far, straight, diag, live, rows_x, w_ref, local, cross, stats, kept, gates, message):
+    put_gates(live, rows_x, w_ref, parts, gates)
     slots, width = straight.shape[1], straight.shape[2]
     chip = here()[1]
     top, bottom = slice(0, slots), slice(slots, 2 * slots)
@@ -510,31 +494,36 @@
             cross[part, bottom] = diag[part]
             cross[2 + part] = near[2 + part]
 
-    live = cross[0, :, :HEAD].astype(F32) < MARK_LIMIT
-    mask = jnp.concatenate([live] * (2 * slots // HEAD), axis=1)
+    alive = cross[0, :, :HEAD].astype(F32) < MARK_LIMIT
+    mask = jnp.concatenate([alive] * (2 * slots // HEAD), axis=1)
     heads = width // HEAD
     for h in range(heads):
         cols = slice(h * HEAD, (h + 1) * HEAD)
         scores = jnp.where(mask, nt(cross[0, :, cols], cross[2, :, cols]) * scale, NEG_FILL)
         kept_stats(scores, nt(cross[1, :, cols], cross[3, :, cols]), kept, stats, h)
-
-
-def cross_stats(near, far, straight, diag):
+    for i in range(3):
+        message[i] = jnp.where(chip == 0, stats[i], local[i, heads:])
+    message[3] = jnp.broadcast_to(gates[...], message.shape[1:])
+
+
+def cross_stats(near, far, straight, diag, live, rows_x, w_full, local, parts):
     _, slots, width = straight.shape
     heads = width // HEAD
     return pl.pallas_call(
-        functools.partial(cross_stats_kernel, HEAD**-0.5),
+        functools.partial(cross_stats_kernel, HEAD**-0.5, parts),
         out_shape=[
             pltpu.VMEM((4, 2 * slots, width), BF16),
             jax.ShapeDtypeStruct((3, heads, 2 * slots), F32),
             pltpu.VMEM((2, heads, 2 * slots, 2 * slots), BF16),
+            jax.ShapeDtypeStruct(live.shape, F32),
+            jax.ShapeDtypeStruct((4, heads, 2 * slots), F32),
         ],
-        in_specs=[VMEM] * 4,
-        out_specs=[VMEM] * 3,
+        in_specs=[VMEM] * 8,
+        out_specs=[VMEM] * 5,
         compiler_params=params(),
         cost_estimate=cost(16 * slots * slots * width, 32 * slots * width, 4 * slots * slots * heads),
         name="cross_stats",
-    )(near, far, straight, diag)
+    )(near, far, straight, diag, live, rows_x, w_full, local)
 
 
 NONE = (-3e38, 0.0, 0.0)
@@ -598,7 +587,23 @@
     )(pair, local, stats, gates)
 
 
-def cross_grad_kernel(scale, cross, kept, stats, local, heard, gates, near_dq, near_sum, straight, diag, dq_out, keep, final, sum_out):
+def put_terms(grad, rows_x, out_ref):
+    high = grad.astype(BF16)
+    rest = grad - high.astype(F32)
+    mid = rest.astype(BF16)
+    low = (rest - mid.astype(F32)).astype(BF16)
+    slots = rows_x.shape[1]
+    row = lax.broadcasted_iota(jnp.int32, (8, grad.shape[1]), 0)
+    lhs = jnp.where(row == 0, high.astype(F32), jnp.where(row == 1, mid.astype(F32), jnp.where(row == 2, low.astype(F32), 0.0)))
+    lhs = lhs.astype(BF16)
+    term = jnp.sum(nn(lhs[:, :slots], rows_x[0]) + nn(lhs[:, slots:], rows_x[1]), axis=0, keepdims=True)
+    parts, copies, _, chunk = out_ref.shape
+    for j in range(parts):
+        for i in range(copies):
+            out_ref[j, i] = term[:, j * chunk : (j + 1) * chunk]
+
+
+def cross_grad_kernel(scale, cross, kept, stats, local, heard, gates, near_dq, near_sum, rows_x, straight, diag, dq_out, keep, final, terms):
     slots, width = straight.shape[1], straight.shape[2]
     heads = width // HEAD
     first = here()[1] == 0
@@ -610,7 +615,6 @@
     factor, delta = merge(mine, choose(first, other, near))
     factor = factor * jnp.where(first, heard[3], jnp.broadcast_to(gates[...], factor.shape))
     final[0], final[1] = merge(far, choose(first, NONE, other))
-    sum_out[...] = near_sum[...] + jnp.sum(final[1], axis=0, keepdims=True)
     for h in range(heads):
         cols = slice(h * HEAD, (h + 1) * HEAD)
         row = slice(h, h + 1)
@@ -626,9 +630,11 @@
         diag[0, :, cols] = sent[slots:]
         straight[1, :, cols] = dv[:slots].astype(BF16)
         diag[1, :, cols] = dv[slots:].astype(BF16)
-
-
-def cross_grad(cross, kept, stats, local, heard, gates, near_dq, near_sum):
+    sums = near_sum[...] + jnp.sum(final[1], axis=0, keepdims=True)
+    put_terms(sums * gates[...] * (1.0 - gates[...]), rows_x, terms)
+
+
+def cross_grad(cross, kept, stats, local, heard, gates, near_dq, near_sum, rows_x, parts, copies):
     _, rows, width = cross.shape
     slots = rows // 2
     out = pltpu.VMEM((2, slots, width), BF16)
@@ -640,14 +646,14 @@
             pltpu.VMEM((rows, width), BF16),
             pltpu.VMEM((2, rows, width), BF16),
             jax.ShapeDtypeStruct((2, width // HEAD, rows), F32),
-            jax.ShapeDtypeStruct((1, rows), F32),
+            pltpu.VMEM((parts, copies, 1, rows_x.shape[2] // parts), F32),
         ],
-        in_specs=[VMEM] * 8,
+        in_specs=[VMEM] * 9,
         out_specs=[VMEM] * 6,
         compiler_params=params(),
         cost_estimate=cost(24 * slots * slots * width, 64 * slots * width),
         name="cross_grad",
-    )(cross, kept, stats, local, heard, gates, near_dq, near_sum)
+    )(cross, kept, stats, local, heard, gates, near_dq, near_sum, rows_x)
 
 
 def far_grad_kernel(scale, pair, local, final, gates, keep, near_dq, near_own, near_sib, own_out, sib_out):
@@ -791,37 +797,6 @@
     )(waiting, sib, straight, diag, *in_hbm(*outs))
 
 
-def pair_router_kernel(gates_ref, sum_ref, rows_x, out_ref):
-    gates = gates_ref[...]
-    grad = sum_ref[...] * gates * (1.0 - gates)
-    high = grad.astype(BF16)
-    rest = grad - high.astype(F32)
-    mid = rest.astype(BF16)
-    low = (rest - mid.astype(F32)).astype(BF16)
-    slots = rows_x.shape[1]
-    row = lax.broadcasted_iota(jnp.int32, (8, grad.shape[1]), 0)
-    lhs = jnp.where(row == 0, high.astype(F32), jnp.where(row == 1, mid.astype(F32), jnp.where(row == 2, low.astype(F32), 0.0)))
-    lhs = lhs.astype(BF16)
-    term = jnp.sum(nn(lhs[:, :slots], rows_x[0]) + nn(lhs[:, slots:], rows_x[1]), axis=0, keepdims=True)
-    parts, copies, _, chunk = out_ref.shape
-    for j in range(parts):
-        for i in range(copies):
-            out_ref[j, i] = term[:, j * chunk : (j + 1) * chunk]
-
-
-def pair_router(gates, sums, rows_x, parts, copies):
-    chunk = rows_x.shape[-1] // parts
-    return pl.pallas_call(
-        pair_router_kernel,
-        out_shape=jax.ShapeDtypeStruct((parts, copies, 1, chunk), F32),
-        in_specs=[VMEM] * 3,
-        out_specs=VMEM,
-        compiler_params=params(),
-        cost_estimate=cost(32 * rows_x.size, rows_x.size * 4),
-        name="router_terms",
-    )(gates, sums, rows_x)
-
-
 def swap_body(route_pos, x_routed, w_router, queries, keys, values, d_gated):
     slots = queries.shape[1]
     n, ndp = lax.axis_size("ctx"), lax.axis_size("dp")
@@ -869,19 +844,17 @@
         w_part = widen(w_part, 1, theirs)
     sib, x_sib, w_part = beside(exchange_phase, x_routed, w_part, theirs)
     local, live, near, far, rows_x = local_stats(route_pos, keys, values, queries, d_gated, sib, x_routed, x_sib)
-    cross, stats, kept = cross_stats(near, far, in_s, in_d)
     if ndp > 2:
-        w_part = widen(w_part, ndp // 2, stats)
-    gates, message = pair_gate(live, rows_x, w_part, local, stats, ndp)
+        w_part = widen(w_part, ndp // 2, local, in_s, in_d)
+    cross, stats, kept, gates, message = cross_stats(near, far, in_s, in_d, live, rows_x, w_part, local, ndp)
 
     heard = send(message, 2)
     near_dq, near_own, near_sib, near_sum = near_grad(near, local, stats, gates)
-    back_s, back_d, dq_low, keep, final, sums = cross_grad(
-        cross, kept, stats, local, heard, gates, near_dq, near_sum
+    back_s, back_d, dq_low, keep, final, terms = cross_grad(
+        cross, kept, stats, local, heard, gates, near_dq, near_sum, rows_x, ndp, n
     )
 
     ret_s, ret_d = send(back_s, 2), send(back_d, 3)
-    terms = pair_router(gates, sums, rows_x, ndp, n)
     outs, waiting, sib_in, router_grad = beside(
         tail_phase, terms, far, local, final, gates, keep, dq_low, near_own, near_sib
     )

time: 42.6 us -> 42.3 us (level)
    pallas_call x3 -> x1, Pallas kernels: 2.52 us -> 1.42 us  [cross_stats(): pl.pallas_call(functools.partial(cross_stats_kernel, HEAD ** (-0.5), part...]
    pallas_call x1, Pallas kernels: 0.69 us -> 1.57 us  [cross_grad(): pl.pallas_call(functools.partial(cross_grad_kernel, HEAD ** (-0.5)), out_...]
  transfers between devices with their start and end apart: 12 -> 12, of which waited for: 6 -> 6; matrix products, arithmetic and copies ran while one was open for 0% -> 0% of each run, Pallas kernels for 26% -> 22%
where the time goes in v14:
time: 42.3 us; the launch traced here: 42.1 us
  starting transfers between devices  18.1 us (43%)
  Pallas kernels  16 us (38%)
  waiting for transfers between devices  6.96 us (16%)
  between operations  0.79 us (2%)
    ppermute x8, starting transfers between devices, send(): return lax.ppermute(a, 'ctx', [(i, i ^ flip) for i in range(n)])  6.89 us
    ppermute x3, starting transfers between devices, widen(): other = lax.ppermute(part, 'dp', [(i, i ^ step) for i in range(ndp)])  5.68 us
    all_to_all x1, starting transfers between devices, tail_phase(): lax.all_to_all(terms.reshape(ndp * n, 1, -1), ('dp', 'ctx'), 0, 0, tiled=...  5.55 us
    all_to_all x1, waiting for transfers between devices, tail_phase(): lax.all_to_all(terms.reshape(ndp * n, 1, -1), ('dp', 'ctx'), 0, 0, tiled=...  3.15 us
    ppermute x3, waiting for transfers between devices, widen(): other = lax.ppermute(part, 'dp', [(i, i ^ step) for i in range(ndp)])  2.74 us
    pallas_call x1, Pallas kernels, local_stats(): pl.pallas_call(functools.partial(local_stats_kernel, HEAD ** (-0.5)), out...  2.69 us
    pallas_call x1, Pallas kernels, finish(): pl.pallas_call(finish_kernel, out_shape=[pltpu.HBM(o.shape, F32) for o in...  2.4 us
    pallas_call x1, Pallas kernels, own_join(): pl.pallas_call(own_join_kernel, out_shape=[out] * 3 + [jax.ShapeDtypeStru...  1.9 us
  transfers between devices with their start and end apart: 12, of which 6 were waited for; matrix products, arithmetic and copies ran while one was open for 0% of the time, Pallas kernels for 22%

profile of v14, /device:TPU:0, one launch (start us, length us, event | category | flops | bytes accessed | tf_op | source)
XLA Modules:
  0.0 42.1 jit_solution(4323773731760460805)
XLA Ops:
  0.6 1.3 %cross_pack.1 = (bf16[2,128,512]{2,1,0:T(8,128)(2,1)S(1)}, bf16[2,128,512]{2,1,0:T(8,128)(2,1)S(1)}, f32[1,512]{1,0:T(1,128)S(1)}) custom-call(s32[1,128]{1,0:T(1,128)} %pos_ref.2, bf16[512]{0:T(512)(128)(2,1)} %w_any.1, bf16[1,128,2048]{2,1,0:T(8,128)(2,1)} %k_ref.5, bf16[1,128,2048]{2,1,0:T(8,128)(2,1)} %v_ref.5, bf16[1,128,2048]{2,1,0:T(8,128)(2,1)} %q_ref.5, ...), custom_call_target="tpu_custom_call" | custom-call | flops 1 | bytes 1 | tf_op jit(solution)/shard_map/cross_pack/pallas_call | solution.py:314
  2.0 2.4 %collective-permute-start.6 = (bf16[2,128,512]{2,1,0:T(8,128)(2,1)S(1)}, bf16[2,128,512]{2,1,0:T(8,128)(2,1)S(1)}, u32[]{:S(2)}, u32[]{:S(2)}) collective-permute-start(bf16[2,128,512]{2,1,0:T(8,128)(2,1)S(1)} %get-tuple-element.125), channel_id=1, source_target_pairs={{0,3},{1,2},{2,1},{3,0},{4,7},{5,6},{6,5},{7,4},{8,11},{9,10},{10,... | collective-permute-start | bytes 786440 | tf_op jit(solution)/shard_map/ppermute | solution.py:805
  4.4 0.6 %collective-permute-start.5 = (bf16[2,128,512]{2,1,0:T(8,128)(2,1)S(1)}, bf16[2,128,512]{2,1,0:T(8,128)(2,1)S(1)}, u32[]{:S(2)}, u32[]{:S(2)}) collective-permute-start(bf16[2,128,512]{2,1,0:T(8,128)(2,1)S(1)} %get-tuple-element.116), channel_id=1, source_target_pairs={{0,2},{1,3},{2,0},{3,1},{4,6},{5,7},{6,4},{7,5},{8,10},{9,11},{10,... | collective-permute-start | bytes 786440 | tf_op jit(solution)/shard_map/ppermute | solution.py:805
  5.0 1.5 %collective-permute-start.4 = (f32[1,512]{1,0:T(1,128)S(1)}, f32[1,512]{1,0:T(1,128)S(1)}, u32[]{:S(2)}, u32[]{:S(2)}) collective-permute-start(f32[1,512]{1,0:T(1,128)S(1)} %get-tuple-element.118), channel_id=1, source_target_pairs={{0,4},{4,0},{8,12},{12,8},{16,20},{20,16},{24,28},{28,24},{1,5},{5... | collective-permute-start | bytes 6152 | tf_op jit(solution)/shard_map/ppermute | solution.py:817
  6.6 1.3 %sib_pack.1 = bf16[4,128,1024]{2,1,0:T(8,128)(2,1)S(1)} custom-call(s32[1,128]{1,0:T(1,128)S(1)} %copy-done.1, bf16[1,128,2048]{2,1,0:T(8,128)(2,1)} %k_ref.5, bf16[1,128,2048]{2,1,0:T(8,128)(2,1)} %v_ref.5, bf16[1,128,2048]{2,1,0:T(8,128)(2,1)} %q_ref.5, f32[1,128,2048]{2,1,0:T(8,128)} %dg_ref.5), custom_call_target="tpu_custom_call" | custom-call | flops 1 | bytes 1 | tf_op jit(solution)/shard_map/sib_pack/pallas_call | solution.py:350
  7.9 0.7 %collective-permute-done.4 = f32[1,512]{1,0:T(1,128)S(1)} collective-permute-done((f32[1,512]{1,0:T(1,128)S(1)}, f32[1,512]{1,0:T(1,128)S(1)}, u32[]{:S(2)}, u32[]{:S(2)}) %collective-permute-start.4) | collective-permute-done | bytes 2080 | tf_op jit(solution)/shard_map/ppermute | solution.py:817
  8.6 4.4 %conditional.3 = (bf16[4,128,1024]{2,1,0:T(8,128)(2,1)}, bf16[1,128,4096]{2,1,0:T(8,128)(2,1)}, f32[1,2048]{1,0:T(1,128)S(1)}) conditional(s32[]{:T(128)} %bitcast.2, () %tuple.36, (bf16[4,128,1024]{2,1,0:T(8,128)(2,1)S(1)}, bf16[1,128,4096]{2,1,0:T(8,128)(2,1)S(1)}, f32[1,1024]{1,0:T(1,128)S(1)}) %tuple.49), branch_computations={%region_0.0_spmd, %region_1.0_spmd} | conditional | flops 2048 | bytes 8421520 | solution.py:811
  9.2 1.6 %collective-permute-start.3 = (f32[1,1024]{1,0:T(1,128)S(1)}, f32[1,1024]{1,0:T(1,128)S(1)}, u32[]{:S(2)}, u32[]{:S(2)}) collective-permute-start(f32[1,1024]{1,0:T(1,128)S(1)} %get-tuple-element.44), channel_id=1, source_target_pairs={{0,8},{4,12},{8,0},{12,4},{16,24},{20,28},{24,16},{28,20},{1,9},{5... | collective-permute-start | bytes 12296 | tf_op jit(solution)/shard_map/cond/branch_1_fun/ppermute | solution.py:817
  10.8 2.0 %collective-permute-done.3 = f32[1,1024]{1,0:T(1,128)S(1)} collective-permute-done((f32[1,1024]{1,0:T(1,128)S(1)}, f32[1,1024]{1,0:T(1,128)S(1)}, u32[]{:S(2)}, u32[]{:S(2)}) %collective-permute-start.3) | collective-permute-done | bytes 4128 | tf_op jit(solution)/shard_map/cond/branch_1_fun/ppermute | solution.py:817
  13.0 2.6 %collective-permute-start.7 = (f32[1,2048]{1,0:T(1,128)S(1)}, f32[1,2048]{1,0:T(1,128)S(1)}, u32[]{:S(2)}, u32[]{:S(2)}) collective-permute-start(f32[1,2048]{1,0:T(1,128)S(1)} %get-tuple-element.128), channel_id=1, source_target_pairs={{0,16},{4,20},{8,24},{12,28},{16,0},{20,4},{24,8},{28,12},{1,17},{... | collective-permute-start | bytes 24584 | tf_op jit(solution)/shard_map/ppermute | solution.py:817
  15.6 2.7 %local_stats.1 = (f32[3,8,256]{2,1,0:T(8,128)S(1)}, f32[1,256]{1,0:T(1,128)S(1)}, bf16[4,256,512]{2,1,0:T(8,128)(2,1)S(1)}, bf16[4,256,512]{2,1,0:T(8,128)(2,1)S(1)}, bf16[2,128,4096]{2,1,0:T(8,128)(2,1)S(1)}) custom-call(s32[1,128]{1,0:T(1,128)S(1)} %copy-done.1, bf16[1,128,2048]{2,1,0:T(8,128)(2,1)} %k_ref.5, bf16[1,128,2048]{2,1,0:T(8,128)(2,1)} %v_ref.5, ...), custom_call_target="tpu_custom_call" | custom-call | flops 1 | bytes 1 | tf_op jit(solution)/shard_map/local_stats/pallas_call | solution.py:459
  18.4 1.4 %cross_stats.1 = (bf16[4,256,512]{2,1,0:T(8,128)(2,1)S(1)}, f32[3,4,256]{2,1,0:T(4,128)S(1)}, bf16[2,4,256,256]{3,2,1,0:T(8,128)(2,1)S(1)}, f32[1,256]{1,0:T(1,128)S(1)}, f32[4,4,256]{2,1,0:T(4,128)S(1)}) custom-call(bf16[4,256,512]{2,1,0:T(8,128)(2,1)S(1)} %get-tuple-element.124.near.pair, bf16[4,256,512]{2,1,0:T(8,128)(2,1)S(1)} %get-tuple-element.122.far, ...), custom_call_target="tpu_custom_call" | custom-call | flops 1 | bytes 1 | tf_op jit(solution)/shard_map/cross_stats/pallas_call | solution.py:512
  19.8 1.5 %collective-permute-start.8 = (f32[4,4,256]{2,1,0:T(4,128)S(1)}, f32[4,4,256]{2,1,0:T(4,128)S(1)}, u32[]{:S(2)}, u32[]{:S(2)}) collective-permute-start(f32[4,4,256]{2,1,0:T(4,128)S(1)} %get-tuple-element.133), channel_id=1, source_target_pairs={{0,2},{1,3},{2,0},{3,1},{4,6},{5,7},{6,4},{7,5},{8,10},{9,11},{10,... | collective-permute-start | bytes 49160 | tf_op jit(solution)/shard_map/ppermute | solution.py:805
  21.3 1.6 %near_grad.1 = (f32[256,512]{1,0:T(8,128)S(1)}, bf16[2,128,512]{2,1,0:T(8,128)(2,1)S(1)}, bf16[2,128,512]{2,1,0:T(8,128)(2,1)S(1)}, f32[1,256]{1,0:T(1,128)S(1)}) custom-call(bf16[4,256,512]{2,1,0:T(8,128)(2,1)S(1)} %get-tuple-element.124.near.pair, f32[3,8,256]{2,1,0:T(8,128)S(1)} %get-tuple-element.123.local, f32[3,4,256]{2,1,0:T(4,128)S(1)} %get-tuple-element.132.stats, ...), custom_call_target="tpu_custom_call" | custom-call | flops 1 | bytes 1 | tf_op jit(solution)/shard_map/near_grad/pallas_call | solution.py:579
  22.9 0.6 %collective-permute-done.8.heard = f32[4,4,256]{2,1,0:T(4,128)S(1)} collective-permute-done((f32[4,4,256]{2,1,0:T(4,128)S(1)}, f32[4,4,256]{2,1,0:T(4,128)S(1)}, u32[]{:S(2)}, u32[]{:S(2)}) %collective-permute-start.8) | collective-permute-done | bytes 16416 | tf_op jit(solution)/shard_map/ppermute | solution.py:805
  23.6 1.6 %cross_grad.1 = (bf16[2,128,512]{2,1,0:T(8,128)(2,1)S(1)}, bf16[2,128,512]{2,1,0:T(8,128)(2,1)S(1)}, bf16[256,512]{1,0:T(8,128)(2,1)S(1)}, bf16[2,256,512]{2,1,0...) custom-call(bf16[4,256,512]{2,1,0:T(8,128)(2,1)S(1)} %get-tuple-element.130.cross, ...), custom_call_target="tpu_custom_call" | custom-call | flops 1 | bytes 1 | tf_op jit(solution)/shard_map/cross_grad/pallas_call | solution.py:641
  25.2 1.4 %collective-permute-start.9 = (bf16[2,128,512]{2,1,0:T(8,128)(2,1)S(1)}, bf16[2,128,512]{2,1,0:T(8,128)(2,1)S(1)}, u32[]{:S(2)}, u32[]{:S(2)}) collective-permute-start(bf16[2,128,512]{2,1,0:T(8,128)(2,1)S(1)} %get-tuple-element.145), channel_id=1, source_target_pairs={{0,2},{1,3},{2,0},{3,1},{4,6},{5,7},{6,4},{7,5},{8,10},{9,11},{10,... | collective-permute-start | bytes 786440 | tf_op jit(solution)/shard_map/ppermute | solution.py:805
  26.6 13.0 %conditional.4 = (f32[1,128,2048]{2,1,0:T(8,128)}, f32[1,128,2048]{2,1,0:T(8,128)}, f32[1,128,2048]{2,1,0:T(8,128)}, bf16[2,128,512]{2,1,0:T(8,128)(2,1)}, bf16[...) conditional(s32[]{:T(128)} %bitcast.2, () %tuple.35, (s32[1,128]{1,0:T(1,128)S(1)}, bf16[4,256,512]{2,1,0:T(8,128)(2,1)S(1)}, ...), branch_computations={%region_2.0_spmd, %region_3.0_spmd} | conditional | flops 16388 | bytes 4462810 | solution.py:811
  26.6 5.6 %all-to-all-start = ((f32[32,1,512]{2,1,0:T(1,128)}), f32[32,1,512]{2,1,0:T(1,128)S(1)}, u32[]{:S(2)}, u32[]{:S(2)}) async-start(f32[32,1,512]{2,1,0:T(1,128)} %bitcast.1), calls=%async_computation | async-start | bytes 131072 | tf_op jit(solution)/shard_map/cond/branch_1_fun/all_to_all | solution.py:835
  32.2 4.2 %conditional = (f32[1,128,2048]{2,1,0:T(8,128)}, f32[1,128,2048]{2,1,0:T(8,128)}, f32[1,128,2048]{2,1,0:T(8,128)}, bf16[2,128,512]{2,1,0:T(8,128)(2,1)}, bf16[3,128,1024]{2,1,0:T(8,128)(2,1)}) conditional(s32[]{:T(128)} %bitcast, () %tuple.23, (bf16[4,256,512]{2,1,0:T(8,128)(2,1)S(1)}, f32[3,8,256]{2,1,0:T(8,128)S(1)}, f32[2,4,256]{2,1,0:T(4,128)S(1)}, ...), branch_computations={%region_4.0_spmd, %region_5.0_spmd} | conditional | flops 2 | bytes 4194360 | solution.py:811
  32.2 1.7 %far_grad.1 = (bf16[3,128,1024]{2,1,0:T(8,128)(2,1)S(1)}, bf16[3,128,1024]{2,1,0:T(8,128)(2,1)S(1)}) custom-call(bf16[4,256,512]{2,1,0:T(8,128)(2,1)S(1)} %get-tuple-element.45.pair, f32[3,8,256]{2,1,0:T(8,128)S(1)} %get-tuple-element.46.local, f32[2,4,256]{2,1,0:T(4,128)S(1)} %get-tuple-element.47.final, f32[1,256]{1,0:T(1,128)S(1)} %get-tuple-element.48.gates, ...), custom_call_target="tpu_custom_call" | custom-call | flops 1 | bytes 1 | tf_op jit(solution)/shard_map/cond/branch_1_fun/cond/branch_1_fun/far_grad/pallas_call | solution.py:687
  34.3 1.9 %own_join.1 = (f32[1,128,2048]{2,1,0:T(8,128)}, f32[1,128,2048]{2,1,0:T(8,128)}, f32[1,128,2048]{2,1,0:T(8,128)}, bf16[2,128,512]{2,1,0:T(8,128)(2,1)}) custom-call(bf16[3,128,1024]{2,1,0:T(8,128)(2,1)S(1)} %get-tuple-element.53.own), custom_call_target="tpu_custom_call" | custom-call | flops 1 | bytes 1 | tf_op jit(solution)/shard_map/cond/branch_1_fun/cond/branch_1_fun/own_join/pallas_call | solution.py:718
  36.4 3.2 %all-to-all-done = f32[32,1,512]{2,1,0:T(1,128)S(1)} async-done(((f32[32,1,512]{2,1,0:T(1,128)}), f32[32,1,512]{2,1,0:T(1,128)S(1)}, u32[]{:S(2)}, u32[]{:S(2)}) %all-to-all-start) | async-done | bytes 65568 | tf_op jit(solution)/shard_map/cond/branch_1_fun/all_to_all | solution.py:835
  39.7 2.4 %finish.1 = (f32[1,128,2048]{2,1,0:T(8,128)}, f32[1,128,2048]{2,1,0:T(8,128)}, f32[1,128,2048]{2,1,0:T(8,128)}) custom-call(bf16[2,128,512]{2,1,0:T(8,128)(2,1)} %get-tuple-element.143.waiting, bf16[3,128,1024]{2,1,0:T(8,128)(2,1)} %get-tuple-element.144.sib, ...), custom_call_target="tpu_custom_call", output_to_operand_aliasing={{0}: (4, {}), {1}: (5, {}), {2}: (6, {})} | custom-call | flops 1 | bytes 1 | tf_op jit(solution)/shard_map/finish/pallas_call | solution.py:780
  (23 shorter events, 1.4 us)
Async XLA Ops:
  0.6 5.9 %copy-start.1 = (s32[1,128]{1,0:T(1,128)S(1)}, s32[1,128]{1,0:T(1,128)}, u32[]{:S(2)}) copy-start(s32[1,128]{1,0:T(1,128)} %pos_ref.2) | copy-start | bytes 1540
  2.0 6.6 %copy-start = (bf16[1,128,4096]{2,1,0:T(8,128)(2,1)S(1)}, bf16[1,128,4096]{2,1,0:T(8,128)(2,1)}, u32[]{:S(2)}) copy-start(bf16[1,128,4096]{2,1,0:T(8,128)(2,1)} %x_ref.1) | copy-start | bytes 3145732
  2.0 16.3 %collective-permute-start.6 = (bf16[2,128,512]{2,1,0:T(8,128)(2,1)S(1)}, bf16[2,128,512]{2,1,0:T(8,128)(2,1)S(1)}, u32[]{:S(2)}, u32[]{:S(2)}) collective-permute-start(bf16[2,128,512]{2,1,0:T(8,128)(2,1)S(1)} %get-tuple-element.125), channel_id=1, source_target_pairs={{0,3},{1,2},{2,1},{3,0},{4,7},{5,6},{6,5},{7,4},{8,11},{9,10},{10,... | collective-permute-start | bytes 786440 | tf_op jit(solution)/shard_map/ppermute | solution.py:805
  4.4 13.9 %collective-permute-start.5 = (bf16[2,128,512]{2,1,0:T(8,128)(2,1)S(1)}, bf16[2,128,512]{2,1,0:T(8,128)(2,1)S(1)}, u32[]{:S(2)}, u32[]{:S(2)}) collective-permute-start(bf16[2,128,512]{2,1,0:T(8,128)(2,1)S(1)} %get-tuple-element.116), channel_id=1, source_target_pairs={{0,2},{1,3},{2,0},{3,1},{4,6},{5,7},{6,4},{7,5},{8,10},{9,11},{10,... | collective-permute-start | bytes 786440 | tf_op jit(solution)/shard_map/ppermute | solution.py:805
  5.0 3.6 %collective-permute-start.4 = (f32[1,512]{1,0:T(1,128)S(1)}, f32[1,512]{1,0:T(1,128)S(1)}, u32[]{:S(2)}, u32[]{:S(2)}) collective-permute-start(f32[1,512]{1,0:T(1,128)S(1)} %get-tuple-element.118), channel_id=1, source_target_pairs={{0,4},{4,0},{8,12},{12,8},{16,20},{20,16},{24,28},{28,24},{1,5},{5... | collective-permute-start | bytes 6152 | tf_op jit(solution)/shard_map/ppermute | solution.py:817
  8.7 4.2 %collective-permute-start.1 = (bf16[4,128,1024]{2,1,0:T(8,128)(2,1)S(1)}, bf16[4,128,1024]{2,1,0:T(8,128)(2,1)}, u32[]{:S(2)}, u32[]{:S(2)}) collective-permute-start(bf16[4,128,1024]{2,1,0:T(8,128)(2,1)S(1)} %get-tuple-element.42), channel_id=1, source_target_pairs={{0,1},{1,0},{2,3},{3,2},{4,5},{5,4},{6,7},{7,6},{8,9},{9,8},{10,11... | collective-permute-start | bytes 3145736 | tf_op jit(solution)/shard_map/cond/branch_1_fun/ppermute | solution.py:805
  8.7 4.3 %collective-permute-start.2 = (bf16[1,128,4096]{2,1,0:T(8,128)(2,1)S(1)}, bf16[1,128,4096]{2,1,0:T(8,128)(2,1)}, u32[]{:S(2)}, u32[]{:S(2)}) collective-permute-start(bf16[1,128,4096]{2,1,0:T(8,128)(2,1)S(1)} %get-tuple-element.43), channel_id=1, source_target_pairs={{0,1},{1,0},{2,3},{3,2},{4,5},{5,4},{6,7},{7,6},{8,9},{9,8},{10,11... | collective-permute-start | bytes 3145736 | tf_op jit(solution)/shard_map/cond/branch_1_fun/ppermute | solution.py:805
  9.2 3.6 %collective-permute-start.3 = (f32[1,1024]{1,0:T(1,128)S(1)}, f32[1,1024]{1,0:T(1,128)S(1)}, u32[]{:S(2)}, u32[]{:S(2)}) collective-permute-start(f32[1,1024]{1,0:T(1,128)S(1)} %get-tuple-element.44), channel_id=1, source_target_pairs={{0,8},{4,12},{8,0},{12,4},{16,24},{20,28},{24,16},{28,20},{1,9},{5... | collective-permute-start | bytes 12296 | tf_op jit(solution)/shard_map/cond/branch_1_fun/ppermute | solution.py:817
  13.0 5.3 %collective-permute-start.7 = (f32[1,2048]{1,0:T(1,128)S(1)}, f32[1,2048]{1,0:T(1,128)S(1)}, u32[]{:S(2)}, u32[]{:S(2)}) collective-permute-start(f32[1,2048]{1,0:T(1,128)S(1)} %get-tuple-element.128), channel_id=1, source_target_pairs={{0,16},{4,20},{8,24},{12,28},{16,0},{20,4},{24,8},{28,12},{1,17},{... | collective-permute-start | bytes 24584 | tf_op jit(solution)/shard_map/ppermute | solution.py:817
  19.8 3.8 %collective-permute-start.8 = (f32[4,4,256]{2,1,0:T(4,128)S(1)}, f32[4,4,256]{2,1,0:T(4,128)S(1)}, u32[]{:S(2)}, u32[]{:S(2)}) collective-permute-start(f32[4,4,256]{2,1,0:T(4,128)S(1)} %get-tuple-element.133), channel_id=1, source_target_pairs={{0,2},{1,3},{2,0},{3,1},{4,6},{5,7},{6,4},{7,5},{8,10},{9,11},{10,... | collective-permute-start | bytes 49160 | tf_op jit(solution)/shard_map/ppermute | solution.py:805
  25.2 14.5 %collective-permute-start.9 = (bf16[2,128,512]{2,1,0:T(8,128)(2,1)S(1)}, bf16[2,128,512]{2,1,0:T(8,128)(2,1)S(1)}, u32[]{:S(2)}, u32[]{:S(2)}) collective-permute-start(bf16[2,128,512]{2,1,0:T(8,128)(2,1)S(1)} %get-tuple-element.145), channel_id=1, source_target_pairs={{0,2},{1,3},{2,0},{3,1},{4,6},{5,7},{6,4},{7,5},{8,10},{9,11},{10,... | collective-permute-start | bytes 786440 | tf_op jit(solution)/shard_map/ppermute | solution.py:805
  26.6 13.1 %collective-permute-start.10 = (bf16[2,128,512]{2,1,0:T(8,128)(2,1)S(1)}, bf16[2,128,512]{2,1,0:T(8,128)(2,1)S(1)}, u32[]{:S(2)}, u32[]{:S(2)}) collective-permute-start(bf16[2,128,512]{2,1,0:T(8,128)(2,1)S(1)} %get-tuple-element.146), channel_id=1, source_target_pairs={{0,3},{1,2},{2,1},{3,0},{4,7},{5,6},{6,5},{7,4},{8,11},{9,10},{10,... | collective-permute-start | bytes 786440 | tf_op jit(solution)/shard_map/ppermute | solution.py:805
  26.6 13.0 %all-to-all-start = ((f32[32,1,512]{2,1,0:T(1,128)}), f32[32,1,512]{2,1,0:T(1,128)S(1)}, u32[]{:S(2)}, u32[]{:S(2)}) async-start(f32[32,1,512]{2,1,0:T(1,128)} %bitcast.1), calls=%async_computation | async-start | bytes 131072 | tf_op jit(solution)/shard_map/cond/branch_1_fun/all_to_all | solution.py:835
  33.9 2.5 %collective-permute-start = (bf16[3,128,1024]{2,1,0:T(8,128)(2,1)S(1)}, bf16[3,128,1024]{2,1,0:T(8,128)(2,1)}, u32[]{:S(2)}, u32[]{:S(2)}) collective-permute-start(bf16[3,128,1024]{2,1,0:T(8,128)(2,1)S(1)} %get-tuple-element.58), channel_id=1, source_target_pairs={{0,1},{1,0},{2,3},{3,2},{4,5},{5,4},{6,7},{7,6},{8,9},{9,8},{10,11... | collective-permute-start | bytes 2359304 | tf_op jit(solution)/shard_map/cond/branch_1_fun/cond/branch_1_fun/ppermute | solution.py:805
  39.7 2.4 %copy-start.2 = (f32[512]{0:T(512)}, f32[512]{0:T(512)S(1)}, u32[]{:S(2)}) copy-start(f32[512]{0:T(512)S(1)} %get-tuple-element.115) | copy-start | bytes 6148

commit v15 on v13

--- a/solution.py
+++ b/solution.py
@@ -856,11 +856,6 @@
         *outs, waiting = own_join(own_out, queries.shape)
         return outs, waiting, sib_in
 
-    def tail_phase(terms, *operands):
-        shared = lax.all_to_all(terms.reshape(ndp * n, 1, -1), ("dp", "ctx"), 0, 0, tiled=True)
-        results = beside(far_phase, *operands)
-        return *results, jnp.sum(shared, axis=0)[0] / float(ndp * n * slots // 2)
-
     out_s, out_d, w_part = cross_pack(route_pos, w_router, keys, values, queries, d_gated)
     in_s, in_d = send(out_s, 2), send(out_d, 3)
 
@@ -882,10 +877,10 @@
 
     ret_s, ret_d = send(back_s, 2), send(back_d, 3)
     terms = pair_router(gates, sums, rows_x, ndp, n)
-    outs, waiting, sib_in, router_grad = beside(
-        tail_phase, terms, far, local, final, gates, keep, dq_low, near_own, near_sib
-    )
+    shared = lax.all_to_all(terms.reshape(ndp * n, 1, -1), ("dp", "ctx"), 0, 0, tiled=True)
+    outs, waiting, sib_in = beside(far_phase, far, local, final, gates, keep, dq_low, near_own, near_sib)
     dq, dk, dv = finish(waiting, sib_in, ret_s, ret_d, outs)
+    router_grad = jnp.sum(after(shared, dq), axis=0)[0] / float(ndp * n * slots // 2)
     return dq, dk, dv, router_grad
 
 

time: 42.6 us -> 40.7 us (0.955)
  waiting for transfers between devices: 6.99 us -> 5.33 us
  Pallas kernels: 16.2 us -> 15.5 us
  other arithmetic: 0.11 us -> 0.68 us
    all_to_all x1, waiting for transfers between devices: 3.15 us -> 0.78 us  [swap_body(): lax.all_to_all(terms.reshape(ndp * n, 1, -1), ('dp', 'ctx'), 0, 0, tiled=...]
    ppermute x8, waiting for transfers between devices: 1.09 us -> 1.81 us  [send(): return lax.ppermute(a, 'ctx', [(i, i ^ flip) for i in range(n)])]
    pallas_call x1, Pallas kernels: 1.92 us -> 1.2 us  [own_join(): pl.pallas_call(own_join_kernel, out_shape=[out] * 3 + [jax.ShapeDtypeStru...]
    div x1, other arithmetic: 0.01 us -> 0.58 us  [swap_body(): jnp.sum(after(shared, dq), axis=0)[0] / float(ndp * n * slots // 2)]
  transfers between devices with their start and end apart: 12 -> 12, of which waited for: 6 -> 6; matrix products, arithmetic and copies ran while one was open for 0% -> 0% of each run, Pallas kernels for 26% -> 32%
where the time goes in v15:
time: 40.7 us; the launch traced here: 40.5 us
  starting transfers between devices  18.1 us (44%)
  Pallas kernels  15.5 us (38%)
  waiting for transfers between devices  5.33 us (13%)
  between operations  0.79 us (2%)
  other arithmetic  0.68 us (2%)
    ppermute x8, starting transfers between devices, send(): return lax.ppermute(a, 'ctx', [(i, i ^ flip) for i in range(n)])  6.85 us
    ppermute x3, starting transfers between devices, widen(): other = lax.ppermute(part, 'dp', [(i, i ^ step) for i in range(ndp)])  5.68 us
    all_to_all x1, starting transfers between devices, swap_body(): lax.all_to_all(terms.reshape(ndp * n, 1, -1), ('dp', 'ctx'), 0, 0, tiled=...  5.53 us
    ppermute x3, waiting for transfers between devices, widen(): other = lax.ppermute(part, 'dp', [(i, i ^ step) for i in range(ndp)])  2.74 us
    pallas_call x1, Pallas kernels, local_stats(): pl.pallas_call(functools.partial(local_stats_kernel, HEAD ** (-0.5)), out...  2.71 us
    pallas_call x1, Pallas kernels, finish(): pl.pallas_call(finish_kernel, out_shape=[pltpu.HBM(o.shape, F32) for o in...  2.39 us
    ppermute x8, waiting for transfers between devices, send(): return lax.ppermute(a, 'ctx', [(i, i ^ flip) for i in range(n)])  1.81 us
    pallas_call x1, Pallas kernels, far_grad(): pl.pallas_call(functools.partial(far_grad_kernel, HEAD ** (-0.5)), out_sh...  1.71 us
  transfers between devices with their start and end apart: 12, of which 6 were waited for; matrix products, arithmetic and copies ran while one was open for 0% of the time, Pallas kernels for 32%

profile of v15, /device:TPU:0, one launch (start us, length us, event | category | flops | bytes accessed | tf_op | source)
XLA Modules:
  0.0 40.5 jit_solution(11953860425750463199)
XLA Ops:
  0.6 1.3 %cross_pack.1 = (bf16[2,128,512]{2,1,0:T(8,128)(2,1)S(1)}, bf16[2,128,512]{2,1,0:T(8,128)(2,1)S(1)}, f32[1,512]{1,0:T(1,128)S(1)}) custom-call(s32[1,128]{1,0:T(1,128)} %pos_ref.2, bf16[512]{0:T(512)(128)(2,1)} %w_any.1, bf16[1,128,2048]{2,1,0:T(8,128)(2,1)} %k_ref.5, bf16[1,128,2048]{2,1,0:T(8,128)(2,1)} %v_ref.5, bf16[1,128,2048]{2,1,0:T(8,128)(2,1)} %q_ref.5, ...), custom_call_target="tpu_custom_call" | custom-call | flops 1 | bytes 1 | tf_op jit(solution)/shard_map/cross_pack/pallas_call | solution.py:314
  2.0 2.4 %collective-permute-start.6 = (bf16[2,128,512]{2,1,0:T(8,128)(2,1)S(1)}, bf16[2,128,512]{2,1,0:T(8,128)(2,1)S(1)}, u32[]{:S(2)}, u32[]{:S(2)}) collective-permute-start(bf16[2,128,512]{2,1,0:T(8,128)(2,1)S(1)} %get-tuple-element.90), channel_id=1, source_target_pairs={{0,3},{1,2},{2,1},{3,0},{4,7},{5,6},{6,5},{7,4},{8,11},{9,10},{10,... | collective-permute-start | bytes 786440 | tf_op jit(solution)/shard_map/ppermute | solution.py:830
  5.0 1.5 %collective-permute-start.4 = (f32[1,512]{1,0:T(1,128)S(1)}, f32[1,512]{1,0:T(1,128)S(1)}, u32[]{:S(2)}, u32[]{:S(2)}) collective-permute-start(f32[1,512]{1,0:T(1,128)S(1)} %get-tuple-element.83), channel_id=1, source_target_pairs={{0,4},{4,0},{8,12},{12,8},{16,20},{20,16},{24,28},{28,24},{1,5},{5... | collective-permute-start | bytes 6152 | tf_op jit(solution)/shard_map/ppermute | solution.py:842
  6.6 1.3 %sib_pack.1 = bf16[4,128,1024]{2,1,0:T(8,128)(2,1)S(1)} custom-call(s32[1,128]{1,0:T(1,128)S(1)} %copy-done, bf16[1,128,2048]{2,1,0:T(8,128)(2,1)} %k_ref.5, bf16[1,128,2048]{2,1,0:T(8,128)(2,1)} %v_ref.5, bf16[1,128,2048]{2,1,0:T(8,128)(2,1)} %q_ref.5, f32[1,128,2048]{2,1,0:T(8,128)} %dg_ref.5), custom_call_target="tpu_custom_call" | custom-call | flops 1 | bytes 1 | tf_op jit(solution)/shard_map/sib_pack/pallas_call | solution.py:350
  7.9 0.7 %collective-permute-done.4 = f32[1,512]{1,0:T(1,128)S(1)} collective-permute-done((f32[1,512]{1,0:T(1,128)S(1)}, f32[1,512]{1,0:T(1,128)S(1)}, u32[]{:S(2)}, u32[]{:S(2)}) %collective-permute-start.4) | collective-permute-done | bytes 2080 | tf_op jit(solution)/shard_map/ppermute | solution.py:842
  8.6 4.4 %conditional.2 = (bf16[4,128,1024]{2,1,0:T(8,128)(2,1)}, bf16[1,128,4096]{2,1,0:T(8,128)(2,1)}, f32[1,2048]{1,0:T(1,128)S(1)}) conditional(s32[]{:T(128)} %bitcast, () %tuple.29, (bf16[4,128,1024]{2,1,0:T(8,128)(2,1)S(1)}, bf16[1,128,4096]{2,1,0:T(8,128)(2,1)S(1)}, f32[1,1024]{1,0:T(1,128)S(1)}) %tuple.41), branch_computations={%region_0.0_spmd, %region_1.0_spmd} | conditional | flops 2048 | bytes 8421520 | solution.py:836
  9.2 1.6 %collective-permute-start.3 = (f32[1,1024]{1,0:T(1,128)S(1)}, f32[1,1024]{1,0:T(1,128)S(1)}, u32[]{:S(2)}, u32[]{:S(2)}) collective-permute-start(f32[1,1024]{1,0:T(1,128)S(1)} %get-tuple-element.24), channel_id=1, source_target_pairs={{0,8},{4,12},{8,0},{12,4},{16,24},{20,28},{24,16},{28,20},{1,9},{5... | collective-permute-start | bytes 12296 | tf_op jit(solution)/shard_map/cond/branch_1_fun/ppermute | solution.py:842
  10.8 2.0 %collective-permute-done.3 = f32[1,1024]{1,0:T(1,128)S(1)} collective-permute-done((f32[1,1024]{1,0:T(1,128)S(1)}, f32[1,1024]{1,0:T(1,128)S(1)}, u32[]{:S(2)}, u32[]{:S(2)}) %collective-permute-start.3) | collective-permute-done | bytes 4128 | tf_op jit(solution)/shard_map/cond/branch_1_fun/ppermute | solution.py:842
  13.0 2.6 %collective-permute-start.7 = (f32[1,2048]{1,0:T(1,128)S(1)}, f32[1,2048]{1,0:T(1,128)S(1)}, u32[]{:S(2)}, u32[]{:S(2)}) collective-permute-start(f32[1,2048]{1,0:T(1,128)S(1)} %get-tuple-element.96), channel_id=1, source_target_pairs={{0,16},{4,20},{8,24},{12,28},{16,0},{20,4},{24,8},{28,12},{1,17},{... | collective-permute-start | bytes 24584 | tf_op jit(solution)/shard_map/ppermute | solution.py:842
  15.6 2.7 %local_stats.1 = (f32[3,8,256]{2,1,0:T(8,128)S(1)}, f32[1,256]{1,0:T(1,128)S(1)}, bf16[4,256,512]{2,1,0:T(8,128)(2,1)S(1)}, bf16[4,256,512]{2,1,0:T(8,128)(2,1)S(1)}, bf16[2,128,4096]{2,1,0:T(8,128)(2,1)S(1)}) custom-call(s32[1,128]{1,0:T(1,128)S(1)} %copy-done, bf16[1,128,2048]{2,1,0:T(8,128)(2,1)} %k_ref.5, bf16[1,128,2048]{2,1,0:T(8,128)(2,1)} %v_ref.5, ...), custom_call_target="tpu_custom_call" | custom-call | flops 1 | bytes 1 | tf_op jit(solution)/shard_map/local_stats/pallas_call | solution.py:476
  18.3 0.8 %cross_stats.1 = (bf16[4,256,512]{2,1,0:T(8,128)(2,1)S(1)}, f32[3,4,256]{2,1,0:T(4,128)S(1)}, bf16[2,4,256,256]{3,2,1,0:T(8,128)(2,1)S(1)}) custom-call(bf16[4,256,512]{2,1,0:T(8,128)(2,1)S(1)} %get-tuple-element.89.near.pair, bf16[4,256,512]{2,1,0:T(8,128)(2,1)S(1)} %get-tuple-element.87.far, bf16[2,128,512]{2,1,0:T(8,128)(2,1)S(1)} %collective-permute-done.5.straight, ...), custom_call_target="tpu_custom_call" | custom-call | flops 1 | bytes 1 | tf_op jit(solution)/shard_map/cross_stats/pallas_call | solution.py:525
  19.9 1.5 %collective-permute-start.8 = (f32[4,4,256]{2,1,0:T(4,128)S(1)}, f32[4,4,256]{2,1,0:T(4,128)S(1)}, u32[]{:S(2)}, u32[]{:S(2)}) collective-permute-start(f32[4,4,256]{2,1,0:T(4,128)S(1)} %get-tuple-element.98), channel_id=1, source_target_pairs={{0,2},{1,3},{2,0},{3,1},{4,6},{5,7},{6,4},{7,5},{8,10},{9,11},{10,... | collective-permute-start | bytes 49160 | tf_op jit(solution)/shard_map/ppermute | solution.py:830
  21.3 1.6 %near_grad.1 = (f32[256,512]{1,0:T(8,128)S(1)}, bf16[2,128,512]{2,1,0:T(8,128)(2,1)S(1)}, bf16[2,128,512]{2,1,0:T(8,128)(2,1)S(1)}, f32[1,256]{1,0:T(1,128)S(1)}) custom-call(bf16[4,256,512]{2,1,0:T(8,128)(2,1)S(1)} %get-tuple-element.89.near.pair, f32[3,8,256]{2,1,0:T(8,128)S(1)} %get-tuple-element.88.local, f32[3,4,256]{2,1,0:T(4,128)S(1)} %get-tuple-element.93.stats, ...), custom_call_target="tpu_custom_call" | custom-call | flops 1 | bytes 1 | tf_op jit(solution)/shard_map/near_grad/pallas_call | solution.py:590
  23.0 0.7 %collective-permute-done.8.heard = f32[4,4,256]{2,1,0:T(4,128)S(1)} collective-permute-done((f32[4,4,256]{2,1,0:T(4,128)S(1)}, f32[4,4,256]{2,1,0:T(4,128)S(1)}, u32[]{:S(2)}, u32[]{:S(2)}) %collective-permute-start.8) | collective-permute-done | bytes 16416 | tf_op jit(solution)/shard_map/ppermute | solution.py:830
  23.7 0.7 %cross_grad.1 = (bf16[2,128,512]{2,1,0:T(8,128)(2,1)S(1)}, bf16[2,128,512]{2,1,0:T(8,128)(2,1)S(1)}, bf16[256,512]{1,0:T(8,128)(2,1)S(1)}, bf16[2,256,512]{2,1,0...) custom-call(bf16[4,256,512]{2,1,0:T(8,128)(2,1)S(1)} %get-tuple-element.91.cross, ...), custom_call_target="tpu_custom_call" | custom-call | flops 1 | bytes 1 | tf_op jit(solution)/shard_map/cross_grad/pallas_call | solution.py:635
  24.4 1.5 %collective-permute-start.9 = (bf16[2,128,512]{2,1,0:T(8,128)(2,1)S(1)}, bf16[2,128,512]{2,1,0:T(8,128)(2,1)S(1)}, u32[]{:S(2)}, u32[]{:S(2)}) collective-permute-start(bf16[2,128,512]{2,1,0:T(8,128)(2,1)S(1)} %get-tuple-element.109), channel_id=1, source_target_pairs={{0,2},{1,3},{2,0},{3,1},{4,6},{5,7},{6,4},{7,5},{8,10},{9,11},{10,... | collective-permute-start | bytes 786440 | tf_op jit(solution)/shard_map/ppermute | solution.py:830
  25.8 1.0 %router_terms.1 = f32[8,4,1,512]{3,2,1,0:T(1,128)} custom-call(f32[1,256]{1,0:T(1,128)S(1)} %get-tuple-element.99.gates.gates_ref, f32[1,256]{1,0:T(1,128)S(1)} %get-tuple-element.117.sum_ref, bf16[2,128,4096]{2,1,0:T(8,128)(2,1)S(1)} %get-tuple-element.95.rows_x), custom_call_target="tpu_custom_call" | custom-call | flops 1 | bytes 1 | tf_op jit(solution)/shard_map/router_terms/pallas_call | solution.py:814
  26.9 5.5 %all-to-all-start = ((f32[32,1,512]{2,1,0:T(1,128)}), f32[32,1,512]{2,1,0:T(1,128)S(1)}, u32[]{:S(2)}, u32[]{:S(2)}) async-start(f32[32,1,512]{2,1,0:T(1,128)} %bitcast.1), calls=%async_computation | async-start | bytes 131072 | tf_op jit(solution)/shard_map/all_to_all | solution.py:880
  32.4 4.2 %conditional.3 = (f32[1,128,2048]{2,1,0:T(8,128)}, f32[1,128,2048]{2,1,0:T(8,128)}, f32[1,128,2048]{2,1,0:T(8,128)}, bf16[2,128,512]{2,1,0:T(8,128)(2,1)S(1)}, bf16[3,128,1024]{2,1,0:T(8,128)(2,1)}) conditional(s32[]{:T(128)} %bitcast, () %tuple.28, (bf16[4,256,512]{2,1,0:T(8,128)(2,1)S(1)}, f32[3,8,256]{2,1,0:T(8,128)S(1)}, ...), branch_computations={%region_2.0_spmd, %region_3.0_spmd} | conditional | flops 2 | bytes 4194360 | solution.py:836
  32.4 1.7 %far_grad.1 = (bf16[3,128,1024]{2,1,0:T(8,128)(2,1)S(1)}, bf16[3,128,1024]{2,1,0:T(8,128)(2,1)S(1)}) custom-call(bf16[4,256,512]{2,1,0:T(8,128)(2,1)S(1)} %get-tuple-element.25.pair, f32[3,8,256]{2,1,0:T(8,128)S(1)} %get-tuple-element.26.local, f32[2,4,256]{2,1,0:T(4,128)S(1)} %get-tuple-element.27.final, f32[1,256]{1,0:T(1,128)S(1)} %get-tuple-element.28.gates, ...), custom_call_target="tpu_custom_call" | custom-call | flops 1 | bytes 1 | tf_op jit(solution)/shard_map/cond/branch_1_fun/far_grad/pallas_call | solution.py:681
  34.5 1.2 %own_join.1 = (f32[1,128,2048]{2,1,0:T(8,128)}, f32[1,128,2048]{2,1,0:T(8,128)}, f32[1,128,2048]{2,1,0:T(8,128)}, bf16[2,128,512]{2,1,0:T(8,128)(2,1)S(1)}) custom-call(bf16[3,128,1024]{2,1,0:T(8,128)(2,1)S(1)} %get-tuple-element.33.own), custom_call_target="tpu_custom_call" | custom-call | flops 1 | bytes 1 | tf_op jit(solution)/shard_map/cond/branch_1_fun/own_join/pallas_call | solution.py:712
  35.7 1.0 %collective-permute-done = bf16[3,128,1024]{2,1,0:T(8,128)(2,1)} collective-permute-done((bf16[3,128,1024]{2,1,0:T(8,128)(2,1)S(1)}, bf16[3,128,1024]{2,1,0:T(8,128)(2,1)}, u32[]{:S(2)}, u32[]{:S(2)}) %collective-permute-start) | collective-permute-done | bytes 786464 | tf_op jit(solution)/shard_map/cond/branch_1_fun/ppermute | solution.py:830
  36.6 2.4 %finish.1 = (f32[1,128,2048]{2,1,0:T(8,128)}, f32[1,128,2048]{2,1,0:T(8,128)}, f32[1,128,2048]{2,1,0:T(8,128)}) custom-call(bf16[2,128,512]{2,1,0:T(8,128)(2,1)S(1)} %get-tuple-element.107.waiting, bf16[3,128,1024]{2,1,0:T(8,128)(2,1)} %get-tuple-element.108.sib, ...), custom_call_target="tpu_custom_call", output_to_operand_aliasing={{0}: (4, {}), {1}: (5, {}), {2}: (6, {})} | custom-call | flops 1 | bytes 1 | tf_op jit(solution)/shard_map/finish/pallas_call | solution.py:774
  39.0 0.8 %all-to-all-done = f32[32,1,512]{2,1,0:T(1,128)S(1)} async-done(((f32[32,1,512]{2,1,0:T(1,128)}), f32[32,1,512]{2,1,0:T(1,128)S(1)}, u32[]{:S(2)}, u32[]{:S(2)}) %all-to-all-start) | async-done | bytes 65568 | tf_op jit(solution)/shard_map/all_to_all | solution.py:880
  (22 shorter events, 3.1 us)
Async XLA Ops:
  0.6 5.9 %copy-start = (s32[1,128]{1,0:T(1,128)S(1)}, s32[1,128]{1,0:T(1,128)}, u32[]{:S(2)}) copy-start(s32[1,128]{1,0:T(1,128)} %pos_ref.2) | copy-start | bytes 1540
  2.0 6.6 %copy-start.1 = (bf16[1,128,4096]{2,1,0:T(8,128)(2,1)S(1)}, bf16[1,128,4096]{2,1,0:T(8,128)(2,1)}, u32[]{:S(2)}) copy-start(bf16[1,128,4096]{2,1,0:T(8,128)(2,1)} %x_ref.1) | copy-start | bytes 3145732
  2.0 16.3 %collective-permute-start.6 = (bf16[2,128,512]{2,1,0:T(8,128)(2,1)S(1)}, bf16[2,128,512]{2,1,0:T(8,128)(2,1)S(1)}, u32[]{:S(2)}, u32[]{:S(2)}) collective-permute-start(bf16[2,128,512]{2,1,0:T(8,128)(2,1)S(1)} %get-tuple-element.90), channel_id=1, source_target_pairs={{0,3},{1,2},{2,1},{3,0},{4,7},{5,6},{6,5},{7,4},{8,11},{9,10},{10,... | collective-permute-start | bytes 786440 | tf_op jit(solution)/shard_map/ppermute | solution.py:830
  4.4 13.9 %collective-permute-start.5 = (bf16[2,128,512]{2,1,0:T(8,128)(2,1)S(1)}, bf16[2,128,512]{2,1,0:T(8,128)(2,1)S(1)}, u32[]{:S(2)}, u32[]{:S(2)}) collective-permute-start(bf16[2,128,512]{2,1,0:T(8,128)(2,1)S(1)} %get-tuple-element.81), channel_id=1, source_target_pairs={{0,2},{1,3},{2,0},{3,1},{4,6},{5,7},{6,4},{7,5},{8,10},{9,11},{10,... | collective-permute-start | bytes 786440 | tf_op jit(solution)/shard_map/ppermute | solution.py:830
  5.0 3.6 %collective-permute-start.4 = (f32[1,512]{1,0:T(1,128)S(1)}, f32[1,512]{1,0:T(1,128)S(1)}, u32[]{:S(2)}, u32[]{:S(2)}) collective-permute-start(f32[1,512]{1,0:T(1,128)S(1)} %get-tuple-element.83), channel_id=1, source_target_pairs={{0,4},{4,0},{8,12},{12,8},{16,20},{20,16},{24,28},{28,24},{1,5},{5... | collective-permute-start | bytes 6152 | tf_op jit(solution)/shard_map/ppermute | solution.py:842
  8.7 4.2 %collective-permute-start.1 = (bf16[4,128,1024]{2,1,0:T(8,128)(2,1)S(1)}, bf16[4,128,1024]{2,1,0:T(8,128)(2,1)}, u32[]{:S(2)}, u32[]{:S(2)}) collective-permute-start(bf16[4,128,1024]{2,1,0:T(8,128)(2,1)S(1)} %get-tuple-element.22), channel_id=1, source_target_pairs={{0,1},{1,0},{2,3},{3,2},{4,5},{5,4},{6,7},{7,6},{8,9},{9,8},{10,11... | collective-permute-start | bytes 3145736 | tf_op jit(solution)/shard_map/cond/branch_1_fun/ppermute | solution.py:830
  8.7 4.3 %collective-permute-start.2 = (bf16[1,128,4096]{2,1,0:T(8,128)(2,1)S(1)}, bf16[1,128,4096]{2,1,0:T(8,128)(2,1)}, u32[]{:S(2)}, u32[]{:S(2)}) collective-permute-start(bf16[1,128,4096]{2,1,0:T(8,128)(2,1)S(1)} %get-tuple-element.23), channel_id=1, source_target_pairs={{0,1},{1,0},{2,3},{3,2},{4,5},{5,4},{6,7},{7,6},{8,9},{9,8},{10,11... | collective-permute-start | bytes 3145736 | tf_op jit(solution)/shard_map/cond/branch_1_fun/ppermute | solution.py:830
  9.2 3.6 %collective-permute-start.3 = (f32[1,1024]{1,0:T(1,128)S(1)}, f32[1,1024]{1,0:T(1,128)S(1)}, u32[]{:S(2)}, u32[]{:S(2)}) collective-permute-start(f32[1,1024]{1,0:T(1,128)S(1)} %get-tuple-element.24), channel_id=1, source_target_pairs={{0,8},{4,12},{8,0},{12,4},{16,24},{20,28},{24,16},{28,20},{1,9},{5... | collective-permute-start | bytes 12296 | tf_op jit(solution)/shard_map/cond/branch_1_fun/ppermute | solution.py:842
  13.0 6.1 %collective-permute-start.7 = (f32[1,2048]{1,0:T(1,128)S(1)}, f32[1,2048]{1,0:T(1,128)S(1)}, u32[]{:S(2)}, u32[]{:S(2)}) collective-permute-start(f32[1,2048]{1,0:T(1,128)S(1)} %get-tuple-element.96), channel_id=1, source_target_pairs={{0,16},{4,20},{8,24},{12,28},{16,0},{20,4},{24,8},{28,12},{1,17},{... | collective-permute-start | bytes 24584 | tf_op jit(solution)/shard_map/ppermute | solution.py:842
  19.9 3.8 %collective-permute-start.8 = (f32[4,4,256]{2,1,0:T(4,128)S(1)}, f32[4,4,256]{2,1,0:T(4,128)S(1)}, u32[]{:S(2)}, u32[]{:S(2)}) collective-permute-start(f32[4,4,256]{2,1,0:T(4,128)S(1)} %get-tuple-element.98), channel_id=1, source_target_pairs={{0,2},{1,3},{2,0},{3,1},{4,6},{5,7},{6,4},{7,5},{8,10},{9,11},{10,... | collective-permute-start | bytes 49160 | tf_op jit(solution)/shard_map/ppermute | solution.py:830
  24.4 12.3 %collective-permute-start.9 = (bf16[2,128,512]{2,1,0:T(8,128)(2,1)S(1)}, bf16[2,128,512]{2,1,0:T(8,128)(2,1)S(1)}, u32[]{:S(2)}, u32[]{:S(2)}) collective-permute-start(bf16[2,128,512]{2,1,0:T(8,128)(2,1)S(1)} %get-tuple-element.109), channel_id=1, source_target_pairs={{0,2},{1,3},{2,0},{3,1},{4,6},{5,7},{6,4},{7,5},{8,10},{9,11},{10,... | collective-permute-start | bytes 786440 | tf_op jit(solution)/shard_map/ppermute | solution.py:830
  25.8 10.8 %collective-permute-start.10 = (bf16[2,128,512]{2,1,0:T(8,128)(2,1)S(1)}, bf16[2,128,512]{2,1,0:T(8,128)(2,1)S(1)}, u32[]{:S(2)}, u32[]{:S(2)}) collective-permute-start(bf16[2,128,512]{2,1,0:T(8,128)(2,1)S(1)} %get-tuple-element.110), channel_id=1, source_target_pairs={{0,3},{1,2},{2,1},{3,0},{4,7},{5,6},{6,5},{7,4},{8,11},{9,10},{10,... | collective-permute-start | bytes 786440 | tf_op jit(solution)/shard_map/ppermute | solution.py:830
  26.9 12.9 %all-to-all-start = ((f32[32,1,512]{2,1,0:T(1,128)}), f32[32,1,512]{2,1,0:T(1,128)S(1)}, u32[]{:S(2)}, u32[]{:S(2)}) async-start(f32[32,1,512]{2,1,0:T(1,128)} %bitcast.1), calls=%async_computation | async-start | bytes 131072 | tf_op jit(solution)/shard_map/all_to_all | solution.py:880
  34.1 2.5 %collective-permute-start = (bf16[3,128,1024]{2,1,0:T(8,128)(2,1)S(1)}, bf16[3,128,1024]{2,1,0:T(8,128)(2,1)}, u32[]{:S(2)}, u32[]{:S(2)}) collective-permute-start(bf16[3,128,1024]{2,1,0:T(8,128)(2,1)S(1)} %get-tuple-element.38), channel_id=1, source_target_pairs={{0,1},{1,0},{2,3},{3,2},{4,5},{5,4},{6,7},{7,6},{8,9},{9,8},{10,11... | collective-permute-start | bytes 2359304 | tf_op jit(solution)/shard_map/cond/branch_1_fun/ppermute | solution.py:830

commit v16 on v15

--- a/solution.py
+++ b/solution.py
@@ -598,7 +598,23 @@
     )(pair, local, stats, gates)
 
 
-def cross_grad_kernel(scale, cross, kept, stats, local, heard, gates, near_dq, near_sum, straight, diag, dq_out, keep, final, sum_out):
+def put_terms(grad, rows_x, out_ref):
+    high = grad.astype(BF16)
+    rest = grad - high.astype(F32)
+    mid = rest.astype(BF16)
+    low = (rest - mid.astype(F32)).astype(BF16)
+    slots = rows_x.shape[1]
+    row = lax.broadcasted_iota(jnp.int32, (8, grad.shape[1]), 0)
+    lhs = jnp.where(row == 0, high.astype(F32), jnp.where(row == 1, mid.astype(F32), jnp.where(row == 2, low.astype(F32), 0.0)))
+    lhs = lhs.astype(BF16)
+    term = jnp.sum(nn(lhs[:, :slots], rows_x[0]) + nn(lhs[:, slots:], rows_x[1]), axis=0, keepdims=True)
+    parts, copies, _, chunk = out_ref.shape
+    for j in range(parts):
+        for i in range(copies):
+            out_ref[j, i] = term[:, j * chunk : (j + 1) * chunk]
+
+
+def cross_grad_kernel(scale, total, cross, kept, stats, local, heard, gates, near_dq, near_sum, rows_x, straight, diag, dq_out, keep, final, terms, held, sem):
     slots, width = straight.shape[1], straight.shape[2]
     heads = width // HEAD
     first = here()[1] == 0
@@ -610,7 +626,10 @@
     factor, delta = merge(mine, choose(first, other, near))
     factor = factor * jnp.where(first, heard[3], jnp.broadcast_to(gates[...], factor.shape))
     final[0], final[1] = merge(far, choose(first, NONE, other))
-    sum_out[...] = near_sum[...] + jnp.sum(final[1], axis=0, keepdims=True)
+    sums = near_sum[...] + jnp.sum(final[1], axis=0, keepdims=True)
+    put_terms(sums * gates[...] * (1.0 - gates[...]) * (1.0 / total), rows_x, held)
+    leaving = pltpu.make_async_copy(held, terms, sem)
+    leaving.start()
     for h in range(heads):
         cols = slice(h * HEAD, (h + 1) * HEAD)
         row = slice(h, h + 1)
@@ -626,28 +645,31 @@
         diag[0, :, cols] = sent[slots:]
         straight[1, :, cols] = dv[:slots].astype(BF16)
         diag[1, :, cols] = dv[slots:].astype(BF16)
-
-
-def cross_grad(cross, kept, stats, local, heard, gates, near_dq, near_sum):
+    leaving.wait()
+
+
+def cross_grad(cross, kept, stats, local, heard, gates, near_dq, near_sum, rows_x, parts, copies, total):
     _, rows, width = cross.shape
     slots = rows // 2
     out = pltpu.VMEM((2, slots, width), BF16)
-    return pl.pallas_call(
-        functools.partial(cross_grad_kernel, HEAD**-0.5),
+    spread = (parts, copies, 1, rows_x.shape[2] // parts)
+    return pl.pallas_call(
+        functools.partial(cross_grad_kernel, HEAD**-0.5, total),
         out_shape=[
             out,
             out,
             pltpu.VMEM((rows, width), BF16),
             pltpu.VMEM((2, rows, width), BF16),
             jax.ShapeDtypeStruct((2, width // HEAD, rows), F32),
-            jax.ShapeDtypeStruct((1, rows), F32),
+            pltpu.HBM(spread, F32),
         ],
-        in_specs=[VMEM] * 8,
-        out_specs=[VMEM] * 6,
+        in_specs=[VMEM] * 9,
+        out_specs=[VMEM] * 5 + [pl.BlockSpec(memory_space=pltpu.HBM)],
+        scratch_shapes=[pltpu.VMEM(spread, F32), pltpu.SemaphoreType.DMA],
         compiler_params=params(),
         cost_estimate=cost(24 * slots * slots * width, 64 * slots * width),
         name="cross_grad",
-    )(cross, kept, stats, local, heard, gates, near_dq, near_sum)
+    )(cross, kept, stats, local, heard, gates, near_dq, near_sum, rows_x)
 
 
 def far_grad_kernel(scale, pair, local, final, gates, keep, near_dq, near_own, near_sib, own_out, sib_out):
@@ -791,37 +813,6 @@
     )(waiting, sib, straight, diag, *in_hbm(*outs))
 
 
-def pair_router_kernel(gates_ref, sum_ref, rows_x, out_ref):
-    gates = gates_ref[...]
-    grad = sum_ref[...] * gates * (1.0 - gates)
-    high = grad.astype(BF16)
-    rest = grad - high.astype(F32)
-    mid = rest.astype(BF16)
-    low = (rest - mid.astype(F32)).astype(BF16)
-    slots = rows_x.shape[1]
-    row = lax.broadcasted_iota(jnp.int32, (8, grad.shape[1]), 0)
-    lhs = jnp.where(row == 0, high.astype(F32), jnp.where(row == 1, mid.astype(F32), jnp.where(row == 2, low.astype(F32), 0.0)))
-    lhs = lhs.astype(BF16)
-    term = jnp.sum(nn(lhs[:, :slots], rows_x[0]) + nn(lhs[:, slots:], rows_x[1]), axis=0, keepdims=True)
-    parts, copies, _, chunk = out_ref.shape
-    for j in range(parts):
-        for i in range(copies):
-            out_ref[j, i] = term[:, j * chunk : (j + 1) * chunk]
-
-
-def pair_router(gates, sums, rows_x, parts, copies):
-    chunk = rows_x.shape[-1] // parts
-    return pl.pallas_call(
-        pair_router_kernel,
-        out_shape=jax.ShapeDtypeStruct((parts, copies, 1, chunk), F32),
-        in_specs=[VMEM] * 3,
-        out_specs=VMEM,
-        compiler_params=params(),
-        cost_estimate=cost(32 * rows_x.size, rows_x.size * 4),
-        name="router_terms",
-    )(gates, sums, rows_x)
-
-
 def swap_body(route_pos, x_routed, w_router, queries, keys, values, d_gated):
     slots = queries.shape[1]
     n, ndp = lax.axis_size("ctx"), lax.axis_size("dp")
@@ -871,16 +862,16 @@
 
     heard = send(message, 2)
     near_dq, near_own, near_sib, near_sum = near_grad(near, local, stats, gates)
-    back_s, back_d, dq_low, keep, final, sums = cross_grad(
-        cross, kept, stats, local, heard, gates, near_dq, near_sum
+    total = float(ndp * n * slots // 2)
+    back_s, back_d, dq_low, keep, final, terms = cross_grad(
+        cross, kept, stats, local, heard, gates, near_dq, near_sum, rows_x, ndp, n, total
     )
 
     ret_s, ret_d = send(back_s, 2), send(back_d, 3)
-    terms = pair_router(gates, sums, rows_x, ndp, n)
     shared = lax.all_to_all(terms.reshape(ndp * n, 1, -1), ("dp", "ctx"), 0, 0, tiled=True)
     outs, waiting, sib_in = beside(far_phase, far, local, final, gates, keep, dq_low, near_own, near_sib)
     dq, dk, dv = finish(waiting, sib_in, ret_s, ret_d, outs)
-    router_grad = jnp.sum(after(shared, dq), axis=0)[0] / float(ndp * n * slots // 2)
+    router_grad = jnp.sum(after(shared, dq), axis=(0, 1))
     return dq, dk, dv, router_grad
 
 

time: 40.7 us -> 41.1 us (level)
  the two profiles are of different devices: /device:TPU:0 before, /device:TPU:1 now
where the time goes in v16:
time: 41.1 us; the launch traced here: 40.9 us
  starting transfers between devices  18.9 us (46%)
  Pallas kernels  14.9 us (36%)
  waiting for transfers between devices  5.47 us (13%)
  between operations  0.82 us (2%)
  other arithmetic  0.68 us (2%)
    ppermute x8, starting transfers between devices, send(): return lax.ppermute(a, 'ctx', [(i, i ^ flip) for i in range(n)])  8.72 us
    ppermute x3, starting transfers between devices, widen(): other = lax.ppermute(part, 'dp', [(i, i ^ step) for i in range(ndp)])  5.14 us
    all_to_all x1, starting transfers between devices, swap_body(): lax.all_to_all(terms.reshape(ndp * n, 1, -1), ('dp', 'ctx'), 0, 0, tiled=...  5.06 us
    ppermute x8, waiting for transfers between devices, send(): return lax.ppermute(a, 'ctx', [(i, i ^ flip) for i in range(n)])  4.3 us
    pallas_call x1, Pallas kernels, local_stats(): pl.pallas_call(functools.partial(local_stats_kernel, HEAD ** (-0.5)), out...  2.69 us
    pallas_call x1, Pallas kernels, finish(): pl.pallas_call(finish_kernel, out_shape=[pltpu.HBM(o.shape, F32) for o in...  2.39 us
    pallas_call x1, Pallas kernels, far_grad(): pl.pallas_call(functools.partial(far_grad_kernel, HEAD ** (-0.5)), out_sh...  1.71 us
    pallas_call x1, Pallas kernels, near_grad(): pl.pallas_call(functools.partial(near_grad_kernel, HEAD ** (-0.5)), out_s...  1.64 us
  transfers between devices with their start and end apart: 12, of which 4 were waited for; matrix products, arithmetic and copies ran while one was open for 0% of the time, Pallas kernels for 29%

profile of v16, /device:TPU:1, one launch (start us, length us, event | category | flops | bytes accessed | tf_op | source)
XLA Modules:
  0.0 40.9 jit_solution(17772180713293286391)
XLA Ops:
  0.6 1.3 %cross_pack.1 = (bf16[2,128,512]{2,1,0:T(8,128)(2,1)S(1)}, bf16[2,128,512]{2,1,0:T(8,128)(2,1)S(1)}, f32[1,512]{1,0:T(1,128)S(1)}) custom-call(s32[1,128]{1,0:T(1,128)} %pos_ref.2, bf16[512]{0:T(512)(128)(2,1)} %w_any.1, bf16[1,128,2048]{2,1,0:T(8,128)(2,1)} %k_ref.5, bf16[1,128,2048]{2,1,0:T(8,128)(2,1)} %v_ref.5, bf16[1,128,2048]{2,1,0:T(8,128)(2,1)} %q_ref.5, ...), custom_call_target="tpu_custom_call" | custom-call | flops 1 | bytes 1 | tf_op jit(solution)/shard_map/cross_pack/pallas_call | solution.py:314
  2.0 2.6 %collective-permute-start.6 = (bf16[2,128,512]{2,1,0:T(8,128)(2,1)S(1)}, bf16[2,128,512]{2,1,0:T(8,128)(2,1)S(1)}, u32[]{:S(2)}, u32[]{:S(2)}) collective-permute-start(bf16[2,128,512]{2,1,0:T(8,128)(2,1)S(1)} %get-tuple-element.90), channel_id=1, source_target_pairs={{0,3},{1,2},{2,1},{3,0},{4,7},{5,6},{6,5},{7,4},{8,11},{9,10},{10,... | collective-permute-start | bytes 786440 | tf_op jit(solution)/shard_map/ppermute | solution.py:821
  4.6 1.5 %collective-permute-start.4 = (f32[1,512]{1,0:T(1,128)S(1)}, f32[1,512]{1,0:T(1,128)S(1)}, u32[]{:S(2)}, u32[]{:S(2)}) collective-permute-start(f32[1,512]{1,0:T(1,128)S(1)} %get-tuple-element.83), channel_id=1, source_target_pairs={{0,4},{4,0},{8,12},{12,8},{16,20},{20,16},{24,28},{28,24},{1,5},{5... | collective-permute-start | bytes 6152 | tf_op jit(solution)/shard_map/ppermute | solution.py:833
  6.2 1.3 %sib_pack.1 = bf16[4,128,1024]{2,1,0:T(8,128)(2,1)S(1)} custom-call(s32[1,128]{1,0:T(1,128)S(1)} %copy-done, bf16[1,128,2048]{2,1,0:T(8,128)(2,1)} %k_ref.5, bf16[1,128,2048]{2,1,0:T(8,128)(2,1)} %v_ref.5, bf16[1,128,2048]{2,1,0:T(8,128)(2,1)} %q_ref.5, f32[1,128,2048]{2,1,0:T(8,128)} %dg_ref.5), custom_call_target="tpu_custom_call" | custom-call | flops 1 | bytes 1 | tf_op jit(solution)/shard_map/sib_pack/pallas_call | solution.py:350
  7.6 5.1 %conditional.2 = (bf16[4,128,1024]{2,1,0:T(8,128)(2,1)}, bf16[1,128,4096]{2,1,0:T(8,128)(2,1)}, f32[1,2048]{1,0:T(1,128)S(1)}) conditional(s32[]{:T(128)} %bitcast, () %tuple.29, (bf16[4,128,1024]{2,1,0:T(8,128)(2,1)S(1)}, bf16[1,128,4096]{2,1,0:T(8,128)(2,1)S(1)}, f32[1,1024]{1,0:T(1,128)S(1)}) %tuple.41), branch_computations={%region_0.0_spmd, %region_1.0_spmd} | conditional | flops 2048 | bytes 8421520 | solution.py:827
  7.6 1.2 %collective-permute-start.1 = (bf16[4,128,1024]{2,1,0:T(8,128)(2,1)S(1)}, bf16[4,128,1024]{2,1,0:T(8,128)(2,1)}, u32[]{:S(2)}, u32[]{:S(2)}) collective-permute-start(bf16[4,128,1024]{2,1,0:T(8,128)(2,1)S(1)} %get-tuple-element.22), channel_id=1, source_target_pairs={{0,1},{1,0},{2,3},{3,2},{4,5},{5,4},{6,7},{7,6},{8,9},{9,8},{10,11... | collective-permute-start | bytes 3145736 | tf_op jit(solution)/shard_map/cond/branch_1_fun/ppermute | solution.py:821
  8.9 1.3 %collective-permute-start.3 = (f32[1,1024]{1,0:T(1,128)S(1)}, f32[1,1024]{1,0:T(1,128)S(1)}, u32[]{:S(2)}, u32[]{:S(2)}) collective-permute-start(f32[1,1024]{1,0:T(1,128)S(1)} %get-tuple-element.24), channel_id=1, source_target_pairs={{0,8},{4,12},{8,0},{12,4},{16,24},{20,28},{24,16},{28,20},{1,9},{5... | collective-permute-start | bytes 12296 | tf_op jit(solution)/shard_map/cond/branch_1_fun/ppermute | solution.py:833
  10.2 1.2 %collective-permute-done.3 = f32[1,1024]{1,0:T(1,128)S(1)} collective-permute-done((f32[1,1024]{1,0:T(1,128)S(1)}, f32[1,1024]{1,0:T(1,128)S(1)}, u32[]{:S(2)}, u32[]{:S(2)}) %collective-permute-start.3) | collective-permute-done | bytes 4128 | tf_op jit(solution)/shard_map/cond/branch_1_fun/ppermute | solution.py:833
  11.3 1.4 %collective-permute-done.2 = bf16[1,128,4096]{2,1,0:T(8,128)(2,1)} collective-permute-done((bf16[1,128,4096]{2,1,0:T(8,128)(2,1)S(1)}, bf16[1,128,4096]{2,1,0:T(8,128)(2,1)}, u32[]{:S(2)}, u32[]{:S(2)}) %collective-permute-start.2) | collective-permute-done | bytes 1048608 | tf_op jit(solution)/shard_map/cond/branch_1_fun/ppermute | solution.py:821
  12.7 2.3 %collective-permute-start.7 = (f32[1,2048]{1,0:T(1,128)S(1)}, f32[1,2048]{1,0:T(1,128)S(1)}, u32[]{:S(2)}, u32[]{:S(2)}) collective-permute-start(f32[1,2048]{1,0:T(1,128)S(1)} %get-tuple-element.96), channel_id=1, source_target_pairs={{0,16},{4,20},{8,24},{12,28},{16,0},{20,4},{24,8},{28,12},{1,17},{... | collective-permute-start | bytes 24584 | tf_op jit(solution)/shard_map/ppermute | solution.py:833
  15.0 2.7 %local_stats.1 = (f32[3,8,256]{2,1,0:T(8,128)S(1)}, f32[1,256]{1,0:T(1,128)S(1)}, bf16[4,256,512]{2,1,0:T(8,128)(2,1)S(1)}, bf16[4,256,512]{2,1,0:T(8,128)(2,1)S(1)}, bf16[2,128,4096]{2,1,0:T(8,128)(2,1)S(1)}) custom-call(s32[1,128]{1,0:T(1,128)S(1)} %copy-done, bf16[1,128,2048]{2,1,0:T(8,128)(2,1)} %k_ref.5, bf16[1,128,2048]{2,1,0:T(8,128)(2,1)} %v_ref.5, ...), custom_call_target="tpu_custom_call" | custom-call | flops 1 | bytes 1 | tf_op jit(solution)/shard_map/local_stats/pallas_call | solution.py:476
  17.7 0.8 %cross_stats.1 = (bf16[4,256,512]{2,1,0:T(8,128)(2,1)S(1)}, f32[3,4,256]{2,1,0:T(4,128)S(1)}, bf16[2,4,256,256]{3,2,1,0:T(8,128)(2,1)S(1)}) custom-call(bf16[4,256,512]{2,1,0:T(8,128)(2,1)S(1)} %get-tuple-element.89.near.pair, bf16[4,256,512]{2,1,0:T(8,128)(2,1)S(1)} %get-tuple-element.87.far, bf16[2,128,512]{2,1,0:T(8,128)(2,1)S(1)} %collective-permute-done.5.straight, ...), custom_call_target="tpu_custom_call" | custom-call | flops 1 | bytes 1 | tf_op jit(solution)/shard_map/cross_stats/pallas_call | solution.py:525
  19.3 1.2 %collective-permute-start.8 = (f32[4,4,256]{2,1,0:T(4,128)S(1)}, f32[4,4,256]{2,1,0:T(4,128)S(1)}, u32[]{:S(2)}, u32[]{:S(2)}) collective-permute-start(f32[4,4,256]{2,1,0:T(4,128)S(1)} %get-tuple-element.98), channel_id=1, source_target_pairs={{0,2},{1,3},{2,0},{3,1},{4,6},{5,7},{6,4},{7,5},{8,10},{9,11},{10,... | collective-permute-start | bytes 49160 | tf_op jit(solution)/shard_map/ppermute | solution.py:821
  20.4 1.6 %near_grad.1 = (f32[256,512]{1,0:T(8,128)S(1)}, bf16[2,128,512]{2,1,0:T(8,128)(2,1)S(1)}, bf16[2,128,512]{2,1,0:T(8,128)(2,1)S(1)}, f32[1,256]{1,0:T(1,128)S(1)}) custom-call(bf16[4,256,512]{2,1,0:T(8,128)(2,1)S(1)} %get-tuple-element.89.near.pair, f32[3,8,256]{2,1,0:T(8,128)S(1)} %get-tuple-element.88.local, f32[3,4,256]{2,1,0:T(4,128)S(1)} %get-tuple-element.93.stats, ...), custom_call_target="tpu_custom_call" | custom-call | flops 1 | bytes 1 | tf_op jit(solution)/shard_map/near_grad/pallas_call | solution.py:590
  22.1 1.1 %cross_grad.1 = (bf16[2,128,512]{2,1,0:T(8,128)(2,1)S(1)}, bf16[2,128,512]{2,1,0:T(8,128)(2,1)S(1)}, bf16[256,512]{1,0:T(8,128)(2,1)S(1)}, bf16[2,256,512]{2,1,0...) custom-call(bf16[4,256,512]{2,1,0:T(8,128)(2,1)S(1)} %get-tuple-element.91.cross, ...), custom_call_target="tpu_custom_call" | custom-call | flops 1 | bytes 1 | tf_op jit(solution)/shard_map/cross_grad/pallas_call | solution.py:656
  23.2 1.0 %collective-permute-start.9 = (bf16[2,128,512]{2,1,0:T(8,128)(2,1)S(1)}, bf16[2,128,512]{2,1,0:T(8,128)(2,1)S(1)}, u32[]{:S(2)}, u32[]{:S(2)}) collective-permute-start(bf16[2,128,512]{2,1,0:T(8,128)(2,1)S(1)} %get-tuple-element.109), channel_id=1, source_target_pairs={{0,2},{1,3},{2,0},{3,1},{4,6},{5,7},{6,4},{7,5},{8,10},{9,11},{10,... | collective-permute-start | bytes 786440 | tf_op jit(solution)/shard_map/ppermute | solution.py:821
  24.2 2.3 %collective-permute-start.10 = (bf16[2,128,512]{2,1,0:T(8,128)(2,1)S(1)}, bf16[2,128,512]{2,1,0:T(8,128)(2,1)S(1)}, u32[]{:S(2)}, u32[]{:S(2)}) collective-permute-start(bf16[2,128,512]{2,1,0:T(8,128)(2,1)S(1)} %get-tuple-element.110), channel_id=1, source_target_pairs={{0,3},{1,2},{2,1},{3,0},{4,7},{5,6},{6,5},{7,4},{8,11},{9,10},{10,... | collective-permute-start | bytes 786440 | tf_op jit(solution)/shard_map/ppermute | solution.py:821
  26.5 5.1 %all-to-all-start = ((f32[32,1,512]{2,1,0:T(1,128)}), f32[32,1,512]{2,1,0:T(1,128)S(1)}, u32[]{:S(2)}, u32[]{:S(2)}) async-start(f32[32,1,512]{2,1,0:T(1,128)} %bitcast.4), calls=%async_computation | async-start | bytes 131072 | tf_op jit(solution)/shard_map/all_to_all | solution.py:871
  31.6 4.2 %conditional.3 = (f32[1,128,2048]{2,1,0:T(8,128)}, f32[1,128,2048]{2,1,0:T(8,128)}, f32[1,128,2048]{2,1,0:T(8,128)}, bf16[2,128,512]{2,1,0:T(8,128)(2,1)S(1)}, bf16[3,128,1024]{2,1,0:T(8,128)(2,1)}) conditional(s32[]{:T(128)} %bitcast, () %tuple.28, (bf16[4,256,512]{2,1,0:T(8,128)(2,1)S(1)}, f32[3,8,256]{2,1,0:T(8,128)S(1)}, ...), branch_computations={%region_2.0_spmd, %region_3.0_spmd} | conditional | flops 2 | bytes 4194360 | solution.py:827
  31.6 1.7 %far_grad.1 = (bf16[3,128,1024]{2,1,0:T(8,128)(2,1)S(1)}, bf16[3,128,1024]{2,1,0:T(8,128)(2,1)S(1)}) custom-call(bf16[4,256,512]{2,1,0:T(8,128)(2,1)S(1)} %get-tuple-element.25.pair, f32[3,8,256]{2,1,0:T(8,128)S(1)} %get-tuple-element.26.local, f32[2,4,256]{2,1,0:T(4,128)S(1)} %get-tuple-element.27.final, f32[1,256]{1,0:T(1,128)S(1)} %get-tuple-element.28.gates, ...), custom_call_target="tpu_custom_call" | custom-call | flops 1 | bytes 1 | tf_op jit(solution)/shard_map/cond/branch_1_fun/far_grad/pallas_call | solution.py:703
  33.7 1.2 %own_join.1 = (f32[1,128,2048]{2,1,0:T(8,128)}, f32[1,128,2048]{2,1,0:T(8,128)}, f32[1,128,2048]{2,1,0:T(8,128)}, bf16[2,128,512]{2,1,0:T(8,128)(2,1)S(1)}) custom-call(bf16[3,128,1024]{2,1,0:T(8,128)(2,1)S(1)} %get-tuple-element.33.own), custom_call_target="tpu_custom_call" | custom-call | flops 1 | bytes 1 | tf_op jit(solution)/shard_map/cond/branch_1_fun/own_join/pallas_call | solution.py:734
  34.9 1.0 %collective-permute-done = bf16[3,128,1024]{2,1,0:T(8,128)(2,1)} collective-permute-done((bf16[3,128,1024]{2,1,0:T(8,128)(2,1)S(1)}, bf16[3,128,1024]{2,1,0:T(8,128)(2,1)}, u32[]{:S(2)}, u32[]{:S(2)}) %collective-permute-start) | collective-permute-done | bytes 786464 | tf_op jit(solution)/shard_map/cond/branch_1_fun/ppermute | solution.py:821
  35.8 2.0 %collective-permute-done.10.diag = bf16[2,128,512]{2,1,0:T(8,128)(2,1)S(1)} collective-permute-done((bf16[2,128,512]{2,1,0:T(8,128)(2,1)S(1)}, bf16[2,128,512]{2,1,0:T(8,128)(2,1)S(1)}, u32[]{:S(2)}, u32[]{:S(2)}) %collective-permute-start.10) | collective-permute-done | bytes 262176 | tf_op jit(solution)/shard_map/ppermute | solution.py:821
  37.8 2.4 %finish.1 = (f32[1,128,2048]{2,1,0:T(8,128)}, f32[1,128,2048]{2,1,0:T(8,128)}, f32[1,128,2048]{2,1,0:T(8,128)}) custom-call(bf16[2,128,512]{2,1,0:T(8,128)(2,1)S(1)} %get-tuple-element.107.waiting, bf16[3,128,1024]{2,1,0:T(8,128)(2,1)} %get-tuple-element.108.sib, ...), custom_call_target="tpu_custom_call", output_to_operand_aliasing={{0}: (4, {}), {1}: (5, {}), {2}: (6, {})} | custom-call | flops 1 | bytes 1 | tf_op jit(solution)/shard_map/finish/pallas_call | solution.py:796
  (20 shorter events, 1.8 us)
Async XLA Ops:
  0.6 5.5 %copy-start = (s32[1,128]{1,0:T(1,128)S(1)}, s32[1,128]{1,0:T(1,128)}, u32[]{:S(2)}) copy-start(s32[1,128]{1,0:T(1,128)} %pos_ref.2) | copy-start | bytes 1540
  2.0 5.6 %copy-start.1 = (bf16[1,128,4096]{2,1,0:T(8,128)(2,1)S(1)}, bf16[1,128,4096]{2,1,0:T(8,128)(2,1)}, u32[]{:S(2)}) copy-start(bf16[1,128,4096]{2,1,0:T(8,128)(2,1)} %x_ref.1) | copy-start | bytes 3145732
  2.0 15.7 %collective-permute-start.6 = (bf16[2,128,512]{2,1,0:T(8,128)(2,1)S(1)}, bf16[2,128,512]{2,1,0:T(8,128)(2,1)S(1)}, u32[]{:S(2)}, u32[]{:S(2)}) collective-permute-start(bf16[2,128,512]{2,1,0:T(8,128)(2,1)S(1)} %get-tuple-element.90), channel_id=1, source_target_pairs={{0,3},{1,2},{2,1},{3,0},{4,7},{5,6},{6,5},{7,4},{8,11},{9,10},{10,... | collective-permute-start | bytes 786440 | tf_op jit(solution)/shard_map/ppermute | solution.py:821
  4.6 13.1 %collective-permute-start.5 = (bf16[2,128,512]{2,1,0:T(8,128)(2,1)S(1)}, bf16[2,128,512]{2,1,0:T(8,128)(2,1)S(1)}, u32[]{:S(2)}, u32[]{:S(2)}) collective-permute-start(bf16[2,128,512]{2,1,0:T(8,128)(2,1)S(1)} %get-tuple-element.81), channel_id=1, source_target_pairs={{0,2},{1,3},{2,0},{3,1},{4,6},{5,7},{6,4},{7,5},{8,10},{9,11},{10,... | collective-permute-start | bytes 786440 | tf_op jit(solution)/shard_map/ppermute | solution.py:821
  4.6 2.9 %collective-permute-start.4 = (f32[1,512]{1,0:T(1,128)S(1)}, f32[1,512]{1,0:T(1,128)S(1)}, u32[]{:S(2)}, u32[]{:S(2)}) collective-permute-start(f32[1,512]{1,0:T(1,128)S(1)} %get-tuple-element.83), channel_id=1, source_target_pairs={{0,4},{4,0},{8,12},{12,8},{16,20},{20,16},{24,28},{28,24},{1,5},{5... | collective-permute-start | bytes 6152 | tf_op jit(solution)/shard_map/ppermute | solution.py:833
  7.6 3.8 %collective-permute-start.1 = (bf16[4,128,1024]{2,1,0:T(8,128)(2,1)S(1)}, bf16[4,128,1024]{2,1,0:T(8,128)(2,1)}, u32[]{:S(2)}, u32[]{:S(2)}) collective-permute-start(bf16[4,128,1024]{2,1,0:T(8,128)(2,1)S(1)} %get-tuple-element.22), channel_id=1, source_target_pairs={{0,1},{1,0},{2,3},{3,2},{4,5},{5,4},{6,7},{7,6},{8,9},{9,8},{10,11... | collective-permute-start | bytes 3145736 | tf_op jit(solution)/shard_map/cond/branch_1_fun/ppermute | solution.py:821
  8.8 3.9 %collective-permute-start.2 = (bf16[1,128,4096]{2,1,0:T(8,128)(2,1)S(1)}, bf16[1,128,4096]{2,1,0:T(8,128)(2,1)}, u32[]{:S(2)}, u32[]{:S(2)}) collective-permute-start(bf16[1,128,4096]{2,1,0:T(8,128)(2,1)S(1)} %get-tuple-element.23), channel_id=1, source_target_pairs={{0,1},{1,0},{2,3},{3,2},{4,5},{5,4},{6,7},{7,6},{8,9},{9,8},{10,11... | collective-permute-start | bytes 3145736 | tf_op jit(solution)/shard_map/cond/branch_1_fun/ppermute | solution.py:821
  8.9 2.5 %collective-permute-start.3 = (f32[1,1024]{1,0:T(1,128)S(1)}, f32[1,1024]{1,0:T(1,128)S(1)}, u32[]{:S(2)}, u32[]{:S(2)}) collective-permute-start(f32[1,1024]{1,0:T(1,128)S(1)} %get-tuple-element.24), channel_id=1, source_target_pairs={{0,8},{4,12},{8,0},{12,4},{16,24},{20,28},{24,16},{28,20},{1,9},{5... | collective-permute-start | bytes 12296 | tf_op jit(solution)/shard_map/cond/branch_1_fun/ppermute | solution.py:833
  12.7 5.8 %collective-permute-start.7 = (f32[1,2048]{1,0:T(1,128)S(1)}, f32[1,2048]{1,0:T(1,128)S(1)}, u32[]{:S(2)}, u32[]{:S(2)}) collective-permute-start(f32[1,2048]{1,0:T(1,128)S(1)} %get-tuple-element.96), channel_id=1, source_target_pairs={{0,16},{4,20},{8,24},{12,28},{16,0},{20,4},{24,8},{28,12},{1,17},{... | collective-permute-start | bytes 24584 | tf_op jit(solution)/shard_map/ppermute | solution.py:833
  19.3 2.8 %collective-permute-start.8 = (f32[4,4,256]{2,1,0:T(4,128)S(1)}, f32[4,4,256]{2,1,0:T(4,128)S(1)}, u32[]{:S(2)}, u32[]{:S(2)}) collective-permute-start(f32[4,4,256]{2,1,0:T(4,128)S(1)} %get-tuple-element.98), channel_id=1, source_target_pairs={{0,2},{1,3},{2,0},{3,1},{4,6},{5,7},{6,4},{7,5},{8,10},{9,11},{10,... | collective-permute-start | bytes 49160 | tf_op jit(solution)/shard_map/ppermute | solution.py:821
  23.2 12.6 %collective-permute-start.9 = (bf16[2,128,512]{2,1,0:T(8,128)(2,1)S(1)}, bf16[2,128,512]{2,1,0:T(8,128)(2,1)S(1)}, u32[]{:S(2)}, u32[]{:S(2)}) collective-permute-start(bf16[2,128,512]{2,1,0:T(8,128)(2,1)S(1)} %get-tuple-element.109), channel_id=1, source_target_pairs={{0,2},{1,3},{2,0},{3,1},{4,6},{5,7},{6,4},{7,5},{8,10},{9,11},{10,... | collective-permute-start | bytes 786440 | tf_op jit(solution)/shard_map/ppermute | solution.py:821
  24.2 13.6 %collective-permute-start.10 = (bf16[2,128,512]{2,1,0:T(8,128)(2,1)S(1)}, bf16[2,128,512]{2,1,0:T(8,128)(2,1)S(1)}, u32[]{:S(2)}, u32[]{:S(2)}) collective-permute-start(bf16[2,128,512]{2,1,0:T(8,128)(2,1)S(1)} %get-tuple-element.110), channel_id=1, source_target_pairs={{0,3},{1,2},{2,1},{3,0},{4,7},{5,6},{6,5},{7,4},{8,11},{9,10},{10,... | collective-permute-start | bytes 786440 | tf_op jit(solution)/shard_map/ppermute | solution.py:821
  26.5 13.7 %all-to-all-start = ((f32[32,1,512]{2,1,0:T(1,128)}), f32[32,1,512]{2,1,0:T(1,128)S(1)}, u32[]{:S(2)}, u32[]{:S(2)}) async-start(f32[32,1,512]{2,1,0:T(1,128)} %bitcast.4), calls=%async_computation | async-start | bytes 131072 | tf_op jit(solution)/shard_map/all_to_all | solution.py:871
  33.3 2.5 %collective-permute-start = (bf16[3,128,1024]{2,1,0:T(8,128)(2,1)S(1)}, bf16[3,128,1024]{2,1,0:T(8,128)(2,1)}, u32[]{:S(2)}, u32[]{:S(2)}) collective-permute-start(bf16[3,128,1024]{2,1,0:T(8,128)(2,1)S(1)} %get-tuple-element.38), channel_id=1, source_target_pairs={{0,1},{1,0},{2,3},{3,2},{4,5},{5,4},{6,7},{7,6},{8,9},{9,8},{10,11... | collective-permute-start | bytes 2359304 | tf_op jit(solution)/shard_map/cond/branch_1_fun/ppermute | solution.py:821

commit v17 on v16

--- a/solution.py
+++ b/solution.py
@@ -743,74 +743,91 @@
     )(own)
 
 
-def finish_kernel(waiting, sib, straight, diag, dq_in, dk_in, dv_in, dq_out, dk_out, dv_out, low, held, total, added, in_sems, out_sems):
+def sib_join_kernel(sib, dq_in, dk_in, dv_in, dq_out, dk_out, dv_out, waiting, low, total, in_sems, out_sems):
     half = sib.shape[2]
     width = half // 2
     core, chip = here()
-    early, late = jnp.where(chip == 0, 1.0, 0.0), jnp.where(chip == 0, 0.0, 1.0)
     loads = [pltpu.make_async_copy(sib.at[j], low.at[j], in_sems.at[j]) for j in range(3)]
-    loads += [pltpu.make_async_copy(waiting.at[j], held.at[j], in_sems.at[3 + j]) for j in range(2)]
     for c in loads:
         c.start()
     cols = pl.ds(pl.multiple_of((1 - core) * half, HEAD), half)
     stores = []
     for j, out in enumerate((dq_out, dk_out, dv_out)):
         loads[j].wait()
-        first, second = low[j, :, :width].astype(F32), low[j, :, width:].astype(F32)
-        if j == 0:
-            second = second + late * diag[0].astype(F32)
-        else:
-            first = first + early * diag[j - 1].astype(F32)
-        total[j, :, :width] = first
-        total[j, :, width:] = second
+        total[j] = low[j].astype(F32)
         stores.append(pltpu.make_async_copy(total.at[j], out.at[0, :, cols], out_sems.at[j]))
         stores[-1].start()
-    for j in range(2):
-        loads[3 + j].wait()
-        added[j] = held[j].astype(F32) + straight[j].astype(F32)
-
-    def store(j, out, offset):
-        at = pl.ds(pl.multiple_of(core * half + offset, HEAD), width)
-        copy = pltpu.make_async_copy(added.at[j], out.at[0, :, at], out_sems.at[3 + j])
+    waiting[0] = jnp.where(chip == 0, total[1, :, :width], total[0, :, width:]).astype(BF16)
+    waiting[1] = low[2, :, :width]
+    for c in stores:
+        c.wait()
+
+
+def sib_join(sib, outs):
+    _, slots, half = sib.shape
+    hbm = pl.BlockSpec(memory_space=pltpu.HBM)
+    return pl.pallas_call(
+        sib_join_kernel,
+        out_shape=[pltpu.HBM(o.shape, F32) for o in outs] + [pltpu.VMEM((2, slots, half // 2), BF16)],
+        in_specs=[pl.BlockSpec(memory_space=pl.ANY)] + [hbm] * 3,
+        out_specs=[hbm] * 3 + [VMEM],
+        scratch_shapes=[
+            pltpu.VMEM((3, slots, half), BF16),
+            pltpu.VMEM((3, slots, half), F32),
+            pltpu.SemaphoreType.DMA((3,)),
+            pltpu.SemaphoreType.DMA((3,)),
+        ],
+        input_output_aliases={1: 0, 2: 1, 3: 2},
+        compiler_params=params(),
+        cost_estimate=cost(0, 12 * sib.size),
+        name="sib_join",
+    )(sib, *in_hbm(*outs))
+
+
+def add_back_kernel(own, sib, straight, diag, dq_in, dk_in, dv_in, dq_out, dk_out, dv_out, total, sems):
+    width = straight.shape[2]
+    core, chip = here()
+    ends = ((own, straight, 2 * core * width), (sib, diag, 2 * (1 - core) * width))
+
+    def store(i, j, out, offset):
+        cols = pl.ds(pl.multiple_of(ends[i][2] + offset, HEAD), width)
+        copy = pltpu.make_async_copy(total.at[i, j], out.at[0, :, cols], sems.at[2 * i + j])
         copy.start()
         return copy
 
     @pl.when(chip == 0)
     def _():
-        copies = [store(0, dk_out, 0), store(1, dv_out, 0)]
+        copies = []
+        for i, (waiting, back, _) in enumerate(ends):
+            for j, out in enumerate((dk_out, dv_out)):
+                total[i, j] = waiting[j].astype(F32) + back[j].astype(F32)
+                copies.append(store(i, j, out, 0))
         for c in copies:
             c.wait()
 
     @pl.when(chip != 0)
     def _():
-        store(0, dq_out, width).wait()
-
-    for c in stores:
-        c.wait()
-
-
-def finish(waiting, sib, straight, diag, outs):
-    _, slots, half = sib.shape
+        copies = []
+        for i, (waiting, back, _) in enumerate(ends):
+            total[i, 0] = waiting[0].astype(F32) + back[0].astype(F32)
+            copies.append(store(i, 0, dq_out, width))
+        for c in copies:
+            c.wait()
+
+
+def add_back(own, sib, straight, diag, outs):
     hbm = pl.BlockSpec(memory_space=pltpu.HBM)
-    anywhere = pl.BlockSpec(memory_space=pl.ANY)
-    return pl.pallas_call(
-        finish_kernel,
+    return pl.pallas_call(
+        add_back_kernel,
         out_shape=[pltpu.HBM(o.shape, F32) for o in outs],
-        in_specs=[anywhere] * 2 + [VMEM] * 2 + [hbm] * 3,
+        in_specs=[VMEM] * 4 + [hbm] * 3,
         out_specs=[hbm] * 3,
-        scratch_shapes=[
-            pltpu.VMEM((3, slots, half), BF16),
-            pltpu.VMEM(waiting.shape, BF16),
-            pltpu.VMEM((3, slots, half), F32),
-            pltpu.VMEM(waiting.shape, F32),
-            pltpu.SemaphoreType.DMA((5,)),
-            pltpu.SemaphoreType.DMA((5,)),
-        ],
+        scratch_shapes=[pltpu.VMEM((2, *own.shape), F32), pltpu.SemaphoreType.DMA((4,))],
         input_output_aliases={4: 0, 5: 1, 6: 2},
         compiler_params=params(),
-        cost_estimate=cost(0, 12 * sib.size),
-        name="finish",
-    )(waiting, sib, straight, diag, *in_hbm(*outs))
+        cost_estimate=cost(0, 24 * own.size),
+        name="add_back",
+    )(own, sib, straight, diag, *in_hbm(*outs))
 
 
 def swap_body(route_pos, x_routed, w_router, queries, keys, values, d_gated):
@@ -870,7 +887,8 @@
     ret_s, ret_d = send(back_s, 2), send(back_d, 3)
     shared = lax.all_to_all(terms.reshape(ndp * n, 1, -1), ("dp", "ctx"), 0, 0, tiled=True)
     outs, waiting, sib_in = beside(far_phase, far, local, final, gates, keep, dq_low, near_own, near_sib)
-    dq, dk, dv = finish(waiting, sib_in, ret_s, ret_d, outs)
+    *outs, waiting_sib = sib_join(sib_in, outs)
+    dq, dk, dv = add_back(waiting, waiting_sib, ret_s, ret_d, outs)
     router_grad = jnp.sum(after(shared, dq), axis=(0, 1))
     return dq, dk, dv, router_grad
 

time: 41.1 us -> 40.2 us (0.978)
  the two profiles are of different devices: /device:TPU:1 before, /device:TPU:0 now
where the time goes in v17:
time: 40.2 us; the launch traced here: 39.9 us
  starting transfers between devices  18.1 us (45%)
  Pallas kernels  15.7 us (39%)
  waiting for transfers between devices  4.57 us (11%)
  between operations  0.82 us (2%)
  other arithmetic  0.68 us (2%)
    ppermute x8, starting transfers between devices, send(): return lax.ppermute(a, 'ctx', [(i, i ^ flip) for i in range(n)])  6.84 us
    ppermute x3, starting transfers between devices, widen(): other = lax.ppermute(part, 'dp', [(i, i ^ step) for i in range(ndp)])  5.68 us
    all_to_all x1, starting transfers between devices, swap_body(): lax.all_to_all(terms.reshape(ndp * n, 1, -1), ('dp', 'ctx'), 0, 0, tiled=...  5.55 us
    ppermute x3, waiting for transfers between devices, widen(): other = lax.ppermute(part, 'dp', [(i, i ^ step) for i in range(ndp)])  2.74 us
    pallas_call x1, Pallas kernels, local_stats(): pl.pallas_call(functools.partial(local_stats_kernel, HEAD ** (-0.5)), out...  2.69 us
    pallas_call x1, Pallas kernels, sib_join(): pl.pallas_call(sib_join_kernel, out_shape=[pltpu.HBM(o.shape, F32) for o...  2.17 us
    ppermute x8, waiting for transfers between devices, send(): return lax.ppermute(a, 'ctx', [(i, i ^ flip) for i in range(n)])  1.82 us
    pallas_call x1, Pallas kernels, far_grad(): pl.pallas_call(functools.partial(far_grad_kernel, HEAD ** (-0.5)), out_sh...  1.72 us
  transfers between devices with their start and end apart: 12, of which 5 were waited for; matrix products, arithmetic and copies ran while one was open for 0% of the time, Pallas kernels for 31%

profile of v17, /device:TPU:0, one launch (start us, length us, event | category | flops | bytes accessed | tf_op | source)
XLA Modules:
  0.0 39.9 jit_solution(9621650654865438711)
XLA Ops:
  0.6 1.3 %cross_pack.1 = (bf16[2,128,512]{2,1,0:T(8,128)(2,1)S(1)}, bf16[2,128,512]{2,1,0:T(8,128)(2,1)S(1)}, f32[1,512]{1,0:T(1,128)S(1)}) custom-call(s32[1,128]{1,0:T(1,128)} %pos_ref.2, bf16[512]{0:T(512)(128)(2,1)} %w_any.1, bf16[1,128,2048]{2,1,0:T(8,128)(2,1)} %k_ref.5, bf16[1,128,2048]{2,1,0:T(8,128)(2,1)} %v_ref.5, bf16[1,128,2048]{2,1,0:T(8,128)(2,1)} %q_ref.5, ...), custom_call_target="tpu_custom_call" | custom-call | flops 1 | bytes 1 | tf_op jit(solution)/shard_map/cross_pack/pallas_call | solution.py:314
  2.0 2.4 %collective-permute-start.6 = (bf16[2,128,512]{2,1,0:T(8,128)(2,1)S(1)}, bf16[2,128,512]{2,1,0:T(8,128)(2,1)S(1)}, u32[]{:S(2)}, u32[]{:S(2)}) collective-permute-start(bf16[2,128,512]{2,1,0:T(8,128)(2,1)S(1)} %get-tuple-element.94), channel_id=1, source_target_pairs={{0,3},{1,2},{2,1},{3,0},{4,7},{5,6},{6,5},{7,4},{8,11},{9,10},{10,... | collective-permute-start | bytes 786440 | tf_op jit(solution)/shard_map/ppermute | solution.py:838
  5.0 1.5 %collective-permute-start.4 = (f32[1,512]{1,0:T(1,128)S(1)}, f32[1,512]{1,0:T(1,128)S(1)}, u32[]{:S(2)}, u32[]{:S(2)}) collective-permute-start(f32[1,512]{1,0:T(1,128)S(1)} %get-tuple-element.87), channel_id=1, source_target_pairs={{0,4},{4,0},{8,12},{12,8},{16,20},{20,16},{24,28},{28,24},{1,5},{5... | collective-permute-start | bytes 6152 | tf_op jit(solution)/shard_map/ppermute | solution.py:850
  6.6 1.3 %sib_pack.1 = bf16[4,128,1024]{2,1,0:T(8,128)(2,1)S(1)} custom-call(s32[1,128]{1,0:T(1,128)S(1)} %copy-done, bf16[1,128,2048]{2,1,0:T(8,128)(2,1)} %k_ref.5, bf16[1,128,2048]{2,1,0:T(8,128)(2,1)} %v_ref.5, bf16[1,128,2048]{2,1,0:T(8,128)(2,1)} %q_ref.5, f32[1,128,2048]{2,1,0:T(8,128)} %dg_ref.5), custom_call_target="tpu_custom_call" | custom-call | flops 1 | bytes 1 | tf_op jit(solution)/shard_map/sib_pack/pallas_call | solution.py:350
  7.9 0.7 %collective-permute-done.4 = f32[1,512]{1,0:T(1,128)S(1)} collective-permute-done((f32[1,512]{1,0:T(1,128)S(1)}, f32[1,512]{1,0:T(1,128)S(1)}, u32[]{:S(2)}, u32[]{:S(2)}) %collective-permute-start.4) | collective-permute-done | bytes 2080 | tf_op jit(solution)/shard_map/ppermute | solution.py:850
  8.6 4.4 %conditional.2 = (bf16[4,128,1024]{2,1,0:T(8,128)(2,1)}, bf16[1,128,4096]{2,1,0:T(8,128)(2,1)}, f32[1,2048]{1,0:T(1,128)S(1)}) conditional(s32[]{:T(128)} %bitcast, () %tuple.29, (bf16[4,128,1024]{2,1,0:T(8,128)(2,1)S(1)}, bf16[1,128,4096]{2,1,0:T(8,128)(2,1)S(1)}, f32[1,1024]{1,0:T(1,128)S(1)}) %tuple.41), branch_computations={%region_0.0_spmd, %region_1.0_spmd} | conditional | flops 2048 | bytes 8421520 | solution.py:844
  9.2 1.6 %collective-permute-start.3 = (f32[1,1024]{1,0:T(1,128)S(1)}, f32[1,1024]{1,0:T(1,128)S(1)}, u32[]{:S(2)}, u32[]{:S(2)}) collective-permute-start(f32[1,1024]{1,0:T(1,128)S(1)} %get-tuple-element.24), channel_id=1, source_target_pairs={{0,8},{4,12},{8,0},{12,4},{16,24},{20,28},{24,16},{28,20},{1,9},{5... | collective-permute-start | bytes 12296 | tf_op jit(solution)/shard_map/cond/branch_1_fun/ppermute | solution.py:850
  10.8 2.0 %collective-permute-done.3 = f32[1,1024]{1,0:T(1,128)S(1)} collective-permute-done((f32[1,1024]{1,0:T(1,128)S(1)}, f32[1,1024]{1,0:T(1,128)S(1)}, u32[]{:S(2)}, u32[]{:S(2)}) %collective-permute-start.3) | collective-permute-done | bytes 4128 | tf_op jit(solution)/shard_map/cond/branch_1_fun/ppermute | solution.py:850
  13.0 2.6 %collective-permute-start.7 = (f32[1,2048]{1,0:T(1,128)S(1)}, f32[1,2048]{1,0:T(1,128)S(1)}, u32[]{:S(2)}, u32[]{:S(2)}) collective-permute-start(f32[1,2048]{1,0:T(1,128)S(1)} %get-tuple-element.100), channel_id=1, source_target_pairs={{0,16},{4,20},{8,24},{12,28},{16,0},{20,4},{24,8},{28,12},{1,17},{... | collective-permute-start | bytes 24584 | tf_op jit(solution)/shard_map/ppermute | solution.py:850
  15.6 2.7 %local_stats.1 = (f32[3,8,256]{2,1,0:T(8,128)S(1)}, f32[1,256]{1,0:T(1,128)S(1)}, bf16[4,256,512]{2,1,0:T(8,128)(2,1)S(1)}, bf16[4,256,512]{2,1,0:T(8,128)(2,1)S(1)}, bf16[2,128,4096]{2,1,0:T(8,128)(2,1)S(1)}) custom-call(s32[1,128]{1,0:T(1,128)S(1)} %copy-done, bf16[1,128,2048]{2,1,0:T(8,128)(2,1)} %k_ref.5, bf16[1,128,2048]{2,1,0:T(8,128)(2,1)} %v_ref.5, ...), custom_call_target="tpu_custom_call" | custom-call | flops 1 | bytes 1 | tf_op jit(solution)/shard_map/local_stats/pallas_call | solution.py:476
  18.3 0.8 %cross_stats.1 = (bf16[4,256,512]{2,1,0:T(8,128)(2,1)S(1)}, f32[3,4,256]{2,1,0:T(4,128)S(1)}, bf16[2,4,256,256]{3,2,1,0:T(8,128)(2,1)S(1)}) custom-call(bf16[4,256,512]{2,1,0:T(8,128)(2,1)S(1)} %get-tuple-element.93.near.pair, bf16[4,256,512]{2,1,0:T(8,128)(2,1)S(1)} %get-tuple-element.91.far, bf16[2,128,512]{2,1,0:T(8,128)(2,1)S(1)} %collective-permute-done.5.straight, ...), custom_call_target="tpu_custom_call" | custom-call | flops 1 | bytes 1 | tf_op jit(solution)/shard_map/cross_stats/pallas_call | solution.py:525
  19.2 0.7 %router_gate.1 = (f32[1,256]{1,0:T(1,128)S(1)}, f32[4,4,256]{2,1,0:T(4,128)S(1)}) custom-call(f32[1,256]{1,0:T(1,128)S(1)} %get-tuple-element.98.live_ref, bf16[2,128,4096]{2,1,0:T(8,128)(2,1)S(1)} %get-tuple-element.99.rows_x, f32[1,4096]{1,0:T(1,128)S(1)} %pad_maximum_fusion.1.w_ref, f32[3,8,256]{2,1,0:T(8,128)S(1)} %get-tuple-element.92.local, ...), custom_call_target="tpu_custom_call" | custom-call | flops 1 | bytes 1 | tf_op jit(solution)/shard_map/router_gate/pallas_call | solution.py:382
  19.8 1.5 %collective-permute-start.8 = (f32[4,4,256]{2,1,0:T(4,128)S(1)}, f32[4,4,256]{2,1,0:T(4,128)S(1)}, u32[]{:S(2)}, u32[]{:S(2)}) collective-permute-start(f32[4,4,256]{2,1,0:T(4,128)S(1)} %get-tuple-element.102), channel_id=1, source_target_pairs={{0,2},{1,3},{2,0},{3,1},{4,6},{5,7},{6,4},{7,5},{8,10},{9,11},{10,... | collective-permute-start | bytes 49160 | tf_op jit(solution)/shard_map/ppermute | solution.py:838
  21.3 1.6 %near_grad.1 = (f32[256,512]{1,0:T(8,128)S(1)}, bf16[2,128,512]{2,1,0:T(8,128)(2,1)S(1)}, bf16[2,128,512]{2,1,0:T(8,128)(2,1)S(1)}, f32[1,256]{1,0:T(1,128)S(1)}) custom-call(bf16[4,256,512]{2,1,0:T(8,128)(2,1)S(1)} %get-tuple-element.93.near.pair, f32[3,8,256]{2,1,0:T(8,128)S(1)} %get-tuple-element.92.local, f32[3,4,256]{2,1,0:T(4,128)S(1)} %get-tuple-element.97.stats, ...), custom_call_target="tpu_custom_call" | custom-call | flops 1 | bytes 1 | tf_op jit(solution)/shard_map/near_grad/pallas_call | solution.py:590
  23.0 0.7 %collective-permute-done.8.heard = f32[4,4,256]{2,1,0:T(4,128)S(1)} collective-permute-done((f32[4,4,256]{2,1,0:T(4,128)S(1)}, f32[4,4,256]{2,1,0:T(4,128)S(1)}, u32[]{:S(2)}, u32[]{:S(2)}) %collective-permute-start.8) | collective-permute-done | bytes 16416 | tf_op jit(solution)/shard_map/ppermute | solution.py:838
  23.7 1.1 %cross_grad.1 = (bf16[2,128,512]{2,1,0:T(8,128)(2,1)S(1)}, bf16[2,128,512]{2,1,0:T(8,128)(2,1)S(1)}, bf16[256,512]{1,0:T(8,128)(2,1)S(1)}, bf16[2,256,512]{2,1,0...) custom-call(bf16[4,256,512]{2,1,0:T(8,128)(2,1)S(1)} %get-tuple-element.95.cross, ...), custom_call_target="tpu_custom_call" | custom-call | flops 1 | bytes 1 | tf_op jit(solution)/shard_map/cross_grad/pallas_call | solution.py:656
  24.8 1.5 %collective-permute-start.9 = (bf16[2,128,512]{2,1,0:T(8,128)(2,1)S(1)}, bf16[2,128,512]{2,1,0:T(8,128)(2,1)S(1)}, u32[]{:S(2)}, u32[]{:S(2)}) collective-permute-start(bf16[2,128,512]{2,1,0:T(8,128)(2,1)S(1)} %get-tuple-element.117), channel_id=1, source_target_pairs={{0,2},{1,3},{2,0},{3,1},{4,6},{5,7},{6,4},{7,5},{8,10},{9,11},{10,... | collective-permute-start | bytes 786440 | tf_op jit(solution)/shard_map/ppermute | solution.py:838
  26.3 5.5 %all-to-all-start = ((f32[32,1,512]{2,1,0:T(1,128)}), f32[32,1,512]{2,1,0:T(1,128)S(1)}, u32[]{:S(2)}, u32[]{:S(2)}) async-start(f32[32,1,512]{2,1,0:T(1,128)} %bitcast.4), calls=%async_computation | async-start | bytes 131072 | tf_op jit(solution)/shard_map/all_to_all | solution.py:888
  31.8 4.2 %conditional.3 = (f32[1,128,2048]{2,1,0:T(8,128)}, f32[1,128,2048]{2,1,0:T(8,128)}, f32[1,128,2048]{2,1,0:T(8,128)}, bf16[2,128,512]{2,1,0:T(8,128)(2,1)S(1)}, bf16[3,128,1024]{2,1,0:T(8,128)(2,1)}) conditional(s32[]{:T(128)} %bitcast, () %tuple.28, (bf16[4,256,512]{2,1,0:T(8,128)(2,1)S(1)}, f32[3,8,256]{2,1,0:T(8,128)S(1)}, ...), branch_computations={%region_2.0_spmd, %region_3.0_spmd} | conditional | flops 2 | bytes 4194360 | solution.py:844
  31.8 1.7 %far_grad.1 = (bf16[3,128,1024]{2,1,0:T(8,128)(2,1)S(1)}, bf16[3,128,1024]{2,1,0:T(8,128)(2,1)S(1)}) custom-call(bf16[4,256,512]{2,1,0:T(8,128)(2,1)S(1)} %get-tuple-element.25.pair, f32[3,8,256]{2,1,0:T(8,128)S(1)} %get-tuple-element.26.local, f32[2,4,256]{2,1,0:T(4,128)S(1)} %get-tuple-element.27.final, f32[1,256]{1,0:T(1,128)S(1)} %get-tuple-element.28.gates, ...), custom_call_target="tpu_custom_call" | custom-call | flops 1 | bytes 1 | tf_op jit(solution)/shard_map/cond/branch_1_fun/far_grad/pallas_call | solution.py:703
  33.9 1.2 %own_join.1 = (f32[1,128,2048]{2,1,0:T(8,128)}, f32[1,128,2048]{2,1,0:T(8,128)}, f32[1,128,2048]{2,1,0:T(8,128)}, bf16[2,128,512]{2,1,0:T(8,128)(2,1)S(1)}) custom-call(bf16[3,128,1024]{2,1,0:T(8,128)(2,1)S(1)} %get-tuple-element.33.own), custom_call_target="tpu_custom_call" | custom-call | flops 1 | bytes 1 | tf_op jit(solution)/shard_map/cond/branch_1_fun/own_join/pallas_call | solution.py:734
  35.1 1.0 %collective-permute-done = bf16[3,128,1024]{2,1,0:T(8,128)(2,1)} collective-permute-done((bf16[3,128,1024]{2,1,0:T(8,128)(2,1)S(1)}, bf16[3,128,1024]{2,1,0:T(8,128)(2,1)}, u32[]{:S(2)}, u32[]{:S(2)}) %collective-permute-start) | collective-permute-done | bytes 786464 | tf_op jit(solution)/shard_map/cond/branch_1_fun/ppermute | solution.py:838
  36.0 2.2 %sib_join.1 = (f32[1,128,2048]{2,1,0:T(8,128)}, f32[1,128,2048]{2,1,0:T(8,128)}, f32[1,128,2048]{2,1,0:T(8,128)}, bf16[2,128,512]{2,1,0:T(8,128)(2,1)S(1)}) custom-call(bf16[3,128,1024]{2,1,0:T(8,128)(2,1)} %get-tuple-element.112.sib, f32[1,128,2048]{2,1,0:T(8,128)} %get-tuple-element.113.dq_in, ...), custom_call_target="tpu_custom_call", output_to_operand_aliasing={{0}: (1, {}), {1}: (2, {}), {2}: (3, {})} | custom-call | flops 1 | bytes 1 | tf_op jit(solution)/shard_map/sib_join/pallas_call | solution.py:769
  38.2 1.0 %add_back.1 = (f32[1,128,2048]{2,1,0:T(8,128)}, f32[1,128,2048]{2,1,0:T(8,128)}, f32[1,128,2048]{2,1,0:T(8,128)}) custom-call(bf16[2,128,512]{2,1,0:T(8,128)(2,1)S(1)} %get-tuple-element.111.own, bf16[2,128,512]{2,1,0:T(8,128)(2,1)S(1)} %get-tuple-element.116.sib, ...), custom_call_target="tpu_custom_call", output_to_operand_aliasing={{0}: (4, {}), {1}: (5, {}), {2}: (6, {})} | custom-call | flops 1 | bytes 1 | tf_op jit(solution)/shard_map/add_back/pallas_call | solution.py:820
  (21 shorter events, 2.4 us)
Async XLA Ops:
  0.6 5.9 %copy-start = (s32[1,128]{1,0:T(1,128)S(1)}, s32[1,128]{1,0:T(1,128)}, u32[]{:S(2)}) copy-start(s32[1,128]{1,0:T(1,128)} %pos_ref.2) | copy-start | bytes 1540
  2.0 6.6 %copy-start.1 = (bf16[1,128,4096]{2,1,0:T(8,128)(2,1)S(1)}, bf16[1,128,4096]{2,1,0:T(8,128)(2,1)}, u32[]{:S(2)}) copy-start(bf16[1,128,4096]{2,1,0:T(8,128)(2,1)} %x_ref.1) | copy-start | bytes 3145732
  2.0 16.3 %collective-permute-start.6 = (bf16[2,128,512]{2,1,0:T(8,128)(2,1)S(1)}, bf16[2,128,512]{2,1,0:T(8,128)(2,1)S(1)}, u32[]{:S(2)}, u32[]{:S(2)}) collective-permute-start(bf16[2,128,512]{2,1,0:T(8,128)(2,1)S(1)} %get-tuple-element.94), channel_id=1, source_target_pairs={{0,3},{1,2},{2,1},{3,0},{4,7},{5,6},{6,5},{7,4},{8,11},{9,10},{10,... | collective-permute-start | bytes 786440 | tf_op jit(solution)/shard_map/ppermute | solution.py:838
  4.4 13.9 %collective-permute-start.5 = (bf16[2,128,512]{2,1,0:T(8,128)(2,1)S(1)}, bf16[2,128,512]{2,1,0:T(8,128)(2,1)S(1)}, u32[]{:S(2)}, u32[]{:S(2)}) collective-permute-start(bf16[2,128,512]{2,1,0:T(8,128)(2,1)S(1)} %get-tuple-element.85), channel_id=1, source_target_pairs={{0,2},{1,3},{2,0},{3,1},{4,6},{5,7},{6,4},{7,5},{8,10},{9,11},{10,... | collective-permute-start | bytes 786440 | tf_op jit(solution)/shard_map/ppermute | solution.py:838
  5.0 3.6 %collective-permute-start.4 = (f32[1,512]{1,0:T(1,128)S(1)}, f32[1,512]{1,0:T(1,128)S(1)}, u32[]{:S(2)}, u32[]{:S(2)}) collective-permute-start(f32[1,512]{1,0:T(1,128)S(1)} %get-tuple-element.87), channel_id=1, source_target_pairs={{0,4},{4,0},{8,12},{12,8},{16,20},{20,16},{24,28},{28,24},{1,5},{5... | collective-permute-start | bytes 6152 | tf_op jit(solution)/shard_map/ppermute | solution.py:850
  8.7 4.2 %collective-permute-start.1 = (bf16[4,128,1024]{2,1,0:T(8,128)(2,1)S(1)}, bf16[4,128,1024]{2,1,0:T(8,128)(2,1)}, u32[]{:S(2)}, u32[]{:S(2)}) collective-permute-start(bf16[4,128,1024]{2,1,0:T(8,128)(2,1)S(1)} %get-tuple-element.22), channel_id=1, source_target_pairs={{0,1},{1,0},{2,3},{3,2},{4,5},{5,4},{6,7},{7,6},{8,9},{9,8},{10,11... | collective-permute-start | bytes 3145736 | tf_op jit(solution)/shard_map/cond/branch_1_fun/ppermute | solution.py:838
  8.7 4.3 %collective-permute-start.2 = (bf16[1,128,4096]{2,1,0:T(8,128)(2,1)S(1)}, bf16[1,128,4096]{2,1,0:T(8,128)(2,1)}, u32[]{:S(2)}, u32[]{:S(2)}) collective-permute-start(bf16[1,128,4096]{2,1,0:T(8,128)(2,1)S(1)} %get-tuple-element.23), channel_id=1, source_target_pairs={{0,1},{1,0},{2,3},{3,2},{4,5},{5,4},{6,7},{7,6},{8,9},{9,8},{10,11... | collective-permute-start | bytes 3145736 | tf_op jit(solution)/shard_map/cond/branch_1_fun/ppermute | solution.py:838
  9.2 3.6 %collective-permute-start.3 = (f32[1,1024]{1,0:T(1,128)S(1)}, f32[1,1024]{1,0:T(1,128)S(1)}, u32[]{:S(2)}, u32[]{:S(2)}) collective-permute-start(f32[1,1024]{1,0:T(1,128)S(1)} %get-tuple-element.24), channel_id=1, source_target_pairs={{0,8},{4,12},{8,0},{12,4},{16,24},{20,28},{24,16},{28,20},{1,9},{5... | collective-permute-start | bytes 12296 | tf_op jit(solution)/shard_map/cond/branch_1_fun/ppermute | solution.py:850
  13.0 6.1 %collective-permute-start.7 = (f32[1,2048]{1,0:T(1,128)S(1)}, f32[1,2048]{1,0:T(1,128)S(1)}, u32[]{:S(2)}, u32[]{:S(2)}) collective-permute-start(f32[1,2048]{1,0:T(1,128)S(1)} %get-tuple-element.100), channel_id=1, source_target_pairs={{0,16},{4,20},{8,24},{12,28},{16,0},{20,4},{24,8},{28,12},{1,17},{... | collective-permute-start | bytes 24584 | tf_op jit(solution)/shard_map/ppermute | solution.py:850
  19.8 3.8 %collective-permute-start.8 = (f32[4,4,256]{2,1,0:T(4,128)S(1)}, f32[4,4,256]{2,1,0:T(4,128)S(1)}, u32[]{:S(2)}, u32[]{:S(2)}) collective-permute-start(f32[4,4,256]{2,1,0:T(4,128)S(1)} %get-tuple-element.102), channel_id=1, source_target_pairs={{0,2},{1,3},{2,0},{3,1},{4,6},{5,7},{6,4},{7,5},{8,10},{9,11},{10,... | collective-permute-start | bytes 49160 | tf_op jit(solution)/shard_map/ppermute | solution.py:838
  24.8 13.4 %collective-permute-start.9 = (bf16[2,128,512]{2,1,0:T(8,128)(2,1)S(1)}, bf16[2,128,512]{2,1,0:T(8,128)(2,1)S(1)}, u32[]{:S(2)}, u32[]{:S(2)}) collective-permute-start(bf16[2,128,512]{2,1,0:T(8,128)(2,1)S(1)} %get-tuple-element.117), channel_id=1, source_target_pairs={{0,2},{1,3},{2,0},{3,1},{4,6},{5,7},{6,4},{7,5},{8,10},{9,11},{10,... | collective-permute-start | bytes 786440 | tf_op jit(solution)/shard_map/ppermute | solution.py:838
  26.3 12.0 %collective-permute-start.10 = (bf16[2,128,512]{2,1,0:T(8,128)(2,1)S(1)}, bf16[2,128,512]{2,1,0:T(8,128)(2,1)S(1)}, u32[]{:S(2)}, u32[]{:S(2)}) collective-permute-start(bf16[2,128,512]{2,1,0:T(8,128)(2,1)S(1)} %get-tuple-element.118), channel_id=1, source_target_pairs={{0,3},{1,2},{2,1},{3,0},{4,7},{5,6},{6,5},{7,4},{8,11},{9,10},{10,... | collective-permute-start | bytes 786440 | tf_op jit(solution)/shard_map/ppermute | solution.py:838
  26.3 13.0 %all-to-all-start = ((f32[32,1,512]{2,1,0:T(1,128)}), f32[32,1,512]{2,1,0:T(1,128)S(1)}, u32[]{:S(2)}, u32[]{:S(2)}) async-start(f32[32,1,512]{2,1,0:T(1,128)} %bitcast.4), calls=%async_computation | async-start | bytes 131072 | tf_op jit(solution)/shard_map/all_to_all | solution.py:888
  33.6 2.5 %collective-permute-start = (bf16[3,128,1024]{2,1,0:T(8,128)(2,1)S(1)}, bf16[3,128,1024]{2,1,0:T(8,128)(2,1)}, u32[]{:S(2)}, u32[]{:S(2)}) collective-permute-start(bf16[3,128,1024]{2,1,0:T(8,128)(2,1)S(1)} %get-tuple-element.38), channel_id=1, source_target_pairs={{0,1},{1,0},{2,3},{3,2},{4,5},{5,4},{6,7},{7,6},{8,9},{9,8},{10,11... | collective-permute-start | bytes 2359304 | tf_op jit(solution)/shard_map/cond/branch_1_fun/ppermute | solution.py:838

commit v18 on v17

--- a/solution.py
+++ b/solution.py
@@ -862,7 +862,8 @@
         own_out, sib_out = far_grad(*operands)
         sib_in = send(sib_out, 1)
         *outs, waiting = own_join(own_out, queries.shape)
-        return outs, waiting, sib_in
+        *outs, waiting_sib = sib_join(sib_in, outs)
+        return outs, waiting, waiting_sib
 
     out_s, out_d, w_part = cross_pack(route_pos, w_router, keys, values, queries, d_gated)
     in_s, in_d = send(out_s, 2), send(out_d, 3)
@@ -886,8 +887,7 @@
 
     ret_s, ret_d = send(back_s, 2), send(back_d, 3)
     shared = lax.all_to_all(terms.reshape(ndp * n, 1, -1), ("dp", "ctx"), 0, 0, tiled=True)
-    outs, waiting, sib_in = beside(far_phase, far, local, final, gates, keep, dq_low, near_own, near_sib)
-    *outs, waiting_sib = sib_join(sib_in, outs)
+    outs, waiting, waiting_sib = beside(far_phase, far, local, final, gates, keep, dq_low, near_own, near_sib)
     dq, dk, dv = add_back(waiting, waiting_sib, ret_s, ret_d, outs)
     router_grad = jnp.sum(after(shared, dq), axis=(0, 1))
     return dq, dk, dv, router_grad

time: 40.2 us -> 41 us (1.020)
  waiting for transfers between devices: 4.57 us -> 5.61 us
    all_to_all x1, waiting for transfers between devices: 0.01 us -> 1.18 us  [swap_body(): lax.all_to_all(terms.reshape(ndp * n, 1, -1), ('dp', 'ctx'), 0, 0, tiled=...]
    pallas_call x1, Pallas kernels: 2.17 us -> 1.28 us  [sib_join(): pl.pallas_call(sib_join_kernel, out_shape=[pltpu.HBM(o.shape, F32) for o...]
    pallas_call x1, Pallas kernels: 1.14 us -> 1.83 us  [cross_grad(): pl.pallas_call(functools.partial(cross_grad_kernel, HEAD ** (-0.5), total...]
  transfers between devices with their start and end apart: 12 -> 12, of which waited for: 5 -> 6; matrix products, arithmetic and copies ran while one was open for 0% -> 0% of each run, Pallas kernels for 31% -> 29%
where the time goes in v18:
time: 41 us; the launch traced here: 40.8 us
  starting transfers between devices  18.1 us (44%)
  Pallas kernels  15.5 us (38%)
  waiting for transfers between devices  5.61 us (14%)
  between operations  0.81 us (2%)
  other arithmetic  0.68 us (2%)
    ppermute x8, starting transfers between devices, send(): return lax.ppermute(a, 'ctx', [(i, i ^ flip) for i in range(n)])  6.84 us
    ppermute x3, starting transfers between devices, widen(): other = lax.ppermute(part, 'dp', [(i, i ^ step) for i in range(ndp)])  5.68 us
    all_to_all x1, starting transfers between devices, swap_body(): lax.all_to_all(terms.reshape(ndp * n, 1, -1), ('dp', 'ctx'), 0, 0, tiled=...  5.55 us
    ppermute x3, waiting for transfers between devices, widen(): other = lax.ppermute(part, 'dp', [(i, i ^ step) for i in range(ndp)])  2.74 us
    pallas_call x1, Pallas kernels, local_stats(): pl.pallas_call(functools.partial(local_stats_kernel, HEAD ** (-0.5)), out...  2.69 us
    pallas_call x1, Pallas kernels, cross_grad(): pl.pallas_call(functools.partial(cross_grad_kernel, HEAD ** (-0.5), total...  1.83 us
    pallas_call x1, Pallas kernels, far_grad(): pl.pallas_call(functools.partial(far_grad_kernel, HEAD ** (-0.5)), out_sh...  1.71 us
    ppermute x8, waiting for transfers between devices, send(): return lax.ppermute(a, 'ctx', [(i, i ^ flip) for i in range(n)])  1.69 us
  transfers between devices with their start and end apart: 12, of which 6 were waited for; matrix products, arithmetic and copies ran while one was open for 0% of the time, Pallas kernels for 29%

profile of v18, /device:TPU:0, one launch (start us, length us, event | category | flops | bytes accessed | tf_op | source)
XLA Modules:
  0.0 40.8 jit_solution(6350257945912984196)
XLA Ops:
  0.6 1.3 %cross_pack.1 = (bf16[2,128,512]{2,1,0:T(8,128)(2,1)S(1)}, bf16[2,128,512]{2,1,0:T(8,128)(2,1)S(1)}, f32[1,512]{1,0:T(1,128)S(1)}) custom-call(s32[1,128]{1,0:T(1,128)} %pos_ref.2, bf16[512]{0:T(512)(128)(2,1)} %w_any.1, bf16[1,128,2048]{2,1,0:T(8,128)(2,1)} %k_ref.5, bf16[1,128,2048]{2,1,0:T(8,128)(2,1)} %v_ref.5, bf16[1,128,2048]{2,1,0:T(8,128)(2,1)} %q_ref.5, ...), custom_call_target="tpu_custom_call" | custom-call | flops 1 | bytes 1 | tf_op jit(solution)/shard_map/cross_pack/pallas_call | solution.py:314
  2.0 2.4 %collective-permute-start.6 = (bf16[2,128,512]{2,1,0:T(8,128)(2,1)S(1)}, bf16[2,128,512]{2,1,0:T(8,128)(2,1)S(1)}, u32[]{:S(2)}, u32[]{:S(2)}) collective-permute-start(bf16[2,128,512]{2,1,0:T(8,128)(2,1)S(1)} %get-tuple-element.94), channel_id=1, source_target_pairs={{0,3},{1,2},{2,1},{3,0},{4,7},{5,6},{6,5},{7,4},{8,11},{9,10},{10,... | collective-permute-start | bytes 786440 | tf_op jit(solution)/shard_map/ppermute | solution.py:838
  5.0 1.5 %collective-permute-start.4 = (f32[1,512]{1,0:T(1,128)S(1)}, f32[1,512]{1,0:T(1,128)S(1)}, u32[]{:S(2)}, u32[]{:S(2)}) collective-permute-start(f32[1,512]{1,0:T(1,128)S(1)} %get-tuple-element.87), channel_id=1, source_target_pairs={{0,4},{4,0},{8,12},{12,8},{16,20},{20,16},{24,28},{28,24},{1,5},{5... | collective-permute-start | bytes 6152 | tf_op jit(solution)/shard_map/ppermute | solution.py:850
  6.6 1.3 %sib_pack.1 = bf16[4,128,1024]{2,1,0:T(8,128)(2,1)S(1)} custom-call(s32[1,128]{1,0:T(1,128)S(1)} %copy-done, bf16[1,128,2048]{2,1,0:T(8,128)(2,1)} %k_ref.5, bf16[1,128,2048]{2,1,0:T(8,128)(2,1)} %v_ref.5, bf16[1,128,2048]{2,1,0:T(8,128)(2,1)} %q_ref.5, f32[1,128,2048]{2,1,0:T(8,128)} %dg_ref.5), custom_call_target="tpu_custom_call" | custom-call | flops 1 | bytes 1 | tf_op jit(solution)/shard_map/sib_pack/pallas_call | solution.py:350
  7.9 0.7 %collective-permute-done.4 = f32[1,512]{1,0:T(1,128)S(1)} collective-permute-done((f32[1,512]{1,0:T(1,128)S(1)}, f32[1,512]{1,0:T(1,128)S(1)}, u32[]{:S(2)}, u32[]{:S(2)}) %collective-permute-start.4) | collective-permute-done | bytes 2080 | tf_op jit(solution)/shard_map/ppermute | solution.py:850
  8.6 4.4 %conditional.2 = (bf16[4,128,1024]{2,1,0:T(8,128)(2,1)}, bf16[1,128,4096]{2,1,0:T(8,128)(2,1)}, f32[1,2048]{1,0:T(1,128)S(1)}) conditional(s32[]{:T(128)} %bitcast, () %tuple.29, (bf16[4,128,1024]{2,1,0:T(8,128)(2,1)S(1)}, bf16[1,128,4096]{2,1,0:T(8,128)(2,1)S(1)}, f32[1,1024]{1,0:T(1,128)S(1)}) %tuple.41), branch_computations={%region_0.0_spmd, %region_1.0_spmd} | conditional | flops 2048 | bytes 8421520 | solution.py:844
  9.2 1.6 %collective-permute-start.3 = (f32[1,1024]{1,0:T(1,128)S(1)}, f32[1,1024]{1,0:T(1,128)S(1)}, u32[]{:S(2)}, u32[]{:S(2)}) collective-permute-start(f32[1,1024]{1,0:T(1,128)S(1)} %get-tuple-element.24), channel_id=1, source_target_pairs={{0,8},{4,12},{8,0},{12,4},{16,24},{20,28},{24,16},{28,20},{1,9},{5... | collective-permute-start | bytes 12296 | tf_op jit(solution)/shard_map/cond/branch_1_fun/ppermute | solution.py:850
  10.8 2.0 %collective-permute-done.3 = f32[1,1024]{1,0:T(1,128)S(1)} collective-permute-done((f32[1,1024]{1,0:T(1,128)S(1)}, f32[1,1024]{1,0:T(1,128)S(1)}, u32[]{:S(2)}, u32[]{:S(2)}) %collective-permute-start.3) | collective-permute-done | bytes 4128 | tf_op jit(solution)/shard_map/cond/branch_1_fun/ppermute | solution.py:850
  13.0 2.6 %collective-permute-start.7 = (f32[1,2048]{1,0:T(1,128)S(1)}, f32[1,2048]{1,0:T(1,128)S(1)}, u32[]{:S(2)}, u32[]{:S(2)}) collective-permute-start(f32[1,2048]{1,0:T(1,128)S(1)} %get-tuple-element.100), channel_id=1, source_target_pairs={{0,16},{4,20},{8,24},{12,28},{16,0},{20,4},{24,8},{28,12},{1,17},{... | collective-permute-start | bytes 24584 | tf_op jit(solution)/shard_map/ppermute | solution.py:850
  15.6 2.7 %local_stats.1 = (f32[3,8,256]{2,1,0:T(8,128)S(1)}, f32[1,256]{1,0:T(1,128)S(1)}, bf16[4,256,512]{2,1,0:T(8,128)(2,1)S(1)}, bf16[4,256,512]{2,1,0:T(8,128)(2,1)S(1)}, bf16[2,128,4096]{2,1,0:T(8,128)(2,1)S(1)}) custom-call(s32[1,128]{1,0:T(1,128)S(1)} %copy-done, bf16[1,128,2048]{2,1,0:T(8,128)(2,1)} %k_ref.5, bf16[1,128,2048]{2,1,0:T(8,128)(2,1)} %v_ref.5, ...), custom_call_target="tpu_custom_call" | custom-call | flops 1 | bytes 1 | tf_op jit(solution)/shard_map/local_stats/pallas_call | solution.py:476
  18.3 0.8 %cross_stats.1 = (bf16[4,256,512]{2,1,0:T(8,128)(2,1)S(1)}, f32[3,4,256]{2,1,0:T(4,128)S(1)}, bf16[2,4,256,256]{3,2,1,0:T(8,128)(2,1)S(1)}) custom-call(bf16[4,256,512]{2,1,0:T(8,128)(2,1)S(1)} %get-tuple-element.93.near.pair, bf16[4,256,512]{2,1,0:T(8,128)(2,1)S(1)} %get-tuple-element.91.far, bf16[2,128,512]{2,1,0:T(8,128)(2,1)S(1)} %collective-permute-done.5.straight, ...), custom_call_target="tpu_custom_call" | custom-call | flops 1 | bytes 1 | tf_op jit(solution)/shard_map/cross_stats/pallas_call | solution.py:525
  19.8 1.5 %collective-permute-start.8 = (f32[4,4,256]{2,1,0:T(4,128)S(1)}, f32[4,4,256]{2,1,0:T(4,128)S(1)}, u32[]{:S(2)}, u32[]{:S(2)}) collective-permute-start(f32[4,4,256]{2,1,0:T(4,128)S(1)} %get-tuple-element.102), channel_id=1, source_target_pairs={{0,2},{1,3},{2,0},{3,1},{4,6},{5,7},{6,4},{7,5},{8,10},{9,11},{10,... | collective-permute-start | bytes 49160 | tf_op jit(solution)/shard_map/ppermute | solution.py:838
  21.3 1.6 %near_grad.1 = (f32[256,512]{1,0:T(8,128)S(1)}, bf16[2,128,512]{2,1,0:T(8,128)(2,1)S(1)}, bf16[2,128,512]{2,1,0:T(8,128)(2,1)S(1)}, f32[1,256]{1,0:T(1,128)S(1)}) custom-call(bf16[4,256,512]{2,1,0:T(8,128)(2,1)S(1)} %get-tuple-element.93.near.pair, f32[3,8,256]{2,1,0:T(8,128)S(1)} %get-tuple-element.92.local, f32[3,4,256]{2,1,0:T(4,128)S(1)} %get-tuple-element.97.stats, ...), custom_call_target="tpu_custom_call" | custom-call | flops 1 | bytes 1 | tf_op jit(solution)/shard_map/near_grad/pallas_call | solution.py:590
  23.0 0.7 %collective-permute-done.8.heard = f32[4,4,256]{2,1,0:T(4,128)S(1)} collective-permute-done((f32[4,4,256]{2,1,0:T(4,128)S(1)}, f32[4,4,256]{2,1,0:T(4,128)S(1)}, u32[]{:S(2)}, u32[]{:S(2)}) %collective-permute-start.8) | collective-permute-done | bytes 16416 | tf_op jit(solution)/shard_map/ppermute | solution.py:838
  23.7 1.8 %cross_grad.1 = (bf16[2,128,512]{2,1,0:T(8,128)(2,1)}, bf16[2,128,512]{2,1,0:T(8,128)(2,1)S(1)}, bf16[256,512]{1,0:T(8,128)(2,1)S(1)}, bf16[2,256,512]{2,1,0:T(8...) custom-call(bf16[4,256,512]{2,1,0:T(8,128)(2,1)S(1)} %get-tuple-element.95.cross, ...), custom_call_target="tpu_custom_call" | custom-call | flops 1 | bytes 1 | tf_op jit(solution)/shard_map/cross_grad/pallas_call | solution.py:656
  25.5 1.5 %collective-permute-start.9 = (bf16[2,128,512]{2,1,0:T(8,128)(2,1)}, bf16[2,128,512]{2,1,0:T(8,128)(2,1)S(1)}, u32[]{:S(2)}, u32[]{:S(2)}) collective-permute-start(bf16[2,128,512]{2,1,0:T(8,128)(2,1)} %get-tuple-element.113), channel_id=1, source_target_pairs={{0,2},{1,3},{2,0},{3,1},{4,6},{5,7},{6,4},{7,5},{8,10},{9,11},{10,... | collective-permute-start | bytes 786440 | tf_op jit(solution)/shard_map/ppermute | solution.py:838
  27.0 5.5 %all-to-all-start = ((f32[32,1,512]{2,1,0:T(1,128)}), f32[32,1,512]{2,1,0:T(1,128)S(1)}, u32[]{:S(2)}, u32[]{:S(2)}) async-start(f32[32,1,512]{2,1,0:T(1,128)} %bitcast.4), calls=%async_computation | async-start | bytes 131072 | tf_op jit(solution)/shard_map/all_to_all | solution.py:889
  32.5 5.4 %conditional.3 = (f32[1,128,2048]{2,1,0:T(8,128)}, f32[1,128,2048]{2,1,0:T(8,128)}, f32[1,128,2048]{2,1,0:T(8,128)}, bf16[2,128,512]{2,1,0:T(8,128)(2,1)S(1)}, bf16[2,128,512]{2,1,0:T(8,128)(2,1)S(1)}) conditional(s32[]{:T(128)} %bitcast, () %tuple.28, (bf16[4,256,512]{2,1,0:T(8,128)(2,1)S(1)}, f32[3,8,256]{2,1,0:T(8,128)S(1)}, ...), branch_computations={%region_2.0_spmd, %region_3.0_spmd} | conditional | flops 3 | bytes 3670072 | solution.py:844
  32.5 1.7 %far_grad.1 = (bf16[3,128,1024]{2,1,0:T(8,128)(2,1)S(1)}, bf16[3,128,1024]{2,1,0:T(8,128)(2,1)S(1)}) custom-call(bf16[4,256,512]{2,1,0:T(8,128)(2,1)S(1)} %get-tuple-element.25.pair, f32[3,8,256]{2,1,0:T(8,128)S(1)} %get-tuple-element.26.local, f32[2,4,256]{2,1,0:T(4,128)S(1)} %get-tuple-element.27.final, f32[1,256]{1,0:T(1,128)S(1)} %get-tuple-element.28.gates, ...), custom_call_target="tpu_custom_call" | custom-call | flops 1 | bytes 1 | tf_op jit(solution)/shard_map/cond/branch_1_fun/far_grad/pallas_call | solution.py:703
  34.6 1.2 %own_join.1 = (f32[1,128,2048]{2,1,0:T(8,128)}, f32[1,128,2048]{2,1,0:T(8,128)}, f32[1,128,2048]{2,1,0:T(8,128)}, bf16[2,128,512]{2,1,0:T(8,128)(2,1)S(1)}) custom-call(bf16[3,128,1024]{2,1,0:T(8,128)(2,1)S(1)} %get-tuple-element.34.own), custom_call_target="tpu_custom_call" | custom-call | flops 1 | bytes 1 | tf_op jit(solution)/shard_map/cond/branch_1_fun/own_join/pallas_call | solution.py:734
  35.8 0.8 %collective-permute-done.sib = bf16[3,128,1024]{2,1,0:T(8,128)(2,1)S(1)} collective-permute-done((bf16[3,128,1024]{2,1,0:T(8,128)(2,1)S(1)}, bf16[3,128,1024]{2,1,0:T(8,128)(2,1)S(1)}, u32[]{:S(2)}, u32[]{:S(2)}) %collective-permute-start) | collective-permute-done | bytes 786464 | tf_op jit(solution)/shard_map/cond/branch_1_fun/ppermute | solution.py:838
  36.6 1.3 %sib_join.1 = (f32[1,128,2048]{2,1,0:T(8,128)}, f32[1,128,2048]{2,1,0:T(8,128)}, f32[1,128,2048]{2,1,0:T(8,128)}, bf16[2,128,512]{2,1,0:T(8,128)(2,1)S(1)}) custom-call(bf16[3,128,1024]{2,1,0:T(8,128)(2,1)S(1)} %collective-permute-done.sib, f32[1,128,2048]{2,1,0:T(8,128)} %get-tuple-element.35.dq_in, ...), custom_call_target="tpu_custom_call", output_to_operand_aliasing={{0}: (1, {}), {1}: (2, {}), {2}: (3, {})} | custom-call | flops 1 | bytes 1 | tf_op jit(solution)/shard_map/cond/branch_1_fun/sib_join/pallas_call | solution.py:769
  37.9 1.0 %add_back.1 = (f32[1,128,2048]{2,1,0:T(8,128)}, f32[1,128,2048]{2,1,0:T(8,128)}, f32[1,128,2048]{2,1,0:T(8,128)}) custom-call(bf16[2,128,512]{2,1,0:T(8,128)(2,1)S(1)} %get-tuple-element.111.own, bf16[2,128,512]{2,1,0:T(8,128)(2,1)S(1)} %get-tuple-element.112.sib, ...), custom_call_target="tpu_custom_call", output_to_operand_aliasing={{0}: (4, {}), {1}: (5, {}), {2}: (6, {})} | custom-call | flops 1 | bytes 1 | tf_op jit(solution)/shard_map/add_back/pallas_call | solution.py:820
  39.0 1.2 %all-to-all-done = f32[32,1,512]{2,1,0:T(1,128)S(1)} async-done(((f32[32,1,512]{2,1,0:T(1,128)}), f32[32,1,512]{2,1,0:T(1,128)S(1)}, u32[]{:S(2)}, u32[]{:S(2)}) %all-to-all-start) | async-done | bytes 65568 | tf_op jit(solution)/shard_map/all_to_all | solution.py:889
  (21 shorter events, 3.1 us)
Async XLA Ops:
  0.6 5.9 %copy-start = (s32[1,128]{1,0:T(1,128)S(1)}, s32[1,128]{1,0:T(1,128)}, u32[]{:S(2)}) copy-start(s32[1,128]{1,0:T(1,128)} %pos_ref.2) | copy-start | bytes 1540
  2.0 6.6 %copy-start.1 = (bf16[1,128,4096]{2,1,0:T(8,128)(2,1)S(1)}, bf16[1,128,4096]{2,1,0:T(8,128)(2,1)}, u32[]{:S(2)}) copy-start(bf16[1,128,4096]{2,1,0:T(8,128)(2,1)} %x_ref.1) | copy-start | bytes 3145732
  2.0 16.3 %collective-permute-start.6 = (bf16[2,128,512]{2,1,0:T(8,128)(2,1)S(1)}, bf16[2,128,512]{2,1,0:T(8,128)(2,1)S(1)}, u32[]{:S(2)}, u32[]{:S(2)}) collective-permute-start(bf16[2,128,512]{2,1,0:T(8,128)(2,1)S(1)} %get-tuple-element.94), channel_id=1, source_target_pairs={{0,3},{1,2},{2,1},{3,0},{4,7},{5,6},{6,5},{7,4},{8,11},{9,10},{10,... | collective-permute-start | bytes 786440 | tf_op jit(solution)/shard_map/ppermute | solution.py:838
  4.4 13.9 %collective-permute-start.5 = (bf16[2,128,512]{2,1,0:T(8,128)(2,1)S(1)}, bf16[2,128,512]{2,1,0:T(8,128)(2,1)S(1)}, u32[]{:S(2)}, u32[]{:S(2)}) collective-permute-start(bf16[2,128,512]{2,1,0:T(8,128)(2,1)S(1)} %get-tuple-element.85), channel_id=1, source_target_pairs={{0,2},{1,3},{2,0},{3,1},{4,6},{5,7},{6,4},{7,5},{8,10},{9,11},{10,... | collective-permute-start | bytes 786440 | tf_op jit(solution)/shard_map/ppermute | solution.py:838
  5.0 3.6 %collective-permute-start.4 = (f32[1,512]{1,0:T(1,128)S(1)}, f32[1,512]{1,0:T(1,128)S(1)}, u32[]{:S(2)}, u32[]{:S(2)}) collective-permute-start(f32[1,512]{1,0:T(1,128)S(1)} %get-tuple-element.87), channel_id=1, source_target_pairs={{0,4},{4,0},{8,12},{12,8},{16,20},{20,16},{24,28},{28,24},{1,5},{5... | collective-permute-start | bytes 6152 | tf_op jit(solution)/shard_map/ppermute | solution.py:850
  8.7 4.2 %collective-permute-start.1 = (bf16[4,128,1024]{2,1,0:T(8,128)(2,1)S(1)}, bf16[4,128,1024]{2,1,0:T(8,128)(2,1)}, u32[]{:S(2)}, u32[]{:S(2)}) collective-permute-start(bf16[4,128,1024]{2,1,0:T(8,128)(2,1)S(1)} %get-tuple-element.22), channel_id=1, source_target_pairs={{0,1},{1,0},{2,3},{3,2},{4,5},{5,4},{6,7},{7,6},{8,9},{9,8},{10,11... | collective-permute-start | bytes 3145736 | tf_op jit(solution)/shard_map/cond/branch_1_fun/ppermute | solution.py:838
  8.7 4.3 %collective-permute-start.2 = (bf16[1,128,4096]{2,1,0:T(8,128)(2,1)S(1)}, bf16[1,128,4096]{2,1,0:T(8,128)(2,1)}, u32[]{:S(2)}, u32[]{:S(2)}) collective-permute-start(bf16[1,128,4096]{2,1,0:T(8,128)(2,1)S(1)} %get-tuple-element.23), channel_id=1, source_target_pairs={{0,1},{1,0},{2,3},{3,2},{4,5},{5,4},{6,7},{7,6},{8,9},{9,8},{10,11... | collective-permute-start | bytes 3145736 | tf_op jit(solution)/shard_map/cond/branch_1_fun/ppermute | solution.py:838
  9.2 3.6 %collective-permute-start.3 = (f32[1,1024]{1,0:T(1,128)S(1)}, f32[1,1024]{1,0:T(1,128)S(1)}, u32[]{:S(2)}, u32[]{:S(2)}) collective-permute-start(f32[1,1024]{1,0:T(1,128)S(1)} %get-tuple-element.24), channel_id=1, source_target_pairs={{0,8},{4,12},{8,0},{12,4},{16,24},{20,28},{24,16},{28,20},{1,9},{5... | collective-permute-start | bytes 12296 | tf_op jit(solution)/shard_map/cond/branch_1_fun/ppermute | solution.py:850
  13.0 6.1 %collective-permute-start.7 = (f32[1,2048]{1,0:T(1,128)S(1)}, f32[1,2048]{1,0:T(1,128)S(1)}, u32[]{:S(2)}, u32[]{:S(2)}) collective-permute-start(f32[1,2048]{1,0:T(1,128)S(1)} %get-tuple-element.100), channel_id=1, source_target_pairs={{0,16},{4,20},{8,24},{12,28},{16,0},{20,4},{24,8},{28,12},{1,17},{... | collective-permute-start | bytes 24584 | tf_op jit(solution)/shard_map/ppermute | solution.py:850
  19.8 3.8 %collective-permute-start.8 = (f32[4,4,256]{2,1,0:T(4,128)S(1)}, f32[4,4,256]{2,1,0:T(4,128)S(1)}, u32[]{:S(2)}, u32[]{:S(2)}) collective-permute-start(f32[4,4,256]{2,1,0:T(4,128)S(1)} %get-tuple-element.102), channel_id=1, source_target_pairs={{0,2},{1,3},{2,0},{3,1},{4,6},{5,7},{6,4},{7,5},{8,10},{9,11},{10,... | collective-permute-start | bytes 49160 | tf_op jit(solution)/shard_map/ppermute | solution.py:838
  25.5 12.4 %collective-permute-start.9 = (bf16[2,128,512]{2,1,0:T(8,128)(2,1)}, bf16[2,128,512]{2,1,0:T(8,128)(2,1)S(1)}, u32[]{:S(2)}, u32[]{:S(2)}) collective-permute-start(bf16[2,128,512]{2,1,0:T(8,128)(2,1)} %get-tuple-element.113), channel_id=1, source_target_pairs={{0,2},{1,3},{2,0},{3,1},{4,6},{5,7},{6,4},{7,5},{8,10},{9,11},{10,... | collective-permute-start | bytes 786440 | tf_op jit(solution)/shard_map/ppermute | solution.py:838
  27.0 11.0 %collective-permute-start.10 = (bf16[2,128,512]{2,1,0:T(8,128)(2,1)S(1)}, bf16[2,128,512]{2,1,0:T(8,128)(2,1)S(1)}, u32[]{:S(2)}, u32[]{:S(2)}) collective-permute-start(bf16[2,128,512]{2,1,0:T(8,128)(2,1)S(1)} %get-tuple-element.114), channel_id=1, source_target_pairs={{0,3},{1,2},{2,1},{3,0},{4,7},{5,6},{6,5},{7,4},{8,11},{9,10},{10,... | collective-permute-start | bytes 786440 | tf_op jit(solution)/shard_map/ppermute | solution.py:838
  27.0 13.2 %all-to-all-start = ((f32[32,1,512]{2,1,0:T(1,128)}), f32[32,1,512]{2,1,0:T(1,128)S(1)}, u32[]{:S(2)}, u32[]{:S(2)}) async-start(f32[32,1,512]{2,1,0:T(1,128)} %bitcast.4), calls=%async_computation | async-start | bytes 131072 | tf_op jit(solution)/shard_map/all_to_all | solution.py:889
  34.3 2.4 %collective-permute-start = (bf16[3,128,1024]{2,1,0:T(8,128)(2,1)S(1)}, bf16[3,128,1024]{2,1,0:T(8,128)(2,1)S(1)}, u32[]{:S(2)}, u32[]{:S(2)}) collective-permute-start(bf16[3,128,1024]{2,1,0:T(8,128)(2,1)S(1)} %get-tuple-element.33), channel_id=1, source_target_pairs={{0,1},{1,0},{2,3},{3,2},{4,5},{5,4},{6,7},{7,6},{8,9},{9,8},{10,11... | collective-permute-start | bytes 2359304 | tf_op jit(solution)/shard_map/cond/branch_1_fun/ppermute | solution.py:838

commit v19 on v18

--- a/solution.py
+++ b/solution.py
@@ -88,7 +88,7 @@
         out_shape=jax.ShapeDtypeStruct(route_pos.shape, F32),
         in_specs=[SMEM] + [VMEM] * (2 + parts),
         out_specs=VMEM,
-        compiler_params=params(),
+        compiler_params=params(8),
         cost_estimate=cost(16 * x_routed.size, x_routed.size * 2),
         name="router_gate",
     )(offsets, route_pos, x_routed, *w_parts)
@@ -322,7 +322,7 @@
             pltpu.VMEM(w_router.shape, BF16),
             pltpu.SemaphoreType.DMA((6,)),
         ],
-        compiler_params=params(),
+        compiler_params=params(6),
         cost_estimate=cost(0, 10 * slots * full),
         name="cross_pack",
     )(*in_hbm(route_pos, w_router, keys, values, queries, d_gated))
@@ -353,7 +353,7 @@
         in_specs=[VMEM, hbm, hbm, hbm, hbm],
         out_specs=VMEM,
         scratch_shapes=[pltpu.VMEM((slots, full // 2), F32), pltpu.SemaphoreType.DMA((4,))],
-        compiler_params=params(),
+        compiler_params=params(8),
         cost_estimate=cost(0, 20 * slots * full),
         name="sib_pack",
     )(route_pos, *in_hbm(keys, values, queries, d_gated))
@@ -485,7 +485,7 @@
         in_specs=[VMEM] + [anywhere] * 7,
         out_specs=[VMEM] * 5,
         scratch_shapes=[pltpu.VMEM((slots, half), F32), pltpu.SemaphoreType.DMA((16,)), pltpu.SemaphoreType.DMA((4,))],
-        compiler_params=params(),
+        compiler_params=params(14),
         cost_estimate=cost(16 * slots * slots * half, 16 * slots * half, 4 * slots * slots * half // HEAD),
         name="local_stats",
     )(route_pos, *in_hbm(keys, values, queries, d_gated), sib, x_routed, x_sib)
@@ -531,7 +531,7 @@
         ],
         in_specs=[VMEM] * 4,
         out_specs=[VMEM] * 3,
-        compiler_params=params(),
+        compiler_params=params(10),
         cost_estimate=cost(16 * slots * slots * width, 32 * slots * width, 4 * slots * slots * heads),
         name="cross_stats",
     )(near, far, straight, diag)
@@ -592,7 +592,7 @@
         out_shape=[pltpu.VMEM((2 * slots, width), F32), out, out, jax.ShapeDtypeStruct(gates.shape, F32)],
         in_specs=[VMEM] * 4,
         out_specs=[VMEM] * 4,
-        compiler_params=params(),
+        compiler_params=params(8),
         cost_estimate=cost(20 * slots * slots * width, 40 * slots * width),
         name="near_grad",
     )(pair, local, stats, gates)
@@ -666,7 +666,7 @@
         in_specs=[VMEM] * 9,
         out_specs=[VMEM] * 5 + [pl.BlockSpec(memory_space=pltpu.HBM)],
         scratch_shapes=[pltpu.VMEM(spread, F32), pltpu.SemaphoreType.DMA],
-        compiler_params=params(),
+        compiler_params=params(12),
         cost_estimate=cost(24 * slots * slots * width, 64 * slots * width),
         name="cross_grad",
     )(cross, kept, stats, local, heard, gates, near_dq, near_sum, rows_x)
@@ -705,7 +705,7 @@
         out_shape=[out, out],
         in_specs=[VMEM] * 8,
         out_specs=[VMEM] * 2,
-        compiler_params=params(),
+        compiler_params=params(10),
         cost_estimate=cost(20 * slots * slots * half, 40 * slots * half),
         name="far_grad",
     )(pair, local, final, gates, keep, near_dq, near_own, near_sib)
@@ -737,7 +737,7 @@
         in_specs=[VMEM],
         out_specs=[hbm] * 3 + [VMEM],
         scratch_shapes=[pltpu.VMEM((3, slots, half), F32), pltpu.SemaphoreType.DMA((3,))],
-        compiler_params=params(),
+        compiler_params=params(5),
         cost_estimate=cost(0, 18 * own.size),
         name="own_join",
     )(own)
@@ -778,7 +778,7 @@
             pltpu.SemaphoreType.DMA((3,)),
         ],
         input_output_aliases={1: 0, 2: 1, 3: 2},
-        compiler_params=params(),
+        compiler_params=params(6),
         cost_estimate=cost(0, 12 * sib.size),
         name="sib_join",
     )(sib, *in_hbm(*outs))
@@ -824,7 +824,7 @@
         out_specs=[hbm] * 3,
         scratch_shapes=[pltpu.VMEM((2, *own.shape), F32), pltpu.SemaphoreType.DMA((4,))],
         input_output_aliases={4: 0, 5: 1, 6: 2},
-        compiler_params=params(),
+        compiler_params=params(5),
         cost_estimate=cost(0, 24 * own.size),
         name="add_back",
     )(own, sib, straight, diag, *in_hbm(*outs))

time: 41 us -> 41 us (level)
  no operation moved by 1% of the time
where the time goes in v19:
time: 41 us; the launch traced here: 40.8 us
  starting transfers between devices  18.1 us (44%)
  Pallas kernels  15.5 us (38%)
  waiting for transfers between devices  5.61 us (14%)
  between operations  0.81 us (2%)
  other arithmetic  0.68 us (2%)
    ppermute x8, starting transfers between devices, send(): return lax.ppermute(a, 'ctx', [(i, i ^ flip) for i in range(n)])  6.84 us
    ppermute x3, starting transfers between devices, widen(): other = lax.ppermute(part, 'dp', [(i, i ^ step) for i in range(ndp)])  5.68 us
    all_to_all x1, starting transfers between devices, swap_body(): lax.all_to_all(terms.reshape(ndp * n, 1, -1), ('dp', 'ctx'), 0, 0, tiled=...  5.55 us
    ppermute x3, waiting for transfers between devices, widen(): other = lax.ppermute(part, 'dp', [(i, i ^ step) for i in range(ndp)])  2.74 us
    pallas_call x1, Pallas kernels, local_stats(): pl.pallas_call(functools.partial(local_stats_kernel, HEAD ** (-0.5)), out...  2.69 us
    pallas_call x1, Pallas kernels, cross_grad(): pl.pallas_call(functools.partial(cross_grad_kernel, HEAD ** (-0.5), total...  1.83 us
    pallas_call x1, Pallas kernels, far_grad(): pl.pallas_call(functools.partial(far_grad_kernel, HEAD ** (-0.5)), out_sh...  1.71 us
    ppermute x8, waiting for transfers between devices, send(): return lax.ppermute(a, 'ctx', [(i, i ^ flip) for i in range(n)])  1.69 us
  transfers between devices with their start and end apart: 12, of which 6 were waited for; matrix products, arithmetic and copies ran while one was open for 0% of the time, Pallas kernels for 29%

profile of v19, /device:TPU:0, one launch (start us, length us, event | category | flops | bytes accessed | tf_op | source)
XLA Modules:
  0.0 40.8 jit_solution(8307714127059294188)
XLA Ops:
  0.6 1.3 %cross_pack.1 = (bf16[2,128,512]{2,1,0:T(8,128)(2,1)S(1)}, bf16[2,128,512]{2,1,0:T(8,128)(2,1)S(1)}, f32[1,512]{1,0:T(1,128)S(1)}) custom-call(s32[1,128]{1,0:T(1,128)} %pos_ref.2, bf16[512]{0:T(512)(128)(2,1)} %w_any.1, bf16[1,128,2048]{2,1,0:T(8,128)(2,1)} %k_ref.5, bf16[1,128,2048]{2,1,0:T(8,128)(2,1)} %v_ref.5, bf16[1,128,2048]{2,1,0:T(8,128)(2,1)} %q_ref.5, ...), custom_call_target="tpu_custom_call" | custom-call | flops 1 | bytes 1 | tf_op jit(solution)/shard_map/cross_pack/pallas_call | solution.py:314
  2.0 2.4 %collective-permute-start.6 = (bf16[2,128,512]{2,1,0:T(8,128)(2,1)S(1)}, bf16[2,128,512]{2,1,0:T(8,128)(2,1)S(1)}, u32[]{:S(2)}, u32[]{:S(2)}) collective-permute-start(bf16[2,128,512]{2,1,0:T(8,128)(2,1)S(1)} %get-tuple-element.94), channel_id=1, source_target_pairs={{0,3},{1,2},{2,1},{3,0},{4,7},{5,6},{6,5},{7,4},{8,11},{9,10},{10,... | collective-permute-start | bytes 786440 | tf_op jit(solution)/shard_map/ppermute | solution.py:838
  5.0 1.5 %collective-permute-start.4 = (f32[1,512]{1,0:T(1,128)S(1)}, f32[1,512]{1,0:T(1,128)S(1)}, u32[]{:S(2)}, u32[]{:S(2)}) collective-permute-start(f32[1,512]{1,0:T(1,128)S(1)} %get-tuple-element.87), channel_id=1, source_target_pairs={{0,4},{4,0},{8,12},{12,8},{16,20},{20,16},{24,28},{28,24},{1,5},{5... | collective-permute-start | bytes 6152 | tf_op jit(solution)/shard_map/ppermute | solution.py:850
  6.6 1.3 %sib_pack.1 = bf16[4,128,1024]{2,1,0:T(8,128)(2,1)S(1)} custom-call(s32[1,128]{1,0:T(1,128)S(1)} %copy-done, bf16[1,128,2048]{2,1,0:T(8,128)(2,1)} %k_ref.5, bf16[1,128,2048]{2,1,0:T(8,128)(2,1)} %v_ref.5, bf16[1,128,2048]{2,1,0:T(8,128)(2,1)} %q_ref.5, f32[1,128,2048]{2,1,0:T(8,128)} %dg_ref.5), custom_call_target="tpu_custom_call" | custom-call | flops 1 | bytes 1 | tf_op jit(solution)/shard_map/sib_pack/pallas_call | solution.py:350
  7.9 0.7 %collective-permute-done.4 = f32[1,512]{1,0:T(1,128)S(1)} collective-permute-done((f32[1,512]{1,0:T(1,128)S(1)}, f32[1,512]{1,0:T(1,128)S(1)}, u32[]{:S(2)}, u32[]{:S(2)}) %collective-permute-start.4) | collective-permute-done | bytes 2080 | tf_op jit(solution)/shard_map/ppermute | solution.py:850
  8.6 4.4 %conditional.2 = (bf16[4,128,1024]{2,1,0:T(8,128)(2,1)}, bf16[1,128,4096]{2,1,0:T(8,128)(2,1)}, f32[1,2048]{1,0:T(1,128)S(1)}) conditional(s32[]{:T(128)} %bitcast, () %tuple.29, (bf16[4,128,1024]{2,1,0:T(8,128)(2,1)S(1)}, bf16[1,128,4096]{2,1,0:T(8,128)(2,1)S(1)}, f32[1,1024]{1,0:T(1,128)S(1)}) %tuple.41), branch_computations={%region_0.0_spmd, %region_1.0_spmd} | conditional | flops 2048 | bytes 8421520 | solution.py:844
  9.2 1.6 %collective-permute-start.3 = (f32[1,1024]{1,0:T(1,128)S(1)}, f32[1,1024]{1,0:T(1,128)S(1)}, u32[]{:S(2)}, u32[]{:S(2)}) collective-permute-start(f32[1,1024]{1,0:T(1,128)S(1)} %get-tuple-element.24), channel_id=1, source_target_pairs={{0,8},{4,12},{8,0},{12,4},{16,24},{20,28},{24,16},{28,20},{1,9},{5... | collective-permute-start | bytes 12296 | tf_op jit(solution)/shard_map/cond/branch_1_fun/ppermute | solution.py:850
  10.8 2.0 %collective-permute-done.3 = f32[1,1024]{1,0:T(1,128)S(1)} collective-permute-done((f32[1,1024]{1,0:T(1,128)S(1)}, f32[1,1024]{1,0:T(1,128)S(1)}, u32[]{:S(2)}, u32[]{:S(2)}) %collective-permute-start.3) | collective-permute-done | bytes 4128 | tf_op jit(solution)/shard_map/cond/branch_1_fun/ppermute | solution.py:850
  13.0 2.6 %collective-permute-start.7 = (f32[1,2048]{1,0:T(1,128)S(1)}, f32[1,2048]{1,0:T(1,128)S(1)}, u32[]{:S(2)}, u32[]{:S(2)}) collective-permute-start(f32[1,2048]{1,0:T(1,128)S(1)} %get-tuple-element.100), channel_id=1, source_target_pairs={{0,16},{4,20},{8,24},{12,28},{16,0},{20,4},{24,8},{28,12},{1,17},{... | collective-permute-start | bytes 24584 | tf_op jit(solution)/shard_map/ppermute | solution.py:850
  15.6 2.7 %local_stats.1 = (f32[3,8,256]{2,1,0:T(8,128)S(1)}, f32[1,256]{1,0:T(1,128)S(1)}, bf16[4,256,512]{2,1,0:T(8,128)(2,1)S(1)}, bf16[4,256,512]{2,1,0:T(8,128)(2,1)S(1)}, bf16[2,128,4096]{2,1,0:T(8,128)(2,1)S(1)}) custom-call(s32[1,128]{1,0:T(1,128)S(1)} %copy-done, bf16[1,128,2048]{2,1,0:T(8,128)(2,1)} %k_ref.5, bf16[1,128,2048]{2,1,0:T(8,128)(2,1)} %v_ref.5, ...), custom_call_target="tpu_custom_call" | custom-call | flops 1 | bytes 1 | tf_op jit(solution)/shard_map/local_stats/pallas_call | solution.py:476
  18.3 0.8 %cross_stats.1 = (bf16[4,256,512]{2,1,0:T(8,128)(2,1)S(1)}, f32[3,4,256]{2,1,0:T(4,128)S(1)}, bf16[2,4,256,256]{3,2,1,0:T(8,128)(2,1)S(1)}) custom-call(bf16[4,256,512]{2,1,0:T(8,128)(2,1)S(1)} %get-tuple-element.93.near.pair, bf16[4,256,512]{2,1,0:T(8,128)(2,1)S(1)} %get-tuple-element.91.far, bf16[2,128,512]{2,1,0:T(8,128)(2,1)S(1)} %collective-permute-done.5.straight, ...), custom_call_target="tpu_custom_call" | custom-call | flops 1 | bytes 1 | tf_op jit(solution)/shard_map/cross_stats/pallas_call | solution.py:525
  19.8 1.5 %collective-permute-start.8 = (f32[4,4,256]{2,1,0:T(4,128)S(1)}, f32[4,4,256]{2,1,0:T(4,128)S(1)}, u32[]{:S(2)}, u32[]{:S(2)}) collective-permute-start(f32[4,4,256]{2,1,0:T(4,128)S(1)} %get-tuple-element.102), channel_id=1, source_target_pairs={{0,2},{1,3},{2,0},{3,1},{4,6},{5,7},{6,4},{7,5},{8,10},{9,11},{10,... | collective-permute-start | bytes 49160 | tf_op jit(solution)/shard_map/ppermute | solution.py:838
  21.3 1.6 %near_grad.1 = (f32[256,512]{1,0:T(8,128)S(1)}, bf16[2,128,512]{2,1,0:T(8,128)(2,1)S(1)}, bf16[2,128,512]{2,1,0:T(8,128)(2,1)S(1)}, f32[1,256]{1,0:T(1,128)S(1)}) custom-call(bf16[4,256,512]{2,1,0:T(8,128)(2,1)S(1)} %get-tuple-element.93.near.pair, f32[3,8,256]{2,1,0:T(8,128)S(1)} %get-tuple-element.92.local, f32[3,4,256]{2,1,0:T(4,128)S(1)} %get-tuple-element.97.stats, ...), custom_call_target="tpu_custom_call" | custom-call | flops 1 | bytes 1 | tf_op jit(solution)/shard_map/near_grad/pallas_call | solution.py:590
  23.0 0.7 %collective-permute-done.8.heard = f32[4,4,256]{2,1,0:T(4,128)S(1)} collective-permute-done((f32[4,4,256]{2,1,0:T(4,128)S(1)}, f32[4,4,256]{2,1,0:T(4,128)S(1)}, u32[]{:S(2)}, u32[]{:S(2)}) %collective-permute-start.8) | collective-permute-done | bytes 16416 | tf_op jit(solution)/shard_map/ppermute | solution.py:838
  23.7 1.8 %cross_grad.1 = (bf16[2,128,512]{2,1,0:T(8,128)(2,1)}, bf16[2,128,512]{2,1,0:T(8,128)(2,1)S(1)}, bf16[256,512]{1,0:T(8,128)(2,1)S(1)}, bf16[2,256,512]{2,1,0:T(8...) custom-call(bf16[4,256,512]{2,1,0:T(8,128)(2,1)S(1)} %get-tuple-element.95.cross, ...), custom_call_target="tpu_custom_call" | custom-call | flops 1 | bytes 1 | tf_op jit(solution)/shard_map/cross_grad/pallas_call | solution.py:656
  25.5 1.5 %collective-permute-start.9 = (bf16[2,128,512]{2,1,0:T(8,128)(2,1)}, bf16[2,128,512]{2,1,0:T(8,128)(2,1)S(1)}, u32[]{:S(2)}, u32[]{:S(2)}) collective-permute-start(bf16[2,128,512]{2,1,0:T(8,128)(2,1)} %get-tuple-element.113), channel_id=1, source_target_pairs={{0,2},{1,3},{2,0},{3,1},{4,6},{5,7},{6,4},{7,5},{8,10},{9,11},{10,... | collective-permute-start | bytes 786440 | tf_op jit(solution)/shard_map/ppermute | solution.py:838
  27.0 5.5 %all-to-all-start = ((f32[32,1,512]{2,1,0:T(1,128)}), f32[32,1,512]{2,1,0:T(1,128)S(1)}, u32[]{:S(2)}, u32[]{:S(2)}) async-start(f32[32,1,512]{2,1,0:T(1,128)} %bitcast.4), calls=%async_computation | async-start | bytes 131072 | tf_op jit(solution)/shard_map/all_to_all | solution.py:889
  32.5 5.4 %conditional.3 = (f32[1,128,2048]{2,1,0:T(8,128)}, f32[1,128,2048]{2,1,0:T(8,128)}, f32[1,128,2048]{2,1,0:T(8,128)}, bf16[2,128,512]{2,1,0:T(8,128)(2,1)S(1)}, bf16[2,128,512]{2,1,0:T(8,128)(2,1)S(1)}) conditional(s32[]{:T(128)} %bitcast, () %tuple.28, (bf16[4,256,512]{2,1,0:T(8,128)(2,1)S(1)}, f32[3,8,256]{2,1,0:T(8,128)S(1)}, ...), branch_computations={%region_2.0_spmd, %region_3.0_spmd} | conditional | flops 3 | bytes 3670072 | solution.py:844
  32.5 1.7 %far_grad.1 = (bf16[3,128,1024]{2,1,0:T(8,128)(2,1)S(1)}, bf16[3,128,1024]{2,1,0:T(8,128)(2,1)S(1)}) custom-call(bf16[4,256,512]{2,1,0:T(8,128)(2,1)S(1)} %get-tuple-element.25.pair, f32[3,8,256]{2,1,0:T(8,128)S(1)} %get-tuple-element.26.local, f32[2,4,256]{2,1,0:T(4,128)S(1)} %get-tuple-element.27.final, f32[1,256]{1,0:T(1,128)S(1)} %get-tuple-element.28.gates, ...), custom_call_target="tpu_custom_call" | custom-call | flops 1 | bytes 1 | tf_op jit(solution)/shard_map/cond/branch_1_fun/far_grad/pallas_call | solution.py:703
  34.6 1.2 %own_join.1 = (f32[1,128,2048]{2,1,0:T(8,128)}, f32[1,128,2048]{2,1,0:T(8,128)}, f32[1,128,2048]{2,1,0:T(8,128)}, bf16[2,128,512]{2,1,0:T(8,128)(2,1)S(1)}) custom-call(bf16[3,128,1024]{2,1,0:T(8,128)(2,1)S(1)} %get-tuple-element.34.own), custom_call_target="tpu_custom_call" | custom-call | flops 1 | bytes 1 | tf_op jit(solution)/shard_map/cond/branch_1_fun/own_join/pallas_call | solution.py:734
  35.8 0.8 %collective-permute-done.sib = bf16[3,128,1024]{2,1,0:T(8,128)(2,1)S(1)} collective-permute-done((bf16[3,128,1024]{2,1,0:T(8,128)(2,1)S(1)}, bf16[3,128,1024]{2,1,0:T(8,128)(2,1)S(1)}, u32[]{:S(2)}, u32[]{:S(2)}) %collective-permute-start) | collective-permute-done | bytes 786464 | tf_op jit(solution)/shard_map/cond/branch_1_fun/ppermute | solution.py:838
  36.6 1.3 %sib_join.1 = (f32[1,128,2048]{2,1,0:T(8,128)}, f32[1,128,2048]{2,1,0:T(8,128)}, f32[1,128,2048]{2,1,0:T(8,128)}, bf16[2,128,512]{2,1,0:T(8,128)(2,1)S(1)}) custom-call(bf16[3,128,1024]{2,1,0:T(8,128)(2,1)S(1)} %collective-permute-done.sib, f32[1,128,2048]{2,1,0:T(8,128)} %get-tuple-element.35.dq_in, ...), custom_call_target="tpu_custom_call", output_to_operand_aliasing={{0}: (1, {}), {1}: (2, {}), {2}: (3, {})} | custom-call | flops 1 | bytes 1 | tf_op jit(solution)/shard_map/cond/branch_1_fun/sib_join/pallas_call | solution.py:769
  37.9 1.0 %add_back.1 = (f32[1,128,2048]{2,1,0:T(8,128)}, f32[1,128,2048]{2,1,0:T(8,128)}, f32[1,128,2048]{2,1,0:T(8,128)}) custom-call(bf16[2,128,512]{2,1,0:T(8,128)(2,1)S(1)} %get-tuple-element.111.own, bf16[2,128,512]{2,1,0:T(8,128)(2,1)S(1)} %get-tuple-element.112.sib, ...), custom_call_target="tpu_custom_call", output_to_operand_aliasing={{0}: (4, {}), {1}: (5, {}), {2}: (6, {})} | custom-call | flops 1 | bytes 1 | tf_op jit(solution)/shard_map/add_back/pallas_call | solution.py:820
  39.0 1.2 %all-to-all-done = f32[32,1,512]{2,1,0:T(1,128)S(1)} async-done(((f32[32,1,512]{2,1,0:T(1,128)}), f32[32,1,512]{2,1,0:T(1,128)S(1)}, u32[]{:S(2)}, u32[]{:S(2)}) %all-to-all-start) | async-done | bytes 65568 | tf_op jit(solution)/shard_map/all_to_all | solution.py:889
  (21 shorter events, 3.1 us)
Async XLA Ops:
  0.6 5.9 %copy-start = (s32[1,128]{1,0:T(1,128)S(1)}, s32[1,128]{1,0:T(1,128)}, u32[]{:S(2)}) copy-start(s32[1,128]{1,0:T(1,128)} %pos_ref.2) | copy-start | bytes 1540
  2.0 6.6 %copy-start.1 = (bf16[1,128,4096]{2,1,0:T(8,128)(2,1)S(1)}, bf16[1,128,4096]{2,1,0:T(8,128)(2,1)}, u32[]{:S(2)}) copy-start(bf16[1,128,4096]{2,1,0:T(8,128)(2,1)} %x_ref.1) | copy-start | bytes 3145732
  2.0 16.3 %collective-permute-start.6 = (bf16[2,128,512]{2,1,0:T(8,128)(2,1)S(1)}, bf16[2,128,512]{2,1,0:T(8,128)(2,1)S(1)}, u32[]{:S(2)}, u32[]{:S(2)}) collective-permute-start(bf16[2,128,512]{2,1,0:T(8,128)(2,1)S(1)} %get-tuple-element.94), channel_id=1, source_target_pairs={{0,3},{1,2},{2,1},{3,0},{4,7},{5,6},{6,5},{7,4},{8,11},{9,10},{10,... | collective-permute-start | bytes 786440 | tf_op jit(solution)/shard_map/ppermute | solution.py:838
  4.4 13.9 %collective-permute-start.5 = (bf16[2,128,512]{2,1,0:T(8,128)(2,1)S(1)}, bf16[2,128,512]{2,1,0:T(8,128)(2,1)S(1)}, u32[]{:S(2)}, u32[]{:S(2)}) collective-permute-start(bf16[2,128,512]{2,1,0:T(8,128)(2,1)S(1)} %get-tuple-element.85), channel_id=1, source_target_pairs={{0,2},{1,3},{2,0},{3,1},{4,6},{5,7},{6,4},{7,5},{8,10},{9,11},{10,... | collective-permute-start | bytes 786440 | tf_op jit(solution)/shard_map/ppermute | solution.py:838
  5.0 3.6 %collective-permute-start.4 = (f32[1,512]{1,0:T(1,128)S(1)}, f32[1,512]{1,0:T(1,128)S(1)}, u32[]{:S(2)}, u32[]{:S(2)}) collective-permute-start(f32[1,512]{1,0:T(1,128)S(1)} %get-tuple-element.87), channel_id=1, source_target_pairs={{0,4},{4,0},{8,12},{12,8},{16,20},{20,16},{24,28},{28,24},{1,5},{5... | collective-permute-start | bytes 6152 | tf_op jit(solution)/shard_map/ppermute | solution.py:850
  8.7 4.2 %collective-permute-start.1 = (bf16[4,128,1024]{2,1,0:T(8,128)(2,1)S(1)}, bf16[4,128,1024]{2,1,0:T(8,128)(2,1)}, u32[]{:S(2)}, u32[]{:S(2)}) collective-permute-start(bf16[4,128,1024]{2,1,0:T(8,128)(2,1)S(1)} %get-tuple-element.22), channel_id=1, source_target_pairs={{0,1},{1,0},{2,3},{3,2},{4,5},{5,4},{6,7},{7,6},{8,9},{9,8},{10,11... | collective-permute-start | bytes 3145736 | tf_op jit(solution)/shard_map/cond/branch_1_fun/ppermute | solution.py:838
  8.7 4.3 %collective-permute-start.2 = (bf16[1,128,4096]{2,1,0:T(8,128)(2,1)S(1)}, bf16[1,128,4096]{2,1,0:T(8,128)(2,1)}, u32[]{:S(2)}, u32[]{:S(2)}) collective-permute-start(bf16[1,128,4096]{2,1,0:T(8,128)(2,1)S(1)} %get-tuple-element.23), channel_id=1, source_target_pairs={{0,1},{1,0},{2,3},{3,2},{4,5},{5,4},{6,7},{7,6},{8,9},{9,8},{10,11... | collective-permute-start | bytes 3145736 | tf_op jit(solution)/shard_map/cond/branch_1_fun/ppermute | solution.py:838
  9.2 3.6 %collective-permute-start.3 = (f32[1,1024]{1,0:T(1,128)S(1)}, f32[1,1024]{1,0:T(1,128)S(1)}, u32[]{:S(2)}, u32[]{:S(2)}) collective-permute-start(f32[1,1024]{1,0:T(1,128)S(1)} %get-tuple-element.24), channel_id=1, source_target_pairs={{0,8},{4,12},{8,0},{12,4},{16,24},{20,28},{24,16},{28,20},{1,9},{5... | collective-permute-start | bytes 12296 | tf_op jit(solution)/shard_map/cond/branch_1_fun/ppermute | solution.py:850
  13.0 6.1 %collective-permute-start.7 = (f32[1,2048]{1,0:T(1,128)S(1)}, f32[1,2048]{1,0:T(1,128)S(1)}, u32[]{:S(2)}, u32[]{:S(2)}) collective-permute-start(f32[1,2048]{1,0:T(1,128)S(1)} %get-tuple-element.100), channel_id=1, source_target_pairs={{0,16},{4,20},{8,24},{12,28},{16,0},{20,4},{24,8},{28,12},{1,17},{... | collective-permute-start | bytes 24584 | tf_op jit(solution)/shard_map/ppermute | solution.py:850
  19.8 3.8 %collective-permute-start.8 = (f32[4,4,256]{2,1,0:T(4,128)S(1)}, f32[4,4,256]{2,1,0:T(4,128)S(1)}, u32[]{:S(2)}, u32[]{:S(2)}) collective-permute-start(f32[4,4,256]{2,1,0:T(4,128)S(1)} %get-tuple-element.102), channel_id=1, source_target_pairs={{0,2},{1,3},{2,0},{3,1},{4,6},{5,7},{6,4},{7,5},{8,10},{9,11},{10,... | collective-permute-start | bytes 49160 | tf_op jit(solution)/shard_map/ppermute | solution.py:838
  25.5 12.4 %collective-permute-start.9 = (bf16[2,128,512]{2,1,0:T(8,128)(2,1)}, bf16[2,128,512]{2,1,0:T(8,128)(2,1)S(1)}, u32[]{:S(2)}, u32[]{:S(2)}) collective-permute-start(bf16[2,128,512]{2,1,0:T(8,128)(2,1)} %get-tuple-element.113), channel_id=1, source_target_pairs={{0,2},{1,3},{2,0},{3,1},{4,6},{5,7},{6,4},{7,5},{8,10},{9,11},{10,... | collective-permute-start | bytes 786440 | tf_op jit(solution)/shard_map/ppermute | solution.py:838
  27.0 11.0 %collective-permute-start.10 = (bf16[2,128,512]{2,1,0:T(8,128)(2,1)S(1)}, bf16[2,128,512]{2,1,0:T(8,128)(2,1)S(1)}, u32[]{:S(2)}, u32[]{:S(2)}) collective-permute-start(bf16[2,128,512]{2,1,0:T(8,128)(2,1)S(1)} %get-tuple-element.114), channel_id=1, source_target_pairs={{0,3},{1,2},{2,1},{3,0},{4,7},{5,6},{6,5},{7,4},{8,11},{9,10},{10,... | collective-permute-start | bytes 786440 | tf_op jit(solution)/shard_map/ppermute | solution.py:838
  27.0 13.2 %all-to-all-start = ((f32[32,1,512]{2,1,0:T(1,128)}), f32[32,1,512]{2,1,0:T(1,128)S(1)}, u32[]{:S(2)}, u32[]{:S(2)}) async-start(f32[32,1,512]{2,1,0:T(1,128)} %bitcast.4), calls=%async_computation | async-start | bytes 131072 | tf_op jit(solution)/shard_map/all_to_all | solution.py:889
  34.3 2.4 %collective-permute-start = (bf16[3,128,1024]{2,1,0:T(8,128)(2,1)S(1)}, bf16[3,128,1024]{2,1,0:T(8,128)(2,1)S(1)}, u32[]{:S(2)}, u32[]{:S(2)}) collective-permute-start(bf16[3,128,1024]{2,1,0:T(8,128)(2,1)S(1)} %get-tuple-element.33), channel_id=1, source_target_pairs={{0,1},{1,0},{2,3},{3,2},{4,5},{5,4},{6,7},{7,6},{8,9},{9,8},{10,11... | collective-permute-start | bytes 2359304 | tf_op jit(solution)/shard_map/cond/branch_1_fun/ppermute | solution.py:838

commit v20 on v18

--- a/solution.py
+++ b/solution.py
@@ -614,7 +614,7 @@
             out_ref[j, i] = term[:, j * chunk : (j + 1) * chunk]
 
 
-def cross_grad_kernel(scale, total, cross, kept, stats, local, heard, gates, near_dq, near_sum, rows_x, straight, diag, dq_out, keep, final, terms, held, sem):
+def cross_grad_kernel(scale, total, cross, kept, stats, local, heard, gates, near_dq, near_sum, rows_x, near_own, near_sib, straight, diag, own_low, sib_low, keep, final, terms, held, sem):
     slots, width = straight.shape[1], straight.shape[2]
     heads = width // HEAD
     first = here()[1] == 0
@@ -630,6 +630,9 @@
     put_terms(sums * gates[...] * (1.0 - gates[...]) * (1.0 / total), rows_x, held)
     leaving = pltpu.make_async_copy(held, terms, sem)
     leaving.start()
+    for i in range(2):
+        own_low[1 + i] = near_own[i]
+        sib_low[1 + i] = near_sib[i]
     for h in range(heads):
         cols = slice(h * HEAD, (h + 1) * HEAD)
         row = slice(h, h + 1)
@@ -637,7 +640,9 @@
             cross[2, :, cols], cross[0, :, cols], cross[3, :, cols],
             kept[0, h].astype(F32), kept[1, h].astype(F32), scale, factor[row], delta[row],
         )
-        dq_out[:, cols] = (near_dq[:, cols] + late * dq).astype(BF16)
+        whole = (near_dq[:, cols] + late * dq).astype(BF16)
+        own_low[0, :, cols] = whole[:slots]
+        sib_low[0, :, cols] = whole[slots:]
         keep[0, :, cols] = dk.astype(BF16)
         keep[1, :, cols] = dv.astype(BF16)
         sent = jnp.where(first, dq, dk).astype(BF16)
@@ -648,7 +653,7 @@
     leaving.wait()
 
 
-def cross_grad(cross, kept, stats, local, heard, gates, near_dq, near_sum, rows_x, parts, copies, total):
+def cross_grad(cross, kept, stats, local, heard, gates, near_dq, near_sum, rows_x, near_own, near_sib, parts, copies, total):
     _, rows, width = cross.shape
     slots = rows // 2
     out = pltpu.VMEM((2, slots, width), BF16)
@@ -658,33 +663,28 @@
         out_shape=[
             out,
             out,
-            pltpu.VMEM((rows, width), BF16),
+            pltpu.VMEM((3, slots, width), BF16),
+            pltpu.VMEM((3, slots, width), BF16),
             pltpu.VMEM((2, rows, width), BF16),
             jax.ShapeDtypeStruct((2, width // HEAD, rows), F32),
             pltpu.HBM(spread, F32),
         ],
-        in_specs=[VMEM] * 9,
-        out_specs=[VMEM] * 5 + [pl.BlockSpec(memory_space=pltpu.HBM)],
+        in_specs=[VMEM] * 11,
+        out_specs=[VMEM] * 6 + [pl.BlockSpec(memory_space=pltpu.HBM)],
         scratch_shapes=[pltpu.VMEM(spread, F32), pltpu.SemaphoreType.DMA],
         compiler_params=params(),
         cost_estimate=cost(24 * slots * slots * width, 64 * slots * width),
         name="cross_grad",
-    )(cross, kept, stats, local, heard, gates, near_dq, near_sum, rows_x)
-
-
-def far_grad_kernel(scale, pair, local, final, gates, keep, near_dq, near_own, near_sib, own_out, sib_out):
+    )(cross, kept, stats, local, heard, gates, near_dq, near_sum, rows_x, near_own, near_sib)
+
+
+def far_grad_kernel(scale, pair, local, final, gates, keep, own_out, sib_out):
     slots, width = pair.shape[1] // 2, pair.shape[2]
     heads = width // HEAD
     early = jnp.where(here()[1] == 0, 1.0, 0.0)
     factor = final[0] * gates[...]
     mask = local_mask(here()[0], pair)
-    own_out[0, :, :width] = near_dq[:slots]
-    sib_out[0, :, :width] = near_dq[slots:]
-    for i in range(2):
-        own_out[1 + i, :, :width] = near_own[i]
-        sib_out[1 + i, :, :width] = near_sib[i]
     for h in range(heads):
-        cols = slice(width + h * HEAD, width + (h + 1) * HEAD)
         at = slice(h * HEAD, (h + 1) * HEAD)
         row = slice(h, h + 1)
         top = local[0, heads + h : heads + h + 1]
@@ -692,96 +692,100 @@
         dk = dk + early * keep[0, :, at].astype(F32)
         dv = dv + early * keep[1, :, at].astype(F32)
         for i, part in enumerate((dq, dk, dv)):
-            own_out[i, :, cols] = part[:slots].astype(BF16)
-            sib_out[i, :, cols] = part[slots:].astype(BF16)
-
-
-def far_grad(pair, local, final, gates, keep, near_dq, near_own, near_sib):
+            own_out[i, :, at] = part[:slots].astype(BF16)
+            sib_out[i, :, at] = part[slots:].astype(BF16)
+
+
+def far_grad(pair, local, final, gates, keep):
     _, rows, width = pair.shape
-    slots, half = rows // 2, 2 * width
-    out = jax.ShapeDtypeStruct((3, slots, half), BF16)
+    slots = rows // 2
+    out = jax.ShapeDtypeStruct((3, slots, width), BF16)
     return pl.pallas_call(
         functools.partial(far_grad_kernel, HEAD**-0.5),
         out_shape=[out, out],
-        in_specs=[VMEM] * 8,
+        in_specs=[VMEM] * 5,
         out_specs=[VMEM] * 2,
         compiler_params=params(),
-        cost_estimate=cost(20 * slots * slots * half, 40 * slots * half),
+        cost_estimate=cost(20 * slots * slots * width, 40 * slots * width),
         name="far_grad",
-    )(pair, local, final, gates, keep, near_dq, near_own, near_sib)
-
-
-def own_join_kernel(own, dq_out, dk_out, dv_out, waiting, total, sems):
-    slots, half = own.shape[1], own.shape[2]
-    width = half // 2
+    )(pair, local, final, gates, keep)
+
+
+def own_join_kernel(low, high, dq_out, dk_out, dv_out, waiting, total, sems):
+    width = low.shape[2]
     core, chip = here()
-    cols = pl.ds(pl.multiple_of(core * half, HEAD), half)
+    cols = pl.ds(pl.multiple_of(core * 2 * width, HEAD), 2 * width)
     stores = []
     for j, out in enumerate((dq_out, dk_out, dv_out)):
-        total[j] = own[j].astype(F32)
+        total[j, :, :width] = low[j].astype(F32)
+        total[j, :, width:] = high[j].astype(F32)
         stores.append(pltpu.make_async_copy(total.at[j], out.at[0, :, cols], sems.at[j]))
         stores[-1].start()
     waiting[0] = jnp.where(chip == 0, total[1, :, :width], total[0, :, width:]).astype(BF16)
-    waiting[1] = own[2, :, :width]
+    waiting[1] = low[2]
     for c in stores:
         c.wait()
 
 
-def own_join(own, shape):
+def own_join(low, high, shape):
     out = pltpu.HBM(shape, F32)
-    _, slots, half = own.shape
+    _, slots, width = low.shape
     hbm = pl.BlockSpec(memory_space=pltpu.HBM)
     return pl.pallas_call(
         own_join_kernel,
-        out_shape=[out] * 3 + [jax.ShapeDtypeStruct((2, slots, half // 2), BF16)],
-        in_specs=[VMEM],
+        out_shape=[out] * 3 + [jax.ShapeDtypeStruct((2, slots, width), BF16)],
+        in_specs=[VMEM] * 2,
         out_specs=[hbm] * 3 + [VMEM],
-        scratch_shapes=[pltpu.VMEM((3, slots, half), F32), pltpu.SemaphoreType.DMA((3,))],
-        compiler_params=params(),
-        cost_estimate=cost(0, 18 * own.size),
+        scratch_shapes=[pltpu.VMEM((3, slots, 2 * width), F32), pltpu.SemaphoreType.DMA((3,))],
+        compiler_params=params(),
+        cost_estimate=cost(0, 36 * low.size),
         name="own_join",
-    )(own)
-
-
-def sib_join_kernel(sib, dq_in, dk_in, dv_in, dq_out, dk_out, dv_out, waiting, low, total, in_sems, out_sems):
-    half = sib.shape[2]
-    width = half // 2
+    )(low, high)
+
+
+def sib_join_kernel(low, high, dq_in, dk_in, dv_in, dq_out, dk_out, dv_out, waiting, parts, total, in_sems, out_sems):
+    width = low.shape[2]
     core, chip = here()
-    loads = [pltpu.make_async_copy(sib.at[j], low.at[j], in_sems.at[j]) for j in range(3)]
-    for c in loads:
-        c.start()
-    cols = pl.ds(pl.multiple_of((1 - core) * half, HEAD), half)
+    loads = [
+        [pltpu.make_async_copy(ref.at[j], parts.at[i, j], in_sems.at[3 * i + j]) for i, ref in enumerate((low, high))]
+        for j in range(3)
+    ]
+    for pair in loads:
+        for c in pair:
+            c.start()
+    cols = pl.ds(pl.multiple_of((1 - core) * 2 * width, HEAD), 2 * width)
     stores = []
     for j, out in enumerate((dq_out, dk_out, dv_out)):
-        loads[j].wait()
-        total[j] = low[j].astype(F32)
+        for i in range(2):
+            loads[j][i].wait()
+            total[j, :, i * width : (i + 1) * width] = parts[i, j].astype(F32)
         stores.append(pltpu.make_async_copy(total.at[j], out.at[0, :, cols], out_sems.at[j]))
         stores[-1].start()
     waiting[0] = jnp.where(chip == 0, total[1, :, :width], total[0, :, width:]).astype(BF16)
-    waiting[1] = low[2, :, :width]
+    waiting[1] = parts[0, 2]
     for c in stores:
         c.wait()
 
 
-def sib_join(sib, outs):
-    _, slots, half = sib.shape
+def sib_join(low, high, outs):
+    _, slots, width = low.shape
     hbm = pl.BlockSpec(memory_space=pltpu.HBM)
     return pl.pallas_call(
         sib_join_kernel,
-        out_shape=[pltpu.HBM(o.shape, F32) for o in outs] + [pltpu.VMEM((2, slots, half // 2), BF16)],
-        in_specs=[pl.BlockSpec(memory_space=pl.ANY)] + [hbm] * 3,
+        out_shape=[pltpu.HBM(o.shape, F32) for o in outs] + [pltpu.VMEM((2, slots, width), BF16)],
+        in_specs=[pl.BlockSpec(memory_space=pl.ANY)] * 2 + [hbm] * 3,
         out_specs=[hbm] * 3 + [VMEM],
         scratch_shapes=[
-            pltpu.VMEM((3, slots, half), BF16),
-            pltpu.VMEM((3, slots, half), F32),
-            pltpu.SemaphoreType.DMA((3,)),
+            pltpu.VMEM((2, 3, slots, width), BF16),
+            pltpu.VMEM((3, slots, 2 * width), F32),
+            pltpu.SemaphoreType.DMA((6,)),
             pltpu.SemaphoreType.DMA((3,)),
         ],
-        input_output_aliases={1: 0, 2: 1, 3: 2},
-        compiler_params=params(),
-        cost_estimate=cost(0, 12 * sib.size),
+        input_output_aliases={2: 0, 3: 1, 4: 2},
+        compiler_params=params(),
+        cost_estimate=cost(0, 24 * low.size),
         name="sib_join",
-    )(sib, *in_hbm(*outs))
+    )(low, high, *in_hbm(*outs))
 
 
 def add_back_kernel(own, sib, straight, diag, dq_in, dk_in, dv_in, dq_out, dk_out, dv_out, total, sems):
@@ -858,11 +862,12 @@
             step *= 2
         return sib, x_sib, w_part
 
-    def far_phase(*operands):
-        own_out, sib_out = far_grad(*operands)
-        sib_in = send(sib_out, 1)
-        *outs, waiting = own_join(own_out, queries.shape)
-        *outs, waiting_sib = sib_join(sib_in, outs)
+    def far_phase(own_low, sib_low, *operands):
+        sib_in = [send(sib_low, 1)]
+        own_high, sib_high = far_grad(*operands)
+        sib_in.append(send(sib_high, 1))
+        *outs, waiting = own_join(own_low, own_high, queries.shape)
+        *outs, waiting_sib = sib_join(*sib_in, outs)
         return outs, waiting, waiting_sib
 
     out_s, out_d, w_part = cross_pack(route_pos, w_router, keys, values, queries, d_gated)
@@ -881,13 +886,13 @@
     heard = send(message, 2)
     near_dq, near_own, near_sib, near_sum = near_grad(near, local, stats, gates)
     total = float(ndp * n * slots // 2)
-    back_s, back_d, dq_low, keep, final, terms = cross_grad(
-        cross, kept, stats, local, heard, gates, near_dq, near_sum, rows_x, ndp, n, total
+    back_s, back_d, own_low, sib_low, keep, final, terms = cross_grad(
+        cross, kept, stats, local, heard, gates, near_dq, near_sum, rows_x, near_own, near_sib, ndp, n, total
     )
 
     ret_s, ret_d = send(back_s, 2), send(back_d, 3)
     shared = lax.all_to_all(terms.reshape(ndp * n, 1, -1), ("dp", "ctx"), 0, 0, tiled=True)
-    outs, waiting, waiting_sib = beside(far_phase, far, local, final, gates, keep, dq_low, near_own, near_sib)
+    outs, waiting, waiting_sib = beside(far_phase, own_low, sib_low, far, local, final, gates, keep)
     dq, dk, dv = add_back(waiting, waiting_sib, ret_s, ret_d, outs)
     router_grad = jnp.sum(after(shared, dq), axis=(0, 1))
     return dq, dk, dv, router_grad

time: 41 us -> 41 us (level)
  waiting for transfers between devices: 5.61 us -> 4.4 us
  Pallas kernels: 15.5 us -> 16.4 us
    pallas_call x1, Pallas kernels: 1.28 us -> 2.24 us  [sib_join(): pl.pallas_call(sib_join_kernel, out_shape=[pltpu.HBM(o.shape, F32) for o...]
    all_to_all x1, waiting for transfers between devices: 1.18 us -> 0.55 us  [swap_body(): lax.all_to_all(terms.reshape(ndp * n, 1, -1), ('dp', 'ctx'), 0, 0, tiled=...]
    ppermute x8 -> x9, waiting for transfers between devices: 1.69 us -> 1.11 us  [send(): return lax.ppermute(a, 'ctx', [(i, i ^ flip) for i in range(n)])]
    ppermute x8 -> x9, starting transfers between devices: 6.84 us -> 7.17 us  [send(): return lax.ppermute(a, 'ctx', [(i, i ^ flip) for i in range(n)])]
  transfers between devices with their start and end apart: 12 -> 13, of which waited for: 6 -> 6; matrix products, arithmetic and copies ran while one was open for 0% -> 0% of each run, Pallas kernels for 29% -> 31%
where the time goes in v20:
time: 41 us; the launch traced here: 40.8 us
  starting transfers between devices  18.4 us (45%)
  Pallas kernels  16.4 us (40%)
  waiting for transfers between devices  4.4 us (11%)
  between operations  0.81 us (2%)
  other arithmetic  0.68 us (2%)
    ppermute x9, starting transfers between devices, send(): return lax.ppermute(a, 'ctx', [(i, i ^ flip) for i in range(n)])  7.17 us
    ppermute x3, starting transfers between devices, widen(): other = lax.ppermute(part, 'dp', [(i, i ^ step) for i in range(ndp)])  5.68 us
    all_to_all x1, starting transfers between devices, swap_body(): lax.all_to_all(terms.reshape(ndp * n, 1, -1), ('dp', 'ctx'), 0, 0, tiled=...  5.55 us
    ppermute x3, waiting for transfers between devices, widen(): other = lax.ppermute(part, 'dp', [(i, i ^ step) for i in range(ndp)])  2.74 us
    pallas_call x1, Pallas kernels, local_stats(): pl.pallas_call(functools.partial(local_stats_kernel, HEAD ** (-0.5)), out...  2.69 us
    pallas_call x1, Pallas kernels, sib_join(): pl.pallas_call(sib_join_kernel, out_shape=[pltpu.HBM(o.shape, F32) for o...  2.24 us
    pallas_call x1, Pallas kernels, cross_grad(): pl.pallas_call(functools.partial(cross_grad_kernel, HEAD ** (-0.5), total...  1.84 us
    pallas_call x1, Pallas kernels, far_grad(): pl.pallas_call(functools.partial(far_grad_kernel, HEAD ** (-0.5)), out_sh...  1.64 us
  transfers between devices with their start and end apart: 13, of which 6 were waited for; matrix products, arithmetic and copies ran while one was open for 0% of the time, Pallas kernels for 31%

profile of v20, /device:TPU:0, one launch (start us, length us, event | category | flops | bytes accessed | tf_op | source)
XLA Modules:
  0.0 40.8 jit_solution(9108087106872106122)
XLA Ops:
  0.6 1.3 %cross_pack.1 = (bf16[2,128,512]{2,1,0:T(8,128)(2,1)S(1)}, bf16[2,128,512]{2,1,0:T(8,128)(2,1)S(1)}, f32[1,512]{1,0:T(1,128)S(1)}) custom-call(s32[1,128]{1,0:T(1,128)} %pos_ref.2, bf16[512]{0:T(512)(128)(2,1)} %w_any.1, bf16[1,128,2048]{2,1,0:T(8,128)(2,1)} %k_ref.5, bf16[1,128,2048]{2,1,0:T(8,128)(2,1)} %v_ref.5, bf16[1,128,2048]{2,1,0:T(8,128)(2,1)} %q_ref.5, ...), custom_call_target="tpu_custom_call" | custom-call | flops 1 | bytes 1 | tf_op jit(solution)/shard_map/cross_pack/pallas_call | solution.py:314
  2.0 2.4 %collective-permute-start.7 = (bf16[2,128,512]{2,1,0:T(8,128)(2,1)S(1)}, bf16[2,128,512]{2,1,0:T(8,128)(2,1)S(1)}, u32[]{:S(2)}, u32[]{:S(2)}) collective-permute-start(bf16[2,128,512]{2,1,0:T(8,128)(2,1)S(1)} %get-tuple-element.91), channel_id=1, source_target_pairs={{0,3},{1,2},{2,1},{3,0},{4,7},{5,6},{6,5},{7,4},{8,11},{9,10},{10,... | collective-permute-start | bytes 786440 | tf_op jit(solution)/shard_map/ppermute | solution.py:842
  5.0 1.5 %collective-permute-start.5 = (f32[1,512]{1,0:T(1,128)S(1)}, f32[1,512]{1,0:T(1,128)S(1)}, u32[]{:S(2)}, u32[]{:S(2)}) collective-permute-start(f32[1,512]{1,0:T(1,128)S(1)} %get-tuple-element.85), channel_id=1, source_target_pairs={{0,4},{4,0},{8,12},{12,8},{16,20},{20,16},{24,28},{28,24},{1,5},{5... | collective-permute-start | bytes 6152 | tf_op jit(solution)/shard_map/ppermute | solution.py:854
  6.6 1.3 %sib_pack.1 = bf16[4,128,1024]{2,1,0:T(8,128)(2,1)S(1)} custom-call(s32[1,128]{1,0:T(1,128)S(1)} %copy-done, bf16[1,128,2048]{2,1,0:T(8,128)(2,1)} %k_ref.5, bf16[1,128,2048]{2,1,0:T(8,128)(2,1)} %v_ref.5, bf16[1,128,2048]{2,1,0:T(8,128)(2,1)} %q_ref.5, f32[1,128,2048]{2,1,0:T(8,128)} %dg_ref.5), custom_call_target="tpu_custom_call" | custom-call | flops 1 | bytes 1 | tf_op jit(solution)/shard_map/sib_pack/pallas_call | solution.py:350
  7.9 0.7 %collective-permute-done.5 = f32[1,512]{1,0:T(1,128)S(1)} collective-permute-done((f32[1,512]{1,0:T(1,128)S(1)}, f32[1,512]{1,0:T(1,128)S(1)}, u32[]{:S(2)}, u32[]{:S(2)}) %collective-permute-start.5) | collective-permute-done | bytes 2080 | tf_op jit(solution)/shard_map/ppermute | solution.py:854
  8.6 4.4 %conditional.2 = (bf16[4,128,1024]{2,1,0:T(8,128)(2,1)}, bf16[1,128,4096]{2,1,0:T(8,128)(2,1)}, f32[1,2048]{1,0:T(1,128)S(1)}) conditional(s32[]{:T(128)} %bitcast, () %tuple.29, (bf16[4,128,1024]{2,1,0:T(8,128)(2,1)S(1)}, bf16[1,128,4096]{2,1,0:T(8,128)(2,1)S(1)}, f32[1,1024]{1,0:T(1,128)S(1)}) %tuple.41), branch_computations={%region_0.0_spmd, %region_1.0_spmd} | conditional | flops 2048 | bytes 8421520 | solution.py:848
  9.2 1.6 %collective-permute-start.4 = (f32[1,1024]{1,0:T(1,128)S(1)}, f32[1,1024]{1,0:T(1,128)S(1)}, u32[]{:S(2)}, u32[]{:S(2)}) collective-permute-start(f32[1,1024]{1,0:T(1,128)S(1)} %get-tuple-element.22), channel_id=1, source_target_pairs={{0,8},{4,12},{8,0},{12,4},{16,24},{20,28},{24,16},{28,20},{1,9},{5... | collective-permute-start | bytes 12296 | tf_op jit(solution)/shard_map/cond/branch_1_fun/ppermute | solution.py:854
  10.8 2.0 %collective-permute-done.4 = f32[1,1024]{1,0:T(1,128)S(1)} collective-permute-done((f32[1,1024]{1,0:T(1,128)S(1)}, f32[1,1024]{1,0:T(1,128)S(1)}, u32[]{:S(2)}, u32[]{:S(2)}) %collective-permute-start.4) | collective-permute-done | bytes 4128 | tf_op jit(solution)/shard_map/cond/branch_1_fun/ppermute | solution.py:854
  13.0 2.6 %collective-permute-start.8 = (f32[1,2048]{1,0:T(1,128)S(1)}, f32[1,2048]{1,0:T(1,128)S(1)}, u32[]{:S(2)}, u32[]{:S(2)}) collective-permute-start(f32[1,2048]{1,0:T(1,128)S(1)} %get-tuple-element.98), channel_id=1, source_target_pairs={{0,16},{4,20},{8,24},{12,28},{16,0},{20,4},{24,8},{28,12},{1,17},{... | collective-permute-start | bytes 24584 | tf_op jit(solution)/shard_map/ppermute | solution.py:854
  15.6 2.7 %local_stats.1 = (f32[3,8,256]{2,1,0:T(8,128)S(1)}, f32[1,256]{1,0:T(1,128)S(1)}, bf16[4,256,512]{2,1,0:T(8,128)(2,1)S(1)}, bf16[4,256,512]{2,1,0:T(8,128)(2,1)S(1)}, bf16[2,128,4096]{2,1,0:T(8,128)(2,1)S(1)}) custom-call(s32[1,128]{1,0:T(1,128)S(1)} %copy-done, bf16[1,128,2048]{2,1,0:T(8,128)(2,1)} %k_ref.5, bf16[1,128,2048]{2,1,0:T(8,128)(2,1)} %v_ref.5, ...), custom_call_target="tpu_custom_call" | custom-call | flops 1 | bytes 1 | tf_op jit(solution)/shard_map/local_stats/pallas_call | solution.py:476
  18.3 0.8 %cross_stats.1 = (bf16[4,256,512]{2,1,0:T(8,128)(2,1)S(1)}, f32[3,4,256]{2,1,0:T(4,128)S(1)}, bf16[2,4,256,256]{3,2,1,0:T(8,128)(2,1)S(1)}) custom-call(bf16[4,256,512]{2,1,0:T(8,128)(2,1)S(1)} %get-tuple-element.89.near.pair, bf16[4,256,512]{2,1,0:T(8,128)(2,1)S(1)} %get-tuple-element.90.far, bf16[2,128,512]{2,1,0:T(8,128)(2,1)S(1)} %collective-permute-done.6.straight, ...), custom_call_target="tpu_custom_call" | custom-call | flops 1 | bytes 1 | tf_op jit(solution)/shard_map/cross_stats/pallas_call | solution.py:525
  19.2 0.7 %router_gate.1 = (f32[1,256]{1,0:T(1,128)S(1)}, f32[4,4,256]{2,1,0:T(4,128)S(1)}) custom-call(f32[1,256]{1,0:T(1,128)S(1)} %get-tuple-element.96.live_ref, bf16[2,128,4096]{2,1,0:T(8,128)(2,1)S(1)} %get-tuple-element.97.rows_x, f32[1,4096]{1,0:T(1,128)S(1)} %pad_maximum_fusion.1.w_ref, f32[3,8,256]{2,1,0:T(8,128)S(1)} %get-tuple-element.95.local, ...), custom_call_target="tpu_custom_call" | custom-call | flops 1 | bytes 1 | tf_op jit(solution)/shard_map/router_gate/pallas_call | solution.py:382
  19.8 1.5 %collective-permute-start.9 = (f32[4,4,256]{2,1,0:T(4,128)S(1)}, f32[4,4,256]{2,1,0:T(4,128)S(1)}, u32[]{:S(2)}, u32[]{:S(2)}) collective-permute-start(f32[4,4,256]{2,1,0:T(4,128)S(1)} %get-tuple-element.100), channel_id=1, source_target_pairs={{0,2},{1,3},{2,0},{3,1},{4,6},{5,7},{6,4},{7,5},{8,10},{9,11},{10,... | collective-permute-start | bytes 49160 | tf_op jit(solution)/shard_map/ppermute | solution.py:842
  21.3 1.6 %near_grad.1 = (f32[256,512]{1,0:T(8,128)S(1)}, bf16[2,128,512]{2,1,0:T(8,128)(2,1)S(1)}, bf16[2,128,512]{2,1,0:T(8,128)(2,1)S(1)}, f32[1,256]{1,0:T(1,128)S(1)}) custom-call(bf16[4,256,512]{2,1,0:T(8,128)(2,1)S(1)} %get-tuple-element.89.near.pair, f32[3,8,256]{2,1,0:T(8,128)S(1)} %get-tuple-element.95.local, f32[3,4,256]{2,1,0:T(4,128)S(1)} %get-tuple-element.94.stats, ...), custom_call_target="tpu_custom_call" | custom-call | flops 1 | bytes 1 | tf_op jit(solution)/shard_map/near_grad/pallas_call | solution.py:590
  23.0 0.7 %collective-permute-done.9.heard = f32[4,4,256]{2,1,0:T(4,128)S(1)} collective-permute-done((f32[4,4,256]{2,1,0:T(4,128)S(1)}, f32[4,4,256]{2,1,0:T(4,128)S(1)}, u32[]{:S(2)}, u32[]{:S(2)}) %collective-permute-start.9) | collective-permute-done | bytes 16416 | tf_op jit(solution)/shard_map/ppermute | solution.py:842
  23.7 1.8 %cross_grad.1 = (bf16[2,128,512]{2,1,0:T(8,128)(2,1)}, bf16[2,128,512]{2,1,0:T(8,128)(2,1)S(1)}, bf16[3,128,512]{2,1,0:T(8,128)(2,1)S(1)}, bf16[3,128,512]{2,1,0...) custom-call(bf16[4,256,512]{2,1,0:T(8,128)(2,1)S(1)} %get-tuple-element.92., ...), custom_call_target="tpu_custom_call" | custom-call | flops 1 | bytes 1 | tf_op jit(solution)/shard_map/cross_grad/pallas_call | solution.py:661
  25.5 1.5 %collective-permute-start.10 = (bf16[2,128,512]{2,1,0:T(8,128)(2,1)}, bf16[2,128,512]{2,1,0:T(8,128)(2,1)S(1)}, u32[]{:S(2)}, u32[]{:S(2)}) collective-permute-start(bf16[2,128,512]{2,1,0:T(8,128)(2,1)} %get-tuple-element.112), channel_id=1, source_target_pairs={{0,2},{1,3},{2,0},{3,1},{4,6},{5,7},{6,4},{7,5},{8,10},{9,11},{10,... | collective-permute-start | bytes 786440 | tf_op jit(solution)/shard_map/ppermute | solution.py:842
  27.0 5.6 %all-to-all-start = ((f32[32,1,512]{2,1,0:T(1,128)}), f32[32,1,512]{2,1,0:T(1,128)S(1)}, u32[]{:S(2)}, u32[]{:S(2)}) async-start(f32[32,1,512]{2,1,0:T(1,128)} %bitcast.4), calls=%async_computation | async-start | bytes 131072 | tf_op jit(solution)/shard_map/all_to_all | solution.py:894
  32.5 6.0 %conditional.3 = (f32[1,128,2048]{2,1,0:T(8,128)}, f32[1,128,2048]{2,1,0:T(8,128)}, f32[1,128,2048]{2,1,0:T(8,128)}, bf16[2,128,512]{2,1,0:T(8,128)(2,1)S(1)}, bf16[2,128,512]{2,1,0:T(8,128)(2,1)S(1)}) conditional(s32[]{:T(128)} %bitcast, () %tuple.28, (bf16[3,128,512]{2,1,0:T(8,128)(2,1)S(1)}, bf16[4,256,512]{2,1,0:T(8,128)(2,1)S(1)}, ...), branch_computations={%region_2.0_spmd, %region_3.0_spmd} | conditional | flops 3 | bytes 3670072 | solution.py:848
  32.9 1.6 %far_grad.1 = (bf16[3,128,512]{2,1,0:T(8,128)(2,1)S(1)}, bf16[3,128,512]{2,1,0:T(8,128)(2,1)S(1)}) custom-call(bf16[4,256,512]{2,1,0:T(8,128)(2,1)S(1)} %get-tuple-element.24.pair, f32[3,8,256]{2,1,0:T(8,128)S(1)} %get-tuple-element.25.local, f32[2,4,256]{2,1,0:T(4,128)S(1)} %get-tuple-element.26.final, f32[1,256]{1,0:T(1,128)S(1)} %get-tuple-element.27.gates, ...), custom_call_target="tpu_custom_call" | custom-call | flops 1 | bytes 1 | tf_op jit(solution)/shard_map/cond/branch_1_fun/far_grad/pallas_call | solution.py:703
  34.8 1.2 %own_join.1 = (f32[1,128,2048]{2,1,0:T(8,128)}, f32[1,128,2048]{2,1,0:T(8,128)}, f32[1,128,2048]{2,1,0:T(8,128)}, bf16[2,128,512]{2,1,0:T(8,128)(2,1)S(1)}) custom-call(bf16[3,128,512]{2,1,0:T(8,128)(2,1)S(1)} %get-tuple-element.30.low, bf16[3,128,512]{2,1,0:T(8,128)(2,1)S(1)} %get-tuple-element.31.high), custom_call_target="tpu_custom_call" | custom-call | flops 1 | bytes 1 | tf_op jit(solution)/shard_map/cond/branch_1_fun/own_join/pallas_call | solution.py:734
  36.3 2.2 %sib_join.1 = (f32[1,128,2048]{2,1,0:T(8,128)}, f32[1,128,2048]{2,1,0:T(8,128)}, f32[1,128,2048]{2,1,0:T(8,128)}, bf16[2,128,512]{2,1,0:T(8,128)(2,1)S(1)}) custom-call(bf16[3,128,512]{2,1,0:T(8,128)(2,1)S(1)} %collective-permute-done.low, ...), custom_call_target="tpu_custom_call", output_to_operand_aliasing={{0}: (2, {}), {1}: (3, {}), {2}: (4, {})} | custom-call | flops 1 | bytes 1 | tf_op jit(solution)/shard_map/cond/branch_1_fun/sib_join/pallas_call | solution.py:773
  38.6 1.0 %add_back.1 = (f32[1,128,2048]{2,1,0:T(8,128)}, f32[1,128,2048]{2,1,0:T(8,128)}, f32[1,128,2048]{2,1,0:T(8,128)}) custom-call(bf16[2,128,512]{2,1,0:T(8,128)(2,1)S(1)} %get-tuple-element.110.own, bf16[2,128,512]{2,1,0:T(8,128)(2,1)S(1)} %get-tuple-element.111.sib, ...), custom_call_target="tpu_custom_call", output_to_operand_aliasing={{0}: (4, {}), {1}: (5, {}), {2}: (6, {})} | custom-call | flops 1 | bytes 1 | tf_op jit(solution)/shard_map/add_back/pallas_call | solution.py:824
  40.2 0.6 %reduce_sum.9 = f32[512]{0:T(512)} reduce(f32[32,1,512]{2,1,0:T(1,128)S(1)} %all-to-all-done, f32[]{:T(128)} %constant.9.clone.1), dimensions={0,1}, to_apply=%region_4.0 | reduce | flops 15872 | bytes 67588 | tf_op jit(solution)/shard_map/reduce_sum | solution.py:897
  (23 shorter events, 2.9 us)
Async XLA Ops:
  0.6 5.9 %copy-start = (s32[1,128]{1,0:T(1,128)S(1)}, s32[1,128]{1,0:T(1,128)}, u32[]{:S(2)}) copy-start(s32[1,128]{1,0:T(1,128)} %pos_ref.2) | copy-start | bytes 1540
  2.0 6.6 %copy-start.1 = (bf16[1,128,4096]{2,1,0:T(8,128)(2,1)S(1)}, bf16[1,128,4096]{2,1,0:T(8,128)(2,1)}, u32[]{:S(2)}) copy-start(bf16[1,128,4096]{2,1,0:T(8,128)(2,1)} %x_ref.1) | copy-start | bytes 3145732
  2.0 16.3 %collective-permute-start.7 = (bf16[2,128,512]{2,1,0:T(8,128)(2,1)S(1)}, bf16[2,128,512]{2,1,0:T(8,128)(2,1)S(1)}, u32[]{:S(2)}, u32[]{:S(2)}) collective-permute-start(bf16[2,128,512]{2,1,0:T(8,128)(2,1)S(1)} %get-tuple-element.91), channel_id=1, source_target_pairs={{0,3},{1,2},{2,1},{3,0},{4,7},{5,6},{6,5},{7,4},{8,11},{9,10},{10,... | collective-permute-start | bytes 786440 | tf_op jit(solution)/shard_map/ppermute | solution.py:842
  4.4 13.9 %collective-permute-start.6 = (bf16[2,128,512]{2,1,0:T(8,128)(2,1)S(1)}, bf16[2,128,512]{2,1,0:T(8,128)(2,1)S(1)}, u32[]{:S(2)}, u32[]{:S(2)}) collective-permute-start(bf16[2,128,512]{2,1,0:T(8,128)(2,1)S(1)} %get-tuple-element.83), channel_id=1, source_target_pairs={{0,2},{1,3},{2,0},{3,1},{4,6},{5,7},{6,4},{7,5},{8,10},{9,11},{10,... | collective-permute-start | bytes 786440 | tf_op jit(solution)/shard_map/ppermute | solution.py:842
  5.0 3.6 %collective-permute-start.5 = (f32[1,512]{1,0:T(1,128)S(1)}, f32[1,512]{1,0:T(1,128)S(1)}, u32[]{:S(2)}, u32[]{:S(2)}) collective-permute-start(f32[1,512]{1,0:T(1,128)S(1)} %get-tuple-element.85), channel_id=1, source_target_pairs={{0,4},{4,0},{8,12},{12,8},{16,20},{20,16},{24,28},{28,24},{1,5},{5... | collective-permute-start | bytes 6152 | tf_op jit(solution)/shard_map/ppermute | solution.py:854
  8.7 4.2 %collective-permute-start.2 = (bf16[4,128,1024]{2,1,0:T(8,128)(2,1)S(1)}, bf16[4,128,1024]{2,1,0:T(8,128)(2,1)}, u32[]{:S(2)}, u32[]{:S(2)}) collective-permute-start(bf16[4,128,1024]{2,1,0:T(8,128)(2,1)S(1)} %get-tuple-element.20), channel_id=1, source_target_pairs={{0,1},{1,0},{2,3},{3,2},{4,5},{5,4},{6,7},{7,6},{8,9},{9,8},{10,11... | collective-permute-start | bytes 3145736 | tf_op jit(solution)/shard_map/cond/branch_1_fun/ppermute | solution.py:842
  8.7 4.3 %collective-permute-start.3 = (bf16[1,128,4096]{2,1,0:T(8,128)(2,1)S(1)}, bf16[1,128,4096]{2,1,0:T(8,128)(2,1)}, u32[]{:S(2)}, u32[]{:S(2)}) collective-permute-start(bf16[1,128,4096]{2,1,0:T(8,128)(2,1)S(1)} %get-tuple-element.21), channel_id=1, source_target_pairs={{0,1},{1,0},{2,3},{3,2},{4,5},{5,4},{6,7},{7,6},{8,9},{9,8},{10,11... | collective-permute-start | bytes 3145736 | tf_op jit(solution)/shard_map/cond/branch_1_fun/ppermute | solution.py:842
  9.2 3.6 %collective-permute-start.4 = (f32[1,1024]{1,0:T(1,128)S(1)}, f32[1,1024]{1,0:T(1,128)S(1)}, u32[]{:S(2)}, u32[]{:S(2)}) collective-permute-start(f32[1,1024]{1,0:T(1,128)S(1)} %get-tuple-element.22), channel_id=1, source_target_pairs={{0,8},{4,12},{8,0},{12,4},{16,24},{20,28},{24,16},{28,20},{1,9},{5... | collective-permute-start | bytes 12296 | tf_op jit(solution)/shard_map/cond/branch_1_fun/ppermute | solution.py:854
  13.0 6.1 %collective-permute-start.8 = (f32[1,2048]{1,0:T(1,128)S(1)}, f32[1,2048]{1,0:T(1,128)S(1)}, u32[]{:S(2)}, u32[]{:S(2)}) collective-permute-start(f32[1,2048]{1,0:T(1,128)S(1)} %get-tuple-element.98), channel_id=1, source_target_pairs={{0,16},{4,20},{8,24},{12,28},{16,0},{20,4},{24,8},{28,12},{1,17},{... | collective-permute-start | bytes 24584 | tf_op jit(solution)/shard_map/ppermute | solution.py:854
  19.8 3.8 %collective-permute-start.9 = (f32[4,4,256]{2,1,0:T(4,128)S(1)}, f32[4,4,256]{2,1,0:T(4,128)S(1)}, u32[]{:S(2)}, u32[]{:S(2)}) collective-permute-start(f32[4,4,256]{2,1,0:T(4,128)S(1)} %get-tuple-element.100), channel_id=1, source_target_pairs={{0,2},{1,3},{2,0},{3,1},{4,6},{5,7},{6,4},{7,5},{8,10},{9,11},{10,... | collective-permute-start | bytes 49160 | tf_op jit(solution)/shard_map/ppermute | solution.py:842
  25.5 13.0 %collective-permute-start.10 = (bf16[2,128,512]{2,1,0:T(8,128)(2,1)}, bf16[2,128,512]{2,1,0:T(8,128)(2,1)S(1)}, u32[]{:S(2)}, u32[]{:S(2)}) collective-permute-start(bf16[2,128,512]{2,1,0:T(8,128)(2,1)} %get-tuple-element.112), channel_id=1, source_target_pairs={{0,2},{1,3},{2,0},{3,1},{4,6},{5,7},{6,4},{7,5},{8,10},{9,11},{10,... | collective-permute-start | bytes 786440 | tf_op jit(solution)/shard_map/ppermute | solution.py:842
  27.0 11.6 %collective-permute-start.11 = (bf16[2,128,512]{2,1,0:T(8,128)(2,1)S(1)}, bf16[2,128,512]{2,1,0:T(8,128)(2,1)S(1)}, u32[]{:S(2)}, u32[]{:S(2)}) collective-permute-start(bf16[2,128,512]{2,1,0:T(8,128)(2,1)S(1)} %get-tuple-element.113), channel_id=1, source_target_pairs={{0,3},{1,2},{2,1},{3,0},{4,7},{5,6},{6,5},{7,4},{8,11},{9,10},{10,... | collective-permute-start | bytes 786440 | tf_op jit(solution)/shard_map/ppermute | solution.py:842
  27.0 13.2 %all-to-all-start = ((f32[32,1,512]{2,1,0:T(1,128)}), f32[32,1,512]{2,1,0:T(1,128)S(1)}, u32[]{:S(2)}, u32[]{:S(2)}) async-start(f32[32,1,512]{2,1,0:T(1,128)} %bitcast.4), calls=%async_computation | async-start | bytes 131072 | tf_op jit(solution)/shard_map/all_to_all | solution.py:894
  32.5 3.5 %collective-permute-start = (bf16[3,128,512]{2,1,0:T(8,128)(2,1)S(1)}, bf16[3,128,512]{2,1,0:T(8,128)(2,1)S(1)}, u32[]{:S(2)}, u32[]{:S(2)}) collective-permute-start(bf16[3,128,512]{2,1,0:T(8,128)(2,1)S(1)} %get-tuple-element.23), channel_id=1, source_target_pairs={{0,1},{1,0},{2,3},{3,2},{4,5},{5,4},{6,7},{7,6},{8,9},{9,8},{10,11... | collective-permute-start | bytes 1179656 | tf_op jit(solution)/shard_map/cond/branch_1_fun/ppermute | solution.py:842
  34.5 1.8 %collective-permute-start.1 = (bf16[3,128,512]{2,1,0:T(8,128)(2,1)S(1)}, bf16[3,128,512]{2,1,0:T(8,128)(2,1)S(1)}, u32[]{:S(2)}, u32[]{:S(2)}) collective-permute-start(bf16[3,128,512]{2,1,0:T(8,128)(2,1)S(1)} %get-tuple-element.29), channel_id=1, source_target_pairs={{0,1},{1,0},{2,3},{3,2},{4,5},{5,4},{6,7},{7,6},{8,9},{9,8},{10,11... | collective-permute-start | bytes 1179656 | tf_op jit(solution)/shard_map/cond/branch_1_fun/ppermute | solution.py:842

commit v21 on v20

--- a/solution.py
+++ b/solution.py
@@ -867,8 +867,7 @@
         own_high, sib_high = far_grad(*operands)
         sib_in.append(send(sib_high, 1))
         *outs, waiting = own_join(own_low, own_high, queries.shape)
-        *outs, waiting_sib = sib_join(*sib_in, outs)
-        return outs, waiting, waiting_sib
+        return outs, waiting, sib_in
 
     out_s, out_d, w_part = cross_pack(route_pos, w_router, keys, values, queries, d_gated)
     in_s, in_d = send(out_s, 2), send(out_d, 3)
@@ -892,7 +891,8 @@
 
     ret_s, ret_d = send(back_s, 2), send(back_d, 3)
     shared = lax.all_to_all(terms.reshape(ndp * n, 1, -1), ("dp", "ctx"), 0, 0, tiled=True)
-    outs, waiting, waiting_sib = beside(far_phase, own_low, sib_low, far, local, final, gates, keep)
+    outs, waiting, sib_in = beside(far_phase, own_low, sib_low, far, local, final, gates, keep)
+    *outs, waiting_sib = sib_join(*sib_in, outs)
     dq, dk, dv = add_back(waiting, waiting_sib, ret_s, ret_d, outs)
     router_grad = jnp.sum(after(shared, dq), axis=(0, 1))
     return dq, dk, dv, router_grad

time: 41 us -> 40.5 us (0.988)
  no operation moved by 1% of the time
where the time goes in v21:
time: 40.5 us; the launch traced here: 40.2 us
  starting transfers between devices  18.4 us (45%)
  Pallas kernels  16 us (40%)
  waiting for transfers between devices  4.23 us (10%)
  between operations  0.81 us (2%)
  other arithmetic  0.68 us (2%)
    ppermute x9, starting transfers between devices, send(): return lax.ppermute(a, 'ctx', [(i, i ^ flip) for i in range(n)])  7.16 us
    ppermute x3, starting transfers between devices, widen(): other = lax.ppermute(part, 'dp', [(i, i ^ step) for i in range(ndp)])  5.68 us
    all_to_all x1, starting transfers between devices, swap_body(): lax.all_to_all(terms.reshape(ndp * n, 1, -1), ('dp', 'ctx'), 0, 0, tiled=...  5.54 us
    ppermute x3, waiting for transfers between devices, widen(): other = lax.ppermute(part, 'dp', [(i, i ^ step) for i in range(ndp)])  2.74 us
    pallas_call x1, Pallas kernels, local_stats(): pl.pallas_call(functools.partial(local_stats_kernel, HEAD ** (-0.5)), out...  2.71 us
    pallas_call x1, Pallas kernels, sib_join(): pl.pallas_call(sib_join_kernel, out_shape=[pltpu.HBM(o.shape, F32) for o...  2.2 us
    pallas_call x1, Pallas kernels, near_grad(): pl.pallas_call(functools.partial(near_grad_kernel, HEAD ** (-0.5)), out_s...  1.65 us
    pallas_call x1, Pallas kernels, far_grad(): pl.pallas_call(functools.partial(far_grad_kernel, HEAD ** (-0.5)), out_sh...  1.64 us
  transfers between devices with their start and end apart: 13, of which 6 were waited for; matrix products, arithmetic and copies ran while one was open for 0% of the time, Pallas kernels for 31%

profile of v21, /device:TPU:0, one launch (start us, length us, event | category | flops | bytes accessed | tf_op | source)
XLA Modules:
  0.0 40.2 jit_solution(10424221538230716387)
XLA Ops:
  0.6 1.3 %cross_pack.1 = (bf16[2,128,512]{2,1,0:T(8,128)(2,1)S(1)}, bf16[2,128,512]{2,1,0:T(8,128)(2,1)S(1)}, f32[1,512]{1,0:T(1,128)S(1)}) custom-call(s32[1,128]{1,0:T(1,128)} %pos_ref.2, bf16[512]{0:T(512)(128)(2,1)} %w_any.1, bf16[1,128,2048]{2,1,0:T(8,128)(2,1)} %k_ref.5, bf16[1,128,2048]{2,1,0:T(8,128)(2,1)} %v_ref.5, bf16[1,128,2048]{2,1,0:T(8,128)(2,1)} %q_ref.5, ...), custom_call_target="tpu_custom_call" | custom-call | flops 1 | bytes 1 | tf_op jit(solution)/shard_map/cross_pack/pallas_call | solution.py:314
  2.0 2.4 %collective-permute-start.7 = (bf16[2,128,512]{2,1,0:T(8,128)(2,1)S(1)}, bf16[2,128,512]{2,1,0:T(8,128)(2,1)S(1)}, u32[]{:S(2)}, u32[]{:S(2)}) collective-permute-start(bf16[2,128,512]{2,1,0:T(8,128)(2,1)S(1)} %get-tuple-element.93), channel_id=1, source_target_pairs={{0,3},{1,2},{2,1},{3,0},{4,7},{5,6},{6,5},{7,4},{8,11},{9,10},{10,... | collective-permute-start | bytes 786440 | tf_op jit(solution)/shard_map/ppermute | solution.py:842
  5.0 1.5 %collective-permute-start.5 = (f32[1,512]{1,0:T(1,128)S(1)}, f32[1,512]{1,0:T(1,128)S(1)}, u32[]{:S(2)}, u32[]{:S(2)}) collective-permute-start(f32[1,512]{1,0:T(1,128)S(1)} %get-tuple-element.86), channel_id=1, source_target_pairs={{0,4},{4,0},{8,12},{12,8},{16,20},{20,16},{24,28},{28,24},{1,5},{5... | collective-permute-start | bytes 6152 | tf_op jit(solution)/shard_map/ppermute | solution.py:854
  6.6 1.3 %sib_pack.1 = bf16[4,128,1024]{2,1,0:T(8,128)(2,1)S(1)} custom-call(s32[1,128]{1,0:T(1,128)S(1)} %copy-done, bf16[1,128,2048]{2,1,0:T(8,128)(2,1)} %k_ref.5, bf16[1,128,2048]{2,1,0:T(8,128)(2,1)} %v_ref.5, bf16[1,128,2048]{2,1,0:T(8,128)(2,1)} %q_ref.5, f32[1,128,2048]{2,1,0:T(8,128)} %dg_ref.5), custom_call_target="tpu_custom_call" | custom-call | flops 1 | bytes 1 | tf_op jit(solution)/shard_map/sib_pack/pallas_call | solution.py:350
  7.9 0.7 %collective-permute-done.5 = f32[1,512]{1,0:T(1,128)S(1)} collective-permute-done((f32[1,512]{1,0:T(1,128)S(1)}, f32[1,512]{1,0:T(1,128)S(1)}, u32[]{:S(2)}, u32[]{:S(2)}) %collective-permute-start.5) | collective-permute-done | bytes 2080 | tf_op jit(solution)/shard_map/ppermute | solution.py:854
  8.6 4.4 %conditional.2 = (bf16[4,128,1024]{2,1,0:T(8,128)(2,1)}, bf16[1,128,4096]{2,1,0:T(8,128)(2,1)}, f32[1,2048]{1,0:T(1,128)S(1)}) conditional(s32[]{:T(128)} %bitcast, () %tuple.29, (bf16[4,128,1024]{2,1,0:T(8,128)(2,1)S(1)}, bf16[1,128,4096]{2,1,0:T(8,128)(2,1)S(1)}, f32[1,1024]{1,0:T(1,128)S(1)}) %tuple.41), branch_computations={%region_0.0_spmd, %region_1.0_spmd} | conditional | flops 2048 | bytes 8421520 | solution.py:848
  9.2 1.6 %collective-permute-start.4 = (f32[1,1024]{1,0:T(1,128)S(1)}, f32[1,1024]{1,0:T(1,128)S(1)}, u32[]{:S(2)}, u32[]{:S(2)}) collective-permute-start(f32[1,1024]{1,0:T(1,128)S(1)} %get-tuple-element.22), channel_id=1, source_target_pairs={{0,8},{4,12},{8,0},{12,4},{16,24},{20,28},{24,16},{28,20},{1,9},{5... | collective-permute-start | bytes 12296 | tf_op jit(solution)/shard_map/cond/branch_1_fun/ppermute | solution.py:854
  10.8 2.0 %collective-permute-done.4 = f32[1,1024]{1,0:T(1,128)S(1)} collective-permute-done((f32[1,1024]{1,0:T(1,128)S(1)}, f32[1,1024]{1,0:T(1,128)S(1)}, u32[]{:S(2)}, u32[]{:S(2)}) %collective-permute-start.4) | collective-permute-done | bytes 4128 | tf_op jit(solution)/shard_map/cond/branch_1_fun/ppermute | solution.py:854
  13.0 2.6 %collective-permute-start.8 = (f32[1,2048]{1,0:T(1,128)S(1)}, f32[1,2048]{1,0:T(1,128)S(1)}, u32[]{:S(2)}, u32[]{:S(2)}) collective-permute-start(f32[1,2048]{1,0:T(1,128)S(1)} %get-tuple-element.99), channel_id=1, source_target_pairs={{0,16},{4,20},{8,24},{12,28},{16,0},{20,4},{24,8},{28,12},{1,17},{... | collective-permute-start | bytes 24584 | tf_op jit(solution)/shard_map/ppermute | solution.py:854
  15.6 2.7 %local_stats.1 = (f32[3,8,256]{2,1,0:T(8,128)S(1)}, f32[1,256]{1,0:T(1,128)S(1)}, bf16[4,256,512]{2,1,0:T(8,128)(2,1)S(1)}, bf16[4,256,512]{2,1,0:T(8,128)(2,1)S(1)}, bf16[2,128,4096]{2,1,0:T(8,128)(2,1)S(1)}) custom-call(s32[1,128]{1,0:T(1,128)S(1)} %copy-done, bf16[1,128,2048]{2,1,0:T(8,128)(2,1)} %k_ref.5, bf16[1,128,2048]{2,1,0:T(8,128)(2,1)} %v_ref.5, ...), custom_call_target="tpu_custom_call" | custom-call | flops 1 | bytes 1 | tf_op jit(solution)/shard_map/local_stats/pallas_call | solution.py:476
  18.3 0.8 %cross_stats.1 = (bf16[4,256,512]{2,1,0:T(8,128)(2,1)S(1)}, f32[3,4,256]{2,1,0:T(4,128)S(1)}, bf16[2,4,256,256]{3,2,1,0:T(8,128)(2,1)S(1)}) custom-call(bf16[4,256,512]{2,1,0:T(8,128)(2,1)S(1)} %get-tuple-element.92.near.pair, bf16[4,256,512]{2,1,0:T(8,128)(2,1)S(1)} %get-tuple-element.90.far, bf16[2,128,512]{2,1,0:T(8,128)(2,1)S(1)} %collective-permute-done.6.straight, ...), custom_call_target="tpu_custom_call" | custom-call | flops 1 | bytes 1 | tf_op jit(solution)/shard_map/cross_stats/pallas_call | solution.py:525
  19.2 0.7 %router_gate.1 = (f32[1,256]{1,0:T(1,128)S(1)}, f32[4,4,256]{2,1,0:T(4,128)S(1)}) custom-call(f32[1,256]{1,0:T(1,128)S(1)} %get-tuple-element.97.live_ref, bf16[2,128,4096]{2,1,0:T(8,128)(2,1)S(1)} %get-tuple-element.98.rows_x, f32[1,4096]{1,0:T(1,128)S(1)} %pad_maximum_fusion.1.w_ref, f32[3,8,256]{2,1,0:T(8,128)S(1)} %get-tuple-element.91.local, ...), custom_call_target="tpu_custom_call" | custom-call | flops 1 | bytes 1 | tf_op jit(solution)/shard_map/router_gate/pallas_call | solution.py:382
  19.9 1.5 %collective-permute-start.9 = (f32[4,4,256]{2,1,0:T(4,128)S(1)}, f32[4,4,256]{2,1,0:T(4,128)S(1)}, u32[]{:S(2)}, u32[]{:S(2)}) collective-permute-start(f32[4,4,256]{2,1,0:T(4,128)S(1)} %get-tuple-element.101), channel_id=1, source_target_pairs={{0,2},{1,3},{2,0},{3,1},{4,6},{5,7},{6,4},{7,5},{8,10},{9,11},{10,... | collective-permute-start | bytes 49160 | tf_op jit(solution)/shard_map/ppermute | solution.py:842
  21.3 1.6 %near_grad.1 = (f32[256,512]{1,0:T(8,128)S(1)}, bf16[2,128,512]{2,1,0:T(8,128)(2,1)S(1)}, bf16[2,128,512]{2,1,0:T(8,128)(2,1)S(1)}, f32[1,256]{1,0:T(1,128)S(1)}) custom-call(bf16[4,256,512]{2,1,0:T(8,128)(2,1)S(1)} %get-tuple-element.92.near.pair, f32[3,8,256]{2,1,0:T(8,128)S(1)} %get-tuple-element.91.local, f32[3,4,256]{2,1,0:T(4,128)S(1)} %get-tuple-element.96.stats, ...), custom_call_target="tpu_custom_call" | custom-call | flops 1 | bytes 1 | tf_op jit(solution)/shard_map/near_grad/pallas_call | solution.py:590
  23.0 0.7 %collective-permute-done.9.heard = f32[4,4,256]{2,1,0:T(4,128)S(1)} collective-permute-done((f32[4,4,256]{2,1,0:T(4,128)S(1)}, f32[4,4,256]{2,1,0:T(4,128)S(1)}, u32[]{:S(2)}, u32[]{:S(2)}) %collective-permute-start.9) | collective-permute-done | bytes 16416 | tf_op jit(solution)/shard_map/ppermute | solution.py:842
  23.7 1.5 %cross_grad.1 = (bf16[2,128,512]{2,1,0:T(8,128)(2,1)S(1)}, bf16[2,128,512]{2,1,0:T(8,128)(2,1)S(1)}, bf16[3,128,512]{2,1,0:T(8,128)(2,1)S(1)}, bf16[3,128,512]{2...) custom-call(bf16[4,256,512]{2,1,0:T(8,128)(2,1)S(1)} %get-tuple-element, ...), custom_call_target="tpu_custom_call" | custom-call | flops 1 | bytes 1 | tf_op jit(solution)/shard_map/cross_grad/pallas_call | solution.py:661
  25.2 1.5 %collective-permute-start.10 = (bf16[2,128,512]{2,1,0:T(8,128)(2,1)S(1)}, bf16[2,128,512]{2,1,0:T(8,128)(2,1)S(1)}, u32[]{:S(2)}, u32[]{:S(2)}) collective-permute-start(bf16[2,128,512]{2,1,0:T(8,128)(2,1)S(1)} %get-tuple-element.118), channel_id=1, source_target_pairs={{0,2},{1,3},{2,0},{3,1},{4,6},{5,7},{6,4},{7,5},{8,10},{9,11},{10,... | collective-permute-start | bytes 786440 | tf_op jit(solution)/shard_map/ppermute | solution.py:842
  26.6 5.5 %all-to-all-start = ((f32[32,1,512]{2,1,0:T(1,128)}), f32[32,1,512]{2,1,0:T(1,128)S(1)}, u32[]{:S(2)}, u32[]{:S(2)}) async-start(f32[32,1,512]{2,1,0:T(1,128)} %bitcast.4), calls=%async_computation | async-start | bytes 131072 | tf_op jit(solution)/shard_map/all_to_all | solution.py:893
  32.2 3.9 %conditional.3 = (f32[1,128,2048]{2,1,0:T(8,128)}, f32[1,128,2048]{2,1,0:T(8,128)}, f32[1,128,2048]{2,1,0:T(8,128)}, bf16[2,128,512]{2,1,0:T(8,128)(2,1)S(1)}, b...) conditional(s32[]{:T(128)} %bitcast, () %tuple.28, (bf16[4,256,512]{2,1,0:T(8,128)(2,1)S(1)}, ...), branch_computations={%region_2.0_spmd, %region_3.0_spmd} | conditional | flops 2 | bytes 4194370 | solution.py:848
  32.5 1.6 %far_grad.1 = (bf16[3,128,512]{2,1,0:T(8,128)(2,1)S(1)}, bf16[3,128,512]{2,1,0:T(8,128)(2,1)S(1)}) custom-call(bf16[4,256,512]{2,1,0:T(8,128)(2,1)S(1)} %get-tuple-element.24.pair, f32[3,8,256]{2,1,0:T(8,128)S(1)} %get-tuple-element.25.local, f32[2,4,256]{2,1,0:T(4,128)S(1)} %get-tuple-element.26.final, f32[1,256]{1,0:T(1,128)S(1)} %get-tuple-element.27.gates, ...), custom_call_target="tpu_custom_call" | custom-call | flops 1 | bytes 1 | tf_op jit(solution)/shard_map/cond/branch_1_fun/far_grad/pallas_call | solution.py:703
  34.5 1.2 %own_join.1 = (f32[1,128,2048]{2,1,0:T(8,128)}, f32[1,128,2048]{2,1,0:T(8,128)}, f32[1,128,2048]{2,1,0:T(8,128)}, bf16[2,128,512]{2,1,0:T(8,128)(2,1)S(1)}) custom-call(bf16[3,128,512]{2,1,0:T(8,128)(2,1)S(1)} %get-tuple-element.23.low, bf16[3,128,512]{2,1,0:T(8,128)(2,1)S(1)} %get-tuple-element.29.high), custom_call_target="tpu_custom_call" | custom-call | flops 1 | bytes 1 | tf_op jit(solution)/shard_map/cond/branch_1_fun/own_join/pallas_call | solution.py:734
  36.1 2.2 %sib_join.1 = (f32[1,128,2048]{2,1,0:T(8,128)}, f32[1,128,2048]{2,1,0:T(8,128)}, f32[1,128,2048]{2,1,0:T(8,128)}, bf16[2,128,512]{2,1,0:T(8,128)(2,1)S(1)}) custom-call(bf16[3,128,512]{2,1,0:T(8,128)(2,1)} %get-tuple-element.112.low, bf16[3,128,512]{2,1,0:T(8,128)(2,1)} %get-tuple-element.113.high, ...), custom_call_target="tpu_custom_call", output_to_operand_aliasing={{0}: (2, {}), {1}: (3, {}), {2}: (4, {})} | custom-call | flops 1 | bytes 1 | tf_op jit(solution)/shard_map/sib_join/pallas_call | solution.py:773
  38.3 1.0 %add_back.1 = (f32[1,128,2048]{2,1,0:T(8,128)}, f32[1,128,2048]{2,1,0:T(8,128)}, f32[1,128,2048]{2,1,0:T(8,128)}) custom-call(bf16[2,128,512]{2,1,0:T(8,128)(2,1)S(1)} %get-tuple-element.111.own, bf16[2,128,512]{2,1,0:T(8,128)(2,1)S(1)} %get-tuple-element.117.sib, ...), custom_call_target="tpu_custom_call", output_to_operand_aliasing={{0}: (4, {}), {1}: (5, {}), {2}: (6, {})} | custom-call | flops 1 | bytes 1 | tf_op jit(solution)/shard_map/add_back/pallas_call | solution.py:824
  39.6 0.6 %reduce_sum.9 = f32[512]{0:T(512)} reduce(f32[32,1,512]{2,1,0:T(1,128)S(1)} %all-to-all-done, f32[]{:T(128)} %constant.2.clone.1), dimensions={0,1}, to_apply=%region_4.0 | reduce | flops 15872 | bytes 67588 | tf_op jit(solution)/shard_map/reduce_sum | solution.py:897
  (23 shorter events, 2.7 us)
Async XLA Ops:
  0.6 5.9 %copy-start = (s32[1,128]{1,0:T(1,128)S(1)}, s32[1,128]{1,0:T(1,128)}, u32[]{:S(2)}) copy-start(s32[1,128]{1,0:T(1,128)} %pos_ref.2) | copy-start | bytes 1540
  2.0 6.6 %copy-start.1 = (bf16[1,128,4096]{2,1,0:T(8,128)(2,1)S(1)}, bf16[1,128,4096]{2,1,0:T(8,128)(2,1)}, u32[]{:S(2)}) copy-start(bf16[1,128,4096]{2,1,0:T(8,128)(2,1)} %x_ref.1) | copy-start | bytes 3145732
  2.0 16.3 %collective-permute-start.7 = (bf16[2,128,512]{2,1,0:T(8,128)(2,1)S(1)}, bf16[2,128,512]{2,1,0:T(8,128)(2,1)S(1)}, u32[]{:S(2)}, u32[]{:S(2)}) collective-permute-start(bf16[2,128,512]{2,1,0:T(8,128)(2,1)S(1)} %get-tuple-element.93), channel_id=1, source_target_pairs={{0,3},{1,2},{2,1},{3,0},{4,7},{5,6},{6,5},{7,4},{8,11},{9,10},{10,... | collective-permute-start | bytes 786440 | tf_op jit(solution)/shard_map/ppermute | solution.py:842
  4.4 13.9 %collective-permute-start.6 = (bf16[2,128,512]{2,1,0:T(8,128)(2,1)S(1)}, bf16[2,128,512]{2,1,0:T(8,128)(2,1)S(1)}, u32[]{:S(2)}, u32[]{:S(2)}) collective-permute-start(bf16[2,128,512]{2,1,0:T(8,128)(2,1)S(1)} %get-tuple-element.84), channel_id=1, source_target_pairs={{0,2},{1,3},{2,0},{3,1},{4,6},{5,7},{6,4},{7,5},{8,10},{9,11},{10,... | collective-permute-start | bytes 786440 | tf_op jit(solution)/shard_map/ppermute | solution.py:842
  5.0 3.6 %collective-permute-start.5 = (f32[1,512]{1,0:T(1,128)S(1)}, f32[1,512]{1,0:T(1,128)S(1)}, u32[]{:S(2)}, u32[]{:S(2)}) collective-permute-start(f32[1,512]{1,0:T(1,128)S(1)} %get-tuple-element.86), channel_id=1, source_target_pairs={{0,4},{4,0},{8,12},{12,8},{16,20},{20,16},{24,28},{28,24},{1,5},{5... | collective-permute-start | bytes 6152 | tf_op jit(solution)/shard_map/ppermute | solution.py:854
  8.7 4.2 %collective-permute-start.2 = (bf16[4,128,1024]{2,1,0:T(8,128)(2,1)S(1)}, bf16[4,128,1024]{2,1,0:T(8,128)(2,1)}, u32[]{:S(2)}, u32[]{:S(2)}) collective-permute-start(bf16[4,128,1024]{2,1,0:T(8,128)(2,1)S(1)} %get-tuple-element.20), channel_id=1, source_target_pairs={{0,1},{1,0},{2,3},{3,2},{4,5},{5,4},{6,7},{7,6},{8,9},{9,8},{10,11... | collective-permute-start | bytes 3145736 | tf_op jit(solution)/shard_map/cond/branch_1_fun/ppermute | solution.py:842
  8.7 4.3 %collective-permute-start.3 = (bf16[1,128,4096]{2,1,0:T(8,128)(2,1)S(1)}, bf16[1,128,4096]{2,1,0:T(8,128)(2,1)}, u32[]{:S(2)}, u32[]{:S(2)}) collective-permute-start(bf16[1,128,4096]{2,1,0:T(8,128)(2,1)S(1)} %get-tuple-element.21), channel_id=1, source_target_pairs={{0,1},{1,0},{2,3},{3,2},{4,5},{5,4},{6,7},{7,6},{8,9},{9,8},{10,11... | collective-permute-start | bytes 3145736 | tf_op jit(solution)/shard_map/cond/branch_1_fun/ppermute | solution.py:842
  9.2 3.6 %collective-permute-start.4 = (f32[1,1024]{1,0:T(1,128)S(1)}, f32[1,1024]{1,0:T(1,128)S(1)}, u32[]{:S(2)}, u32[]{:S(2)}) collective-permute-start(f32[1,1024]{1,0:T(1,128)S(1)} %get-tuple-element.22), channel_id=1, source_target_pairs={{0,8},{4,12},{8,0},{12,4},{16,24},{20,28},{24,16},{28,20},{1,9},{5... | collective-permute-start | bytes 12296 | tf_op jit(solution)/shard_map/cond/branch_1_fun/ppermute | solution.py:854
  13.0 6.1 %collective-permute-start.8 = (f32[1,2048]{1,0:T(1,128)S(1)}, f32[1,2048]{1,0:T(1,128)S(1)}, u32[]{:S(2)}, u32[]{:S(2)}) collective-permute-start(f32[1,2048]{1,0:T(1,128)S(1)} %get-tuple-element.99), channel_id=1, source_target_pairs={{0,16},{4,20},{8,24},{12,28},{16,0},{20,4},{24,8},{28,12},{1,17},{... | collective-permute-start | bytes 24584 | tf_op jit(solution)/shard_map/ppermute | solution.py:854
  19.9 3.8 %collective-permute-start.9 = (f32[4,4,256]{2,1,0:T(4,128)S(1)}, f32[4,4,256]{2,1,0:T(4,128)S(1)}, u32[]{:S(2)}, u32[]{:S(2)}) collective-permute-start(f32[4,4,256]{2,1,0:T(4,128)S(1)} %get-tuple-element.101), channel_id=1, source_target_pairs={{0,2},{1,3},{2,0},{3,1},{4,6},{5,7},{6,4},{7,5},{8,10},{9,11},{10,... | collective-permute-start | bytes 49160 | tf_op jit(solution)/shard_map/ppermute | solution.py:842
  25.2 13.1 %collective-permute-start.10 = (bf16[2,128,512]{2,1,0:T(8,128)(2,1)S(1)}, bf16[2,128,512]{2,1,0:T(8,128)(2,1)S(1)}, u32[]{:S(2)}, u32[]{:S(2)}) collective-permute-start(bf16[2,128,512]{2,1,0:T(8,128)(2,1)S(1)} %get-tuple-element.118), channel_id=1, source_target_pairs={{0,2},{1,3},{2,0},{3,1},{4,6},{5,7},{6,4},{7,5},{8,10},{9,11},{10,... | collective-permute-start | bytes 786440 | tf_op jit(solution)/shard_map/ppermute | solution.py:842
  26.6 11.7 %collective-permute-start.11 = (bf16[2,128,512]{2,1,0:T(8,128)(2,1)S(1)}, bf16[2,128,512]{2,1,0:T(8,128)(2,1)S(1)}, u32[]{:S(2)}, u32[]{:S(2)}) collective-permute-start(bf16[2,128,512]{2,1,0:T(8,128)(2,1)S(1)} %get-tuple-element.119), channel_id=1, source_target_pairs={{0,3},{1,2},{2,1},{3,0},{4,7},{5,6},{6,5},{7,4},{8,11},{9,10},{10,... | collective-permute-start | bytes 786440 | tf_op jit(solution)/shard_map/ppermute | solution.py:842
  26.6 13.0 %all-to-all-start = ((f32[32,1,512]{2,1,0:T(1,128)}), f32[32,1,512]{2,1,0:T(1,128)S(1)}, u32[]{:S(2)}, u32[]{:S(2)}) async-start(f32[32,1,512]{2,1,0:T(1,128)} %bitcast.4), calls=%async_computation | async-start | bytes 131072 | tf_op jit(solution)/shard_map/all_to_all | solution.py:893
  32.2 3.5 %collective-permute-start = (bf16[3,128,512]{2,1,0:T(8,128)(2,1)S(1)}, bf16[3,128,512]{2,1,0:T(8,128)(2,1)}, u32[]{:S(2)}, u32[]{:S(2)}) collective-permute-start(bf16[3,128,512]{2,1,0:T(8,128)(2,1)S(1)} %get-tuple-element.34), channel_id=1, source_target_pairs={{0,1},{1,0},{2,3},{3,2},{4,5},{5,4},{6,7},{7,6},{8,9},{9,8},{10,11... | collective-permute-start | bytes 1179656 | tf_op jit(solution)/shard_map/cond/branch_1_fun/ppermute | solution.py:842
  34.2 1.9 %collective-permute-start.1 = (bf16[3,128,512]{2,1,0:T(8,128)(2,1)S(1)}, bf16[3,128,512]{2,1,0:T(8,128)(2,1)}, u32[]{:S(2)}, u32[]{:S(2)}) collective-permute-start(bf16[3,128,512]{2,1,0:T(8,128)(2,1)S(1)} %get-tuple-element.35), channel_id=1, source_target_pairs={{0,1},{1,0},{2,3},{3,2},{4,5},{5,4},{6,7},{7,6},{8,9},{9,8},{10,11... | collective-permute-start | bytes 1179656 | tf_op jit(solution)/shard_map/cond/branch_1_fun/ppermute | solution.py:842

commit v22 on v21

--- a/solution.py
+++ b/solution.py
@@ -579,14 +579,14 @@
         dq, dk, dv = local_gradients(pair, h, mask, scale, near[0][row], factor[row], delta[row])
         dq_out[:, cols] = dq
         for i, part in enumerate((dk, dv)):
-            own_out[i, :, cols] = part[:slots].astype(BF16)
-            sib_out[i, :, cols] = part[slots:].astype(BF16)
+            own_out[1 + i, :, cols] = part[:slots].astype(BF16)
+            sib_out[1 + i, :, cols] = part[slots:].astype(BF16)
 
 
 def near_grad(pair, local, stats, gates):
     _, rows, width = pair.shape
     slots = rows // 2
-    out = pltpu.VMEM((2, slots, width), BF16)
+    out = pltpu.VMEM((3, slots, width), BF16)
     return pl.pallas_call(
         functools.partial(near_grad_kernel, HEAD**-0.5),
         out_shape=[pltpu.VMEM((2 * slots, width), F32), out, out, jax.ShapeDtypeStruct(gates.shape, F32)],
@@ -630,9 +630,6 @@
     put_terms(sums * gates[...] * (1.0 - gates[...]) * (1.0 / total), rows_x, held)
     leaving = pltpu.make_async_copy(held, terms, sem)
     leaving.start()
-    for i in range(2):
-        own_low[1 + i] = near_own[i]
-        sib_low[1 + i] = near_sib[i]
     for h in range(heads):
         cols = slice(h * HEAD, (h + 1) * HEAD)
         row = slice(h, h + 1)
@@ -672,6 +669,7 @@
         in_specs=[VMEM] * 11,
         out_specs=[VMEM] * 6 + [pl.BlockSpec(memory_space=pltpu.HBM)],
         scratch_shapes=[pltpu.VMEM(spread, F32), pltpu.SemaphoreType.DMA],
+        input_output_aliases={9: 2, 10: 3},
         compiler_params=params(),
         cost_estimate=cost(24 * slots * slots * width, 64 * slots * width),
         name="cross_grad",

time: 40.5 us -> 40.4 us (level)
  no operation moved by 1% of the time
where the time goes in v22:
time: 40.4 us; the launch traced here: 40.2 us
  starting transfers between devices  18.4 us (46%)
  Pallas kernels  16 us (40%)
  waiting for transfers between devices  4.23 us (10%)
  between operations  0.81 us (2%)
  other arithmetic  0.68 us (2%)
    ppermute x9, starting transfers between devices, send(): return lax.ppermute(a, 'ctx', [(i, i ^ flip) for i in range(n)])  7.15 us
    ppermute x3, starting transfers between devices, widen(): other = lax.ppermute(part, 'dp', [(i, i ^ step) for i in range(ndp)])  5.68 us
    all_to_all x1, starting transfers between devices, swap_body(): lax.all_to_all(terms.reshape(ndp * n, 1, -1), ('dp', 'ctx'), 0, 0, tiled=...  5.54 us
    ppermute x3, waiting for transfers between devices, widen(): other = lax.ppermute(part, 'dp', [(i, i ^ step) for i in range(ndp)])  2.74 us
    pallas_call x1, Pallas kernels, local_stats(): pl.pallas_call(functools.partial(local_stats_kernel, HEAD ** (-0.5)), out...  2.71 us
    pallas_call x1, Pallas kernels, sib_join(): pl.pallas_call(sib_join_kernel, out_shape=[pltpu.HBM(o.shape, F32) for o...  2.2 us
    pallas_call x1, Pallas kernels, near_grad(): pl.pallas_call(functools.partial(near_grad_kernel, HEAD ** (-0.5)), out_s...  1.65 us
    pallas_call x1, Pallas kernels, far_grad(): pl.pallas_call(functools.partial(far_grad_kernel, HEAD ** (-0.5)), out_sh...  1.64 us
  transfers between devices with their start and end apart: 13, of which 6 were waited for; matrix products, arithmetic and copies ran while one was open for 0% of the time, Pallas kernels for 31%

profile of v22, /device:TPU:0, one launch (start us, length us, event | category | flops | bytes accessed | tf_op | source)
XLA Modules:
  0.0 40.2 jit_solution(10172924597034253877)
XLA Ops:
  0.6 1.3 %cross_pack.1 = (bf16[2,128,512]{2,1,0:T(8,128)(2,1)S(1)}, bf16[2,128,512]{2,1,0:T(8,128)(2,1)S(1)}, f32[1,512]{1,0:T(1,128)S(1)}) custom-call(s32[1,128]{1,0:T(1,128)} %pos_ref.2, bf16[512]{0:T(512)(128)(2,1)} %w_any.1, bf16[1,128,2048]{2,1,0:T(8,128)(2,1)} %k_ref.5, bf16[1,128,2048]{2,1,0:T(8,128)(2,1)} %v_ref.5, bf16[1,128,2048]{2,1,0:T(8,128)(2,1)} %q_ref.5, ...), custom_call_target="tpu_custom_call" | custom-call | flops 1 | bytes 1 | tf_op jit(solution)/shard_map/cross_pack/pallas_call | solution.py:314
  2.0 2.4 %collective-permute-start.7 = (bf16[2,128,512]{2,1,0:T(8,128)(2,1)S(1)}, bf16[2,128,512]{2,1,0:T(8,128)(2,1)S(1)}, u32[]{:S(2)}, u32[]{:S(2)}) collective-permute-start(bf16[2,128,512]{2,1,0:T(8,128)(2,1)S(1)} %get-tuple-element.93), channel_id=1, source_target_pairs={{0,3},{1,2},{2,1},{3,0},{4,7},{5,6},{6,5},{7,4},{8,11},{9,10},{10,... | collective-permute-start | bytes 786440 | tf_op jit(solution)/shard_map/ppermute | solution.py:840
  5.0 1.5 %collective-permute-start.5 = (f32[1,512]{1,0:T(1,128)S(1)}, f32[1,512]{1,0:T(1,128)S(1)}, u32[]{:S(2)}, u32[]{:S(2)}) collective-permute-start(f32[1,512]{1,0:T(1,128)S(1)} %get-tuple-element.86), channel_id=1, source_target_pairs={{0,4},{4,0},{8,12},{12,8},{16,20},{20,16},{24,28},{28,24},{1,5},{5... | collective-permute-start | bytes 6152 | tf_op jit(solution)/shard_map/ppermute | solution.py:852
  6.6 1.3 %sib_pack.1 = bf16[4,128,1024]{2,1,0:T(8,128)(2,1)S(1)} custom-call(s32[1,128]{1,0:T(1,128)S(1)} %copy-done, bf16[1,128,2048]{2,1,0:T(8,128)(2,1)} %k_ref.5, bf16[1,128,2048]{2,1,0:T(8,128)(2,1)} %v_ref.5, bf16[1,128,2048]{2,1,0:T(8,128)(2,1)} %q_ref.5, f32[1,128,2048]{2,1,0:T(8,128)} %dg_ref.5), custom_call_target="tpu_custom_call" | custom-call | flops 1 | bytes 1 | tf_op jit(solution)/shard_map/sib_pack/pallas_call | solution.py:350
  7.9 0.7 %collective-permute-done.5 = f32[1,512]{1,0:T(1,128)S(1)} collective-permute-done((f32[1,512]{1,0:T(1,128)S(1)}, f32[1,512]{1,0:T(1,128)S(1)}, u32[]{:S(2)}, u32[]{:S(2)}) %collective-permute-start.5) | collective-permute-done | bytes 2080 | tf_op jit(solution)/shard_map/ppermute | solution.py:852
  8.6 4.4 %conditional.2 = (bf16[4,128,1024]{2,1,0:T(8,128)(2,1)}, bf16[1,128,4096]{2,1,0:T(8,128)(2,1)}, f32[1,2048]{1,0:T(1,128)S(1)}) conditional(s32[]{:T(128)} %bitcast, () %tuple.29, (bf16[4,128,1024]{2,1,0:T(8,128)(2,1)S(1)}, bf16[1,128,4096]{2,1,0:T(8,128)(2,1)S(1)}, f32[1,1024]{1,0:T(1,128)S(1)}) %tuple.41), branch_computations={%region_0.0_spmd, %region_1.0_spmd} | conditional | flops 2048 | bytes 8421520 | solution.py:846
  9.2 1.6 %collective-permute-start.4 = (f32[1,1024]{1,0:T(1,128)S(1)}, f32[1,1024]{1,0:T(1,128)S(1)}, u32[]{:S(2)}, u32[]{:S(2)}) collective-permute-start(f32[1,1024]{1,0:T(1,128)S(1)} %get-tuple-element.22), channel_id=1, source_target_pairs={{0,8},{4,12},{8,0},{12,4},{16,24},{20,28},{24,16},{28,20},{1,9},{5... | collective-permute-start | bytes 12296 | tf_op jit(solution)/shard_map/cond/branch_1_fun/ppermute | solution.py:852
  10.8 2.0 %collective-permute-done.4 = f32[1,1024]{1,0:T(1,128)S(1)} collective-permute-done((f32[1,1024]{1,0:T(1,128)S(1)}, f32[1,1024]{1,0:T(1,128)S(1)}, u32[]{:S(2)}, u32[]{:S(2)}) %collective-permute-start.4) | collective-permute-done | bytes 4128 | tf_op jit(solution)/shard_map/cond/branch_1_fun/ppermute | solution.py:852
  13.0 2.6 %collective-permute-start.8 = (f32[1,2048]{1,0:T(1,128)S(1)}, f32[1,2048]{1,0:T(1,128)S(1)}, u32[]{:S(2)}, u32[]{:S(2)}) collective-permute-start(f32[1,2048]{1,0:T(1,128)S(1)} %get-tuple-element.99), channel_id=1, source_target_pairs={{0,16},{4,20},{8,24},{12,28},{16,0},{20,4},{24,8},{28,12},{1,17},{... | collective-permute-start | bytes 24584 | tf_op jit(solution)/shard_map/ppermute | solution.py:852
  15.6 2.7 %local_stats.1 = (f32[3,8,256]{2,1,0:T(8,128)S(1)}, f32[1,256]{1,0:T(1,128)S(1)}, bf16[4,256,512]{2,1,0:T(8,128)(2,1)S(1)}, bf16[4,256,512]{2,1,0:T(8,128)(2,1)S(1)}, bf16[2,128,4096]{2,1,0:T(8,128)(2,1)S(1)}) custom-call(s32[1,128]{1,0:T(1,128)S(1)} %copy-done, bf16[1,128,2048]{2,1,0:T(8,128)(2,1)} %k_ref.5, bf16[1,128,2048]{2,1,0:T(8,128)(2,1)} %v_ref.5, ...), custom_call_target="tpu_custom_call" | custom-call | flops 1 | bytes 1 | tf_op jit(solution)/shard_map/local_stats/pallas_call | solution.py:476
  18.3 0.8 %cross_stats.1 = (bf16[4,256,512]{2,1,0:T(8,128)(2,1)S(1)}, f32[3,4,256]{2,1,0:T(4,128)S(1)}, bf16[2,4,256,256]{3,2,1,0:T(8,128)(2,1)S(1)}) custom-call(bf16[4,256,512]{2,1,0:T(8,128)(2,1)S(1)} %get-tuple-element.92.near.pair, bf16[4,256,512]{2,1,0:T(8,128)(2,1)S(1)} %get-tuple-element.90.far, bf16[2,128,512]{2,1,0:T(8,128)(2,1)S(1)} %collective-permute-done.6.straight, ...), custom_call_target="tpu_custom_call" | custom-call | flops 1 | bytes 1 | tf_op jit(solution)/shard_map/cross_stats/pallas_call | solution.py:525
  19.2 0.7 %router_gate.1 = (f32[1,256]{1,0:T(1,128)S(1)}, f32[4,4,256]{2,1,0:T(4,128)S(1)}) custom-call(f32[1,256]{1,0:T(1,128)S(1)} %get-tuple-element.97.live_ref, bf16[2,128,4096]{2,1,0:T(8,128)(2,1)S(1)} %get-tuple-element.98.rows_x, f32[1,4096]{1,0:T(1,128)S(1)} %pad_maximum_fusion.1.w_ref, f32[3,8,256]{2,1,0:T(8,128)S(1)} %get-tuple-element.91.local, ...), custom_call_target="tpu_custom_call" | custom-call | flops 1 | bytes 1 | tf_op jit(solution)/shard_map/router_gate/pallas_call | solution.py:382
  19.9 1.5 %collective-permute-start.9 = (f32[4,4,256]{2,1,0:T(4,128)S(1)}, f32[4,4,256]{2,1,0:T(4,128)S(1)}, u32[]{:S(2)}, u32[]{:S(2)}) collective-permute-start(f32[4,4,256]{2,1,0:T(4,128)S(1)} %get-tuple-element.101), channel_id=1, source_target_pairs={{0,2},{1,3},{2,0},{3,1},{4,6},{5,7},{6,4},{7,5},{8,10},{9,11},{10,... | collective-permute-start | bytes 49160 | tf_op jit(solution)/shard_map/ppermute | solution.py:840
  21.3 1.6 %near_grad.1 = (f32[256,512]{1,0:T(8,128)S(1)}, bf16[3,128,512]{2,1,0:T(8,128)(2,1)S(1)}, bf16[3,128,512]{2,1,0:T(8,128)(2,1)S(1)}, f32[1,256]{1,0:T(1,128)S(1)}) custom-call(bf16[4,256,512]{2,1,0:T(8,128)(2,1)S(1)} %get-tuple-element.92.near.pair, f32[3,8,256]{2,1,0:T(8,128)S(1)} %get-tuple-element.91.local, f32[3,4,256]{2,1,0:T(4,128)S(1)} %get-tuple-element.96.stats, ...), custom_call_target="tpu_custom_call" | custom-call | flops 1 | bytes 1 | tf_op jit(solution)/shard_map/near_grad/pallas_call | solution.py:590
  23.0 0.7 %collective-permute-done.9.heard = f32[4,4,256]{2,1,0:T(4,128)S(1)} collective-permute-done((f32[4,4,256]{2,1,0:T(4,128)S(1)}, f32[4,4,256]{2,1,0:T(4,128)S(1)}, u32[]{:S(2)}, u32[]{:S(2)}) %collective-permute-start.9) | collective-permute-done | bytes 16416 | tf_op jit(solution)/shard_map/ppermute | solution.py:840
  23.7 1.5 %cross_grad.1 = (bf16[2,128,512]{2,1,0:T(8,128)(2,1)S(1)}, bf16[2,128,512]{2,1,0:T(8,128)(2,1)S(1)}, bf16[3,128,512]{2,1,0:T(8,128)(2,1)S(1)}, bf16[3,128,512]{2...) custom-call(bf16[4,256,512]{2,1,0:T(8,128)(2,1)S(1)} %get-tuple-elem, ...), custom_call_target="tpu_custom_call", output_to_operand_aliasing={{2}: (9, {}), {3}: (10, {})} | custom-call | flops 1 | bytes 1 | tf_op jit(solution)/shard_map/cross_grad/pallas_call | solution.py:658
  25.1 1.5 %collective-permute-start.10 = (bf16[2,128,512]{2,1,0:T(8,128)(2,1)S(1)}, bf16[2,128,512]{2,1,0:T(8,128)(2,1)S(1)}, u32[]{:S(2)}, u32[]{:S(2)}) collective-permute-start(bf16[2,128,512]{2,1,0:T(8,128)(2,1)S(1)} %get-tuple-element.118), channel_id=1, source_target_pairs={{0,2},{1,3},{2,0},{3,1},{4,6},{5,7},{6,4},{7,5},{8,10},{9,11},{10,... | collective-permute-start | bytes 786440 | tf_op jit(solution)/shard_map/ppermute | solution.py:840
  26.6 5.5 %all-to-all-start = ((f32[32,1,512]{2,1,0:T(1,128)}), f32[32,1,512]{2,1,0:T(1,128)S(1)}, u32[]{:S(2)}, u32[]{:S(2)}) async-start(f32[32,1,512]{2,1,0:T(1,128)} %bitcast.4), calls=%async_computation | async-start | bytes 131072 | tf_op jit(solution)/shard_map/all_to_all | solution.py:891
  32.1 3.9 %conditional.3 = (f32[1,128,2048]{2,1,0:T(8,128)}, f32[1,128,2048]{2,1,0:T(8,128)}, f32[1,128,2048]{2,1,0:T(8,128)}, bf16[2,128,512]{2,1,0:T(8,128)(2,1)S(1)}, b...) conditional(s32[]{:T(128)} %bitcast, () %tuple.28, (bf16[4,256,512]{2,1,0:T(8,128)(2,1)S(1)}, ...), branch_computations={%region_2.0_spmd, %region_3.0_spmd} | conditional | flops 2 | bytes 4194370 | solution.py:846
  32.5 1.6 %far_grad.1 = (bf16[3,128,512]{2,1,0:T(8,128)(2,1)S(1)}, bf16[3,128,512]{2,1,0:T(8,128)(2,1)S(1)}) custom-call(bf16[4,256,512]{2,1,0:T(8,128)(2,1)S(1)} %get-tuple-element.24.pair, f32[3,8,256]{2,1,0:T(8,128)S(1)} %get-tuple-element.25.local, f32[2,4,256]{2,1,0:T(4,128)S(1)} %get-tuple-element.26.final, f32[1,256]{1,0:T(1,128)S(1)} %get-tuple-element.27.gates, ...), custom_call_target="tpu_custom_call" | custom-call | flops 1 | bytes 1 | tf_op jit(solution)/shard_map/cond/branch_1_fun/far_grad/pallas_call | solution.py:701
  34.4 1.2 %own_join.1 = (f32[1,128,2048]{2,1,0:T(8,128)}, f32[1,128,2048]{2,1,0:T(8,128)}, f32[1,128,2048]{2,1,0:T(8,128)}, bf16[2,128,512]{2,1,0:T(8,128)(2,1)S(1)}) custom-call(bf16[3,128,512]{2,1,0:T(8,128)(2,1)S(1)} %get-tuple-element.23.low, bf16[3,128,512]{2,1,0:T(8,128)(2,1)S(1)} %get-tuple-element.29.high), custom_call_target="tpu_custom_call" | custom-call | flops 1 | bytes 1 | tf_op jit(solution)/shard_map/cond/branch_1_fun/own_join/pallas_call | solution.py:732
  36.0 2.2 %sib_join.1 = (f32[1,128,2048]{2,1,0:T(8,128)}, f32[1,128,2048]{2,1,0:T(8,128)}, f32[1,128,2048]{2,1,0:T(8,128)}, bf16[2,128,512]{2,1,0:T(8,128)(2,1)S(1)}) custom-call(bf16[3,128,512]{2,1,0:T(8,128)(2,1)} %get-tuple-element.112.low, bf16[3,128,512]{2,1,0:T(8,128)(2,1)} %get-tuple-element.113.high, ...), custom_call_target="tpu_custom_call", output_to_operand_aliasing={{0}: (2, {}), {1}: (3, {}), {2}: (4, {})} | custom-call | flops 1 | bytes 1 | tf_op jit(solution)/shard_map/sib_join/pallas_call | solution.py:771
  38.3 1.0 %add_back.1 = (f32[1,128,2048]{2,1,0:T(8,128)}, f32[1,128,2048]{2,1,0:T(8,128)}, f32[1,128,2048]{2,1,0:T(8,128)}) custom-call(bf16[2,128,512]{2,1,0:T(8,128)(2,1)S(1)} %get-tuple-element.111.own, bf16[2,128,512]{2,1,0:T(8,128)(2,1)S(1)} %get-tuple-element.117.sib, ...), custom_call_target="tpu_custom_call", output_to_operand_aliasing={{0}: (4, {}), {1}: (5, {}), {2}: (6, {})} | custom-call | flops 1 | bytes 1 | tf_op jit(solution)/shard_map/add_back/pallas_call | solution.py:822
  39.6 0.6 %reduce_sum.9 = f32[512]{0:T(512)} reduce(f32[32,1,512]{2,1,0:T(1,128)S(1)} %all-to-all-done, f32[]{:T(128)} %constant.2.clone.1), dimensions={0,1}, to_apply=%region_4.0 | reduce | flops 15872 | bytes 67588 | tf_op jit(solution)/shard_map/reduce_sum | solution.py:895
  (23 shorter events, 2.7 us)
Async XLA Ops:
  0.6 5.9 %copy-start = (s32[1,128]{1,0:T(1,128)S(1)}, s32[1,128]{1,0:T(1,128)}, u32[]{:S(2)}) copy-start(s32[1,128]{1,0:T(1,128)} %pos_ref.2) | copy-start | bytes 1540
  2.0 6.6 %copy-start.1 = (bf16[1,128,4096]{2,1,0:T(8,128)(2,1)S(1)}, bf16[1,128,4096]{2,1,0:T(8,128)(2,1)}, u32[]{:S(2)}) copy-start(bf16[1,128,4096]{2,1,0:T(8,128)(2,1)} %x_ref.1) | copy-start | bytes 3145732
  2.0 16.3 %collective-permute-start.7 = (bf16[2,128,512]{2,1,0:T(8,128)(2,1)S(1)}, bf16[2,128,512]{2,1,0:T(8,128)(2,1)S(1)}, u32[]{:S(2)}, u32[]{:S(2)}) collective-permute-start(bf16[2,128,512]{2,1,0:T(8,128)(2,1)S(1)} %get-tuple-element.93), channel_id=1, source_target_pairs={{0,3},{1,2},{2,1},{3,0},{4,7},{5,6},{6,5},{7,4},{8,11},{9,10},{10,... | collective-permute-start | bytes 786440 | tf_op jit(solution)/shard_map/ppermute | solution.py:840
  4.4 13.9 %collective-permute-start.6 = (bf16[2,128,512]{2,1,0:T(8,128)(2,1)S(1)}, bf16[2,128,512]{2,1,0:T(8,128)(2,1)S(1)}, u32[]{:S(2)}, u32[]{:S(2)}) collective-permute-start(bf16[2,128,512]{2,1,0:T(8,128)(2,1)S(1)} %get-tuple-element.84), channel_id=1, source_target_pairs={{0,2},{1,3},{2,0},{3,1},{4,6},{5,7},{6,4},{7,5},{8,10},{9,11},{10,... | collective-permute-start | bytes 786440 | tf_op jit(solution)/shard_map/ppermute | solution.py:840
  5.0 3.6 %collective-permute-start.5 = (f32[1,512]{1,0:T(1,128)S(1)}, f32[1,512]{1,0:T(1,128)S(1)}, u32[]{:S(2)}, u32[]{:S(2)}) collective-permute-start(f32[1,512]{1,0:T(1,128)S(1)} %get-tuple-element.86), channel_id=1, source_target_pairs={{0,4},{4,0},{8,12},{12,8},{16,20},{20,16},{24,28},{28,24},{1,5},{5... | collective-permute-start | bytes 6152 | tf_op jit(solution)/shard_map/ppermute | solution.py:852
  8.7 4.2 %collective-permute-start.2 = (bf16[4,128,1024]{2,1,0:T(8,128)(2,1)S(1)}, bf16[4,128,1024]{2,1,0:T(8,128)(2,1)}, u32[]{:S(2)}, u32[]{:S(2)}) collective-permute-start(bf16[4,128,1024]{2,1,0:T(8,128)(2,1)S(1)} %get-tuple-element.20), channel_id=1, source_target_pairs={{0,1},{1,0},{2,3},{3,2},{4,5},{5,4},{6,7},{7,6},{8,9},{9,8},{10,11... | collective-permute-start | bytes 3145736 | tf_op jit(solution)/shard_map/cond/branch_1_fun/ppermute | solution.py:840
  8.7 4.3 %collective-permute-start.3 = (bf16[1,128,4096]{2,1,0:T(8,128)(2,1)S(1)}, bf16[1,128,4096]{2,1,0:T(8,128)(2,1)}, u32[]{:S(2)}, u32[]{:S(2)}) collective-permute-start(bf16[1,128,4096]{2,1,0:T(8,128)(2,1)S(1)} %get-tuple-element.21), channel_id=1, source_target_pairs={{0,1},{1,0},{2,3},{3,2},{4,5},{5,4},{6,7},{7,6},{8,9},{9,8},{10,11... | collective-permute-start | bytes 3145736 | tf_op jit(solution)/shard_map/cond/branch_1_fun/ppermute | solution.py:840
  9.2 3.6 %collective-permute-start.4 = (f32[1,1024]{1,0:T(1,128)S(1)}, f32[1,1024]{1,0:T(1,128)S(1)}, u32[]{:S(2)}, u32[]{:S(2)}) collective-permute-start(f32[1,1024]{1,0:T(1,128)S(1)} %get-tuple-element.22), channel_id=1, source_target_pairs={{0,8},{4,12},{8,0},{12,4},{16,24},{20,28},{24,16},{28,20},{1,9},{5... | collective-permute-start | bytes 12296 | tf_op jit(solution)/shard_map/cond/branch_1_fun/ppermute | solution.py:852
  13.0 6.1 %collective-permute-start.8 = (f32[1,2048]{1,0:T(1,128)S(1)}, f32[1,2048]{1,0:T(1,128)S(1)}, u32[]{:S(2)}, u32[]{:S(2)}) collective-permute-start(f32[1,2048]{1,0:T(1,128)S(1)} %get-tuple-element.99), channel_id=1, source_target_pairs={{0,16},{4,20},{8,24},{12,28},{16,0},{20,4},{24,8},{28,12},{1,17},{... | collective-permute-start | bytes 24584 | tf_op jit(solution)/shard_map/ppermute | solution.py:852
  19.9 3.8 %collective-permute-start.9 = (f32[4,4,256]{2,1,0:T(4,128)S(1)}, f32[4,4,256]{2,1,0:T(4,128)S(1)}, u32[]{:S(2)}, u32[]{:S(2)}) collective-permute-start(f32[4,4,256]{2,1,0:T(4,128)S(1)} %get-tuple-element.101), channel_id=1, source_target_pairs={{0,2},{1,3},{2,0},{3,1},{4,6},{5,7},{6,4},{7,5},{8,10},{9,11},{10,... | collective-permute-start | bytes 49160 | tf_op jit(solution)/shard_map/ppermute | solution.py:840
  25.1 13.1 %collective-permute-start.10 = (bf16[2,128,512]{2,1,0:T(8,128)(2,1)S(1)}, bf16[2,128,512]{2,1,0:T(8,128)(2,1)S(1)}, u32[]{:S(2)}, u32[]{:S(2)}) collective-permute-start(bf16[2,128,512]{2,1,0:T(8,128)(2,1)S(1)} %get-tuple-element.118), channel_id=1, source_target_pairs={{0,2},{1,3},{2,0},{3,1},{4,6},{5,7},{6,4},{7,5},{8,10},{9,11},{10,... | collective-permute-start | bytes 786440 | tf_op jit(solution)/shard_map/ppermute | solution.py:840
  26.6 11.7 %collective-permute-start.11 = (bf16[2,128,512]{2,1,0:T(8,128)(2,1)S(1)}, bf16[2,128,512]{2,1,0:T(8,128)(2,1)S(1)}, u32[]{:S(2)}, u32[]{:S(2)}) collective-permute-start(bf16[2,128,512]{2,1,0:T(8,128)(2,1)S(1)} %get-tuple-element.119), channel_id=1, source_target_pairs={{0,3},{1,2},{2,1},{3,0},{4,7},{5,6},{6,5},{7,4},{8,11},{9,10},{10,... | collective-permute-start | bytes 786440 | tf_op jit(solution)/shard_map/ppermute | solution.py:840
  26.6 13.0 %all-to-all-start = ((f32[32,1,512]{2,1,0:T(1,128)}), f32[32,1,512]{2,1,0:T(1,128)S(1)}, u32[]{:S(2)}, u32[]{:S(2)}) async-start(f32[32,1,512]{2,1,0:T(1,128)} %bitcast.4), calls=%async_computation | async-start | bytes 131072 | tf_op jit(solution)/shard_map/all_to_all | solution.py:891
  32.2 3.5 %collective-permute-start = (bf16[3,128,512]{2,1,0:T(8,128)(2,1)S(1)}, bf16[3,128,512]{2,1,0:T(8,128)(2,1)}, u32[]{:S(2)}, u32[]{:S(2)}) collective-permute-start(bf16[3,128,512]{2,1,0:T(8,128)(2,1)S(1)} %get-tuple-element.34), channel_id=1, source_target_pairs={{0,1},{1,0},{2,3},{3,2},{4,5},{5,4},{6,7},{7,6},{8,9},{9,8},{10,11... | collective-permute-start | bytes 1179656 | tf_op jit(solution)/shard_map/cond/branch_1_fun/ppermute | solution.py:840
  34.1 1.9 %collective-permute-start.1 = (bf16[3,128,512]{2,1,0:T(8,128)(2,1)S(1)}, bf16[3,128,512]{2,1,0:T(8,128)(2,1)}, u32[]{:S(2)}, u32[]{:S(2)}) collective-permute-start(bf16[3,128,512]{2,1,0:T(8,128)(2,1)S(1)} %get-tuple-element.35), channel_id=1, source_target_pairs={{0,1},{1,0},{2,3},{3,2},{4,5},{5,4},{6,7},{7,6},{8,9},{9,8},{10,11... | collective-permute-start | bytes 1179656 | tf_op jit(solution)/shard_map/cond/branch_1_fun/ppermute | solution.py:840

commit v23 on v17

--- a/solution.py
+++ b/solution.py
@@ -784,7 +784,7 @@
     )(sib, *in_hbm(*outs))
 
 
-def add_back_kernel(own, sib, straight, diag, dq_in, dk_in, dv_in, dq_out, dk_out, dv_out, total, sems):
+def add_back_kernel(own, sib, diag, straight, dq_in, dk_in, dv_in, dq_out, dk_out, dv_out, total, sems):
     width = straight.shape[2]
     core, chip = here()
     ends = ((own, straight, 2 * core * width), (sib, diag, 2 * (1 - core) * width))
@@ -827,7 +827,7 @@
         compiler_params=params(),
         cost_estimate=cost(0, 24 * own.size),
         name="add_back",
-    )(own, sib, straight, diag, *in_hbm(*outs))
+    )(own, sib, diag, straight, *in_hbm(*outs))
 
 
 def swap_body(route_pos, x_routed, w_router, queries, keys, values, d_gated):
@@ -884,7 +884,7 @@
         cross, kept, stats, local, heard, gates, near_dq, near_sum, rows_x, ndp, n, total
     )
 
-    ret_s, ret_d = send(back_s, 2), send(back_d, 3)
+    ret_d, ret_s = send(back_d, 3), send(back_s, 2)
     shared = lax.all_to_all(terms.reshape(ndp * n, 1, -1), ("dp", "ctx"), 0, 0, tiled=True)
     outs, waiting, sib_in = beside(far_phase, far, local, final, gates, keep, dq_low, near_own, near_sib)
     *outs, waiting_sib = sib_join(sib_in, outs)

time: 40.2 us -> 41.5 us (1.032)
  waiting for transfers between devices: 4.57 us -> 6.24 us
    ppermute x8, waiting for transfers between devices: 1.82 us -> 3.37 us  [send(): return lax.ppermute(a, 'ctx', [(i, i ^ flip) for i in range(n)])]
  transfers between devices with their start and end apart: 12 -> 12, of which waited for: 5 -> 7; matrix products, arithmetic and copies ran while one was open for 0% -> 0% of each run, Pallas kernels for 31% -> 30%
where the time goes in v23:
time: 41.5 us; the launch traced here: 41.3 us
  starting transfers between devices  17.8 us (43%)
  Pallas kernels  15.7 us (38%)
  waiting for transfers between devices  6.24 us (15%)
  between operations  0.81 us (2%)
  other arithmetic  0.68 us (2%)
    ppermute x8, starting transfers between devices, send(): return lax.ppermute(a, 'ctx', [(i, i ^ flip) for i in range(n)])  6.91 us
    ppermute x3, starting transfers between devices, widen(): other = lax.ppermute(part, 'dp', [(i, i ^ step) for i in range(ndp)])  5.68 us
    all_to_all x1, starting transfers between devices, swap_body(): lax.all_to_all(terms.reshape(ndp * n, 1, -1), ('dp', 'ctx'), 0, 0, tiled=...  5.19 us
    ppermute x8, waiting for transfers between devices, send(): return lax.ppermute(a, 'ctx', [(i, i ^ flip) for i in range(n)])  3.37 us
    ppermute x3, waiting for transfers between devices, widen(): other = lax.ppermute(part, 'dp', [(i, i ^ step) for i in range(ndp)])  2.74 us
    pallas_call x1, Pallas kernels, local_stats(): pl.pallas_call(functools.partial(local_stats_kernel, HEAD ** (-0.5)), out...  2.69 us
    pallas_call x1, Pallas kernels, sib_join(): pl.pallas_call(sib_join_kernel, out_shape=[pltpu.HBM(o.shape, F32) for o...  2.17 us
    pallas_call x1, Pallas kernels, far_grad(): pl.pallas_call(functools.partial(far_grad_kernel, HEAD ** (-0.5)), out_sh...  1.71 us
  transfers between devices with their start and end apart: 12, of which 7 were waited for; matrix products, arithmetic and copies ran while one was open for 0% of the time, Pallas kernels for 30%

profile of v23, /device:TPU:0, one launch (start us, length us, event | category | flops | bytes accessed | tf_op | source)
XLA Modules:
  0.0 41.3 jit_solution(9413297796576185470)
XLA Ops:
  0.6 1.3 %cross_pack.1 = (bf16[2,128,512]{2,1,0:T(8,128)(2,1)S(1)}, bf16[2,128,512]{2,1,0:T(8,128)(2,1)S(1)}, f32[1,512]{1,0:T(1,128)S(1)}) custom-call(s32[1,128]{1,0:T(1,128)} %pos_ref.2, bf16[512]{0:T(512)(128)(2,1)} %w_any.1, bf16[1,128,2048]{2,1,0:T(8,128)(2,1)} %k_ref.5, bf16[1,128,2048]{2,1,0:T(8,128)(2,1)} %v_ref.5, bf16[1,128,2048]{2,1,0:T(8,128)(2,1)} %q_ref.5, ...), custom_call_target="tpu_custom_call" | custom-call | flops 1 | bytes 1 | tf_op jit(solution)/shard_map/cross_pack/pallas_call | solution.py:314
  2.0 2.4 %collective-permute-start.6 = (bf16[2,128,512]{2,1,0:T(8,128)(2,1)S(1)}, bf16[2,128,512]{2,1,0:T(8,128)(2,1)S(1)}, u32[]{:S(2)}, u32[]{:S(2)}) collective-permute-start(bf16[2,128,512]{2,1,0:T(8,128)(2,1)S(1)} %get-tuple-element.94), channel_id=1, source_target_pairs={{0,3},{1,2},{2,1},{3,0},{4,7},{5,6},{6,5},{7,4},{8,11},{9,10},{10,... | collective-permute-start | bytes 786440 | tf_op jit(solution)/shard_map/ppermute | solution.py:838
  5.0 1.5 %collective-permute-start.4 = (f32[1,512]{1,0:T(1,128)S(1)}, f32[1,512]{1,0:T(1,128)S(1)}, u32[]{:S(2)}, u32[]{:S(2)}) collective-permute-start(f32[1,512]{1,0:T(1,128)S(1)} %get-tuple-element.87), channel_id=1, source_target_pairs={{0,4},{4,0},{8,12},{12,8},{16,20},{20,16},{24,28},{28,24},{1,5},{5... | collective-permute-start | bytes 6152 | tf_op jit(solution)/shard_map/ppermute | solution.py:850
  6.6 1.3 %sib_pack.1 = bf16[4,128,1024]{2,1,0:T(8,128)(2,1)S(1)} custom-call(s32[1,128]{1,0:T(1,128)S(1)} %copy-done, bf16[1,128,2048]{2,1,0:T(8,128)(2,1)} %k_ref.5, bf16[1,128,2048]{2,1,0:T(8,128)(2,1)} %v_ref.5, bf16[1,128,2048]{2,1,0:T(8,128)(2,1)} %q_ref.5, f32[1,128,2048]{2,1,0:T(8,128)} %dg_ref.5), custom_call_target="tpu_custom_call" | custom-call | flops 1 | bytes 1 | tf_op jit(solution)/shard_map/sib_pack/pallas_call | solution.py:350
  7.9 0.7 %collective-permute-done.4 = f32[1,512]{1,0:T(1,128)S(1)} collective-permute-done((f32[1,512]{1,0:T(1,128)S(1)}, f32[1,512]{1,0:T(1,128)S(1)}, u32[]{:S(2)}, u32[]{:S(2)}) %collective-permute-start.4) | collective-permute-done | bytes 2080 | tf_op jit(solution)/shard_map/ppermute | solution.py:850
  8.6 4.4 %conditional.2 = (bf16[4,128,1024]{2,1,0:T(8,128)(2,1)}, bf16[1,128,4096]{2,1,0:T(8,128)(2,1)}, f32[1,2048]{1,0:T(1,128)S(1)}) conditional(s32[]{:T(128)} %bitcast, () %tuple.29, (bf16[4,128,1024]{2,1,0:T(8,128)(2,1)S(1)}, bf16[1,128,4096]{2,1,0:T(8,128)(2,1)S(1)}, f32[1,1024]{1,0:T(1,128)S(1)}) %tuple.41), branch_computations={%region_0.0_spmd, %region_1.0_spmd} | conditional | flops 2048 | bytes 8421520 | solution.py:844
  9.2 1.6 %collective-permute-start.3 = (f32[1,1024]{1,0:T(1,128)S(1)}, f32[1,1024]{1,0:T(1,128)S(1)}, u32[]{:S(2)}, u32[]{:S(2)}) collective-permute-start(f32[1,1024]{1,0:T(1,128)S(1)} %get-tuple-element.24), channel_id=1, source_target_pairs={{0,8},{4,12},{8,0},{12,4},{16,24},{20,28},{24,16},{28,20},{1,9},{5... | collective-permute-start | bytes 12296 | tf_op jit(solution)/shard_map/cond/branch_1_fun/ppermute | solution.py:850
  10.8 2.0 %collective-permute-done.3 = f32[1,1024]{1,0:T(1,128)S(1)} collective-permute-done((f32[1,1024]{1,0:T(1,128)S(1)}, f32[1,1024]{1,0:T(1,128)S(1)}, u32[]{:S(2)}, u32[]{:S(2)}) %collective-permute-start.3) | collective-permute-done | bytes 4128 | tf_op jit(solution)/shard_map/cond/branch_1_fun/ppermute | solution.py:850
  13.0 2.6 %collective-permute-start.7 = (f32[1,2048]{1,0:T(1,128)S(1)}, f32[1,2048]{1,0:T(1,128)S(1)}, u32[]{:S(2)}, u32[]{:S(2)}) collective-permute-start(f32[1,2048]{1,0:T(1,128)S(1)} %get-tuple-element.100), channel_id=1, source_target_pairs={{0,16},{4,20},{8,24},{12,28},{16,0},{20,4},{24,8},{28,12},{1,17},{... | collective-permute-start | bytes 24584 | tf_op jit(solution)/shard_map/ppermute | solution.py:850
  15.6 2.7 %local_stats.1 = (f32[3,8,256]{2,1,0:T(8,128)S(1)}, f32[1,256]{1,0:T(1,128)S(1)}, bf16[4,256,512]{2,1,0:T(8,128)(2,1)S(1)}, bf16[4,256,512]{2,1,0:T(8,128)(2,1)S(1)}, bf16[2,128,4096]{2,1,0:T(8,128)(2,1)S(1)}) custom-call(s32[1,128]{1,0:T(1,128)S(1)} %copy-done, bf16[1,128,2048]{2,1,0:T(8,128)(2,1)} %k_ref.5, bf16[1,128,2048]{2,1,0:T(8,128)(2,1)} %v_ref.5, ...), custom_call_target="tpu_custom_call" | custom-call | flops 1 | bytes 1 | tf_op jit(solution)/shard_map/local_stats/pallas_call | solution.py:476
  18.3 0.8 %cross_stats.1 = (bf16[4,256,512]{2,1,0:T(8,128)(2,1)S(1)}, f32[3,4,256]{2,1,0:T(4,128)S(1)}, bf16[2,4,256,256]{3,2,1,0:T(8,128)(2,1)S(1)}) custom-call(bf16[4,256,512]{2,1,0:T(8,128)(2,1)S(1)} %get-tuple-element.93.near.pair, bf16[4,256,512]{2,1,0:T(8,128)(2,1)S(1)} %get-tuple-element.91.far, bf16[2,128,512]{2,1,0:T(8,128)(2,1)S(1)} %collective-permute-done.5.straight, ...), custom_call_target="tpu_custom_call" | custom-call | flops 1 | bytes 1 | tf_op jit(solution)/shard_map/cross_stats/pallas_call | solution.py:525
  19.8 1.5 %collective-permute-start.8 = (f32[4,4,256]{2,1,0:T(4,128)S(1)}, f32[4,4,256]{2,1,0:T(4,128)S(1)}, u32[]{:S(2)}, u32[]{:S(2)}) collective-permute-start(f32[4,4,256]{2,1,0:T(4,128)S(1)} %get-tuple-element.102), channel_id=1, source_target_pairs={{0,2},{1,3},{2,0},{3,1},{4,6},{5,7},{6,4},{7,5},{8,10},{9,11},{10,... | collective-permute-start | bytes 49160 | tf_op jit(solution)/shard_map/ppermute | solution.py:838
  21.3 1.6 %near_grad.1 = (f32[256,512]{1,0:T(8,128)S(1)}, bf16[2,128,512]{2,1,0:T(8,128)(2,1)S(1)}, bf16[2,128,512]{2,1,0:T(8,128)(2,1)S(1)}, f32[1,256]{1,0:T(1,128)S(1)}) custom-call(bf16[4,256,512]{2,1,0:T(8,128)(2,1)S(1)} %get-tuple-element.93.near.pair, f32[3,8,256]{2,1,0:T(8,128)S(1)} %get-tuple-element.92.local, f32[3,4,256]{2,1,0:T(4,128)S(1)} %get-tuple-element.97.stats, ...), custom_call_target="tpu_custom_call" | custom-call | flops 1 | bytes 1 | tf_op jit(solution)/shard_map/near_grad/pallas_call | solution.py:590
  23.0 0.7 %collective-permute-done.8.heard = f32[4,4,256]{2,1,0:T(4,128)S(1)} collective-permute-done((f32[4,4,256]{2,1,0:T(4,128)S(1)}, f32[4,4,256]{2,1,0:T(4,128)S(1)}, u32[]{:S(2)}, u32[]{:S(2)}) %collective-permute-start.8) | collective-permute-done | bytes 16416 | tf_op jit(solution)/shard_map/ppermute | solution.py:838
  23.7 1.1 %cross_grad.1 = (bf16[2,128,512]{2,1,0:T(8,128)(2,1)S(1)}, bf16[2,128,512]{2,1,0:T(8,128)(2,1)S(1)}, bf16[256,512]{1,0:T(8,128)(2,1)S(1)}, bf16[2,256,512]{2,1,0...) custom-call(bf16[4,256,512]{2,1,0:T(8,128)(2,1)S(1)} %get-tuple-element.95.cross, ...), custom_call_target="tpu_custom_call" | custom-call | flops 1 | bytes 1 | tf_op jit(solution)/shard_map/cross_grad/pallas_call | solution.py:656
  24.9 1.5 %collective-permute-start.10 = (bf16[2,128,512]{2,1,0:T(8,128)(2,1)S(1)}, bf16[2,128,512]{2,1,0:T(8,128)(2,1)S(1)}, u32[]{:S(2)}, u32[]{:S(2)}) collective-permute-start(bf16[2,128,512]{2,1,0:T(8,128)(2,1)S(1)} %get-tuple-element.118), channel_id=1, source_target_pairs={{0,2},{1,3},{2,0},{3,1},{4,6},{5,7},{6,4},{7,5},{8,10},{9,11},{10,... | collective-permute-start | bytes 786440 | tf_op jit(solution)/shard_map/ppermute | solution.py:838
  26.3 5.2 %all-to-all-start = ((f32[32,1,512]{2,1,0:T(1,128)}), f32[32,1,512]{2,1,0:T(1,128)S(1)}, u32[]{:S(2)}, u32[]{:S(2)}) async-start(f32[32,1,512]{2,1,0:T(1,128)} %bitcast.4), calls=%async_computation | async-start | bytes 131072 | tf_op jit(solution)/shard_map/all_to_all | solution.py:888
  31.5 4.2 %conditional.3 = (f32[1,128,2048]{2,1,0:T(8,128)}, f32[1,128,2048]{2,1,0:T(8,128)}, f32[1,128,2048]{2,1,0:T(8,128)}, bf16[2,128,512]{2,1,0:T(8,128)(2,1)S(1)}, bf16[3,128,1024]{2,1,0:T(8,128)(2,1)}) conditional(s32[]{:T(128)} %bitcast, () %tuple.28, (bf16[4,256,512]{2,1,0:T(8,128)(2,1)S(1)}, f32[3,8,256]{2,1,0:T(8,128)S(1)}, ...), branch_computations={%region_2.0_spmd, %region_3.0_spmd} | conditional | flops 2 | bytes 4194360 | solution.py:844
  31.6 1.7 %far_grad.1 = (bf16[3,128,1024]{2,1,0:T(8,128)(2,1)S(1)}, bf16[3,128,1024]{2,1,0:T(8,128)(2,1)S(1)}) custom-call(bf16[4,256,512]{2,1,0:T(8,128)(2,1)S(1)} %get-tuple-element.25.pair, f32[3,8,256]{2,1,0:T(8,128)S(1)} %get-tuple-element.26.local, f32[2,4,256]{2,1,0:T(4,128)S(1)} %get-tuple-element.27.final, f32[1,256]{1,0:T(1,128)S(1)} %get-tuple-element.28.gates, ...), custom_call_target="tpu_custom_call" | custom-call | flops 1 | bytes 1 | tf_op jit(solution)/shard_map/cond/branch_1_fun/far_grad/pallas_call | solution.py:703
  33.6 1.2 %own_join.1 = (f32[1,128,2048]{2,1,0:T(8,128)}, f32[1,128,2048]{2,1,0:T(8,128)}, f32[1,128,2048]{2,1,0:T(8,128)}, bf16[2,128,512]{2,1,0:T(8,128)(2,1)S(1)}) custom-call(bf16[3,128,1024]{2,1,0:T(8,128)(2,1)S(1)} %get-tuple-element.33.own), custom_call_target="tpu_custom_call" | custom-call | flops 1 | bytes 1 | tf_op jit(solution)/shard_map/cond/branch_1_fun/own_join/pallas_call | solution.py:734
  34.8 1.0 %collective-permute-done = bf16[3,128,1024]{2,1,0:T(8,128)(2,1)} collective-permute-done((bf16[3,128,1024]{2,1,0:T(8,128)(2,1)S(1)}, bf16[3,128,1024]{2,1,0:T(8,128)(2,1)}, u32[]{:S(2)}, u32[]{:S(2)}) %collective-permute-start) | collective-permute-done | bytes 786464 | tf_op jit(solution)/shard_map/cond/branch_1_fun/ppermute | solution.py:838
  35.8 2.2 %sib_join.1 = (f32[1,128,2048]{2,1,0:T(8,128)}, f32[1,128,2048]{2,1,0:T(8,128)}, f32[1,128,2048]{2,1,0:T(8,128)}, bf16[2,128,512]{2,1,0:T(8,128)(2,1)S(1)}) custom-call(bf16[3,128,1024]{2,1,0:T(8,128)(2,1)} %get-tuple-element.112.sib, f32[1,128,2048]{2,1,0:T(8,128)} %get-tuple-element.113.dq_in, ...), custom_call_target="tpu_custom_call", output_to_operand_aliasing={{0}: (1, {}), {1}: (2, {}), {2}: (3, {})} | custom-call | flops 1 | bytes 1 | tf_op jit(solution)/shard_map/sib_join/pallas_call | solution.py:769
  38.0 1.6 %collective-permute-done.10.straight = bf16[2,128,512]{2,1,0:T(8,128)(2,1)S(1)} collective-permute-done((bf16[2,128,512]{2,1,0:T(8,128)(2,1)S(1)}, bf16[2,128,512]{2,1,0:T(8,128)(2,1)S(1)}, u32[]{:S(2)}, u32[]{:S(2)}) %collective-permute-start.10) | collective-permute-done | bytes 262176 | tf_op jit(solution)/shard_map/ppermute | solution.py:838
  39.5 1.0 %add_back.1 = (f32[1,128,2048]{2,1,0:T(8,128)}, f32[1,128,2048]{2,1,0:T(8,128)}, f32[1,128,2048]{2,1,0:T(8,128)}) custom-call(bf16[2,128,512]{2,1,0:T(8,128)(2,1)S(1)} %get-tuple-element.111.own, bf16[2,128,512]{2,1,0:T(8,128)(2,1)S(1)} %get-tuple-element.116.sib, ...), custom_call_target="tpu_custom_call", output_to_operand_aliasing={{0}: (4, {}), {1}: (5, {}), {2}: (6, {})} | custom-call | flops 1 | bytes 1 | tf_op jit(solution)/shard_map/add_back/pallas_call | solution.py:820
  (21 shorter events, 3.2 us)
Async XLA Ops:
  0.6 5.9 %copy-start = (s32[1,128]{1,0:T(1,128)S(1)}, s32[1,128]{1,0:T(1,128)}, u32[]{:S(2)}) copy-start(s32[1,128]{1,0:T(1,128)} %pos_ref.2) | copy-start | bytes 1540
  2.0 6.6 %copy-start.1 = (bf16[1,128,4096]{2,1,0:T(8,128)(2,1)S(1)}, bf16[1,128,4096]{2,1,0:T(8,128)(2,1)}, u32[]{:S(2)}) copy-start(bf16[1,128,4096]{2,1,0:T(8,128)(2,1)} %x_ref.1) | copy-start | bytes 3145732
  2.0 16.3 %collective-permute-start.6 = (bf16[2,128,512]{2,1,0:T(8,128)(2,1)S(1)}, bf16[2,128,512]{2,1,0:T(8,128)(2,1)S(1)}, u32[]{:S(2)}, u32[]{:S(2)}) collective-permute-start(bf16[2,128,512]{2,1,0:T(8,128)(2,1)S(1)} %get-tuple-element.94), channel_id=1, source_target_pairs={{0,3},{1,2},{2,1},{3,0},{4,7},{5,6},{6,5},{7,4},{8,11},{9,10},{10,... | collective-permute-start | bytes 786440 | tf_op jit(solution)/shard_map/ppermute | solution.py:838
  4.4 13.9 %collective-permute-start.5 = (bf16[2,128,512]{2,1,0:T(8,128)(2,1)S(1)}, bf16[2,128,512]{2,1,0:T(8,128)(2,1)S(1)}, u32[]{:S(2)}, u32[]{:S(2)}) collective-permute-start(bf16[2,128,512]{2,1,0:T(8,128)(2,1)S(1)} %get-tuple-element.85), channel_id=1, source_target_pairs={{0,2},{1,3},{2,0},{3,1},{4,6},{5,7},{6,4},{7,5},{8,10},{9,11},{10,... | collective-permute-start | bytes 786440 | tf_op jit(solution)/shard_map/ppermute | solution.py:838
  5.0 3.6 %collective-permute-start.4 = (f32[1,512]{1,0:T(1,128)S(1)}, f32[1,512]{1,0:T(1,128)S(1)}, u32[]{:S(2)}, u32[]{:S(2)}) collective-permute-start(f32[1,512]{1,0:T(1,128)S(1)} %get-tuple-element.87), channel_id=1, source_target_pairs={{0,4},{4,0},{8,12},{12,8},{16,20},{20,16},{24,28},{28,24},{1,5},{5... | collective-permute-start | bytes 6152 | tf_op jit(solution)/shard_map/ppermute | solution.py:850
  8.7 4.2 %collective-permute-start.1 = (bf16[4,128,1024]{2,1,0:T(8,128)(2,1)S(1)}, bf16[4,128,1024]{2,1,0:T(8,128)(2,1)}, u32[]{:S(2)}, u32[]{:S(2)}) collective-permute-start(bf16[4,128,1024]{2,1,0:T(8,128)(2,1)S(1)} %get-tuple-element.22), channel_id=1, source_target_pairs={{0,1},{1,0},{2,3},{3,2},{4,5},{5,4},{6,7},{7,6},{8,9},{9,8},{10,11... | collective-permute-start | bytes 3145736 | tf_op jit(solution)/shard_map/cond/branch_1_fun/ppermute | solution.py:838
  8.7 4.3 %collective-permute-start.2 = (bf16[1,128,4096]{2,1,0:T(8,128)(2,1)S(1)}, bf16[1,128,4096]{2,1,0:T(8,128)(2,1)}, u32[]{:S(2)}, u32[]{:S(2)}) collective-permute-start(bf16[1,128,4096]{2,1,0:T(8,128)(2,1)S(1)} %get-tuple-element.23), channel_id=1, source_target_pairs={{0,1},{1,0},{2,3},{3,2},{4,5},{5,4},{6,7},{7,6},{8,9},{9,8},{10,11... | collective-permute-start | bytes 3145736 | tf_op jit(solution)/shard_map/cond/branch_1_fun/ppermute | solution.py:838
  9.2 3.6 %collective-permute-start.3 = (f32[1,1024]{1,0:T(1,128)S(1)}, f32[1,1024]{1,0:T(1,128)S(1)}, u32[]{:S(2)}, u32[]{:S(2)}) collective-permute-start(f32[1,1024]{1,0:T(1,128)S(1)} %get-tuple-element.24), channel_id=1, source_target_pairs={{0,8},{4,12},{8,0},{12,4},{16,24},{20,28},{24,16},{28,20},{1,9},{5... | collective-permute-start | bytes 12296 | tf_op jit(solution)/shard_map/cond/branch_1_fun/ppermute | solution.py:850
  13.0 6.1 %collective-permute-start.7 = (f32[1,2048]{1,0:T(1,128)S(1)}, f32[1,2048]{1,0:T(1,128)S(1)}, u32[]{:S(2)}, u32[]{:S(2)}) collective-permute-start(f32[1,2048]{1,0:T(1,128)S(1)} %get-tuple-element.100), channel_id=1, source_target_pairs={{0,16},{4,20},{8,24},{12,28},{16,0},{20,4},{24,8},{28,12},{1,17},{... | collective-permute-start | bytes 24584 | tf_op jit(solution)/shard_map/ppermute | solution.py:850
  19.8 3.8 %collective-permute-start.8 = (f32[4,4,256]{2,1,0:T(4,128)S(1)}, f32[4,4,256]{2,1,0:T(4,128)S(1)}, u32[]{:S(2)}, u32[]{:S(2)}) collective-permute-start(f32[4,4,256]{2,1,0:T(4,128)S(1)} %get-tuple-element.102), channel_id=1, source_target_pairs={{0,2},{1,3},{2,0},{3,1},{4,6},{5,7},{6,4},{7,5},{8,10},{9,11},{10,... | collective-permute-start | bytes 49160 | tf_op jit(solution)/shard_map/ppermute | solution.py:838
  24.8 13.1 %collective-permute-start.9 = (bf16[2,128,512]{2,1,0:T(8,128)(2,1)S(1)}, bf16[2,128,512]{2,1,0:T(8,128)(2,1)S(1)}, u32[]{:S(2)}, u32[]{:S(2)}) collective-permute-start(bf16[2,128,512]{2,1,0:T(8,128)(2,1)S(1)} %get-tuple-element.117), channel_id=1, source_target_pairs={{0,3},{1,2},{2,1},{3,0},{4,7},{5,6},{6,5},{7,4},{8,11},{9,10},{10,... | collective-permute-start | bytes 786440 | tf_op jit(solution)/shard_map/ppermute | solution.py:838
  24.9 14.6 %collective-permute-start.10 = (bf16[2,128,512]{2,1,0:T(8,128)(2,1)S(1)}, bf16[2,128,512]{2,1,0:T(8,128)(2,1)S(1)}, u32[]{:S(2)}, u32[]{:S(2)}) collective-permute-start(bf16[2,128,512]{2,1,0:T(8,128)(2,1)S(1)} %get-tuple-element.118), channel_id=1, source_target_pairs={{0,2},{1,3},{2,0},{3,1},{4,6},{5,7},{6,4},{7,5},{8,10},{9,11},{10,... | collective-permute-start | bytes 786440 | tf_op jit(solution)/shard_map/ppermute | solution.py:838
  26.3 14.3 %all-to-all-start = ((f32[32,1,512]{2,1,0:T(1,128)}), f32[32,1,512]{2,1,0:T(1,128)S(1)}, u32[]{:S(2)}, u32[]{:S(2)}) async-start(f32[32,1,512]{2,1,0:T(1,128)} %bitcast.4), calls=%async_computation | async-start | bytes 131072 | tf_op jit(solution)/shard_map/all_to_all | solution.py:888
  33.3 2.5 %collective-permute-start = (bf16[3,128,1024]{2,1,0:T(8,128)(2,1)S(1)}, bf16[3,128,1024]{2,1,0:T(8,128)(2,1)}, u32[]{:S(2)}, u32[]{:S(2)}) collective-permute-start(bf16[3,128,1024]{2,1,0:T(8,128)(2,1)S(1)} %get-tuple-element.38), channel_id=1, source_target_pairs={{0,1},{1,0},{2,3},{3,2},{4,5},{5,4},{6,7},{7,6},{8,9},{9,8},{10,11... | collective-permute-start | bytes 2359304 | tf_op jit(solution)/shard_map/cond/branch_1_fun/ppermute | solution.py:838
